TPU v7x, 32 devices: a whole 2x2x4 slice. The times are simulated.
32 devices in a mesh: role: 4 (over x, core), ctx: 4 (over z), tp: 2 (over y).
Axes of the slice: x: 2, y: 2, z: 4, core: 2. Of those that a mesh axis runs over, the one named last changes fastest.
Arguments:
- prefill_q: bfloat16 [4, 1024, 64, 128], P('role', 'ctx', 'tp'), may hold values from -6 to 6
- prefill_k: bfloat16 [4, 1024, 8, 128], P('role', 'ctx', 'tp'), may hold values from -6 to 6
- prefill_v: bfloat16 [4, 1024, 8, 128], P('role', 'ctx', 'tp'), may hold values from -6 to 6
- decode_q: bfloat16 [512, 4, 64, 128], P(('role', 'ctx'), None, 'tp'), may hold values from -6 to 6
- decode_k: bfloat16 [512, 4, 8, 128], P(('role', 'ctx'), None, 'tp'), may hold values from -6 to 6
- decode_v: bfloat16 [512, 4, 8, 128], P(('role', 'ctx'), None, 'tp'), may hold values from -6 to 6
- cache_k: bfloat16 [512, 128, 8, 128], P(('role', 'ctx'), None, 'tp'), may hold values from -6 to 6
- cache_v: bfloat16 [512, 128, 8, 128], P(('role', 'ctx'), None, 'tp'), may hold values from -6 to 6
- cache_len: int32 [512], P(('role', 'ctx')), may hold values from 1 to 128
- page_list: int32 [512, 4], P(('role', 'ctx')), may hold values from 0 to 31, as said below
Outputs:
- prefill_out: bfloat16 [4, 1024, 64, 128], P('role', 'ctx', 'tp')
- decode_out: bfloat16 [512, 4, 8192], P(('role', 'ctx', 'tp'))
Inputs may be any that keep to these rules, and one draw needn't show every extreme that they name: `page_list`: each request names 4 pages of 4 different owners, where the owner of page p is p // 2. Among the requests of one device (aligned blocks of 32 rows), all pages named from one owner are the same page.
All inputs are finite; a program needn't handle non-finite values.
Results may differ from a plain program's by a relative error of at most 0.0033.
Values may be sent and summed in bfloat16 or wider, within the bound.
No kernel may reach another device: no remote copies, remote signals or barrier semaphores. Data moves between devices by JAX's collectives and lax.ppermute only.
A program may use at most 192 MiB of HBM per device.

v0:
```python
import math

import jax
import jax.numpy as jnp
from jax import lax
from jax.sharding import PartitionSpec as P

PAGE = 128


def shards(
    prefill_q,
    prefill_k,
    prefill_v,
    decode_q,
    decode_k,
    decode_v,
    cache_k,
    cache_v,
    cache_len,
    page_list,
):
    tok_local = prefill_q.shape[1]
    q_heads = prefill_q.shape[2]
    kv_local = prefill_k.shape[2]
    width = prefill_q.shape[3]
    group = q_heads // kv_local
    inverse_root = 1.0 / math.sqrt(width)
    ctx_index = lax.axis_index("ctx")
    rows_here = ctx_index * tok_local + jnp.arange(tok_local)
    grouped = prefill_q[0].reshape(tok_local, kv_local, group, width).transpose(1, 2, 0, 3)

    def attend_block(carry, inputs):
        running_max, running_sum, running_acc = carry
        keys_block, values_block, first = inputs
        columns = first + jnp.arange(tok_local)
        scores = (
            jnp.einsum("kgqd,pkd->kgqp", grouped, keys_block, preferred_element_type=jnp.float32)
            * inverse_root
        )
        allowed = columns[None, :] <= rows_here[:, None]
        scores = jnp.where(allowed, scores, -1e30)
        new_max = jnp.maximum(running_max, jnp.max(scores, axis=-1))
        weights = jnp.where(allowed, jnp.exp(scores - new_max[..., None]), 0.0)
        shrink = jnp.exp(running_max - new_max)
        running_sum = running_sum * shrink + jnp.sum(weights, axis=-1)
        update = jnp.einsum(
            "kgqp,pkd->kgqd",
            weights.astype(jnp.bfloat16),
            values_block,
            preferred_element_type=jnp.float32,
        )
        running_acc = running_acc * shrink[..., None] + update
        return ((new_max, running_sum, running_acc), None)

    initial = (
        jnp.full((kv_local, group, tok_local), -1e30, jnp.float32),
        jnp.zeros((kv_local, group, tok_local), jnp.float32),
        jnp.zeros((kv_local, group, tok_local, width), jnp.float32),
    )
    carry = initial
    keys_all = lax.all_gather(prefill_k, "ctx", axis=1, tiled=True)
    values_all = lax.all_gather(prefill_v, "ctx", axis=1, tiled=True)
    blocks = keys_all.shape[1] // tok_local
    keys_blocks = keys_all[0].reshape(blocks, tok_local, kv_local, width)
    values_blocks = values_all[0].reshape(blocks, tok_local, kv_local, width)
    firsts = tok_local * jnp.arange(blocks)
    carry, _ = lax.scan(attend_block, carry, (keys_blocks, values_blocks, firsts))
    final_max, final_sum, final_acc = carry
    prefill_out = (
        (final_acc / final_sum[..., None])
        .transpose(2, 0, 1, 3)
        .reshape(1, tok_local, q_heads, width)
        .astype(jnp.bfloat16)
    )
    own_count = tok_local // PAGE
    page_keys = prefill_k[0].reshape(own_count, PAGE, kv_local, width)
    page_values = prefill_v[0].reshape(own_count, PAGE, kv_local, width)
    requests_local = decode_q.shape[0]
    all_keys, all_values = (
        lax.all_gather(page_keys, ("role", "ctx"), axis=0, tiled=True),
        lax.all_gather(page_values, ("role", "ctx"), axis=0, tiled=True),
    )
    chosen_keys = all_keys[page_list]
    chosen_values = all_values[page_list]
    extra_len = chosen_keys.shape[1] * PAGE
    cache_slots = cache_k.shape[1]
    steps_count = decode_q.shape[1]
    keys_list = jnp.concatenate(
        [chosen_keys.reshape(requests_local, extra_len, kv_local, width), cache_k, decode_k], axis=1
    )
    values_list = jnp.concatenate(
        [chosen_values.reshape(requests_local, extra_len, kv_local, width), cache_v, decode_v],
        axis=1,
    )
    total = keys_list.shape[1]
    position = jnp.arange(total)
    in_cache = (position >= extra_len) & (position < extra_len + cache_slots)
    cache_ok = (position - extra_len)[None, :] < cache_len[:, None]
    new_pos = position - extra_len - cache_slots
    causal = new_pos[None, :] <= jnp.arange(steps_count)[:, None]
    allowed = jnp.where(
        in_cache[None, None, :],
        cache_ok[:, None, :],
        jnp.where(new_pos[None, None, :] >= 0, causal[None], True),
    )
    queries = decode_q.reshape(requests_local, steps_count, kv_local, group, width)
    scores = (
        jnp.einsum("rtkgd,rnkd->rkgtn", queries, keys_list, preferred_element_type=jnp.float32)
        * inverse_root
    )
    scores = jnp.where(allowed[:, None, None], scores, -1e30)
    peak = jnp.max(scores, axis=-1, keepdims=True)
    weights = jnp.where(allowed[:, None, None], jnp.exp(scores - peak), 0.0)
    denominator = jnp.sum(weights, axis=-1)
    summed = jnp.einsum(
        "rkgtn,rnkd->rtkgd",
        weights.astype(jnp.bfloat16),
        values_list,
        preferred_element_type=jnp.float32,
    )
    merged = summed / denominator.transpose(0, 3, 1, 2)[..., None]
    merged = merged.reshape(requests_local, steps_count, q_heads * width).astype(jnp.bfloat16)
    decode_out = lax.all_to_all(merged, "tp", split_axis=0, concat_axis=2, tiled=True)
    return (prefill_out, decode_out)


def solution(mesh):
    return jax.shard_map(
        shards,
        mesh=mesh,
        in_specs=(
            P("role", "ctx", "tp", None),
            P("role", "ctx", "tp", None),
            P("role", "ctx", "tp", None),
            P(("role", "ctx"), None, "tp", None),
            P(("role", "ctx"), None, "tp", None),
            P(("role", "ctx"), None, "tp", None),
            P(("role", "ctx"), None, "tp", None),
            P(("role", "ctx"), None, "tp", None),
            P(("role", "ctx")),
            P(("role", "ctx"), None),
        ),
        out_specs=(P("role", "ctx", "tp", None), P(("role", "ctx", "tp"), None, None)),
        check_vma=False,
    )
```

profile of v0, /device:TPU:24, one launch (start us, length us, event | category | flops | bytes accessed | tf_op | source)
XLA Modules:
  0.0 267.9 jit_solution(4435576648460572812)
XLA Ops:
  7.2 1.8 copy.82
  9.1 1.7 copy.84
  10.9 1.7 copy.96
  12.6 1.7 copy.89
  14.4 0.7 compare_select_fusion
  15.4 5.5 %copy.99 = bf16[32,128,4,128]{3,1,2,0:T(8,128)(2,1)} copy(bf16[32,128,4,128]{3,2,1,0:T(4,128)(2,1)} %param.18) | data formatting | bytes 8388608 | tf_op args[6]
  20.8 0.7 copy.100
  21.6 3.2 %copy.93 = bf16[32,128,4,128]{3,1,2,0:T(8,128)(2,1)} copy(bf16[32,128,4,128]{3,2,1,0:T(4,128)(2,1)S(1)} %copy-done.3) | data formatting | bytes 8388608 | tf_op args[7]
  24.8 0.8 copy.83
  25.9 11.8 %all-gather.5.cloned.1.call-done = bf16[1,1024,4,128]{3,1,2,0:T(8,128)(2,1)} async-done(((bf16[1,256,4,128]{3,1,2,0:T(8,128)(2,1)}), bf16[1,1024,4,128]{3,1,2,0:T(8,128)(2,1)}) %all-gather.5.cloned.1.call-update) | async-done | bytes 1048592 | tf_op jit(solution)/shard_map/all_gather | solution.py:62
  37.7 29.6 %all-gather.7.cloned.1.call-done = bf16[1,1024,4,128]{3,1,2,0:T(8,128)(2,1)} async-done(((bf16[1,256,4,128]{3,1,2,0:T(8,128)(2,1)}), bf16[1,1024,4,128]{3,1,2,0:T(8,128)(2,1)}) %all-gather.7.cloned.1.call-update) | async-done | bytes 1048592 | tf_op jit(solution)/shard_map/all_gather | solution.py:63
  67.3 78.0 %while.15 = (s32[]{:T(128)}, f32[4,8,256]{2,1,0:T(8,128)S(1)}, f32[4,8,256]{2,1,0:T(8,128)S(1)}, f32[4,8,256,128]{3,2,1,0:T(8,128)}, s32[4]{0:T(128)S(1)}, /*ind...) while((s32[]{:T(128)}, f32[4,8,256]{2,1,0:T(8,128)S(1)}, ...), condition=%wide.region_3.4_spmd.clone, body=%wide.region_0.3_spmd.clone.sunk | while | flops 1104257536 | bytes 70522024 | solution.py:68
  67.9 0.6 iota_add_fusion.5
  68.6 5.5 %fusion.69 = (f32[4,8,256]{2,1,0:T(8,128)S(1)}, f32[4,256,8,256]{3,1,2,0:T(8,128)}) fusion(pred[256,256]{0,1:T(8,128)(4,1)S(1)} %broadcast_compare_fusion.4, bf16[4,8,256,128]{3,2,1,0:T(8,128)(2,1)S(1)} %get-tuple-element.250, bf16[4,256,4,128]{3,1,0,2:T(8,128)(2,1)} %get-tuple-element.249, s32[]{:T(128)} %get-tuple-element.233), kind=kOutput, calls=%fused_computation.5.clone.1 | convolution fusion | flops 543154176 | bytes 10846720 | tf_op jit(solution)/shard_map/while/body/eval_jaxpr/kgqd,pkd->kgqp/dot_general | solution.py:38
  74.2 4.6 %fusion.70 = f32[4,8,256]{2,1,0:T(8,128)S(1)} fusion(f32[4,256,8,256]{3,1,2,0:T(8,128)} %get-tuple-element.219, f32[4,8,256]{2,1,0:T(8,128)S(1)} %select_maximum_fusion.2, pred[256,256]{0,1:T(8,128)(4,1)S(1)} %broadcast_compare_fusion.4), kind=kLoop, calls=%fused_computation.7.clone.1 | loop fusion | flops 10477568 | bytes 8519680 | tf_op jit(solution)/shard_map/while/body/eval_jaxpr/reduce_sum | solution.py:46
  78.9 1.4 copy-done.2
  80.3 5.8 %fusion.72 = f32[4,8,256,128]{3,2,1,0:T(8,128)} fusion(f32[4,8,256,128]{3,2,1,0:T(8,128)} %get-tuple-element.236, f32[4,8,256]{2,1,0:T(8,128)S(1)} %get-tuple-element.221, pred[]{:T(512)S(6)} %compare.3, f32[4,256,8,256]{3,1,2,0:T(8,128)S(1)} %copy-done.2, f32[4,8,256]{2,1,0:T(8,128)S(1)} %select_maximum_fusion.2, ...), kind=kOutput, calls=%fused_computation.10.clone.1 | convolution fusion | flops 550502400 | bytes 17170944 | tf_op jit(solution)/shard_map/while/body/eval_jaxpr/kgqp,pkd->kgqd/dot_general | solution.py:47
  86.6 0.6 iota_add_fusion.5
  87.4 5.5 %fusion.69 = (f32[4,8,256]{2,1,0:T(8,128)S(1)}, f32[4,256,8,256]{3,1,2,0:T(8,128)}) fusion(pred[256,256]{0,1:T(8,128)(4,1)S(1)} %broadcast_compare_fusion.4, bf16[4,8,256,128]{3,2,1,0:T(8,128)(2,1)S(1)} %get-tuple-element.250, bf16[4,256,4,128]{3,1,0,2:T(8,128)(2,1)} %get-tuple-element.249, s32[]{:T(128)} %get-tuple-element.233), kind=kOutput, calls=%fused_computation.5.clone.1 | convolution fusion | flops 543154176 | bytes 10846720 | tf_op jit(solution)/shard_map/while/body/eval_jaxpr/kgqd,pkd->kgqp/dot_general | solution.py:38
  92.9 4.6 %fusion.70 = f32[4,8,256]{2,1,0:T(8,128)S(1)} fusion(f32[4,256,8,256]{3,1,2,0:T(8,128)} %get-tuple-element.219, f32[4,8,256]{2,1,0:T(8,128)S(1)} %select_maximum_fusion.2, pred[256,256]{0,1:T(8,128)(4,1)S(1)} %broadcast_compare_fusion.4), kind=kLoop, calls=%fused_computation.7.clone.1 | loop fusion | flops 10477568 | bytes 8519680 | tf_op jit(solution)/shard_map/while/body/eval_jaxpr/reduce_sum | solution.py:46
  97.6 1.7 copy-done.2
  99.3 6.8 %fusion.72 = f32[4,8,256,128]{3,2,1,0:T(8,128)} fusion(f32[4,8,256,128]{3,2,1,0:T(8,128)} %get-tuple-element.236, f32[4,8,256]{2,1,0:T(8,128)S(1)} %get-tuple-element.221, pred[]{:T(512)S(6)} %compare.3, f32[4,256,8,256]{3,1,2,0:T(8,128)S(1)} %copy-done.2, f32[4,8,256]{2,1,0:T(8,128)S(1)} %select_maximum_fusion.2, ...), kind=kOutput, calls=%fused_computation.10.clone.1 | convolution fusion | flops 550502400 | bytes 17170944 | tf_op jit(solution)/shard_map/while/body/eval_jaxpr/kgqp,pkd->kgqd/dot_general | solution.py:47
  106.6 0.6 iota_add_fusion.5
  107.4 5.5 %fusion.69 = (f32[4,8,256]{2,1,0:T(8,128)S(1)}, f32[4,256,8,256]{3,1,2,0:T(8,128)}) fusion(pred[256,256]{0,1:T(8,128)(4,1)S(1)} %broadcast_compare_fusion.4, bf16[4,8,256,128]{3,2,1,0:T(8,128)(2,1)S(1)} %get-tuple-element.250, bf16[4,256,4,128]{3,1,0,2:T(8,128)(2,1)} %get-tuple-element.249, s32[]{:T(128)} %get-tuple-element.233), kind=kOutput, calls=%fused_computation.5.clone.1 | convolution fusion | flops 543154176 | bytes 10846720 | tf_op jit(solution)/shard_map/while/body/eval_jaxpr/kgqd,pkd->kgqp/dot_general | solution.py:38
  112.9 4.7 %fusion.70 = f32[4,8,256]{2,1,0:T(8,128)S(1)} fusion(f32[4,256,8,256]{3,1,2,0:T(8,128)} %get-tuple-element.219, f32[4,8,256]{2,1,0:T(8,128)S(1)} %select_maximum_fusion.2, pred[256,256]{0,1:T(8,128)(4,1)S(1)} %broadcast_compare_fusion.4), kind=kLoop, calls=%fused_computation.7.clone.1 | loop fusion | flops 10477568 | bytes 8519680 | tf_op jit(solution)/shard_map/while/body/eval_jaxpr/reduce_sum | solution.py:46
  117.7 1.3 copy-done.2
  119.0 6.8 %fusion.72 = f32[4,8,256,128]{3,2,1,0:T(8,128)} fusion(f32[4,8,256,128]{3,2,1,0:T(8,128)} %get-tuple-element.236, f32[4,8,256]{2,1,0:T(8,128)S(1)} %get-tuple-element.221, pred[]{:T(512)S(6)} %compare.3, f32[4,256,8,256]{3,1,2,0:T(8,128)S(1)} %copy-done.2, f32[4,8,256]{2,1,0:T(8,128)S(1)} %select_maximum_fusion.2, ...), kind=kOutput, calls=%fused_computation.10.clone.1 | convolution fusion | flops 550502400 | bytes 17170944 | tf_op jit(solution)/shard_map/while/body/eval_jaxpr/kgqp,pkd->kgqd/dot_general | solution.py:47
  125.7 0.6 dynamic_slice.29
  126.3 0.6 iota_add_fusion.5
  127.1 5.5 %fusion.69 = (f32[4,8,256]{2,1,0:T(8,128)S(1)}, f32[4,256,8,256]{3,1,2,0:T(8,128)}) fusion(pred[256,256]{0,1:T(8,128)(4,1)S(1)} %broadcast_compare_fusion.4, bf16[4,8,256,128]{3,2,1,0:T(8,128)(2,1)S(1)} %get-tuple-element.250, bf16[4,256,4,128]{3,1,0,2:T(8,128)(2,1)} %get-tuple-element.249, s32[]{:T(128)} %get-tuple-element.233), kind=kOutput, calls=%fused_computation.5.clone.1 | convolution fusion | flops 543154176 | bytes 10846720 | tf_op jit(solution)/shard_map/while/body/eval_jaxpr/kgqd,pkd->kgqp/dot_general | solution.py:38
  132.6 4.7 %fusion.70 = f32[4,8,256]{2,1,0:T(8,128)S(1)} fusion(f32[4,256,8,256]{3,1,2,0:T(8,128)} %get-tuple-element.219, f32[4,8,256]{2,1,0:T(8,128)S(1)} %select_maximum_fusion.2, pred[256,256]{0,1:T(8,128)(4,1)S(1)} %broadcast_compare_fusion.4), kind=kLoop, calls=%fused_computation.7.clone.1 | loop fusion | flops 10477568 | bytes 8519680 | tf_op jit(solution)/shard_map/while/body/eval_jaxpr/reduce_sum | solution.py:46
  137.3 1.2 copy-done.2
  138.5 6.8 %fusion.72 = f32[4,8,256,128]{3,2,1,0:T(8,128)} fusion(f32[4,8,256,128]{3,2,1,0:T(8,128)} %get-tuple-element.236, f32[4,8,256]{2,1,0:T(8,128)S(1)} %get-tuple-element.221, pred[]{:T(512)S(6)} %compare.3, f32[4,256,8,256]{3,1,2,0:T(8,128)S(1)} %copy-done.2, f32[4,8,256]{2,1,0:T(8,128)S(1)} %select_maximum_fusion.2, ...), kind=kOutput, calls=%fused_computation.10.clone.1 | convolution fusion | flops 550502400 | bytes 17170944 | tf_op jit(solution)/shard_map/while/body/eval_jaxpr/kgqp,pkd->kgqd/dot_general | solution.py:47
  145.2 10.5 %gather_fusion.1 = bf16[128,128,4,128]{3,1,2,0:T(8,128)(2,1)} fusion(bf16[32,128,4,128]{3,1,2,0:T(8,128)(2,1)} %all-gather.11.cloned.1.call-done, s32[1024]{0:T(1024)S(1)} %pad_clamp_fusion), kind=kCustom, calls=%fused_computation.1 | custom fusion | bytes 33554944 | tf_op jit(solution)/shard_map/gather | solution.py:84
  155.7 14.2 %copy.97 = bf16[128,128,4,128]{3,1,0,2:T(8,128)(2,1)} copy(bf16[128,128,4,128]{3,1,2,0:T(8,128)(2,1)} %gather_fusion.1) | data formatting | bytes 33554432 | tf_op jit(solution)/shard_map/gather | solution.py:84
  170.0 0.8 all-gather.9.cloned.1.call-done
  170.8 10.6 %gather_fusion = bf16[128,128,4,128]{3,1,2,0:T(8,128)(2,1)} fusion(bf16[32,128,4,128]{3,1,2,0:T(8,128)(2,1)} %all-gather.9.cloned.1.call-done, s32[1024]{0:T(1024)S(1)} %pad_clamp_fusion), kind=kCustom, calls=%fused_computation | custom fusion | bytes 33554944 | tf_op jit(solution)/shard_map/gather | solution.py:85
  181.4 14.2 %copy.91 = bf16[128,128,4,128]{3,1,0,2:T(8,128)(2,1)} copy(bf16[128,128,4,128]{3,1,2,0:T(8,128)(2,1)} %gather_fusion) | data formatting | bytes 33554432 | tf_op jit(solution)/shard_map/gather | solution.py:85
  195.6 16.5 %fusion.32 = f32[32,4,644,4,8]{2,4,3,1,0:T(8,128)} fusion(bf16[32,4,4,128]{3,1,2,0:T(4,128)(2,1)S(1)} %copy-done.7, bf16[32,128,4,128]{3,1,2,0:T(8,128)(2,1)} %copy.99, bf16[32,512,4,128]{3,1,0,2:T(8,128)(2,1)} %bitcast.101, bf16[32,4,32,128]{3,2,1,0:T(8,128)(2,1)S(1)} %copy-done), kind=kOutput, calls=%fused_computation.41 | convolution fusion | flops 738590720 | bytes 32702464 | tf_op jit(solution)/shard_map/rtkgd,rnkd->rkgtn/dot_general | solution.py:109
  212.0 16.1 %fusion.53 = (f32[32,4,8,4]{2,3,1,0:T(4,128)S(1)}, bf16[32,4,8,4,644]{4,2,3,1,0:T(8,128)(2,1)}) fusion(f32[32,4,644,4,8]{2,4,3,1,0:T(8,128)} %fusion.32, pred[32,4,644]{2,1,0:T(4,128)(4,1)S(1)} %broadcast_select_fusion), kind=kOutput, calls=%fused_computation.76 | output fusion | flops 21103236 | bytes 15925760 | tf_op jit(solution)/shard_map/sub | solution.py:114
  228.1 10.9 %fusion.42 = bf16[32,4,4,8,128]{4,3,1,2,0:T(8,128)(2,1)S(1)} fusion(bf16[32,4,8,4,644]{4,2,3,1,0:T(8,128)(2,1)} %get-tuple-element.152, bf16[32,4,4,128]{3,1,2,0:T(4,128)(2,1)S(1)} %copy.94, bf16[32,128,4,128]{3,1,2,0:T(8,128)(2,1)} %copy.93, f32[32,4,4,8]{3,1,2,0:T(4,128)S(1)} %bitcast.108, bf16[32,512,4,128]{3,1,0,2:T(8,128)(2,1)} %bitcast.100), kind=kOutput, calls=%fused_computation.55 | convolution fusion | flops 739639296 | bytes 27443200 | tf_op jit(solution)/shard_map/rkgtn,rnkd->rtkgd/dot_general | solution.py:116
  239.2 1.1 reshape.151
  240.3 3.6 %all-to-all-start = ((bf16[32,4,4096]{2,1,0:T(4,128)(2,1)}), bf16[32,4,4096]{2,1,0:T(4,128)(2,1)S(1)}, u32[]{:S(2)}, u32[]{:S(2)}) async-start(bf16[32,4,4096]{2,1,0:T(4,128)(2,1)} %reshape.151), calls=%async_computation | async-start | bytes 2097152 | tf_op jit(solution)/shard_map/all_to_all | solution.py:124
  243.9 2.9 %fusion.43 = bf16[256,4,8,128]{3,0,2,1:T(8,128)(2,1)S(1)} fusion(f32[4,8,256,128]{3,2,1,0:T(8,128)} %get-tuple-element.50, f32[4,8,256]{2,1,0:T(8,128)S(1)} %get-tuple-element.51), kind=kLoop, calls=%fused_computation.57 | loop fusion | flops 2097152 | bytes 6324224 | tf_op jit(solution)/shard_map/convert_element_type | solution.py:74
  246.8 2.7 copy.131
  249.5 8.7 %all-to-all-done = bf16[32,4,4096]{2,1,0:T(4,128)(2,1)S(1)} async-done(((bf16[32,4,4096]{2,1,0:T(4,128)(2,1)}), bf16[32,4,4096]{2,1,0:T(4,128)(2,1)S(1)}, u32[]{:S(2)}, u32[]{:S(2)}) %all-to-all-start) | async-done | bytes 1048608 | tf_op jit(solution)/shard_map/all_to_all | solution.py:124
  258.7 1.1 copy.117
  259.8 1.5 reshape.152
  (65 shorter events, 3.8 us)
Async XLA Ops:
  7.2 188.4 %copy-start = (bf16[32,4,32,128]{3,2,1,0:T(8,128)(2,1)S(1)}, bf16[32,4,32,128]{3,2,1,0:T(8,128)(2,1)}, u32[]{:S(2)}) copy-start(bf16[32,4,32,128]{3,2,1,0:T(8,128)(2,1)} %param.15) | copy-start | bytes 3145732
  7.2 13.7 %copy-start.5 = (bf16[32,4,4,128]{3,2,1,0:T(4,128)(2,1)S(1)}, bf16[32,4,4,128]{3,2,1,0:T(4,128)(2,1)}, u32[]{:S(2)}) copy-start(bf16[32,4,4,128]{3,2,1,0:T(4,128)(2,1)} %param.16) | copy-start | bytes 393220
  7.2 30.5 %all-gather.5.cloned.1.call-start = ((), (), s32[]{:S(2)}) async-start(), calls=%async_computation.1 | async-start | bytes 1310720 | tf_op jit(solution)/shard_map/all_gather | solution.py:62
  9.0 58.2 %all-gather.7.cloned.1.call-start = ((), (), s32[]{:S(2)}) async-start(), calls=%async_computation.2 | async-start | bytes 1310720 | tf_op jit(solution)/shard_map/all_gather | solution.py:63
  10.8 134.4 %all-gather.11.cloned.1.call-start = ((), (), s32[]{:S(2)}) async-start(), calls=%async_computation.4 | async-start | bytes 4456448 | tf_op jit(solution)/shard_map/all_gather | solution.py:81
  12.6 158.3 %all-gather.9.cloned.1.call-start = ((), (), s32[]{:S(2)}) async-start(), calls=%async_computation.3 | async-start | bytes 4456448 | tf_op jit(solution)/shard_map/all_gather | solution.py:82
  15.3 6.3 %copy-start.3 = (bf16[32,128,4,128]{3,2,1,0:T(4,128)(2,1)S(1)}, bf16[32,128,4,128]{3,2,1,0:T(4,128)(2,1)}, u32[]{:S(2)}) copy-start(bf16[32,128,4,128]{3,2,1,0:T(4,128)(2,1)} %param.19) | copy-start | bytes 12582916
  15.3 9.4 %copy-start.6 = (bf16[32,4,4,128]{3,2,1,0:T(4,128)(2,1)S(1)}, bf16[32,4,4,128]{3,2,1,0:T(4,128)(2,1)}, u32[]{:S(2)}) copy-start(bf16[32,4,4,128]{3,2,1,0:T(4,128)(2,1)} %param.17) | copy-start | bytes 393220
  15.3 9.5 %copy-start.4 = (bf16[1,256,32,128]{3,2,1,0:T(8,128)(2,1)S(1)}, bf16[1,256,32,128]{3,2,1,0:T(8,128)(2,1)}, u32[]{:S(2)}) copy-start(bf16[1,256,32,128]{3,2,1,0:T(8,128)(2,1)} %param.12) | copy-start | bytes 6291460
  20.8 4.8 %copy-start.8 = (s32[32]{0:T(128)S(1)}, s32[32]{0:T(128)}, u32[]{:S(2)}) copy-start(s32[32]{0:T(128)} %param.20) | copy-start | bytes 388
  74.2 6.1 %copy-start.2 = (f32[4,256,8,256]{3,1,2,0:T(8,128)S(1)}, f32[4,256,8,256]{3,1,2,0:T(8,128)}, u32[]{:S(2)}) copy-start(f32[4,256,8,256]{3,1,2,0:T(8,128)} %get-tuple-element.219) | copy-start | bytes 25165828 | tf_op jit(solution)/shard_map/while
  92.9 6.4 %copy-start.2 = (f32[4,256,8,256]{3,1,2,0:T(8,128)S(1)}, f32[4,256,8,256]{3,1,2,0:T(8,128)}, u32[]{:S(2)}) copy-start(f32[4,256,8,256]{3,1,2,0:T(8,128)} %get-tuple-element.219) | copy-start | bytes 25165828 | tf_op jit(solution)/shard_map/while
  112.9 6.0 %copy-start.2 = (f32[4,256,8,256]{3,1,2,0:T(8,128)S(1)}, f32[4,256,8,256]{3,1,2,0:T(8,128)}, u32[]{:S(2)}) copy-start(f32[4,256,8,256]{3,1,2,0:T(8,128)} %get-tuple-element.219) | copy-start | bytes 25165828 | tf_op jit(solution)/shard_map/while
  132.6 5.9 %copy-start.2 = (f32[4,256,8,256]{3,1,2,0:T(8,128)S(1)}, f32[4,256,8,256]{3,1,2,0:T(8,128)}, u32[]{:S(2)}) copy-start(f32[4,256,8,256]{3,1,2,0:T(8,128)} %get-tuple-element.219) | copy-start | bytes 25165828 | tf_op jit(solution)/shard_map/while
  181.4 14.2 %copy-start.7 = (bf16[32,4,4,128]{3,1,2,0:T(4,128)(2,1)S(1)}, bf16[32,4,4,128]{3,1,2,0:T(4,128)(2,1)}, u32[]{:S(2)}) copy-start(bf16[32,4,4,128]{3,1,2,0:T(4,128)(2,1)} %copy.100) | copy-start | bytes 393220
  240.3 17.9 %all-to-all-start = ((bf16[32,4,4096]{2,1,0:T(4,128)(2,1)}), bf16[32,4,4096]{2,1,0:T(4,128)(2,1)S(1)}, u32[]{:S(2)}, u32[]{:S(2)}) async-start(bf16[32,4,4096]{2,1,0:T(4,128)(2,1)} %reshape.151), calls=%async_computation | async-start | bytes 2097152 | tf_op jit(solution)/shard_map/all_to_all | solution.py:124
  243.9 17.5 %copy-start.1 = (bf16[32,4,32,128]{3,2,1,0:T(8,128)(2,1)S(1)}, bf16[32,4,32,128]{3,2,1,0:T(8,128)(2,1)}, u32[]{:S(2)}) copy-start(bf16[32,4,32,128]{3,2,1,0:T(8,128)(2,1)} %param.15) | copy-start | bytes 3145732
Sparse Core Ops, SparseCore 0:
  10.2 27.4 all-gather.4
  39.8 27.4 all-gather.6
  69.5 49.9 all-gather.10
  121.6 49.2 all-gather.8
where the time goes:
time: 272 us; the launch traced here: 268 us
  local copies, waits for them, and re-layouts  81.8 us (30%)
  matrix products  75.5 us (28%)
  waiting for transfers between devices  51 us (19%)
  other arithmetic  41.7 us (15%)
  between operations  14 us (5%)
  starting transfers between devices  3.74 us (1%)
    all_gather x1, waiting for transfers between devices, shards(): values_all = lax.all_gather(prefill_v, 'ctx', axis=1, tiled=True)  29.6 us
    dot_general x4, matrix products, attend_block(): jnp.einsum('kgqp,pkd->kgqd', weights.astype(jnp.bfloat16), values_block,...  26 us
    gather x2, local copies, waits for them, and re-layouts, shards(): chosen_keys = all_keys[page_list]  24.7 us
    gather x2, local copies, waits for them, and re-layouts, shards(): chosen_values = all_values[page_list]  24.7 us
    dot_general x4, matrix products, attend_block(): jnp.einsum('kgqd,pkd->kgqp', grouped, keys_block, preferred_element_type=...  22.1 us
    reduce_sum x4, other arithmetic, attend_block(): running_sum = running_sum * shrink + jnp.sum(weights, axis=-1)  18.7 us
    dot_general x1, matrix products, shards(): jnp.einsum('rtkgd,rnkd->rkgtn', queries, keys_list, preferred_element_typ...  16.5 us
    unnamed x25, local copies, waits for them, and re-layouts  16.4 us
  transfers between devices with their start and end apart: 5, of which 4 were waited for; matrix products, arithmetic and copies ran while one was open for 44% of the time, Pallas kernels for 0%

commit v1 on v0

v1 whole, which is shorter than its diff:
```python
import functools
import math

import jax
import jax.numpy as jnp
from jax import lax
from jax.experimental import pallas as pl
from jax.experimental.pallas import tpu as pltpu
from jax.sharding import PartitionSpec as P

PAGE = 128
CHUNKS = 2
LOG2E = 1.4426950408889634
NEG = -1e30
VMEM_LIMIT = 48 * 1024 * 1024


def nt(a, b):
    return lax.dot_general(a, b, (((1,), (1,)), ((), ())), preferred_element_type=jnp.float32)


def nn(a, b):
    return jnp.dot(a, b, preferred_element_type=jnp.float32)


def params():
    return pltpu.CompilerParams(vmem_limit_bytes=VMEM_LIMIT)


def one_hot(out_rows, in_rows, source):
    row = lax.broadcasted_iota(jnp.int32, (out_rows, in_rows), 0)
    col = lax.broadcasted_iota(jnp.int32, (out_rows, in_rows), 1)
    return jnp.where(col == source(row), 1.0, 0.0).astype(jnp.bfloat16)


def split_kernel(heads, per_chunk, tokens, k_ref, v_ref, *outs):
    rows = min(tokens * heads, 256)
    step = rows // heads
    pick = one_hot(rows, rows, lambda i: (i % step) * heads + i // step)
    for which, ref in enumerate((k_ref, v_ref)):
        for j in range(tokens // step):
            moved = nn(pick, ref[pl.ds(j * rows, rows), :]).astype(jnp.bfloat16)
            for h in range(heads):
                outs[h // per_chunk][h % per_chunk, which, pl.ds(j * step, step), :] = moved[
                    h * step : (h + 1) * step
                ]


def split_heads(k, v, chunks):
    _, tokens, heads, width = k.shape
    per_chunk = heads // chunks
    shape = jax.ShapeDtypeStruct((per_chunk, 2, tokens, width), jnp.bfloat16)
    return pl.pallas_call(
        functools.partial(split_kernel, heads, per_chunk, tokens),
        out_shape=[shape] * chunks,
        compiler_params=params(),
        cost_estimate=pl.CostEstimate(flops=10**8, bytes_accessed=2 * 10**6, transcendentals=0),
    )(k.reshape(tokens * heads, width), v.reshape(tokens * heads, width))


def stage_kernel(heads, per_chunk, group, steps, cache, q_ref, dk_ref, dv_ref, ck_ref, cv_ref, *outs):
    chunks = heads // per_chunk
    rows = min(cache * heads, 256)
    step = rows // heads
    pick = one_hot(rows, rows, lambda i: (i % step) * heads + i // step)
    extra = one_hot(
        heads * 16,
        steps * heads,
        lambda i: jnp.where(i % 16 < steps, (i % 16) * heads + i // 16, -1),
    )
    each = group * steps
    q_rows = heads * each
    q_pick = one_hot(
        q_rows,
        q_rows,
        lambda i: (i % steps) * (heads * group) + (i // each) * group + (i % each) // steps,
    )
    for r in range(q_ref.shape[0]):
        moved = nn(q_pick, q_ref[r]).astype(jnp.bfloat16)
        for h in range(heads):
            outs[h // per_chunk][h % per_chunk, r] = moved[h * each : (h + 1) * each]
        for which, (old, new) in enumerate(((ck_ref, dk_ref), (cv_ref, dv_ref))):
            base = (1 + which) * chunks
            for j in range(cache // step):
                moved = nn(pick, old[r, pl.ds(j * rows, rows), :]).astype(jnp.bfloat16)
                for h in range(heads):
                    outs[base + h // per_chunk][h % per_chunk, r, pl.ds(j * step, step), :] = moved[
                        h * step : (h + 1) * step
                    ]
            moved = nn(extra, new[r]).astype(jnp.bfloat16)
            for h in range(heads):
                outs[base + h // per_chunk][h % per_chunk, r, pl.ds(cache, 16), :] = moved[
                    h * 16 : (h + 1) * 16
                ]


def stage_decode(decode_q, decode_k, decode_v, cache_k, cache_v, chunks):
    requests, steps, q_heads, width = decode_q.shape
    heads = cache_k.shape[2]
    cache = cache_k.shape[1]
    group = q_heads // heads
    per_chunk = heads // chunks
    block = min(4, requests)
    q = decode_q.reshape(requests, steps * q_heads, width)
    dk = decode_k.reshape(requests, steps * heads, width)
    dv = decode_v.reshape(requests, steps * heads, width)
    ck = cache_k.reshape(requests, cache * heads, width)
    cv = cache_v.reshape(requests, cache * heads, width)
    in_specs = [
        pl.BlockSpec((block, a.shape[1], width), lambda i: (i, 0, 0)) for a in (q, dk, dv, ck, cv)
    ]
    out_specs, out_shape = [], []
    for length in (group * steps, cache + 16, cache + 16):
        for _ in range(chunks):
            out_specs.append(pl.BlockSpec((per_chunk, block, length, width), lambda i: (0, i, 0, 0)))
            out_shape.append(
                jax.ShapeDtypeStruct((per_chunk, requests, length, width), jnp.bfloat16)
            )
    outs = pl.pallas_call(
        functools.partial(stage_kernel, heads, per_chunk, group, steps, cache),
        grid=(requests // block,),
        in_specs=in_specs,
        out_specs=out_specs,
        out_shape=out_shape,
        compiler_params=params(),
        cost_estimate=pl.CostEstimate(flops=10**9, bytes_accessed=20 * 10**6, transcendentals=0),
    )(q, dk, dv, ck, cv)
    return [(outs[c], outs[chunks + c], outs[2 * chunks + c]) for c in range(chunks)]


def prefill_kernel(
    kinds, group, tokens, scale, earlier_ref, *refs
):
    parts, ring, per_chunk, aliased = kinds
    block = refs[0].shape[1]
    q_ref = refs[0]
    blocks = refs[1 : 1 + parts * ring]
    rest = refs[1 + parts * ring + (1 if aliased else 0) :]
    out_ref, buf, sems = rest
    i = pl.program_id(0)
    heads = parts * per_chunk

    def copies():
        found = []
        place = jnp.int32(0)
        for s in range(1, ring):
            for part in range(parts):
                found.append(
                    (
                        earlier_ref[s],
                        pltpu.make_async_copy(
                            blocks[part * ring + s], buf.at[place, part], sems.at[s, part]
                        ),
                    )
                )
            place = place + earlier_ref[s]
        return found

    @pl.when(i == 0)
    def _():
        for flag, copy in copies():
            @pl.when(flag == 1)
            def _():
                copy.start()
        for flag, copy in copies():
            @pl.when(flag == 1)
            def _():
                copy.wait()

    rows = block * group
    queries = q_ref[0].astype(jnp.float32)
    q = [
        queries[:, h * group : (h + 1) * group, :].reshape(rows, -1).astype(jnp.bfloat16)
        for h in range(heads)
    ]
    row_token = lax.broadcasted_iota(jnp.int32, (rows, tokens), 0) // group + i * block
    column = lax.broadcasted_iota(jnp.int32, (rows, tokens), 1)
    allowed = column <= row_token
    state = []
    for h in range(heads):
        own = blocks[(h // per_chunk) * ring]
        s = nt(q[h], own[h % per_chunk, 0])
        s = jnp.where(allowed, s, NEG)
        m = jnp.max(s, axis=1, keepdims=True)
        p = jnp.exp2((s - m) * scale)
        l = jnp.sum(p, axis=1, keepdims=True)
        acc = nn(p.astype(jnp.bfloat16), own[h % per_chunk, 1])
        state.append((m, l, acc))

    def step(b, state):
        out = []
        for h in range(heads):
            m, l, acc = state[h]
            s = nt(q[h], buf[b, h // per_chunk, h % per_chunk, 0])
            new = jnp.maximum(m, jnp.max(s, axis=1, keepdims=True))
            p = jnp.exp2((s - new) * scale)
            shrink = jnp.exp2((m - new) * scale)
            l = l * shrink + jnp.sum(p, axis=1, keepdims=True)
            acc = acc * shrink + nn(
                p.astype(jnp.bfloat16), buf[b, h // per_chunk, h % per_chunk, 1]
            )
            out.append((new, l, acc))
        return tuple(out)

    state = lax.fori_loop(0, earlier_ref[0], step, tuple(state))
    out = [(acc / l).reshape(block, group, -1) for _, l, acc in state]
    out_ref[0] = jnp.concatenate(out, axis=1).astype(out_ref.dtype)


def prefill(q, parts, earlier, column, previous):
    _, tokens, q_heads, width = q.shape
    ring = len(parts[0])
    per_chunk = parts[0][0].shape[0]
    heads = per_chunk * len(parts)
    group = 8
    block = 64
    q_spec = pl.BlockSpec((1, block, heads * group, width), lambda i, *_: (0, i, column, 0))
    own_spec = pl.BlockSpec(parts[0][0].shape, lambda i, *_: (0, 0, 0, 0))
    any_spec = pl.BlockSpec(memory_space=pl.ANY)
    in_specs = [q_spec]
    operands = [q]
    for part in parts:
        in_specs += [own_spec] + [any_spec] * (ring - 1)
        operands += part
    aliases = {}
    if previous is not None:
        aliases = {1 + len(operands): 0}
        operands.append(previous)
        in_specs.append(any_spec)
    full = q_heads * tokens * tokens * 4 * width * 2
    return pl.pallas_call(
        functools.partial(
            prefill_kernel,
            (len(parts), ring, per_chunk, previous is not None),
            group,
            tokens,
            LOG2E / math.sqrt(width),
        ),
        grid_spec=pltpu.PrefetchScalarGridSpec(
            num_scalar_prefetch=1,
            grid=(tokens // block,),
            in_specs=in_specs,
            out_specs=pl.BlockSpec((1, block, heads * group, width), lambda i, *_: (0, i, column, 0)),
            scratch_shapes=[
                pltpu.VMEM((max(ring - 1, 1), len(parts)) + parts[0][0].shape, jnp.bfloat16),
                pltpu.SemaphoreType.DMA((ring, len(parts))),
            ],
        ),
        out_shape=jax.ShapeDtypeStruct(q.shape, jnp.bfloat16),
        input_output_aliases=aliases,
        compiler_params=params(),
        cost_estimate=pl.CostEstimate(
            flops=full * heads * group // q_heads,
            bytes_accessed=4 * 10**6,
            transcendentals=tokens * heads * group * 1024,
        ),
    )(earlier, *operands)


def decode_kernel(slots, extra, steps, targets, per_block, scale, *refs):
    slot_ref, pick_ref, len_ref, meta_ref = refs[:4]
    q_ref, kc_ref, vc_ref = refs[4:7]
    blocks = refs[7 : 7 + slots]
    outs = refs[7 + slots : 7 + slots + targets]
    buf, sems = refs[7 + slots + targets :]
    i = pl.program_id(0)
    heads, block, q_rows, width = q_ref.shape
    first = ((i + meta_ref[1] * per_block) % (targets * per_block)) * block

    def copies():
        for s in range(slots):
            start = pl.multiple_of(pick_ref[s] * PAGE, PAGE)
            yield pltpu.make_async_copy(
                blocks[s].at[:, :, pl.ds(start, PAGE), :], buf.at[s], sems.at[s]
            )

    @pl.when(i == 0)
    def _():
        for copy in copies():
            copy.start()
        for copy in copies():
            copy.wait()

    length = kc_ref.shape[2]
    cache = length - 16
    column = lax.broadcasted_iota(jnp.int32, (q_rows, length), 1)
    t = lax.broadcasted_iota(jnp.int32, (q_rows, length), 0) % steps
    later = (column >= cache) & (column - cache <= t)

    def attend(r, target):
        request = first + r
        allowed = (column < len_ref[request]) | later
        places = [slot_ref[request * extra + j] for j in range(extra)]
        for h in range(heads):
            q = q_ref[h, r]
            old = jnp.where(allowed, nt(q, kc_ref[h, r]), NEG)
            pages = [nt(q, buf[place, h, 0]) for place in places]
            top = functools.reduce(jnp.maximum, pages)
            m = jnp.maximum(
                jnp.max(top, axis=1, keepdims=True), jnp.max(old, axis=1, keepdims=True)
            )
            p_old = jnp.exp2((old - m) * scale)
            p_pages = [jnp.exp2((s - m) * scale) for s in pages]
            total = jnp.sum(functools.reduce(jnp.add, p_pages), axis=1, keepdims=True)
            total = total + jnp.sum(p_old, axis=1, keepdims=True)
            acc = nn(p_old.astype(jnp.bfloat16), vc_ref[h, r])
            for p, place in zip(p_pages, places):
                acc = acc + nn(p.astype(jnp.bfloat16), buf[place, h, 1])
            target[r, pl.ds(h * q_rows, q_rows), :] = (acc / total).astype(jnp.bfloat16)

    for k in range(targets):
        @pl.when(i // per_block == k)
        def _():
            unroll = min(4, block)

            def body(g, carry):
                for u in range(unroll):
                    attend(g * unroll + u, outs[k])
                return carry

            lax.fori_loop(0, block // unroll, body, 0)


def decode(operands, blocks, scalars, steps, extra, targets):
    q, kc, vc = operands
    heads, requests, q_rows, width = q.shape
    per_target = requests // targets
    block = min(8, per_target)
    per_block = per_target // block
    slots = len(blocks)
    grid = targets * per_block

    def here(i, slot, pick, lens, meta):
        return (0, (i + meta[1] * per_block) % grid, 0, 0)

    in_specs = [pl.BlockSpec((heads, block) + a.shape[2:], here) for a in (q, kc, vc)]
    in_specs += [pl.BlockSpec(memory_space=pl.ANY)] * slots

    def out_index(k):
        return lambda i, *_: (jnp.clip(i - k * per_block, 0, per_block - 1), 0, 0)

    out_specs = [
        pl.BlockSpec((block, heads * q_rows, width), out_index(k)) for k in range(targets)
    ]
    shape = jax.ShapeDtypeStruct((per_target, heads * q_rows, width), jnp.bfloat16)
    keys = extra * PAGE + kc.shape[2]
    return pl.pallas_call(
        functools.partial(
            decode_kernel, slots, extra, steps, targets, per_block, LOG2E / math.sqrt(width)
        ),
        grid_spec=pltpu.PrefetchScalarGridSpec(
            num_scalar_prefetch=4,
            grid=(grid,),
            in_specs=in_specs,
            out_specs=out_specs,
            scratch_shapes=[
                pltpu.VMEM((slots, heads, 2, PAGE, width), jnp.bfloat16),
                pltpu.SemaphoreType.DMA((slots,)),
            ],
        ),
        out_shape=[shape] * targets,
        compiler_params=params(),
        cost_estimate=pl.CostEstimate(
            flops=requests * heads * q_rows * keys * width * 4 * 4,
            bytes_accessed=8 * 10**6,
            transcendentals=requests * heads * q_rows * keys,
        ),
    )(*scalars, q, kc, vc, *blocks)


def join_kernel(targets, chunks, steps, meta_ref, *refs):
    out_ref = refs[-1]
    k = pl.program_id(0)
    rows = refs[0].shape[1]
    each = rows // steps
    for s in range(targets):
        @pl.when(lax.rem(meta_ref[1] + (targets - s), targets) == k)
        def _():
            for c in range(chunks):
                source = refs[s * chunks + c]

                def body(r, carry):
                    value = source[r]
                    for g in range(each):
                        out_ref[r, :, (c * each + g) * 128 : (c * each + g + 1) * 128] = value[
                            g * steps : (g + 1) * steps
                        ]
                    return carry

                lax.fori_loop(0, out_ref.shape[0], body, 0)


def join(pieces, meta, steps, targets, chunks):
    per_target, rows, width = pieces[0].shape
    half = chunks * (rows // steps) * width
    spec = pl.BlockSpec((per_target, rows, width), lambda k, *_: (0, 0, 0))
    return pl.pallas_call(
        functools.partial(join_kernel, targets, chunks, steps),
        grid_spec=pltpu.PrefetchScalarGridSpec(
            num_scalar_prefetch=1,
            grid=(targets,),
            in_specs=[spec] * len(pieces),
            out_specs=pl.BlockSpec((per_target, steps, half), lambda k, *_: (0, 0, k)),
        ),
        out_shape=jax.ShapeDtypeStruct((per_target, steps, half * targets), jnp.bfloat16),
        compiler_params=params(),
        cost_estimate=pl.CostEstimate(flops=0, bytes_accessed=2 * 10**6, transcendentals=0),
    )(meta, *pieces)


def ring_place(index, size):
    return jnp.where(index % 2 == 0, index // 2, size - 1 - index // 2)


def shards(
    roles,
    ring,
    targets,
    prefill_q,
    prefill_k,
    prefill_v,
    decode_q,
    decode_k,
    decode_v,
    cache_k,
    cache_v,
    cache_len,
    page_list,
):
    tokens = prefill_q.shape[1]
    heads = prefill_k.shape[2]
    own_pages = tokens // PAGE
    requests, steps = decode_q.shape[:2]
    extra = page_list.shape[1]
    chunks = math.gcd(CHUNKS, heads)
    role = lax.axis_index("role")
    ctx = lax.axis_index("ctx")
    tp = lax.axis_index("tp")

    order = list(range(0, ring, 2)) + list(range(ring - 1, 0, -2))
    along = [(order[j], order[(j + 1) % ring]) for j in range(ring)]
    flips = [1 << b for b in reversed(range(roles.bit_length() - 1))]

    own = split_heads(prefill_k, prefill_v, chunks)
    gathered = []
    for c in range(chunks):
        line = [own[c]]
        for s in range(1, ring):
            line.append(lax.ppermute(line[-1], "ctx", along))
        by_role = {0: line}
        for flip in flips:
            pairs = [(j, j ^ flip) for j in range(roles)]
            for seen in list(by_role):
                by_role[seen ^ flip] = [lax.ppermute(a, "role", pairs) for a in by_role[seen]]
        gathered.append(by_role)

    owner = page_list // own_pages
    place = (ring_place(ctx, ring) - ring_place(owner % ring, ring)) % ring
    slot = ((owner // ring) ^ role) * ring + place
    hot = slot.reshape(-1, 1) == jnp.arange(roles * ring)[None, :]
    pick = jnp.max(jnp.where(hot, (page_list % own_pages).reshape(-1, 1), 0), axis=0)
    meta = jnp.stack([ctx, tp]).astype(jnp.int32)
    scalars = (
        slot.reshape(-1).astype(jnp.int32),
        pick.astype(jnp.int32),
        cache_len.astype(jnp.int32),
        meta,
    )
    position = jnp.arange(ring)
    before = [order[(order.index(0) - s) % ring] for s in range(ring)]
    del before
    where = ring_place(ctx, ring)
    source = (where - position) % ring
    source_ctx = jnp.where(source < (ring + 1) // 2, 2 * source, 2 * (ring - 1 - source) + 1)
    flags = (source_ctx < ctx).astype(jnp.int32)
    earlier = jnp.where(position == 0, jnp.sum(flags), flags).astype(jnp.int32)

    staged = stage_decode(decode_q, decode_k, decode_v, cache_k, cache_v, chunks)

    pieces = [[] for _ in range(targets)]
    prefill_out = None
    for c in range(chunks):
        prefill_out = prefill(prefill_q, [gathered[c][0]], earlier, c, prefill_out)
        blocks = [a for r in range(roles) for a in gathered[c][r]]
        outs = decode(staged[c], blocks, scalars, steps, extra, targets)
        for s in range(targets):
            if s == 0:
                pieces[0].append(outs[0])
            else:
                shift = [(j, (j + s) % targets) for j in range(targets)]
                pieces[s].append(lax.ppermute(outs[s], "tp", shift))
    decode_out = join(
        [a for piece in pieces for a in piece], meta, steps, targets, chunks
    )
    return (prefill_out, decode_out)


def solution(mesh):
    body = functools.partial(shards, mesh.shape["role"], mesh.shape["ctx"], mesh.shape["tp"])
    return jax.shard_map(
        body,
        mesh=mesh,
        in_specs=(
            P("role", "ctx", "tp", None),
            P("role", "ctx", "tp", None),
            P("role", "ctx", "tp", None),
            P(("role", "ctx"), None, "tp", None),
            P(("role", "ctx"), None, "tp", None),
            P(("role", "ctx"), None, "tp", None),
            P(("role", "ctx"), None, "tp", None),
            P(("role", "ctx"), None, "tp", None),
            P(("role", "ctx")),
            P(("role", "ctx"), None),
        ),
        out_specs=(P("role", "ctx", "tp", None), P(("role", "ctx", "tp"), None, None)),
        check_vma=False,
    )
```

time: 272 us -> 162 us (0.60); the launches traced: 268 us -> 161 us
  Pallas kernels: 0 us -> 99 us
  matrix products: 75.5 us -> 0 us
  local copies, waits for them, and re-layouts: 81.8 us -> 8.87 us
  other arithmetic: 41.7 us -> 2.34 us
  waiting for transfers between devices: 51 us -> 31.9 us
  starting transfers between devices: 3.74 us -> 18.2 us
  between operations: 14 us -> 0.81 us
    pallas_call x0 -> x7, Pallas kernels: none -> 99 us  [the longest x2 54.2 us: decode(): pl.pallas_call(functools.partial(decode_kernel, slots, extra, steps, targ...]
    dot_general x10 -> x0, matrix products: 75.5 us -> none  [the longest x4 26 us: attend_block(): jnp.einsum('kgqp,pkd->kgqd', weights.astype(jnp.bfloat16), values_block,...]
    gather x4 -> x0, local copies, waits for them, and re-layouts: 49.5 us -> none  [the longest x2 24.7 us: shards(): chosen_keys = all_keys[page_list]]
    all_gather x4 -> x0, waiting for transfers between devices: 42.2 us -> none  [the longest x1 29.6 us: shards(): values_all = lax.all_gather(prefill_v, 'ctx', axis=1, tiled=True)]
    ppermute x0 -> x32, waiting for transfers between devices: none -> 31.9 us  [the longest x6 20.4 us: shards(): line.append(lax.ppermute(line[-1], 'ctx', along))]
    ppermute x0 -> x32, starting transfers between devices: none -> 18.2 us  [the longest x24 11.8 us: shards(): lax.ppermute(a, 'role', pairs)]
    reduce_sum x4 -> x1, other arithmetic: 18.7 us -> 0.72 us  [shards(): earlier = jnp.where(position == 0, jnp.sum(flags), flags).astype(jnp.int32)]
    sub x3 -> x0, other arithmetic: 16.1 us -> none  [the longest x1 16.1 us: shards(): weights = jnp.where(allowed[:, None, None], jnp.exp(scores - peak), 0.0)]
  transfers between devices with their start and end apart: 5 -> 32, of which waited for: 4 -> 11; matrix products, arithmetic and copies ran while one was open for 44% -> 2% of each run, Pallas kernels for 0% -> 60%
where the time goes in v1:
time: 162 us; the launch traced here: 161 us
  Pallas kernels  99 us (61%)
  waiting for transfers between devices  31.9 us (20%)
  starting transfers between devices  18.2 us (11%)
  local copies, waits for them, and re-layouts  8.87 us (5%)
  other arithmetic  2.34 us (1%)
    pallas_call x2, Pallas kernels, decode(): pl.pallas_call(functools.partial(decode_kernel, slots, extra, steps, targ...  54.2 us
    pallas_call x2, Pallas kernels, prefill(): pl.pallas_call(functools.partial(prefill_kernel, (len(parts), ring, per_c...  31.2 us
    ppermute x6, waiting for transfers between devices, shards(): line.append(lax.ppermute(line[-1], 'ctx', along))  20.4 us
    ppermute x24, starting transfers between devices, shards(): lax.ppermute(a, 'role', pairs)  11.8 us
    ppermute x24, waiting for transfers between devices, shards(): lax.ppermute(a, 'role', pairs)  11.6 us
    pallas_call x1, Pallas kernels, stage_decode(): pl.pallas_call(functools.partial(stage_kernel, heads, per_chunk, group, s...  11.3 us
    unnamed x28, local copies, waits for them, and re-layouts  8.49 us
    ppermute x6, starting transfers between devices, shards(): line.append(lax.ppermute(line[-1], 'ctx', along))  4.24 us
  transfers between devices with their start and end apart: 32, of which 11 were waited for; matrix products, arithmetic and copies ran while one was open for 2% of the time, Pallas kernels for 60%

profile of v1, /device:TPU:24, one launch (start us, length us, event | category | flops | bytes accessed | tf_op | source)
XLA Modules:
  0.0 161.2 jit_solution(14870862376797119405)
XLA Ops:
  0.6 0.9 copy-done.1
  1.6 0.9 copy-done.2
  2.5 0.4 shard_map.113
  3.3 1.5 collective-permute-start.22
  4.8 0.5 collective-permute-start.3
  5.5 6.7 %collective-permute-done.refs_2_.refs_8_ = bf16[2,2,256,128]{3,2,1,0:T(8,128)(2,1)S(1)} collective-permute-done((bf16[2,2,256,128]{3,2,1,0:T(8,128)(2,1)S(1)}, bf16[2,2,256,128]{3,2,1,0:T(8,128)(2,1)S(1)}, u32[]{:S(2)}, u32[]{:S(2)}) %collective-permute-start) | collective-permute-done | bytes 262176 | tf_op jit(solution)/shard_map/ppermute | solution.py:449
  12.6 0.9 collective-permute-start.1
  13.4 1.5 collective-permute-start.23
  14.9 2.9 %collective-permute-done.3.refs_2_.refs_8_ = bf16[2,2,256,128]{3,2,1,0:T(8,128)(2,1)S(1)} collective-permute-done((bf16[2,2,256,128]{3,2,1,0:T(8,128)(2,1)S(1)}, bf16[2,2,256,128]{3,2,1,0:T(8,128)(2,1)S(1)}, u32[]{:S(2)}, u32[]{:S(2)}) %collective-permute-start.3) | collective-permute-done | bytes 262176 | tf_op jit(solution)/shard_map/ppermute | solution.py:449
  17.8 0.5 collective-permute-start.26
  18.3 0.5 collective-permute-start.4
  18.8 4.6 %collective-permute-done.1.refs_3_.refs_9_ = bf16[2,2,256,128]{3,2,1,0:T(8,128)(2,1)S(1)} collective-permute-done((bf16[2,2,256,128]{3,2,1,0:T(8,128)(2,1)S(1)}, bf16[2,2,256,128]{3,2,1,0:T(8,128)(2,1)S(1)}, u32[]{:S(2)}, u32[]{:S(2)}) %collective-permute-start.1) | collective-permute-done | bytes 262176 | tf_op jit(solution)/shard_map/ppermute | solution.py:449
  23.4 1.5 collective-permute-start.11
  25.0 0.7 copy-done.9
  25.6 0.5 collective-permute-start.14
  26.2 0.7 copy-done.11
  26.9 0.5 collective-permute-start.2
  27.3 0.6 collective-permute-done.4.refs_3_.refs_9_
  27.9 1.5 collective-permute-start.24
  29.4 0.5 collective-permute-done.11.refs_16_
  29.9 0.5 collective-permute-start.27
  30.4 0.7 copy-done.7
  31.1 1.6 collective-permute-start.5
  32.7 3.4 %collective-permute-done.2.refs_4_.refs_10_ = bf16[2,2,256,128]{3,2,1,0:T(8,128)(2,1)S(1)} collective-permute-done((bf16[2,2,256,128]{3,2,1,0:T(8,128)(2,1)S(1)}, bf16[2,2,256,128]{3,2,1,0:T(8,128)(2,1)S(1)}, u32[]{:S(2)}, u32[]{:S(2)}) %collective-permute-start.2) | collective-permute-done | bytes 262176 | tf_op jit(solution)/shard_map/ppermute | solution.py:449
  36.0 2.0 %collective-permute-start.12 = (bf16[2,2,256,128]{3,2,1,0:T(8,128)(2,1)S(1)}, bf16[2,2,256,128]{3,2,1,0:T(8,128)(2,1)}, u32[]{:S(2)}, u32[]{:S(2)}) collective-permute-start(bf16[2,2,256,128]{3,2,1,0:T(8,128)(2,1)S(1)} %collective-permute-done.4.refs_3_.refs_9_), channel_id=1, source_target_pairs={{0,16},{8,24},{16,0},{24,8},{1,17},{9,25},{17,1},{25,9},{2,18},{10... | collective-permute-start | bytes 786440 | tf_op jit(solution)/shard_map/ppermute | solution.py:454
  38.1 0.5 collective-permute-start.28
  38.6 2.2 %collective-permute-done.5.refs_4_.refs_10_ = bf16[2,2,256,128]{3,2,1,0:T(8,128)(2,1)} collective-permute-done((bf16[2,2,256,128]{3,2,1,0:T(8,128)(2,1)S(1)}, bf16[2,2,256,128]{3,2,1,0:T(8,128)(2,1)}, u32[]{:S(2)}, u32[]{:S(2)}) %collective-permute-start.5) | collective-permute-done | bytes 262176 | tf_op jit(solution)/shard_map/ppermute | solution.py:449
  40.8 0.5 collective-permute-start.13
  41.3 4.0 %collective-permute-done.25.refs_18_ = bf16[2,2,256,128]{3,2,1,0:T(8,128)(2,1)} collective-permute-done((bf16[2,2,256,128]{3,2,1,0:T(8,128)(2,1)S(1)}, bf16[2,2,256,128]{3,2,1,0:T(8,128)(2,1)}, u32[]{:S(2)}, u32[]{:S(2)}) %collective-permute-start.25) | collective-permute-done | bytes 262176 | tf_op jit(solution)/shard_map/ppermute | solution.py:454
  45.4 0.7 add_select_fusion
  46.7 4.3 %collective-permute-done.12.refs_17_ = bf16[2,2,256,128]{3,2,1,0:T(8,128)(2,1)} collective-permute-done((bf16[2,2,256,128]{3,2,1,0:T(8,128)(2,1)S(1)}, bf16[2,2,256,128]{3,2,1,0:T(8,128)(2,1)}, u32[]{:S(2)}, u32[]{:S(2)}) %collective-permute-start.12) | collective-permute-done | bytes 262176 | tf_op jit(solution)/shard_map/ppermute | solution.py:454
  51.0 0.5 collective-permute-start.15
  51.6 2.3 %collective-permute-done.13.refs_18_ = bf16[2,2,256,128]{3,2,1,0:T(8,128)(2,1)} collective-permute-done((bf16[2,2,256,128]{3,2,1,0:T(8,128)(2,1)}, bf16[2,2,256,128]{3,2,1,0:T(8,128)(2,1)}, u32[]{:S(2)}, u32[]{:S(2)}) %collective-permute-start.13) | collective-permute-done | bytes 262176 | tf_op jit(solution)/shard_map/ppermute | solution.py:454
  53.9 0.5 collective-permute-start.17
  54.4 1.2 copy-done
  55.6 0.9 copy-done.3
  56.5 0.9 copy-done.4
  57.5 11.3 %shard_map.116 = (bf16[2,32,32,128]{3,2,1,0:T(8,128)(2,1)S(1)}, bf16[2,32,32,128]{3,2,1,0:T(8,128)(2,1)S(1)}, bf16[2,32,144,128]{3,2,1,0:T(8,128)(2,1)S(1)}, bf1...) custom-call(bf16[32,128,128]{2,1,0:T(8,128)(2,1)S(1)} %bitcast.9, ...), custom_call_target="tpu_custom_call" | custom-call | flops 1000000000 | bytes 20000000 | tf_op jit(solution)/shard_map/pallas_call | solution.py:119
  68.7 1.4 copy-done.5
  70.2 0.7 fusion.12
  70.9 27.1 %shard_map.118 = (bf16[16,64,128]{2,1,0:T(8,128)(2,1)S(1)}, bf16[16,64,128]{2,1,0:T(8,128)(2,1)S(1)}) custom-call(s32[128]{0:T(128)S(1)} %reshape.34.refs_0_, s32[16]{0:T(128)S(1)} %select_reduce_fusion.refs_1_, s32[32]{0:T(128)S(1)} %copy-done.13, s32[2]{0:T(128)S(1)} %pad_add_fusion.refs_3_.meta_ref, ...), custom_call_target="tpu_custom_call" | custom-call | flops 2751463424 | bytes 8000000 | tf_op jit(solution)/shard_map/pallas_call | solution.py:347
  98.0 1.6 collective-permute-start.31
  99.7 27.0 %shard_map.117 = (bf16[16,64,128]{2,1,0:T(8,128)(2,1)S(1)}, bf16[16,64,128]{2,1,0:T(8,128)(2,1)S(1)}) custom-call(s32[128]{0:T(128)S(1)} %reshape.34.refs_0_, s32[16]{0:T(128)S(1)} %select_reduce_fusion.refs_1_, s32[32]{0:T(128)S(1)} %copy-done.13, s32[2]{0:T(128)S(1)} %pad_add_fusion.refs_3_.meta_ref, ...), custom_call_target="tpu_custom_call" | custom-call | flops 2751463424 | bytes 8000000 | tf_op jit(solution)/shard_map/pallas_call | solution.py:347
  126.7 0.6 collective-permute-start.30
  127.3 0.7 compare_select_fusion.3.earlier_ref
  128.0 16.1 %shard_map.114.refs_5_ = bf16[1,256,32,128]{3,2,1,0:T(8,128)(2,1)} custom-call(s32[4]{0:T(128)S(1)} %compare_select_fusion.3.earlier_ref, bf16[1,256,32,128]{3,2,1,0:T(8,128)(2,1)S(1)} %copy-done.6, bf16[2,2,256,128]{3,2,1,0:T(8,128)(2,1)S(1)} %get-tuple-element.15.refs_1_.refs_7_, bf16[2,2,256,128]{3,2,1,0:T(8,128)(2,1)S(1)} %collective-permute-done.3.refs_2_.refs_8_, ...), custom_call_target="tpu_custom_call" | custom-call | flops 1073741824 | bytes 4000000 | tf_op jit(solution)/shard_map/pallas_call | solution.py:231
  144.1 15.2 %shard_map.115 = bf16[1,256,32,128]{3,2,1,0:T(8,128)(2,1)} custom-call(s32[4]{0:T(128)S(1)} %compare_select_fusion.3.earlier_ref, bf16[1,256,32,128]{3,2,1,0:T(8,128)(2,1)S(1)} %copy-done.6, bf16[2,2,256,128]{3,2,1,0:T(8,128)(2,1)S(1)} %get-tuple-element.14.refs_1_.refs_7_, ...), custom_call_target="tpu_custom_call", output_to_operand_aliasing={{}: (6, {})} | custom-call | flops 1073741824 | bytes 4000000 | tf_op jit(solution)/shard_map/pallas_call | solution.py:231
  159.3 1.9 %shard_map.119 = bf16[16,4,8192]{2,1,0:T(4,128)(2,1)} custom-call(s32[2]{0:T(128)S(1)} %pad_add_fusion.refs_3_.meta_ref, bf16[16,64,128]{2,1,0:T(8,128)(2,1)S(1)} %get-tuple-element.19.refs_0_, bf16[16,64,128]{2,1,0:T(8,128)(2,1)S(1)} %get-tuple-element.23.refs_1_, bf16[16,64,128]{2,1,0:T(8,128)(2,1)S(1)} %collective-permute-done.30.refs_2_, ...), custom_call_target="tpu_custom_call" | custom-call | bytes 2000000 | tf_op jit(solution)/shard_map/pallas_call | solution.py:397
  (60 shorter events, 1.7 us)
Async XLA Ops:
  0.6 1.0 copy-start.1
  1.6 0.9 copy-start.2
  3.0 9.2 %collective-permute-start = (bf16[2,2,256,128]{3,2,1,0:T(8,128)(2,1)S(1)}, bf16[2,2,256,128]{3,2,1,0:T(8,128)(2,1)S(1)}, u32[]{:S(2)}, u32[]{:S(2)}) collective-permute-start(bf16[2,2,256,128]{3,2,1,0:T(8,128)(2,1)S(1)} %get-tuple-element.14.refs_1_.refs_7_), channel_id=1, source_target_pairs={{0,4},{4,6},{6,2},{2,0},{1,5},{5,7},{7,3},{3,1},{8,12},{12,14},{14... | collective-permute-start | bytes 786440 | tf_op jit(solution)/shard_map/ppermute | solution.py:449
  3.3 9.2 %collective-permute-start.22 = (bf16[2,2,256,128]{3,2,1,0:T(8,128)(2,1)S(1)}, bf16[2,2,256,128]{3,2,1,0:T(8,128)(2,1)S(1)}, u32[]{:S(2)}, u32[]{:S(2)}) collective-permute-start(bf16[2,2,256,128]{3,2,1,0:T(8,128)(2,1)S(1)} %get-tuple-element.14.refs_1_.refs_7_), channel_id=1, source_target_pairs={{0,16},{8,24},{16,0},{24,8},{1,17},{9,25},{17,1},{25,9},{2,18},{10... | collective-permute-start | bytes 786440 | tf_op jit(solution)/shard_map/ppermute | solution.py:454
  4.8 8.6 %collective-permute-start.18 = (bf16[2,2,256,128]{3,2,1,0:T(8,128)(2,1)S(1)}, bf16[2,2,256,128]{3,2,1,0:T(8,128)(2,1)S(1)}, u32[]{:S(2)}, u32[]{:S(2)}) collective-permute-start(bf16[2,2,256,128]{3,2,1,0:T(8,128)(2,1)S(1)} %get-tuple-element.14.refs_1_.refs_7_), channel_id=1, source_target_pairs={{0,8},{8,0},{16,24},{24,16},{1,9},{9,1},{17,25},{25,17},{2,10},{10... | collective-permute-start | bytes 786440 | tf_op jit(solution)/shard_map/ppermute | solution.py:454
  4.8 13.0 %collective-permute-start.3 = (bf16[2,2,256,128]{3,2,1,0:T(8,128)(2,1)S(1)}, bf16[2,2,256,128]{3,2,1,0:T(8,128)(2,1)S(1)}, u32[]{:S(2)}, u32[]{:S(2)}) collective-permute-start(bf16[2,2,256,128]{3,2,1,0:T(8,128)(2,1)S(1)} %get-tuple-element.15.refs_1_.refs_7_), channel_id=1, source_target_pairs={{0,4},{4,6},{6,2},{2,0},{1,5},{5,7},{7,3},{3,1},{8,12},{12,14},{14... | collective-permute-start | bytes 786440 | tf_op jit(solution)/shard_map/ppermute | solution.py:449
  5.3 12.5 %collective-permute-start.10 = (bf16[2,2,256,128]{3,2,1,0:T(8,128)(2,1)S(1)}, bf16[2,2,256,128]{3,2,1,0:T(8,128)(2,1)S(1)}, u32[]{:S(2)}, u32[]{:S(2)}) collective-permute-start(bf16[2,2,256,128]{3,2,1,0:T(8,128)(2,1)S(1)} %get-tuple-element.15.refs_1_.refs_7_), channel_id=1, source_target_pairs={{0,16},{8,24},{16,0},{24,8},{1,17},{9,25},{17,1},{25,9},{2,18},{10... | collective-permute-start | bytes 786440 | tf_op jit(solution)/shard_map/ppermute | solution.py:454
  12.2 6.1 %collective-permute-start.6 = (bf16[2,2,256,128]{3,2,1,0:T(8,128)(2,1)S(1)}, bf16[2,2,256,128]{3,2,1,0:T(8,128)(2,1)S(1)}, u32[]{:S(2)}, u32[]{:S(2)}) collective-permute-start(bf16[2,2,256,128]{3,2,1,0:T(8,128)(2,1)S(1)} %get-tuple-element.15.refs_1_.refs_7_), channel_id=1, source_target_pairs={{0,8},{8,0},{16,24},{24,16},{1,9},{9,1},{17,25},{25,17},{2,10},{10... | collective-permute-start | bytes 786440 | tf_op jit(solution)/shard_map/ppermute | solution.py:454
  12.6 10.9 %collective-permute-start.1 = (bf16[2,2,256,128]{3,2,1,0:T(8,128)(2,1)S(1)}, bf16[2,2,256,128]{3,2,1,0:T(8,128)(2,1)S(1)}, u32[]{:S(2)}, u32[]{:S(2)}) collective-permute-start(bf16[2,2,256,128]{3,2,1,0:T(8,128)(2,1)S(1)} %collective-permute-done.refs_2_.refs_8_), channel_id=1, source_target_pairs={{0,4},{4,6},{6,2},{2,0},{1,5},{5,7},{7,3},{3,1},{8,12},{12,14},{14... | collective-permute-start | bytes 786440 | tf_op jit(solution)/shard_map/ppermute | solution.py:449
  13.4 11.5 %collective-permute-start.23 = (bf16[2,2,256,128]{3,2,1,0:T(8,128)(2,1)S(1)}, bf16[2,2,256,128]{3,2,1,0:T(8,128)(2,1)}, u32[]{:S(2)}, u32[]{:S(2)}) collective-permute-start(bf16[2,2,256,128]{3,2,1,0:T(8,128)(2,1)S(1)} %collective-permute-done.refs_2_.refs_8_), channel_id=1, source_target_pairs={{0,16},{8,24},{16,0},{24,8},{1,17},{9,25},{17,1},{25,9},{2,18},{10... | collective-permute-start | bytes 786440 | tf_op jit(solution)/shard_map/ppermute | solution.py:454
  17.8 7.1 %collective-permute-start.19 = (bf16[2,2,256,128]{3,2,1,0:T(8,128)(2,1)S(1)}, bf16[2,2,256,128]{3,2,1,0:T(8,128)(2,1)S(1)}, u32[]{:S(2)}, u32[]{:S(2)}) collective-permute-start(bf16[2,2,256,128]{3,2,1,0:T(8,128)(2,1)S(1)} %collective-permute-done.refs_2_.refs_8_), channel_id=1, source_target_pairs={{0,8},{8,0},{16,24},{24,16},{1,9},{9,1},{17,25},{25,17},{2,10},{10... | collective-permute-start | bytes 786440 | tf_op jit(solution)/shard_map/ppermute | solution.py:454
  17.8 8.3 %collective-permute-start.26 = (bf16[2,2,256,128]{3,2,1,0:T(8,128)(2,1)S(1)}, bf16[2,2,256,128]{3,2,1,0:T(8,128)(2,1)S(1)}, u32[]{:S(2)}, u32[]{:S(2)}) collective-permute-start(bf16[2,2,256,128]{3,2,1,0:T(8,128)(2,1)S(1)} %collective-permute-done.22.refs_15_), channel_id=1, source_target_pairs={{0,8},{8,0},{16,24},{24,16},{1,9},{9,1},{17,25},{25,17},{2,10},{10... | collective-permute-start | bytes 786440 | tf_op jit(solution)/shard_map/ppermute | solution.py:454
  18.3 9.6 %collective-permute-start.4 = (bf16[2,2,256,128]{3,2,1,0:T(8,128)(2,1)S(1)}, bf16[2,2,256,128]{3,2,1,0:T(8,128)(2,1)S(1)}, u32[]{:S(2)}, u32[]{:S(2)}) collective-permute-start(bf16[2,2,256,128]{3,2,1,0:T(8,128)(2,1)S(1)} %collective-permute-done.3.refs_2_.refs_8_), channel_id=1, source_target_pairs={{0,4},{4,6},{6,2},{2,0},{1,5},{5,7},{7,3},{3,1},{8,12},{12,14},{14... | collective-permute-start | bytes 786440 | tf_op jit(solution)/shard_map/ppermute | solution.py:449
  23.4 6.4 %collective-permute-start.11 = (bf16[2,2,256,128]{3,2,1,0:T(8,128)(2,1)S(1)}, bf16[2,2,256,128]{3,2,1,0:T(8,128)(2,1)S(1)}, u32[]{:S(2)}, u32[]{:S(2)}) collective-permute-start(bf16[2,2,256,128]{3,2,1,0:T(8,128)(2,1)S(1)} %collective-permute-done.3.refs_2_.refs_8_), channel_id=1, source_target_pairs={{0,16},{8,24},{16,0},{24,8},{1,17},{9,25},{17,1},{25,9},{2,18},{10... | collective-permute-start | bytes 786440 | tf_op jit(solution)/shard_map/ppermute | solution.py:454
  24.9 5.0 %collective-permute-start.7 = (bf16[2,2,256,128]{3,2,1,0:T(8,128)(2,1)S(1)}, bf16[2,2,256,128]{3,2,1,0:T(8,128)(2,1)S(1)}, u32[]{:S(2)}, u32[]{:S(2)}) collective-permute-start(bf16[2,2,256,128]{3,2,1,0:T(8,128)(2,1)S(1)} %collective-permute-done.3.refs_2_.refs_8_), channel_id=1, source_target_pairs={{0,8},{8,0},{16,24},{24,16},{1,9},{9,1},{17,25},{25,17},{2,10},{10... | collective-permute-start | bytes 786440 | tf_op jit(solution)/shard_map/ppermute | solution.py:454
  24.9 0.7 copy-start.9
  25.6 4.8 %collective-permute-start.14 = (bf16[2,2,256,128]{3,2,1,0:T(8,128)(2,1)S(1)}, bf16[2,2,256,128]{3,2,1,0:T(8,128)(2,1)S(1)}, u32[]{:S(2)}, u32[]{:S(2)}) collective-permute-start(bf16[2,2,256,128]{3,2,1,0:T(8,128)(2,1)S(1)} %collective-permute-done.10.refs_15_), channel_id=1, source_target_pairs={{0,8},{8,0},{16,24},{24,16},{1,9},{9,1},{17,25},{25,17},{2,10},{10... | collective-permute-start | bytes 786440 | tf_op jit(solution)/shard_map/ppermute | solution.py:454
  26.2 0.7 copy-start.11
  26.9 9.2 %collective-permute-start.2 = (bf16[2,2,256,128]{3,2,1,0:T(8,128)(2,1)S(1)}, bf16[2,2,256,128]{3,2,1,0:T(8,128)(2,1)S(1)}, u32[]{:S(2)}, u32[]{:S(2)}) collective-permute-start(bf16[2,2,256,128]{3,2,1,0:T(8,128)(2,1)S(1)} %collective-permute-done.1.refs_3_.refs_9_), channel_id=1, source_target_pairs={{0,4},{4,6},{6,2},{2,0},{1,5},{5,7},{7,3},{3,1},{8,12},{12,14},{14... | collective-permute-start | bytes 786440 | tf_op jit(solution)/shard_map/ppermute | solution.py:449
  27.9 8.1 %collective-permute-start.24 = (bf16[2,2,256,128]{3,2,1,0:T(8,128)(2,1)S(1)}, bf16[2,2,256,128]{3,2,1,0:T(8,128)(2,1)}, u32[]{:S(2)}, u32[]{:S(2)}) collective-permute-start(bf16[2,2,256,128]{3,2,1,0:T(8,128)(2,1)S(1)} %collective-permute-done.1.refs_3_.refs_9_), channel_id=1, source_target_pairs={{0,16},{8,24},{16,0},{24,8},{1,17},{9,25},{17,1},{25,9},{2,18},{10... | collective-permute-start | bytes 786440 | tf_op jit(solution)/shard_map/ppermute | solution.py:454
  29.9 8.2 %collective-permute-start.20 = (bf16[2,2,256,128]{3,2,1,0:T(8,128)(2,1)S(1)}, bf16[2,2,256,128]{3,2,1,0:T(8,128)(2,1)}, u32[]{:S(2)}, u32[]{:S(2)}) collective-permute-start(bf16[2,2,256,128]{3,2,1,0:T(8,128)(2,1)S(1)} %collective-permute-done.1.refs_3_.refs_9_), channel_id=1, source_target_pairs={{0,8},{8,0},{16,24},{24,16},{1,9},{9,1},{17,25},{25,17},{2,10},{10... | collective-permute-start | bytes 786440 | tf_op jit(solution)/shard_map/ppermute | solution.py:454
  29.9 8.2 %collective-permute-start.27 = (bf16[2,2,256,128]{3,2,1,0:T(8,128)(2,1)}, bf16[2,2,256,128]{3,2,1,0:T(8,128)(2,1)}, u32[]{:S(2)}, u32[]{:S(2)}) collective-permute-start(bf16[2,2,256,128]{3,2,1,0:T(8,128)(2,1)} %collective-permute-done.23.refs_16_), channel_id=1, source_target_pairs={{0,8},{8,0},{16,24},{24,16},{1,9},{9,1},{17,25},{25,17},{2,10},{10... | collective-permute-start | bytes 786440 | tf_op jit(solution)/shard_map/ppermute | solution.py:454
  30.4 0.7 copy-start.7
  31.1 9.7 %collective-permute-start.5 = (bf16[2,2,256,128]{3,2,1,0:T(8,128)(2,1)S(1)}, bf16[2,2,256,128]{3,2,1,0:T(8,128)(2,1)}, u32[]{:S(2)}, u32[]{:S(2)}) collective-permute-start(bf16[2,2,256,128]{3,2,1,0:T(8,128)(2,1)S(1)} %collective-permute-done.4.refs_3_.refs_9_), channel_id=1, source_target_pairs={{0,4},{4,6},{6,2},{2,0},{1,5},{5,7},{7,3},{3,1},{8,12},{12,14},{14... | collective-permute-start | bytes 786440 | tf_op jit(solution)/shard_map/ppermute | solution.py:449
  36.0 9.3 %collective-permute-start.25 = (bf16[2,2,256,128]{3,2,1,0:T(8,128)(2,1)S(1)}, bf16[2,2,256,128]{3,2,1,0:T(8,128)(2,1)}, u32[]{:S(2)}, u32[]{:S(2)}) collective-permute-start(bf16[2,2,256,128]{3,2,1,0:T(8,128)(2,1)S(1)} %collective-permute-done.2.refs_4_.refs_10_), channel_id=1, source_target_pairs={{0,16},{8,24},{16,0},{24,8},{1,17},{9,25},{17,1},{25,9},{2,18},{10... | collective-permute-start | bytes 786440 | tf_op jit(solution)/shard_map/ppermute | solution.py:454
  36.0 15.0 %collective-permute-start.12 = (bf16[2,2,256,128]{3,2,1,0:T(8,128)(2,1)S(1)}, bf16[2,2,256,128]{3,2,1,0:T(8,128)(2,1)}, u32[]{:S(2)}, u32[]{:S(2)}) collective-permute-start(bf16[2,2,256,128]{3,2,1,0:T(8,128)(2,1)S(1)} %collective-permute-done.4.refs_3_.refs_9_), channel_id=1, source_target_pairs={{0,16},{8,24},{16,0},{24,8},{1,17},{9,25},{17,1},{25,9},{2,18},{10... | collective-permute-start | bytes 786440 | tf_op jit(solution)/shard_map/ppermute | solution.py:454
  38.1 12.9 %collective-permute-start.21 = (bf16[2,2,256,128]{3,2,1,0:T(8,128)(2,1)S(1)}, bf16[2,2,256,128]{3,2,1,0:T(8,128)(2,1)}, u32[]{:S(2)}, u32[]{:S(2)}) collective-permute-start(bf16[2,2,256,128]{3,2,1,0:T(8,128)(2,1)S(1)} %collective-permute-done.2.refs_4_.refs_10_), channel_id=1, source_target_pairs={{0,8},{8,0},{16,24},{24,16},{1,9},{9,1},{17,25},{25,17},{2,10},{10... | collective-permute-start | bytes 786440 | tf_op jit(solution)/shard_map/ppermute | solution.py:454
  38.1 13.4 %collective-permute-start.28 = (bf16[2,2,256,128]{3,2,1,0:T(8,128)(2,1)}, bf16[2,2,256,128]{3,2,1,0:T(8,128)(2,1)}, u32[]{:S(2)}, u32[]{:S(2)}) collective-permute-start(bf16[2,2,256,128]{3,2,1,0:T(8,128)(2,1)} %collective-permute-done.24.refs_17_), channel_id=1, source_target_pairs={{0,8},{8,0},{16,24},{24,16},{1,9},{9,1},{17,25},{25,17},{2,10},{10... | collective-permute-start | bytes 786440 | tf_op jit(solution)/shard_map/ppermute | solution.py:454
  40.8 13.1 %collective-permute-start.13 = (bf16[2,2,256,128]{3,2,1,0:T(8,128)(2,1)}, bf16[2,2,256,128]{3,2,1,0:T(8,128)(2,1)}, u32[]{:S(2)}, u32[]{:S(2)}) collective-permute-start(bf16[2,2,256,128]{3,2,1,0:T(8,128)(2,1)} %collective-permute-done.5.refs_4_.refs_10_), channel_id=1, source_target_pairs={{0,16},{8,24},{16,0},{24,8},{1,17},{9,25},{17,1},{25,9},{2,18},{10... | collective-permute-start | bytes 786440 | tf_op jit(solution)/shard_map/ppermute | solution.py:454
  45.4 8.5 %collective-permute-start.29 = (bf16[2,2,256,128]{3,2,1,0:T(8,128)(2,1)}, bf16[2,2,256,128]{3,2,1,0:T(8,128)(2,1)}, u32[]{:S(2)}, u32[]{:S(2)}) collective-permute-start(bf16[2,2,256,128]{3,2,1,0:T(8,128)(2,1)} %collective-permute-done.25.refs_18_), channel_id=1, source_target_pairs={{0,8},{8,0},{16,24},{24,16},{1,9},{9,1},{17,25},{25,17},{2,10},{10... | collective-permute-start | bytes 786440 | tf_op jit(solution)/shard_map/ppermute | solution.py:454
  51.0 47.0 %collective-permute-start.8 = (bf16[2,2,256,128]{3,2,1,0:T(8,128)(2,1)S(1)}, bf16[2,2,256,128]{3,2,1,0:T(8,128)(2,1)S(1)}, u32[]{:S(2)}, u32[]{:S(2)}) collective-permute-start(bf16[2,2,256,128]{3,2,1,0:T(8,128)(2,1)S(1)} %collective-permute-done.4.refs_3_.refs_9_), channel_id=1, source_target_pairs={{0,8},{8,0},{16,24},{24,16},{1,9},{9,1},{17,25},{25,17},{2,10},{10... | collective-permute-start | bytes 786440 | tf_op jit(solution)/shard_map/ppermute | solution.py:454
  51.0 48.6 %collective-permute-start.15 = (bf16[2,2,256,128]{3,2,1,0:T(8,128)(2,1)S(1)}, bf16[2,2,256,128]{3,2,1,0:T(8,128)(2,1)S(1)}, u32[]{:S(2)}, u32[]{:S(2)}) collective-permute-start(bf16[2,2,256,128]{3,2,1,0:T(8,128)(2,1)S(1)} %collective-permute-done.11.refs_16_), channel_id=1, source_target_pairs={{0,8},{8,0},{16,24},{24,16},{1,9},{9,1},{17,25},{25,17},{2,10},{10... | collective-permute-start | bytes 786440 | tf_op jit(solution)/shard_map/ppermute | solution.py:454
  51.5 48.1 %collective-permute-start.9 = (bf16[2,2,256,128]{3,2,1,0:T(8,128)(2,1)}, bf16[2,2,256,128]{3,2,1,0:T(8,128)(2,1)S(1)}, u32[]{:S(2)}, u32[]{:S(2)}) collective-permute-start(bf16[2,2,256,128]{3,2,1,0:T(8,128)(2,1)} %collective-permute-done.5.refs_4_.refs_10_), channel_id=1, source_target_pairs={{0,8},{8,0},{16,24},{24,16},{1,9},{9,1},{17,25},{25,17},{2,10},{10... | collective-permute-start | bytes 786440 | tf_op jit(solution)/shard_map/ppermute | solution.py:454
  53.9 45.7 %collective-permute-start.16 = (bf16[2,2,256,128]{3,2,1,0:T(8,128)(2,1)}, bf16[2,2,256,128]{3,2,1,0:T(8,128)(2,1)S(1)}, u32[]{:S(2)}, u32[]{:S(2)}) collective-permute-start(bf16[2,2,256,128]{3,2,1,0:T(8,128)(2,1)} %collective-permute-done.12.refs_17_), channel_id=1, source_target_pairs={{0,8},{8,0},{16,24},{24,16},{1,9},{9,1},{17,25},{25,17},{2,10},{10... | collective-permute-start | bytes 786440 | tf_op jit(solution)/shard_map/ppermute | solution.py:454
  53.9 45.7 %collective-permute-start.17 = (bf16[2,2,256,128]{3,2,1,0:T(8,128)(2,1)}, bf16[2,2,256,128]{3,2,1,0:T(8,128)(2,1)S(1)}, u32[]{:S(2)}, u32[]{:S(2)}) collective-permute-start(bf16[2,2,256,128]{3,2,1,0:T(8,128)(2,1)} %collective-permute-done.13.refs_18_), channel_id=1, source_target_pairs={{0,8},{8,0},{16,24},{24,16},{1,9},{9,1},{17,25},{25,17},{2,10},{10... | collective-permute-start | bytes 786440 | tf_op jit(solution)/shard_map/ppermute | solution.py:454
  54.4 1.2 copy-start
  55.6 0.9 copy-start.3
  56.5 0.9 copy-start.4
  57.4 13.4 %copy-start.10 = (bf16[2,2,256,128]{3,2,1,0:T(8,128)(2,1)S(1)}, bf16[2,2,256,128]{3,2,1,0:T(8,128)(2,1)}, u32[]{:S(2)}) copy-start(bf16[2,2,256,128]{3,2,1,0:T(8,128)(2,1)} %copy-done.9) | copy-start | bytes 786436
  57.4 13.4 %copy-start.12 = (bf16[2,2,256,128]{3,2,1,0:T(8,128)(2,1)S(1)}, bf16[2,2,256,128]{3,2,1,0:T(8,128)(2,1)}, u32[]{:S(2)}) copy-start(bf16[2,2,256,128]{3,2,1,0:T(8,128)(2,1)} %copy-done.11) | copy-start | bytes 786436
  57.4 13.4 %copy-start.13 = (s32[32]{0:T(128)S(1)}, s32[32]{0:T(128)}, u32[]{:S(2)}) copy-start(s32[32]{0:T(128)} %refs_2_.3) | copy-start | bytes 388
  68.7 1.4 copy-start.5
  70.9 28.8 %copy-start.8 = (bf16[2,2,256,128]{3,2,1,0:T(8,128)(2,1)S(1)}, bf16[2,2,256,128]{3,2,1,0:T(8,128)(2,1)}, u32[]{:S(2)}) copy-start(bf16[2,2,256,128]{3,2,1,0:T(8,128)(2,1)} %copy-done.7) | copy-start | bytes 786436
  98.0 61.2 %collective-permute-start.31 = (bf16[16,64,128]{2,1,0:T(8,128)(2,1)S(1)}, bf16[16,64,128]{2,1,0:T(8,128)(2,1)S(1)}, u32[]{:S(2)}, u32[]{:S(2)}) collective-permute-start(bf16[16,64,128]{2,1,0:T(8,128)(2,1)S(1)} %get-tuple-element.25), channel_id=1, source_target_pairs={{0,1},{1,0},{2,3},{3,2},{4,5},{5,4},{6,7},{7,6},{8,9},{9,8},{10,11... | collective-permute-start | bytes 786440 | tf_op jit(solution)/shard_map/ppermute | solution.py:491
  99.7 28.3 %copy-start.6 = (bf16[1,256,32,128]{3,2,1,0:T(8,128)(2,1)S(1)}, bf16[1,256,32,128]{3,2,1,0:T(8,128)(2,1)}, u32[]{:S(2)}) copy-start(bf16[1,256,32,128]{3,2,1,0:T(8,128)(2,1)} %refs_0_.3) | copy-start | bytes 6291460
  126.7 32.6 %collective-permute-start.30 = (bf16[16,64,128]{2,1,0:T(8,128)(2,1)S(1)}, bf16[16,64,128]{2,1,0:T(8,128)(2,1)S(1)}, u32[]{:S(2)}, u32[]{:S(2)}) collective-permute-start(bf16[16,64,128]{2,1,0:T(8,128)(2,1)S(1)} %get-tuple-element.24), channel_id=1, source_target_pairs={{0,1},{1,0},{2,3},{3,2},{4,5},{5,4},{6,7},{7,6},{8,9},{9,8},{10,11... | collective-permute-start | bytes 786440 | tf_op jit(solution)/shard_map/ppermute | solution.py:491

commit v2 on v1

v2 whole, which is shorter than its diff:
```python
import functools
import math

import jax
import jax.numpy as jnp
from jax import lax
from jax.experimental import pallas as pl
from jax.experimental.pallas import tpu as pltpu
from jax.sharding import PartitionSpec as P

PAGE = 128
CHUNKS = 2
LOG2E = 1.4426950408889634
NEG = -1e30
VMEM_LIMIT = 48 * 1024 * 1024


def nt(a, b):
    return lax.dot_general(a, b, (((1,), (1,)), ((), ())), preferred_element_type=jnp.float32)


def nn(a, b):
    return jnp.dot(a, b, preferred_element_type=jnp.float32)


def tn(a, b):
    return lax.dot_general(a, b, (((0,), (0,)), ((), ())), preferred_element_type=jnp.float32)


def params():
    return pltpu.CompilerParams(vmem_limit_bytes=VMEM_LIMIT)


def one_hot(out_rows, in_rows, source):
    row = lax.broadcasted_iota(jnp.int32, (out_rows, in_rows), 0)
    col = lax.broadcasted_iota(jnp.int32, (out_rows, in_rows), 1)
    return jnp.where(col == source(row), 1.0, 0.0).astype(jnp.bfloat16)


def split_kernel(heads, per_chunk, tokens, k_ref, v_ref, *outs):
    rows = min(tokens * heads, 256)
    step = rows // heads
    pick = one_hot(rows, rows, lambda i: (i % step) * heads + i // step)
    moved = []
    for j in range(tokens // step):
        keys = nn(pick, k_ref[pl.ds(j * rows, rows), :]).astype(jnp.bfloat16)
        moved.append(nn(pick, v_ref[pl.ds(j * rows, rows), :]))
        for h in range(heads):
            outs[h // per_chunk][h % per_chunk, 0, pl.ds(j * step, step), :] = keys[
                h * step : (h + 1) * step
            ]
    for h in range(heads):
        values = jnp.concatenate([a[h * step : (h + 1) * step] for a in moved], axis=0)
        for page in range(tokens // PAGE):
            outs[h // per_chunk][h % per_chunk, 1, pl.ds(page * PAGE, PAGE), :] = values[
                page * PAGE : (page + 1) * PAGE
            ].T.astype(jnp.bfloat16)


def split_heads(k, v, chunks):
    _, tokens, heads, width = k.shape
    per_chunk = heads // chunks
    shape = jax.ShapeDtypeStruct((per_chunk, 2, tokens, width), jnp.bfloat16)
    return pl.pallas_call(
        functools.partial(split_kernel, heads, per_chunk, tokens),
        out_shape=[shape] * chunks,
        compiler_params=params(),
        cost_estimate=pl.CostEstimate(flops=10**8, bytes_accessed=2 * 10**6, transcendentals=0),
    )(k.reshape(tokens * heads, width), v.reshape(tokens * heads, width))


def prefill_kernel(ring, aliased, group, tokens, scale, earlier_ref, *refs):
    q_ref = refs[0]
    blocks = refs[1 : 1 + ring]
    out_ref, buf, m_ref, l_ref, acc_ref, sems = refs[1 + ring + aliased :]
    own = blocks[0]
    heads = own.shape[0]
    block = q_ref.shape[1]
    i = pl.program_id(0)

    def copies():
        found = []
        place = jnp.int32(0)
        for s in range(1, ring):
            copy = pltpu.make_async_copy(blocks[s], buf.at[place], sems.at[s])
            found.append((earlier_ref[s], copy))
            place = place + earlier_ref[s]
        return found

    @pl.when(i == 0)
    def _():
        for flag, copy in copies():
            @pl.when(flag == 1)
            def _():
                copy.start()
        for flag, copy in copies():
            @pl.when(flag == 1)
            def _():
                copy.wait()

    rows = block * group
    queries = q_ref[0].astype(jnp.float32)
    q = [
        queries[:, h * group : (h + 1) * group, :].reshape(rows, -1).astype(jnp.bfloat16)
        for h in range(heads)
    ]

    def first(keys):
        token = lax.broadcasted_iota(jnp.int32, (keys, rows), 1) // group + i * block
        allowed = lax.broadcasted_iota(jnp.int32, (keys, rows), 0) <= token
        for h in range(heads):
            s = jnp.where(allowed, nt(own[h, 0, pl.ds(0, keys), :], q[h]), NEG)
            m = jnp.max(s, axis=0, keepdims=True)
            p = jnp.exp2((s - m) * scale)
            m_ref[h] = m
            l_ref[h] = jnp.sum(p, axis=0, keepdims=True)
            p = p.astype(jnp.bfloat16)
            values = [own[h, 1, pl.ds(j * PAGE, PAGE), :] for j in range(keys // PAGE)]
            acc_ref[h] = nn(jnp.concatenate(values, axis=1), p)

    pages = tokens // PAGE
    for j in range(pages):
        @pl.when((i * block) // PAGE == j)
        def _():
            first((j + 1) * PAGE)

    def step(b, carry):
        for h in range(heads):
            s = nt(buf[b, h, 0], q[h])
            m = m_ref[h]
            new = jnp.maximum(m, jnp.max(s, axis=0, keepdims=True))
            p = jnp.exp2((s - new) * scale)
            shrink = jnp.exp2((m - new) * scale)
            m_ref[h] = new
            l_ref[h] = l_ref[h] * shrink + jnp.sum(p, axis=0, keepdims=True)
            p = p.astype(jnp.bfloat16)
            values = [buf[b, h, 1, pl.ds(j * PAGE, PAGE), :] for j in range(pages)]
            acc_ref[h] = acc_ref[h] * shrink + nn(jnp.concatenate(values, axis=1), p)
        return carry

    lax.fori_loop(0, earlier_ref[0], step, 0)
    out = [(acc_ref[h] / l_ref[h]).T.reshape(block, group, -1) for h in range(heads)]
    out_ref[0] = jnp.concatenate(out, axis=1).astype(out_ref.dtype)


def prefill(q, blocks, earlier, column, previous):
    _, tokens, q_heads, width = q.shape
    ring = len(blocks)
    heads = blocks[0].shape[0]
    group = 8
    block = 64
    rows = block * group
    q_spec = pl.BlockSpec((1, block, heads * group, width), lambda i, *_: (0, i, column, 0))
    own_spec = pl.BlockSpec(blocks[0].shape, lambda i, *_: (0, 0, 0, 0))
    any_spec = pl.BlockSpec(memory_space=pl.ANY)
    in_specs = [q_spec, own_spec] + [any_spec] * (ring - 1)
    operands = [q] + list(blocks)
    aliases = {}
    if previous is not None:
        aliases = {1 + len(operands): 0}
        operands.append(previous)
        in_specs.append(any_spec)
    return pl.pallas_call(
        functools.partial(
            prefill_kernel,
            ring,
            len(aliases),
            group,
            tokens,
            LOG2E / math.sqrt(width),
        ),
        grid_spec=pltpu.PrefetchScalarGridSpec(
            num_scalar_prefetch=1,
            grid=(tokens // block,),
            in_specs=in_specs,
            out_specs=q_spec,
            scratch_shapes=[
                pltpu.VMEM((max(ring - 1, 1),) + blocks[0].shape, jnp.bfloat16),
                pltpu.VMEM((heads, 1, rows), jnp.float32),
                pltpu.VMEM((heads, 1, rows), jnp.float32),
                pltpu.VMEM((heads, width, rows), jnp.float32),
                pltpu.SemaphoreType.DMA((ring,)),
            ],
        ),
        out_shape=jax.ShapeDtypeStruct(q.shape, jnp.bfloat16),
        input_output_aliases=aliases,
        compiler_params=params(),
        cost_estimate=pl.CostEstimate(
            flops=16 * heads * group * tokens * tokens * ring * width,
            bytes_accessed=4 * 10**6,
            transcendentals=tokens * tokens * ring * heads * group,
        ),
    )(earlier, *operands)


def decode_kernel(
    slots, extra, steps, target, targets, chunk, kv_heads, group, scale, pack, unroll, *refs
):
    slot_ref, pick_ref, len_ref, meta_ref = refs[:4]
    q_ref, dk_ref, dv_ref, ck_ref, cv_ref = refs[4:9]
    blocks = refs[9 : 9 + slots]
    out_ref, buf, sems = refs[9 + slots :]
    heads = buf.shape[1]
    block = q_ref.shape[0]
    width = q_ref.shape[2]
    blocks_each = pl.num_programs(0)
    i = pl.program_id(0)
    first = (lax.rem(meta_ref[1] + target, targets) * blocks_each + i) * block

    def copies():
        for s in range(slots):
            start = pl.multiple_of(pick_ref[s] * PAGE, PAGE)
            yield pltpu.make_async_copy(
                blocks[s].at[:, :, pl.ds(start, PAGE), :], buf.at[s], sems.at[s]
            )

    @pl.when(i == 0)
    def _():
        for copy in copies():
            copy.start()
        for copy in copies():
            copy.wait()

    per_step = heads * group
    per_request = steps * per_step
    lanes = pack * per_request
    units = [(p, h) for p in range(pack) for h in range(heads)]

    def unit_of(index):
        return index // per_request * heads + index % per_step // group

    q_row = lax.broadcasted_iota(jnp.int32, (lanes, width), 0)
    unit_rows = [
        jnp.where(unit_of(q_row) == u, 1.0, 0.0).astype(jnp.bfloat16) for u in range(len(units))
    ]
    request_rows = [
        jnp.where(q_row // per_request == p, 1.0, 0.0).astype(jnp.bfloat16) for p in range(pack)
    ]
    lane = lax.broadcasted_iota(jnp.int32, (width, lanes), 1)
    lane_unit = unit_of(lane)
    lane_request = lane // per_request

    def raw_mask(rows):
        row = lax.broadcasted_iota(jnp.int32, (rows, lanes), 0)
        column = lax.broadcasted_iota(jnp.int32, (rows, lanes), 1)
        same = row % kv_heads == column % per_step // group + chunk * heads
        return jnp.where(same, row // kv_heads, 1 << 20), column

    cache_place, _ = raw_mask(ck_ref.shape[1])
    new_place, new_column = raw_mask(dk_ref.shape[1])
    new_allowed = new_place <= new_column % per_request // per_step
    one_lane = lax.broadcasted_iota(jnp.int32, (1, lanes), 1) // per_request
    order = one_hot(
        lanes,
        lanes,
        lambda r: r // per_request * per_request
        + r % steps * per_step
        + r % per_request // steps,
    )

    def queries(r):
        if heads == kv_heads:
            return q_ref[r]
        total = kv_heads * group
        return jnp.concatenate(
            [
                q_ref[r, pl.ds(t * total + chunk * per_step, per_step), :]
                for t in range(steps)
            ],
            axis=0,
        )

    def attend(sets):
        scores = []
        for s in sets:
            base = s * pack
            q = [queries(base + p) for p in range(pack)]
            q = q[0] if pack == 1 else jnp.concatenate(q, axis=0)
            q_units = jnp.concatenate([q * a for a in unit_rows], axis=1)
            q_raw = q if pack == 1 else jnp.concatenate([q * a for a in request_rows], axis=1)
            places = [
                [slot_ref[(first + base + p) * extra + j] for j in range(extra)]
                for p in range(pack)
            ]
            keys = jnp.concatenate(
                [
                    jnp.concatenate([buf[places[p][j], h, 0] for p, h in units], axis=1)
                    for j in range(extra)
                ],
                axis=0,
            )
            raw = jnp.concatenate([ck_ref[base + p] for p in range(pack)], axis=1)
            new = jnp.concatenate([dk_ref[base + p] for p in range(pack)], axis=1)
            length = jnp.zeros((1, lanes), jnp.int32)
            for p in range(pack):
                length = jnp.where(one_lane == p, len_ref[first + base + p], length)
            scores.append(
                (
                    base,
                    places,
                    nt(keys, q_units),
                    jnp.where(cache_place < length, nt(raw, q_raw), NEG),
                    jnp.where(new_allowed, nt(new, q_raw), NEG),
                )
            )
        weights = []
        for base, places, pages, old, new in scores:
            m = jnp.maximum(
                jnp.max(pages, axis=0, keepdims=True), jnp.max(old, axis=0, keepdims=True)
            )
            m = jnp.maximum(m, jnp.max(new, axis=0, keepdims=True))
            pages = jnp.exp2((pages - m) * scale)
            old = jnp.exp2((old - m) * scale)
            new = jnp.exp2((new - m) * scale)
            total = (
                jnp.sum(pages, axis=0, keepdims=True)
                + jnp.sum(old, axis=0, keepdims=True)
                + jnp.sum(new, axis=0, keepdims=True)
            )
            weights.append(
                (
                    base,
                    places,
                    pages.astype(jnp.bfloat16),
                    old.astype(jnp.bfloat16),
                    new.astype(jnp.bfloat16),
                    total,
                )
            )
        for base, places, pages, old, new, total in weights:
            values = jnp.concatenate(
                [
                    jnp.concatenate([buf[places[p][j], h, 1] for j in range(extra)], axis=1)
                    for p, h in units
                ],
                axis=0,
            )
            every = nn(values, pages)
            acc = jnp.zeros((width, lanes), jnp.float32)
            for u in range(len(units)):
                acc = jnp.where(lane_unit == u, every[u * width : (u + 1) * width], acc)
            rest = jnp.zeros((width, lanes), jnp.float32)
            for p in range(pack):
                part = tn(cv_ref[base + p], old) + tn(dv_ref[base + p], new)
                rest = part if pack == 1 else jnp.where(lane_request == p, part, rest)
            result = ((acc + rest) / total).astype(jnp.bfloat16)
            result = nt(order, result).astype(jnp.bfloat16)
            for p in range(pack):
                out_ref[base + p] = result[p * per_request : (p + 1) * per_request]

    def body(g, carry):
        attend([g * unroll + u for u in range(unroll)])
        return carry

    lax.fori_loop(0, block // (pack * unroll), body, 0)


def decode(arrays, blocks, scalars, chunk, target, targets, extra):
    q, dk, dv, ck, cv = arrays
    requests, steps, q_heads, width = q.shape
    kv_heads = ck.shape[2]
    group = q_heads // kv_heads
    heads = blocks[0].shape[0]
    pack = max(1, 4 // heads)
    per_target = requests // targets
    block = min(8, per_target)
    pack = math.gcd(pack, block)
    unroll = math.gcd(2, block // pack)
    per_block = per_target // block
    slots = len(blocks)
    raw = [a.reshape(requests, -1, width) for a in (q, dk, dv, ck, cv)]
    per_request = heads * group * steps

    def here(i, slot, pick, lens, meta):
        return (lax.rem(meta[1] + target, targets) * per_block + i, 0, 0)

    in_specs = [pl.BlockSpec((block,) + a.shape[1:], here) for a in raw]
    in_specs += [pl.BlockSpec(memory_space=pl.ANY)] * slots
    keys = extra * PAGE + ck.shape[1]
    return pl.pallas_call(
        functools.partial(
            decode_kernel,
            slots,
            extra,
            steps,
            target,
            targets,
            chunk,
            kv_heads,
            group,
            LOG2E / math.sqrt(width),
            pack,
            unroll,
        ),
        grid_spec=pltpu.PrefetchScalarGridSpec(
            num_scalar_prefetch=4,
            grid=(per_block,),
            in_specs=in_specs,
            out_specs=pl.BlockSpec((block, per_request, width), lambda i, *_: (i, 0, 0)),
            scratch_shapes=[
                pltpu.VMEM((slots, heads, 2, PAGE, width), jnp.bfloat16),
                pltpu.SemaphoreType.DMA((slots,)),
            ],
        ),
        out_shape=jax.ShapeDtypeStruct((per_target, per_request, width), jnp.bfloat16),
        compiler_params=params(),
        cost_estimate=pl.CostEstimate(
            flops=per_target * per_request * keys * width * 4 * 4,
            bytes_accessed=8 * 10**6,
            transcendentals=per_target * per_request * keys,
        ),
    )(*scalars, *raw, *blocks)


def join_kernel(targets, chunks, steps, meta_ref, *refs):
    out_ref = refs[-1]
    k = pl.program_id(0)
    rows = refs[0].shape[1]
    each = rows // steps
    for s in range(targets):
        @pl.when(lax.rem(meta_ref[1] + (targets - s), targets) == k)
        def _():
            for c in range(chunks):
                source = refs[s * chunks + c]

                def body(r, carry):
                    value = source[r]
                    for g in range(each):
                        out_ref[r, :, (c * each + g) * 128 : (c * each + g + 1) * 128] = value[
                            g * steps : (g + 1) * steps
                        ]
                    return carry

                lax.fori_loop(0, out_ref.shape[0], body, 0)


def join(pieces, meta, steps, targets, chunks):
    per_target, rows, width = pieces[0].shape
    half = chunks * (rows // steps) * width
    spec = pl.BlockSpec((per_target, rows, width), lambda k, *_: (0, 0, 0))
    return pl.pallas_call(
        functools.partial(join_kernel, targets, chunks, steps),
        grid_spec=pltpu.PrefetchScalarGridSpec(
            num_scalar_prefetch=1,
            grid=(targets,),
            in_specs=[spec] * len(pieces),
            out_specs=pl.BlockSpec((per_target, steps, half), lambda k, *_: (0, 0, k)),
        ),
        out_shape=jax.ShapeDtypeStruct((per_target, steps, half * targets), jnp.bfloat16),
        compiler_params=params(),
        cost_estimate=pl.CostEstimate(flops=0, bytes_accessed=2 * 10**6, transcendentals=0),
    )(meta, *pieces)


def ring_place(index, size):
    return jnp.where(index % 2 == 0, index // 2, size - 1 - index // 2)


def shards(
    roles,
    ring,
    targets,
    prefill_q,
    prefill_k,
    prefill_v,
    decode_q,
    decode_k,
    decode_v,
    cache_k,
    cache_v,
    cache_len,
    page_list,
):
    tokens = prefill_q.shape[1]
    heads = prefill_k.shape[2]
    own_pages = tokens // PAGE
    requests, steps = decode_q.shape[:2]
    extra = page_list.shape[1]
    chunks = math.gcd(CHUNKS, heads)
    role = lax.axis_index("role")
    ctx = lax.axis_index("ctx")
    tp = lax.axis_index("tp")

    order = list(range(0, ring, 2)) + list(range(ring - 1, 0, -2))
    along = [(order[j], order[(j + 1) % ring]) for j in range(ring)]
    flips = [1 << b for b in reversed(range(roles.bit_length() - 1))]

    own = split_heads(prefill_k, prefill_v, chunks)
    gathered = []
    for c in range(chunks):
        line = [own[c]]
        for s in range(1, ring):
            line.append(lax.ppermute(line[-1], "ctx", along))
        by_role = {0: line}
        for flip in flips:
            pairs = [(j, j ^ flip) for j in range(roles)]
            for seen in list(by_role):
                by_role[seen ^ flip] = [lax.ppermute(a, "role", pairs) for a in by_role[seen]]
        gathered.append(by_role)

    owner = page_list // own_pages
    place = (ring_place(ctx, ring) - ring_place(owner % ring, ring)) % ring
    slot = ((owner // ring) ^ role) * ring + place
    hot = slot.reshape(-1, 1) == jnp.arange(roles * ring)[None, :]
    pick = jnp.max(jnp.where(hot, (page_list % own_pages).reshape(-1, 1), 0), axis=0)
    meta = jnp.stack([ctx, tp]).astype(jnp.int32)
    scalars = (
        slot.reshape(-1).astype(jnp.int32),
        pick.astype(jnp.int32),
        cache_len.astype(jnp.int32),
        meta,
    )
    position = jnp.arange(ring)
    where = ring_place(ctx, ring)
    source = (where - position) % ring
    source_ctx = jnp.where(source < (ring + 1) // 2, 2 * source, 2 * (ring - 1 - source) + 1)
    flags = (source_ctx < ctx).astype(jnp.int32)
    earlier = jnp.where(position == 0, jnp.sum(flags), flags).astype(jnp.int32)

    arrays = (decode_q, decode_k, decode_v, cache_k, cache_v)
    pieces = [[] for _ in range(targets)]
    prefill_out = None
    for c in range(chunks):
        prefill_out = prefill(prefill_q, gathered[c][0], earlier, c, prefill_out)
        blocks = [a for r in range(roles) for a in gathered[c][r]]
        for s in reversed(range(targets)):
            out = decode(arrays, blocks, scalars, c, s, targets, extra)
            if s:
                shift = [(j, (j + s) % targets) for j in range(targets)]
                out = lax.ppermute(out, "tp", shift)
            pieces[s].append(out)
    decode_out = join(
        [a for piece in pieces for a in piece], meta, steps, targets, chunks
    )
    return (prefill_out, decode_out)


def solution(mesh):
    body = functools.partial(shards, mesh.shape["role"], mesh.shape["ctx"], mesh.shape["tp"])
    return jax.shard_map(
        body,
        mesh=mesh,
        in_specs=(
            P("role", "ctx", "tp", None),
            P("role", "ctx", "tp", None),
            P("role", "ctx", "tp", None),
            P(("role", "ctx"), None, "tp", None),
            P(("role", "ctx"), None, "tp", None),
            P(("role", "ctx"), None, "tp", None),
            P(("role", "ctx"), None, "tp", None),
            P(("role", "ctx"), None, "tp", None),
            P(("role", "ctx")),
            P(("role", "ctx"), None),
        ),
        out_specs=(P("role", "ctx", "tp", None), P(("role", "ctx", "tp"), None, None)),
        check_vma=False,
    )
```

time: 162 us -> 138 us (0.85)
  Pallas kernels: 99 us -> 76.1 us
  waiting for transfers between devices: 31.9 us -> 37.8 us
  local copies, waits for them, and re-layouts: 8.87 us -> 4.61 us
  starting transfers between devices: 18.2 us -> 15.7 us
    pallas_call x2 -> x4, Pallas kernels: 54.2 us -> 41.4 us  [decode(): pl.pallas_call(functools.partial(decode_kernel, slots, extra, steps, targ...]
    ppermute x24, waiting for transfers between devices: 11.6 us -> 23.5 us  [shards(): lax.ppermute(a, 'role', pairs)]
    pallas_call x3 -> x2, Pallas kernels: 42.5 us -> 32.2 us  [prefill(): pl.pallas_call(functools.partial(prefill_kernel, ring, len(aliases), grou...]
    ppermute x6, waiting for transfers between devices: 20.4 us -> 14.4 us  [shards(): line.append(lax.ppermute(line[-1], 'ctx', along))]
    unnamed x28 -> x20, local copies, waits for them, and re-layouts: 8.49 us -> 4.22 us
  transfers between devices with their start and end apart: 32 -> 32, of which waited for: 11 -> 13; matrix products, arithmetic and copies ran while one was open for 2% -> 2% of each run, Pallas kernels for 60% -> 54%
where the time goes in v2:
time: 138 us; the launch traced here: 137 us
  Pallas kernels  76.1 us (55%)
  waiting for transfers between devices  37.8 us (27%)
  starting transfers between devices  15.7 us (11%)
  local copies, waits for them, and re-layouts  4.61 us (3%)
  other arithmetic  2.24 us (2%)
    pallas_call x4, Pallas kernels, decode(): pl.pallas_call(functools.partial(decode_kernel, slots, extra, steps, targ...  41.4 us
    pallas_call x2, Pallas kernels, prefill(): pl.pallas_call(functools.partial(prefill_kernel, ring, len(aliases), grou...  32.2 us
    ppermute x24, waiting for transfers between devices, shards(): lax.ppermute(a, 'role', pairs)  23.5 us
    ppermute x6, waiting for transfers between devices, shards(): line.append(lax.ppermute(line[-1], 'ctx', along))  14.4 us
    ppermute x24, starting transfers between devices, shards(): lax.ppermute(a, 'role', pairs)  10.8 us
    unnamed x20, local copies, waits for them, and re-layouts  4.22 us
  transfers between devices with their start and end apart: 32, of which 13 were waited for; matrix products, arithmetic and copies ran while one was open for 2% of the time, Pallas kernels for 54%

profile of v2, /device:TPU:24, one launch (start us, length us, event | category | flops | bytes accessed | tf_op | source)
XLA Modules:
  0.0 137.3 jit_solution(17072908555106652782)
XLA Ops:
  0.6 0.9 copy-done.5
  1.6 0.9 copy-done.6
  2.5 0.5 shard_map.113
  3.0 1.6 %collective-permute-start.22 = (bf16[2,2,256,128]{3,2,1,0:T(8,128)(2,1)S(1)}, bf16[2,2,256,128]{3,2,1,0:T(8,128)(2,1)S(1)}, u32[]{:S(2)}, u32[]{:S(2)}) collective-permute-start(bf16[2,2,256,128]{3,2,1,0:T(8,128)(2,1)S(1)} %get-tuple-element.4.refs_1_.refs_9_), channel_id=1, source_target_pairs={{0,16},{8,24},{16,0},{24,8},{1,17},{9,25},{17,1},{25,9},{2,18},{10... | collective-permute-start | bytes 786440 | tf_op jit(solution)/shard_map/ppermute | solution.py:498
  4.6 0.3 collective-permute-start
  4.9 0.5 collective-permute-start.10
  5.5 6.8 %collective-permute-done.22.refs_17_ = bf16[2,2,256,128]{3,2,1,0:T(8,128)(2,1)S(1)} collective-permute-done((bf16[2,2,256,128]{3,2,1,0:T(8,128)(2,1)S(1)}, bf16[2,2,256,128]{3,2,1,0:T(8,128)(2,1)S(1)}, u32[]{:S(2)}, u32[]{:S(2)}) %collective-permute-start.22) | collective-permute-done | bytes 262176 | tf_op jit(solution)/shard_map/ppermute | solution.py:498
  12.3 0.3 collective-permute-start.3
  12.6 1.1 collective-permute-done.refs_2_.refs_10_
  13.7 0.5 collective-permute-start.23
  14.2 3.5 %collective-permute-done.10.refs_17_ = bf16[2,2,256,128]{3,2,1,0:T(8,128)(2,1)S(1)} collective-permute-done((bf16[2,2,256,128]{3,2,1,0:T(8,128)(2,1)S(1)}, bf16[2,2,256,128]{3,2,1,0:T(8,128)(2,1)S(1)}, u32[]{:S(2)}, u32[]{:S(2)}) %collective-permute-start.10) | collective-permute-done | bytes 262176 | tf_op jit(solution)/shard_map/ppermute | solution.py:498
  17.7 1.2 collective-permute-done.3.refs_2_.refs_10_
  18.9 1.2 collective-permute-start.11
  20.2 2.5 %collective-permute-done.23.refs_18_ = bf16[2,2,256,128]{3,2,1,0:T(8,128)(2,1)S(1)} collective-permute-done((bf16[2,2,256,128]{3,2,1,0:T(8,128)(2,1)S(1)}, bf16[2,2,256,128]{3,2,1,0:T(8,128)(2,1)S(1)}, u32[]{:S(2)}, u32[]{:S(2)}) %collective-permute-start.23) | collective-permute-done | bytes 262176 | tf_op jit(solution)/shard_map/ppermute | solution.py:498
  22.7 4.2 %collective-permute-done.1.refs_3_.refs_11_ = bf16[2,2,256,128]{3,2,1,0:T(8,128)(2,1)} collective-permute-done((bf16[2,2,256,128]{3,2,1,0:T(8,128)(2,1)S(1)}, bf16[2,2,256,128]{3,2,1,0:T(8,128)(2,1)}, u32[]{:S(2)}, u32[]{:S(2)}) %collective-permute-start.1) | collective-permute-done | bytes 262176 | tf_op jit(solution)/shard_map/ppermute | solution.py:493
  26.9 1.0 collective-permute-start.2
  28.0 1.6 %collective-permute-start.24 = (bf16[2,2,256,128]{3,2,1,0:T(8,128)(2,1)}, bf16[2,2,256,128]{3,2,1,0:T(8,128)(2,1)}, u32[]{:S(2)}, u32[]{:S(2)}) collective-permute-start(bf16[2,2,256,128]{3,2,1,0:T(8,128)(2,1)} %collective-permute-done.1.refs_3_.refs_11_), channel_id=1, source_target_pairs={{0,16},{8,24},{16,0},{24,8},{1,17},{9,25},{17,1},{25,9},{2,18},{10... | collective-permute-start | bytes 786440 | tf_op jit(solution)/shard_map/ppermute | solution.py:498
  29.6 0.7 copy-done.3
  30.3 0.2 collective-permute-start.20
  30.5 2.1 %collective-permute-done.4.refs_3_.refs_11_ = bf16[2,2,256,128]{3,2,1,0:T(8,128)(2,1)} collective-permute-done((bf16[2,2,256,128]{3,2,1,0:T(8,128)(2,1)S(1)}, bf16[2,2,256,128]{3,2,1,0:T(8,128)(2,1)}, u32[]{:S(2)}, u32[]{:S(2)}) %collective-permute-start.4) | collective-permute-done | bytes 262176 | tf_op jit(solution)/shard_map/ppermute | solution.py:493
  32.5 1.0 collective-permute-start.5
  33.5 4.6 %collective-permute-done.2.refs_4_.refs_12_ = bf16[2,2,256,128]{3,2,1,0:T(8,128)(2,1)} collective-permute-done((bf16[2,2,256,128]{3,2,1,0:T(8,128)(2,1)}, bf16[2,2,256,128]{3,2,1,0:T(8,128)(2,1)}, u32[]{:S(2)}, u32[]{:S(2)}) %collective-permute-start.2) | collective-permute-done | bytes 262176 | tf_op jit(solution)/shard_map/ppermute | solution.py:493
  38.1 1.5 %collective-permute-start.25 = (bf16[2,2,256,128]{3,2,1,0:T(8,128)(2,1)}, bf16[2,2,256,128]{3,2,1,0:T(8,128)(2,1)}, u32[]{:S(2)}, u32[]{:S(2)}) collective-permute-start(bf16[2,2,256,128]{3,2,1,0:T(8,128)(2,1)} %collective-permute-done.2.refs_4_.refs_12_), channel_id=1, source_target_pairs={{0,16},{8,24},{16,0},{24,8},{1,17},{9,25},{17,1},{25,9},{2,18},{10... | collective-permute-start | bytes 786440 | tf_op jit(solution)/shard_map/ppermute | solution.py:498
  39.6 0.7 fusion.12
  40.3 0.7 add_select_fusion
  41.1 0.6 collective-permute-start.12
  41.7 0.5 collective-permute-start.28
  42.2 1.2 collective-permute-done.5.refs_4_.refs_12_
  43.4 1.5 %collective-permute-start.13 = (bf16[2,2,256,128]{3,2,1,0:T(8,128)(2,1)}, bf16[2,2,256,128]{3,2,1,0:T(8,128)(2,1)}, u32[]{:S(2)}, u32[]{:S(2)}) collective-permute-start(bf16[2,2,256,128]{3,2,1,0:T(8,128)(2,1)} %collective-permute-done.5.refs_4_.refs_12_), channel_id=1, source_target_pairs={{0,16},{8,24},{16,0},{24,8},{1,17},{9,25},{17,1},{25,9},{2,18},{10... | collective-permute-start | bytes 786440 | tf_op jit(solution)/shard_map/ppermute | solution.py:498
  44.9 2.8 %collective-permute-done.25.refs_20_ = bf16[2,2,256,128]{3,2,1,0:T(8,128)(2,1)} collective-permute-done((bf16[2,2,256,128]{3,2,1,0:T(8,128)(2,1)}, bf16[2,2,256,128]{3,2,1,0:T(8,128)(2,1)}, u32[]{:S(2)}, u32[]{:S(2)}) %collective-permute-start.25) | collective-permute-done | bytes 262176 | tf_op jit(solution)/shard_map/ppermute | solution.py:498
  47.7 0.6 compare_select_fusion.3.earlier_ref
  48.4 0.1 broadcast_in_dim.20
  48.6 0.1 reshape.22.refs_0_
  48.8 0.1 select_reduce_fusion.refs_1_
  49.0 4.3 %collective-permute-done.12.refs_19_ = bf16[2,2,256,128]{3,2,1,0:T(8,128)(2,1)} collective-permute-done((bf16[2,2,256,128]{3,2,1,0:T(8,128)(2,1)}, bf16[2,2,256,128]{3,2,1,0:T(8,128)(2,1)}, u32[]{:S(2)}, u32[]{:S(2)}) %collective-permute-start.12) | collective-permute-done | bytes 262176 | tf_op jit(solution)/shard_map/ppermute | solution.py:498
  53.3 0.5 collective-permute-start.15
  53.9 3.3 %collective-permute-done.13.refs_20_ = bf16[2,2,256,128]{3,2,1,0:T(8,128)(2,1)} collective-permute-done((bf16[2,2,256,128]{3,2,1,0:T(8,128)(2,1)}, bf16[2,2,256,128]{3,2,1,0:T(8,128)(2,1)}, u32[]{:S(2)}, u32[]{:S(2)}) %collective-permute-start.13) | collective-permute-done | bytes 262176 | tf_op jit(solution)/shard_map/ppermute | solution.py:498
  57.3 0.5 collective-permute-start.17
  57.8 1.6 %copy-done.8 = bf16[1,256,32,128]{3,2,1,0:T(8,128)(2,1)S(1)} copy-done((bf16[1,256,32,128]{3,2,1,0:T(8,128)(2,1)S(1)}, bf16[1,256,32,128]{3,2,1,0:T(8,128)(2,1)}, u32[]{:S(2)}) %copy-start.8) | copy-done | bytes 2097176
  59.4 16.1 %shard_map.114.refs_5_ = bf16[1,256,32,128]{3,2,1,0:T(8,128)(2,1)} custom-call(s32[4]{0:T(128)S(1)} %compare_select_fusion.3.earlier_ref, bf16[1,256,32,128]{3,2,1,0:T(8,128)(2,1)S(1)} %copy-done.8, bf16[2,2,256,128]{3,2,1,0:T(8,128)(2,1)S(1)} %get-tuple-element.5.refs_1_.refs_9_, bf16[2,2,256,128]{3,2,1,0:T(8,128)(2,1)S(1)} %collective-permute-done.3.refs_2_.refs_10_, ...), custom_call_target="tpu_custom_call" | custom-call | flops 8589934592 | bytes 4000000 | tf_op jit(solution)/shard_map/pallas_call | solution.py:163
  75.5 10.4 %shard_map.119 = bf16[16,64,128]{2,1,0:T(8,128)(2,1)S(1)} custom-call(s32[128]{0:T(128)S(1)} %reshape.22.refs_0_, s32[16]{0:T(128)S(1)} %select_reduce_fusion.refs_1_, s32[32]{0:T(128)S(1)} %copy-done.7, s32[2]{0:T(128)S(1)} %pad_add_fusion.refs_3_.meta_ref, bf16[32,128,128]{2,1,0:T(8,128)(2,1)S(1)} %bitcast.9, bf16[32,16,128]{2,1,0:T(8,128)(2,1)S(1)} %bitcast.13, ...), custom_call_target="tpu_custom_call" | custom-call | flops 1342177280 | bytes 8000000 | tf_op jit(solution)/shard_map/pallas_call | solution.py:380
  86.0 1.6 %collective-permute-start.31 = (bf16[16,64,128]{2,1,0:T(8,128)(2,1)S(1)}, bf16[16,64,128]{2,1,0:T(8,128)(2,1)S(1)}, u32[]{:S(2)}, u32[]{:S(2)}) collective-permute-start(bf16[16,64,128]{2,1,0:T(8,128)(2,1)S(1)} %shard_map.119), channel_id=1, source_target_pairs={{0,1},{1,0},{2,3},{3,2},{4,5},{5,4},{6,7},{7,6},{8,9},{9,8},{10,11... | collective-permute-start | bytes 786440 | tf_op jit(solution)/shard_map/ppermute | solution.py:530
  87.6 10.3 %shard_map.118 = bf16[16,64,128]{2,1,0:T(8,128)(2,1)S(1)} custom-call(s32[128]{0:T(128)S(1)} %reshape.22.refs_0_, s32[16]{0:T(128)S(1)} %select_reduce_fusion.refs_1_, s32[32]{0:T(128)S(1)} %copy-done.7, s32[2]{0:T(128)S(1)} %pad_add_fusion.refs_3_.meta_ref, bf16[32,128,128]{2,1,0:T(8,128)(2,1)S(1)} %bitcast.10, bf16[32,16,128]{2,1,0:T(8,128)(2,1)S(1)} %bitcast.14, ...), custom_call_target="tpu_custom_call" | custom-call | flops 1342177280 | bytes 8000000 | tf_op jit(solution)/shard_map/pallas_call | solution.py:380
  97.9 0.6 collective-permute-start.30
  98.5 16.1 %shard_map.115 = bf16[1,256,32,128]{3,2,1,0:T(8,128)(2,1)} custom-call(s32[4]{0:T(128)S(1)} %compare_select_fusion.3.earlier_ref, bf16[1,256,32,128]{3,2,1,0:T(8,128)(2,1)S(1)} %copy-done.9, bf16[2,2,256,128]{3,2,1,0:T(8,128)(2,1)S(1)} %get-tuple-element.4.refs_1_.refs_9_, ...), custom_call_target="tpu_custom_call", output_to_operand_aliasing={{}: (6, {})} | custom-call | flops 8589934592 | bytes 4000000 | tf_op jit(solution)/shard_map/pallas_call | solution.py:163
  114.6 10.4 %shard_map.117.refs_1_ = bf16[16,64,128]{2,1,0:T(8,128)(2,1)S(1)} custom-call(s32[128]{0:T(128)S(1)} %reshape.22.refs_0_, s32[16]{0:T(128)S(1)} %select_reduce_fusion.refs_1_, s32[32]{0:T(128)S(1)} %copy-done.7, s32[2]{0:T(128)S(1)} %pad_add_fusion.refs_3_.meta_ref, bf16[32,128,128]{2,1,0:T(8,128)(2,1)S(1)} %bitcast.11, bf16[32,16,128]{2,1,0:T(8,128)(2,1)S(1)} %bitcast.15, ...), custom_call_target="tpu_custom_call" | custom-call | flops 1342177280 | bytes 8000000 | tf_op jit(solution)/shard_map/pallas_call | solution.py:380
  125.0 10.3 %shard_map.116.refs_0_ = bf16[16,64,128]{2,1,0:T(8,128)(2,1)S(1)} custom-call(s32[128]{0:T(128)S(1)} %reshape.22.refs_0_, s32[16]{0:T(128)S(1)} %select_reduce_fusion.refs_1_, s32[32]{0:T(128)S(1)} %copy-done.7, s32[2]{0:T(128)S(1)} %pad_add_fusion.refs_3_.meta_ref, bf16[32,128,128]{2,1,0:T(8,128)(2,1)S(1)} %bitcast.12, bf16[32,16,128]{2,1,0:T(8,128)(2,1)S(1)} %bitcast.16, ...), custom_call_target="tpu_custom_call" | custom-call | flops 1342177280 | bytes 8000000 | tf_op jit(solution)/shard_map/pallas_call | solution.py:380
  135.4 1.9 %shard_map.120 = bf16[16,4,8192]{2,1,0:T(4,128)(2,1)} custom-call(s32[2]{0:T(128)S(1)} %pad_add_fusion.refs_3_.meta_ref, bf16[16,64,128]{2,1,0:T(8,128)(2,1)S(1)} %shard_map.116.refs_0_, bf16[16,64,128]{2,1,0:T(8,128)(2,1)S(1)} %shard_map.117.refs_1_, bf16[16,64,128]{2,1,0:T(8,128)(2,1)S(1)} %collective-permute-done.30.refs_2_, ...), custom_call_target="tpu_custom_call" | custom-call | bytes 2000000 | tf_op jit(solution)/shard_map/pallas_call | solution.py:441
  (53 shorter events, 0.6 us)
Async XLA Ops:
  0.6 1.0 copy-start.5
  1.6 0.9 copy-start.6
  3.0 9.3 %collective-permute-start.22 = (bf16[2,2,256,128]{3,2,1,0:T(8,128)(2,1)S(1)}, bf16[2,2,256,128]{3,2,1,0:T(8,128)(2,1)S(1)}, u32[]{:S(2)}, u32[]{:S(2)}) collective-permute-start(bf16[2,2,256,128]{3,2,1,0:T(8,128)(2,1)S(1)} %get-tuple-element.4.refs_1_.refs_9_), channel_id=1, source_target_pairs={{0,16},{8,24},{16,0},{24,8},{1,17},{9,25},{17,1},{25,9},{2,18},{10... | collective-permute-start | bytes 786440 | tf_op jit(solution)/shard_map/ppermute | solution.py:498
  4.6 8.0 %collective-permute-start.18 = (bf16[2,2,256,128]{3,2,1,0:T(8,128)(2,1)S(1)}, bf16[2,2,256,128]{3,2,1,0:T(8,128)(2,1)S(1)}, u32[]{:S(2)}, u32[]{:S(2)}) collective-permute-start(bf16[2,2,256,128]{3,2,1,0:T(8,128)(2,1)S(1)} %get-tuple-element.4.refs_1_.refs_9_), channel_id=1, source_target_pairs={{0,8},{8,0},{16,24},{24,16},{1,9},{9,1},{17,25},{25,17},{2,10},{10... | collective-permute-start | bytes 786440 | tf_op jit(solution)/shard_map/ppermute | solution.py:498
  4.6 9.1 %collective-permute-start = (bf16[2,2,256,128]{3,2,1,0:T(8,128)(2,1)S(1)}, bf16[2,2,256,128]{3,2,1,0:T(8,128)(2,1)S(1)}, u32[]{:S(2)}, u32[]{:S(2)}) collective-permute-start(bf16[2,2,256,128]{3,2,1,0:T(8,128)(2,1)S(1)} %get-tuple-element.4.refs_1_.refs_9_), channel_id=1, source_target_pairs={{0,4},{4,6},{6,2},{2,0},{1,5},{5,7},{7,3},{3,1},{8,12},{12,14},{14... | collective-permute-start | bytes 786440 | tf_op jit(solution)/shard_map/ppermute | solution.py:493
  4.9 12.8 %collective-permute-start.10 = (bf16[2,2,256,128]{3,2,1,0:T(8,128)(2,1)S(1)}, bf16[2,2,256,128]{3,2,1,0:T(8,128)(2,1)S(1)}, u32[]{:S(2)}, u32[]{:S(2)}) collective-permute-start(bf16[2,2,256,128]{3,2,1,0:T(8,128)(2,1)S(1)} %get-tuple-element.5.refs_1_.refs_9_), channel_id=1, source_target_pairs={{0,16},{8,24},{16,0},{24,8},{1,17},{9,25},{17,1},{25,9},{2,18},{10... | collective-permute-start | bytes 786440 | tf_op jit(solution)/shard_map/ppermute | solution.py:498
  5.4 12.3 %collective-permute-start.6 = (bf16[2,2,256,128]{3,2,1,0:T(8,128)(2,1)S(1)}, bf16[2,2,256,128]{3,2,1,0:T(8,128)(2,1)S(1)}, u32[]{:S(2)}, u32[]{:S(2)}) collective-permute-start(bf16[2,2,256,128]{3,2,1,0:T(8,128)(2,1)S(1)} %get-tuple-element.5.refs_1_.refs_9_), channel_id=1, source_target_pairs={{0,8},{8,0},{16,24},{24,16},{1,9},{9,1},{17,25},{25,17},{2,10},{10... | collective-permute-start | bytes 786440 | tf_op jit(solution)/shard_map/ppermute | solution.py:498
  12.3 6.6 %collective-permute-start.3 = (bf16[2,2,256,128]{3,2,1,0:T(8,128)(2,1)S(1)}, bf16[2,2,256,128]{3,2,1,0:T(8,128)(2,1)S(1)}, u32[]{:S(2)}, u32[]{:S(2)}) collective-permute-start(bf16[2,2,256,128]{3,2,1,0:T(8,128)(2,1)S(1)} %get-tuple-element.5.refs_1_.refs_9_), channel_id=1, source_target_pairs={{0,4},{4,6},{6,2},{2,0},{1,5},{5,7},{7,3},{3,1},{8,12},{12,14},{14... | collective-permute-start | bytes 786440 | tf_op jit(solution)/shard_map/ppermute | solution.py:493
  12.6 6.3 %collective-permute-start.26 = (bf16[2,2,256,128]{3,2,1,0:T(8,128)(2,1)S(1)}, bf16[2,2,256,128]{3,2,1,0:T(8,128)(2,1)S(1)}, u32[]{:S(2)}, u32[]{:S(2)}) collective-permute-start(bf16[2,2,256,128]{3,2,1,0:T(8,128)(2,1)S(1)} %collective-permute-done.22.refs_17_), channel_id=1, source_target_pairs={{0,8},{8,0},{16,24},{24,16},{1,9},{9,1},{17,25},{25,17},{2,10},{10... | collective-permute-start | bytes 786440 | tf_op jit(solution)/shard_map/ppermute | solution.py:498
  13.7 9.0 %collective-permute-start.23 = (bf16[2,2,256,128]{3,2,1,0:T(8,128)(2,1)S(1)}, bf16[2,2,256,128]{3,2,1,0:T(8,128)(2,1)S(1)}, u32[]{:S(2)}, u32[]{:S(2)}) collective-permute-start(bf16[2,2,256,128]{3,2,1,0:T(8,128)(2,1)S(1)} %collective-permute-done.refs_2_.refs_10_), channel_id=1, source_target_pairs={{0,16},{8,24},{16,0},{24,8},{1,17},{9,25},{17,1},{25,9},{2,18},{10... | collective-permute-start | bytes 786440 | tf_op jit(solution)/shard_map/ppermute | solution.py:498
  17.7 4.9 %collective-permute-start.19 = (bf16[2,2,256,128]{3,2,1,0:T(8,128)(2,1)S(1)}, bf16[2,2,256,128]{3,2,1,0:T(8,128)(2,1)S(1)}, u32[]{:S(2)}, u32[]{:S(2)}) collective-permute-start(bf16[2,2,256,128]{3,2,1,0:T(8,128)(2,1)S(1)} %collective-permute-done.refs_2_.refs_10_), channel_id=1, source_target_pairs={{0,8},{8,0},{16,24},{24,16},{1,9},{9,1},{17,25},{25,17},{2,10},{10... | collective-permute-start | bytes 786440 | tf_op jit(solution)/shard_map/ppermute | solution.py:498
  17.7 9.2 %collective-permute-start.1 = (bf16[2,2,256,128]{3,2,1,0:T(8,128)(2,1)S(1)}, bf16[2,2,256,128]{3,2,1,0:T(8,128)(2,1)}, u32[]{:S(2)}, u32[]{:S(2)}) collective-permute-start(bf16[2,2,256,128]{3,2,1,0:T(8,128)(2,1)S(1)} %collective-permute-done.refs_2_.refs_10_), channel_id=1, source_target_pairs={{0,4},{4,6},{6,2},{2,0},{1,5},{5,7},{7,3},{3,1},{8,12},{12,14},{14... | collective-permute-start | bytes 786440 | tf_op jit(solution)/shard_map/ppermute | solution.py:493
  18.9 9.0 %collective-permute-start.14 = (bf16[2,2,256,128]{3,2,1,0:T(8,128)(2,1)S(1)}, bf16[2,2,256,128]{3,2,1,0:T(8,128)(2,1)S(1)}, u32[]{:S(2)}, u32[]{:S(2)}) collective-permute-start(bf16[2,2,256,128]{3,2,1,0:T(8,128)(2,1)S(1)} %collective-permute-done.10.refs_17_), channel_id=1, source_target_pairs={{0,8},{8,0},{16,24},{24,16},{1,9},{9,1},{17,25},{25,17},{2,10},{10... | collective-permute-start | bytes 786440 | tf_op jit(solution)/shard_map/ppermute | solution.py:498
  18.9 9.1 %collective-permute-start.11 = (bf16[2,2,256,128]{3,2,1,0:T(8,128)(2,1)S(1)}, bf16[2,2,256,128]{3,2,1,0:T(8,128)(2,1)S(1)}, u32[]{:S(2)}, u32[]{:S(2)}) collective-permute-start(bf16[2,2,256,128]{3,2,1,0:T(8,128)(2,1)S(1)} %collective-permute-done.3.refs_2_.refs_10_), channel_id=1, source_target_pairs={{0,16},{8,24},{16,0},{24,8},{1,17},{9,25},{17,1},{25,9},{2,18},{10... | collective-permute-start | bytes 786440 | tf_op jit(solution)/shard_map/ppermute | solution.py:498
  22.6 7.0 %collective-permute-start.7 = (bf16[2,2,256,128]{3,2,1,0:T(8,128)(2,1)S(1)}, bf16[2,2,256,128]{3,2,1,0:T(8,128)(2,1)S(1)}, u32[]{:S(2)}, u32[]{:S(2)}) collective-permute-start(bf16[2,2,256,128]{3,2,1,0:T(8,128)(2,1)S(1)} %collective-permute-done.3.refs_2_.refs_10_), channel_id=1, source_target_pairs={{0,8},{8,0},{16,24},{24,16},{1,9},{9,1},{17,25},{25,17},{2,10},{10... | collective-permute-start | bytes 786440 | tf_op jit(solution)/shard_map/ppermute | solution.py:498
  22.6 9.9 %collective-permute-start.4 = (bf16[2,2,256,128]{3,2,1,0:T(8,128)(2,1)S(1)}, bf16[2,2,256,128]{3,2,1,0:T(8,128)(2,1)}, u32[]{:S(2)}, u32[]{:S(2)}) collective-permute-start(bf16[2,2,256,128]{3,2,1,0:T(8,128)(2,1)S(1)} %collective-permute-done.3.refs_2_.refs_10_), channel_id=1, source_target_pairs={{0,4},{4,6},{6,2},{2,0},{1,5},{5,7},{7,3},{3,1},{8,12},{12,14},{14... | collective-permute-start | bytes 786440 | tf_op jit(solution)/shard_map/ppermute | solution.py:493
  26.9 11.2 %collective-permute-start.2 = (bf16[2,2,256,128]{3,2,1,0:T(8,128)(2,1)}, bf16[2,2,256,128]{3,2,1,0:T(8,128)(2,1)}, u32[]{:S(2)}, u32[]{:S(2)}) collective-permute-start(bf16[2,2,256,128]{3,2,1,0:T(8,128)(2,1)} %collective-permute-done.1.refs_3_.refs_11_), channel_id=1, source_target_pairs={{0,4},{4,6},{6,2},{2,0},{1,5},{5,7},{7,3},{3,1},{8,12},{12,14},{14... | collective-permute-start | bytes 786440 | tf_op jit(solution)/shard_map/ppermute | solution.py:493
  27.9 13.2 %collective-permute-start.27 = (bf16[2,2,256,128]{3,2,1,0:T(8,128)(2,1)S(1)}, bf16[2,2,256,128]{3,2,1,0:T(8,128)(2,1)}, u32[]{:S(2)}, u32[]{:S(2)}) collective-permute-start(bf16[2,2,256,128]{3,2,1,0:T(8,128)(2,1)S(1)} %collective-permute-done.23.refs_18_), channel_id=1, source_target_pairs={{0,8},{8,0},{16,24},{24,16},{1,9},{9,1},{17,25},{25,17},{2,10},{10... | collective-permute-start | bytes 786440 | tf_op jit(solution)/shard_map/ppermute | solution.py:498
  28.0 13.7 %collective-permute-start.24 = (bf16[2,2,256,128]{3,2,1,0:T(8,128)(2,1)}, bf16[2,2,256,128]{3,2,1,0:T(8,128)(2,1)}, u32[]{:S(2)}, u32[]{:S(2)}) collective-permute-start(bf16[2,2,256,128]{3,2,1,0:T(8,128)(2,1)} %collective-permute-done.1.refs_3_.refs_11_), channel_id=1, source_target_pairs={{0,16},{8,24},{16,0},{24,8},{1,17},{9,25},{17,1},{25,9},{2,18},{10... | collective-permute-start | bytes 786440 | tf_op jit(solution)/shard_map/ppermute | solution.py:498
  29.6 0.7 copy-start.3
  30.3 11.4 %collective-permute-start.20 = (bf16[2,2,256,128]{3,2,1,0:T(8,128)(2,1)}, bf16[2,2,256,128]{3,2,1,0:T(8,128)(2,1)}, u32[]{:S(2)}, u32[]{:S(2)}) collective-permute-start(bf16[2,2,256,128]{3,2,1,0:T(8,128)(2,1)} %collective-permute-done.1.refs_3_.refs_11_), channel_id=1, source_target_pairs={{0,8},{8,0},{16,24},{24,16},{1,9},{9,1},{17,25},{25,17},{2,10},{10... | collective-permute-start | bytes 786440 | tf_op jit(solution)/shard_map/ppermute | solution.py:498
  32.5 10.9 %collective-permute-start.5 = (bf16[2,2,256,128]{3,2,1,0:T(8,128)(2,1)}, bf16[2,2,256,128]{3,2,1,0:T(8,128)(2,1)}, u32[]{:S(2)}, u32[]{:S(2)}) collective-permute-start(bf16[2,2,256,128]{3,2,1,0:T(8,128)(2,1)} %collective-permute-done.4.refs_3_.refs_11_), channel_id=1, source_target_pairs={{0,4},{4,6},{6,2},{2,0},{1,5},{5,7},{7,3},{3,1},{8,12},{12,14},{14... | collective-permute-start | bytes 786440 | tf_op jit(solution)/shard_map/ppermute | solution.py:493
  38.1 9.6 %collective-permute-start.25 = (bf16[2,2,256,128]{3,2,1,0:T(8,128)(2,1)}, bf16[2,2,256,128]{3,2,1,0:T(8,128)(2,1)}, u32[]{:S(2)}, u32[]{:S(2)}) collective-permute-start(bf16[2,2,256,128]{3,2,1,0:T(8,128)(2,1)} %collective-permute-done.2.refs_4_.refs_12_), channel_id=1, source_target_pairs={{0,16},{8,24},{16,0},{24,8},{1,17},{9,25},{17,1},{25,9},{2,18},{10... | collective-permute-start | bytes 786440 | tf_op jit(solution)/shard_map/ppermute | solution.py:498
  41.1 12.3 %collective-permute-start.12 = (bf16[2,2,256,128]{3,2,1,0:T(8,128)(2,1)}, bf16[2,2,256,128]{3,2,1,0:T(8,128)(2,1)}, u32[]{:S(2)}, u32[]{:S(2)}) collective-permute-start(bf16[2,2,256,128]{3,2,1,0:T(8,128)(2,1)} %collective-permute-done.4.refs_3_.refs_11_), channel_id=1, source_target_pairs={{0,16},{8,24},{16,0},{24,8},{1,17},{9,25},{17,1},{25,9},{2,18},{10... | collective-permute-start | bytes 786440 | tf_op jit(solution)/shard_map/ppermute | solution.py:498
  41.7 12.2 %collective-permute-start.21 = (bf16[2,2,256,128]{3,2,1,0:T(8,128)(2,1)}, bf16[2,2,256,128]{3,2,1,0:T(8,128)(2,1)}, u32[]{:S(2)}, u32[]{:S(2)}) collective-permute-start(bf16[2,2,256,128]{3,2,1,0:T(8,128)(2,1)} %collective-permute-done.2.refs_4_.refs_12_), channel_id=1, source_target_pairs={{0,8},{8,0},{16,24},{24,16},{1,9},{9,1},{17,25},{25,17},{2,10},{10... | collective-permute-start | bytes 786440 | tf_op jit(solution)/shard_map/ppermute | solution.py:498
  41.7 11.7 %collective-permute-start.28 = (bf16[2,2,256,128]{3,2,1,0:T(8,128)(2,1)}, bf16[2,2,256,128]{3,2,1,0:T(8,128)(2,1)}, u32[]{:S(2)}, u32[]{:S(2)}) collective-permute-start(bf16[2,2,256,128]{3,2,1,0:T(8,128)(2,1)} %collective-permute-done.24.refs_19_), channel_id=1, source_target_pairs={{0,8},{8,0},{16,24},{24,16},{1,9},{9,1},{17,25},{25,17},{2,10},{10... | collective-permute-start | bytes 786440 | tf_op jit(solution)/shard_map/ppermute | solution.py:498
  43.4 13.9 %collective-permute-start.13 = (bf16[2,2,256,128]{3,2,1,0:T(8,128)(2,1)}, bf16[2,2,256,128]{3,2,1,0:T(8,128)(2,1)}, u32[]{:S(2)}, u32[]{:S(2)}) collective-permute-start(bf16[2,2,256,128]{3,2,1,0:T(8,128)(2,1)} %collective-permute-done.5.refs_4_.refs_12_), channel_id=1, source_target_pairs={{0,16},{8,24},{16,0},{24,8},{1,17},{9,25},{17,1},{25,9},{2,18},{10... | collective-permute-start | bytes 786440 | tf_op jit(solution)/shard_map/ppermute | solution.py:498
  47.7 9.6 %collective-permute-start.29 = (bf16[2,2,256,128]{3,2,1,0:T(8,128)(2,1)}, bf16[2,2,256,128]{3,2,1,0:T(8,128)(2,1)}, u32[]{:S(2)}, u32[]{:S(2)}) collective-permute-start(bf16[2,2,256,128]{3,2,1,0:T(8,128)(2,1)} %collective-permute-done.25.refs_20_), channel_id=1, source_target_pairs={{0,8},{8,0},{16,24},{24,16},{1,9},{9,1},{17,25},{25,17},{2,10},{10... | collective-permute-start | bytes 786440 | tf_op jit(solution)/shard_map/ppermute | solution.py:498
  48.9 26.6 %copy-start = (bf16[32,4,32,128]{3,2,1,0:T(8,128)(2,1)S(1)}, bf16[32,4,32,128]{3,2,1,0:T(8,128)(2,1)}, u32[]{:S(2)}) copy-start(bf16[32,4,32,128]{3,2,1,0:T(8,128)(2,1)} %param.13) | copy-start | bytes 3145732
  48.9 26.6 %copy-start.1 = (bf16[32,4,4,128]{3,2,1,0:T(4,128)(2,1)S(1)}, bf16[32,4,4,128]{3,2,1,0:T(4,128)(2,1)}, u32[]{:S(2)}) copy-start(bf16[32,4,4,128]{3,2,1,0:T(4,128)(2,1)} %param.14) | copy-start | bytes 393220
  49.0 26.6 %copy-start.2 = (bf16[32,4,4,128]{3,2,1,0:T(4,128)(2,1)S(1)}, bf16[32,4,4,128]{3,2,1,0:T(4,128)(2,1)}, u32[]{:S(2)}) copy-start(bf16[32,4,4,128]{3,2,1,0:T(4,128)(2,1)} %param.15) | copy-start | bytes 393220
  49.0 26.6 %copy-start.7 = (s32[32]{0:T(128)S(1)}, s32[32]{0:T(128)}, u32[]{:S(2)}) copy-start(s32[32]{0:T(128)} %refs_2_.7) | copy-start | bytes 388
  53.3 34.2 %collective-permute-start.8 = (bf16[2,2,256,128]{3,2,1,0:T(8,128)(2,1)}, bf16[2,2,256,128]{3,2,1,0:T(8,128)(2,1)S(1)}, u32[]{:S(2)}, u32[]{:S(2)}) collective-permute-start(bf16[2,2,256,128]{3,2,1,0:T(8,128)(2,1)} %collective-permute-done.4.refs_3_.refs_11_), channel_id=1, source_target_pairs={{0,8},{8,0},{16,24},{24,16},{1,9},{9,1},{17,25},{25,17},{2,10},{10... | collective-permute-start | bytes 786440 | tf_op jit(solution)/shard_map/ppermute | solution.py:498
  53.3 32.6 %collective-permute-start.15 = (bf16[2,2,256,128]{3,2,1,0:T(8,128)(2,1)S(1)}, bf16[2,2,256,128]{3,2,1,0:T(8,128)(2,1)S(1)}, u32[]{:S(2)}, u32[]{:S(2)}) collective-permute-start(bf16[2,2,256,128]{3,2,1,0:T(8,128)(2,1)S(1)} %collective-permute-done.11.refs_18_), channel_id=1, source_target_pairs={{0,8},{8,0},{16,24},{24,16},{1,9},{9,1},{17,25},{25,17},{2,10},{10... | collective-permute-start | bytes 786440 | tf_op jit(solution)/shard_map/ppermute | solution.py:498
  53.8 33.7 %collective-permute-start.9 = (bf16[2,2,256,128]{3,2,1,0:T(8,128)(2,1)}, bf16[2,2,256,128]{3,2,1,0:T(8,128)(2,1)S(1)}, u32[]{:S(2)}, u32[]{:S(2)}) collective-permute-start(bf16[2,2,256,128]{3,2,1,0:T(8,128)(2,1)} %collective-permute-done.5.refs_4_.refs_12_), channel_id=1, source_target_pairs={{0,8},{8,0},{16,24},{24,16},{1,9},{9,1},{17,25},{25,17},{2,10},{10... | collective-permute-start | bytes 786440 | tf_op jit(solution)/shard_map/ppermute | solution.py:498
  57.2 30.3 %collective-permute-start.16 = (bf16[2,2,256,128]{3,2,1,0:T(8,128)(2,1)}, bf16[2,2,256,128]{3,2,1,0:T(8,128)(2,1)S(1)}, u32[]{:S(2)}, u32[]{:S(2)}) collective-permute-start(bf16[2,2,256,128]{3,2,1,0:T(8,128)(2,1)} %collective-permute-done.12.refs_19_), channel_id=1, source_target_pairs={{0,8},{8,0},{16,24},{24,16},{1,9},{9,1},{17,25},{25,17},{2,10},{10... | collective-permute-start | bytes 786440 | tf_op jit(solution)/shard_map/ppermute | solution.py:498
  57.3 30.3 %collective-permute-start.17 = (bf16[2,2,256,128]{3,2,1,0:T(8,128)(2,1)}, bf16[2,2,256,128]{3,2,1,0:T(8,128)(2,1)S(1)}, u32[]{:S(2)}, u32[]{:S(2)}) collective-permute-start(bf16[2,2,256,128]{3,2,1,0:T(8,128)(2,1)} %collective-permute-done.13.refs_20_), channel_id=1, source_target_pairs={{0,8},{8,0},{16,24},{24,16},{1,9},{9,1},{17,25},{25,17},{2,10},{10... | collective-permute-start | bytes 786440 | tf_op jit(solution)/shard_map/ppermute | solution.py:498
  57.8 1.6 %copy-start.8 = (bf16[1,256,32,128]{3,2,1,0:T(8,128)(2,1)S(1)}, bf16[1,256,32,128]{3,2,1,0:T(8,128)(2,1)}, u32[]{:S(2)}) copy-start(bf16[1,256,32,128]{3,2,1,0:T(8,128)(2,1)} %refs_0_.3) | copy-start | bytes 6291460
  75.5 12.0 %copy-start.4 = (bf16[2,2,256,128]{3,2,1,0:T(8,128)(2,1)S(1)}, bf16[2,2,256,128]{3,2,1,0:T(8,128)(2,1)}, u32[]{:S(2)}) copy-start(bf16[2,2,256,128]{3,2,1,0:T(8,128)(2,1)} %copy-done.3) | copy-start | bytes 786436
  85.9 12.6 %copy-start.9 = (bf16[1,256,32,128]{3,2,1,0:T(8,128)(2,1)S(1)}, bf16[1,256,32,128]{3,2,1,0:T(8,128)(2,1)}, u32[]{:S(2)}) copy-start(bf16[1,256,32,128]{3,2,1,0:T(8,128)(2,1)} %refs_0_.3) | copy-start | bytes 6291460
  86.0 49.4 %collective-permute-start.31 = (bf16[16,64,128]{2,1,0:T(8,128)(2,1)S(1)}, bf16[16,64,128]{2,1,0:T(8,128)(2,1)S(1)}, u32[]{:S(2)}, u32[]{:S(2)}) collective-permute-start(bf16[16,64,128]{2,1,0:T(8,128)(2,1)S(1)} %shard_map.119), channel_id=1, source_target_pairs={{0,1},{1,0},{2,3},{3,2},{4,5},{5,4},{6,7},{7,6},{8,9},{9,8},{10,11... | collective-permute-start | bytes 786440 | tf_op jit(solution)/shard_map/ppermute | solution.py:530
  97.9 37.4 %collective-permute-start.30 = (bf16[16,64,128]{2,1,0:T(8,128)(2,1)S(1)}, bf16[16,64,128]{2,1,0:T(8,128)(2,1)S(1)}, u32[]{:S(2)}, u32[]{:S(2)}) collective-permute-start(bf16[16,64,128]{2,1,0:T(8,128)(2,1)S(1)} %shard_map.118), channel_id=1, source_target_pairs={{0,1},{1,0},{2,3},{3,2},{4,5},{5,4},{6,7},{7,6},{8,9},{9,8},{10,11... | collective-permute-start | bytes 786440 | tf_op jit(solution)/shard_map/ppermute | solution.py:530

commit v3 on v2

v3 whole, which is shorter than its diff:
```python
import functools
import math

import jax
import jax.numpy as jnp
from jax import lax
from jax.experimental import pallas as pl
from jax.experimental.pallas import tpu as pltpu
from jax.sharding import PartitionSpec as P

PAGE = 128
LOG2E = 1.4426950408889634
NEG = -1e30
VMEM_LIMIT = 48 * 1024 * 1024


def nt(a, b):
    return lax.dot_general(a, b, (((1,), (1,)), ((), ())), preferred_element_type=jnp.float32)


def nn(a, b):
    return jnp.dot(a, b, preferred_element_type=jnp.float32)


def params():
    return pltpu.CompilerParams(vmem_limit_bytes=VMEM_LIMIT)


def one_hot(out_rows, in_rows, source):
    row = lax.broadcasted_iota(jnp.int32, (out_rows, in_rows), 0)
    col = lax.broadcasted_iota(jnp.int32, (out_rows, in_rows), 1)
    return jnp.where(col == source(row), 1.0, 0.0).astype(jnp.bfloat16)


def split_kernel(heads, tokens, k_ref, v_ref, out_ref):
    rows = min(tokens * heads, 256)
    step = rows // heads
    pick = one_hot(rows, rows, lambda i: (i % step) * heads + i // step)
    moved = []
    for j in range(tokens // step):
        moved.append(nn(pick, k_ref[pl.ds(j * rows, rows), :]))
        values = nn(pick, v_ref[pl.ds(j * rows, rows), :]).astype(jnp.bfloat16)
        for h in range(heads):
            out_ref[h, 1, pl.ds(j * step, step), :] = values[h * step : (h + 1) * step]
    for h in range(heads):
        keys = jnp.concatenate([a[h * step : (h + 1) * step] for a in moved], axis=0)
        for page in range(tokens // PAGE):
            out_ref[h, 0, pl.ds(page * PAGE, PAGE), :] = keys[
                page * PAGE : (page + 1) * PAGE
            ].T.astype(jnp.bfloat16)


def split_heads(k, v):
    _, tokens, heads, width = k.shape
    return pl.pallas_call(
        functools.partial(split_kernel, heads, tokens),
        out_shape=jax.ShapeDtypeStruct((heads, 2, tokens, width), jnp.bfloat16),
        compiler_params=params(),
        cost_estimate=pl.CostEstimate(flops=10**8, bytes_accessed=2 * 10**6, transcendentals=0),
    )(k.reshape(tokens * heads, width), v.reshape(tokens * heads, width))


def prefill_kernel(ring, group, tokens, scale, earlier_ref, *refs):
    q_ref = refs[0]
    blocks = refs[1 : 1 + ring]
    out_ref, buf, s_ref, m_ref, l_ref, acc_ref, sems = refs[1 + ring :]
    own = blocks[0]
    heads = own.shape[0]
    block = q_ref.shape[1]
    pages = tokens // PAGE
    i = pl.program_id(0)

    def copies():
        found = []
        place = jnp.int32(0)
        for s in range(1, ring):
            copy = pltpu.make_async_copy(blocks[s], buf.at[place], sems.at[s])
            found.append((earlier_ref[s], copy))
            place = place + earlier_ref[s]
        return found

    @pl.when(i == 0)
    def _():
        for flag, copy in copies():
            @pl.when(flag == 1)
            def _():
                copy.start()
        for flag, copy in copies():
            @pl.when(flag == 1)
            def _():
                copy.wait()

    rows = block * group
    queries = q_ref[0].astype(jnp.float32)
    q = [
        queries[:, h * group : (h + 1) * group, :].reshape(rows, -1).astype(jnp.bfloat16)
        for h in range(heads)
    ]

    def fold(a, op):
        return functools.reduce(op, [a[:, j * 128 : (j + 1) * 128] for j in range(a.shape[1] // 128)])

    token = lax.broadcasted_iota(jnp.int32, (rows, tokens), 0) // group + i * block
    allowed = lax.broadcasted_iota(jnp.int32, (rows, tokens), 1) <= token

    def keys(ref, h):
        return jnp.concatenate([ref[h, 0, pl.ds(j * PAGE, PAGE), :] for j in range(pages)], axis=1)

    last = ring - 1
    for h in range(heads):
        s = jnp.where(allowed, nn(q[h], keys(own, h)), NEG)
        s_ref[last, h] = s
        m_ref[h] = fold(s, jnp.maximum)

    def look(b, carry):
        for h in range(heads):
            s = nn(q[h], keys(buf.at[b], h))
            s_ref[b, h] = s
            m_ref[h] = jnp.maximum(m_ref[h], fold(s, jnp.maximum))
        return carry

    lax.fori_loop(0, earlier_ref[0], look, 0)
    for h in range(heads):
        m = jnp.max(m_ref[h], axis=1, keepdims=True)
        m_ref[h] = jnp.broadcast_to(m, m_ref.shape[1:])
        p = jnp.exp2((s_ref[last, h] - m) * scale)
        l_ref[h] = fold(p, jnp.add)
        acc_ref[h] = nn(p.astype(jnp.bfloat16), own[h, 1])

    def weigh(b, carry):
        for h in range(heads):
            m = m_ref[h]
            p = [
                jnp.exp2((s_ref[b, h, :, pl.ds(j * 128, 128)] - m) * scale)
                for j in range(tokens // 128)
            ]
            l_ref[h] = l_ref[h] + functools.reduce(jnp.add, p)
            p = jnp.concatenate([a.astype(jnp.bfloat16) for a in p], axis=1)
            acc_ref[h] = acc_ref[h] + nn(p, buf[b, h, 1])
        return carry

    lax.fori_loop(0, earlier_ref[0], weigh, 0)
    out = []
    for h in range(heads):
        total = jnp.sum(l_ref[h], axis=1, keepdims=True)
        out.append((acc_ref[h] / total).reshape(block, group, -1))
    out_ref[0] = jnp.concatenate(out, axis=1).astype(out_ref.dtype)


def prefill(q, blocks, earlier):
    _, tokens, q_heads, width = q.shape
    ring = len(blocks)
    heads = blocks[0].shape[0]
    group = q_heads // heads
    block = 64
    rows = block * group
    q_spec = pl.BlockSpec((1, block, q_heads, width), lambda i, *_: (0, i, 0, 0))
    own_spec = pl.BlockSpec(blocks[0].shape, lambda i, *_: (0, 0, 0, 0))
    return pl.pallas_call(
        functools.partial(prefill_kernel, ring, group, tokens, LOG2E / math.sqrt(width)),
        grid_spec=pltpu.PrefetchScalarGridSpec(
            num_scalar_prefetch=1,
            grid=(tokens // block,),
            in_specs=[q_spec, own_spec] + [pl.BlockSpec(memory_space=pl.ANY)] * (ring - 1),
            out_specs=q_spec,
            scratch_shapes=[
                pltpu.VMEM((max(ring - 1, 1),) + blocks[0].shape, jnp.bfloat16),
                pltpu.VMEM((ring, heads, rows, tokens), jnp.float32),
                pltpu.VMEM((heads, rows, width), jnp.float32),
                pltpu.VMEM((heads, rows, width), jnp.float32),
                pltpu.VMEM((heads, rows, width), jnp.float32),
                pltpu.SemaphoreType.DMA((ring,)),
            ],
        ),
        out_shape=jax.ShapeDtypeStruct(q.shape, jnp.bfloat16),
        compiler_params=params(),
        cost_estimate=pl.CostEstimate(
            flops=16 * q_heads * tokens * tokens * ring * width,
            bytes_accessed=4 * 10**6,
            transcendentals=tokens * tokens * ring * q_heads,
        ),
    )(earlier, q, *blocks)


def by_head(raw, steps, heads, group):
    raw = raw.astype(jnp.float32)
    return jnp.concatenate(
        [
            raw[(t * heads + h) * group : (t * heads + h + 1) * group]
            for h in range(heads)
            for t in range(steps)
        ],
        axis=0,
    ).astype(jnp.bfloat16)


def cache_kernel(steps, heads, group, scale, len_ref, q_ref, dk_ref, dv_ref, ck_ref, cv_ref, acc_ref, ml_ref):
    block, rows, width = q_ref.shape
    cache = ck_ref.shape[1]
    new = dk_ref.shape[1]

    def mask(columns):
        row = lax.broadcasted_iota(jnp.int32, (rows, columns), 0)
        column = lax.broadcasted_iota(jnp.int32, (rows, columns), 1)
        same = column % heads == row // (steps * group)
        return jnp.where(same, column // heads, 1 << 20), row % (steps * group) // group

    place, _ = mask(cache)
    new_place, step = mask(new)
    new_allowed = new_place <= step
    half = lax.broadcasted_iota(jnp.int32, (rows, width), 1) < width // 2
    first = pl.program_id(0) * block
    unroll = math.gcd(4, block)

    def body(g, carry):
        scores = []
        for u in range(unroll):
            r = g * unroll + u
            q = by_head(q_ref[r], steps, heads, group)
            old = jnp.where(place < len_ref[first + r], nt(q, ck_ref[r]), NEG)
            add = jnp.where(new_allowed, nt(q, dk_ref[r]), NEG)
            scores.append((r, old, add))
        weights = []
        for r, old, add in scores:
            m = jnp.maximum(
                jnp.max(old, axis=1, keepdims=True), jnp.max(add, axis=1, keepdims=True)
            )
            old = jnp.exp2((old - m) * scale)
            add = jnp.exp2((add - m) * scale)
            l = jnp.sum(old, axis=1, keepdims=True) + jnp.sum(add, axis=1, keepdims=True)
            ml_ref[r] = jnp.where(half, m, l)
            weights.append((r, old.astype(jnp.bfloat16), add.astype(jnp.bfloat16)))
        for r, old, add in weights:
            acc_ref[r] = nn(old, cv_ref[r]) + nn(add, dv_ref[r])
        return carry

    lax.fori_loop(0, block // unroll, body, 0)


def cache_part(q, dk, dv, ck, cv, lens, steps, heads, group):
    requests, rows, width = q.shape
    block = math.gcd(8, requests)
    spec = [
        pl.BlockSpec((block,) + a.shape[1:], lambda i, *_: (i, 0, 0)) for a in (q, dk, dv, ck, cv)
    ]
    out = pl.BlockSpec((block, rows, width), lambda i, *_: (i, 0, 0))
    shape = jax.ShapeDtypeStruct((requests, rows, width), jnp.float32)
    return pl.pallas_call(
        functools.partial(cache_kernel, steps, heads, group, LOG2E / math.sqrt(width)),
        grid_spec=pltpu.PrefetchScalarGridSpec(
            num_scalar_prefetch=1, grid=(requests // block,), in_specs=spec, out_specs=[out, out]
        ),
        out_shape=[shape, shape],
        compiler_params=params(),
        cost_estimate=pl.CostEstimate(
            flops=requests * rows * ck.shape[1] * width * 16,
            bytes_accessed=14 * 10**6,
            transcendentals=requests * rows * ck.shape[1],
        ),
    )(lens, q, dk, dv, ck, cv)


def decode_kernel(slots, extra, steps, target, targets, heads, group, scale, *refs):
    slot_ref, pick_ref, meta_ref = refs[:3]
    q_ref, acc_ref, ml_ref = refs[3:6]
    blocks = refs[6 : 6 + slots]
    out_ref, buf, sems = refs[6 + slots :]
    block, rows, width = q_ref.shape
    i = pl.program_id(0)
    first = (lax.rem(meta_ref[1] + target, targets) * pl.num_programs(0) + i) * block

    def copies():
        for s in range(slots):
            start = pl.multiple_of(pick_ref[s] * PAGE, PAGE)
            yield pltpu.make_async_copy(
                blocks[s].at[:, :, pl.ds(start, PAGE), :], buf.at[s], sems.at[s]
            )

    @pl.when(i == 0)
    def _():
        for copy in copies():
            copy.start()
        for copy in copies():
            copy.wait()

    each = steps * group
    wide = math.gcd(2, heads)
    order = one_hot(
        rows, rows, lambda r: r // each * each + r % steps * group + r % each // steps
    )
    unroll = math.gcd(2, block)

    def body(g, carry):
        scores = []
        for u in range(unroll):
            r = g * unroll + u
            q = by_head(q_ref[r], steps, heads, group)
            places = [slot_ref[(first + r) * extra + j] for j in range(extra)]
            s = [
                nn(
                    q[h * each : (h + 1) * each],
                    jnp.concatenate([buf[place, h, 0] for place in places], axis=1),
                )
                for h in range(heads)
            ]
            scores.append((r, places, jnp.concatenate(s, axis=0)))
        weights = []
        for r, places, s in scores:
            ml = ml_ref[r]
            old, l = ml[:, :1], ml[:, width // 2 : width // 2 + 1]
            m = jnp.maximum(jnp.max(s, axis=1, keepdims=True), old)
            p = jnp.exp2((s - m) * scale)
            shrink = jnp.exp2((old - m) * scale)
            l = l * shrink + jnp.sum(p, axis=1, keepdims=True)
            weights.append((r, places, p.astype(jnp.bfloat16), shrink, l))
        for r, places, p, shrink, l in weights:
            parts = []
            for h in range(0, heads, wide):
                values = jnp.concatenate(
                    [
                        jnp.concatenate([buf[place, h + w, 1] for w in range(wide)], axis=1)
                        for place in places
                    ],
                    axis=0,
                )
                both = nn(p[h * each : (h + wide) * each], values)
                for w in range(wide):
                    parts.append(both[w * each : (w + 1) * each, w * width : (w + 1) * width])
            acc = acc_ref[r] * shrink + jnp.concatenate(parts, axis=0)
            result = (acc / l).astype(jnp.bfloat16)
            out_ref[r] = nn(order, result).astype(jnp.bfloat16)
        return carry

    lax.fori_loop(0, block // unroll, body, 0)


def decode(q, acc, ml, blocks, scalars, target, targets, extra, steps, heads, group):
    requests, rows, width = q.shape
    per_target = requests // targets
    block = math.gcd(8, per_target)
    per_block = per_target // block
    slots = len(blocks)

    def here(i, slot, pick, meta):
        return (lax.rem(meta[1] + target, targets) * per_block + i, 0, 0)

    in_specs = [pl.BlockSpec((block, rows, width), here)] * 3
    in_specs += [pl.BlockSpec(memory_space=pl.ANY)] * slots
    return pl.pallas_call(
        functools.partial(
            decode_kernel,
            slots,
            extra,
            steps,
            target,
            targets,
            heads,
            group,
            LOG2E / math.sqrt(width),
        ),
        grid_spec=pltpu.PrefetchScalarGridSpec(
            num_scalar_prefetch=3,
            grid=(per_block,),
            in_specs=in_specs,
            out_specs=pl.BlockSpec((block, rows, width), lambda i, *_: (i, 0, 0)),
            scratch_shapes=[
                pltpu.VMEM((slots, heads, 2, PAGE, width), jnp.bfloat16),
                pltpu.SemaphoreType.DMA((slots,)),
            ],
        ),
        out_shape=jax.ShapeDtypeStruct((per_target, rows, width), jnp.bfloat16),
        compiler_params=params(),
        cost_estimate=pl.CostEstimate(
            flops=per_target * rows * extra * PAGE * width * 16,
            bytes_accessed=8 * 10**6,
            transcendentals=per_target * rows * extra * PAGE,
        ),
    )(*scalars, q, acc, ml, *blocks)


def join_kernel(targets, chunks, steps, meta_ref, *refs):
    out_ref = refs[-1]
    k = pl.program_id(0)
    rows = refs[0].shape[1]
    each = rows // steps
    for s in range(targets):
        @pl.when(lax.rem(meta_ref[1] + (targets - s), targets) == k)
        def _():
            for c in range(chunks):
                source = refs[s * chunks + c]

                def body(r, carry):
                    value = source[r]
                    for g in range(each):
                        out_ref[r, :, (c * each + g) * 128 : (c * each + g + 1) * 128] = value[
                            g * steps : (g + 1) * steps
                        ]
                    return carry

                lax.fori_loop(0, out_ref.shape[0], body, 0)


def join(pieces, meta, steps, targets, chunks):
    per_target, rows, width = pieces[0].shape
    half = chunks * (rows // steps) * width
    spec = pl.BlockSpec((per_target, rows, width), lambda k, *_: (0, 0, 0))
    return pl.pallas_call(
        functools.partial(join_kernel, targets, chunks, steps),
        grid_spec=pltpu.PrefetchScalarGridSpec(
            num_scalar_prefetch=1,
            grid=(targets,),
            in_specs=[spec] * len(pieces),
            out_specs=pl.BlockSpec((per_target, steps, half), lambda k, *_: (0, 0, k)),
        ),
        out_shape=jax.ShapeDtypeStruct((per_target, steps, half * targets), jnp.bfloat16),
        compiler_params=params(),
        cost_estimate=pl.CostEstimate(flops=0, bytes_accessed=2 * 10**6, transcendentals=0),
    )(meta, *pieces)


def ring_place(index, size):
    return jnp.where(index % 2 == 0, index // 2, size - 1 - index // 2)


def shards(
    roles,
    ring,
    targets,
    prefill_q,
    prefill_k,
    prefill_v,
    decode_q,
    decode_k,
    decode_v,
    cache_k,
    cache_v,
    cache_len,
    page_list,
):
    tokens, q_heads = prefill_q.shape[1:3]
    heads, width = prefill_k.shape[2:]
    group = q_heads // heads
    own_pages = tokens // PAGE
    requests, steps = decode_q.shape[:2]
    extra = page_list.shape[1]
    role = lax.axis_index("role")
    ctx = lax.axis_index("ctx")
    tp = lax.axis_index("tp")

    order = list(range(0, ring, 2)) + list(range(ring - 1, 0, -2))
    along = [(order[j], order[(j + 1) % ring]) for j in range(ring)]
    flips = [1 << b for b in reversed(range(roles.bit_length() - 1))]

    line = [split_heads(prefill_k, prefill_v)]
    for _ in range(1, ring):
        line.append(lax.ppermute(line[-1], "ctx", along))
    by_role = {0: line}
    for flip in flips:
        pairs = [(j, j ^ flip) for j in range(roles)]
        for seen in list(by_role):
            by_role[seen ^ flip] = [lax.ppermute(a, "role", pairs) for a in by_role[seen]]

    owner = page_list // own_pages
    place = (ring_place(ctx, ring) - ring_place(owner % ring, ring)) % ring
    slot = ((owner // ring) ^ role) * ring + place
    hot = slot.reshape(-1, 1) == jnp.arange(roles * ring)[None, :]
    pick = jnp.max(jnp.where(hot, (page_list % own_pages).reshape(-1, 1), 0), axis=0)
    meta = jnp.stack([ctx, tp]).astype(jnp.int32)
    scalars = (
        slot.reshape(-1).astype(jnp.int32),
        pick.astype(jnp.int32),
        meta,
    )
    position = jnp.arange(ring)
    where = ring_place(ctx, ring)
    source = (where - position) % ring
    source_ctx = jnp.where(source < (ring + 1) // 2, 2 * source, 2 * (ring - 1 - source) + 1)
    flags = (source_ctx < ctx).astype(jnp.int32)
    earlier = jnp.where(position == 0, jnp.sum(flags), flags).astype(jnp.int32)

    raw = [
        a.reshape(requests, -1, width) for a in (decode_q, decode_k, decode_v, cache_k, cache_v)
    ]
    acc, ml = cache_part(*raw, cache_len.astype(jnp.int32), steps, heads, group)
    prefill_out = prefill(prefill_q, line, earlier)
    blocks = [a for r in range(roles) for a in by_role[r]]
    pieces = [None] * targets
    for s in reversed(range(targets)):
        out = decode(raw[0], acc, ml, blocks, scalars, s, targets, extra, steps, heads, group)
        if s:
            shift = [(j, (j + s) % targets) for j in range(targets)]
            out = lax.ppermute(out, "tp", shift)
        pieces[s] = out
    decode_out = join(pieces, meta, steps, targets, 1)
    return (prefill_out, decode_out)


def solution(mesh):
    body = functools.partial(shards, mesh.shape["role"], mesh.shape["ctx"], mesh.shape["tp"])
    return jax.shard_map(
        body,
        mesh=mesh,
        in_specs=(
            P("role", "ctx", "tp", None),
            P("role", "ctx", "tp", None),
            P("role", "ctx", "tp", None),
            P(("role", "ctx"), None, "tp", None),
            P(("role", "ctx"), None, "tp", None),
            P(("role", "ctx"), None, "tp", None),
            P(("role", "ctx"), None, "tp", None),
            P(("role", "ctx"), None, "tp", None),
            P(("role", "ctx")),
            P(("role", "ctx"), None),
        ),
        out_specs=(P("role", "ctx", "tp", None), P(("role", "ctx", "tp"), None, None)),
        check_vma=False,
    )
```

time: 138 us -> 132 us (0.957)
  Pallas kernels: 76.1 us -> 57.2 us
  waiting for transfers between devices: 37.8 us -> 50.9 us
  starting transfers between devices: 15.7 us -> 11.5 us
  local copies, waits for them, and re-layouts: 4.61 us -> 8.6 us
    ppermute x6 -> x3, waiting for transfers between devices: 14.4 us -> 31.1 us  [shards(): line.append(lax.ppermute(line[-1], 'ctx', along))]
    pallas_call x4 -> x2, Pallas kernels: 41.4 us -> 29 us  [decode(): pl.pallas_call(functools.partial(decode_kernel, slots, extra, steps, targ...]
    pallas_call x3, Pallas kernels: 32.7 us -> 26.5 us  [the longest x1 17.9 us: prefill(): pl.pallas_call(functools.partial(prefill_kernel, ring, group, tokens, LOG...]
    ppermute x24 -> x12, starting transfers between devices: 10.8 us -> 6.11 us  [shards(): lax.ppermute(a, 'role', pairs)]
    unnamed x20 -> x18, local copies, waits for them, and re-layouts: 4.22 us -> 8.21 us
    ppermute x24 -> x12, waiting for transfers between devices: 23.5 us -> 19.8 us  [shards(): lax.ppermute(a, 'role', pairs)]
    ppermute x6 -> x3, starting transfers between devices: 2.7 us -> 3.75 us  [shards(): line.append(lax.ppermute(line[-1], 'ctx', along))]
  transfers between devices with their start and end apart: 32 -> 16, of which waited for: 13 -> 6; matrix products, arithmetic and copies ran while one was open for 2% -> 2% of each run, Pallas kernels for 54% -> 31%
where the time goes in v3:
time: 132 us; the launch traced here: 131 us
  Pallas kernels  57.2 us (43%)
  waiting for transfers between devices  50.9 us (39%)
  starting transfers between devices  11.5 us (9%)
  local copies, waits for them, and re-layouts  8.6 us (7%)
  other arithmetic  2.22 us (2%)
    ppermute x3, waiting for transfers between devices, shards(): line.append(lax.ppermute(line[-1], 'ctx', along))  31.1 us
    pallas_call x2, Pallas kernels, decode(): pl.pallas_call(functools.partial(decode_kernel, slots, extra, steps, targ...  29 us
    ppermute x12, waiting for transfers between devices, shards(): lax.ppermute(a, 'role', pairs)  19.8 us
    pallas_call x1, Pallas kernels, prefill(): pl.pallas_call(functools.partial(prefill_kernel, ring, group, tokens, LOG...  17.9 us
    unnamed x18, local copies, waits for them, and re-layouts  8.21 us
    pallas_call x1, Pallas kernels, cache_part(): pl.pallas_call(functools.partial(cache_kernel, steps, heads, group, LOG2E...  8.13 us
    ppermute x12, starting transfers between devices, shards(): lax.ppermute(a, 'role', pairs)  6.11 us
    ppermute x3, starting transfers between devices, shards(): line.append(lax.ppermute(line[-1], 'ctx', along))  3.75 us
  transfers between devices with their start and end apart: 16, of which 6 were waited for; matrix products, arithmetic and copies ran while one was open for 2% of the time, Pallas kernels for 31%

profile of v3, /device:TPU:24, one launch (start us, length us, event | category | flops | bytes accessed | tf_op | source)
XLA Modules:
  0.0 131.2 jit_solution(10877593016814656306)
XLA Ops:
  0.6 0.9 copy-done.3
  1.6 0.9 copy-done.4
  2.5 0.5 shard_map.113.refs_1_.refs_6_
  3.0 0.4 collective-permute-start
  3.4 13.3 %collective-permute-done.refs_2_.refs_7_ = bf16[4,2,256,128]{3,2,1,0:T(8,128)(2,1)S(1)} collective-permute-done((bf16[4,2,256,128]{3,2,1,0:T(8,128)(2,1)S(1)}, bf16[4,2,256,128]{3,2,1,0:T(8,128)(2,1)S(1)}, u32[]{:S(2)}, u32[]{:S(2)}) %collective-permute-start) | collective-permute-done | bytes 524320 | tf_op jit(solution)/shard_map/ppermute | solution.py:456
  16.7 1.2 collective-permute-start.1
  18.0 1.5 %collective-permute-start.7 = (bf16[4,2,256,128]{3,2,1,0:T(8,128)(2,1)S(1)}, bf16[4,2,256,128]{3,2,1,0:T(8,128)(2,1)S(1)}, u32[]{:S(2)}, u32[]{:S(2)}) collective-permute-start(bf16[4,2,256,128]{3,2,1,0:T(8,128)(2,1)S(1)} %shard_map.113.refs_1_.refs_6_), channel_id=1, source_target_pairs={{0,16},{8,24},{16,0},{24,8},{1,17},{9,25},{17,1},{25,9},{2,18},{10... | collective-permute-start | bytes 1572872 | tf_op jit(solution)/shard_map/ppermute | solution.py:461
  19.5 0.0 collective-permute-start.3
  19.5 10.1 %collective-permute-done.1.refs_3_.refs_8_ = bf16[4,2,256,128]{3,2,1,0:T(8,128)(2,1)S(1)} collective-permute-done((bf16[4,2,256,128]{3,2,1,0:T(8,128)(2,1)S(1)}, bf16[4,2,256,128]{3,2,1,0:T(8,128)(2,1)S(1)}, u32[]{:S(2)}, u32[]{:S(2)}) %collective-permute-start.1) | collective-permute-done | bytes 524320 | tf_op jit(solution)/shard_map/ppermute | solution.py:456
  29.5 2.1 %collective-permute-start.2 = (bf16[4,2,256,128]{3,2,1,0:T(8,128)(2,1)S(1)}, bf16[4,2,256,128]{3,2,1,0:T(8,128)(2,1)S(1)}, u32[]{:S(2)}, u32[]{:S(2)}) collective-permute-start(bf16[4,2,256,128]{3,2,1,0:T(8,128)(2,1)S(1)} %collective-permute-done.1.refs_3_.refs_8_), channel_id=1, source_target_pairs={{0,4},{4,6},{6,2},{2,0},{1,5},{5,7},{7,3},{3,1},{8,12},{12,14},{14... | collective-permute-start | bytes 1572872 | tf_op jit(solution)/shard_map/ppermute | solution.py:456
  31.7 1.5 %collective-permute-start.8 = (bf16[4,2,256,128]{3,2,1,0:T(8,128)(2,1)S(1)}, bf16[4,2,256,128]{3,2,1,0:T(8,128)(2,1)}, u32[]{:S(2)}, u32[]{:S(2)}) collective-permute-start(bf16[4,2,256,128]{3,2,1,0:T(8,128)(2,1)S(1)} %collective-permute-done.refs_2_.refs_7_), channel_id=1, source_target_pairs={{0,16},{8,24},{16,0},{24,8},{1,17},{9,25},{17,1},{25,9},{2,18},{10... | collective-permute-start | bytes 1572872 | tf_op jit(solution)/shard_map/ppermute | solution.py:461
  33.2 0.0 collective-permute-start.4
  33.2 0.0 collective-permute-done.7.refs_14_
  33.2 0.5 collective-permute-start.11
  33.7 0.5 collective-permute-start.9
  34.2 7.7 %collective-permute-done.2.refs_4_.refs_9_ = bf16[4,2,256,128]{3,2,1,0:T(8,128)(2,1)S(1)} collective-permute-done((bf16[4,2,256,128]{3,2,1,0:T(8,128)(2,1)S(1)}, bf16[4,2,256,128]{3,2,1,0:T(8,128)(2,1)S(1)}, u32[]{:S(2)}, u32[]{:S(2)}) %collective-permute-start.2) | collective-permute-done | bytes 524320 | tf_op jit(solution)/shard_map/ppermute | solution.py:456
  41.9 1.5 %collective-permute-start.10 = (bf16[4,2,256,128]{3,2,1,0:T(8,128)(2,1)S(1)}, bf16[4,2,256,128]{3,2,1,0:T(8,128)(2,1)}, u32[]{:S(2)}, u32[]{:S(2)}) collective-permute-start(bf16[4,2,256,128]{3,2,1,0:T(8,128)(2,1)S(1)} %collective-permute-done.2.refs_4_.refs_9_), channel_id=1, source_target_pairs={{0,16},{8,24},{16,0},{24,8},{1,17},{9,25},{17,1},{25,9},{2,18},{10... | collective-permute-start | bytes 1572872 | tf_op jit(solution)/shard_map/ppermute | solution.py:461
  43.4 0.6 fusion.12
  44.0 0.7 compare_select_fusion.3.earlier_ref
  44.7 0.7 add_select_fusion
  45.4 1.2 collective-permute-done.8.refs_15_
  46.6 0.0 collective-permute-start.5
  46.6 0.0 collective-permute-done.4.refs_11_
  46.6 0.5 collective-permute-start.12
  47.1 0.0 collective-permute-done.11.refs_18_
  47.1 0.1 collective-permute-start.6
  47.2 10.6 %collective-permute-done.9.refs_16_ = bf16[4,2,256,128]{3,2,1,0:T(8,128)(2,1)} collective-permute-done((bf16[4,2,256,128]{3,2,1,0:T(8,128)(2,1)S(1)}, bf16[4,2,256,128]{3,2,1,0:T(8,128)(2,1)}, u32[]{:S(2)}, u32[]{:S(2)}) %collective-permute-start.9) | collective-permute-done | bytes 524320 | tf_op jit(solution)/shard_map/ppermute | solution.py:461
  57.9 8.0 %collective-permute-done.10.refs_17_ = bf16[4,2,256,128]{3,2,1,0:T(8,128)(2,1)} collective-permute-done((bf16[4,2,256,128]{3,2,1,0:T(8,128)(2,1)S(1)}, bf16[4,2,256,128]{3,2,1,0:T(8,128)(2,1)}, u32[]{:S(2)}, u32[]{:S(2)}) %collective-permute-start.10) | collective-permute-done | bytes 524320 | tf_op jit(solution)/shard_map/ppermute | solution.py:461
  65.8 0.1 pad_add_fusion.refs_2_.meta_ref
  65.9 0.1 copy.17
  66.0 0.1 broadcast_in_dim.20
  66.1 0.1 copy.16
  66.2 0.1 reshape.34.refs_0_
  66.3 0.1 select_reduce_fusion.refs_1_
  66.4 0.0 copy-start.2
  66.4 1.2 copy-done.2
  67.6 0.9 copy-done.6
  68.5 0.9 copy-done.7
  69.4 0.7 copy-done.8
  70.1 8.1 %shard_map.115 = (f32[32,128,128]{2,1,0:T(8,128)S(1)}, f32[32,128,128]{2,1,0:T(8,128)S(1)}) custom-call(s32[32]{0:T(128)S(1)} %copy-done.8, bf16[32,128,128]{2,1,0:T(8,128)(2,1)S(1)} %bitcast.11, bf16[32,16,128]{2,1,0:T(8,128)(2,1)S(1)} %bitcast.14, bf16[32,16,128]{2,1,0:T(8,128)(2,1)S(1)} %bitcast.15, bf16[32,512,128]{2,1,0:T(8,128)(2,1)} %bitcast.16, ...), custom_call_target="tpu_custom_call" | custom-call | flops 4294967296 | bytes 14000000 | tf_op jit(solution)/shard_map/pallas_call | solution.py:248
  78.3 1.3 %copy-done = f32[32,128,128]{2,1,0:T(8,128)} copy-done((f32[32,128,128]{2,1,0:T(8,128)}, f32[32,128,128]{2,1,0:T(8,128)S(1)}, u32[]{:S(2)}) %copy-start) | copy-done | bytes 2097176
  79.6 1.3 copy-done.1
  80.9 0.0 copy-start.5
  80.9 14.5 %shard_map.117 = bf16[16,128,128]{2,1,0:T(8,128)(2,1)S(1)} custom-call(s32[128]{0:T(128)S(1)} %reshape.34.refs_0_, s32[16]{0:T(128)S(1)} %select_reduce_fusion.refs_1_, s32[2]{0:T(128)S(1)} %pad_add_fusion.refs_2_.meta_ref, bf16[32,128,128]{2,1,0:T(8,128)(2,1)} %bitcast.9, f32[32,128,128]{2,1,0:T(8,128)} %copy-done, f32[32,128,128]{2,1,0:T(8,128)} %copy-done.1, ...), custom_call_target="tpu_custom_call" | custom-call | flops 2147483648 | bytes 8000000 | tf_op jit(solution)/shard_map/pallas_call | solution.py:349
  95.4 1.6 %collective-permute-start.15 = (bf16[16,128,128]{2,1,0:T(8,128)(2,1)S(1)}, bf16[16,128,128]{2,1,0:T(8,128)(2,1)S(1)}, u32[]{:S(2)}, u32[]{:S(2)}) collective-permute-start(bf16[16,128,128]{2,1,0:T(8,128)(2,1)S(1)} %shard_map.117), channel_id=1, source_target_pairs={{0,1},{1,0},{2,3},{3,2},{4,5},{5,4},{6,7},{7,6},{8,9},{9,8},{10,11... | collective-permute-start | bytes 1572872 | tf_op jit(solution)/shard_map/ppermute | solution.py:492
  97.0 17.9 %shard_map.114 = bf16[1,256,32,128]{3,2,1,0:T(8,128)(2,1)} custom-call(s32[4]{0:T(128)S(1)} %compare_select_fusion.3.earlier_ref, bf16[1,256,32,128]{3,2,1,0:T(8,128)(2,1)S(1)} %copy-done.5, bf16[4,2,256,128]{3,2,1,0:T(8,128)(2,1)S(1)} %shard_map.113.refs_1_.refs_6_, bf16[4,2,256,128]{3,2,1,0:T(8,128)(2,1)S(1)} %collective-permute-done.refs_2_.refs_7_, ...), custom_call_target="tpu_custom_call" | custom-call | flops 17179869184 | bytes 4000000 | tf_op jit(solution)/shard_map/pallas_call | solution.py:159
  114.9 14.5 %shard_map.116.refs_0_ = bf16[16,128,128]{2,1,0:T(8,128)(2,1)S(1)} custom-call(s32[128]{0:T(128)S(1)} %reshape.34.refs_0_, s32[16]{0:T(128)S(1)} %select_reduce_fusion.refs_1_, s32[2]{0:T(128)S(1)} %pad_add_fusion.refs_2_.meta_ref, bf16[32,128,128]{2,1,0:T(8,128)(2,1)} %bitcast.10, f32[32,128,128]{2,1,0:T(8,128)} %copy-done, f32[32,128,128]{2,1,0:T(8,128)} %copy-done.1, ...), custom_call_target="tpu_custom_call" | custom-call | flops 2147483648 | bytes 8000000 | tf_op jit(solution)/shard_map/pallas_call | solution.py:349
  129.4 1.8 %shard_map.118 = bf16[16,4,8192]{2,1,0:T(4,128)(2,1)} custom-call(s32[2]{0:T(128)S(1)} %pad_add_fusion.refs_2_.meta_ref, bf16[16,128,128]{2,1,0:T(8,128)(2,1)S(1)} %shard_map.116.refs_0_, bf16[16,128,128]{2,1,0:T(8,128)(2,1)S(1)} %collective-permute-done.15.refs_1_), custom_call_target="tpu_custom_call" | custom-call | bytes 2000000 | tf_op jit(solution)/shard_map/pallas_call | solution.py:407
  (17 shorter events, 0.0 us)
Async XLA Ops:
  0.6 1.0 copy-start.3
  1.6 0.9 copy-start.4
  3.0 13.7 %collective-permute-start = (bf16[4,2,256,128]{3,2,1,0:T(8,128)(2,1)S(1)}, bf16[4,2,256,128]{3,2,1,0:T(8,128)(2,1)S(1)}, u32[]{:S(2)}, u32[]{:S(2)}) collective-permute-start(bf16[4,2,256,128]{3,2,1,0:T(8,128)(2,1)S(1)} %shard_map.113.refs_1_.refs_6_), channel_id=1, source_target_pairs={{0,4},{4,6},{6,2},{2,0},{1,5},{5,7},{7,3},{3,1},{8,12},{12,14},{14... | collective-permute-start | bytes 1572872 | tf_op jit(solution)/shard_map/ppermute | solution.py:456
  16.7 12.8 %collective-permute-start.1 = (bf16[4,2,256,128]{3,2,1,0:T(8,128)(2,1)S(1)}, bf16[4,2,256,128]{3,2,1,0:T(8,128)(2,1)S(1)}, u32[]{:S(2)}, u32[]{:S(2)}) collective-permute-start(bf16[4,2,256,128]{3,2,1,0:T(8,128)(2,1)S(1)} %collective-permute-done.refs_2_.refs_7_), channel_id=1, source_target_pairs={{0,4},{4,6},{6,2},{2,0},{1,5},{5,7},{7,3},{3,1},{8,12},{12,14},{14... | collective-permute-start | bytes 1572872 | tf_op jit(solution)/shard_map/ppermute | solution.py:456
  18.0 15.2 %collective-permute-start.7 = (bf16[4,2,256,128]{3,2,1,0:T(8,128)(2,1)S(1)}, bf16[4,2,256,128]{3,2,1,0:T(8,128)(2,1)S(1)}, u32[]{:S(2)}, u32[]{:S(2)}) collective-permute-start(bf16[4,2,256,128]{3,2,1,0:T(8,128)(2,1)S(1)} %shard_map.113.refs_1_.refs_6_), channel_id=1, source_target_pairs={{0,16},{8,24},{16,0},{24,8},{1,17},{9,25},{17,1},{25,9},{2,18},{10... | collective-permute-start | bytes 1572872 | tf_op jit(solution)/shard_map/ppermute | solution.py:461
  19.5 14.2 %collective-permute-start.3 = (bf16[4,2,256,128]{3,2,1,0:T(8,128)(2,1)S(1)}, bf16[4,2,256,128]{3,2,1,0:T(8,128)(2,1)S(1)}, u32[]{:S(2)}, u32[]{:S(2)}) collective-permute-start(bf16[4,2,256,128]{3,2,1,0:T(8,128)(2,1)S(1)} %shard_map.113.refs_1_.refs_6_), channel_id=1, source_target_pairs={{0,8},{8,0},{16,24},{24,16},{1,9},{9,1},{17,25},{25,17},{2,10},{10... | collective-permute-start | bytes 1572872 | tf_op jit(solution)/shard_map/ppermute | solution.py:461
  29.5 12.4 %collective-permute-start.2 = (bf16[4,2,256,128]{3,2,1,0:T(8,128)(2,1)S(1)}, bf16[4,2,256,128]{3,2,1,0:T(8,128)(2,1)S(1)}, u32[]{:S(2)}, u32[]{:S(2)}) collective-permute-start(bf16[4,2,256,128]{3,2,1,0:T(8,128)(2,1)S(1)} %collective-permute-done.1.refs_3_.refs_8_), channel_id=1, source_target_pairs={{0,4},{4,6},{6,2},{2,0},{1,5},{5,7},{7,3},{3,1},{8,12},{12,14},{14... | collective-permute-start | bytes 1572872 | tf_op jit(solution)/shard_map/ppermute | solution.py:456
  31.7 15.0 %collective-permute-start.8 = (bf16[4,2,256,128]{3,2,1,0:T(8,128)(2,1)S(1)}, bf16[4,2,256,128]{3,2,1,0:T(8,128)(2,1)}, u32[]{:S(2)}, u32[]{:S(2)}) collective-permute-start(bf16[4,2,256,128]{3,2,1,0:T(8,128)(2,1)S(1)} %collective-permute-done.refs_2_.refs_7_), channel_id=1, source_target_pairs={{0,16},{8,24},{16,0},{24,8},{1,17},{9,25},{17,1},{25,9},{2,18},{10... | collective-permute-start | bytes 1572872 | tf_op jit(solution)/shard_map/ppermute | solution.py:461
  33.2 13.5 %collective-permute-start.4 = (bf16[4,2,256,128]{3,2,1,0:T(8,128)(2,1)S(1)}, bf16[4,2,256,128]{3,2,1,0:T(8,128)(2,1)}, u32[]{:S(2)}, u32[]{:S(2)}) collective-permute-start(bf16[4,2,256,128]{3,2,1,0:T(8,128)(2,1)S(1)} %collective-permute-done.refs_2_.refs_7_), channel_id=1, source_target_pairs={{0,8},{8,0},{16,24},{24,16},{1,9},{9,1},{17,25},{25,17},{2,10},{10... | collective-permute-start | bytes 1572872 | tf_op jit(solution)/shard_map/ppermute | solution.py:461
  33.2 14.0 %collective-permute-start.11 = (bf16[4,2,256,128]{3,2,1,0:T(8,128)(2,1)S(1)}, bf16[4,2,256,128]{3,2,1,0:T(8,128)(2,1)}, u32[]{:S(2)}, u32[]{:S(2)}) collective-permute-start(bf16[4,2,256,128]{3,2,1,0:T(8,128)(2,1)S(1)} %collective-permute-done.7.refs_14_), channel_id=1, source_target_pairs={{0,8},{8,0},{16,24},{24,16},{1,9},{9,1},{17,25},{25,17},{2,10},{10... | collective-permute-start | bytes 1572872 | tf_op jit(solution)/shard_map/ppermute | solution.py:461
  33.7 24.2 %collective-permute-start.9 = (bf16[4,2,256,128]{3,2,1,0:T(8,128)(2,1)S(1)}, bf16[4,2,256,128]{3,2,1,0:T(8,128)(2,1)}, u32[]{:S(2)}, u32[]{:S(2)}) collective-permute-start(bf16[4,2,256,128]{3,2,1,0:T(8,128)(2,1)S(1)} %collective-permute-done.1.refs_3_.refs_8_), channel_id=1, source_target_pairs={{0,16},{8,24},{16,0},{24,8},{1,17},{9,25},{17,1},{25,9},{2,18},{10... | collective-permute-start | bytes 1572872 | tf_op jit(solution)/shard_map/ppermute | solution.py:461
  41.9 23.9 %collective-permute-start.10 = (bf16[4,2,256,128]{3,2,1,0:T(8,128)(2,1)S(1)}, bf16[4,2,256,128]{3,2,1,0:T(8,128)(2,1)}, u32[]{:S(2)}, u32[]{:S(2)}) collective-permute-start(bf16[4,2,256,128]{3,2,1,0:T(8,128)(2,1)S(1)} %collective-permute-done.2.refs_4_.refs_9_), channel_id=1, source_target_pairs={{0,16},{8,24},{16,0},{24,8},{1,17},{9,25},{17,1},{25,9},{2,18},{10... | collective-permute-start | bytes 1572872 | tf_op jit(solution)/shard_map/ppermute | solution.py:461
  46.6 34.3 %collective-permute-start.5 = (bf16[4,2,256,128]{3,2,1,0:T(8,128)(2,1)S(1)}, bf16[4,2,256,128]{3,2,1,0:T(8,128)(2,1)}, u32[]{:S(2)}, u32[]{:S(2)}) collective-permute-start(bf16[4,2,256,128]{3,2,1,0:T(8,128)(2,1)S(1)} %collective-permute-done.1.refs_3_.refs_8_), channel_id=1, source_target_pairs={{0,8},{8,0},{16,24},{24,16},{1,9},{9,1},{17,25},{25,17},{2,10},{10... | collective-permute-start | bytes 1572872 | tf_op jit(solution)/shard_map/ppermute | solution.py:461
  46.6 34.3 %collective-permute-start.12 = (bf16[4,2,256,128]{3,2,1,0:T(8,128)(2,1)}, bf16[4,2,256,128]{3,2,1,0:T(8,128)(2,1)}, u32[]{:S(2)}, u32[]{:S(2)}) collective-permute-start(bf16[4,2,256,128]{3,2,1,0:T(8,128)(2,1)} %collective-permute-done.8.refs_15_), channel_id=1, source_target_pairs={{0,8},{8,0},{16,24},{24,16},{1,9},{9,1},{17,25},{25,17},{2,10},{10... | collective-permute-start | bytes 1572872 | tf_op jit(solution)/shard_map/ppermute | solution.py:461
  47.1 33.8 %collective-permute-start.6 = (bf16[4,2,256,128]{3,2,1,0:T(8,128)(2,1)S(1)}, bf16[4,2,256,128]{3,2,1,0:T(8,128)(2,1)}, u32[]{:S(2)}, u32[]{:S(2)}) collective-permute-start(bf16[4,2,256,128]{3,2,1,0:T(8,128)(2,1)S(1)} %collective-permute-done.2.refs_4_.refs_9_), channel_id=1, source_target_pairs={{0,8},{8,0},{16,24},{24,16},{1,9},{9,1},{17,25},{25,17},{2,10},{10... | collective-permute-start | bytes 1572872 | tf_op jit(solution)/shard_map/ppermute | solution.py:461
  57.9 23.0 %collective-permute-start.13 = (bf16[4,2,256,128]{3,2,1,0:T(8,128)(2,1)}, bf16[4,2,256,128]{3,2,1,0:T(8,128)(2,1)}, u32[]{:S(2)}, u32[]{:S(2)}) collective-permute-start(bf16[4,2,256,128]{3,2,1,0:T(8,128)(2,1)} %collective-permute-done.9.refs_16_), channel_id=1, source_target_pairs={{0,8},{8,0},{16,24},{24,16},{1,9},{9,1},{17,25},{25,17},{2,10},{10... | collective-permute-start | bytes 1572872 | tf_op jit(solution)/shard_map/ppermute | solution.py:461
  65.8 15.1 %collective-permute-start.14 = (bf16[4,2,256,128]{3,2,1,0:T(8,128)(2,1)}, bf16[4,2,256,128]{3,2,1,0:T(8,128)(2,1)}, u32[]{:S(2)}, u32[]{:S(2)}) collective-permute-start(bf16[4,2,256,128]{3,2,1,0:T(8,128)(2,1)} %collective-permute-done.10.refs_17_), channel_id=1, source_target_pairs={{0,8},{8,0},{16,24},{24,16},{1,9},{9,1},{17,25},{25,17},{2,10},{10... | collective-permute-start | bytes 1572872 | tf_op jit(solution)/shard_map/ppermute | solution.py:461
  66.4 1.2 copy-start.2
  67.6 0.9 copy-start.6
  68.5 0.9 copy-start.7
  69.4 0.7 copy-start.8
  78.2 1.3 %copy-start = (f32[32,128,128]{2,1,0:T(8,128)}, f32[32,128,128]{2,1,0:T(8,128)S(1)}, u32[]{:S(2)}) copy-start(f32[32,128,128]{2,1,0:T(8,128)S(1)} %get-tuple-element.4.refs_4_) | copy-start | bytes 6291460
  79.6 1.3 copy-start.1
  80.9 16.1 %copy-start.5 = (bf16[1,256,32,128]{3,2,1,0:T(8,128)(2,1)S(1)}, bf16[1,256,32,128]{3,2,1,0:T(8,128)(2,1)}, u32[]{:S(2)}) copy-start(bf16[1,256,32,128]{3,2,1,0:T(8,128)(2,1)} %refs_0_.1) | copy-start | bytes 6291460
  95.4 33.9 %collective-permute-start.15 = (bf16[16,128,128]{2,1,0:T(8,128)(2,1)S(1)}, bf16[16,128,128]{2,1,0:T(8,128)(2,1)S(1)}, u32[]{:S(2)}, u32[]{:S(2)}) collective-permute-start(bf16[16,128,128]{2,1,0:T(8,128)(2,1)S(1)} %shard_map.117), channel_id=1, source_target_pairs={{0,1},{1,0},{2,3},{3,2},{4,5},{5,4},{6,7},{7,6},{8,9},{9,8},{10,11... | collective-permute-start | bytes 1572872 | tf_op jit(solution)/shard_map/ppermute | solution.py:492

commit v4 on v3

--- a/solution.py
+++ b/solution.py
@@ -38,14 +38,14 @@
     pick = one_hot(rows, rows, lambda i: (i % step) * heads + i // step)
     moved = []
     for j in range(tokens // step):
-        moved.append(nn(pick, k_ref[pl.ds(j * rows, rows), :]))
-        values = nn(pick, v_ref[pl.ds(j * rows, rows), :]).astype(jnp.bfloat16)
+        keys = nn(pick, k_ref[pl.ds(j * rows, rows), :]).astype(jnp.bfloat16)
+        moved.append(nn(pick, v_ref[pl.ds(j * rows, rows), :]))
         for h in range(heads):
-            out_ref[h, 1, pl.ds(j * step, step), :] = values[h * step : (h + 1) * step]
+            out_ref[h, 0, pl.ds(j * step, step), :] = keys[h * step : (h + 1) * step]
     for h in range(heads):
-        keys = jnp.concatenate([a[h * step : (h + 1) * step] for a in moved], axis=0)
+        values = jnp.concatenate([a[h * step : (h + 1) * step] for a in moved], axis=0)
         for page in range(tokens // PAGE):
-            out_ref[h, 0, pl.ds(page * PAGE, PAGE), :] = keys[
+            out_ref[h, 1, pl.ds(page * PAGE, PAGE), :] = values[
                 page * PAGE : (page + 1) * PAGE
             ].T.astype(jnp.bfloat16)
 
@@ -103,18 +103,18 @@
     token = lax.broadcasted_iota(jnp.int32, (rows, tokens), 0) // group + i * block
     allowed = lax.broadcasted_iota(jnp.int32, (rows, tokens), 1) <= token
 
-    def keys(ref, h):
-        return jnp.concatenate([ref[h, 0, pl.ds(j * PAGE, PAGE), :] for j in range(pages)], axis=1)
+    def values(ref, h):
+        return jnp.concatenate([ref[h, 1, pl.ds(j * PAGE, PAGE), :] for j in range(pages)], axis=1)
 
     last = ring - 1
     for h in range(heads):
-        s = jnp.where(allowed, nn(q[h], keys(own, h)), NEG)
+        s = jnp.where(allowed, nt(q[h], own[h, 0]), NEG)
         s_ref[last, h] = s
         m_ref[h] = fold(s, jnp.maximum)
 
     def look(b, carry):
         for h in range(heads):
-            s = nn(q[h], keys(buf.at[b], h))
+            s = nt(q[h], buf[b, h, 0])
             s_ref[b, h] = s
             m_ref[h] = jnp.maximum(m_ref[h], fold(s, jnp.maximum))
         return carry
@@ -125,7 +125,7 @@
         m_ref[h] = jnp.broadcast_to(m, m_ref.shape[1:])
         p = jnp.exp2((s_ref[last, h] - m) * scale)
         l_ref[h] = fold(p, jnp.add)
-        acc_ref[h] = nn(p.astype(jnp.bfloat16), own[h, 1])
+        acc_ref[h] = nt(p.astype(jnp.bfloat16), values(own, h))
 
     def weigh(b, carry):
         for h in range(heads):
@@ -136,7 +136,7 @@
             ]
             l_ref[h] = l_ref[h] + functools.reduce(jnp.add, p)
             p = jnp.concatenate([a.astype(jnp.bfloat16) for a in p], axis=1)
-            acc_ref[h] = acc_ref[h] + nn(p, buf[b, h, 1])
+            acc_ref[h] = acc_ref[h] + nt(p, values(buf.at[b], h))
         return carry
 
     lax.fori_loop(0, earlier_ref[0], weigh, 0)
@@ -182,33 +182,24 @@
     )(earlier, q, *blocks)
 
 
-def by_head(raw, steps, heads, group):
-    raw = raw.astype(jnp.float32)
-    return jnp.concatenate(
-        [
-            raw[(t * heads + h) * group : (t * heads + h + 1) * group]
-            for h in range(heads)
-            for t in range(steps)
-        ],
-        axis=0,
-    ).astype(jnp.bfloat16)
-
-
-def cache_kernel(steps, heads, group, scale, len_ref, q_ref, dk_ref, dv_ref, ck_ref, cv_ref, acc_ref, ml_ref):
+def cache_kernel(
+    steps, heads, group, scale, len_ref, q_ref, dk_ref, dv_ref, ck_ref, cv_ref, acc_ref, ml_ref
+):
     block, rows, width = q_ref.shape
     cache = ck_ref.shape[1]
     new = dk_ref.shape[1]
+    per_step = heads * group
 
     def mask(columns):
         row = lax.broadcasted_iota(jnp.int32, (rows, columns), 0)
         column = lax.broadcasted_iota(jnp.int32, (rows, columns), 1)
-        same = column % heads == row // (steps * group)
-        return jnp.where(same, column // heads, 1 << 20), row % (steps * group) // group
+        same = column % heads == row % per_step // group
+        return jnp.where(same, column // heads, 1 << 20), row // per_step
 
     place, _ = mask(cache)
     new_place, step = mask(new)
     new_allowed = new_place <= step
-    half = lax.broadcasted_iota(jnp.int32, (rows, width), 1) < width // 2
+    low = lax.broadcasted_iota(jnp.int32, (rows, width), 1) < 4
     first = pl.program_id(0) * block
     unroll = math.gcd(4, block)
 
@@ -216,7 +207,7 @@
         scores = []
         for u in range(unroll):
             r = g * unroll + u
-            q = by_head(q_ref[r], steps, heads, group)
+            q = q_ref[r]
             old = jnp.where(place < len_ref[first + r], nt(q, ck_ref[r]), NEG)
             add = jnp.where(new_allowed, nt(q, dk_ref[r]), NEG)
             scores.append((r, old, add))
@@ -228,10 +219,10 @@
             old = jnp.exp2((old - m) * scale)
             add = jnp.exp2((add - m) * scale)
             l = jnp.sum(old, axis=1, keepdims=True) + jnp.sum(add, axis=1, keepdims=True)
-            ml_ref[r] = jnp.where(half, m, l)
+            ml_ref[r] = jnp.where(low, m, l).T[:8]
             weights.append((r, old.astype(jnp.bfloat16), add.astype(jnp.bfloat16)))
         for r, old, add in weights:
-            acc_ref[r] = nn(old, cv_ref[r]) + nn(add, dv_ref[r])
+            acc_ref[r] = (nn(old, cv_ref[r]) + nn(add, dv_ref[r])).T
         return carry
 
     lax.fori_loop(0, block // unroll, body, 0)
@@ -243,14 +234,16 @@
     spec = [
         pl.BlockSpec((block,) + a.shape[1:], lambda i, *_: (i, 0, 0)) for a in (q, dk, dv, ck, cv)
     ]
-    out = pl.BlockSpec((block, rows, width), lambda i, *_: (i, 0, 0))
-    shape = jax.ShapeDtypeStruct((requests, rows, width), jnp.float32)
+    shapes = [(requests, width, rows), (requests, 8, rows)]
     return pl.pallas_call(
         functools.partial(cache_kernel, steps, heads, group, LOG2E / math.sqrt(width)),
         grid_spec=pltpu.PrefetchScalarGridSpec(
-            num_scalar_prefetch=1, grid=(requests // block,), in_specs=spec, out_specs=[out, out]
-        ),
-        out_shape=[shape, shape],
+            num_scalar_prefetch=1,
+            grid=(requests // block,),
+            in_specs=spec,
+            out_specs=[pl.BlockSpec((block,) + a[1:], lambda i, *_: (i, 0, 0)) for a in shapes],
+        ),
+        out_shape=[jax.ShapeDtypeStruct(a, jnp.float32) for a in shapes],
         compiler_params=params(),
         cost_estimate=pl.CostEstimate(
             flops=requests * rows * ck.shape[1] * width * 16,
@@ -265,7 +258,7 @@
     q_ref, acc_ref, ml_ref = refs[3:6]
     blocks = refs[6 : 6 + slots]
     out_ref, buf, sems = refs[6 + slots :]
-    block, rows, width = q_ref.shape
+    block, lanes, width = q_ref.shape
     i = pl.program_id(0)
     first = (lax.rem(meta_ref[1] + target, targets) * pl.num_programs(0) + i) * block
 
@@ -283,59 +276,57 @@
         for copy in copies():
             copy.wait()
 
-    each = steps * group
-    wide = math.gcd(2, heads)
-    order = one_hot(
-        rows, rows, lambda r: r // each * each + r % steps * group + r % each // steps
-    )
+    per_step = heads * group
+    row_head = lax.broadcasted_iota(jnp.int32, (lanes, width), 0) % per_step // group
+    head_rows = [jnp.where(row_head == h, 1.0, 0.0).astype(jnp.bfloat16) for h in range(heads)]
+    lane_head = lax.broadcasted_iota(jnp.int32, (width, lanes), 1) % per_step // group
+    order = one_hot(lanes, lanes, lambda r: r % steps * per_step + r // steps)
     unroll = math.gcd(2, block)
 
     def body(g, carry):
         scores = []
         for u in range(unroll):
             r = g * unroll + u
-            q = by_head(q_ref[r], steps, heads, group)
+            q = q_ref[r]
             places = [slot_ref[(first + r) * extra + j] for j in range(extra)]
-            s = [
-                nn(
-                    q[h * each : (h + 1) * each],
-                    jnp.concatenate([buf[place, h, 0] for place in places], axis=1),
-                )
-                for h in range(heads)
-            ]
-            scores.append((r, places, jnp.concatenate(s, axis=0)))
+            keys = jnp.concatenate(
+                [
+                    jnp.concatenate([buf[place, h, 0] for h in range(heads)], axis=1)
+                    for place in places
+                ],
+                axis=0,
+            )
+            spread = jnp.concatenate([q * a for a in head_rows], axis=1)
+            scores.append((r, places, nt(keys, spread)))
         weights = []
         for r, places, s in scores:
-            ml = ml_ref[r]
-            old, l = ml[:, :1], ml[:, width // 2 : width // 2 + 1]
-            m = jnp.maximum(jnp.max(s, axis=1, keepdims=True), old)
+            old = ml_ref[r, 0:1]
+            m = jnp.maximum(jnp.max(s, axis=0, keepdims=True), old)
             p = jnp.exp2((s - m) * scale)
             shrink = jnp.exp2((old - m) * scale)
-            l = l * shrink + jnp.sum(p, axis=1, keepdims=True)
+            l = ml_ref[r, 4:5] * shrink + jnp.sum(p, axis=0, keepdims=True)
             weights.append((r, places, p.astype(jnp.bfloat16), shrink, l))
         for r, places, p, shrink, l in weights:
-            parts = []
-            for h in range(0, heads, wide):
-                values = jnp.concatenate(
-                    [
-                        jnp.concatenate([buf[place, h + w, 1] for w in range(wide)], axis=1)
-                        for place in places
-                    ],
-                    axis=0,
-                )
-                both = nn(p[h * each : (h + wide) * each], values)
-                for w in range(wide):
-                    parts.append(both[w * each : (w + 1) * each, w * width : (w + 1) * width])
-            acc = acc_ref[r] * shrink + jnp.concatenate(parts, axis=0)
-            result = (acc / l).astype(jnp.bfloat16)
-            out_ref[r] = nn(order, result).astype(jnp.bfloat16)
+            values = jnp.concatenate(
+                [
+                    jnp.concatenate([buf[place, h, 1] for place in places], axis=1)
+                    for h in range(heads)
+                ],
+                axis=0,
+            )
+            every = nn(values, p)
+            part = every[:width]
+            for h in range(1, heads):
+                part = jnp.where(lane_head == h, every[h * width : (h + 1) * width], part)
+            result = ((acc_ref[r] * shrink + part) / l).astype(jnp.bfloat16)
+            out_ref[r] = nt(order, result).astype(jnp.bfloat16)
         return carry
 
     lax.fori_loop(0, block // unroll, body, 0)
 
 
 def decode(q, acc, ml, blocks, scalars, target, targets, extra, steps, heads, group):
-    requests, rows, width = q.shape
+    requests, lanes, width = q.shape
     per_target = requests // targets
     block = math.gcd(8, per_target)
     per_block = per_target // block
@@ -344,7 +335,7 @@
     def here(i, slot, pick, meta):
         return (lax.rem(meta[1] + target, targets) * per_block + i, 0, 0)
 
-    in_specs = [pl.BlockSpec((block, rows, width), here)] * 3
+    in_specs = [pl.BlockSpec((block,) + a.shape[1:], here) for a in (q, acc, ml)]
     in_specs += [pl.BlockSpec(memory_space=pl.ANY)] * slots
     return pl.pallas_call(
         functools.partial(
@@ -362,18 +353,18 @@
             num_scalar_prefetch=3,
             grid=(per_block,),
             in_specs=in_specs,
-            out_specs=pl.BlockSpec((block, rows, width), lambda i, *_: (i, 0, 0)),
+            out_specs=pl.BlockSpec((block, lanes, width), lambda i, *_: (i, 0, 0)),
             scratch_shapes=[
                 pltpu.VMEM((slots, heads, 2, PAGE, width), jnp.bfloat16),
                 pltpu.SemaphoreType.DMA((slots,)),
             ],
         ),
-        out_shape=jax.ShapeDtypeStruct((per_target, rows, width), jnp.bfloat16),
+        out_shape=jax.ShapeDtypeStruct((per_target, lanes, width), jnp.bfloat16),
         compiler_params=params(),
         cost_estimate=pl.CostEstimate(
-            flops=per_target * rows * extra * PAGE * width * 16,
+            flops=per_target * lanes * extra * PAGE * width * 16,
             bytes_accessed=8 * 10**6,
-            transcendentals=per_target * rows * extra * PAGE,
+            transcendentals=per_target * lanes * extra * PAGE,
         ),
     )(*scalars, q, acc, ml, *blocks)
 
@@ -451,15 +442,6 @@
     along = [(order[j], order[(j + 1) % ring]) for j in range(ring)]
     flips = [1 << b for b in reversed(range(roles.bit_length() - 1))]
 
-    line = [split_heads(prefill_k, prefill_v)]
-    for _ in range(1, ring):
-        line.append(lax.ppermute(line[-1], "ctx", along))
-    by_role = {0: line}
-    for flip in flips:
-        pairs = [(j, j ^ flip) for j in range(roles)]
-        for seen in list(by_role):
-            by_role[seen ^ flip] = [lax.ppermute(a, "role", pairs) for a in by_role[seen]]
-
     owner = page_list // own_pages
     place = (ring_place(ctx, ring) - ring_place(owner % ring, ring)) % ring
     slot = ((owner // ring) ^ role) * ring + place
@@ -481,9 +463,33 @@
     raw = [
         a.reshape(requests, -1, width) for a in (decode_q, decode_k, decode_v, cache_k, cache_v)
     ]
-    acc, ml = cache_part(*raw, cache_len.astype(jnp.int32), steps, heads, group)
-    prefill_out = prefill(prefill_q, line, earlier)
-    blocks = [a for r in range(roles) for a in by_role[r]]
+
+    gathered = {(0, 0): split_heads(prefill_k, prefill_v)}
+    fresh = [(0, 0)]
+    for k in range(ring + len(flips) - 1):
+        arrived = {}
+        for code, s in fresh:
+            block = gathered[code, s]
+            if code == 0 and s + 1 < ring:
+                arrived[0, s + 1] = lax.ppermute(block, "ctx", along)
+            for flip in flips:
+                if code == 0 or flip < code & -code:
+                    pairs = [(j, j ^ flip) for j in range(roles)]
+                    arrived[code ^ flip, s] = lax.ppermute(block, "role", pairs)
+        beside = ()
+        if k == 0:
+            beside = cache_part(*raw, cache_len.astype(jnp.int32), steps, heads, group)
+        if k == ring - 1:
+            beside = prefill(prefill_q, [gathered[0, s] for s in range(ring)], earlier)
+        arrived, beside = lax.optimization_barrier((arrived, beside))
+        if k == 0:
+            acc, ml = beside
+        if k == ring - 1:
+            prefill_out = beside
+        gathered.update(arrived)
+        fresh = list(arrived)
+
+    blocks = [gathered[r, s] for r in range(roles) for s in range(ring)]
     pieces = [None] * targets
     for s in reversed(range(targets)):
         out = decode(raw[0], acc, ml, blocks, scalars, s, targets, extra, steps, heads, group)

time: 132 us -> 113 us (0.86)
  waiting for transfers between devices: 50.9 us -> 28.2 us
  Pallas kernels: 57.2 us -> 61.6 us
  local copies, waits for them, and re-layouts: 8.6 us -> 11.5 us
  starting transfers between devices: 11.5 us -> 8.86 us
    ppermute x15, waiting for transfers between devices: 50.9 us -> 28.2 us  [the longest x12 25 us: shards(): arrived[code ^ flip, s] = lax.ppermute(block, 'role', pairs)]
    unnamed x18 -> x26, local copies, waits for them, and re-layouts: 8.21 us -> 11.1 us
    ppermute x15, starting transfers between devices: 9.87 us -> 7.27 us  [the longest x12 5.16 us: shards(): arrived[code ^ flip, s] = lax.ppermute(block, 'role', pairs)]
    pallas_call x1, Pallas kernels: 8.13 us -> 9.7 us  [cache_part(): pl.pallas_call(functools.partial(cache_kernel, steps, heads, group, LOG2E...]
    pallas_call x2, Pallas kernels: 29 us -> 30.4 us  [decode(): pl.pallas_call(functools.partial(decode_kernel, slots, extra, steps, targ...]
    pallas_call x1, Pallas kernels: 17.9 us -> 19.2 us  [prefill(): pl.pallas_call(functools.partial(prefill_kernel, ring, group, tokens, LOG...]
  transfers between devices with their start and end apart: 16 -> 16, of which waited for: 6 -> 6; matrix products, arithmetic and copies ran while one was open for 2% -> 2% of each run, Pallas kernels for 31% -> 39%
where the time goes in v4:
time: 113 us; the launch traced here: 112 us
  Pallas kernels  61.6 us (55%)
  waiting for transfers between devices  28.2 us (25%)
  local copies, waits for them, and re-layouts  11.5 us (10%)
  starting transfers between devices  8.86 us (8%)
  other arithmetic  1.55 us (1%)
    pallas_call x2, Pallas kernels, decode(): pl.pallas_call(functools.partial(decode_kernel, slots, extra, steps, targ...  30.4 us
    ppermute x12, waiting for transfers between devices, shards(): arrived[code ^ flip, s] = lax.ppermute(block, 'role', pairs)  25 us
    pallas_call x1, Pallas kernels, prefill(): pl.pallas_call(functools.partial(prefill_kernel, ring, group, tokens, LOG...  19.2 us
    unnamed x26, local copies, waits for them, and re-layouts  11.1 us
    pallas_call x1, Pallas kernels, cache_part(): pl.pallas_call(functools.partial(cache_kernel, steps, heads, group, LOG2E...  9.7 us
    ppermute x12, starting transfers between devices, shards(): arrived[code ^ flip, s] = lax.ppermute(block, 'role', pairs)  5.16 us
    ppermute x3, waiting for transfers between devices, shards(): arrived[0, s + 1] = lax.ppermute(block, 'ctx', along)  3.21 us
  transfers between devices with their start and end apart: 16, of which 6 were waited for; matrix products, arithmetic and copies ran while one was open for 2% of the time, Pallas kernels for 39%

profile of v4, /device:TPU:24, one launch (start us, length us, event | category | flops | bytes accessed | tf_op | source)
XLA Modules:
  0.0 112.5 jit_solution(12570290930879863630)
XLA Ops:
  0.6 0.9 copy-done.4
  1.6 0.9 copy-done.5
  2.5 0.5 shard_map.113.refs_1_.refs_6_
  3.0 1.6 %collective-permute-start.2 = (bf16[4,2,256,128]{3,2,1,0:T(8,128)(2,1)S(1)}, bf16[4,2,256,128]{3,2,1,0:T(8,128)(2,1)S(1)}, u32[]{:S(2)}, u32[]{:S(2)}) collective-permute-start(bf16[4,2,256,128]{3,2,1,0:T(8,128)(2,1)S(1)} %shard_map.113.refs_1_.refs_6_), channel_id=1, source_target_pairs={{0,16},{8,24},{16,0},{24,8},{1,17},{9,25},{17,1},{25,9},{2,18},{10... | collective-permute-start | bytes 1572872 | tf_op jit(solution)/shard_map/ppermute | solution.py:478
  4.6 0.0 collective-permute-start.1
  4.6 0.3 collective-permute-start
  4.9 1.2 %copy-done.1 = bf16[32,4,32,128]{3,2,1,0:T(8,128)(2,1)S(1)} copy-done((bf16[32,4,32,128]{3,2,1,0:T(8,128)(2,1)S(1)}, bf16[32,4,32,128]{3,2,1,0:T(8,128)(2,1)}, u32[]{:S(2)}) %copy-start.1) | copy-done | bytes 1048600
  6.1 0.9 copy-done.7
  7.0 0.9 copy-done.8
  7.9 0.7 copy-done.9
  8.6 9.7 %shard_map.114 = (f32[32,128,128]{2,1,0:T(8,128)S(1)}, f32[32,8,128]{2,1,0:T(8,128)S(1)}) custom-call(s32[32]{0:T(128)S(1)} %copy-done.9, bf16[32,128,128]{2,1,0:T(8,128)(2,1)S(1)} %bitcast.11, bf16[32,16,128]{2,1,0:T(8,128)(2,1)S(1)} %bitcast.14, bf16[32,16,128]{2,1,0:T(8,128)(2,1)S(1)} %bitcast.15, bf16[32,512,128]{2,1,0:T(8,128)(2,1)} %bitcast.16, ...), custom_call_target="tpu_custom_call" | custom-call | flops 4294967296 | bytes 14000000 | tf_op jit(solution)/shard_map/pallas_call | solution.py:238
  18.3 1.3 %copy-done = f32[32,128,128]{2,1,0:T(8,128)} copy-done((f32[32,128,128]{2,1,0:T(8,128)}, f32[32,128,128]{2,1,0:T(8,128)S(1)}, u32[]{:S(2)}) %copy-start) | copy-done | bytes 2097176
  19.7 0.0 collective-permute-done.1.refs_10_
  19.7 0.0 collective-permute-done.refs_2_.refs_7_
  19.7 0.3 collective-permute-start.6
  20.0 0.5 collective-permute-start.5
  20.5 0.0 collective-permute-start.4
  20.5 0.4 collective-permute-start.3
  20.9 0.7 collective-permute-done.6.refs_18_
  21.6 12.4 %collective-permute-done.5.refs_15_ = bf16[4,2,256,128]{3,2,1,0:T(8,128)(2,1)S(1)} collective-permute-done((bf16[4,2,256,128]{3,2,1,0:T(8,128)(2,1)S(1)}, bf16[4,2,256,128]{3,2,1,0:T(8,128)(2,1)S(1)}, u32[]{:S(2)}, u32[]{:S(2)}) %collective-permute-start.5) | collective-permute-done | bytes 524320 | tf_op jit(solution)/shard_map/ppermute | solution.py:478
  34.1 0.0 collective-permute-done.4.refs_11_
  34.1 0.9 collective-permute-done.3.refs_3_.refs_8_
  34.9 1.5 %collective-permute-start.9 = (bf16[4,2,256,128]{3,2,1,0:T(8,128)(2,1)}, bf16[4,2,256,128]{3,2,1,0:T(8,128)(2,1)}, u32[]{:S(2)}, u32[]{:S(2)}) collective-permute-start(bf16[4,2,256,128]{3,2,1,0:T(8,128)(2,1)} %collective-permute-done.3.refs_3_.refs_8_), channel_id=1, source_target_pairs={{0,16},{8,24},{16,0},{24,8},{1,17},{9,25},{17,1},{25,9},{2,18},{10... | collective-permute-start | bytes 1572872 | tf_op jit(solution)/shard_map/ppermute | solution.py:478
  36.4 0.2 collective-permute-start.8
  36.7 1.4 %collective-permute-start.7 = (bf16[4,2,256,128]{3,2,1,0:T(8,128)(2,1)}, bf16[4,2,256,128]{3,2,1,0:T(8,128)(2,1)}, u32[]{:S(2)}, u32[]{:S(2)}) collective-permute-start(bf16[4,2,256,128]{3,2,1,0:T(8,128)(2,1)} %collective-permute-done.3.refs_3_.refs_8_), channel_id=1, source_target_pairs={{0,4},{4,6},{6,2},{2,0},{1,5},{5,7},{7,3},{3,1},{8,12},{12,14},{14... | collective-permute-start | bytes 1572872 | tf_op jit(solution)/shard_map/ppermute | solution.py:474
  38.0 0.6 fusion.12
  38.7 0.7 compare_select_fusion.3.earlier_ref
  39.3 10.3 %collective-permute-done.9.refs_16_ = bf16[4,2,256,128]{3,2,1,0:T(8,128)(2,1)} collective-permute-done((bf16[4,2,256,128]{3,2,1,0:T(8,128)(2,1)}, bf16[4,2,256,128]{3,2,1,0:T(8,128)(2,1)}, u32[]{:S(2)}, u32[]{:S(2)}) %collective-permute-start.9) | collective-permute-done | bytes 524320 | tf_op jit(solution)/shard_map/ppermute | solution.py:478
  49.6 2.3 %collective-permute-done.7.refs_4_.refs_9_ = bf16[4,2,256,128]{3,2,1,0:T(8,128)(2,1)} collective-permute-done((bf16[4,2,256,128]{3,2,1,0:T(8,128)(2,1)}, bf16[4,2,256,128]{3,2,1,0:T(8,128)(2,1)}, u32[]{:S(2)}, u32[]{:S(2)}) %collective-permute-start.7) | collective-permute-done | bytes 524320 | tf_op jit(solution)/shard_map/ppermute | solution.py:474
  51.9 0.5 collective-permute-start.12
  52.5 0.5 collective-permute-start.13
  53.0 1.6 %copy-done.6 = bf16[1,256,32,128]{3,2,1,0:T(8,128)(2,1)S(1)} copy-done((bf16[1,256,32,128]{3,2,1,0:T(8,128)(2,1)S(1)}, bf16[1,256,32,128]{3,2,1,0:T(8,128)(2,1)}, u32[]{:S(2)}) %copy-start.6) | copy-done | bytes 2097176
  54.6 19.2 %shard_map.115 = bf16[1,256,32,128]{3,2,1,0:T(8,128)(2,1)} custom-call(s32[4]{0:T(128)S(1)} %compare_select_fusion.3.earlier_ref, bf16[1,256,32,128]{3,2,1,0:T(8,128)(2,1)S(1)} %copy-done.6, bf16[4,2,256,128]{3,2,1,0:T(8,128)(2,1)S(1)} %shard_map.113.refs_1_.refs_6_, bf16[4,2,256,128]{3,2,1,0:T(8,128)(2,1)S(1)} %collective-permute-done.refs_2_.refs_7_, ...), custom_call_target="tpu_custom_call" | custom-call | flops 17179869184 | bytes 4000000 | tf_op jit(solution)/shard_map/pallas_call | solution.py:159
  73.8 0.8 copy-done.11
  74.6 0.8 copy-done.2
  75.4 0.0 collective-permute-start.14
  75.5 0.1 copy.17
  75.5 0.1 broadcast_in_dim.20
  75.6 0.1 copy.16
  75.7 0.1 reshape.39.refs_0_
  75.8 0.1 pad_add_fusion.refs_2_.meta_ref
  75.9 0.1 select_reduce_fusion.refs_1_
  76.0 1.6 %collective-permute-done.14.refs_21_ = bf16[4,2,256,128]{3,2,1,0:T(8,128)(2,1)} collective-permute-done((bf16[4,2,256,128]{3,2,1,0:T(8,128)(2,1)}, bf16[4,2,256,128]{3,2,1,0:T(8,128)(2,1)}, u32[]{:S(2)}, u32[]{:S(2)}) %collective-permute-start.14) | collective-permute-done | bytes 524320 | tf_op jit(solution)/shard_map/ppermute | solution.py:478
  77.7 1.0 copy-done.3
  78.7 15.2 %shard_map.117 = bf16[16,128,128]{2,1,0:T(8,128)(2,1)S(1)} custom-call(s32[128]{0:T(128)S(1)} %reshape.39.refs_0_, s32[16]{0:T(128)S(1)} %select_reduce_fusion.refs_1_, s32[2]{0:T(128)S(1)} %pad_add_fusion.refs_2_.meta_ref, bf16[32,128,128]{2,1,0:T(8,128)(2,1)} %bitcast.9, f32[32,128,128]{2,1,0:T(8,128)} %copy-done, ...), custom_call_target="tpu_custom_call" | custom-call | flops 2147483648 | bytes 8000000 | tf_op jit(solution)/shard_map/pallas_call | solution.py:340
  93.9 1.6 %collective-permute-start.15 = (bf16[16,128,128]{2,1,0:T(8,128)(2,1)S(1)}, bf16[16,128,128]{2,1,0:T(8,128)(2,1)S(1)}, u32[]{:S(2)}, u32[]{:S(2)}) collective-permute-start(bf16[16,128,128]{2,1,0:T(8,128)(2,1)S(1)} %shard_map.117), channel_id=1, source_target_pairs={{0,1},{1,0},{2,3},{3,2},{4,5},{5,4},{6,7},{7,6},{8,9},{9,8},{10,11... | collective-permute-start | bytes 1572872 | tf_op jit(solution)/shard_map/ppermute | solution.py:498
  95.5 15.2 %shard_map.116.refs_0_ = bf16[16,128,128]{2,1,0:T(8,128)(2,1)S(1)} custom-call(s32[128]{0:T(128)S(1)} %reshape.39.refs_0_, s32[16]{0:T(128)S(1)} %select_reduce_fusion.refs_1_, s32[2]{0:T(128)S(1)} %pad_add_fusion.refs_2_.meta_ref, bf16[32,128,128]{2,1,0:T(8,128)(2,1)} %bitcast.10, f32[32,128,128]{2,1,0:T(8,128)} %copy-done, ...), custom_call_target="tpu_custom_call" | custom-call | flops 2147483648 | bytes 8000000 | tf_op jit(solution)/shard_map/pallas_call | solution.py:340
  110.7 1.8 %shard_map.118 = bf16[16,4,8192]{2,1,0:T(4,128)(2,1)} custom-call(s32[2]{0:T(128)S(1)} %pad_add_fusion.refs_2_.meta_ref, bf16[16,128,128]{2,1,0:T(8,128)(2,1)S(1)} %shard_map.116.refs_0_, bf16[16,128,128]{2,1,0:T(8,128)(2,1)S(1)} %collective-permute-done.15.refs_1_), custom_call_target="tpu_custom_call" | custom-call | bytes 2000000 | tf_op jit(solution)/shard_map/pallas_call | solution.py:398
  (25 shorter events, 0.1 us)
Async XLA Ops:
  0.6 1.0 copy-start.4
  1.6 0.9 copy-start.5
  3.0 16.6 %collective-permute-start.2 = (bf16[4,2,256,128]{3,2,1,0:T(8,128)(2,1)S(1)}, bf16[4,2,256,128]{3,2,1,0:T(8,128)(2,1)S(1)}, u32[]{:S(2)}, u32[]{:S(2)}) collective-permute-start(bf16[4,2,256,128]{3,2,1,0:T(8,128)(2,1)S(1)} %shard_map.113.refs_1_.refs_6_), channel_id=1, source_target_pairs={{0,16},{8,24},{16,0},{24,8},{1,17},{9,25},{17,1},{25,9},{2,18},{10... | collective-permute-start | bytes 1572872 | tf_op jit(solution)/shard_map/ppermute | solution.py:478
  4.6 15.1 %collective-permute-start.1 = (bf16[4,2,256,128]{3,2,1,0:T(8,128)(2,1)S(1)}, bf16[4,2,256,128]{3,2,1,0:T(8,128)(2,1)S(1)}, u32[]{:S(2)}, u32[]{:S(2)}) collective-permute-start(bf16[4,2,256,128]{3,2,1,0:T(8,128)(2,1)S(1)} %shard_map.113.refs_1_.refs_6_), channel_id=1, source_target_pairs={{0,8},{8,0},{16,24},{24,16},{1,9},{9,1},{17,25},{25,17},{2,10},{10... | collective-permute-start | bytes 1572872 | tf_op jit(solution)/shard_map/ppermute | solution.py:478
  4.6 15.1 %collective-permute-start = (bf16[4,2,256,128]{3,2,1,0:T(8,128)(2,1)S(1)}, bf16[4,2,256,128]{3,2,1,0:T(8,128)(2,1)S(1)}, u32[]{:S(2)}, u32[]{:S(2)}) collective-permute-start(bf16[4,2,256,128]{3,2,1,0:T(8,128)(2,1)S(1)} %shard_map.113.refs_1_.refs_6_), channel_id=1, source_target_pairs={{0,4},{4,6},{6,2},{2,0},{1,5},{5,7},{7,3},{3,1},{8,12},{12,14},{14... | collective-permute-start | bytes 1572872 | tf_op jit(solution)/shard_map/ppermute | solution.py:474
  4.9 1.2 %copy-start.1 = (bf16[32,4,32,128]{3,2,1,0:T(8,128)(2,1)S(1)}, bf16[32,4,32,128]{3,2,1,0:T(8,128)(2,1)}, u32[]{:S(2)}) copy-start(bf16[32,4,32,128]{3,2,1,0:T(8,128)(2,1)} %param.13) | copy-start | bytes 3145732
  6.1 0.9 copy-start.7
  7.0 0.9 copy-start.8
  7.9 0.7 copy-start.9
  18.3 1.3 %copy-start = (f32[32,128,128]{2,1,0:T(8,128)}, f32[32,128,128]{2,1,0:T(8,128)S(1)}, u32[]{:S(2)}) copy-start(f32[32,128,128]{2,1,0:T(8,128)S(1)} %get-tuple-element.30.refs_4_) | copy-start | bytes 6291460
  19.7 2.0 %collective-permute-start.6 = (bf16[4,2,256,128]{3,2,1,0:T(8,128)(2,1)S(1)}, bf16[4,2,256,128]{3,2,1,0:T(8,128)(2,1)S(1)}, u32[]{:S(2)}, u32[]{:S(2)}) collective-permute-start(bf16[4,2,256,128]{3,2,1,0:T(8,128)(2,1)S(1)} %collective-permute-done.2.refs_14_), channel_id=1, source_target_pairs={{0,8},{8,0},{16,24},{24,16},{1,9},{9,1},{17,25},{25,17},{2,10},{10... | collective-permute-start | bytes 1572872 | tf_op jit(solution)/shard_map/ppermute | solution.py:478
  20.0 14.1 %collective-permute-start.5 = (bf16[4,2,256,128]{3,2,1,0:T(8,128)(2,1)S(1)}, bf16[4,2,256,128]{3,2,1,0:T(8,128)(2,1)S(1)}, u32[]{:S(2)}, u32[]{:S(2)}) collective-permute-start(bf16[4,2,256,128]{3,2,1,0:T(8,128)(2,1)S(1)} %collective-permute-done.refs_2_.refs_7_), channel_id=1, source_target_pairs={{0,16},{8,24},{16,0},{24,8},{1,17},{9,25},{17,1},{25,9},{2,18},{10... | collective-permute-start | bytes 1572872 | tf_op jit(solution)/shard_map/ppermute | solution.py:478
  20.5 13.6 %collective-permute-start.4 = (bf16[4,2,256,128]{3,2,1,0:T(8,128)(2,1)S(1)}, bf16[4,2,256,128]{3,2,1,0:T(8,128)(2,1)S(1)}, u32[]{:S(2)}, u32[]{:S(2)}) collective-permute-start(bf16[4,2,256,128]{3,2,1,0:T(8,128)(2,1)S(1)} %collective-permute-done.refs_2_.refs_7_), channel_id=1, source_target_pairs={{0,8},{8,0},{16,24},{24,16},{1,9},{9,1},{17,25},{25,17},{2,10},{10... | collective-permute-start | bytes 1572872 | tf_op jit(solution)/shard_map/ppermute | solution.py:478
  20.5 14.4 %collective-permute-start.3 = (bf16[4,2,256,128]{3,2,1,0:T(8,128)(2,1)S(1)}, bf16[4,2,256,128]{3,2,1,0:T(8,128)(2,1)}, u32[]{:S(2)}, u32[]{:S(2)}) collective-permute-start(bf16[4,2,256,128]{3,2,1,0:T(8,128)(2,1)S(1)} %collective-permute-done.refs_2_.refs_7_), channel_id=1, source_target_pairs={{0,4},{4,6},{6,2},{2,0},{1,5},{5,7},{7,3},{3,1},{8,12},{12,14},{14... | collective-permute-start | bytes 1572872 | tf_op jit(solution)/shard_map/ppermute | solution.py:474
  21.6 13.3 %copy-start.10 = (bf16[4,2,256,128]{3,2,1,0:T(8,128)(2,1)}, bf16[4,2,256,128]{3,2,1,0:T(8,128)(2,1)S(1)}, u32[]{:S(2)}) copy-start(bf16[4,2,256,128]{3,2,1,0:T(8,128)(2,1)S(1)} %collective-permute-done.6.refs_18_) | copy-start | bytes 1572868
  34.9 4.4 %collective-permute-start.10 = (bf16[4,2,256,128]{3,2,1,0:T(8,128)(2,1)S(1)}, bf16[4,2,256,128]{3,2,1,0:T(8,128)(2,1)}, u32[]{:S(2)}, u32[]{:S(2)}) collective-permute-start(bf16[4,2,256,128]{3,2,1,0:T(8,128)(2,1)S(1)} %collective-permute-done.5.refs_15_), channel_id=1, source_target_pairs={{0,8},{8,0},{16,24},{24,16},{1,9},{9,1},{17,25},{25,17},{2,10},{10... | collective-permute-start | bytes 1572872 | tf_op jit(solution)/shard_map/ppermute | solution.py:478
  34.9 14.7 %collective-permute-start.9 = (bf16[4,2,256,128]{3,2,1,0:T(8,128)(2,1)}, bf16[4,2,256,128]{3,2,1,0:T(8,128)(2,1)}, u32[]{:S(2)}, u32[]{:S(2)}) collective-permute-start(bf16[4,2,256,128]{3,2,1,0:T(8,128)(2,1)} %collective-permute-done.3.refs_3_.refs_8_), channel_id=1, source_target_pairs={{0,16},{8,24},{16,0},{24,8},{1,17},{9,25},{17,1},{25,9},{2,18},{10... | collective-permute-start | bytes 1572872 | tf_op jit(solution)/shard_map/ppermute | solution.py:478
  36.4 13.2 %collective-permute-start.8 = (bf16[4,2,256,128]{3,2,1,0:T(8,128)(2,1)}, bf16[4,2,256,128]{3,2,1,0:T(8,128)(2,1)}, u32[]{:S(2)}, u32[]{:S(2)}) collective-permute-start(bf16[4,2,256,128]{3,2,1,0:T(8,128)(2,1)} %collective-permute-done.3.refs_3_.refs_8_), channel_id=1, source_target_pairs={{0,8},{8,0},{16,24},{24,16},{1,9},{9,1},{17,25},{25,17},{2,10},{10... | collective-permute-start | bytes 1572872 | tf_op jit(solution)/shard_map/ppermute | solution.py:478
  36.7 15.3 %collective-permute-start.7 = (bf16[4,2,256,128]{3,2,1,0:T(8,128)(2,1)}, bf16[4,2,256,128]{3,2,1,0:T(8,128)(2,1)}, u32[]{:S(2)}, u32[]{:S(2)}) collective-permute-start(bf16[4,2,256,128]{3,2,1,0:T(8,128)(2,1)} %collective-permute-done.3.refs_3_.refs_8_), channel_id=1, source_target_pairs={{0,4},{4,6},{6,2},{2,0},{1,5},{5,7},{7,3},{3,1},{8,12},{12,14},{14... | collective-permute-start | bytes 1572872 | tf_op jit(solution)/shard_map/ppermute | solution.py:474
  38.7 36.8 %copy-start.12 = (s32[32,4]{0,1:T(4,128)S(1)}, s32[32,4]{0,1:T(4,128)}, u32[]{:S(2)}) copy-start(s32[32,4]{0,1:T(4,128)} %param.19) | copy-start | bytes 1540
  51.9 21.9 %collective-permute-start.12 = (bf16[4,2,256,128]{3,2,1,0:T(8,128)(2,1)}, bf16[4,2,256,128]{3,2,1,0:T(8,128)(2,1)}, u32[]{:S(2)}, u32[]{:S(2)}) collective-permute-start(bf16[4,2,256,128]{3,2,1,0:T(8,128)(2,1)} %collective-permute-done.7.refs_4_.refs_9_), channel_id=1, source_target_pairs={{0,16},{8,24},{16,0},{24,8},{1,17},{9,25},{17,1},{25,9},{2,18},{10... | collective-permute-start | bytes 1572872 | tf_op jit(solution)/shard_map/ppermute | solution.py:478
  52.5 21.4 %collective-permute-start.11 = (bf16[4,2,256,128]{3,2,1,0:T(8,128)(2,1)}, bf16[4,2,256,128]{3,2,1,0:T(8,128)(2,1)S(1)}, u32[]{:S(2)}, u32[]{:S(2)}) collective-permute-start(bf16[4,2,256,128]{3,2,1,0:T(8,128)(2,1)} %collective-permute-done.7.refs_4_.refs_9_), channel_id=1, source_target_pairs={{0,8},{8,0},{16,24},{24,16},{1,9},{9,1},{17,25},{25,17},{2,10},{10... | collective-permute-start | bytes 1572872 | tf_op jit(solution)/shard_map/ppermute | solution.py:478
  52.5 21.3 %collective-permute-start.13 = (bf16[4,2,256,128]{3,2,1,0:T(8,128)(2,1)}, bf16[4,2,256,128]{3,2,1,0:T(8,128)(2,1)S(1)}, u32[]{:S(2)}, u32[]{:S(2)}) collective-permute-start(bf16[4,2,256,128]{3,2,1,0:T(8,128)(2,1)} %collective-permute-done.9.refs_16_), channel_id=1, source_target_pairs={{0,8},{8,0},{16,24},{24,16},{1,9},{9,1},{17,25},{25,17},{2,10},{10... | collective-permute-start | bytes 1572872 | tf_op jit(solution)/shard_map/ppermute | solution.py:478
  53.0 1.6 %copy-start.6 = (bf16[1,256,32,128]{3,2,1,0:T(8,128)(2,1)S(1)}, bf16[1,256,32,128]{3,2,1,0:T(8,128)(2,1)}, u32[]{:S(2)}) copy-start(bf16[1,256,32,128]{3,2,1,0:T(8,128)(2,1)} %refs_0_.1) | copy-start | bytes 6291460
  73.8 0.8 copy-start.11
  74.6 0.8 copy-start.2
  75.4 2.3 %collective-permute-start.14 = (bf16[4,2,256,128]{3,2,1,0:T(8,128)(2,1)}, bf16[4,2,256,128]{3,2,1,0:T(8,128)(2,1)}, u32[]{:S(2)}, u32[]{:S(2)}) collective-permute-start(bf16[4,2,256,128]{3,2,1,0:T(8,128)(2,1)} %collective-permute-done.12.refs_17_), channel_id=1, source_target_pairs={{0,8},{8,0},{16,24},{24,16},{1,9},{9,1},{17,25},{25,17},{2,10},{10... | collective-permute-start | bytes 1572872 | tf_op jit(solution)/shard_map/ppermute | solution.py:478
  77.7 1.0 copy-start.3
  93.9 16.8 %collective-permute-start.15 = (bf16[16,128,128]{2,1,0:T(8,128)(2,1)S(1)}, bf16[16,128,128]{2,1,0:T(8,128)(2,1)S(1)}, u32[]{:S(2)}, u32[]{:S(2)}) collective-permute-start(bf16[16,128,128]{2,1,0:T(8,128)(2,1)S(1)} %shard_map.117), channel_id=1, source_target_pairs={{0,1},{1,0},{2,3},{3,2},{4,5},{5,4},{6,7},{7,6},{8,9},{9,8},{10,11... | collective-permute-start | bytes 1572872 | tf_op jit(solution)/shard_map/ppermute | solution.py:498

commit v5 on v4

--- a/solution.py
+++ b/solution.py
@@ -11,7 +11,7 @@
 PAGE = 128
 LOG2E = 1.4426950408889634
 NEG = -1e30
-VMEM_LIMIT = 48 * 1024 * 1024
+VMEM_LIMIT = 60 * 1024 * 1024
 
 
 def nt(a, b):
@@ -60,14 +60,32 @@
     )(k.reshape(tokens * heads, width), v.reshape(tokens * heads, width))
 
 
+def fold(a, op):
+    return functools.reduce(op, [a[:, j * 128 : (j + 1) * 128] for j in range(a.shape[1] // 128)])
+
+
+def head_queries(q_ref, heads):
+    block, q_heads, width = q_ref.shape[1:]
+    group = q_heads // heads
+    queries = q_ref[0].astype(jnp.float32)
+    return [
+        queries[:, h * group : (h + 1) * group, :].reshape(block * group, width).astype(jnp.bfloat16)
+        for h in range(heads)
+    ]
+
+
+def page_values(ref, h):
+    pages = ref.shape[2] // PAGE
+    return jnp.concatenate([ref[h, 1, pl.ds(j * PAGE, PAGE), :] for j in range(pages)], axis=1)
+
+
 def prefill_kernel(ring, group, tokens, scale, earlier_ref, *refs):
     q_ref = refs[0]
     blocks = refs[1 : 1 + ring]
-    out_ref, buf, s_ref, m_ref, l_ref, acc_ref, sems = refs[1 + ring :]
+    acc_ref, ml_ref, buf, s_ref, m_ref, l_ref, sems = refs[1 + ring :]
     own = blocks[0]
     heads = own.shape[0]
     block = q_ref.shape[1]
-    pages = tokens // PAGE
     i = pl.program_id(0)
 
     def copies():
@@ -91,20 +109,9 @@
                 copy.wait()
 
     rows = block * group
-    queries = q_ref[0].astype(jnp.float32)
-    q = [
-        queries[:, h * group : (h + 1) * group, :].reshape(rows, -1).astype(jnp.bfloat16)
-        for h in range(heads)
-    ]
-
-    def fold(a, op):
-        return functools.reduce(op, [a[:, j * 128 : (j + 1) * 128] for j in range(a.shape[1] // 128)])
-
+    q = head_queries(q_ref, heads)
     token = lax.broadcasted_iota(jnp.int32, (rows, tokens), 0) // group + i * block
     allowed = lax.broadcasted_iota(jnp.int32, (rows, tokens), 1) <= token
-
-    def values(ref, h):
-        return jnp.concatenate([ref[h, 1, pl.ds(j * PAGE, PAGE), :] for j in range(pages)], axis=1)
 
     last = ring - 1
     for h in range(heads):
@@ -125,7 +132,7 @@
         m_ref[h] = jnp.broadcast_to(m, m_ref.shape[1:])
         p = jnp.exp2((s_ref[last, h] - m) * scale)
         l_ref[h] = fold(p, jnp.add)
-        acc_ref[h] = nt(p.astype(jnp.bfloat16), values(own, h))
+        acc_ref[0, h] = nt(p.astype(jnp.bfloat16), page_values(own, h))
 
     def weigh(b, carry):
         for h in range(heads):
@@ -136,15 +143,14 @@
             ]
             l_ref[h] = l_ref[h] + functools.reduce(jnp.add, p)
             p = jnp.concatenate([a.astype(jnp.bfloat16) for a in p], axis=1)
-            acc_ref[h] = acc_ref[h] + nt(p, values(buf.at[b], h))
+            acc_ref[0, h] = acc_ref[0, h] + nt(p, page_values(buf.at[b], h))
         return carry
 
     lax.fori_loop(0, earlier_ref[0], weigh, 0)
-    out = []
+    low = lax.broadcasted_iota(jnp.int32, m_ref.shape[1:], 1) < 64
     for h in range(heads):
         total = jnp.sum(l_ref[h], axis=1, keepdims=True)
-        out.append((acc_ref[h] / total).reshape(block, group, -1))
-    out_ref[0] = jnp.concatenate(out, axis=1).astype(out_ref.dtype)
+        ml_ref[0, h] = jnp.where(low, m_ref[h], total)
 
 
 def prefill(q, blocks, earlier):
@@ -156,30 +162,85 @@
     rows = block * group
     q_spec = pl.BlockSpec((1, block, q_heads, width), lambda i, *_: (0, i, 0, 0))
     own_spec = pl.BlockSpec(blocks[0].shape, lambda i, *_: (0, 0, 0, 0))
+    state = pl.BlockSpec((1, heads, rows, width), lambda i, *_: (i, 0, 0, 0))
+    shape = jax.ShapeDtypeStruct((tokens // block, heads, rows, width), jnp.float32)
     return pl.pallas_call(
         functools.partial(prefill_kernel, ring, group, tokens, LOG2E / math.sqrt(width)),
         grid_spec=pltpu.PrefetchScalarGridSpec(
             num_scalar_prefetch=1,
             grid=(tokens // block,),
             in_specs=[q_spec, own_spec] + [pl.BlockSpec(memory_space=pl.ANY)] * (ring - 1),
-            out_specs=q_spec,
+            out_specs=[state, state],
             scratch_shapes=[
                 pltpu.VMEM((max(ring - 1, 1),) + blocks[0].shape, jnp.bfloat16),
                 pltpu.VMEM((ring, heads, rows, tokens), jnp.float32),
                 pltpu.VMEM((heads, rows, width), jnp.float32),
                 pltpu.VMEM((heads, rows, width), jnp.float32),
-                pltpu.VMEM((heads, rows, width), jnp.float32),
                 pltpu.SemaphoreType.DMA((ring,)),
             ],
+        ),
+        out_shape=[shape, shape],
+        compiler_params=params(),
+        cost_estimate=pl.CostEstimate(
+            flops=16 * q_heads * tokens * tokens * ring * width,
+            bytes_accessed=12 * 10**6,
+            transcendentals=tokens * tokens * ring * q_heads,
+        ),
+    )(earlier, q, *blocks)
+
+
+def finish_kernel(scale, needed_ref, q_ref, last_ref, acc_ref, ml_ref, out_ref):
+    heads = last_ref.shape[0]
+    block = q_ref.shape[1]
+
+    def give(parts):
+        out = [a.reshape(block, a.shape[0] // block, a.shape[1]) for a in parts]
+        out_ref[0] = jnp.concatenate(out, axis=1).astype(out_ref.dtype)
+
+    @pl.when(needed_ref[0] == 0)
+    def _():
+        give([acc_ref[0, h] / ml_ref[0, h][:, 64:65] for h in range(heads)])
+
+    @pl.when(needed_ref[0] == 1)
+    def _():
+        q = head_queries(q_ref, heads)
+        scores = [nt(q[h], last_ref[h, 0]) for h in range(heads)]
+        parts = []
+        for h in range(heads):
+            s = scores[h]
+            ml = ml_ref[0, h]
+            old, l = ml[:, :1], ml[:, 64:65]
+            m = jnp.maximum(jnp.max(s, axis=1, keepdims=True), old)
+            p = jnp.exp2((s - m) * scale)
+            shrink = jnp.exp2((old - m) * scale)
+            l = l * shrink + jnp.sum(p, axis=1, keepdims=True)
+            acc = acc_ref[0, h] * shrink + nt(p.astype(jnp.bfloat16), page_values(last_ref, h))
+            parts.append(acc / l)
+        give(parts)
+
+
+def prefill_finish(q, last, needed, acc, ml):
+    _, tokens, q_heads, width = q.shape
+    block = tokens // acc.shape[0]
+    q_spec = pl.BlockSpec((1, block, q_heads, width), lambda i, *_: (0, i, 0, 0))
+    last_spec = pl.BlockSpec(last.shape, lambda i, *_: (0, 0, 0, 0))
+    state = pl.BlockSpec((1,) + acc.shape[1:], lambda i, *_: (i, 0, 0, 0))
+    return pl.pallas_call(
+        functools.partial(finish_kernel, LOG2E / math.sqrt(width)),
+        grid_spec=pltpu.PrefetchScalarGridSpec(
+            num_scalar_prefetch=1,
+            grid=(tokens // block,),
+            in_specs=[q_spec, last_spec, state, state],
+            out_specs=q_spec,
         ),
         out_shape=jax.ShapeDtypeStruct(q.shape, jnp.bfloat16),
         compiler_params=params(),
         cost_estimate=pl.CostEstimate(
-            flops=16 * q_heads * tokens * tokens * ring * width,
-            bytes_accessed=4 * 10**6,
-            transcendentals=tokens * tokens * ring * q_heads,
-        ),
-    )(earlier, q, *blocks)
+            flops=16 * q_heads * tokens * tokens * width,
+            bytes_accessed=12 * 10**6,
+            transcendentals=tokens * tokens * q_heads,
+        ),
+    )(needed, q, last, acc, ml)
 
 
 def cache_kernel(
@@ -282,31 +343,41 @@
     lane_head = lax.broadcasted_iota(jnp.int32, (width, lanes), 1) % per_step // group
     order = one_hot(lanes, lanes, lambda r: r % steps * per_step + r // steps)
     unroll = math.gcd(2, block)
-
-    def body(g, carry):
-        scores = []
+    count = block // unroll
+
+    def pages_of(r):
+        return [slot_ref[(first + r) * extra + j] for j in range(extra)]
+
+    def score(g):
+        found = []
         for u in range(unroll):
             r = g * unroll + u
             q = q_ref[r]
-            places = [slot_ref[(first + r) * extra + j] for j in range(extra)]
             keys = jnp.concatenate(
                 [
                     jnp.concatenate([buf[place, h, 0] for h in range(heads)], axis=1)
-                    for place in places
+                    for place in pages_of(r)
                 ],
                 axis=0,
             )
             spread = jnp.concatenate([q * a for a in head_rows], axis=1)
-            scores.append((r, places, nt(keys, spread)))
+            found.append(nt(keys, spread))
+        return tuple(found)
+
+    def body(g, scores):
+        later = score(jnp.minimum(g + 1, count - 1))
         weights = []
-        for r, places, s in scores:
+        for u in range(unroll):
+            r = g * unroll + u
+            s = scores[u]
             old = ml_ref[r, 0:1]
             m = jnp.maximum(jnp.max(s, axis=0, keepdims=True), old)
             p = jnp.exp2((s - m) * scale)
             shrink = jnp.exp2((old - m) * scale)
             l = ml_ref[r, 4:5] * shrink + jnp.sum(p, axis=0, keepdims=True)
-            weights.append((r, places, p.astype(jnp.bfloat16), shrink, l))
-        for r, places, p, shrink, l in weights:
+            weights.append((r, p.astype(jnp.bfloat16), shrink, l))
+        for r, p, shrink, l in weights:
+            places = pages_of(r)
             values = jnp.concatenate(
                 [
                     jnp.concatenate([buf[place, h, 1] for place in places], axis=1)
@@ -320,15 +391,15 @@
                 part = jnp.where(lane_head == h, every[h * width : (h + 1) * width], part)
             result = ((acc_ref[r] * shrink + part) / l).astype(jnp.bfloat16)
             out_ref[r] = nt(order, result).astype(jnp.bfloat16)
-        return carry
-
-    lax.fori_loop(0, block // unroll, body, 0)
+        return later
+
+    lax.fori_loop(0, count, body, score(0))
 
 
 def decode(q, acc, ml, blocks, scalars, target, targets, extra, steps, heads, group):
     requests, lanes, width = q.shape
     per_target = requests // targets
-    block = math.gcd(8, per_target)
+    block = math.gcd(16, per_target)
     per_block = per_target // block
     slots = len(blocks)
 
@@ -458,7 +529,9 @@
     source = (where - position) % ring
     source_ctx = jnp.where(source < (ring + 1) // 2, 2 * source, 2 * (ring - 1 - source) + 1)
     flags = (source_ctx < ctx).astype(jnp.int32)
-    earlier = jnp.where(position == 0, jnp.sum(flags), flags).astype(jnp.int32)
+    flags = jnp.where(position == 0, 0, flags)
+    last_needed = flags[ring - 1 :]
+    earlier = jnp.where(position == 0, jnp.sum(flags[: ring - 1]), flags)
 
     raw = [
         a.reshape(requests, -1, width) for a in (decode_q, decode_k, decode_v, cache_k, cache_v)
@@ -479,11 +552,15 @@
         beside = ()
         if k == 0:
             beside = cache_part(*raw, cache_len.astype(jnp.int32), steps, heads, group)
+        if k == ring - 2:
+            beside = prefill(prefill_q, [gathered[0, s] for s in range(ring - 1)], earlier)
         if k == ring - 1:
-            beside = prefill(prefill_q, [gathered[0, s] for s in range(ring)], earlier)
+            beside = prefill_finish(prefill_q, gathered[0, ring - 1], last_needed, *state)
         arrived, beside = lax.optimization_barrier((arrived, beside))
         if k == 0:
             acc, ml = beside
+        if k == ring - 2:
+            state = beside
         if k == ring - 1:
             prefill_out = beside
         gathered.update(arrived)

time: 113 us -> 113 us (level)
  Pallas kernels: 61.6 us -> 80.4 us
  waiting for transfers between devices: 28.2 us -> 14.5 us
  local copies, waits for them, and re-layouts: 11.5 us -> 2.64 us
  starting transfers between devices: 8.86 us -> 10.7 us
  other arithmetic: 1.55 us -> 3.14 us
    pallas_call x0 -> x1, Pallas kernels: none -> 15.4 us  [prefill_finish(): pl.pallas_call(functools.partial(finish_kernel, LOG2E / math.sqrt(width))...]
    ppermute x12, waiting for transfers between devices: 25 us -> 11.7 us  [shards(): arrived[code ^ flip, s] = lax.ppermute(block, 'role', pairs)]
    unnamed x26 -> x28, local copies, waits for them, and re-layouts: 11.1 us -> 1.65 us
    pallas_call x1, Pallas kernels: 19.2 us -> 17.1 us  [prefill(): pl.pallas_call(functools.partial(prefill_kernel, ring, group, tokens, LOG...]
    pallas_call x1, Pallas kernels: 0.48 us -> 2.31 us  [split_heads(): pl.pallas_call(functools.partial(split_kernel, heads, tokens), out_shape=...]
    ppermute x3, starting transfers between devices: 2.12 us -> 3.7 us  [shards(): arrived[0, s + 1] = lax.ppermute(block, 'ctx', along)]
    pallas_call x1, Pallas kernels: 1.77 us -> 3.08 us  [join(): pl.pallas_call(functools.partial(join_kernel, targets, chunks, steps), gr...]
    pallas_call x2, Pallas kernels: 30.4 us -> 31.7 us  [decode(): pl.pallas_call(functools.partial(decode_kernel, slots, extra, steps, targ...]
  transfers between devices with their start and end apart: 16 -> 16, of which waited for: 6 -> 4; matrix products, arithmetic and copies ran while one was open for 2% -> 4% of each run, Pallas kernels for 39% -> 53%
where the time goes in v5:
time: 113 us; the launch traced here: 112 us
  Pallas kernels  80.4 us (71%)
  waiting for transfers between devices  14.5 us (13%)
  starting transfers between devices  10.7 us (9%)
  other arithmetic  3.14 us (3%)
  local copies, waits for them, and re-layouts  2.64 us (2%)
    pallas_call x2, Pallas kernels, decode(): pl.pallas_call(functools.partial(decode_kernel, slots, extra, steps, targ...  31.7 us
    pallas_call x1, Pallas kernels, prefill(): pl.pallas_call(functools.partial(prefill_kernel, ring, group, tokens, LOG...  17.1 us
    pallas_call x1, Pallas kernels, prefill_finish(): pl.pallas_call(functools.partial(finish_kernel, LOG2E / math.sqrt(width))...  15.4 us
    ppermute x12, waiting for transfers between devices, shards(): arrived[code ^ flip, s] = lax.ppermute(block, 'role', pairs)  11.7 us
    pallas_call x1, Pallas kernels, cache_part(): pl.pallas_call(functools.partial(cache_kernel, steps, heads, group, LOG2E...  10.9 us
    ppermute x12, starting transfers between devices, shards(): arrived[code ^ flip, s] = lax.ppermute(block, 'role', pairs)  5.44 us
    ppermute x3, starting transfers between devices, shards(): arrived[0, s + 1] = lax.ppermute(block, 'ctx', along)  3.7 us
    pallas_call x1, Pallas kernels, join(): pl.pallas_call(functools.partial(join_kernel, targets, chunks, steps), gr...  3.08 us
  transfers between devices with their start and end apart: 16, of which 4 were waited for; matrix products, arithmetic and copies ran while one was open for 4% of the time, Pallas kernels for 53%

profile of v5, /device:TPU:24, one launch (start us, length us, event | category | flops | bytes accessed | tf_op | source)
XLA Modules:
  0.0 112.2 jit_solution(11797855861153636264)
XLA Ops:
  0.6 2.3 %shard_map.113.refs_1_.refs_6_ = bf16[4,2,256,128]{3,2,1,0:T(8,128)(2,1)} custom-call(bf16[1024,128]{1,0:T(8,128)(2,1)} %bitcast.12, bf16[1024,128]{1,0:T(8,128)(2,1)} %bitcast.13), custom_call_target="tpu_custom_call" | custom-call | flops 100000000 | bytes 2000000 | tf_op jit(solution)/shard_map/pallas_call | solution.py:55
  2.9 1.5 %collective-permute-start.2 = (bf16[4,2,256,128]{3,2,1,0:T(8,128)(2,1)}, bf16[4,2,256,128]{3,2,1,0:T(8,128)(2,1)S(1)}, u32[]{:S(2)}, u32[]{:S(2)}) collective-permute-start(bf16[4,2,256,128]{3,2,1,0:T(8,128)(2,1)} %shard_map.113.refs_1_.refs_6_), channel_id=1, source_target_pairs={{0,16},{8,24},{16,0},{24,8},{1,17},{9,25},{17,1},{25,9},{2,18},{10... | collective-permute-start | bytes 1572872 | tf_op jit(solution)/shard_map/ppermute | solution.py:551
  4.4 0.0 collective-permute-start.1
  4.4 0.3 collective-permute-start
  4.8 10.9 %shard_map.114 = (f32[32,128,128]{2,1,0:T(8,128)}, f32[32,8,128]{2,1,0:T(8,128)}) custom-call(s32[32]{0:T(128)} %len_ref.1, bf16[32,128,128]{2,1,0:T(8,128)(2,1)} %bitcast.9, bf16[32,16,128]{2,1,0:T(8,128)(2,1)} %bitcast.16, bf16[32,16,128]{2,1,0:T(8,128)(2,1)} %bitcast.17, bf16[32,512,128]{2,1,0:T(8,128)(2,1)} %bitcast.14, bf16[32,512,128]{2,1,0:T(8,128)(2,1)} %bitcast.15), custom_call_target="tpu_custom_call" | custom-call | flops 4294967296 | bytes 14000000 | tf_op jit(solution)/shard_map/pallas_call | solution.py:299
  15.6 1.2 %collective-permute-done.2.refs_14_ = bf16[4,2,256,128]{3,2,1,0:T(8,128)(2,1)S(1)} collective-permute-done((bf16[4,2,256,128]{3,2,1,0:T(8,128)(2,1)}, bf16[4,2,256,128]{3,2,1,0:T(8,128)(2,1)S(1)}, u32[]{:S(2)}, u32[]{:S(2)}) %collective-permute-start.2) | collective-permute-done | bytes 524320 | tf_op jit(solution)/shard_map/ppermute | solution.py:551
  16.8 0.0 collective-permute-done.1.refs_10_
  16.8 2.2 %collective-permute-done.refs_2_.refs_7_ = bf16[4,2,256,128]{3,2,1,0:T(8,128)(2,1)S(1)} collective-permute-done((bf16[4,2,256,128]{3,2,1,0:T(8,128)(2,1)}, bf16[4,2,256,128]{3,2,1,0:T(8,128)(2,1)S(1)}, u32[]{:S(2)}, u32[]{:S(2)}) %collective-permute-start) | collective-permute-done | bytes 524320 | tf_op jit(solution)/shard_map/ppermute | solution.py:547
  19.0 0.0 collective-permute-start.6
  19.0 0.5 collective-permute-start.5
  19.5 0.2 collective-permute-start.4
  19.8 1.2 %collective-permute-start.3 = (bf16[4,2,256,128]{3,2,1,0:T(8,128)(2,1)S(1)}, bf16[4,2,256,128]{3,2,1,0:T(8,128)(2,1)}, u32[]{:S(2)}, u32[]{:S(2)}) collective-permute-start(bf16[4,2,256,128]{3,2,1,0:T(8,128)(2,1)S(1)} %collective-permute-done.refs_2_.refs_7_), channel_id=1, source_target_pairs={{0,4},{4,6},{6,2},{2,0},{1,5},{5,7},{7,3},{3,1},{8,12},{12,14},{14... | collective-permute-start | bytes 1572872 | tf_op jit(solution)/shard_map/ppermute | solution.py:547
  21.0 0.6 slice_reduce_fusion
  21.6 1.2 %compare_select_fusion.3.earlier_ref = s32[4]{0:T(128)} fusion(s32[]{:T(128)} %slice_reduce_fusion, s32[]{:T(128)} %axis_index.33, s32[]{:T(128)S(6)} %select_n.77), kind=kLoop, calls=%fused_computation.40 | loop fusion | flops 92 | bytes 28 | tf_op jit(solution)/shard_map/jit(_where)/select_n | solution.py:534
  22.9 0.0 collective-permute-done.6.refs_18_
  22.9 10.5 %collective-permute-done.5.refs_15_ = bf16[4,2,256,128]{3,2,1,0:T(8,128)(2,1)S(1)} collective-permute-done((bf16[4,2,256,128]{3,2,1,0:T(8,128)(2,1)S(1)}, bf16[4,2,256,128]{3,2,1,0:T(8,128)(2,1)S(1)}, u32[]{:S(2)}, u32[]{:S(2)}) %collective-permute-start.5) | collective-permute-done | bytes 524320 | tf_op jit(solution)/shard_map/ppermute | solution.py:551
  33.3 0.0 collective-permute-done.4.refs_11_
  33.3 0.6 collective-permute-done.3.refs_3_.refs_8_
  34.0 1.5 %collective-permute-start.9 = (bf16[4,2,256,128]{3,2,1,0:T(8,128)(2,1)}, bf16[4,2,256,128]{3,2,1,0:T(8,128)(2,1)S(1)}, u32[]{:S(2)}, u32[]{:S(2)}) collective-permute-start(bf16[4,2,256,128]{3,2,1,0:T(8,128)(2,1)} %collective-permute-done.3.refs_3_.refs_8_), channel_id=1, source_target_pairs={{0,16},{8,24},{16,0},{24,8},{1,17},{9,25},{17,1},{25,9},{2,18},{10... | collective-permute-start | bytes 1572872 | tf_op jit(solution)/shard_map/ppermute | solution.py:551
  35.5 0.0 collective-permute-start.8
  35.5 2.1 %collective-permute-start.7 = (bf16[4,2,256,128]{3,2,1,0:T(8,128)(2,1)}, bf16[4,2,256,128]{3,2,1,0:T(8,128)(2,1)}, u32[]{:S(2)}, u32[]{:S(2)}) collective-permute-start(bf16[4,2,256,128]{3,2,1,0:T(8,128)(2,1)} %collective-permute-done.3.refs_3_.refs_8_), channel_id=1, source_target_pairs={{0,4},{4,6},{6,2},{2,0},{1,5},{5,7},{7,3},{3,1},{8,12},{12,14},{14... | collective-permute-start | bytes 1572872 | tf_op jit(solution)/shard_map/ppermute | solution.py:547
  37.6 0.2 collective-permute-start.10
  37.8 17.1 %shard_map.115 = (f32[4,4,512,128]{3,2,1,0:T(8,128)}, f32[4,4,512,128]{3,2,1,0:T(8,128)}) custom-call(s32[4]{0:T(128)} %compare_select_fusion.3.earlier_ref, bf16[1,256,32,128]{3,2,1,0:T(8,128)(2,1)} %q_ref.1, bf16[4,2,256,128]{3,2,1,0:T(8,128)(2,1)} %shard_map.113.refs_1_.refs_6_, bf16[4,2,256,128]{3,2,1,0:T(8,128)(2,1)} %copy-done.2, ...), custom_call_target="tpu_custom_call" | custom-call | flops 12884901888 | bytes 12000000 | tf_op jit(solution)/shard_map/pallas_call | solution.py:167
  54.9 0.0 collective-permute-done.10.refs_19_
  55.0 0.0 collective-permute-done.9.refs_16_
  55.0 0.0 collective-permute-done.8.refs_12_
  55.0 0.0 collective-permute-done.7.last_ref.refs_9_
  55.0 0.3 collective-permute-start.13
  55.3 0.5 collective-permute-start.12
  55.9 0.0 collective-permute-start.11
  55.9 0.6 slice.7.needed_ref
  56.5 15.4 %shard_map.116 = bf16[1,256,32,128]{3,2,1,0:T(8,128)(2,1)} custom-call(s32[1]{0:T(128)} %slice.7.needed_ref, bf16[1,256,32,128]{3,2,1,0:T(8,128)(2,1)} %q_ref.1, bf16[4,2,256,128]{3,2,1,0:T(8,128)(2,1)} %collective-permute-done.7.last_ref.refs_9_, f32[4,4,512,128]{3,2,1,0:T(8,128)} %get-tuple-element.35.acc_ref, f32[4,4,512,128]{3,2,1,0:T(8,128)} %get-tuple-element.36.ml_ref), custom_call_target="tpu_custom_call" | custom-call | flops 4294967296 | bytes 12000000 | tf_op jit(solution)/shard_map/pallas_call | solution.py:228
  71.9 0.0 collective-permute-done.12.refs_17_
  71.9 0.0 collective-permute-done.11.refs_13_
  72.0 0.6 collective-permute-start.14
  72.6 0.1 copy.17
  72.6 0.1 broadcast_in_dim.22
  72.8 0.1 copy.16
  72.8 0.1 reshape.39.refs_0_
  73.0 0.6 pad_add_fusion.refs_2_.meta_ref
  73.6 0.6 select_reduce_fusion.refs_1_
  74.2 0.8 copy-done.10
  75.0 15.8 %shard_map.118 = bf16[16,128,128]{2,1,0:T(8,128)(2,1)} custom-call(s32[128]{0:T(128)} %copy-done.12, s32[16]{0:T(128)} %select_reduce_fusion.refs_1_, s32[2]{0:T(128)} %pad_add_fusion.refs_2_.meta_ref, bf16[32,128,128]{2,1,0:T(8,128)(2,1)} %bitcast.10, f32[32,128,128]{2,1,0:T(8,128)} %get-tuple-element.38.refs_4_, f32[32,8,128]{2,1,0:T(8,128)} %get-tuple-element.39.refs_5_, ...), custom_call_target="tpu_custom_call" | custom-call | flops 2147483648 | bytes 8000000 | tf_op jit(solution)/shard_map/pallas_call | solution.py:411
  90.9 1.6 %collective-permute-start.15 = (bf16[16,128,128]{2,1,0:T(8,128)(2,1)}, bf16[16,128,128]{2,1,0:T(8,128)(2,1)S(1)}, u32[]{:S(2)}, u32[]{:S(2)}) collective-permute-start(bf16[16,128,128]{2,1,0:T(8,128)(2,1)} %shard_map.118), channel_id=1, source_target_pairs={{0,1},{1,0},{2,3},{3,2},{4,5},{5,4},{6,7},{7,6},{8,9},{9,8},{10,11... | collective-permute-start | bytes 1572872 | tf_op jit(solution)/shard_map/ppermute | solution.py:575
  92.5 15.8 %shard_map.117.refs_0_ = bf16[16,128,128]{2,1,0:T(8,128)(2,1)} custom-call(s32[128]{0:T(128)} %copy-done.12, s32[16]{0:T(128)} %select_reduce_fusion.refs_1_, s32[2]{0:T(128)} %pad_add_fusion.refs_2_.meta_ref, bf16[32,128,128]{2,1,0:T(8,128)(2,1)} %bitcast.11, f32[32,128,128]{2,1,0:T(8,128)} %get-tuple-element.38.refs_4_, ...), custom_call_target="tpu_custom_call" | custom-call | flops 2147483648 | bytes 8000000 | tf_op jit(solution)/shard_map/pallas_call | solution.py:411
  108.3 0.0 collective-permute-done.15.refs_1_
  108.3 0.8 copy-done.11
  109.1 3.1 %shard_map.119 = bf16[16,4,8192]{2,1,0:T(4,128)(2,1)} custom-call(s32[2]{0:T(128)} %pad_add_fusion.refs_2_.meta_ref, bf16[16,128,128]{2,1,0:T(8,128)(2,1)} %shard_map.117.refs_0_, bf16[16,128,128]{2,1,0:T(8,128)(2,1)} %copy-done.11), custom_call_target="tpu_custom_call" | custom-call | bytes 2000000 | tf_op jit(solution)/shard_map/pallas_call | solution.py:469
  (30 shorter events, 0.1 us)
Async XLA Ops:
  2.9 13.9 %collective-permute-start.2 = (bf16[4,2,256,128]{3,2,1,0:T(8,128)(2,1)}, bf16[4,2,256,128]{3,2,1,0:T(8,128)(2,1)S(1)}, u32[]{:S(2)}, u32[]{:S(2)}) collective-permute-start(bf16[4,2,256,128]{3,2,1,0:T(8,128)(2,1)} %shard_map.113.refs_1_.refs_6_), channel_id=1, source_target_pairs={{0,16},{8,24},{16,0},{24,8},{1,17},{9,25},{17,1},{25,9},{2,18},{10... | collective-permute-start | bytes 1572872 | tf_op jit(solution)/shard_map/ppermute | solution.py:551
  4.4 12.4 %collective-permute-start.1 = (bf16[4,2,256,128]{3,2,1,0:T(8,128)(2,1)}, bf16[4,2,256,128]{3,2,1,0:T(8,128)(2,1)S(1)}, u32[]{:S(2)}, u32[]{:S(2)}) collective-permute-start(bf16[4,2,256,128]{3,2,1,0:T(8,128)(2,1)} %shard_map.113.refs_1_.refs_6_), channel_id=1, source_target_pairs={{0,8},{8,0},{16,24},{24,16},{1,9},{9,1},{17,25},{25,17},{2,10},{10... | collective-permute-start | bytes 1572872 | tf_op jit(solution)/shard_map/ppermute | solution.py:551
  4.4 14.5 %collective-permute-start = (bf16[4,2,256,128]{3,2,1,0:T(8,128)(2,1)}, bf16[4,2,256,128]{3,2,1,0:T(8,128)(2,1)S(1)}, u32[]{:S(2)}, u32[]{:S(2)}) collective-permute-start(bf16[4,2,256,128]{3,2,1,0:T(8,128)(2,1)} %shard_map.113.refs_1_.refs_6_), channel_id=1, source_target_pairs={{0,4},{4,6},{6,2},{2,0},{1,5},{5,7},{7,3},{3,1},{8,12},{12,14},{14... | collective-permute-start | bytes 1572872 | tf_op jit(solution)/shard_map/ppermute | solution.py:547
  16.8 38.1 %copy-start = (bf16[4,2,256,128]{3,2,1,0:T(8,128)(2,1)}, bf16[4,2,256,128]{3,2,1,0:T(8,128)(2,1)S(1)}, u32[]{:S(2)}) copy-start(bf16[4,2,256,128]{3,2,1,0:T(8,128)(2,1)S(1)} %collective-permute-done.2.refs_14_) | copy-start | bytes 1572868
  16.8 38.1 %copy-start.1 = (bf16[4,2,256,128]{3,2,1,0:T(8,128)(2,1)}, bf16[4,2,256,128]{3,2,1,0:T(8,128)(2,1)S(1)}, u32[]{:S(2)}) copy-start(bf16[4,2,256,128]{3,2,1,0:T(8,128)(2,1)S(1)} %collective-permute-done.1.refs_10_) | copy-start | bytes 1572868
  19.0 18.8 %copy-start.2 = (bf16[4,2,256,128]{3,2,1,0:T(8,128)(2,1)}, bf16[4,2,256,128]{3,2,1,0:T(8,128)(2,1)S(1)}, u32[]{:S(2)}) copy-start(bf16[4,2,256,128]{3,2,1,0:T(8,128)(2,1)S(1)} %collective-permute-done.refs_2_.refs_7_) | copy-start | bytes 1572868
  19.0 3.9 %collective-permute-start.6 = (bf16[4,2,256,128]{3,2,1,0:T(8,128)(2,1)S(1)}, bf16[4,2,256,128]{3,2,1,0:T(8,128)(2,1)S(1)}, u32[]{:S(2)}, u32[]{:S(2)}) collective-permute-start(bf16[4,2,256,128]{3,2,1,0:T(8,128)(2,1)S(1)} %collective-permute-done.2.refs_14_), channel_id=1, source_target_pairs={{0,8},{8,0},{16,24},{24,16},{1,9},{9,1},{17,25},{25,17},{2,10},{10... | collective-permute-start | bytes 1572872 | tf_op jit(solution)/shard_map/ppermute | solution.py:551
  19.0 14.3 %collective-permute-start.5 = (bf16[4,2,256,128]{3,2,1,0:T(8,128)(2,1)S(1)}, bf16[4,2,256,128]{3,2,1,0:T(8,128)(2,1)S(1)}, u32[]{:S(2)}, u32[]{:S(2)}) collective-permute-start(bf16[4,2,256,128]{3,2,1,0:T(8,128)(2,1)S(1)} %collective-permute-done.refs_2_.refs_7_), channel_id=1, source_target_pairs={{0,16},{8,24},{16,0},{24,8},{1,17},{9,25},{17,1},{25,9},{2,18},{10... | collective-permute-start | bytes 1572872 | tf_op jit(solution)/shard_map/ppermute | solution.py:551
  19.5 13.8 %collective-permute-start.4 = (bf16[4,2,256,128]{3,2,1,0:T(8,128)(2,1)S(1)}, bf16[4,2,256,128]{3,2,1,0:T(8,128)(2,1)S(1)}, u32[]{:S(2)}, u32[]{:S(2)}) collective-permute-start(bf16[4,2,256,128]{3,2,1,0:T(8,128)(2,1)S(1)} %collective-permute-done.refs_2_.refs_7_), channel_id=1, source_target_pairs={{0,8},{8,0},{16,24},{24,16},{1,9},{9,1},{17,25},{25,17},{2,10},{10... | collective-permute-start | bytes 1572872 | tf_op jit(solution)/shard_map/ppermute | solution.py:551
  19.8 14.2 %collective-permute-start.3 = (bf16[4,2,256,128]{3,2,1,0:T(8,128)(2,1)S(1)}, bf16[4,2,256,128]{3,2,1,0:T(8,128)(2,1)}, u32[]{:S(2)}, u32[]{:S(2)}) collective-permute-start(bf16[4,2,256,128]{3,2,1,0:T(8,128)(2,1)S(1)} %collective-permute-done.refs_2_.refs_7_), channel_id=1, source_target_pairs={{0,4},{4,6},{6,2},{2,0},{1,5},{5,7},{7,3},{3,1},{8,12},{12,14},{14... | collective-permute-start | bytes 1572872 | tf_op jit(solution)/shard_map/ppermute | solution.py:547
  22.9 32.1 %copy-start.3 = (bf16[4,2,256,128]{3,2,1,0:T(8,128)(2,1)}, bf16[4,2,256,128]{3,2,1,0:T(8,128)(2,1)S(1)}, u32[]{:S(2)}) copy-start(bf16[4,2,256,128]{3,2,1,0:T(8,128)(2,1)S(1)} %collective-permute-done.6.refs_18_) | copy-start | bytes 1572868
  33.3 21.6 %copy-start.4 = (bf16[4,2,256,128]{3,2,1,0:T(8,128)(2,1)}, bf16[4,2,256,128]{3,2,1,0:T(8,128)(2,1)S(1)}, u32[]{:S(2)}) copy-start(bf16[4,2,256,128]{3,2,1,0:T(8,128)(2,1)S(1)} %collective-permute-done.5.refs_15_) | copy-start | bytes 1572868
  33.3 21.6 %copy-start.5 = (bf16[4,2,256,128]{3,2,1,0:T(8,128)(2,1)}, bf16[4,2,256,128]{3,2,1,0:T(8,128)(2,1)S(1)}, u32[]{:S(2)}) copy-start(bf16[4,2,256,128]{3,2,1,0:T(8,128)(2,1)S(1)} %collective-permute-done.4.refs_11_) | copy-start | bytes 1572868
  34.0 21.0 %collective-permute-start.9 = (bf16[4,2,256,128]{3,2,1,0:T(8,128)(2,1)}, bf16[4,2,256,128]{3,2,1,0:T(8,128)(2,1)S(1)}, u32[]{:S(2)}, u32[]{:S(2)}) collective-permute-start(bf16[4,2,256,128]{3,2,1,0:T(8,128)(2,1)} %collective-permute-done.3.refs_3_.refs_8_), channel_id=1, source_target_pairs={{0,16},{8,24},{16,0},{24,8},{1,17},{9,25},{17,1},{25,9},{2,18},{10... | collective-permute-start | bytes 1572872 | tf_op jit(solution)/shard_map/ppermute | solution.py:551
  35.5 19.5 %collective-permute-start.8 = (bf16[4,2,256,128]{3,2,1,0:T(8,128)(2,1)}, bf16[4,2,256,128]{3,2,1,0:T(8,128)(2,1)}, u32[]{:S(2)}, u32[]{:S(2)}) collective-permute-start(bf16[4,2,256,128]{3,2,1,0:T(8,128)(2,1)} %collective-permute-done.3.refs_3_.refs_8_), channel_id=1, source_target_pairs={{0,8},{8,0},{16,24},{24,16},{1,9},{9,1},{17,25},{25,17},{2,10},{10... | collective-permute-start | bytes 1572872 | tf_op jit(solution)/shard_map/ppermute | solution.py:551
  35.5 19.5 %collective-permute-start.7 = (bf16[4,2,256,128]{3,2,1,0:T(8,128)(2,1)}, bf16[4,2,256,128]{3,2,1,0:T(8,128)(2,1)}, u32[]{:S(2)}, u32[]{:S(2)}) collective-permute-start(bf16[4,2,256,128]{3,2,1,0:T(8,128)(2,1)} %collective-permute-done.3.refs_3_.refs_8_), channel_id=1, source_target_pairs={{0,4},{4,6},{6,2},{2,0},{1,5},{5,7},{7,3},{3,1},{8,12},{12,14},{14... | collective-permute-start | bytes 1572872 | tf_op jit(solution)/shard_map/ppermute | solution.py:547
  37.6 17.4 %collective-permute-start.10 = (bf16[4,2,256,128]{3,2,1,0:T(8,128)(2,1)S(1)}, bf16[4,2,256,128]{3,2,1,0:T(8,128)(2,1)}, u32[]{:S(2)}, u32[]{:S(2)}) collective-permute-start(bf16[4,2,256,128]{3,2,1,0:T(8,128)(2,1)S(1)} %collective-permute-done.5.refs_15_), channel_id=1, source_target_pairs={{0,8},{8,0},{16,24},{24,16},{1,9},{9,1},{17,25},{25,17},{2,10},{10... | collective-permute-start | bytes 1572872 | tf_op jit(solution)/shard_map/ppermute | solution.py:551
  55.0 16.9 %copy-start.6 = (bf16[4,2,256,128]{3,2,1,0:T(8,128)(2,1)}, bf16[4,2,256,128]{3,2,1,0:T(8,128)(2,1)S(1)}, u32[]{:S(2)}) copy-start(bf16[4,2,256,128]{3,2,1,0:T(8,128)(2,1)S(1)} %collective-permute-done.9.refs_16_) | copy-start | bytes 1572868
  55.0 16.9 %collective-permute-start.13 = (bf16[4,2,256,128]{3,2,1,0:T(8,128)(2,1)S(1)}, bf16[4,2,256,128]{3,2,1,0:T(8,128)(2,1)S(1)}, u32[]{:S(2)}, u32[]{:S(2)}) collective-permute-start(bf16[4,2,256,128]{3,2,1,0:T(8,128)(2,1)S(1)} %collective-permute-done.9.refs_16_), channel_id=1, source_target_pairs={{0,8},{8,0},{16,24},{24,16},{1,9},{9,1},{17,25},{25,17},{2,10},{10... | collective-permute-start | bytes 1572872 | tf_op jit(solution)/shard_map/ppermute | solution.py:551
  55.3 16.6 %collective-permute-start.12 = (bf16[4,2,256,128]{3,2,1,0:T(8,128)(2,1)}, bf16[4,2,256,128]{3,2,1,0:T(8,128)(2,1)S(1)}, u32[]{:S(2)}, u32[]{:S(2)}) collective-permute-start(bf16[4,2,256,128]{3,2,1,0:T(8,128)(2,1)} %collective-permute-done.7.last_ref.refs_9_), channel_id=1, source_target_pairs={{0,16},{8,24},{16,0},{24,8},{1,17},{9,25},{17,1},{25,9},{2,18},{10... | collective-permute-start | bytes 1572872 | tf_op jit(solution)/shard_map/ppermute | solution.py:551
  55.9 16.0 %collective-permute-start.11 = (bf16[4,2,256,128]{3,2,1,0:T(8,128)(2,1)}, bf16[4,2,256,128]{3,2,1,0:T(8,128)(2,1)S(1)}, u32[]{:S(2)}, u32[]{:S(2)}) collective-permute-start(bf16[4,2,256,128]{3,2,1,0:T(8,128)(2,1)} %collective-permute-done.7.last_ref.refs_9_), channel_id=1, source_target_pairs={{0,8},{8,0},{16,24},{24,16},{1,9},{9,1},{17,25},{25,17},{2,10},{10... | collective-permute-start | bytes 1572872 | tf_op jit(solution)/shard_map/ppermute | solution.py:551
  56.5 16.0 %copy-start.13 = (s32[32,4]{0,1:T(4,128)S(1)}, s32[32,4]{0,1:T(4,128)}, u32[]{:S(2)}) copy-start(s32[32,4]{0,1:T(4,128)} %param.19) | copy-start | bytes 1540
  71.9 2.3 %copy-start.7 = (bf16[4,2,256,128]{3,2,1,0:T(8,128)(2,1)}, bf16[4,2,256,128]{3,2,1,0:T(8,128)(2,1)S(1)}, u32[]{:S(2)}) copy-start(bf16[4,2,256,128]{3,2,1,0:T(8,128)(2,1)S(1)} %collective-permute-done.13.refs_20_) | copy-start | bytes 1572868
  71.9 2.3 %copy-start.8 = (bf16[4,2,256,128]{3,2,1,0:T(8,128)(2,1)}, bf16[4,2,256,128]{3,2,1,0:T(8,128)(2,1)S(1)}, u32[]{:S(2)}) copy-start(bf16[4,2,256,128]{3,2,1,0:T(8,128)(2,1)S(1)} %collective-permute-done.12.refs_17_) | copy-start | bytes 1572868
  71.9 2.3 %copy-start.9 = (bf16[4,2,256,128]{3,2,1,0:T(8,128)(2,1)}, bf16[4,2,256,128]{3,2,1,0:T(8,128)(2,1)S(1)}, u32[]{:S(2)}) copy-start(bf16[4,2,256,128]{3,2,1,0:T(8,128)(2,1)S(1)} %collective-permute-done.11.refs_13_) | copy-start | bytes 1572868
  72.0 2.2 %collective-permute-start.14 = (bf16[4,2,256,128]{3,2,1,0:T(8,128)(2,1)S(1)}, bf16[4,2,256,128]{3,2,1,0:T(8,128)(2,1)S(1)}, u32[]{:S(2)}, u32[]{:S(2)}) collective-permute-start(bf16[4,2,256,128]{3,2,1,0:T(8,128)(2,1)S(1)} %collective-permute-done.12.refs_17_), channel_id=1, source_target_pairs={{0,8},{8,0},{16,24},{24,16},{1,9},{9,1},{17,25},{25,17},{2,10},{10... | collective-permute-start | bytes 1572872 | tf_op jit(solution)/shard_map/ppermute | solution.py:551
  73.0 1.3 %copy-start.12 = (s32[128]{0:T(128)}, s32[128]{0:T(128)S(1)}, u32[]{:S(2)}) copy-start(s32[128]{0:T(128)S(1)} %reshape.39.refs_0_) | copy-start | bytes 1540
  74.2 0.8 copy-start.10
  90.9 17.4 %collective-permute-start.15 = (bf16[16,128,128]{2,1,0:T(8,128)(2,1)}, bf16[16,128,128]{2,1,0:T(8,128)(2,1)S(1)}, u32[]{:S(2)}, u32[]{:S(2)}) collective-permute-start(bf16[16,128,128]{2,1,0:T(8,128)(2,1)} %shard_map.118), channel_id=1, source_target_pairs={{0,1},{1,0},{2,3},{3,2},{4,5},{5,4},{6,7},{7,6},{8,9},{9,8},{10,11... | collective-permute-start | bytes 1572872 | tf_op jit(solution)/shard_map/ppermute | solution.py:575
  108.3 0.8 copy-start.11

commit v6 on v4

--- a/solution.py
+++ b/solution.py
@@ -11,7 +11,7 @@
 PAGE = 128
 LOG2E = 1.4426950408889634
 NEG = -1e30
-VMEM_LIMIT = 48 * 1024 * 1024
+VMEM_LIMIT = 60 * 1024 * 1024
 
 
 def nt(a, b):
@@ -36,25 +36,24 @@
     rows = min(tokens * heads, 256)
     step = rows // heads
     pick = one_hot(rows, rows, lambda i: (i % step) * heads + i // step)
-    moved = []
+    moved, kept = [], []
     for j in range(tokens // step):
         keys = nn(pick, k_ref[pl.ds(j * rows, rows), :]).astype(jnp.bfloat16)
         moved.append(nn(pick, v_ref[pl.ds(j * rows, rows), :]))
-        for h in range(heads):
-            out_ref[h, 0, pl.ds(j * step, step), :] = keys[h * step : (h + 1) * step]
+        kept.append(keys)
     for h in range(heads):
+        keys = jnp.concatenate([a[h * step : (h + 1) * step] for a in kept], axis=0)
         values = jnp.concatenate([a[h * step : (h + 1) * step] for a in moved], axis=0)
         for page in range(tokens // PAGE):
-            out_ref[h, 1, pl.ds(page * PAGE, PAGE), :] = values[
-                page * PAGE : (page + 1) * PAGE
-            ].T.astype(jnp.bfloat16)
+            out_ref[page, h, 0] = keys[page * PAGE : (page + 1) * PAGE]
+            out_ref[page, h, 1] = values[page * PAGE : (page + 1) * PAGE].T.astype(jnp.bfloat16)
 
 
 def split_heads(k, v):
     _, tokens, heads, width = k.shape
     return pl.pallas_call(
         functools.partial(split_kernel, heads, tokens),
-        out_shape=jax.ShapeDtypeStruct((heads, 2, tokens, width), jnp.bfloat16),
+        out_shape=jax.ShapeDtypeStruct((tokens // PAGE, heads, 2, PAGE, width), jnp.bfloat16),
         compiler_params=params(),
         cost_estimate=pl.CostEstimate(flops=10**8, bytes_accessed=2 * 10**6, transcendentals=0),
     )(k.reshape(tokens * heads, width), v.reshape(tokens * heads, width))
@@ -65,9 +64,8 @@
     blocks = refs[1 : 1 + ring]
     out_ref, buf, s_ref, m_ref, l_ref, acc_ref, sems = refs[1 + ring :]
     own = blocks[0]
-    heads = own.shape[0]
+    pages, heads = own.shape[:2]
     block = q_ref.shape[1]
-    pages = tokens // PAGE
     i = pl.program_id(0)
 
     def copies():
@@ -103,18 +101,21 @@
     token = lax.broadcasted_iota(jnp.int32, (rows, tokens), 0) // group + i * block
     allowed = lax.broadcasted_iota(jnp.int32, (rows, tokens), 1) <= token
 
+    def keys(ref, h):
+        return jnp.concatenate([ref[j, h, 0] for j in range(pages)], axis=0)
+
     def values(ref, h):
-        return jnp.concatenate([ref[h, 1, pl.ds(j * PAGE, PAGE), :] for j in range(pages)], axis=1)
+        return jnp.concatenate([ref[j, h, 1] for j in range(pages)], axis=1)
 
     last = ring - 1
     for h in range(heads):
-        s = jnp.where(allowed, nt(q[h], own[h, 0]), NEG)
+        s = jnp.where(allowed, nt(q[h], keys(own, h)), NEG)
         s_ref[last, h] = s
         m_ref[h] = fold(s, jnp.maximum)
 
     def look(b, carry):
         for h in range(heads):
-            s = nt(q[h], buf[b, h, 0])
+            s = nt(q[h], keys(buf.at[b], h))
             s_ref[b, h] = s
             m_ref[h] = jnp.maximum(m_ref[h], fold(s, jnp.maximum))
         return carry
@@ -150,12 +151,12 @@
 def prefill(q, blocks, earlier):
     _, tokens, q_heads, width = q.shape
     ring = len(blocks)
-    heads = blocks[0].shape[0]
+    heads = blocks[0].shape[1]
     group = q_heads // heads
     block = 64
     rows = block * group
     q_spec = pl.BlockSpec((1, block, q_heads, width), lambda i, *_: (0, i, 0, 0))
-    own_spec = pl.BlockSpec(blocks[0].shape, lambda i, *_: (0, 0, 0, 0))
+    own_spec = pl.BlockSpec(blocks[0].shape, lambda i, *_: (0, 0, 0, 0, 0))
     return pl.pallas_call(
         functools.partial(prefill_kernel, ring, group, tokens, LOG2E / math.sqrt(width)),
         grid_spec=pltpu.PrefetchScalarGridSpec(
@@ -264,10 +265,7 @@
 
     def copies():
         for s in range(slots):
-            start = pl.multiple_of(pick_ref[s] * PAGE, PAGE)
-            yield pltpu.make_async_copy(
-                blocks[s].at[:, :, pl.ds(start, PAGE), :], buf.at[s], sems.at[s]
-            )
+            yield pltpu.make_async_copy(blocks[s].at[pick_ref[s]], buf.at[s], sems.at[s])
 
     @pl.when(i == 0)
     def _():
@@ -282,31 +280,41 @@
     lane_head = lax.broadcasted_iota(jnp.int32, (width, lanes), 1) % per_step // group
     order = one_hot(lanes, lanes, lambda r: r % steps * per_step + r // steps)
     unroll = math.gcd(2, block)
-
-    def body(g, carry):
-        scores = []
+    count = block // unroll
+
+    def pages_of(r):
+        return [slot_ref[(first + r) * extra + j] for j in range(extra)]
+
+    def score(g):
+        found = []
         for u in range(unroll):
             r = g * unroll + u
             q = q_ref[r]
-            places = [slot_ref[(first + r) * extra + j] for j in range(extra)]
             keys = jnp.concatenate(
                 [
                     jnp.concatenate([buf[place, h, 0] for h in range(heads)], axis=1)
-                    for place in places
+                    for place in pages_of(r)
                 ],
                 axis=0,
             )
             spread = jnp.concatenate([q * a for a in head_rows], axis=1)
-            scores.append((r, places, nt(keys, spread)))
+            found.append(nt(keys, spread))
+        return tuple(found)
+
+    def body(g, scores):
+        later = score(jnp.minimum(g + 1, count - 1))
         weights = []
-        for r, places, s in scores:
+        for u in range(unroll):
+            r = g * unroll + u
+            s = scores[u]
             old = ml_ref[r, 0:1]
             m = jnp.maximum(jnp.max(s, axis=0, keepdims=True), old)
             p = jnp.exp2((s - m) * scale)
             shrink = jnp.exp2((old - m) * scale)
             l = ml_ref[r, 4:5] * shrink + jnp.sum(p, axis=0, keepdims=True)
-            weights.append((r, places, p.astype(jnp.bfloat16), shrink, l))
-        for r, places, p, shrink, l in weights:
+            weights.append((r, p.astype(jnp.bfloat16), shrink, l))
+        for r, p, shrink, l in weights:
+            places = pages_of(r)
             values = jnp.concatenate(
                 [
                     jnp.concatenate([buf[place, h, 1] for place in places], axis=1)
@@ -320,15 +328,15 @@
                 part = jnp.where(lane_head == h, every[h * width : (h + 1) * width], part)
             result = ((acc_ref[r] * shrink + part) / l).astype(jnp.bfloat16)
             out_ref[r] = nt(order, result).astype(jnp.bfloat16)
-        return carry
-
-    lax.fori_loop(0, block // unroll, body, 0)
+        return later
+
+    lax.fori_loop(0, count, body, score(0))
 
 
 def decode(q, acc, ml, blocks, scalars, target, targets, extra, steps, heads, group):
     requests, lanes, width = q.shape
     per_target = requests // targets
-    block = math.gcd(8, per_target)
+    block = math.gcd(16, per_target)
     per_block = per_target // block
     slots = len(blocks)
 
@@ -404,7 +412,7 @@
             out_specs=pl.BlockSpec((per_target, steps, half), lambda k, *_: (0, 0, k)),
         ),
         out_shape=jax.ShapeDtypeStruct((per_target, steps, half * targets), jnp.bfloat16),
-        compiler_params=params(),
+        compiler_params=pltpu.CompilerParams(vmem_limit_bytes=16 * 1024 * 1024),
         cost_estimate=pl.CostEstimate(flops=0, bytes_accessed=2 * 10**6, transcendentals=0),
     )(meta, *pieces)
 
@@ -458,7 +466,7 @@
     source = (where - position) % ring
     source_ctx = jnp.where(source < (ring + 1) // 2, 2 * source, 2 * (ring - 1 - source) + 1)
     flags = (source_ctx < ctx).astype(jnp.int32)
-    earlier = jnp.where(position == 0, jnp.sum(flags), flags).astype(jnp.int32)
+    earlier = jnp.where(position == 0, jnp.sum(flags), flags)
 
     raw = [
         a.reshape(requests, -1, width) for a in (decode_q, decode_k, decode_v, cache_k, cache_v)

time: 113 us -> 113 us (level)
  local copies, waits for them, and re-layouts: 11.5 us -> 3.07 us
  Pallas kernels: 61.6 us -> 67.3 us
  other arithmetic: 1.55 us -> 3.2 us
  starting transfers between devices: 8.86 us -> 10.3 us
    unnamed x26 -> x24, local copies, waits for them, and re-layouts: 11.1 us -> 2.68 us
    ppermute x12, waiting for transfers between devices: 25 us -> 22.9 us  [shards(): arrived[code ^ flip, s] = lax.ppermute(block, 'role', pairs)]
    pallas_call x1, Pallas kernels: 0.48 us -> 2.31 us  [split_heads(): pl.pallas_call(functools.partial(split_kernel, heads, tokens), out_shape=...]
    ppermute x3, starting transfers between devices: 2.12 us -> 3.7 us  [shards(): arrived[0, s + 1] = lax.ppermute(block, 'ctx', along)]
    ppermute x3, waiting for transfers between devices: 3.21 us -> 4.79 us  [shards(): arrived[0, s + 1] = lax.ppermute(block, 'ctx', along)]
    pallas_call x1, Pallas kernels: 19.2 us -> 20.7 us  [prefill(): pl.pallas_call(functools.partial(prefill_kernel, ring, group, tokens, LOG...]
    pallas_call x2, Pallas kernels: 30.4 us -> 31.7 us  [decode(): pl.pallas_call(functools.partial(decode_kernel, slots, extra, steps, targ...]
  transfers between devices with their start and end apart: 16 -> 16, of which waited for: 6 -> 7; matrix products, arithmetic and copies ran while one was open for 2% -> 3% of each run, Pallas kernels for 39% -> 42%
where the time goes in v6:
time: 113 us; the launch traced here: 112 us
  Pallas kernels  67.3 us (60%)
  waiting for transfers between devices  27.7 us (25%)
  starting transfers between devices  10.3 us (9%)
  other arithmetic  3.2 us (3%)
  local copies, waits for them, and re-layouts  3.07 us (3%)
    pallas_call x2, Pallas kernels, decode(): pl.pallas_call(functools.partial(decode_kernel, slots, extra, steps, targ...  31.7 us
    ppermute x12, waiting for transfers between devices, shards(): arrived[code ^ flip, s] = lax.ppermute(block, 'role', pairs)  22.9 us
    pallas_call x1, Pallas kernels, prefill(): pl.pallas_call(functools.partial(prefill_kernel, ring, group, tokens, LOG...  20.7 us
    pallas_call x1, Pallas kernels, cache_part(): pl.pallas_call(functools.partial(cache_kernel, steps, heads, group, LOG2E...  10.8 us
    ppermute x12, starting transfers between devices, shards(): arrived[code ^ flip, s] = lax.ppermute(block, 'role', pairs)  5.03 us
    ppermute x3, waiting for transfers between devices, shards(): arrived[0, s + 1] = lax.ppermute(block, 'ctx', along)  4.79 us
    ppermute x3, starting transfers between devices, shards(): arrived[0, s + 1] = lax.ppermute(block, 'ctx', along)  3.7 us
    unnamed x24, local copies, waits for them, and re-layouts  2.68 us
  transfers between devices with their start and end apart: 16, of which 7 were waited for; matrix products, arithmetic and copies ran while one was open for 3% of the time, Pallas kernels for 42%

profile of v6, /device:TPU:24, one launch (start us, length us, event | category | flops | bytes accessed | tf_op | source)
XLA Modules:
  0.0 112.3 jit_solution(263699253258738148)
XLA Ops:
  0.6 2.3 %shard_map.113.refs_1_.refs_6_ = bf16[2,4,2,128,128]{4,3,2,1,0:T(8,128)(2,1)} custom-call(bf16[1024,128]{1,0:T(8,128)(2,1)} %bitcast.12, bf16[1024,128]{1,0:T(8,128)(2,1)} %bitcast.13), custom_call_target="tpu_custom_call" | custom-call | flops 100000000 | bytes 2000000 | tf_op jit(solution)/shard_map/pallas_call | solution.py:54
  2.9 1.5 %collective-permute-start.2 = (bf16[2,4,2,128,128]{4,3,2,1,0:T(8,128)(2,1)}, bf16[2,4,2,128,128]{4,3,2,1,0:T(8,128)(2,1)S(1)}, u32[]{:S(2)}, u32[]{:S(2)}) collective-permute-start(bf16[2,4,2,128,128]{4,3,2,1,0:T(8,128)(2,1)} %shard_map.113.refs_1_.refs_6_), channel_id=1, source_target_pairs={{0,16},{8,24},{16,0},{24,8},{1,17},{9,25},{17,1},{25,9},{2,18},{10... | collective-permute-start | bytes 1572872 | tf_op jit(solution)/shard_map/ppermute | solution.py:486
  4.4 0.0 collective-permute-start.1
  4.4 0.3 collective-permute-start
  4.8 10.8 %shard_map.114 = (f32[32,128,128]{2,1,0:T(8,128)}, f32[32,8,128]{2,1,0:T(8,128)}) custom-call(s32[32]{0:T(128)} %len_ref.1, bf16[32,128,128]{2,1,0:T(8,128)(2,1)} %bitcast.9, bf16[32,16,128]{2,1,0:T(8,128)(2,1)} %bitcast.16, bf16[32,16,128]{2,1,0:T(8,128)(2,1)} %bitcast.17, bf16[32,512,128]{2,1,0:T(8,128)(2,1)} %bitcast.14, bf16[32,512,128]{2,1,0:T(8,128)(2,1)} %bitcast.15), custom_call_target="tpu_custom_call" | custom-call | flops 4294967296 | bytes 14000000 | tf_op jit(solution)/shard_map/pallas_call | solution.py:239
  15.6 1.2 %collective-permute-done.2.refs_14_ = bf16[2,4,2,128,128]{4,3,2,1,0:T(8,128)(2,1)S(1)} collective-permute-done((bf16[2,4,2,128,128]{4,3,2,1,0:T(8,128)(2,1)}, bf16[2,4,2,128,128]{4,3,2,1,0:T(8,128)(2,1)S(1)}, u32[]{:S(2)}, u32[]{:S(2)}) %collective-permute-start.2) | collective-permute-done | bytes 524320 | tf_op jit(solution)/shard_map/ppermute | solution.py:486
  16.8 0.0 collective-permute-done.1.refs_10_
  16.8 2.2 %collective-permute-done.refs_2_.refs_7_ = bf16[2,4,2,128,128]{4,3,2,1,0:T(8,128)(2,1)S(1)} collective-permute-done((bf16[2,4,2,128,128]{4,3,2,1,0:T(8,128)(2,1)}, bf16[2,4,2,128,128]{4,3,2,1,0:T(8,128)(2,1)S(1)}, u32[]{:S(2)}, u32[]{:S(2)}) %collective-permute-start) | collective-permute-done | bytes 524320 | tf_op jit(solution)/shard_map/ppermute | solution.py:482
  19.0 0.0 collective-permute-start.6
  19.0 0.5 collective-permute-start.5
  19.5 0.2 collective-permute-start.4
  19.8 1.2 %collective-permute-start.3 = (bf16[2,4,2,128,128]{4,3,2,1,0:T(8,128)(2,1)S(1)}, bf16[2,4,2,128,128]{4,3,2,1,0:T(8,128)(2,1)}, u32[]{:S(2)}, u32[]{:S(2)}) collective-permute-start(bf16[2,4,2,128,128]{4,3,2,1,0:T(8,128)(2,1)S(1)} %collective-permute-done.refs_2_.refs_7_), channel_id=1, source_target_pairs={{0,4},{4,6},{6,2},{2,0},{1,5},{5,7},{7,3},{3,1},{8,12},{12,14},{14... | collective-permute-start | bytes 1572872 | tf_op jit(solution)/shard_map/ppermute | solution.py:482
  21.0 0.0 collective-permute-done.6.refs_18_
  21.0 12.3 %collective-permute-done.5.refs_15_ = bf16[2,4,2,128,128]{4,3,2,1,0:T(8,128)(2,1)S(1)} collective-permute-done((bf16[2,4,2,128,128]{4,3,2,1,0:T(8,128)(2,1)S(1)}, bf16[2,4,2,128,128]{4,3,2,1,0:T(8,128)(2,1)S(1)}, u32[]{:S(2)}, u32[]{:S(2)}) %collective-permute-start.5) | collective-permute-done | bytes 524320 | tf_op jit(solution)/shard_map/ppermute | solution.py:486
  33.3 0.0 collective-permute-done.4.refs_11_
  33.3 0.6 collective-permute-done.3.refs_3_.refs_8_
  34.0 0.0 collective-permute-start.10
  34.0 1.5 %collective-permute-start.9 = (bf16[2,4,2,128,128]{4,3,2,1,0:T(8,128)(2,1)}, bf16[2,4,2,128,128]{4,3,2,1,0:T(8,128)(2,1)}, u32[]{:S(2)}, u32[]{:S(2)}) collective-permute-start(bf16[2,4,2,128,128]{4,3,2,1,0:T(8,128)(2,1)} %collective-permute-done.3.refs_3_.refs_8_), channel_id=1, source_target_pairs={{0,16},{8,24},{16,0},{24,8},{1,17},{9,25},{17,1},{25,9},{2,18},{10... | collective-permute-start | bytes 1572872 | tf_op jit(solution)/shard_map/ppermute | solution.py:486
  35.5 0.2 collective-permute-start.8
  35.7 2.1 %collective-permute-start.7 = (bf16[2,4,2,128,128]{4,3,2,1,0:T(8,128)(2,1)}, bf16[2,4,2,128,128]{4,3,2,1,0:T(8,128)(2,1)}, u32[]{:S(2)}, u32[]{:S(2)}) collective-permute-start(bf16[2,4,2,128,128]{4,3,2,1,0:T(8,128)(2,1)} %collective-permute-done.3.refs_3_.refs_8_), channel_id=1, source_target_pairs={{0,4},{4,6},{6,2},{2,0},{1,5},{5,7},{7,3},{3,1},{8,12},{12,14},{14... | collective-permute-start | bytes 1572872 | tf_op jit(solution)/shard_map/ppermute | solution.py:482
  37.8 0.6 fusion.12
  38.5 1.2 %compare_select_fusion.3.earlier_ref = s32[4]{0:T(128)} fusion(s32[]{:T(128)} %fusion.12, s32[]{:T(128)} %axis_index.33, s32[]{:T(128)S(6)} %select_n.73), kind=kLoop, calls=%fused_computation.40 | loop fusion | flops 88 | bytes 28 | tf_op jit(solution)/shard_map/jit(_where)/select_n | solution.py:469
  39.6 0.0 collective-permute-done.10.refs_19_
  39.7 9.0 %collective-permute-done.9.refs_16_ = bf16[2,4,2,128,128]{4,3,2,1,0:T(8,128)(2,1)} collective-permute-done((bf16[2,4,2,128,128]{4,3,2,1,0:T(8,128)(2,1)}, bf16[2,4,2,128,128]{4,3,2,1,0:T(8,128)(2,1)}, u32[]{:S(2)}, u32[]{:S(2)}) %collective-permute-start.9) | collective-permute-done | bytes 524320 | tf_op jit(solution)/shard_map/ppermute | solution.py:486
  48.6 0.0 collective-permute-done.8.refs_12_
  48.6 2.0 %collective-permute-done.7.refs_4_.refs_9_ = bf16[2,4,2,128,128]{4,3,2,1,0:T(8,128)(2,1)} collective-permute-done((bf16[2,4,2,128,128]{4,3,2,1,0:T(8,128)(2,1)}, bf16[2,4,2,128,128]{4,3,2,1,0:T(8,128)(2,1)}, u32[]{:S(2)}, u32[]{:S(2)}) %collective-permute-start.7) | collective-permute-done | bytes 524320 | tf_op jit(solution)/shard_map/ppermute | solution.py:482
  50.6 0.5 collective-permute-start.12
  51.2 0.0 collective-permute-start.11
  51.2 0.5 collective-permute-start.13
  51.7 20.7 %shard_map.115 = bf16[1,256,32,128]{3,2,1,0:T(8,128)(2,1)} custom-call(s32[4]{0:T(128)} %compare_select_fusion.3.earlier_ref, bf16[1,256,32,128]{3,2,1,0:T(8,128)(2,1)} %refs_0_.1, bf16[2,4,2,128,128]{4,3,2,1,0:T(8,128)(2,1)} %shard_map.113.refs_1_.refs_6_, bf16[2,4,2,128,128]{4,3,2,1,0:T(8,128)(2,1)} %copy-done.4, ...), custom_call_target="tpu_custom_call" | custom-call | flops 17179869184 | bytes 4000000 | tf_op jit(solution)/shard_map/pallas_call | solution.py:160
  72.4 0.0 collective-permute-done.13.refs_20_
  72.5 0.8 copy-done.8
  73.2 0.0 collective-permute-done.12.refs_17_
  73.3 0.0 collective-permute-start.14
  73.3 0.1 copy.17
  73.4 0.1 broadcast_in_dim.20
  73.5 0.1 copy.16
  73.6 0.1 reshape.39.refs_0_
  73.7 0.7 pad_add_fusion.refs_2_.meta_ref
  74.4 0.7 select_reduce_fusion.refs_1_
  75.1 0.3 collective-permute-done.14.refs_21_
  75.4 0.8 copy-done.9
  76.2 15.9 %shard_map.117 = bf16[16,128,128]{2,1,0:T(8,128)(2,1)} custom-call(s32[128]{0:T(128)} %copy-done.10, s32[16]{0:T(128)} %select_reduce_fusion.refs_1_, s32[2]{0:T(128)} %pad_add_fusion.refs_2_.meta_ref, bf16[32,128,128]{2,1,0:T(8,128)(2,1)} %bitcast.10, f32[32,128,128]{2,1,0:T(8,128)} %get-tuple-element.30.refs_4_, f32[32,8,128]{2,1,0:T(8,128)} %get-tuple-element.31.refs_5_, ...), custom_call_target="tpu_custom_call" | custom-call | flops 2147483648 | bytes 8000000 | tf_op jit(solution)/shard_map/pallas_call | solution.py:348
  92.1 1.6 %collective-permute-start.15 = (bf16[16,128,128]{2,1,0:T(8,128)(2,1)}, bf16[16,128,128]{2,1,0:T(8,128)(2,1)S(1)}, u32[]{:S(2)}, u32[]{:S(2)}) collective-permute-start(bf16[16,128,128]{2,1,0:T(8,128)(2,1)} %shard_map.117), channel_id=1, source_target_pairs={{0,1},{1,0},{2,3},{3,2},{4,5},{5,4},{6,7},{7,6},{8,9},{9,8},{10,11... | collective-permute-start | bytes 1572872 | tf_op jit(solution)/shard_map/ppermute | solution.py:506
  93.7 15.8 %shard_map.116.refs_0_ = bf16[16,128,128]{2,1,0:T(8,128)(2,1)} custom-call(s32[128]{0:T(128)} %copy-done.10, s32[16]{0:T(128)} %select_reduce_fusion.refs_1_, s32[2]{0:T(128)} %pad_add_fusion.refs_2_.meta_ref, bf16[32,128,128]{2,1,0:T(8,128)(2,1)} %bitcast.11, f32[32,128,128]{2,1,0:T(8,128)} %get-tuple-element.30.refs_4_, ...), custom_call_target="tpu_custom_call" | custom-call | flops 2147483648 | bytes 8000000 | tf_op jit(solution)/shard_map/pallas_call | solution.py:348
  109.5 0.0 collective-permute-done.15.refs_1_
  109.5 1.0 copy-done
  110.6 1.8 %shard_map.118 = bf16[16,4,8192]{2,1,0:T(4,128)(2,1)} custom-call(s32[2]{0:T(128)S(1)} %copy-done.1, bf16[16,128,128]{2,1,0:T(8,128)(2,1)S(1)} %copy-done, bf16[16,128,128]{2,1,0:T(8,128)(2,1)S(1)} %collective-permute-done.15.refs_1_), custom_call_target="tpu_custom_call" | custom-call | bytes 2000000 | tf_op jit(solution)/shard_map/pallas_call | solution.py:406
  (23 shorter events, 0.1 us)
Async XLA Ops:
  2.9 13.9 %collective-permute-start.2 = (bf16[2,4,2,128,128]{4,3,2,1,0:T(8,128)(2,1)}, bf16[2,4,2,128,128]{4,3,2,1,0:T(8,128)(2,1)S(1)}, u32[]{:S(2)}, u32[]{:S(2)}) collective-permute-start(bf16[2,4,2,128,128]{4,3,2,1,0:T(8,128)(2,1)} %shard_map.113.refs_1_.refs_6_), channel_id=1, source_target_pairs={{0,16},{8,24},{16,0},{24,8},{1,17},{9,25},{17,1},{25,9},{2,18},{10... | collective-permute-start | bytes 1572872 | tf_op jit(solution)/shard_map/ppermute | solution.py:486
  4.4 12.4 %collective-permute-start.1 = (bf16[2,4,2,128,128]{4,3,2,1,0:T(8,128)(2,1)}, bf16[2,4,2,128,128]{4,3,2,1,0:T(8,128)(2,1)S(1)}, u32[]{:S(2)}, u32[]{:S(2)}) collective-permute-start(bf16[2,4,2,128,128]{4,3,2,1,0:T(8,128)(2,1)} %shard_map.113.refs_1_.refs_6_), channel_id=1, source_target_pairs={{0,8},{8,0},{16,24},{24,16},{1,9},{9,1},{17,25},{25,17},{2,10},{10... | collective-permute-start | bytes 1572872 | tf_op jit(solution)/shard_map/ppermute | solution.py:486
  4.4 14.5 %collective-permute-start = (bf16[2,4,2,128,128]{4,3,2,1,0:T(8,128)(2,1)}, bf16[2,4,2,128,128]{4,3,2,1,0:T(8,128)(2,1)S(1)}, u32[]{:S(2)}, u32[]{:S(2)}) collective-permute-start(bf16[2,4,2,128,128]{4,3,2,1,0:T(8,128)(2,1)} %shard_map.113.refs_1_.refs_6_), channel_id=1, source_target_pairs={{0,4},{4,6},{6,2},{2,0},{1,5},{5,7},{7,3},{3,1},{8,12},{12,14},{14... | collective-permute-start | bytes 1572872 | tf_op jit(solution)/shard_map/ppermute | solution.py:482
  16.8 55.6 %copy-start.2 = (bf16[2,4,2,128,128]{4,3,2,1,0:T(8,128)(2,1)}, bf16[2,4,2,128,128]{4,3,2,1,0:T(8,128)(2,1)S(1)}, u32[]{:S(2)}) copy-start(bf16[2,4,2,128,128]{4,3,2,1,0:T(8,128)(2,1)S(1)} %collective-permute-done.2.refs_14_) | copy-start | bytes 1572868
  16.8 55.6 %copy-start.3 = (bf16[2,4,2,128,128]{4,3,2,1,0:T(8,128)(2,1)}, bf16[2,4,2,128,128]{4,3,2,1,0:T(8,128)(2,1)S(1)}, u32[]{:S(2)}) copy-start(bf16[2,4,2,128,128]{4,3,2,1,0:T(8,128)(2,1)S(1)} %collective-permute-done.1.refs_10_) | copy-start | bytes 1572868
  19.0 32.7 %copy-start.4 = (bf16[2,4,2,128,128]{4,3,2,1,0:T(8,128)(2,1)}, bf16[2,4,2,128,128]{4,3,2,1,0:T(8,128)(2,1)S(1)}, u32[]{:S(2)}) copy-start(bf16[2,4,2,128,128]{4,3,2,1,0:T(8,128)(2,1)S(1)} %collective-permute-done.refs_2_.refs_7_) | copy-start | bytes 1572868
  19.0 2.0 %collective-permute-start.6 = (bf16[2,4,2,128,128]{4,3,2,1,0:T(8,128)(2,1)S(1)}, bf16[2,4,2,128,128]{4,3,2,1,0:T(8,128)(2,1)S(1)}, u32[]{:S(2)}, u32[]{:S(2)}) collective-permute-start(bf16[2,4,2,128,128]{4,3,2,1,0:T(8,128)(2,1)S(1)} %collective-permute-done.2.refs_14_), channel_id=1, source_target_pairs={{0,8},{8,0},{16,24},{24,16},{1,9},{9,1},{17,25},{25,17},{2,10},{10... | collective-permute-start | bytes 1572872 | tf_op jit(solution)/shard_map/ppermute | solution.py:486
  19.0 14.3 %collective-permute-start.5 = (bf16[2,4,2,128,128]{4,3,2,1,0:T(8,128)(2,1)S(1)}, bf16[2,4,2,128,128]{4,3,2,1,0:T(8,128)(2,1)S(1)}, u32[]{:S(2)}, u32[]{:S(2)}) collective-permute-start(bf16[2,4,2,128,128]{4,3,2,1,0:T(8,128)(2,1)S(1)} %collective-permute-done.refs_2_.refs_7_), channel_id=1, source_target_pairs={{0,16},{8,24},{16,0},{24,8},{1,17},{9,25},{17,1},{25,9},{2,18},{10... | collective-permute-start | bytes 1572872 | tf_op jit(solution)/shard_map/ppermute | solution.py:486
  19.5 13.8 %collective-permute-start.4 = (bf16[2,4,2,128,128]{4,3,2,1,0:T(8,128)(2,1)S(1)}, bf16[2,4,2,128,128]{4,3,2,1,0:T(8,128)(2,1)S(1)}, u32[]{:S(2)}, u32[]{:S(2)}) collective-permute-start(bf16[2,4,2,128,128]{4,3,2,1,0:T(8,128)(2,1)S(1)} %collective-permute-done.refs_2_.refs_7_), channel_id=1, source_target_pairs={{0,8},{8,0},{16,24},{24,16},{1,9},{9,1},{17,25},{25,17},{2,10},{10... | collective-permute-start | bytes 1572872 | tf_op jit(solution)/shard_map/ppermute | solution.py:486
  19.8 14.2 %collective-permute-start.3 = (bf16[2,4,2,128,128]{4,3,2,1,0:T(8,128)(2,1)S(1)}, bf16[2,4,2,128,128]{4,3,2,1,0:T(8,128)(2,1)}, u32[]{:S(2)}, u32[]{:S(2)}) collective-permute-start(bf16[2,4,2,128,128]{4,3,2,1,0:T(8,128)(2,1)S(1)} %collective-permute-done.refs_2_.refs_7_), channel_id=1, source_target_pairs={{0,4},{4,6},{6,2},{2,0},{1,5},{5,7},{7,3},{3,1},{8,12},{12,14},{14... | collective-permute-start | bytes 1572872 | tf_op jit(solution)/shard_map/ppermute | solution.py:482
  21.0 51.4 %copy-start.5 = (bf16[2,4,2,128,128]{4,3,2,1,0:T(8,128)(2,1)}, bf16[2,4,2,128,128]{4,3,2,1,0:T(8,128)(2,1)S(1)}, u32[]{:S(2)}) copy-start(bf16[2,4,2,128,128]{4,3,2,1,0:T(8,128)(2,1)S(1)} %collective-permute-done.6.refs_18_) | copy-start | bytes 1572868
  33.3 39.1 %copy-start.6 = (bf16[2,4,2,128,128]{4,3,2,1,0:T(8,128)(2,1)}, bf16[2,4,2,128,128]{4,3,2,1,0:T(8,128)(2,1)S(1)}, u32[]{:S(2)}) copy-start(bf16[2,4,2,128,128]{4,3,2,1,0:T(8,128)(2,1)S(1)} %collective-permute-done.5.refs_15_) | copy-start | bytes 1572868
  33.3 39.1 %copy-start.7 = (bf16[2,4,2,128,128]{4,3,2,1,0:T(8,128)(2,1)}, bf16[2,4,2,128,128]{4,3,2,1,0:T(8,128)(2,1)S(1)}, u32[]{:S(2)}) copy-start(bf16[2,4,2,128,128]{4,3,2,1,0:T(8,128)(2,1)S(1)} %collective-permute-done.4.refs_11_) | copy-start | bytes 1572868
  34.0 5.7 %collective-permute-start.10 = (bf16[2,4,2,128,128]{4,3,2,1,0:T(8,128)(2,1)S(1)}, bf16[2,4,2,128,128]{4,3,2,1,0:T(8,128)(2,1)}, u32[]{:S(2)}, u32[]{:S(2)}) collective-permute-start(bf16[2,4,2,128,128]{4,3,2,1,0:T(8,128)(2,1)S(1)} %collective-permute-done.5.refs_15_), channel_id=1, source_target_pairs={{0,8},{8,0},{16,24},{24,16},{1,9},{9,1},{17,25},{25,17},{2,10},{10... | collective-permute-start | bytes 1572872 | tf_op jit(solution)/shard_map/ppermute | solution.py:486
  34.0 14.7 %collective-permute-start.9 = (bf16[2,4,2,128,128]{4,3,2,1,0:T(8,128)(2,1)}, bf16[2,4,2,128,128]{4,3,2,1,0:T(8,128)(2,1)}, u32[]{:S(2)}, u32[]{:S(2)}) collective-permute-start(bf16[2,4,2,128,128]{4,3,2,1,0:T(8,128)(2,1)} %collective-permute-done.3.refs_3_.refs_8_), channel_id=1, source_target_pairs={{0,16},{8,24},{16,0},{24,8},{1,17},{9,25},{17,1},{25,9},{2,18},{10... | collective-permute-start | bytes 1572872 | tf_op jit(solution)/shard_map/ppermute | solution.py:486
  35.5 13.2 %collective-permute-start.8 = (bf16[2,4,2,128,128]{4,3,2,1,0:T(8,128)(2,1)}, bf16[2,4,2,128,128]{4,3,2,1,0:T(8,128)(2,1)}, u32[]{:S(2)}, u32[]{:S(2)}) collective-permute-start(bf16[2,4,2,128,128]{4,3,2,1,0:T(8,128)(2,1)} %collective-permute-done.3.refs_3_.refs_8_), channel_id=1, source_target_pairs={{0,8},{8,0},{16,24},{24,16},{1,9},{9,1},{17,25},{25,17},{2,10},{10... | collective-permute-start | bytes 1572872 | tf_op jit(solution)/shard_map/ppermute | solution.py:486
  35.7 14.9 %collective-permute-start.7 = (bf16[2,4,2,128,128]{4,3,2,1,0:T(8,128)(2,1)}, bf16[2,4,2,128,128]{4,3,2,1,0:T(8,128)(2,1)}, u32[]{:S(2)}, u32[]{:S(2)}) collective-permute-start(bf16[2,4,2,128,128]{4,3,2,1,0:T(8,128)(2,1)} %collective-permute-done.3.refs_3_.refs_8_), channel_id=1, source_target_pairs={{0,4},{4,6},{6,2},{2,0},{1,5},{5,7},{7,3},{3,1},{8,12},{12,14},{14... | collective-permute-start | bytes 1572872 | tf_op jit(solution)/shard_map/ppermute | solution.py:482
  39.6 33.6 %copy-start.11 = (s32[32,4]{0,1:T(4,128)S(1)}, s32[32,4]{0,1:T(4,128)}, u32[]{:S(2)}) copy-start(s32[32,4]{0,1:T(4,128)} %param.19) | copy-start | bytes 1540
  50.6 22.6 %collective-permute-start.12 = (bf16[2,4,2,128,128]{4,3,2,1,0:T(8,128)(2,1)}, bf16[2,4,2,128,128]{4,3,2,1,0:T(8,128)(2,1)}, u32[]{:S(2)}, u32[]{:S(2)}) collective-permute-start(bf16[2,4,2,128,128]{4,3,2,1,0:T(8,128)(2,1)} %collective-permute-done.7.refs_4_.refs_9_), channel_id=1, source_target_pairs={{0,16},{8,24},{16,0},{24,8},{1,17},{9,25},{17,1},{25,9},{2,18},{10... | collective-permute-start | bytes 1572872 | tf_op jit(solution)/shard_map/ppermute | solution.py:486
  51.2 22.1 %collective-permute-start.11 = (bf16[2,4,2,128,128]{4,3,2,1,0:T(8,128)(2,1)}, bf16[2,4,2,128,128]{4,3,2,1,0:T(8,128)(2,1)}, u32[]{:S(2)}, u32[]{:S(2)}) collective-permute-start(bf16[2,4,2,128,128]{4,3,2,1,0:T(8,128)(2,1)} %collective-permute-done.7.refs_4_.refs_9_), channel_id=1, source_target_pairs={{0,8},{8,0},{16,24},{24,16},{1,9},{9,1},{17,25},{25,17},{2,10},{10... | collective-permute-start | bytes 1572872 | tf_op jit(solution)/shard_map/ppermute | solution.py:486
  51.2 21.3 %collective-permute-start.13 = (bf16[2,4,2,128,128]{4,3,2,1,0:T(8,128)(2,1)}, bf16[2,4,2,128,128]{4,3,2,1,0:T(8,128)(2,1)S(1)}, u32[]{:S(2)}, u32[]{:S(2)}) collective-permute-start(bf16[2,4,2,128,128]{4,3,2,1,0:T(8,128)(2,1)} %collective-permute-done.9.refs_16_), channel_id=1, source_target_pairs={{0,8},{8,0},{16,24},{24,16},{1,9},{9,1},{17,25},{25,17},{2,10},{10... | collective-permute-start | bytes 1572872 | tf_op jit(solution)/shard_map/ppermute | solution.py:486
  72.5 0.8 copy-start.8
  73.3 2.1 %collective-permute-start.14 = (bf16[2,4,2,128,128]{4,3,2,1,0:T(8,128)(2,1)}, bf16[2,4,2,128,128]{4,3,2,1,0:T(8,128)(2,1)S(1)}, u32[]{:S(2)}, u32[]{:S(2)}) collective-permute-start(bf16[2,4,2,128,128]{4,3,2,1,0:T(8,128)(2,1)} %collective-permute-done.12.refs_17_), channel_id=1, source_target_pairs={{0,8},{8,0},{16,24},{24,16},{1,9},{9,1},{17,25},{25,17},{2,10},{10... | collective-permute-start | bytes 1572872 | tf_op jit(solution)/shard_map/ppermute | solution.py:486
  73.7 1.7 %copy-start.10 = (s32[128]{0:T(128)}, s32[128]{0:T(128)S(1)}, u32[]{:S(2)}) copy-start(s32[128]{0:T(128)S(1)} %reshape.39.refs_0_) | copy-start | bytes 1540
  75.4 0.8 copy-start.9
  92.1 17.5 %copy-start.1 = (s32[2]{0:T(128)S(1)}, s32[2]{0:T(128)}, u32[]{:S(2)}) copy-start(s32[2]{0:T(128)} %pad_add_fusion.refs_2_.meta_ref) | copy-start | bytes 28
  92.1 17.4 %collective-permute-start.15 = (bf16[16,128,128]{2,1,0:T(8,128)(2,1)}, bf16[16,128,128]{2,1,0:T(8,128)(2,1)S(1)}, u32[]{:S(2)}, u32[]{:S(2)}) collective-permute-start(bf16[16,128,128]{2,1,0:T(8,128)(2,1)} %shard_map.117), channel_id=1, source_target_pairs={{0,1},{1,0},{2,3},{3,2},{4,5},{5,4},{6,7},{7,6},{8,9},{9,8},{10,11... | collective-permute-start | bytes 1572872 | tf_op jit(solution)/shard_map/ppermute | solution.py:506
  109.5 1.0 copy-start

commit v7 on v6

--- a/solution.py
+++ b/solution.py
@@ -59,22 +59,27 @@
     )(k.reshape(tokens * heads, width), v.reshape(tokens * heads, width))
 
 
-def prefill_kernel(ring, group, tokens, scale, earlier_ref, *refs):
+def prefill_kernel(own, count, slots, group, tokens, scale, needed_ref, *refs):
     q_ref = refs[0]
-    blocks = refs[1 : 1 + ring]
-    out_ref, buf, s_ref, m_ref, l_ref, acc_ref, sems = refs[1 + ring :]
-    own = blocks[0]
-    pages, heads = own.shape[:2]
+    blocks = refs[1 : 1 + count]
+    refs = refs[1 + count :]
+    if own:
+        out_ref, lse_ref, buf, s_ref, m_ref, l_ref, acc_ref, sems = refs
+    else:
+        old_ref, old_lse_ref, out_ref, buf, s_ref, m_ref, l_ref, acc_ref, sems = refs
+    pages, heads = blocks[0].shape[:2]
     block = q_ref.shape[1]
     i = pl.program_id(0)
+    rest = range(1 if own else 0, count)
+    total = sum(needed_ref[slots[c]] for c in rest)
 
     def copies():
         found = []
         place = jnp.int32(0)
-        for s in range(1, ring):
-            copy = pltpu.make_async_copy(blocks[s], buf.at[place], sems.at[s])
-            found.append((earlier_ref[s], copy))
-            place = place + earlier_ref[s]
+        for c in rest:
+            flag = needed_ref[slots[c]]
+            found.append((flag, pltpu.make_async_copy(blocks[c], buf.at[place], sems.at[c])))
+            place = place + flag
         return found
 
     @pl.when(i == 0)
@@ -98,20 +103,23 @@
     def fold(a, op):
         return functools.reduce(op, [a[:, j * 128 : (j + 1) * 128] for j in range(a.shape[1] // 128)])
 
-    token = lax.broadcasted_iota(jnp.int32, (rows, tokens), 0) // group + i * block
-    allowed = lax.broadcasted_iota(jnp.int32, (rows, tokens), 1) <= token
-
     def keys(ref, h):
         return jnp.concatenate([ref[j, h, 0] for j in range(pages)], axis=0)
 
     def values(ref, h):
         return jnp.concatenate([ref[j, h, 1] for j in range(pages)], axis=1)
 
-    last = ring - 1
-    for h in range(heads):
-        s = jnp.where(allowed, nt(q[h], keys(own, h)), NEG)
-        s_ref[last, h] = s
-        m_ref[h] = fold(s, jnp.maximum)
+    last = count - 1
+    if own:
+        token = lax.broadcasted_iota(jnp.int32, (rows, tokens), 0) // group + i * block
+        allowed = lax.broadcasted_iota(jnp.int32, (rows, tokens), 1) <= token
+        for h in range(heads):
+            s = jnp.where(allowed, nt(q[h], keys(blocks[0], h)), NEG)
+            s_ref[last, h] = s
+            m_ref[h] = fold(s, jnp.maximum)
+    else:
+        for h in range(heads):
+            m_ref[h] = old_lse_ref[0, h]
 
     def look(b, carry):
         for h in range(heads):
@@ -120,13 +128,23 @@
             m_ref[h] = jnp.maximum(m_ref[h], fold(s, jnp.maximum))
         return carry
 
-    lax.fori_loop(0, earlier_ref[0], look, 0)
+    lax.fori_loop(0, total, look, 0)
     for h in range(heads):
-        m = jnp.max(m_ref[h], axis=1, keepdims=True)
-        m_ref[h] = jnp.broadcast_to(m, m_ref.shape[1:])
-        p = jnp.exp2((s_ref[last, h] - m) * scale)
-        l_ref[h] = fold(p, jnp.add)
-        acc_ref[h] = nt(p.astype(jnp.bfloat16), values(own, h))
+        m = jnp.broadcast_to(jnp.max(m_ref[h], axis=1, keepdims=True), m_ref.shape[1:])
+        m_ref[h] = m
+        if own:
+            p = [
+                jnp.exp2((s_ref[last, h, :, pl.ds(j * 128, 128)] - m) * scale)
+                for j in range(tokens // 128)
+            ]
+            l_ref[h] = functools.reduce(jnp.add, p)
+            p = jnp.concatenate([a.astype(jnp.bfloat16) for a in p], axis=1)
+            acc_ref[h] = nt(p, values(blocks[0], h))
+        else:
+            share = jnp.exp2((old_lse_ref[0, h] - m) * scale)
+            first = lax.broadcasted_iota(jnp.int32, share.shape, 1) == 0
+            l_ref[h] = jnp.where(first, share, 0.0)
+            acc_ref[h] = old_ref[0, h] * share
 
     def weigh(b, carry):
         for h in range(heads):
@@ -140,47 +158,65 @@
             acc_ref[h] = acc_ref[h] + nt(p, values(buf.at[b], h))
         return carry
 
-    lax.fori_loop(0, earlier_ref[0], weigh, 0)
+    lax.fori_loop(0, total, weigh, 0)
     out = []
     for h in range(heads):
-        total = jnp.sum(l_ref[h], axis=1, keepdims=True)
-        out.append((acc_ref[h] / total).reshape(block, group, -1))
-    out_ref[0] = jnp.concatenate(out, axis=1).astype(out_ref.dtype)
-
-
-def prefill(q, blocks, earlier):
+        l = jnp.sum(l_ref[h], axis=1, keepdims=True)
+        l = jnp.broadcast_to(l, m_ref.shape[1:])
+        if own:
+            out_ref[0, h] = acc_ref[h] / l
+            lse_ref[0, h] = m_ref[h] + jnp.log2(l) * (1.0 / scale)
+        else:
+            out.append((acc_ref[h] / l).reshape(block, group, -1))
+    if not own:
+        out_ref[0] = jnp.concatenate(out, axis=1).astype(out_ref.dtype)
+
+
+def prefill(q, blocks, slots, needed, state):
     _, tokens, q_heads, width = q.shape
-    ring = len(blocks)
+    own = state is None
+    count = len(blocks)
     heads = blocks[0].shape[1]
     group = q_heads // heads
     block = 64
     rows = block * group
     q_spec = pl.BlockSpec((1, block, q_heads, width), lambda i, *_: (0, i, 0, 0))
     own_spec = pl.BlockSpec(blocks[0].shape, lambda i, *_: (0, 0, 0, 0, 0))
+    any_spec = pl.BlockSpec(memory_space=pl.ANY)
+    state_spec = pl.BlockSpec((1, heads, rows, width), lambda i, *_: (i, 0, 0, 0))
+    shape = jax.ShapeDtypeStruct((tokens // block, heads, rows, width), jnp.float32)
+    if own:
+        in_specs = [q_spec, own_spec] + [any_spec] * (count - 1)
+        out_specs, out_shape, state = [state_spec] * 2, [shape] * 2, ()
+    else:
+        in_specs = [q_spec] + [any_spec] * count + [state_spec] * 2
+        out_specs, out_shape = q_spec, jax.ShapeDtypeStruct(q.shape, jnp.bfloat16)
     return pl.pallas_call(
-        functools.partial(prefill_kernel, ring, group, tokens, LOG2E / math.sqrt(width)),
+        functools.partial(
+            prefill_kernel, own, count, slots, group, tokens, LOG2E / math.sqrt(width)
+        ),
         grid_spec=pltpu.PrefetchScalarGridSpec(
             num_scalar_prefetch=1,
             grid=(tokens // block,),
-            in_specs=[q_spec, own_spec] + [pl.BlockSpec(memory_space=pl.ANY)] * (ring - 1),
-            out_specs=q_spec,
+            in_specs=in_specs,
+            out_specs=out_specs,
             scratch_shapes=[
-                pltpu.VMEM((max(ring - 1, 1),) + blocks[0].shape, jnp.bfloat16),
-                pltpu.VMEM((ring, heads, rows, tokens), jnp.float32),
+                pltpu.VMEM((count,) + blocks[0].shape, jnp.bfloat16),
+                pltpu.VMEM((count, heads, rows, tokens), jnp.float32),
                 pltpu.VMEM((heads, rows, width), jnp.float32),
                 pltpu.VMEM((heads, rows, width), jnp.float32),
                 pltpu.VMEM((heads, rows, width), jnp.float32),
-                pltpu.SemaphoreType.DMA((ring,)),
+                pltpu.SemaphoreType.DMA((count,)),
             ],
         ),
-        out_shape=jax.ShapeDtypeStruct(q.shape, jnp.bfloat16),
+        out_shape=out_shape,
         compiler_params=params(),
         cost_estimate=pl.CostEstimate(
-            flops=16 * q_heads * tokens * tokens * ring * width,
-            bytes_accessed=4 * 10**6,
-            transcendentals=tokens * tokens * ring * q_heads,
-        ),
-    )(earlier, q, *blocks)
+            flops=16 * q_heads * tokens * tokens * count * width,
+            bytes_accessed=12 * 10**6,
+            transcendentals=tokens * tokens * count * q_heads,
+        ),
+    )(needed, q, *blocks, *state)
 
 
 def cache_kernel(
@@ -465,8 +501,7 @@
     where = ring_place(ctx, ring)
     source = (where - position) % ring
     source_ctx = jnp.where(source < (ring + 1) // 2, 2 * source, 2 * (ring - 1 - source) + 1)
-    flags = (source_ctx < ctx).astype(jnp.int32)
-    earlier = jnp.where(position == 0, jnp.sum(flags), flags)
+    needed = (source_ctx < ctx).astype(jnp.int32)
 
     raw = [
         a.reshape(requests, -1, width) for a in (decode_q, decode_k, decode_v, cache_k, cache_v)
@@ -475,23 +510,31 @@
     gathered = {(0, 0): split_heads(prefill_k, prefill_v)}
     fresh = [(0, 0)]
     for k in range(ring + len(flips) - 1):
-        arrived = {}
+        sends = []
         for code, s in fresh:
-            block = gathered[code, s]
-            if code == 0 and s + 1 < ring:
-                arrived[0, s + 1] = lax.ppermute(block, "ctx", along)
-            for flip in flips:
+            for flip in reversed(flips):
                 if code == 0 or flip < code & -code:
                     pairs = [(j, j ^ flip) for j in range(roles)]
-                    arrived[code ^ flip, s] = lax.ppermute(block, "role", pairs)
+                    sends.append((flip, (code, s), (code ^ flip, s), "role", pairs))
+            if code == 0 and s + 1 < ring:
+                sends.append((roles, (code, s), (0, s + 1), "ctx", along))
+        arrived = {
+            to: lax.ppermute(gathered[of], axis, pairs)
+            for _, of, to, axis, pairs in sorted(sends, key=lambda a: a[0])
+        }
         beside = ()
         if k == 0:
             beside = cache_part(*raw, cache_len.astype(jnp.int32), steps, heads, group)
+        if k == 1:
+            beside = prefill(prefill_q, [gathered[0, s] for s in (0, 1)], (0, 1), needed, None)
         if k == ring - 1:
-            beside = prefill(prefill_q, [gathered[0, s] for s in range(ring)], earlier)
+            later = tuple(range(2, ring))
+            beside = prefill(prefill_q, [gathered[0, s] for s in later], later, needed, state)
         arrived, beside = lax.optimization_barrier((arrived, beside))
         if k == 0:
             acc, ml = beside
+        if k == 1:
+            state = beside
         if k == ring - 1:
             prefill_out = beside
         gathered.update(arrived)

time: 113 us -> 107 us (0.947)
  waiting for transfers between devices: 27.7 us -> 16.4 us
  Pallas kernels: 67.3 us -> 75.6 us
  other arithmetic: 3.2 us -> 1.82 us
    ppermute x15, waiting for transfers between devices: 27.7 us -> 16.4 us  [shards(): lax.ppermute(gathered[of], axis, pairs)]
    pallas_call x1 -> x2, Pallas kernels: 20.7 us -> 28.9 us  [prefill(): pl.pallas_call(functools.partial(prefill_kernel, own, count, slots, group...]
    select_n x1 -> x0, other arithmetic: 1.18 us -> none  [shards(): earlier = jnp.where(position == 0, jnp.sum(flags), flags)]
    unnamed x24 -> x30, local copies, waits for them, and re-layouts: 2.68 us -> 1.91 us
  transfers between devices with their start and end apart: 16 -> 16, of which waited for: 7 -> 5; matrix products, arithmetic and copies ran while one was open for 3% -> 2% of each run, Pallas kernels for 42% -> 52%
where the time goes in v7:
time: 107 us
  Pallas kernels  75.6 us (71%)
  waiting for transfers between devices  16.4 us (15%)
  starting transfers between devices  9.61 us (9%)
  local copies, waits for them, and re-layouts  2.29 us (2%)
  other arithmetic  1.82 us (2%)
    pallas_call x2, Pallas kernels, decode(): pl.pallas_call(functools.partial(decode_kernel, slots, extra, steps, targ...  31.7 us
    pallas_call x2, Pallas kernels, prefill(): pl.pallas_call(functools.partial(prefill_kernel, own, count, slots, group...  28.9 us
    ppermute x15, waiting for transfers between devices, shards(): lax.ppermute(gathered[of], axis, pairs)  16.4 us
    pallas_call x1, Pallas kernels, cache_part(): pl.pallas_call(functools.partial(cache_kernel, steps, heads, group, LOG2E...  10.9 us
    ppermute x15, starting transfers between devices, shards(): lax.ppermute(gathered[of], axis, pairs)  8.02 us
    pallas_call x1, Pallas kernels, split_heads(): pl.pallas_call(functools.partial(split_kernel, heads, tokens), out_shape=...  2.31 us
  transfers between devices with their start and end apart: 16, of which 5 were waited for; matrix products, arithmetic and copies ran while one was open for 2% of the time, Pallas kernels for 52%

profile of v7, /device:TPU:24, one launch (start us, length us, event | category | flops | bytes accessed | tf_op | source)
XLA Modules:
  0.0 106.7 jit_solution(2068206487723089564)
XLA Ops:
  0.6 2.3 %shard_map.113.refs_1_.refs_6_ = bf16[2,4,2,128,128]{4,3,2,1,0:T(8,128)(2,1)} custom-call(bf16[1024,128]{1,0:T(8,128)(2,1)} %bitcast.12, bf16[1024,128]{1,0:T(8,128)(2,1)} %bitcast.13), custom_call_target="tpu_custom_call" | custom-call | flops 100000000 | bytes 2000000 | tf_op jit(solution)/shard_map/pallas_call | solution.py:54
  2.9 1.5 %collective-permute-start.2 = (bf16[2,4,2,128,128]{4,3,2,1,0:T(8,128)(2,1)}, bf16[2,4,2,128,128]{4,3,2,1,0:T(8,128)(2,1)S(1)}, u32[]{:S(2)}, u32[]{:S(2)}) collective-permute-start(bf16[2,4,2,128,128]{4,3,2,1,0:T(8,128)(2,1)} %shard_map.113.refs_1_.refs_6_), channel_id=1, source_target_pairs={{0,16},{8,24},{16,0},{24,8},{1,17},{9,25},{17,1},{25,9},{2,18},{10... | collective-permute-start | bytes 1572872 | tf_op jit(solution)/shard_map/ppermute | solution.py:522
  4.4 0.0 collective-permute-start.1
  4.4 0.3 collective-permute-start
  4.8 0.6 compare_convert_fusion.needed_ref
  5.3 10.9 %shard_map.114 = (f32[32,128,128]{2,1,0:T(8,128)}, f32[32,8,128]{2,1,0:T(8,128)}) custom-call(s32[32]{0:T(128)} %len_ref.1, bf16[32,128,128]{2,1,0:T(8,128)(2,1)} %bitcast.9, bf16[32,16,128]{2,1,0:T(8,128)(2,1)} %bitcast.16, bf16[32,16,128]{2,1,0:T(8,128)(2,1)} %bitcast.17, bf16[32,512,128]{2,1,0:T(8,128)(2,1)} %bitcast.14, bf16[32,512,128]{2,1,0:T(8,128)(2,1)} %bitcast.15), custom_call_target="tpu_custom_call" | custom-call | flops 4294967296 | bytes 14000000 | tf_op jit(solution)/shard_map/pallas_call | solution.py:275
  16.2 0.6 collective-permute-done.2.refs_14_
  16.8 0.0 collective-permute-done.1.refs_10_
  16.8 2.2 %collective-permute-done.refs_2_.refs_7_ = bf16[2,4,2,128,128]{4,3,2,1,0:T(8,128)(2,1)S(1)} collective-permute-done((bf16[2,4,2,128,128]{4,3,2,1,0:T(8,128)(2,1)}, bf16[2,4,2,128,128]{4,3,2,1,0:T(8,128)(2,1)S(1)}, u32[]{:S(2)}, u32[]{:S(2)}) %collective-permute-start) | collective-permute-done | bytes 524320 | tf_op jit(solution)/shard_map/ppermute | solution.py:522
  19.0 0.5 collective-permute-start.5
  19.5 0.0 collective-permute-start.4
  19.5 1.2 %collective-permute-start.3 = (bf16[2,4,2,128,128]{4,3,2,1,0:T(8,128)(2,1)S(1)}, bf16[2,4,2,128,128]{4,3,2,1,0:T(8,128)(2,1)S(1)}, u32[]{:S(2)}, u32[]{:S(2)}) collective-permute-start(bf16[2,4,2,128,128]{4,3,2,1,0:T(8,128)(2,1)S(1)} %collective-permute-done.refs_2_.refs_7_), channel_id=1, source_target_pairs={{0,4},{4,6},{6,2},{2,0},{1,5},{5,7},{7,3},{3,1},{8,12},{12,14},{14... | collective-permute-start | bytes 1572872 | tf_op jit(solution)/shard_map/ppermute | solution.py:522
  20.8 0.2 collective-permute-start.6
  21.0 13.5 %shard_map.115 = (f32[4,4,512,128]{3,2,1,0:T(8,128)}, f32[4,4,512,128]{3,2,1,0:T(8,128)}) custom-call(s32[4]{0:T(128)} %compare_convert_fusion.needed_ref, bf16[1,256,32,128]{3,2,1,0:T(8,128)(2,1)} %refs_0_.3, bf16[2,4,2,128,128]{4,3,2,1,0:T(8,128)(2,1)} %shard_map.113.refs_1_.refs_6_, bf16[2,4,2,128,128]{4,3,2,1,0:T(8,128)(2,1)} %copy-done.4), custom_call_target="tpu_custom_call" | custom-call | flops 8589934592 | bytes 12000000 | tf_op jit(solution)/shard_map/pallas_call | solution.py:194
  34.5 0.0 collective-permute-done.6.refs_18_
  34.6 0.0 collective-permute-done.5.refs_15_
  34.6 0.0 collective-permute-done.4.refs_11_
  34.6 0.0 collective-permute-done.3.refs_1_.refs_8_
  34.6 0.0 copy-start.14
  34.6 0.3 collective-permute-start.10
  35.0 1.5 %collective-permute-start.9 = (bf16[2,4,2,128,128]{4,3,2,1,0:T(8,128)(2,1)S(1)}, bf16[2,4,2,128,128]{4,3,2,1,0:T(8,128)(2,1)S(1)}, u32[]{:S(2)}, u32[]{:S(2)}) collective-permute-start(bf16[2,4,2,128,128]{4,3,2,1,0:T(8,128)(2,1)S(1)} %collective-permute-done.3.refs_1_.refs_8_), channel_id=1, source_target_pairs={{0,16},{8,24},{16,0},{24,8},{1,17},{9,25},{17,1},{25,9},{2,18},{10... | collective-permute-start | bytes 1572872 | tf_op jit(solution)/shard_map/ppermute | solution.py:522
  36.5 0.0 collective-permute-start.8
  36.5 1.2 %collective-permute-start.7 = (bf16[2,4,2,128,128]{4,3,2,1,0:T(8,128)(2,1)S(1)}, bf16[2,4,2,128,128]{4,3,2,1,0:T(8,128)(2,1)}, u32[]{:S(2)}, u32[]{:S(2)}) collective-permute-start(bf16[2,4,2,128,128]{4,3,2,1,0:T(8,128)(2,1)S(1)} %collective-permute-done.3.refs_1_.refs_8_), channel_id=1, source_target_pairs={{0,4},{4,6},{6,2},{2,0},{1,5},{5,7},{7,3},{3,1},{8,12},{12,14},{14... | collective-permute-start | bytes 1572872 | tf_op jit(solution)/shard_map/ppermute | solution.py:522
  37.7 0.0 collective-permute-done.10.refs_19_
  37.7 11.3 %collective-permute-done.9.refs_16_ = bf16[2,4,2,128,128]{4,3,2,1,0:T(8,128)(2,1)S(1)} collective-permute-done((bf16[2,4,2,128,128]{4,3,2,1,0:T(8,128)(2,1)S(1)}, bf16[2,4,2,128,128]{4,3,2,1,0:T(8,128)(2,1)S(1)}, u32[]{:S(2)}, u32[]{:S(2)}) %collective-permute-start.9) | collective-permute-done | bytes 524320 | tf_op jit(solution)/shard_map/ppermute | solution.py:522
  49.0 0.0 collective-permute-done.8.refs_12_
  49.0 1.9 %collective-permute-done.7.refs_2_.refs_9_ = bf16[2,4,2,128,128]{4,3,2,1,0:T(8,128)(2,1)} collective-permute-done((bf16[2,4,2,128,128]{4,3,2,1,0:T(8,128)(2,1)S(1)}, bf16[2,4,2,128,128]{4,3,2,1,0:T(8,128)(2,1)}, u32[]{:S(2)}, u32[]{:S(2)}) %collective-permute-start.7) | collective-permute-done | bytes 524320 | tf_op jit(solution)/shard_map/ppermute | solution.py:522
  50.9 0.5 collective-permute-start.12
  51.5 0.0 collective-permute-start.11
  51.5 0.5 collective-permute-start.13
  52.0 15.4 %shard_map.116 = bf16[1,256,32,128]{3,2,1,0:T(8,128)(2,1)} custom-call(s32[4]{0:T(128)} %compare_convert_fusion.needed_ref, bf16[1,256,32,128]{3,2,1,0:T(8,128)(2,1)} %refs_0_.3, bf16[2,4,2,128,128]{4,3,2,1,0:T(8,128)(2,1)} %copy-done.7, bf16[2,4,2,128,128]{4,3,2,1,0:T(8,128)(2,1)} %collective-permute-done.7.refs_2_.refs_9_, ...), custom_call_target="tpu_custom_call" | custom-call | flops 8589934592 | bytes 12000000 | tf_op jit(solution)/shard_map/pallas_call | solution.py:194
  67.5 0.0 collective-permute-done.13.refs_20_
  67.5 0.0 collective-permute-done.12.refs_17_
  67.5 0.1 collective-permute-start.14
  67.6 0.1 copy.17
  67.7 0.1 broadcast_in_dim.15
  67.8 0.1 copy.16
  67.9 0.1 reshape.39.refs_0_
  68.0 0.6 pad_add_fusion.refs_2_.meta_ref
  68.6 0.6 select_reduce_fusion.refs_1_
  69.3 0.4 collective-permute-done.14.refs_21_
  69.7 0.8 copy-done.12
  70.5 15.9 %shard_map.118 = bf16[16,128,128]{2,1,0:T(8,128)(2,1)} custom-call(s32[128]{0:T(128)} %copy-done.13, s32[16]{0:T(128)} %select_reduce_fusion.refs_1_, s32[2]{0:T(128)} %pad_add_fusion.refs_2_.meta_ref, bf16[32,128,128]{2,1,0:T(8,128)(2,1)} %bitcast.10, f32[32,128,128]{2,1,0:T(8,128)} %get-tuple-element.38.refs_4_, f32[32,8,128]{2,1,0:T(8,128)} %get-tuple-element.39.refs_5_, ...), custom_call_target="tpu_custom_call" | custom-call | flops 2147483648 | bytes 8000000 | tf_op jit(solution)/shard_map/pallas_call | solution.py:384
  86.4 1.6 %collective-permute-start.15 = (bf16[16,128,128]{2,1,0:T(8,128)(2,1)}, bf16[16,128,128]{2,1,0:T(8,128)(2,1)S(1)}, u32[]{:S(2)}, u32[]{:S(2)}) collective-permute-start(bf16[16,128,128]{2,1,0:T(8,128)(2,1)} %shard_map.118), channel_id=1, source_target_pairs={{0,1},{1,0},{2,3},{3,2},{4,5},{5,4},{6,7},{7,6},{8,9},{9,8},{10,11... | collective-permute-start | bytes 1572872 | tf_op jit(solution)/shard_map/ppermute | solution.py:549
  88.0 15.9 %shard_map.117.refs_0_ = bf16[16,128,128]{2,1,0:T(8,128)(2,1)} custom-call(s32[128]{0:T(128)} %copy-done.13, s32[16]{0:T(128)} %select_reduce_fusion.refs_1_, s32[2]{0:T(128)} %pad_add_fusion.refs_2_.meta_ref, bf16[32,128,128]{2,1,0:T(8,128)(2,1)} %bitcast.11, f32[32,128,128]{2,1,0:T(8,128)} %get-tuple-element.38.refs_4_, ...), custom_call_target="tpu_custom_call" | custom-call | flops 2147483648 | bytes 8000000 | tf_op jit(solution)/shard_map/pallas_call | solution.py:384
  103.8 0.0 collective-permute-done.15.refs_1_
  103.9 1.0 copy-done
  104.9 1.8 %shard_map.119 = bf16[16,4,8192]{2,1,0:T(4,128)(2,1)} custom-call(s32[2]{0:T(128)S(1)} %copy-done.1, bf16[16,128,128]{2,1,0:T(8,128)(2,1)S(1)} %copy-done, bf16[16,128,128]{2,1,0:T(8,128)(2,1)S(1)} %collective-permute-done.15.refs_1_), custom_call_target="tpu_custom_call" | custom-call | bytes 2000000 | tf_op jit(solution)/shard_map/pallas_call | solution.py:442
  (29 shorter events, 0.1 us)
Async XLA Ops:
  2.9 13.9 %collective-permute-start.2 = (bf16[2,4,2,128,128]{4,3,2,1,0:T(8,128)(2,1)}, bf16[2,4,2,128,128]{4,3,2,1,0:T(8,128)(2,1)S(1)}, u32[]{:S(2)}, u32[]{:S(2)}) collective-permute-start(bf16[2,4,2,128,128]{4,3,2,1,0:T(8,128)(2,1)} %shard_map.113.refs_1_.refs_6_), channel_id=1, source_target_pairs={{0,16},{8,24},{16,0},{24,8},{1,17},{9,25},{17,1},{25,9},{2,18},{10... | collective-permute-start | bytes 1572872 | tf_op jit(solution)/shard_map/ppermute | solution.py:522
  4.4 12.4 %collective-permute-start.1 = (bf16[2,4,2,128,128]{4,3,2,1,0:T(8,128)(2,1)}, bf16[2,4,2,128,128]{4,3,2,1,0:T(8,128)(2,1)S(1)}, u32[]{:S(2)}, u32[]{:S(2)}) collective-permute-start(bf16[2,4,2,128,128]{4,3,2,1,0:T(8,128)(2,1)} %shard_map.113.refs_1_.refs_6_), channel_id=1, source_target_pairs={{0,8},{8,0},{16,24},{24,16},{1,9},{9,1},{17,25},{25,17},{2,10},{10... | collective-permute-start | bytes 1572872 | tf_op jit(solution)/shard_map/ppermute | solution.py:522
  4.4 14.5 %collective-permute-start = (bf16[2,4,2,128,128]{4,3,2,1,0:T(8,128)(2,1)}, bf16[2,4,2,128,128]{4,3,2,1,0:T(8,128)(2,1)S(1)}, u32[]{:S(2)}, u32[]{:S(2)}) collective-permute-start(bf16[2,4,2,128,128]{4,3,2,1,0:T(8,128)(2,1)} %shard_map.113.refs_1_.refs_6_), channel_id=1, source_target_pairs={{0,4},{4,6},{6,2},{2,0},{1,5},{5,7},{7,3},{3,1},{8,12},{12,14},{14... | collective-permute-start | bytes 1572872 | tf_op jit(solution)/shard_map/ppermute | solution.py:522
  16.8 17.7 %copy-start.2 = (bf16[2,4,2,128,128]{4,3,2,1,0:T(8,128)(2,1)}, bf16[2,4,2,128,128]{4,3,2,1,0:T(8,128)(2,1)S(1)}, u32[]{:S(2)}) copy-start(bf16[2,4,2,128,128]{4,3,2,1,0:T(8,128)(2,1)S(1)} %collective-permute-done.2.refs_14_) | copy-start | bytes 1572868
  16.8 17.7 %copy-start.3 = (bf16[2,4,2,128,128]{4,3,2,1,0:T(8,128)(2,1)}, bf16[2,4,2,128,128]{4,3,2,1,0:T(8,128)(2,1)S(1)}, u32[]{:S(2)}) copy-start(bf16[2,4,2,128,128]{4,3,2,1,0:T(8,128)(2,1)S(1)} %collective-permute-done.1.refs_10_) | copy-start | bytes 1572868
  19.0 2.0 %copy-start.4 = (bf16[2,4,2,128,128]{4,3,2,1,0:T(8,128)(2,1)}, bf16[2,4,2,128,128]{4,3,2,1,0:T(8,128)(2,1)S(1)}, u32[]{:S(2)}) copy-start(bf16[2,4,2,128,128]{4,3,2,1,0:T(8,128)(2,1)S(1)} %collective-permute-done.refs_2_.refs_7_) | copy-start | bytes 1572868
  19.0 15.6 %collective-permute-start.5 = (bf16[2,4,2,128,128]{4,3,2,1,0:T(8,128)(2,1)S(1)}, bf16[2,4,2,128,128]{4,3,2,1,0:T(8,128)(2,1)S(1)}, u32[]{:S(2)}, u32[]{:S(2)}) collective-permute-start(bf16[2,4,2,128,128]{4,3,2,1,0:T(8,128)(2,1)S(1)} %collective-permute-done.refs_2_.refs_7_), channel_id=1, source_target_pairs={{0,16},{8,24},{16,0},{24,8},{1,17},{9,25},{17,1},{25,9},{2,18},{10... | collective-permute-start | bytes 1572872 | tf_op jit(solution)/shard_map/ppermute | solution.py:522
  19.5 15.1 %collective-permute-start.4 = (bf16[2,4,2,128,128]{4,3,2,1,0:T(8,128)(2,1)S(1)}, bf16[2,4,2,128,128]{4,3,2,1,0:T(8,128)(2,1)S(1)}, u32[]{:S(2)}, u32[]{:S(2)}) collective-permute-start(bf16[2,4,2,128,128]{4,3,2,1,0:T(8,128)(2,1)S(1)} %collective-permute-done.refs_2_.refs_7_), channel_id=1, source_target_pairs={{0,8},{8,0},{16,24},{24,16},{1,9},{9,1},{17,25},{25,17},{2,10},{10... | collective-permute-start | bytes 1572872 | tf_op jit(solution)/shard_map/ppermute | solution.py:522
  19.5 15.1 %collective-permute-start.3 = (bf16[2,4,2,128,128]{4,3,2,1,0:T(8,128)(2,1)S(1)}, bf16[2,4,2,128,128]{4,3,2,1,0:T(8,128)(2,1)S(1)}, u32[]{:S(2)}, u32[]{:S(2)}) collective-permute-start(bf16[2,4,2,128,128]{4,3,2,1,0:T(8,128)(2,1)S(1)} %collective-permute-done.refs_2_.refs_7_), channel_id=1, source_target_pairs={{0,4},{4,6},{6,2},{2,0},{1,5},{5,7},{7,3},{3,1},{8,12},{12,14},{14... | collective-permute-start | bytes 1572872 | tf_op jit(solution)/shard_map/ppermute | solution.py:522
  20.8 13.8 %collective-permute-start.6 = (bf16[2,4,2,128,128]{4,3,2,1,0:T(8,128)(2,1)S(1)}, bf16[2,4,2,128,128]{4,3,2,1,0:T(8,128)(2,1)S(1)}, u32[]{:S(2)}, u32[]{:S(2)}) collective-permute-start(bf16[2,4,2,128,128]{4,3,2,1,0:T(8,128)(2,1)S(1)} %collective-permute-done.2.refs_14_), channel_id=1, source_target_pairs={{0,8},{8,0},{16,24},{24,16},{1,9},{9,1},{17,25},{25,17},{2,10},{10... | collective-permute-start | bytes 1572872 | tf_op jit(solution)/shard_map/ppermute | solution.py:522
  34.5 32.8 %copy-start.8 = (bf16[2,4,2,128,128]{4,3,2,1,0:T(8,128)(2,1)}, bf16[2,4,2,128,128]{4,3,2,1,0:T(8,128)(2,1)S(1)}, u32[]{:S(2)}) copy-start(bf16[2,4,2,128,128]{4,3,2,1,0:T(8,128)(2,1)S(1)} %collective-permute-done.6.refs_18_) | copy-start | bytes 1572868
  34.6 32.8 %copy-start.5 = (bf16[2,4,2,128,128]{4,3,2,1,0:T(8,128)(2,1)}, bf16[2,4,2,128,128]{4,3,2,1,0:T(8,128)(2,1)S(1)}, u32[]{:S(2)}) copy-start(bf16[2,4,2,128,128]{4,3,2,1,0:T(8,128)(2,1)S(1)} %collective-permute-done.5.refs_15_) | copy-start | bytes 1572868
  34.6 32.8 %copy-start.6 = (bf16[2,4,2,128,128]{4,3,2,1,0:T(8,128)(2,1)}, bf16[2,4,2,128,128]{4,3,2,1,0:T(8,128)(2,1)S(1)}, u32[]{:S(2)}) copy-start(bf16[2,4,2,128,128]{4,3,2,1,0:T(8,128)(2,1)S(1)} %collective-permute-done.4.refs_11_) | copy-start | bytes 1572868
  34.6 17.4 %copy-start.7 = (bf16[2,4,2,128,128]{4,3,2,1,0:T(8,128)(2,1)}, bf16[2,4,2,128,128]{4,3,2,1,0:T(8,128)(2,1)S(1)}, u32[]{:S(2)}) copy-start(bf16[2,4,2,128,128]{4,3,2,1,0:T(8,128)(2,1)S(1)} %collective-permute-done.3.refs_1_.refs_8_) | copy-start | bytes 1572868
  34.6 33.0 %copy-start.14 = (s32[32,4]{0,1:T(4,128)S(1)}, s32[32,4]{0,1:T(4,128)}, u32[]{:S(2)}) copy-start(s32[32,4]{0,1:T(4,128)} %param.19) | copy-start | bytes 1540
  34.6 3.1 %collective-permute-start.10 = (bf16[2,4,2,128,128]{4,3,2,1,0:T(8,128)(2,1)S(1)}, bf16[2,4,2,128,128]{4,3,2,1,0:T(8,128)(2,1)S(1)}, u32[]{:S(2)}, u32[]{:S(2)}) collective-permute-start(bf16[2,4,2,128,128]{4,3,2,1,0:T(8,128)(2,1)S(1)} %collective-permute-done.5.refs_15_), channel_id=1, source_target_pairs={{0,8},{8,0},{16,24},{24,16},{1,9},{9,1},{17,25},{25,17},{2,10},{10... | collective-permute-start | bytes 1572872 | tf_op jit(solution)/shard_map/ppermute | solution.py:522
  35.0 14.1 %collective-permute-start.9 = (bf16[2,4,2,128,128]{4,3,2,1,0:T(8,128)(2,1)S(1)}, bf16[2,4,2,128,128]{4,3,2,1,0:T(8,128)(2,1)S(1)}, u32[]{:S(2)}, u32[]{:S(2)}) collective-permute-start(bf16[2,4,2,128,128]{4,3,2,1,0:T(8,128)(2,1)S(1)} %collective-permute-done.3.refs_1_.refs_8_), channel_id=1, source_target_pairs={{0,16},{8,24},{16,0},{24,8},{1,17},{9,25},{17,1},{25,9},{2,18},{10... | collective-permute-start | bytes 1572872 | tf_op jit(solution)/shard_map/ppermute | solution.py:522
  36.5 12.6 %collective-permute-start.8 = (bf16[2,4,2,128,128]{4,3,2,1,0:T(8,128)(2,1)S(1)}, bf16[2,4,2,128,128]{4,3,2,1,0:T(8,128)(2,1)S(1)}, u32[]{:S(2)}, u32[]{:S(2)}) collective-permute-start(bf16[2,4,2,128,128]{4,3,2,1,0:T(8,128)(2,1)S(1)} %collective-permute-done.3.refs_1_.refs_8_), channel_id=1, source_target_pairs={{0,8},{8,0},{16,24},{24,16},{1,9},{9,1},{17,25},{25,17},{2,10},{10... | collective-permute-start | bytes 1572872 | tf_op jit(solution)/shard_map/ppermute | solution.py:522
  36.5 14.4 %collective-permute-start.7 = (bf16[2,4,2,128,128]{4,3,2,1,0:T(8,128)(2,1)S(1)}, bf16[2,4,2,128,128]{4,3,2,1,0:T(8,128)(2,1)}, u32[]{:S(2)}, u32[]{:S(2)}) collective-permute-start(bf16[2,4,2,128,128]{4,3,2,1,0:T(8,128)(2,1)S(1)} %collective-permute-done.3.refs_1_.refs_8_), channel_id=1, source_target_pairs={{0,4},{4,6},{6,2},{2,0},{1,5},{5,7},{7,3},{3,1},{8,12},{12,14},{14... | collective-permute-start | bytes 1572872 | tf_op jit(solution)/shard_map/ppermute | solution.py:522
  37.7 29.7 %copy-start.9 = (bf16[2,4,2,128,128]{4,3,2,1,0:T(8,128)(2,1)}, bf16[2,4,2,128,128]{4,3,2,1,0:T(8,128)(2,1)S(1)}, u32[]{:S(2)}) copy-start(bf16[2,4,2,128,128]{4,3,2,1,0:T(8,128)(2,1)S(1)} %collective-permute-done.10.refs_19_) | copy-start | bytes 1572868
  49.0 18.4 %copy-start.10 = (bf16[2,4,2,128,128]{4,3,2,1,0:T(8,128)(2,1)}, bf16[2,4,2,128,128]{4,3,2,1,0:T(8,128)(2,1)S(1)}, u32[]{:S(2)}) copy-start(bf16[2,4,2,128,128]{4,3,2,1,0:T(8,128)(2,1)S(1)} %collective-permute-done.9.refs_16_) | copy-start | bytes 1572868
  49.0 18.4 %copy-start.11 = (bf16[2,4,2,128,128]{4,3,2,1,0:T(8,128)(2,1)}, bf16[2,4,2,128,128]{4,3,2,1,0:T(8,128)(2,1)S(1)}, u32[]{:S(2)}) copy-start(bf16[2,4,2,128,128]{4,3,2,1,0:T(8,128)(2,1)S(1)} %collective-permute-done.8.refs_12_) | copy-start | bytes 1572868
  50.9 16.5 %collective-permute-start.12 = (bf16[2,4,2,128,128]{4,3,2,1,0:T(8,128)(2,1)}, bf16[2,4,2,128,128]{4,3,2,1,0:T(8,128)(2,1)}, u32[]{:S(2)}, u32[]{:S(2)}) collective-permute-start(bf16[2,4,2,128,128]{4,3,2,1,0:T(8,128)(2,1)} %collective-permute-done.7.refs_2_.refs_9_), channel_id=1, source_target_pairs={{0,16},{8,24},{16,0},{24,8},{1,17},{9,25},{17,1},{25,9},{2,18},{10... | collective-permute-start | bytes 1572872 | tf_op jit(solution)/shard_map/ppermute | solution.py:522
  51.5 16.0 %collective-permute-start.11 = (bf16[2,4,2,128,128]{4,3,2,1,0:T(8,128)(2,1)}, bf16[2,4,2,128,128]{4,3,2,1,0:T(8,128)(2,1)}, u32[]{:S(2)}, u32[]{:S(2)}) collective-permute-start(bf16[2,4,2,128,128]{4,3,2,1,0:T(8,128)(2,1)} %collective-permute-done.7.refs_2_.refs_9_), channel_id=1, source_target_pairs={{0,8},{8,0},{16,24},{24,16},{1,9},{9,1},{17,25},{25,17},{2,10},{10... | collective-permute-start | bytes 1572872 | tf_op jit(solution)/shard_map/ppermute | solution.py:522
  51.5 16.0 %collective-permute-start.13 = (bf16[2,4,2,128,128]{4,3,2,1,0:T(8,128)(2,1)S(1)}, bf16[2,4,2,128,128]{4,3,2,1,0:T(8,128)(2,1)}, u32[]{:S(2)}, u32[]{:S(2)}) collective-permute-start(bf16[2,4,2,128,128]{4,3,2,1,0:T(8,128)(2,1)S(1)} %collective-permute-done.9.refs_16_), channel_id=1, source_target_pairs={{0,8},{8,0},{16,24},{24,16},{1,9},{9,1},{17,25},{25,17},{2,10},{10... | collective-permute-start | bytes 1572872 | tf_op jit(solution)/shard_map/ppermute | solution.py:522
  67.5 2.2 %collective-permute-start.14 = (bf16[2,4,2,128,128]{4,3,2,1,0:T(8,128)(2,1)}, bf16[2,4,2,128,128]{4,3,2,1,0:T(8,128)(2,1)S(1)}, u32[]{:S(2)}, u32[]{:S(2)}) collective-permute-start(bf16[2,4,2,128,128]{4,3,2,1,0:T(8,128)(2,1)} %collective-permute-done.12.refs_17_), channel_id=1, source_target_pairs={{0,8},{8,0},{16,24},{24,16},{1,9},{9,1},{17,25},{25,17},{2,10},{10... | collective-permute-start | bytes 1572872 | tf_op jit(solution)/shard_map/ppermute | solution.py:522
  68.0 1.7 %copy-start.13 = (s32[128]{0:T(128)}, s32[128]{0:T(128)S(1)}, u32[]{:S(2)}) copy-start(s32[128]{0:T(128)S(1)} %reshape.39.refs_0_) | copy-start | bytes 1540
  69.7 0.8 copy-start.12
  86.4 17.5 %copy-start.1 = (s32[2]{0:T(128)S(1)}, s32[2]{0:T(128)}, u32[]{:S(2)}) copy-start(s32[2]{0:T(128)} %pad_add_fusion.refs_2_.meta_ref) | copy-start | bytes 28
  86.4 17.5 %collective-permute-start.15 = (bf16[16,128,128]{2,1,0:T(8,128)(2,1)}, bf16[16,128,128]{2,1,0:T(8,128)(2,1)S(1)}, u32[]{:S(2)}, u32[]{:S(2)}) collective-permute-start(bf16[16,128,128]{2,1,0:T(8,128)(2,1)} %shard_map.118), channel_id=1, source_target_pairs={{0,1},{1,0},{2,3},{3,2},{4,5},{5,4},{6,7},{7,6},{8,9},{9,8},{10,11... | collective-permute-start | bytes 1572872 | tf_op jit(solution)/shard_map/ppermute | solution.py:549
  103.9 1.0 copy-start

commit v8 on v7

--- a/solution.py
+++ b/solution.py
@@ -315,58 +315,44 @@
     head_rows = [jnp.where(row_head == h, 1.0, 0.0).astype(jnp.bfloat16) for h in range(heads)]
     lane_head = lax.broadcasted_iota(jnp.int32, (width, lanes), 1) % per_step // group
     order = one_hot(lanes, lanes, lambda r: r % steps * per_step + r // steps)
-    unroll = math.gcd(2, block)
-    count = block // unroll
-
-    def pages_of(r):
-        return [slot_ref[(first + r) * extra + j] for j in range(extra)]
-
-    def score(g):
-        found = []
+    unroll = math.gcd(8 if target else 4, block)
+
+    def body(g, carry):
+        scores = []
         for u in range(unroll):
             r = g * unroll + u
             q = q_ref[r]
-            keys = jnp.concatenate(
-                [
-                    jnp.concatenate([buf[place, h, 0] for h in range(heads)], axis=1)
-                    for place in pages_of(r)
-                ],
-                axis=0,
-            )
+            places = [slot_ref[(first + r) * extra + j] for j in range(extra)]
             spread = jnp.concatenate([q * a for a in head_rows], axis=1)
-            found.append(nt(keys, spread))
-        return tuple(found)
-
-    def body(g, scores):
-        later = score(jnp.minimum(g + 1, count - 1))
+            s = [
+                nt(jnp.concatenate([buf[place, h, 0] for h in range(heads)], axis=1), spread)
+                for place in places
+            ]
+            scores.append((r, places, s))
         weights = []
-        for u in range(unroll):
-            r = g * unroll + u
-            s = scores[u]
+        for r, places, s in scores:
             old = ml_ref[r, 0:1]
-            m = jnp.maximum(jnp.max(s, axis=0, keepdims=True), old)
-            p = jnp.exp2((s - m) * scale)
+            m = jnp.max(functools.reduce(jnp.maximum, s), axis=0, keepdims=True)
+            m = jnp.maximum(m, old)
+            p = [jnp.exp2((a - m) * scale) for a in s]
             shrink = jnp.exp2((old - m) * scale)
-            l = ml_ref[r, 4:5] * shrink + jnp.sum(p, axis=0, keepdims=True)
-            weights.append((r, p.astype(jnp.bfloat16), shrink, l))
-        for r, p, shrink, l in weights:
-            places = pages_of(r)
-            values = jnp.concatenate(
-                [
-                    jnp.concatenate([buf[place, h, 1] for place in places], axis=1)
-                    for h in range(heads)
-                ],
-                axis=0,
-            )
-            every = nn(values, p)
-            part = every[:width]
-            for h in range(1, heads):
-                part = jnp.where(lane_head == h, every[h * width : (h + 1) * width], part)
-            result = ((acc_ref[r] * shrink + part) / l).astype(jnp.bfloat16)
+            l = jnp.sum(functools.reduce(jnp.add, p), axis=0, keepdims=True)
+            l = ml_ref[r, 4:5] * shrink + l
+            p = jnp.concatenate([a.astype(jnp.bfloat16) for a in p], axis=0)
+            weights.append((r, places, p, shrink, l))
+        results = []
+        for r, places, p, shrink, l in weights:
+            part = None
+            for h in range(heads):
+                values = jnp.concatenate([buf[place, h, 1] for place in places], axis=1)
+                mine = nn(values, p)
+                part = mine if h == 0 else jnp.where(lane_head == h, mine, part)
+            results.append((r, ((acc_ref[r] * shrink + part) / l).astype(jnp.bfloat16)))
+        for r, result in results:
             out_ref[r] = nt(order, result).astype(jnp.bfloat16)
-        return later
-
-    lax.fori_loop(0, count, body, score(0))
+        return carry
+
+    lax.fori_loop(0, block // unroll, body, 0)
 
 
 def decode(q, acc, ml, blocks, scalars, target, targets, extra, steps, heads, group):

time: 107 us -> 98.3 us (0.919)
  Pallas kernels: 75.6 us -> 65 us
  waiting for transfers between devices: 16.4 us -> 18.2 us
    pallas_call x2, Pallas kernels: 31.7 us -> 21.1 us  [decode(): pl.pallas_call(functools.partial(decode_kernel, slots, extra, steps, targ...]
    ppermute x1, waiting for transfers between devices: 0.01 us -> 1.78 us  [shards(): out = lax.ppermute(out, 'tp', shift)]
  transfers between devices with their start and end apart: 16 -> 16, of which waited for: 5 -> 6; matrix products, arithmetic and copies ran while one was open for 2% -> 2% of each run, Pallas kernels for 52% -> 52%
where the time goes in v8:
time: 98.3 us; the launch traced here: 97.8 us
  Pallas kernels  65 us (66%)
  waiting for transfers between devices  18.2 us (19%)
  starting transfers between devices  9.61 us (10%)
  local copies, waits for them, and re-layouts  2.3 us (2%)
  other arithmetic  1.82 us (2%)
    pallas_call x2, Pallas kernels, prefill(): pl.pallas_call(functools.partial(prefill_kernel, own, count, slots, group...  28.9 us
    pallas_call x2, Pallas kernels, decode(): pl.pallas_call(functools.partial(decode_kernel, slots, extra, steps, targ...  21.1 us
    ppermute x15, waiting for transfers between devices, shards(): lax.ppermute(gathered[of], axis, pairs)  16.4 us
    pallas_call x1, Pallas kernels, cache_part(): pl.pallas_call(functools.partial(cache_kernel, steps, heads, group, LOG2E...  10.9 us
    ppermute x15, starting transfers between devices, shards(): lax.ppermute(gathered[of], axis, pairs)  8.02 us
    pallas_call x1, Pallas kernels, split_heads(): pl.pallas_call(functools.partial(split_kernel, heads, tokens), out_shape=...  2.31 us
  transfers between devices with their start and end apart: 16, of which 6 were waited for; matrix products, arithmetic and copies ran while one was open for 2% of the time, Pallas kernels for 52%

profile of v8, /device:TPU:24, one launch (start us, length us, event | category | flops | bytes accessed | tf_op | source)
XLA Modules:
  0.0 97.8 jit_solution(379865860124839257)
XLA Ops:
  0.6 2.3 %shard_map.113.refs_1_.refs_6_ = bf16[2,4,2,128,128]{4,3,2,1,0:T(8,128)(2,1)} custom-call(bf16[1024,128]{1,0:T(8,128)(2,1)} %bitcast.12, bf16[1024,128]{1,0:T(8,128)(2,1)} %bitcast.13), custom_call_target="tpu_custom_call" | custom-call | flops 100000000 | bytes 2000000 | tf_op jit(solution)/shard_map/pallas_call | solution.py:54
  2.9 1.5 %collective-permute-start.2 = (bf16[2,4,2,128,128]{4,3,2,1,0:T(8,128)(2,1)}, bf16[2,4,2,128,128]{4,3,2,1,0:T(8,128)(2,1)S(1)}, u32[]{:S(2)}, u32[]{:S(2)}) collective-permute-start(bf16[2,4,2,128,128]{4,3,2,1,0:T(8,128)(2,1)} %shard_map.113.refs_1_.refs_6_), channel_id=1, source_target_pairs={{0,16},{8,24},{16,0},{24,8},{1,17},{9,25},{17,1},{25,9},{2,18},{10... | collective-permute-start | bytes 1572872 | tf_op jit(solution)/shard_map/ppermute | solution.py:508
  4.4 0.0 collective-permute-start.1
  4.4 0.3 collective-permute-start
  4.8 0.6 compare_convert_fusion.needed_ref
  5.3 10.9 %shard_map.114 = (f32[32,128,128]{2,1,0:T(8,128)}, f32[32,8,128]{2,1,0:T(8,128)}) custom-call(s32[32]{0:T(128)} %len_ref.1, bf16[32,128,128]{2,1,0:T(8,128)(2,1)} %bitcast.9, bf16[32,16,128]{2,1,0:T(8,128)(2,1)} %bitcast.16, bf16[32,16,128]{2,1,0:T(8,128)(2,1)} %bitcast.17, bf16[32,512,128]{2,1,0:T(8,128)(2,1)} %bitcast.14, bf16[32,512,128]{2,1,0:T(8,128)(2,1)} %bitcast.15), custom_call_target="tpu_custom_call" | custom-call | flops 4294967296 | bytes 14000000 | tf_op jit(solution)/shard_map/pallas_call | solution.py:275
  16.2 0.6 collective-permute-done.2.refs_14_
  16.8 0.0 collective-permute-done.1.refs_10_
  16.8 2.2 %collective-permute-done.refs_2_.refs_7_ = bf16[2,4,2,128,128]{4,3,2,1,0:T(8,128)(2,1)S(1)} collective-permute-done((bf16[2,4,2,128,128]{4,3,2,1,0:T(8,128)(2,1)}, bf16[2,4,2,128,128]{4,3,2,1,0:T(8,128)(2,1)S(1)}, u32[]{:S(2)}, u32[]{:S(2)}) %collective-permute-start) | collective-permute-done | bytes 524320 | tf_op jit(solution)/shard_map/ppermute | solution.py:508
  19.0 0.5 collective-permute-start.5
  19.5 0.0 collective-permute-start.4
  19.5 1.2 %collective-permute-start.3 = (bf16[2,4,2,128,128]{4,3,2,1,0:T(8,128)(2,1)S(1)}, bf16[2,4,2,128,128]{4,3,2,1,0:T(8,128)(2,1)S(1)}, u32[]{:S(2)}, u32[]{:S(2)}) collective-permute-start(bf16[2,4,2,128,128]{4,3,2,1,0:T(8,128)(2,1)S(1)} %collective-permute-done.refs_2_.refs_7_), channel_id=1, source_target_pairs={{0,4},{4,6},{6,2},{2,0},{1,5},{5,7},{7,3},{3,1},{8,12},{12,14},{14... | collective-permute-start | bytes 1572872 | tf_op jit(solution)/shard_map/ppermute | solution.py:508
  20.8 0.2 collective-permute-start.6
  21.0 13.5 %shard_map.115 = (f32[4,4,512,128]{3,2,1,0:T(8,128)}, f32[4,4,512,128]{3,2,1,0:T(8,128)}) custom-call(s32[4]{0:T(128)} %compare_convert_fusion.needed_ref, bf16[1,256,32,128]{3,2,1,0:T(8,128)(2,1)} %refs_0_.3, bf16[2,4,2,128,128]{4,3,2,1,0:T(8,128)(2,1)} %shard_map.113.refs_1_.refs_6_, bf16[2,4,2,128,128]{4,3,2,1,0:T(8,128)(2,1)} %copy-done.4), custom_call_target="tpu_custom_call" | custom-call | flops 8589934592 | bytes 12000000 | tf_op jit(solution)/shard_map/pallas_call | solution.py:194
  34.5 0.0 collective-permute-done.6.refs_18_
  34.6 0.0 collective-permute-done.5.refs_15_
  34.6 0.0 collective-permute-done.4.refs_11_
  34.6 0.0 collective-permute-done.3.refs_1_.refs_8_
  34.6 0.0 copy-start.14
  34.6 0.3 collective-permute-start.10
  35.0 1.5 %collective-permute-start.9 = (bf16[2,4,2,128,128]{4,3,2,1,0:T(8,128)(2,1)S(1)}, bf16[2,4,2,128,128]{4,3,2,1,0:T(8,128)(2,1)S(1)}, u32[]{:S(2)}, u32[]{:S(2)}) collective-permute-start(bf16[2,4,2,128,128]{4,3,2,1,0:T(8,128)(2,1)S(1)} %collective-permute-done.3.refs_1_.refs_8_), channel_id=1, source_target_pairs={{0,16},{8,24},{16,0},{24,8},{1,17},{9,25},{17,1},{25,9},{2,18},{10... | collective-permute-start | bytes 1572872 | tf_op jit(solution)/shard_map/ppermute | solution.py:508
  36.5 0.0 collective-permute-start.8
  36.5 1.2 %collective-permute-start.7 = (bf16[2,4,2,128,128]{4,3,2,1,0:T(8,128)(2,1)S(1)}, bf16[2,4,2,128,128]{4,3,2,1,0:T(8,128)(2,1)}, u32[]{:S(2)}, u32[]{:S(2)}) collective-permute-start(bf16[2,4,2,128,128]{4,3,2,1,0:T(8,128)(2,1)S(1)} %collective-permute-done.3.refs_1_.refs_8_), channel_id=1, source_target_pairs={{0,4},{4,6},{6,2},{2,0},{1,5},{5,7},{7,3},{3,1},{8,12},{12,14},{14... | collective-permute-start | bytes 1572872 | tf_op jit(solution)/shard_map/ppermute | solution.py:508
  37.7 0.0 collective-permute-done.10.refs_19_
  37.7 11.3 %collective-permute-done.9.refs_16_ = bf16[2,4,2,128,128]{4,3,2,1,0:T(8,128)(2,1)S(1)} collective-permute-done((bf16[2,4,2,128,128]{4,3,2,1,0:T(8,128)(2,1)S(1)}, bf16[2,4,2,128,128]{4,3,2,1,0:T(8,128)(2,1)S(1)}, u32[]{:S(2)}, u32[]{:S(2)}) %collective-permute-start.9) | collective-permute-done | bytes 524320 | tf_op jit(solution)/shard_map/ppermute | solution.py:508
  49.0 0.0 collective-permute-done.8.refs_12_
  49.0 1.9 %collective-permute-done.7.refs_2_.refs_9_ = bf16[2,4,2,128,128]{4,3,2,1,0:T(8,128)(2,1)} collective-permute-done((bf16[2,4,2,128,128]{4,3,2,1,0:T(8,128)(2,1)S(1)}, bf16[2,4,2,128,128]{4,3,2,1,0:T(8,128)(2,1)}, u32[]{:S(2)}, u32[]{:S(2)}) %collective-permute-start.7) | collective-permute-done | bytes 524320 | tf_op jit(solution)/shard_map/ppermute | solution.py:508
  50.9 0.5 collective-permute-start.12
  51.5 0.0 collective-permute-start.11
  51.5 0.5 collective-permute-start.13
  52.0 15.4 %shard_map.116 = bf16[1,256,32,128]{3,2,1,0:T(8,128)(2,1)} custom-call(s32[4]{0:T(128)} %compare_convert_fusion.needed_ref, bf16[1,256,32,128]{3,2,1,0:T(8,128)(2,1)} %refs_0_.3, bf16[2,4,2,128,128]{4,3,2,1,0:T(8,128)(2,1)} %copy-done.7, bf16[2,4,2,128,128]{4,3,2,1,0:T(8,128)(2,1)} %collective-permute-done.7.refs_2_.refs_9_, ...), custom_call_target="tpu_custom_call" | custom-call | flops 8589934592 | bytes 12000000 | tf_op jit(solution)/shard_map/pallas_call | solution.py:194
  67.5 0.0 collective-permute-done.13.refs_20_
  67.5 0.0 collective-permute-done.11.refs_13_
  67.5 0.1 collective-permute-start.14
  67.6 0.1 copy.17
  67.7 0.1 broadcast_in_dim.15
  67.8 0.1 copy.16
  67.9 0.1 reshape.39.refs_0_
  68.0 0.6 pad_add_fusion.refs_2_.meta_ref
  68.6 0.6 select_reduce_fusion.refs_1_
  69.3 0.4 collective-permute-done.14.refs_21_
  69.7 0.8 copy-done.12
  70.5 10.2 %shard_map.118 = bf16[16,128,128]{2,1,0:T(8,128)(2,1)} custom-call(s32[128]{0:T(128)} %copy-done.13, s32[16]{0:T(128)} %select_reduce_fusion.refs_1_, s32[2]{0:T(128)} %pad_add_fusion.refs_2_.meta_ref, bf16[32,128,128]{2,1,0:T(8,128)(2,1)} %bitcast.10, f32[32,128,128]{2,1,0:T(8,128)} %get-tuple-element.38.refs_4_, f32[32,8,128]{2,1,0:T(8,128)} %get-tuple-element.39.refs_5_, ...), custom_call_target="tpu_custom_call" | custom-call | flops 2147483648 | bytes 8000000 | tf_op jit(solution)/shard_map/pallas_call | solution.py:370
  80.7 1.6 %collective-permute-start.15 = (bf16[16,128,128]{2,1,0:T(8,128)(2,1)}, bf16[16,128,128]{2,1,0:T(8,128)(2,1)S(1)}, u32[]{:S(2)}, u32[]{:S(2)}) collective-permute-start(bf16[16,128,128]{2,1,0:T(8,128)(2,1)} %shard_map.118), channel_id=1, source_target_pairs={{0,1},{1,0},{2,3},{3,2},{4,5},{5,4},{6,7},{7,6},{8,9},{9,8},{10,11... | collective-permute-start | bytes 1572872 | tf_op jit(solution)/shard_map/ppermute | solution.py:535
  82.3 10.9 %shard_map.117.refs_0_ = bf16[16,128,128]{2,1,0:T(8,128)(2,1)} custom-call(s32[128]{0:T(128)} %copy-done.13, s32[16]{0:T(128)} %select_reduce_fusion.refs_1_, s32[2]{0:T(128)} %pad_add_fusion.refs_2_.meta_ref, bf16[32,128,128]{2,1,0:T(8,128)(2,1)} %bitcast.11, f32[32,128,128]{2,1,0:T(8,128)} %get-tuple-element.38.refs_4_, ...), custom_call_target="tpu_custom_call" | custom-call | flops 2147483648 | bytes 8000000 | tf_op jit(solution)/shard_map/pallas_call | solution.py:370
  93.2 1.8 %collective-permute-done.15.refs_1_ = bf16[16,128,128]{2,1,0:T(8,128)(2,1)S(1)} collective-permute-done((bf16[16,128,128]{2,1,0:T(8,128)(2,1)}, bf16[16,128,128]{2,1,0:T(8,128)(2,1)S(1)}, u32[]{:S(2)}, u32[]{:S(2)}) %collective-permute-start.15) | collective-permute-done | bytes 524320 | tf_op jit(solution)/shard_map/ppermute | solution.py:535
  95.0 1.0 %copy-done = bf16[16,128,128]{2,1,0:T(8,128)(2,1)S(1)} copy-done((bf16[16,128,128]{2,1,0:T(8,128)(2,1)S(1)}, bf16[16,128,128]{2,1,0:T(8,128)(2,1)}, u32[]{:S(2)}) %copy-start) | copy-done | bytes 524312
  96.0 1.8 %shard_map.119 = bf16[16,4,8192]{2,1,0:T(4,128)(2,1)} custom-call(s32[2]{0:T(128)S(1)} %copy-done.1, bf16[16,128,128]{2,1,0:T(8,128)(2,1)S(1)} %copy-done, bf16[16,128,128]{2,1,0:T(8,128)(2,1)S(1)} %collective-permute-done.15.refs_1_), custom_call_target="tpu_custom_call" | custom-call | bytes 2000000 | tf_op jit(solution)/shard_map/pallas_call | solution.py:428
  (29 shorter events, 0.1 us)
Async XLA Ops:
  2.9 13.9 %collective-permute-start.2 = (bf16[2,4,2,128,128]{4,3,2,1,0:T(8,128)(2,1)}, bf16[2,4,2,128,128]{4,3,2,1,0:T(8,128)(2,1)S(1)}, u32[]{:S(2)}, u32[]{:S(2)}) collective-permute-start(bf16[2,4,2,128,128]{4,3,2,1,0:T(8,128)(2,1)} %shard_map.113.refs_1_.refs_6_), channel_id=1, source_target_pairs={{0,16},{8,24},{16,0},{24,8},{1,17},{9,25},{17,1},{25,9},{2,18},{10... | collective-permute-start | bytes 1572872 | tf_op jit(solution)/shard_map/ppermute | solution.py:508
  4.4 12.4 %collective-permute-start.1 = (bf16[2,4,2,128,128]{4,3,2,1,0:T(8,128)(2,1)}, bf16[2,4,2,128,128]{4,3,2,1,0:T(8,128)(2,1)S(1)}, u32[]{:S(2)}, u32[]{:S(2)}) collective-permute-start(bf16[2,4,2,128,128]{4,3,2,1,0:T(8,128)(2,1)} %shard_map.113.refs_1_.refs_6_), channel_id=1, source_target_pairs={{0,8},{8,0},{16,24},{24,16},{1,9},{9,1},{17,25},{25,17},{2,10},{10... | collective-permute-start | bytes 1572872 | tf_op jit(solution)/shard_map/ppermute | solution.py:508
  4.4 14.5 %collective-permute-start = (bf16[2,4,2,128,128]{4,3,2,1,0:T(8,128)(2,1)}, bf16[2,4,2,128,128]{4,3,2,1,0:T(8,128)(2,1)S(1)}, u32[]{:S(2)}, u32[]{:S(2)}) collective-permute-start(bf16[2,4,2,128,128]{4,3,2,1,0:T(8,128)(2,1)} %shard_map.113.refs_1_.refs_6_), channel_id=1, source_target_pairs={{0,4},{4,6},{6,2},{2,0},{1,5},{5,7},{7,3},{3,1},{8,12},{12,14},{14... | collective-permute-start | bytes 1572872 | tf_op jit(solution)/shard_map/ppermute | solution.py:508
  16.8 17.7 %copy-start.2 = (bf16[2,4,2,128,128]{4,3,2,1,0:T(8,128)(2,1)}, bf16[2,4,2,128,128]{4,3,2,1,0:T(8,128)(2,1)S(1)}, u32[]{:S(2)}) copy-start(bf16[2,4,2,128,128]{4,3,2,1,0:T(8,128)(2,1)S(1)} %collective-permute-done.2.refs_14_) | copy-start | bytes 1572868
  16.8 17.7 %copy-start.3 = (bf16[2,4,2,128,128]{4,3,2,1,0:T(8,128)(2,1)}, bf16[2,4,2,128,128]{4,3,2,1,0:T(8,128)(2,1)S(1)}, u32[]{:S(2)}) copy-start(bf16[2,4,2,128,128]{4,3,2,1,0:T(8,128)(2,1)S(1)} %collective-permute-done.1.refs_10_) | copy-start | bytes 1572868
  19.0 2.0 %copy-start.4 = (bf16[2,4,2,128,128]{4,3,2,1,0:T(8,128)(2,1)}, bf16[2,4,2,128,128]{4,3,2,1,0:T(8,128)(2,1)S(1)}, u32[]{:S(2)}) copy-start(bf16[2,4,2,128,128]{4,3,2,1,0:T(8,128)(2,1)S(1)} %collective-permute-done.refs_2_.refs_7_) | copy-start | bytes 1572868
  19.0 15.6 %collective-permute-start.5 = (bf16[2,4,2,128,128]{4,3,2,1,0:T(8,128)(2,1)S(1)}, bf16[2,4,2,128,128]{4,3,2,1,0:T(8,128)(2,1)S(1)}, u32[]{:S(2)}, u32[]{:S(2)}) collective-permute-start(bf16[2,4,2,128,128]{4,3,2,1,0:T(8,128)(2,1)S(1)} %collective-permute-done.refs_2_.refs_7_), channel_id=1, source_target_pairs={{0,16},{8,24},{16,0},{24,8},{1,17},{9,25},{17,1},{25,9},{2,18},{10... | collective-permute-start | bytes 1572872 | tf_op jit(solution)/shard_map/ppermute | solution.py:508
  19.5 15.1 %collective-permute-start.4 = (bf16[2,4,2,128,128]{4,3,2,1,0:T(8,128)(2,1)S(1)}, bf16[2,4,2,128,128]{4,3,2,1,0:T(8,128)(2,1)S(1)}, u32[]{:S(2)}, u32[]{:S(2)}) collective-permute-start(bf16[2,4,2,128,128]{4,3,2,1,0:T(8,128)(2,1)S(1)} %collective-permute-done.refs_2_.refs_7_), channel_id=1, source_target_pairs={{0,8},{8,0},{16,24},{24,16},{1,9},{9,1},{17,25},{25,17},{2,10},{10... | collective-permute-start | bytes 1572872 | tf_op jit(solution)/shard_map/ppermute | solution.py:508
  19.5 15.1 %collective-permute-start.3 = (bf16[2,4,2,128,128]{4,3,2,1,0:T(8,128)(2,1)S(1)}, bf16[2,4,2,128,128]{4,3,2,1,0:T(8,128)(2,1)S(1)}, u32[]{:S(2)}, u32[]{:S(2)}) collective-permute-start(bf16[2,4,2,128,128]{4,3,2,1,0:T(8,128)(2,1)S(1)} %collective-permute-done.refs_2_.refs_7_), channel_id=1, source_target_pairs={{0,4},{4,6},{6,2},{2,0},{1,5},{5,7},{7,3},{3,1},{8,12},{12,14},{14... | collective-permute-start | bytes 1572872 | tf_op jit(solution)/shard_map/ppermute | solution.py:508
  20.8 13.8 %collective-permute-start.6 = (bf16[2,4,2,128,128]{4,3,2,1,0:T(8,128)(2,1)S(1)}, bf16[2,4,2,128,128]{4,3,2,1,0:T(8,128)(2,1)S(1)}, u32[]{:S(2)}, u32[]{:S(2)}) collective-permute-start(bf16[2,4,2,128,128]{4,3,2,1,0:T(8,128)(2,1)S(1)} %collective-permute-done.2.refs_14_), channel_id=1, source_target_pairs={{0,8},{8,0},{16,24},{24,16},{1,9},{9,1},{17,25},{25,17},{2,10},{10... | collective-permute-start | bytes 1572872 | tf_op jit(solution)/shard_map/ppermute | solution.py:508
  34.5 32.8 %copy-start.8 = (bf16[2,4,2,128,128]{4,3,2,1,0:T(8,128)(2,1)}, bf16[2,4,2,128,128]{4,3,2,1,0:T(8,128)(2,1)S(1)}, u32[]{:S(2)}) copy-start(bf16[2,4,2,128,128]{4,3,2,1,0:T(8,128)(2,1)S(1)} %collective-permute-done.6.refs_18_) | copy-start | bytes 1572868
  34.6 32.8 %copy-start.5 = (bf16[2,4,2,128,128]{4,3,2,1,0:T(8,128)(2,1)}, bf16[2,4,2,128,128]{4,3,2,1,0:T(8,128)(2,1)S(1)}, u32[]{:S(2)}) copy-start(bf16[2,4,2,128,128]{4,3,2,1,0:T(8,128)(2,1)S(1)} %collective-permute-done.5.refs_15_) | copy-start | bytes 1572868
  34.6 32.8 %copy-start.6 = (bf16[2,4,2,128,128]{4,3,2,1,0:T(8,128)(2,1)}, bf16[2,4,2,128,128]{4,3,2,1,0:T(8,128)(2,1)S(1)}, u32[]{:S(2)}) copy-start(bf16[2,4,2,128,128]{4,3,2,1,0:T(8,128)(2,1)S(1)} %collective-permute-done.4.refs_11_) | copy-start | bytes 1572868
  34.6 17.4 %copy-start.7 = (bf16[2,4,2,128,128]{4,3,2,1,0:T(8,128)(2,1)}, bf16[2,4,2,128,128]{4,3,2,1,0:T(8,128)(2,1)S(1)}, u32[]{:S(2)}) copy-start(bf16[2,4,2,128,128]{4,3,2,1,0:T(8,128)(2,1)S(1)} %collective-permute-done.3.refs_1_.refs_8_) | copy-start | bytes 1572868
  34.6 33.0 %copy-start.14 = (s32[32,4]{0,1:T(4,128)S(1)}, s32[32,4]{0,1:T(4,128)}, u32[]{:S(2)}) copy-start(s32[32,4]{0,1:T(4,128)} %param.19) | copy-start | bytes 1540
  34.6 3.1 %collective-permute-start.10 = (bf16[2,4,2,128,128]{4,3,2,1,0:T(8,128)(2,1)S(1)}, bf16[2,4,2,128,128]{4,3,2,1,0:T(8,128)(2,1)S(1)}, u32[]{:S(2)}, u32[]{:S(2)}) collective-permute-start(bf16[2,4,2,128,128]{4,3,2,1,0:T(8,128)(2,1)S(1)} %collective-permute-done.5.refs_15_), channel_id=1, source_target_pairs={{0,8},{8,0},{16,24},{24,16},{1,9},{9,1},{17,25},{25,17},{2,10},{10... | collective-permute-start | bytes 1572872 | tf_op jit(solution)/shard_map/ppermute | solution.py:508
  35.0 14.1 %collective-permute-start.9 = (bf16[2,4,2,128,128]{4,3,2,1,0:T(8,128)(2,1)S(1)}, bf16[2,4,2,128,128]{4,3,2,1,0:T(8,128)(2,1)S(1)}, u32[]{:S(2)}, u32[]{:S(2)}) collective-permute-start(bf16[2,4,2,128,128]{4,3,2,1,0:T(8,128)(2,1)S(1)} %collective-permute-done.3.refs_1_.refs_8_), channel_id=1, source_target_pairs={{0,16},{8,24},{16,0},{24,8},{1,17},{9,25},{17,1},{25,9},{2,18},{10... | collective-permute-start | bytes 1572872 | tf_op jit(solution)/shard_map/ppermute | solution.py:508
  36.5 12.6 %collective-permute-start.8 = (bf16[2,4,2,128,128]{4,3,2,1,0:T(8,128)(2,1)S(1)}, bf16[2,4,2,128,128]{4,3,2,1,0:T(8,128)(2,1)S(1)}, u32[]{:S(2)}, u32[]{:S(2)}) collective-permute-start(bf16[2,4,2,128,128]{4,3,2,1,0:T(8,128)(2,1)S(1)} %collective-permute-done.3.refs_1_.refs_8_), channel_id=1, source_target_pairs={{0,8},{8,0},{16,24},{24,16},{1,9},{9,1},{17,25},{25,17},{2,10},{10... | collective-permute-start | bytes 1572872 | tf_op jit(solution)/shard_map/ppermute | solution.py:508
  36.5 14.4 %collective-permute-start.7 = (bf16[2,4,2,128,128]{4,3,2,1,0:T(8,128)(2,1)S(1)}, bf16[2,4,2,128,128]{4,3,2,1,0:T(8,128)(2,1)}, u32[]{:S(2)}, u32[]{:S(2)}) collective-permute-start(bf16[2,4,2,128,128]{4,3,2,1,0:T(8,128)(2,1)S(1)} %collective-permute-done.3.refs_1_.refs_8_), channel_id=1, source_target_pairs={{0,4},{4,6},{6,2},{2,0},{1,5},{5,7},{7,3},{3,1},{8,12},{12,14},{14... | collective-permute-start | bytes 1572872 | tf_op jit(solution)/shard_map/ppermute | solution.py:508
  37.7 29.7 %copy-start.9 = (bf16[2,4,2,128,128]{4,3,2,1,0:T(8,128)(2,1)}, bf16[2,4,2,128,128]{4,3,2,1,0:T(8,128)(2,1)S(1)}, u32[]{:S(2)}) copy-start(bf16[2,4,2,128,128]{4,3,2,1,0:T(8,128)(2,1)S(1)} %collective-permute-done.10.refs_19_) | copy-start | bytes 1572868
  49.0 18.4 %copy-start.10 = (bf16[2,4,2,128,128]{4,3,2,1,0:T(8,128)(2,1)}, bf16[2,4,2,128,128]{4,3,2,1,0:T(8,128)(2,1)S(1)}, u32[]{:S(2)}) copy-start(bf16[2,4,2,128,128]{4,3,2,1,0:T(8,128)(2,1)S(1)} %collective-permute-done.9.refs_16_) | copy-start | bytes 1572868
  49.0 18.4 %copy-start.11 = (bf16[2,4,2,128,128]{4,3,2,1,0:T(8,128)(2,1)}, bf16[2,4,2,128,128]{4,3,2,1,0:T(8,128)(2,1)S(1)}, u32[]{:S(2)}) copy-start(bf16[2,4,2,128,128]{4,3,2,1,0:T(8,128)(2,1)S(1)} %collective-permute-done.8.refs_12_) | copy-start | bytes 1572868
  50.9 16.5 %collective-permute-start.12 = (bf16[2,4,2,128,128]{4,3,2,1,0:T(8,128)(2,1)}, bf16[2,4,2,128,128]{4,3,2,1,0:T(8,128)(2,1)}, u32[]{:S(2)}, u32[]{:S(2)}) collective-permute-start(bf16[2,4,2,128,128]{4,3,2,1,0:T(8,128)(2,1)} %collective-permute-done.7.refs_2_.refs_9_), channel_id=1, source_target_pairs={{0,16},{8,24},{16,0},{24,8},{1,17},{9,25},{17,1},{25,9},{2,18},{10... | collective-permute-start | bytes 1572872 | tf_op jit(solution)/shard_map/ppermute | solution.py:508
  51.5 16.0 %collective-permute-start.11 = (bf16[2,4,2,128,128]{4,3,2,1,0:T(8,128)(2,1)}, bf16[2,4,2,128,128]{4,3,2,1,0:T(8,128)(2,1)}, u32[]{:S(2)}, u32[]{:S(2)}) collective-permute-start(bf16[2,4,2,128,128]{4,3,2,1,0:T(8,128)(2,1)} %collective-permute-done.7.refs_2_.refs_9_), channel_id=1, source_target_pairs={{0,8},{8,0},{16,24},{24,16},{1,9},{9,1},{17,25},{25,17},{2,10},{10... | collective-permute-start | bytes 1572872 | tf_op jit(solution)/shard_map/ppermute | solution.py:508
  51.5 16.0 %collective-permute-start.13 = (bf16[2,4,2,128,128]{4,3,2,1,0:T(8,128)(2,1)S(1)}, bf16[2,4,2,128,128]{4,3,2,1,0:T(8,128)(2,1)}, u32[]{:S(2)}, u32[]{:S(2)}) collective-permute-start(bf16[2,4,2,128,128]{4,3,2,1,0:T(8,128)(2,1)S(1)} %collective-permute-done.9.refs_16_), channel_id=1, source_target_pairs={{0,8},{8,0},{16,24},{24,16},{1,9},{9,1},{17,25},{25,17},{2,10},{10... | collective-permute-start | bytes 1572872 | tf_op jit(solution)/shard_map/ppermute | solution.py:508
  67.5 2.2 %collective-permute-start.14 = (bf16[2,4,2,128,128]{4,3,2,1,0:T(8,128)(2,1)}, bf16[2,4,2,128,128]{4,3,2,1,0:T(8,128)(2,1)S(1)}, u32[]{:S(2)}, u32[]{:S(2)}) collective-permute-start(bf16[2,4,2,128,128]{4,3,2,1,0:T(8,128)(2,1)} %collective-permute-done.12.refs_17_), channel_id=1, source_target_pairs={{0,8},{8,0},{16,24},{24,16},{1,9},{9,1},{17,25},{25,17},{2,10},{10... | collective-permute-start | bytes 1572872 | tf_op jit(solution)/shard_map/ppermute | solution.py:508
  68.0 1.7 %copy-start.13 = (s32[128]{0:T(128)}, s32[128]{0:T(128)S(1)}, u32[]{:S(2)}) copy-start(s32[128]{0:T(128)S(1)} %reshape.39.refs_0_) | copy-start | bytes 1540
  69.7 0.8 copy-start.12
  80.7 14.3 %copy-start.1 = (s32[2]{0:T(128)S(1)}, s32[2]{0:T(128)}, u32[]{:S(2)}) copy-start(s32[2]{0:T(128)} %pad_add_fusion.refs_2_.meta_ref) | copy-start | bytes 28
  80.7 14.2 %collective-permute-start.15 = (bf16[16,128,128]{2,1,0:T(8,128)(2,1)}, bf16[16,128,128]{2,1,0:T(8,128)(2,1)S(1)}, u32[]{:S(2)}, u32[]{:S(2)}) collective-permute-start(bf16[16,128,128]{2,1,0:T(8,128)(2,1)} %shard_map.118), channel_id=1, source_target_pairs={{0,1},{1,0},{2,3},{3,2},{4,5},{5,4},{6,7},{7,6},{8,9},{9,8},{10,11... | collective-permute-start | bytes 1572872 | tf_op jit(solution)/shard_map/ppermute | solution.py:535
  95.0 1.0 %copy-start = (bf16[16,128,128]{2,1,0:T(8,128)(2,1)S(1)}, bf16[16,128,128]{2,1,0:T(8,128)(2,1)}, u32[]{:S(2)}) copy-start(bf16[16,128,128]{2,1,0:T(8,128)(2,1)} %shard_map.117.refs_0_) | copy-start | bytes 1572868

commit v9 on v8

--- a/solution.py
+++ b/solution.py
@@ -233,7 +233,9 @@
         same = column % heads == row % per_step // group
         return jnp.where(same, column // heads, 1 << 20), row // per_step
 
-    place, _ = mask(cache)
+    piece = min(cache, 128)
+    pieces = range(0, cache, piece)
+    place, _ = mask(piece)
     new_place, step = mask(new)
     new_allowed = new_place <= step
     low = lax.broadcasted_iota(jnp.int32, (rows, width), 1) < 4
@@ -245,21 +247,32 @@
         for u in range(unroll):
             r = g * unroll + u
             q = q_ref[r]
-            old = jnp.where(place < len_ref[first + r], nt(q, ck_ref[r]), NEG)
+            length = len_ref[first + r]
+            old = [
+                jnp.where(
+                    place < length - c // heads, nt(q, ck_ref[r, pl.ds(c, piece), :]), NEG
+                )
+                for c in pieces
+            ]
             add = jnp.where(new_allowed, nt(q, dk_ref[r]), NEG)
             scores.append((r, old, add))
         weights = []
         for r, old, add in scores:
+            top = functools.reduce(jnp.maximum, old)
             m = jnp.maximum(
-                jnp.max(old, axis=1, keepdims=True), jnp.max(add, axis=1, keepdims=True)
+                jnp.max(top, axis=1, keepdims=True), jnp.max(add, axis=1, keepdims=True)
             )
-            old = jnp.exp2((old - m) * scale)
+            old = [jnp.exp2((a - m) * scale) for a in old]
             add = jnp.exp2((add - m) * scale)
-            l = jnp.sum(old, axis=1, keepdims=True) + jnp.sum(add, axis=1, keepdims=True)
+            l = jnp.sum(functools.reduce(jnp.add, old), axis=1, keepdims=True)
+            l = l + jnp.sum(add, axis=1, keepdims=True)
             ml_ref[r] = jnp.where(low, m, l).T[:8]
-            weights.append((r, old.astype(jnp.bfloat16), add.astype(jnp.bfloat16)))
+            weights.append((r, [a.astype(jnp.bfloat16) for a in old], add.astype(jnp.bfloat16)))
         for r, old, add in weights:
-            acc_ref[r] = (nn(old, cv_ref[r]) + nn(add, dv_ref[r])).T
+            acc = nn(add, dv_ref[r])
+            for c, p in zip(pieces, old):
+                acc = acc + nn(p, cv_ref[r, pl.ds(c, piece), :])
+            acc_ref[r] = acc.T
         return carry
 
     lax.fori_loop(0, block // unroll, body, 0)
@@ -315,7 +328,8 @@
     head_rows = [jnp.where(row_head == h, 1.0, 0.0).astype(jnp.bfloat16) for h in range(heads)]
     lane_head = lax.broadcasted_iota(jnp.int32, (width, lanes), 1) % per_step // group
     order = one_hot(lanes, lanes, lambda r: r % steps * per_step + r // steps)
-    unroll = math.gcd(8 if target else 4, block)
+    unroll = math.gcd(8, block)
+    both = math.gcd(2 if target else 1, heads)
 
     def body(g, carry):
         scores = []
@@ -324,10 +338,14 @@
             q = q_ref[r]
             places = [slot_ref[(first + r) * extra + j] for j in range(extra)]
             spread = jnp.concatenate([q * a for a in head_rows], axis=1)
-            s = [
-                nt(jnp.concatenate([buf[place, h, 0] for h in range(heads)], axis=1), spread)
+            keys = [
+                jnp.concatenate([buf[place, h, 0] for h in range(heads)], axis=1)
                 for place in places
             ]
+            s = []
+            for j in range(0, extra, both):
+                pair = jnp.concatenate(keys[j : j + both], axis=0)
+                s.append(nt(pair, spread))
             scores.append((r, places, s))
         weights = []
         for r, places, s in scores:
@@ -343,10 +361,15 @@
         results = []
         for r, places, p, shrink, l in weights:
             part = None
-            for h in range(heads):
-                values = jnp.concatenate([buf[place, h, 1] for place in places], axis=1)
-                mine = nn(values, p)
-                part = mine if h == 0 else jnp.where(lane_head == h, mine, part)
+            values = [
+                jnp.concatenate([buf[place, h, 1] for place in places], axis=1)
+                for h in range(heads)
+            ]
+            for h in range(0, heads, both):
+                pair = nn(jnp.concatenate(values[h : h + both], axis=0), p)
+                for w in range(both):
+                    mine = pair[w * width : (w + 1) * width]
+                    part = mine if h + w == 0 else jnp.where(lane_head == h + w, mine, part)
             results.append((r, ((acc_ref[r] * shrink + part) / l).astype(jnp.bfloat16)))
         for r, result in results:
             out_ref[r] = nt(order, result).astype(jnp.bfloat16)
@@ -399,42 +422,34 @@
     )(*scalars, q, acc, ml, *blocks)
 
 
-def join_kernel(targets, chunks, steps, meta_ref, *refs):
+def join_kernel(targets, steps, meta_ref, *refs):
     out_ref = refs[-1]
-    k = pl.program_id(0)
     rows = refs[0].shape[1]
     each = rows // steps
     for s in range(targets):
-        @pl.when(lax.rem(meta_ref[1] + (targets - s), targets) == k)
-        def _():
-            for c in range(chunks):
-                source = refs[s * chunks + c]
-
-                def body(r, carry):
-                    value = source[r]
-                    for g in range(each):
-                        out_ref[r, :, (c * each + g) * 128 : (c * each + g + 1) * 128] = value[
-                            g * steps : (g + 1) * steps
-                        ]
-                    return carry
-
-                lax.fori_loop(0, out_ref.shape[0], body, 0)
-
-
-def join(pieces, meta, steps, targets, chunks):
+        start = lax.rem(meta_ref[1] + (targets - s), targets) * (each * 128)
+        for r in range(out_ref.shape[0]):
+            value = refs[s][r]
+            for g in range(each):
+                column = pl.multiple_of(start + g * 128, 128)
+                out_ref[r, :, pl.ds(column, 128)] = value[g * steps : (g + 1) * steps]
+
+
+def join(pieces, meta, steps, targets):
     per_target, rows, width = pieces[0].shape
-    half = chunks * (rows // steps) * width
-    spec = pl.BlockSpec((per_target, rows, width), lambda k, *_: (0, 0, 0))
+    whole = rows // steps * width * targets
+    block = math.gcd(4, per_target)
+    spec = pl.BlockSpec((block, rows, width), lambda k, *_: (k, 0, 0))
     return pl.pallas_call(
-        functools.partial(join_kernel, targets, chunks, steps),
+        functools.partial(join_kernel, targets, steps),
         grid_spec=pltpu.PrefetchScalarGridSpec(
             num_scalar_prefetch=1,
-            grid=(targets,),
+            grid=(per_target // block,),
             in_specs=[spec] * len(pieces),
-            out_specs=pl.BlockSpec((per_target, steps, half), lambda k, *_: (0, 0, k)),
-        ),
-        out_shape=jax.ShapeDtypeStruct((per_target, steps, half * targets), jnp.bfloat16),
-        compiler_params=pltpu.CompilerParams(vmem_limit_bytes=16 * 1024 * 1024),
+            out_specs=pl.BlockSpec((block, steps, whole), lambda k, *_: (k, 0, 0)),
+        ),
+        out_shape=jax.ShapeDtypeStruct((per_target, steps, whole), jnp.bfloat16),
+        compiler_params=params(),
         cost_estimate=pl.CostEstimate(flops=0, bytes_accessed=2 * 10**6, transcendentals=0),
     )(meta, *pieces)
 
@@ -504,10 +519,9 @@
                     sends.append((flip, (code, s), (code ^ flip, s), "role", pairs))
             if code == 0 and s + 1 < ring:
                 sends.append((roles, (code, s), (0, s + 1), "ctx", along))
-        arrived = {
-            to: lax.ppermute(gathered[of], axis, pairs)
-            for _, of, to, axis, pairs in sorted(sends, key=lambda a: a[0])
-        }
+        sends.sort(key=lambda a: a[0])
+        names = [to for _, _, to, _, _ in sends]
+        arrived = [lax.ppermute(gathered[of], axis, pairs) for _, of, _, axis, pairs in sends]
         beside = ()
         if k == 0:
             beside = cache_part(*raw, cache_len.astype(jnp.int32), steps, heads, group)
@@ -516,15 +530,19 @@
         if k == ring - 1:
             later = tuple(range(2, ring))
             beside = prefill(prefill_q, [gathered[0, s] for s in later], later, needed, state)
+        if k == ring - 2 and k > 1:
+            beside = scalars
         arrived, beside = lax.optimization_barrier((arrived, beside))
         if k == 0:
             acc, ml = beside
         if k == 1:
             state = beside
+        if k == ring - 2 and k > 1:
+            scalars = beside
         if k == ring - 1:
             prefill_out = beside
-        gathered.update(arrived)
-        fresh = list(arrived)
+        gathered.update(zip(names, arrived))
+        fresh = names
 
     blocks = [gathered[r, s] for r in range(roles) for s in range(ring)]
     pieces = [None] * targets
@@ -534,7 +552,7 @@
             shift = [(j, (j + s) % targets) for j in range(targets)]
             out = lax.ppermute(out, "tp", shift)
         pieces[s] = out
-    decode_out = join(pieces, meta, steps, targets, 1)
+    decode_out = join(pieces, scalars[2], steps, targets)
     return (prefill_out, decode_out)
 
 

time: 98.3 us -> 98.1 us (level)
  Pallas kernels: 65 us -> 67.2 us
  waiting for transfers between devices: 18.2 us -> 16.3 us
    pallas_call x1, Pallas kernels: 1.77 us -> 4.32 us  [join(): pl.pallas_call(functools.partial(join_kernel, targets, steps), grid_spec=...]
    ppermute x15, waiting for transfers between devices: 16.4 us -> 13.9 us  [shards(): lax.ppermute(gathered[of], axis, pairs)]
where the time goes in v9:
time: 98.1 us; the launch traced here: 97.3 us
  Pallas kernels  67.2 us (69%)
  waiting for transfers between devices  16.3 us (17%)
  starting transfers between devices  8.64 us (9%)
  local copies, waits for them, and re-layouts  2.48 us (3%)
  other arithmetic  1.86 us (2%)
    pallas_call x2, Pallas kernels, prefill(): pl.pallas_call(functools.partial(prefill_kernel, own, count, slots, group...  29 us
    pallas_call x2, Pallas kernels, decode(): pl.pallas_call(functools.partial(decode_kernel, slots, extra, steps, targ...  20.4 us
    ppermute x15, waiting for transfers between devices, shards(): lax.ppermute(gathered[of], axis, pairs)  13.9 us
    pallas_call x1, Pallas kernels, cache_part(): pl.pallas_call(functools.partial(cache_kernel, steps, heads, group, LOG2E...  11.2 us
    ppermute x15, starting transfers between devices, shards(): lax.ppermute(gathered[of], axis, pairs)  7.05 us
    pallas_call x1, Pallas kernels, join(): pl.pallas_call(functools.partial(join_kernel, targets, steps), grid_spec=...  4.32 us
    ppermute x1, waiting for transfers between devices, shards(): out = lax.ppermute(out, 'tp', shift)  2.42 us
    pallas_call x1, Pallas kernels, split_heads(): pl.pallas_call(functools.partial(split_kernel, heads, tokens), out_shape=...  2.31 us
  transfers between devices with their start and end apart: 16, of which 6 were waited for; matrix products, arithmetic and copies ran while one was open for 2% of the time, Pallas kernels for 52%

profile of v9, /device:TPU:24, one launch (start us, length us, event | category | flops | bytes accessed | tf_op | source)
XLA Modules:
  0.0 97.3 jit_solution(8827400379734264447)
XLA Ops:
  0.6 2.3 %shard_map.113.refs_1_.refs_6_ = bf16[2,4,2,128,128]{4,3,2,1,0:T(8,128)(2,1)} custom-call(bf16[1024,128]{1,0:T(8,128)(2,1)} %bitcast.12, bf16[1024,128]{1,0:T(8,128)(2,1)} %bitcast.13), custom_call_target="tpu_custom_call" | custom-call | flops 100000000 | bytes 2000000 | tf_op jit(solution)/shard_map/pallas_call | solution.py:54
  2.9 0.3 collective-permute-start.2
  3.3 1.5 %collective-permute-start.1 = (bf16[2,4,2,128,128]{4,3,2,1,0:T(8,128)(2,1)}, bf16[2,4,2,128,128]{4,3,2,1,0:T(8,128)(2,1)S(1)}, u32[]{:S(2)}, u32[]{:S(2)}) collective-permute-start(bf16[2,4,2,128,128]{4,3,2,1,0:T(8,128)(2,1)} %shard_map.113.refs_1_.refs_6_), channel_id=1, source_target_pairs={{0,16},{8,24},{16,0},{24,8},{1,17},{9,25},{17,1},{25,9},{2,18},{10... | collective-permute-start | bytes 1572872 | tf_op jit(solution)/shard_map/ppermute | solution.py:524
  4.8 0.0 collective-permute-start
  4.8 0.6 compare_convert_fusion.needed_ref
  5.4 11.2 %shard_map.114 = (f32[32,128,128]{2,1,0:T(8,128)}, f32[32,8,128]{2,1,0:T(8,128)}) custom-call(s32[32]{0:T(128)} %len_ref.1, bf16[32,128,128]{2,1,0:T(8,128)(2,1)} %bitcast.9, bf16[32,16,128]{2,1,0:T(8,128)(2,1)} %bitcast.16, bf16[32,16,128]{2,1,0:T(8,128)(2,1)} %bitcast.17, bf16[32,512,128]{2,1,0:T(8,128)(2,1)} %bitcast.14, bf16[32,512,128]{2,1,0:T(8,128)(2,1)} %bitcast.15), custom_call_target="tpu_custom_call" | custom-call | flops 4294967296 | bytes 14000000 | tf_op jit(solution)/shard_map/pallas_call | solution.py:288
  16.5 0.3 collective-permute-done.2.refs_2_.refs_7_
  16.8 0.1 collective-permute-done.1.refs_14_
  16.9 0.0 collective-permute-done.refs_10_
  16.9 1.3 %collective-permute-start.6 = (bf16[2,4,2,128,128]{4,3,2,1,0:T(8,128)(2,1)S(1)}, bf16[2,4,2,128,128]{4,3,2,1,0:T(8,128)(2,1)S(1)}, u32[]{:S(2)}, u32[]{:S(2)}) collective-permute-start(bf16[2,4,2,128,128]{4,3,2,1,0:T(8,128)(2,1)S(1)} %collective-permute-done.2.refs_2_.refs_7_), channel_id=1, source_target_pairs={{0,4},{4,6},{6,2},{2,0},{1,5},{5,7},{7,3},{3,1},{8,12},{12,14},{14... | collective-permute-start | bytes 1572872 | tf_op jit(solution)/shard_map/ppermute | solution.py:524
  18.1 1.5 %collective-permute-start.5 = (bf16[2,4,2,128,128]{4,3,2,1,0:T(8,128)(2,1)S(1)}, bf16[2,4,2,128,128]{4,3,2,1,0:T(8,128)(2,1)S(1)}, u32[]{:S(2)}, u32[]{:S(2)}) collective-permute-start(bf16[2,4,2,128,128]{4,3,2,1,0:T(8,128)(2,1)S(1)} %collective-permute-done.2.refs_2_.refs_7_), channel_id=1, source_target_pairs={{0,16},{8,24},{16,0},{24,8},{1,17},{9,25},{17,1},{25,9},{2,18},{10... | collective-permute-start | bytes 1572872 | tf_op jit(solution)/shard_map/ppermute | solution.py:524
  19.6 0.0 collective-permute-start.4
  19.6 0.5 collective-permute-start.3
  20.1 13.5 %shard_map.115 = (f32[4,4,512,128]{3,2,1,0:T(8,128)}, f32[4,4,512,128]{3,2,1,0:T(8,128)}) custom-call(s32[4]{0:T(128)} %compare_convert_fusion.needed_ref, bf16[1,256,32,128]{3,2,1,0:T(8,128)(2,1)} %refs_0_.3, bf16[2,4,2,128,128]{4,3,2,1,0:T(8,128)(2,1)} %shard_map.113.refs_1_.refs_6_, bf16[2,4,2,128,128]{4,3,2,1,0:T(8,128)(2,1)} %copy-done), custom_call_target="tpu_custom_call" | custom-call | flops 8589934592 | bytes 12000000 | tf_op jit(solution)/shard_map/pallas_call | solution.py:194
  33.7 0.0 collective-permute-done.3.refs_18_
  33.7 0.0 collective-permute-done.6.refs_1_.refs_8_
  33.7 0.0 collective-permute-done.5.refs_15_
  33.8 0.0 collective-permute-done.4.refs_11_
  33.8 0.1 collective-permute-start.7
  33.9 0.2 collective-permute-start.10
  34.1 0.4 copy-done.6
  34.5 0.5 collective-permute-start.9
  35.1 0.0 collective-permute-start.8
  35.1 0.1 copy.17
  35.2 0.1 broadcast_in_dim.15
  35.3 0.1 copy.16
  35.4 0.1 reshape.39.refs_0_
  35.5 0.6 pad_add_fusion.refs_2_.meta_ref
  36.1 0.6 select_reduce_fusion.refs_1_
  36.8 0.0 collective-permute-done.7.refs_19_
  36.8 11.4 %collective-permute-done.10.refs_2_.refs_9_ = bf16[2,4,2,128,128]{4,3,2,1,0:T(8,128)(2,1)S(1)} collective-permute-done((bf16[2,4,2,128,128]{4,3,2,1,0:T(8,128)(2,1)S(1)}, bf16[2,4,2,128,128]{4,3,2,1,0:T(8,128)(2,1)S(1)}, u32[]{:S(2)}, u32[]{:S(2)}) %collective-permute-start.10) | collective-permute-done | bytes 524320 | tf_op jit(solution)/shard_map/ppermute | solution.py:524
  48.2 0.2 collective-permute-done.9.refs_16_
  48.4 0.0 collective-permute-done.8.refs_12_
  48.4 0.5 collective-permute-start.13
  48.9 0.0 collective-permute-start.12
  48.9 0.5 collective-permute-start.11
  49.4 15.4 %shard_map.116 = bf16[1,256,32,128]{3,2,1,0:T(8,128)(2,1)} custom-call(s32[4]{0:T(128)} %compare_convert_fusion.needed_ref, bf16[1,256,32,128]{3,2,1,0:T(8,128)(2,1)} %refs_0_.3, bf16[2,4,2,128,128]{4,3,2,1,0:T(8,128)(2,1)} %copy-done.3, bf16[2,4,2,128,128]{4,3,2,1,0:T(8,128)(2,1)} %copy-done.8, f32[4,4,512,128]{3,2,1,0:T(8,128)} %get-tuple-element.38.refs_3_, ...), custom_call_target="tpu_custom_call" | custom-call | flops 8589934592 | bytes 12000000 | tf_op jit(solution)/shard_map/pallas_call | solution.py:194
  64.9 0.0 collective-permute-done.11.refs_20_
  64.9 0.0 collective-permute-done.12.refs_13_
  64.9 0.1 collective-permute-start.14
  65.0 1.9 %collective-permute-done.14.refs_21_ = bf16[2,4,2,128,128]{4,3,2,1,0:T(8,128)(2,1)S(1)} collective-permute-done((bf16[2,4,2,128,128]{4,3,2,1,0:T(8,128)(2,1)S(1)}, bf16[2,4,2,128,128]{4,3,2,1,0:T(8,128)(2,1)S(1)}, u32[]{:S(2)}, u32[]{:S(2)}) %collective-permute-start.14) | collective-permute-done | bytes 524320 | tf_op jit(solution)/shard_map/ppermute | solution.py:524
  66.9 0.8 copy-done.11
  67.7 10.2 %shard_map.118 = bf16[16,128,128]{2,1,0:T(8,128)(2,1)} custom-call(s32[128]{0:T(128)} %copy-done.13, s32[16]{0:T(128)} %select_reduce_fusion.refs_1_, s32[2]{0:T(128)} %pad_add_fusion.refs_2_.meta_ref, bf16[32,128,128]{2,1,0:T(8,128)(2,1)} %bitcast.10, f32[32,128,128]{2,1,0:T(8,128)} %get-tuple-element.44.refs_4_, f32[32,8,128]{2,1,0:T(8,128)} %get-tuple-element.45.refs_5_, ...), custom_call_target="tpu_custom_call" | custom-call | flops 2147483648 | bytes 8000000 | tf_op jit(solution)/shard_map/pallas_call | solution.py:393
  77.9 1.6 %collective-permute-start.15 = (bf16[16,128,128]{2,1,0:T(8,128)(2,1)}, bf16[16,128,128]{2,1,0:T(8,128)(2,1)S(1)}, u32[]{:S(2)}, u32[]{:S(2)}) collective-permute-start(bf16[16,128,128]{2,1,0:T(8,128)(2,1)} %shard_map.118), channel_id=1, source_target_pairs={{0,1},{1,0},{2,3},{3,2},{4,5},{5,4},{6,7},{7,6},{8,9},{9,8},{10,11... | collective-permute-start | bytes 1572872 | tf_op jit(solution)/shard_map/ppermute | solution.py:553
  79.5 10.2 %shard_map.117.refs_0_ = bf16[16,128,128]{2,1,0:T(8,128)(2,1)} custom-call(s32[128]{0:T(128)} %copy-done.13, s32[16]{0:T(128)} %select_reduce_fusion.refs_1_, s32[2]{0:T(128)} %pad_add_fusion.refs_2_.meta_ref, bf16[32,128,128]{2,1,0:T(8,128)(2,1)} %bitcast.11, f32[32,128,128]{2,1,0:T(8,128)} %get-tuple-element.44.refs_4_, ...), custom_call_target="tpu_custom_call" | custom-call | flops 2147483648 | bytes 8000000 | tf_op jit(solution)/shard_map/pallas_call | solution.py:393
  89.8 2.4 %collective-permute-done.15.refs_1_ = bf16[16,128,128]{2,1,0:T(8,128)(2,1)S(1)} collective-permute-done((bf16[16,128,128]{2,1,0:T(8,128)(2,1)}, bf16[16,128,128]{2,1,0:T(8,128)(2,1)S(1)}, u32[]{:S(2)}, u32[]{:S(2)}) %collective-permute-start.15) | collective-permute-done | bytes 524320 | tf_op jit(solution)/shard_map/ppermute | solution.py:553
  92.2 0.8 copy-done.12
  93.0 4.3 %shard_map.119 = bf16[16,4,8192]{2,1,0:T(4,128)(2,1)} custom-call(s32[2]{0:T(128)} %pad_add_fusion.refs_2_.meta_ref, bf16[16,128,128]{2,1,0:T(8,128)(2,1)} %shard_map.117.refs_0_, bf16[16,128,128]{2,1,0:T(8,128)(2,1)} %copy-done.12), custom_call_target="tpu_custom_call" | custom-call | bytes 2000000 | tf_op jit(solution)/shard_map/pallas_call | solution.py:443
  (29 shorter events, 0.1 us)
Async XLA Ops:
  2.9 13.9 %collective-permute-start.2 = (bf16[2,4,2,128,128]{4,3,2,1,0:T(8,128)(2,1)}, bf16[2,4,2,128,128]{4,3,2,1,0:T(8,128)(2,1)S(1)}, u32[]{:S(2)}, u32[]{:S(2)}) collective-permute-start(bf16[2,4,2,128,128]{4,3,2,1,0:T(8,128)(2,1)} %shard_map.113.refs_1_.refs_6_), channel_id=1, source_target_pairs={{0,4},{4,6},{6,2},{2,0},{1,5},{5,7},{7,3},{3,1},{8,12},{12,14},{14... | collective-permute-start | bytes 1572872 | tf_op jit(solution)/shard_map/ppermute | solution.py:524
  3.3 13.6 %collective-permute-start.1 = (bf16[2,4,2,128,128]{4,3,2,1,0:T(8,128)(2,1)}, bf16[2,4,2,128,128]{4,3,2,1,0:T(8,128)(2,1)S(1)}, u32[]{:S(2)}, u32[]{:S(2)}) collective-permute-start(bf16[2,4,2,128,128]{4,3,2,1,0:T(8,128)(2,1)} %shard_map.113.refs_1_.refs_6_), channel_id=1, source_target_pairs={{0,16},{8,24},{16,0},{24,8},{1,17},{9,25},{17,1},{25,9},{2,18},{10... | collective-permute-start | bytes 1572872 | tf_op jit(solution)/shard_map/ppermute | solution.py:524
  4.8 12.1 %collective-permute-start = (bf16[2,4,2,128,128]{4,3,2,1,0:T(8,128)(2,1)}, bf16[2,4,2,128,128]{4,3,2,1,0:T(8,128)(2,1)S(1)}, u32[]{:S(2)}, u32[]{:S(2)}) collective-permute-start(bf16[2,4,2,128,128]{4,3,2,1,0:T(8,128)(2,1)} %shard_map.113.refs_1_.refs_6_), channel_id=1, source_target_pairs={{0,8},{8,0},{16,24},{24,16},{1,9},{9,1},{17,25},{25,17},{2,10},{10... | collective-permute-start | bytes 1572872 | tf_op jit(solution)/shard_map/ppermute | solution.py:524
  16.8 3.3 %copy-start = (bf16[2,4,2,128,128]{4,3,2,1,0:T(8,128)(2,1)}, bf16[2,4,2,128,128]{4,3,2,1,0:T(8,128)(2,1)S(1)}, u32[]{:S(2)}) copy-start(bf16[2,4,2,128,128]{4,3,2,1,0:T(8,128)(2,1)S(1)} %collective-permute-done.2.refs_2_.refs_7_) | copy-start | bytes 1572868
  16.9 16.8 %copy-start.1 = (bf16[2,4,2,128,128]{4,3,2,1,0:T(8,128)(2,1)}, bf16[2,4,2,128,128]{4,3,2,1,0:T(8,128)(2,1)S(1)}, u32[]{:S(2)}) copy-start(bf16[2,4,2,128,128]{4,3,2,1,0:T(8,128)(2,1)S(1)} %collective-permute-done.1.refs_14_) | copy-start | bytes 1572868
  16.9 16.8 %copy-start.2 = (bf16[2,4,2,128,128]{4,3,2,1,0:T(8,128)(2,1)}, bf16[2,4,2,128,128]{4,3,2,1,0:T(8,128)(2,1)S(1)}, u32[]{:S(2)}) copy-start(bf16[2,4,2,128,128]{4,3,2,1,0:T(8,128)(2,1)S(1)} %collective-permute-done.refs_10_) | copy-start | bytes 1572868
  16.9 18.2 %copy-start.14 = (s32[32,4]{0,1:T(4,128)S(1)}, s32[32,4]{0,1:T(4,128)}, u32[]{:S(2)}) copy-start(s32[32,4]{0,1:T(4,128)} %param.19) | copy-start | bytes 1540
  16.9 16.8 %collective-permute-start.6 = (bf16[2,4,2,128,128]{4,3,2,1,0:T(8,128)(2,1)S(1)}, bf16[2,4,2,128,128]{4,3,2,1,0:T(8,128)(2,1)S(1)}, u32[]{:S(2)}, u32[]{:S(2)}) collective-permute-start(bf16[2,4,2,128,128]{4,3,2,1,0:T(8,128)(2,1)S(1)} %collective-permute-done.2.refs_2_.refs_7_), channel_id=1, source_target_pairs={{0,4},{4,6},{6,2},{2,0},{1,5},{5,7},{7,3},{3,1},{8,12},{12,14},{14... | collective-permute-start | bytes 1572872 | tf_op jit(solution)/shard_map/ppermute | solution.py:524
  18.1 15.6 %collective-permute-start.5 = (bf16[2,4,2,128,128]{4,3,2,1,0:T(8,128)(2,1)S(1)}, bf16[2,4,2,128,128]{4,3,2,1,0:T(8,128)(2,1)S(1)}, u32[]{:S(2)}, u32[]{:S(2)}) collective-permute-start(bf16[2,4,2,128,128]{4,3,2,1,0:T(8,128)(2,1)S(1)} %collective-permute-done.2.refs_2_.refs_7_), channel_id=1, source_target_pairs={{0,16},{8,24},{16,0},{24,8},{1,17},{9,25},{17,1},{25,9},{2,18},{10... | collective-permute-start | bytes 1572872 | tf_op jit(solution)/shard_map/ppermute | solution.py:524
  19.6 14.1 %collective-permute-start.4 = (bf16[2,4,2,128,128]{4,3,2,1,0:T(8,128)(2,1)S(1)}, bf16[2,4,2,128,128]{4,3,2,1,0:T(8,128)(2,1)S(1)}, u32[]{:S(2)}, u32[]{:S(2)}) collective-permute-start(bf16[2,4,2,128,128]{4,3,2,1,0:T(8,128)(2,1)S(1)} %collective-permute-done.2.refs_2_.refs_7_), channel_id=1, source_target_pairs={{0,8},{8,0},{16,24},{24,16},{1,9},{9,1},{17,25},{25,17},{2,10},{10... | collective-permute-start | bytes 1572872 | tf_op jit(solution)/shard_map/ppermute | solution.py:524
  19.6 14.1 %collective-permute-start.3 = (bf16[2,4,2,128,128]{4,3,2,1,0:T(8,128)(2,1)S(1)}, bf16[2,4,2,128,128]{4,3,2,1,0:T(8,128)(2,1)S(1)}, u32[]{:S(2)}, u32[]{:S(2)}) collective-permute-start(bf16[2,4,2,128,128]{4,3,2,1,0:T(8,128)(2,1)S(1)} %collective-permute-done.1.refs_14_), channel_id=1, source_target_pairs={{0,8},{8,0},{16,24},{24,16},{1,9},{9,1},{17,25},{25,17},{2,10},{10... | collective-permute-start | bytes 1572872 | tf_op jit(solution)/shard_map/ppermute | solution.py:524
  33.7 0.8 copy-start.6
  33.7 15.7 %copy-start.3 = (bf16[2,4,2,128,128]{4,3,2,1,0:T(8,128)(2,1)}, bf16[2,4,2,128,128]{4,3,2,1,0:T(8,128)(2,1)S(1)}, u32[]{:S(2)}) copy-start(bf16[2,4,2,128,128]{4,3,2,1,0:T(8,128)(2,1)S(1)} %collective-permute-done.6.refs_1_.refs_8_) | copy-start | bytes 1572868
  33.7 31.1 %copy-start.4 = (bf16[2,4,2,128,128]{4,3,2,1,0:T(8,128)(2,1)}, bf16[2,4,2,128,128]{4,3,2,1,0:T(8,128)(2,1)S(1)}, u32[]{:S(2)}) copy-start(bf16[2,4,2,128,128]{4,3,2,1,0:T(8,128)(2,1)S(1)} %collective-permute-done.5.refs_15_) | copy-start | bytes 1572868
  33.8 31.1 %copy-start.5 = (bf16[2,4,2,128,128]{4,3,2,1,0:T(8,128)(2,1)}, bf16[2,4,2,128,128]{4,3,2,1,0:T(8,128)(2,1)S(1)}, u32[]{:S(2)}) copy-start(bf16[2,4,2,128,128]{4,3,2,1,0:T(8,128)(2,1)S(1)} %collective-permute-done.4.refs_11_) | copy-start | bytes 1572868
  33.8 3.0 %collective-permute-start.7 = (bf16[2,4,2,128,128]{4,3,2,1,0:T(8,128)(2,1)S(1)}, bf16[2,4,2,128,128]{4,3,2,1,0:T(8,128)(2,1)S(1)}, u32[]{:S(2)}, u32[]{:S(2)}) collective-permute-start(bf16[2,4,2,128,128]{4,3,2,1,0:T(8,128)(2,1)S(1)} %collective-permute-done.5.refs_15_), channel_id=1, source_target_pairs={{0,8},{8,0},{16,24},{24,16},{1,9},{9,1},{17,25},{25,17},{2,10},{10... | collective-permute-start | bytes 1572872 | tf_op jit(solution)/shard_map/ppermute | solution.py:524
  33.9 14.3 %collective-permute-start.10 = (bf16[2,4,2,128,128]{4,3,2,1,0:T(8,128)(2,1)S(1)}, bf16[2,4,2,128,128]{4,3,2,1,0:T(8,128)(2,1)S(1)}, u32[]{:S(2)}, u32[]{:S(2)}) collective-permute-start(bf16[2,4,2,128,128]{4,3,2,1,0:T(8,128)(2,1)S(1)} %collective-permute-done.6.refs_1_.refs_8_), channel_id=1, source_target_pairs={{0,4},{4,6},{6,2},{2,0},{1,5},{5,7},{7,3},{3,1},{8,12},{12,14},{14... | collective-permute-start | bytes 1572872 | tf_op jit(solution)/shard_map/ppermute | solution.py:524
  34.5 13.8 %collective-permute-start.9 = (bf16[2,4,2,128,128]{4,3,2,1,0:T(8,128)(2,1)S(1)}, bf16[2,4,2,128,128]{4,3,2,1,0:T(8,128)(2,1)S(1)}, u32[]{:S(2)}, u32[]{:S(2)}) collective-permute-start(bf16[2,4,2,128,128]{4,3,2,1,0:T(8,128)(2,1)S(1)} %collective-permute-done.6.refs_1_.refs_8_), channel_id=1, source_target_pairs={{0,16},{8,24},{16,0},{24,8},{1,17},{9,25},{17,1},{25,9},{2,18},{10... | collective-permute-start | bytes 1572872 | tf_op jit(solution)/shard_map/ppermute | solution.py:524
  35.1 13.3 %collective-permute-start.8 = (bf16[2,4,2,128,128]{4,3,2,1,0:T(8,128)(2,1)S(1)}, bf16[2,4,2,128,128]{4,3,2,1,0:T(8,128)(2,1)}, u32[]{:S(2)}, u32[]{:S(2)}) collective-permute-start(bf16[2,4,2,128,128]{4,3,2,1,0:T(8,128)(2,1)S(1)} %collective-permute-done.6.refs_1_.refs_8_), channel_id=1, source_target_pairs={{0,8},{8,0},{16,24},{24,16},{1,9},{9,1},{17,25},{25,17},{2,10},{10... | collective-permute-start | bytes 1572872 | tf_op jit(solution)/shard_map/ppermute | solution.py:524
  35.5 29.4 %copy-start.13 = (s32[128]{0:T(128)}, s32[128]{0:T(128)S(1)}, u32[]{:S(2)}) copy-start(s32[128]{0:T(128)S(1)} %reshape.39.refs_0_) | copy-start | bytes 1540
  36.8 28.1 %copy-start.7 = (bf16[2,4,2,128,128]{4,3,2,1,0:T(8,128)(2,1)}, bf16[2,4,2,128,128]{4,3,2,1,0:T(8,128)(2,1)S(1)}, u32[]{:S(2)}) copy-start(bf16[2,4,2,128,128]{4,3,2,1,0:T(8,128)(2,1)S(1)} %collective-permute-done.7.refs_19_) | copy-start | bytes 1572868
  48.2 1.2 %copy-start.8 = (bf16[2,4,2,128,128]{4,3,2,1,0:T(8,128)(2,1)}, bf16[2,4,2,128,128]{4,3,2,1,0:T(8,128)(2,1)S(1)}, u32[]{:S(2)}) copy-start(bf16[2,4,2,128,128]{4,3,2,1,0:T(8,128)(2,1)S(1)} %collective-permute-done.10.refs_2_.refs_9_) | copy-start | bytes 1572868
  48.4 16.5 %copy-start.9 = (bf16[2,4,2,128,128]{4,3,2,1,0:T(8,128)(2,1)}, bf16[2,4,2,128,128]{4,3,2,1,0:T(8,128)(2,1)S(1)}, u32[]{:S(2)}) copy-start(bf16[2,4,2,128,128]{4,3,2,1,0:T(8,128)(2,1)S(1)} %collective-permute-done.9.refs_16_) | copy-start | bytes 1572868
  48.4 16.6 %collective-permute-start.13 = (bf16[2,4,2,128,128]{4,3,2,1,0:T(8,128)(2,1)S(1)}, bf16[2,4,2,128,128]{4,3,2,1,0:T(8,128)(2,1)S(1)}, u32[]{:S(2)}, u32[]{:S(2)}) collective-permute-start(bf16[2,4,2,128,128]{4,3,2,1,0:T(8,128)(2,1)S(1)} %collective-permute-done.10.refs_2_.refs_9_), channel_id=1, source_target_pairs={{0,16},{8,24},{16,0},{24,8},{1,17},{9,25},{17,1},{25,9},{2,18},{10... | collective-permute-start | bytes 1572872 | tf_op jit(solution)/shard_map/ppermute | solution.py:524
  48.9 16.0 %collective-permute-start.12 = (bf16[2,4,2,128,128]{4,3,2,1,0:T(8,128)(2,1)S(1)}, bf16[2,4,2,128,128]{4,3,2,1,0:T(8,128)(2,1)}, u32[]{:S(2)}, u32[]{:S(2)}) collective-permute-start(bf16[2,4,2,128,128]{4,3,2,1,0:T(8,128)(2,1)S(1)} %collective-permute-done.10.refs_2_.refs_9_), channel_id=1, source_target_pairs={{0,8},{8,0},{16,24},{24,16},{1,9},{9,1},{17,25},{25,17},{2,10},{10... | collective-permute-start | bytes 1572872 | tf_op jit(solution)/shard_map/ppermute | solution.py:524
  48.9 16.0 %collective-permute-start.11 = (bf16[2,4,2,128,128]{4,3,2,1,0:T(8,128)(2,1)S(1)}, bf16[2,4,2,128,128]{4,3,2,1,0:T(8,128)(2,1)}, u32[]{:S(2)}, u32[]{:S(2)}) collective-permute-start(bf16[2,4,2,128,128]{4,3,2,1,0:T(8,128)(2,1)S(1)} %collective-permute-done.9.refs_16_), channel_id=1, source_target_pairs={{0,8},{8,0},{16,24},{24,16},{1,9},{9,1},{17,25},{25,17},{2,10},{10... | collective-permute-start | bytes 1572872 | tf_op jit(solution)/shard_map/ppermute | solution.py:524
  64.9 2.0 %copy-start.10 = (bf16[2,4,2,128,128]{4,3,2,1,0:T(8,128)(2,1)}, bf16[2,4,2,128,128]{4,3,2,1,0:T(8,128)(2,1)S(1)}, u32[]{:S(2)}) copy-start(bf16[2,4,2,128,128]{4,3,2,1,0:T(8,128)(2,1)S(1)} %collective-permute-done.13.refs_17_) | copy-start | bytes 1572868
  64.9 2.0 %collective-permute-start.14 = (bf16[2,4,2,128,128]{4,3,2,1,0:T(8,128)(2,1)S(1)}, bf16[2,4,2,128,128]{4,3,2,1,0:T(8,128)(2,1)S(1)}, u32[]{:S(2)}, u32[]{:S(2)}) collective-permute-start(bf16[2,4,2,128,128]{4,3,2,1,0:T(8,128)(2,1)S(1)} %collective-permute-done.13.refs_17_), channel_id=1, source_target_pairs={{0,8},{8,0},{16,24},{24,16},{1,9},{9,1},{17,25},{25,17},{2,10},{10... | collective-permute-start | bytes 1572872 | tf_op jit(solution)/shard_map/ppermute | solution.py:524
  66.9 0.8 copy-start.11
  77.9 14.2 %collective-permute-start.15 = (bf16[16,128,128]{2,1,0:T(8,128)(2,1)}, bf16[16,128,128]{2,1,0:T(8,128)(2,1)S(1)}, u32[]{:S(2)}, u32[]{:S(2)}) collective-permute-start(bf16[16,128,128]{2,1,0:T(8,128)(2,1)} %shard_map.118), channel_id=1, source_target_pairs={{0,1},{1,0},{2,3},{3,2},{4,5},{5,4},{6,7},{7,6},{8,9},{9,8},{10,11... | collective-permute-start | bytes 1572872 | tf_op jit(solution)/shard_map/ppermute | solution.py:553
  92.2 0.8 copy-start.12

commit v10 on v9

--- a/solution.py
+++ b/solution.py
@@ -11,7 +11,7 @@
 PAGE = 128
 LOG2E = 1.4426950408889634
 NEG = -1e30
-VMEM_LIMIT = 60 * 1024 * 1024
+VMEM_LIMIT = 32 * 1024 * 1024
 
 
 def nt(a, b):
@@ -20,6 +20,10 @@
 
 def nn(a, b):
     return jnp.dot(a, b, preferred_element_type=jnp.float32)
+
+
+def in_hbm(*arrays):
+    return [pltpu.with_memory_space_constraint(a, pltpu.HBM) for a in arrays]
 
 
 def params():
@@ -63,13 +67,14 @@
     q_ref = refs[0]
     blocks = refs[1 : 1 + count]
     refs = refs[1 + count :]
+    i = pl.program_id(0)
     if own:
-        out_ref, lse_ref, buf, s_ref, m_ref, l_ref, acc_ref, sems = refs
+        acc_ref, m_ref, l_ref, buf, s_ref, sems = refs
+        acc_ref, m_ref, l_ref = acc_ref.at[i], m_ref.at[i], l_ref.at[i]
     else:
-        old_ref, old_lse_ref, out_ref, buf, s_ref, m_ref, l_ref, acc_ref, sems = refs
+        old_acc_ref, old_m_ref, old_l_ref, out_ref, buf, s_ref, acc_ref, m_ref, l_ref, sems = refs
     pages, heads = blocks[0].shape[:2]
     block = q_ref.shape[1]
-    i = pl.program_id(0)
     rest = range(1 if own else 0, count)
     total = sum(needed_ref[slots[c]] for c in rest)
 
@@ -94,11 +99,14 @@
                 copy.wait()
 
     rows = block * group
+    piece = min(rows, 256)
+    parts = [(h, pl.ds(c, piece)) for h in range(heads) for c in range(0, rows, piece)]
     queries = q_ref[0].astype(jnp.float32)
     q = [
         queries[:, h * group : (h + 1) * group, :].reshape(rows, -1).astype(jnp.bfloat16)
         for h in range(heads)
     ]
+    q = [q[h][c : c + piece] for h in range(heads) for c in range(0, rows, piece)]
 
     def fold(a, op):
         return functools.reduce(op, [a[:, j * 128 : (j + 1) * 128] for j in range(a.shape[1] // 128)])
@@ -109,66 +117,59 @@
     def values(ref, h):
         return jnp.concatenate([ref[j, h, 1] for j in range(pages)], axis=1)
 
+    def weights(place, h, at, m):
+        return [
+            jnp.exp2((s_ref[place, h, at, pl.ds(j * 128, 128)] - m) * scale)
+            for j in range(tokens // 128)
+        ]
+
     last = count - 1
     if own:
-        token = lax.broadcasted_iota(jnp.int32, (rows, tokens), 0) // group + i * block
-        allowed = lax.broadcasted_iota(jnp.int32, (rows, tokens), 1) <= token
+        for n, (h, at) in enumerate(parts):
+            row = lax.broadcasted_iota(jnp.int32, (piece, tokens), 0) + n * piece % rows
+            allowed = lax.broadcasted_iota(jnp.int32, (piece, tokens), 1) <= row // group + i * block
+            s = jnp.where(allowed, nt(q[n], keys(blocks[0], h)), NEG)
+            s_ref[last, h, at] = s
+            m_ref[h, at] = fold(s, jnp.maximum)
+    else:
+        m_ref[...] = old_m_ref[i]
+
+    def look(b, carry):
+        for n, (h, at) in enumerate(parts):
+            s = nt(q[n], keys(buf.at[b], h))
+            s_ref[b, h, at] = s
+            m_ref[h, at] = jnp.maximum(m_ref[h, at], fold(s, jnp.maximum))
+        return carry
+
+    lax.fori_loop(0, total, look, 0)
+    for h, at in parts:
+        m = m_ref[h, at]
+        m = jnp.broadcast_to(jnp.max(m, axis=1, keepdims=True), m.shape)
+        m_ref[h, at] = m
+        if own:
+            p = weights(last, h, at, m)
+            l_ref[h, at] = functools.reduce(jnp.add, p)
+            p = jnp.concatenate([a.astype(jnp.bfloat16) for a in p], axis=1)
+            acc_ref[h, at] = nt(p, values(blocks[0], h))
+        else:
+            share = jnp.exp2((old_m_ref[i, h, at] - m) * scale)
+            l_ref[h, at] = old_l_ref[i, h, at] * share
+            acc_ref[h, at] = old_acc_ref[i, h, at] * share
+
+    def weigh(b, carry):
+        for h, at in parts:
+            p = weights(b, h, at, m_ref[h, at])
+            l_ref[h, at] = l_ref[h, at] + functools.reduce(jnp.add, p)
+            p = jnp.concatenate([a.astype(jnp.bfloat16) for a in p], axis=1)
+            acc_ref[h, at] = acc_ref[h, at] + nt(p, values(buf.at[b], h))
+        return carry
+
+    lax.fori_loop(0, total, weigh, 0)
+    if not own:
+        out = []
         for h in range(heads):
-            s = jnp.where(allowed, nt(q[h], keys(blocks[0], h)), NEG)
-            s_ref[last, h] = s
-            m_ref[h] = fold(s, jnp.maximum)
-    else:
-        for h in range(heads):
-            m_ref[h] = old_lse_ref[0, h]
-
-    def look(b, carry):
-        for h in range(heads):
-            s = nt(q[h], keys(buf.at[b], h))
-            s_ref[b, h] = s
-            m_ref[h] = jnp.maximum(m_ref[h], fold(s, jnp.maximum))
-        return carry
-
-    lax.fori_loop(0, total, look, 0)
-    for h in range(heads):
-        m = jnp.broadcast_to(jnp.max(m_ref[h], axis=1, keepdims=True), m_ref.shape[1:])
-        m_ref[h] = m
-        if own:
-            p = [
-                jnp.exp2((s_ref[last, h, :, pl.ds(j * 128, 128)] - m) * scale)
-                for j in range(tokens // 128)
-            ]
-            l_ref[h] = functools.reduce(jnp.add, p)
-            p = jnp.concatenate([a.astype(jnp.bfloat16) for a in p], axis=1)
-            acc_ref[h] = nt(p, values(blocks[0], h))
-        else:
-            share = jnp.exp2((old_lse_ref[0, h] - m) * scale)
-            first = lax.broadcasted_iota(jnp.int32, share.shape, 1) == 0
-            l_ref[h] = jnp.where(first, share, 0.0)
-            acc_ref[h] = old_ref[0, h] * share
-
-    def weigh(b, carry):
-        for h in range(heads):
-            m = m_ref[h]
-            p = [
-                jnp.exp2((s_ref[b, h, :, pl.ds(j * 128, 128)] - m) * scale)
-                for j in range(tokens // 128)
-            ]
-            l_ref[h] = l_ref[h] + functools.reduce(jnp.add, p)
-            p = jnp.concatenate([a.astype(jnp.bfloat16) for a in p], axis=1)
-            acc_ref[h] = acc_ref[h] + nt(p, values(buf.at[b], h))
-        return carry
-
-    lax.fori_loop(0, total, weigh, 0)
-    out = []
-    for h in range(heads):
-        l = jnp.sum(l_ref[h], axis=1, keepdims=True)
-        l = jnp.broadcast_to(l, m_ref.shape[1:])
-        if own:
-            out_ref[0, h] = acc_ref[h] / l
-            lse_ref[0, h] = m_ref[h] + jnp.log2(l) * (1.0 / scale)
-        else:
+            l = jnp.sum(l_ref[h], axis=1, keepdims=True)
             out.append((acc_ref[h] / l).reshape(block, group, -1))
-    if not own:
         out_ref[0] = jnp.concatenate(out, axis=1).astype(out_ref.dtype)
 
 
@@ -183,14 +184,19 @@
     q_spec = pl.BlockSpec((1, block, q_heads, width), lambda i, *_: (0, i, 0, 0))
     own_spec = pl.BlockSpec(blocks[0].shape, lambda i, *_: (0, 0, 0, 0, 0))
     any_spec = pl.BlockSpec(memory_space=pl.ANY)
-    state_spec = pl.BlockSpec((1, heads, rows, width), lambda i, *_: (i, 0, 0, 0))
-    shape = jax.ShapeDtypeStruct((tokens // block, heads, rows, width), jnp.float32)
+    on_chip = pl.BlockSpec(memory_space=pltpu.VMEM)
+    scratch = [
+        pltpu.VMEM((count,) + blocks[0].shape, jnp.bfloat16),
+        pltpu.VMEM((count, heads, rows, tokens), jnp.float32),
+    ]
     if own:
         in_specs = [q_spec, own_spec] + [any_spec] * (count - 1)
-        out_specs, out_shape, state = [state_spec] * 2, [shape] * 2, ()
+        out_specs, state = [on_chip] * 3, ()
+        out_shape = [pltpu.VMEM((tokens // block, heads, rows, width), jnp.float32)] * 3
     else:
-        in_specs = [q_spec] + [any_spec] * count + [state_spec] * 2
+        in_specs = [q_spec] + [any_spec] * count + [on_chip] * 3
         out_specs, out_shape = q_spec, jax.ShapeDtypeStruct(q.shape, jnp.bfloat16)
+        scratch += [pltpu.VMEM((heads, rows, width), jnp.float32)] * 3
     return pl.pallas_call(
         functools.partial(
             prefill_kernel, own, count, slots, group, tokens, LOG2E / math.sqrt(width)
@@ -200,14 +206,7 @@
             grid=(tokens // block,),
             in_specs=in_specs,
             out_specs=out_specs,
-            scratch_shapes=[
-                pltpu.VMEM((count,) + blocks[0].shape, jnp.bfloat16),
-                pltpu.VMEM((count, heads, rows, tokens), jnp.float32),
-                pltpu.VMEM((heads, rows, width), jnp.float32),
-                pltpu.VMEM((heads, rows, width), jnp.float32),
-                pltpu.VMEM((heads, rows, width), jnp.float32),
-                pltpu.SemaphoreType.DMA((count,)),
-            ],
+            scratch_shapes=scratch + [pltpu.SemaphoreType.DMA((count,))],
         ),
         out_shape=out_shape,
         compiler_params=params(),
@@ -216,12 +215,13 @@
             bytes_accessed=12 * 10**6,
             transcendentals=tokens * tokens * count * q_heads,
         ),
-    )(needed, q, *blocks, *state)
+    )(needed, *in_hbm(q), *blocks, *state)
 
 
 def cache_kernel(
-    steps, heads, group, scale, len_ref, q_ref, dk_ref, dv_ref, ck_ref, cv_ref, acc_ref, ml_ref
+    steps, heads, group, target, targets, scale, len_ref, meta_ref, *refs
 ):
+    q_ref, dk_ref, dv_ref, ck_ref, cv_ref, acc_ref, ml_ref = refs
     block, rows, width = q_ref.shape
     cache = ck_ref.shape[1]
     new = dk_ref.shape[1]
@@ -239,7 +239,8 @@
     new_place, step = mask(new)
     new_allowed = new_place <= step
     low = lax.broadcasted_iota(jnp.int32, (rows, width), 1) < 4
-    first = pl.program_id(0) * block
+    i = pl.program_id(0)
+    first = (lax.rem(meta_ref[1] + target, targets) * pl.num_programs(0) + i) * block
     unroll = math.gcd(4, block)
 
     def body(g, carry):
@@ -266,41 +267,47 @@
             add = jnp.exp2((add - m) * scale)
             l = jnp.sum(functools.reduce(jnp.add, old), axis=1, keepdims=True)
             l = l + jnp.sum(add, axis=1, keepdims=True)
-            ml_ref[r] = jnp.where(low, m, l).T[:8]
+            ml_ref[i * block + r] = jnp.where(low, m, l).T[:8]
             weights.append((r, [a.astype(jnp.bfloat16) for a in old], add.astype(jnp.bfloat16)))
         for r, old, add in weights:
             acc = nn(add, dv_ref[r])
             for c, p in zip(pieces, old):
                 acc = acc + nn(p, cv_ref[r, pl.ds(c, piece), :])
-            acc_ref[r] = acc.T
+            acc_ref[i * block + r] = acc.T
         return carry
 
     lax.fori_loop(0, block // unroll, body, 0)
 
 
-def cache_part(q, dk, dv, ck, cv, lens, steps, heads, group):
+def cache_part(q, dk, dv, ck, cv, lens, meta, target, targets, steps, heads, group):
     requests, rows, width = q.shape
-    block = math.gcd(8, requests)
-    spec = [
-        pl.BlockSpec((block,) + a.shape[1:], lambda i, *_: (i, 0, 0)) for a in (q, dk, dv, ck, cv)
-    ]
-    shapes = [(requests, width, rows), (requests, 8, rows)]
+    per_target = requests // targets
+    block = math.gcd(8, per_target)
+    per_block = per_target // block
+
+    def here(i, lens, meta):
+        return (lax.rem(meta[1] + target, targets) * per_block + i, 0, 0)
+
+    spec = [pl.BlockSpec((block,) + a.shape[1:], here) for a in (q, dk, dv, ck, cv)]
+    shapes = [(per_target, width, rows), (per_target, 8, rows)]
     return pl.pallas_call(
-        functools.partial(cache_kernel, steps, heads, group, LOG2E / math.sqrt(width)),
+        functools.partial(
+            cache_kernel, steps, heads, group, target, targets, LOG2E / math.sqrt(width)
+        ),
         grid_spec=pltpu.PrefetchScalarGridSpec(
-            num_scalar_prefetch=1,
-            grid=(requests // block,),
+            num_scalar_prefetch=2,
+            grid=(per_block,),
             in_specs=spec,
-            out_specs=[pl.BlockSpec((block,) + a[1:], lambda i, *_: (i, 0, 0)) for a in shapes],
-        ),
-        out_shape=[jax.ShapeDtypeStruct(a, jnp.float32) for a in shapes],
+            out_specs=[pl.BlockSpec(memory_space=pltpu.VMEM)] * 2,
+        ),
+        out_shape=[pltpu.VMEM(a, jnp.float32) for a in shapes],
         compiler_params=params(),
         cost_estimate=pl.CostEstimate(
-            flops=requests * rows * ck.shape[1] * width * 16,
-            bytes_accessed=14 * 10**6,
-            transcendentals=requests * rows * ck.shape[1],
-        ),
-    )(lens, q, dk, dv, ck, cv)
+            flops=per_target * rows * ck.shape[1] * width * 16,
+            bytes_accessed=7 * 10**6,
+            transcendentals=per_target * rows * ck.shape[1],
+        ),
+    )(lens, meta, *in_hbm(q, dk, dv, ck, cv))
 
 
 def decode_kernel(slots, extra, steps, target, targets, heads, group, scale, *refs):
@@ -349,13 +356,13 @@
             scores.append((r, places, s))
         weights = []
         for r, places, s in scores:
-            old = ml_ref[r, 0:1]
+            old = ml_ref[i * block + r, 0:1]
             m = jnp.max(functools.reduce(jnp.maximum, s), axis=0, keepdims=True)
             m = jnp.maximum(m, old)
             p = [jnp.exp2((a - m) * scale) for a in s]
             shrink = jnp.exp2((old - m) * scale)
             l = jnp.sum(functools.reduce(jnp.add, p), axis=0, keepdims=True)
-            l = ml_ref[r, 4:5] * shrink + l
+            l = ml_ref[i * block + r, 4:5] * shrink + l
             p = jnp.concatenate([a.astype(jnp.bfloat16) for a in p], axis=0)
             weights.append((r, places, p, shrink, l))
         results = []
@@ -370,7 +377,7 @@
                 for w in range(both):
                     mine = pair[w * width : (w + 1) * width]
                     part = mine if h + w == 0 else jnp.where(lane_head == h + w, mine, part)
-            results.append((r, ((acc_ref[r] * shrink + part) / l).astype(jnp.bfloat16)))
+            results.append((r, ((acc_ref[i * block + r] * shrink + part) / l).astype(jnp.bfloat16)))
         for r, result in results:
             out_ref[r] = nt(order, result).astype(jnp.bfloat16)
         return carry
@@ -388,7 +395,8 @@
     def here(i, slot, pick, meta):
         return (lax.rem(meta[1] + target, targets) * per_block + i, 0, 0)
 
-    in_specs = [pl.BlockSpec((block,) + a.shape[1:], here) for a in (q, acc, ml)]
+    in_specs = [pl.BlockSpec((block,) + q.shape[1:], here)]
+    in_specs += [pl.BlockSpec(memory_space=pltpu.VMEM)] * 2
     in_specs += [pl.BlockSpec(memory_space=pl.ANY)] * slots
     return pl.pallas_call(
         functools.partial(
@@ -419,37 +427,45 @@
             bytes_accessed=8 * 10**6,
             transcendentals=per_target * lanes * extra * PAGE,
         ),
-    )(*scalars, q, acc, ml, *blocks)
-
-
-def join_kernel(targets, steps, meta_ref, *refs):
+    )(*scalars, *in_hbm(q), acc, ml, *blocks)
+
+
+def join_kernel(targets, chunks, steps, meta_ref, *refs):
     out_ref = refs[-1]
+    k = pl.program_id(0)
     rows = refs[0].shape[1]
     each = rows // steps
     for s in range(targets):
-        start = lax.rem(meta_ref[1] + (targets - s), targets) * (each * 128)
-        for r in range(out_ref.shape[0]):
-            value = refs[s][r]
-            for g in range(each):
-                column = pl.multiple_of(start + g * 128, 128)
-                out_ref[r, :, pl.ds(column, 128)] = value[g * steps : (g + 1) * steps]
-
-
-def join(pieces, meta, steps, targets):
+        @pl.when(lax.rem(meta_ref[1] + (targets - s), targets) == k)
+        def _():
+            for c in range(chunks):
+                source = refs[s * chunks + c]
+
+                def body(r, carry):
+                    value = source[r]
+                    for g in range(each):
+                        out_ref[r, :, (c * each + g) * 128 : (c * each + g + 1) * 128] = value[
+                            g * steps : (g + 1) * steps
+                        ]
+                    return carry
+
+                lax.fori_loop(0, out_ref.shape[0], body, 0)
+
+
+def join(pieces, meta, steps, targets, chunks):
     per_target, rows, width = pieces[0].shape
-    whole = rows // steps * width * targets
-    block = math.gcd(4, per_target)
-    spec = pl.BlockSpec((block, rows, width), lambda k, *_: (k, 0, 0))
+    half = chunks * (rows // steps) * width
+    spec = pl.BlockSpec((per_target, rows, width), lambda k, *_: (0, 0, 0))
     return pl.pallas_call(
-        functools.partial(join_kernel, targets, steps),
+        functools.partial(join_kernel, targets, chunks, steps),
         grid_spec=pltpu.PrefetchScalarGridSpec(
             num_scalar_prefetch=1,
-            grid=(per_target // block,),
+            grid=(targets,),
             in_specs=[spec] * len(pieces),
-            out_specs=pl.BlockSpec((block, steps, whole), lambda k, *_: (k, 0, 0)),
-        ),
-        out_shape=jax.ShapeDtypeStruct((per_target, steps, whole), jnp.bfloat16),
-        compiler_params=params(),
+            out_specs=pl.BlockSpec((per_target, steps, half), lambda k, *_: (0, 0, k)),
+        ),
+        out_shape=jax.ShapeDtypeStruct((per_target, steps, half * targets), jnp.bfloat16),
+        compiler_params=pltpu.CompilerParams(vmem_limit_bytes=16 * 1024 * 1024),
         cost_estimate=pl.CostEstimate(flops=0, bytes_accessed=2 * 10**6, transcendentals=0),
     )(meta, *pieces)
 
@@ -508,6 +524,10 @@
         a.reshape(requests, -1, width) for a in (decode_q, decode_k, decode_v, cache_k, cache_v)
     ]
 
+    def cache(target):
+        lens = cache_len.astype(jnp.int32)
+        return cache_part(*raw, lens, meta, target, targets, steps, heads, group)
+
     gathered = {(0, 0): split_heads(prefill_k, prefill_v)}
     fresh = [(0, 0)]
     for k in range(ring + len(flips) - 1):
@@ -524,21 +544,22 @@
         arrived = [lax.ppermute(gathered[of], axis, pairs) for _, of, _, axis, pairs in sends]
         beside = ()
         if k == 0:
-            beside = cache_part(*raw, cache_len.astype(jnp.int32), steps, heads, group)
+            beside = cache(targets - 1)
         if k == 1:
             beside = prefill(prefill_q, [gathered[0, s] for s in (0, 1)], (0, 1), needed, None)
         if k == ring - 1:
             later = tuple(range(2, ring))
             beside = prefill(prefill_q, [gathered[0, s] for s in later], later, needed, state)
         if k == ring - 2 and k > 1:
-            beside = scalars
+            beside = scalars, {s: cache(s) for s in range(targets - 1)}
         arrived, beside = lax.optimization_barrier((arrived, beside))
         if k == 0:
-            acc, ml = beside
+            cached = {targets - 1: beside}
         if k == 1:
             state = beside
         if k == ring - 2 and k > 1:
-            scalars = beside
+            scalars, others = beside
+            cached.update(others)
         if k == ring - 1:
             prefill_out = beside
         gathered.update(zip(names, arrived))
@@ -547,12 +568,12 @@
     blocks = [gathered[r, s] for r in range(roles) for s in range(ring)]
     pieces = [None] * targets
     for s in reversed(range(targets)):
-        out = decode(raw[0], acc, ml, blocks, scalars, s, targets, extra, steps, heads, group)
+        out = decode(raw[0], *cached[s], blocks, scalars, s, targets, extra, steps, heads, group)
         if s:
             shift = [(j, (j + s) % targets) for j in range(targets)]
             out = lax.ppermute(out, "tp", shift)
         pieces[s] = out
-    decode_out = join(pieces, scalars[2], steps, targets)
+    decode_out = join(pieces, scalars[2], steps, targets, 1)
     return (prefill_out, decode_out)
 
 

time: 98.1 us -> 95.6 us (0.975)
  Pallas kernels: 67.2 us -> 55.5 us
  local copies, waits for them, and re-layouts: 2.48 us -> 13.7 us
  other arithmetic: 1.86 us -> 0.24 us
    unnamed x30 -> x34, local copies, waits for them, and re-layouts: 2.1 us -> 13.3 us
    pallas_call x2, Pallas kernels: 29 us -> 24.2 us  [prefill(): pl.pallas_call(functools.partial(prefill_kernel, own, count, slots, group...]
    pallas_call x2, Pallas kernels: 20.4 us -> 16.3 us  [decode(): pl.pallas_call(functools.partial(decode_kernel, slots, extra, steps, targ...]
    ppermute x15, waiting for transfers between devices: 13.9 us -> 11.6 us  [shards(): lax.ppermute(gathered[of], axis, pairs)]
    ppermute x1, waiting for transfers between devices: 2.42 us -> 4.26 us  [shards(): out = lax.ppermute(out, 'tp', shift)]
    pallas_call x1, Pallas kernels: 2.31 us -> 0.48 us  [split_heads(): pl.pallas_call(functools.partial(split_kernel, heads, tokens), out_shape=...]
    pallas_call x2 -> x3, Pallas kernels: 15.5 us -> 14.5 us  [the longest x2 12.8 us: cache_part(): pl.pallas_call(functools.partial(cache_kernel, steps, heads, group, targe...]
  transfers between devices with their start and end apart: 16 -> 16, of which waited for: 6 -> 5; matrix products, arithmetic and copies ran while one was open for 2% -> 1% of each run, Pallas kernels for 52% -> 47%
where the time goes in v10:
time: 95.6 us; the launch traced here: 95.1 us
  Pallas kernels  55.5 us (58%)
  waiting for transfers between devices  15.9 us (17%)
  local copies, waits for them, and re-layouts  13.7 us (14%)
  starting transfers between devices  8.92 us (9%)
    pallas_call x2, Pallas kernels, prefill(): pl.pallas_call(functools.partial(prefill_kernel, own, count, slots, group...  24.2 us
    pallas_call x2, Pallas kernels, decode(): pl.pallas_call(functools.partial(decode_kernel, slots, extra, steps, targ...  16.3 us
    unnamed x34, local copies, waits for them, and re-layouts  13.3 us
    pallas_call x2, Pallas kernels, cache_part(): pl.pallas_call(functools.partial(cache_kernel, steps, heads, group, targe...  12.8 us
    ppermute x15, waiting for transfers between devices, shards(): lax.ppermute(gathered[of], axis, pairs)  11.6 us
    ppermute x15, starting transfers between devices, shards(): lax.ppermute(gathered[of], axis, pairs)  7.34 us
    ppermute x1, waiting for transfers between devices, shards(): out = lax.ppermute(out, 'tp', shift)  4.26 us
  transfers between devices with their start and end apart: 16, of which 5 were waited for; matrix products, arithmetic and copies ran while one was open for 1% of the time, Pallas kernels for 47%

profile of v10, /device:TPU:24, one launch (start us, length us, event | category | flops | bytes accessed | tf_op | source)
XLA Modules:
  0.0 95.1 jit_solution(18259273632956926768)
XLA Ops:
  0.6 0.9 copy-done.6
  1.6 0.9 copy-done.7
  2.5 0.5 shard_map.113.refs_1_.refs_6_
  3.0 0.4 collective-permute-start.2
  3.4 1.5 %collective-permute-start.1 = (bf16[2,4,2,128,128]{4,3,2,1,0:T(8,128)(2,1)S(1)}, bf16[2,4,2,128,128]{4,3,2,1,0:T(8,128)(2,1)S(1)}, u32[]{:S(2)}, u32[]{:S(2)}) collective-permute-start(bf16[2,4,2,128,128]{4,3,2,1,0:T(8,128)(2,1)S(1)} %shard_map.113.refs_1_.refs_6_), channel_id=1, source_target_pairs={{0,16},{8,24},{16,0},{24,8},{1,17},{9,25},{17,1},{25,9},{2,18},{10... | collective-permute-start | bytes 1572872 | tf_op jit(solution)/shard_map/ppermute | solution.py:544
  4.9 0.0 collective-permute-start
  4.9 0.1 pad_add_fusion.meta_ref.refs_2_
  5.0 0.7 copy-done.8
  5.6 6.2 %shard_map.114 = (f32[16,128,128]{2,1,0:T(8,128)S(1)}, f32[16,8,128]{2,1,0:T(8,128)S(1)}) custom-call(s32[32]{0:T(128)S(1)} %copy-done.8, s32[2]{0:T(128)S(1)} %pad_add_fusion.meta_ref.refs_2_, bf16[32,128,128]{2,1,0:T(8,128)(2,1)} %bitcast.11, bf16[32,16,128]{2,1,0:T(8,128)(2,1)} %bitcast.19, bf16[32,16,128]{2,1,0:T(8,128)(2,1)} %bitcast.21, ...), custom_call_target="tpu_custom_call" | custom-call | flops 2147483648 | bytes 7000000 | tf_op jit(solution)/shard_map/pallas_call | solution.py:293
  11.9 0.0 copy-start.4
  11.9 1.0 %copy-done.4 = f32[16,128,128]{2,1,0:T(8,128)} copy-done((f32[16,128,128]{2,1,0:T(8,128)}, f32[16,128,128]{2,1,0:T(8,128)S(1)}, u32[]{:S(2)}) %copy-start.4) | copy-done | bytes 1048600
  12.9 3.9 %collective-permute-done.2.refs_2_.refs_7_ = bf16[2,4,2,128,128]{4,3,2,1,0:T(8,128)(2,1)S(1)} collective-permute-done((bf16[2,4,2,128,128]{4,3,2,1,0:T(8,128)(2,1)S(1)}, bf16[2,4,2,128,128]{4,3,2,1,0:T(8,128)(2,1)S(1)}, u32[]{:S(2)}, u32[]{:S(2)}) %collective-permute-start.2) | collective-permute-done | bytes 524320 | tf_op jit(solution)/shard_map/ppermute | solution.py:544
  16.7 0.1 collective-permute-done.1.refs_14_
  16.8 1.2 %collective-permute-start.6 = (bf16[2,4,2,128,128]{4,3,2,1,0:T(8,128)(2,1)S(1)}, bf16[2,4,2,128,128]{4,3,2,1,0:T(8,128)(2,1)S(1)}, u32[]{:S(2)}, u32[]{:S(2)}) collective-permute-start(bf16[2,4,2,128,128]{4,3,2,1,0:T(8,128)(2,1)S(1)} %collective-permute-done.2.refs_2_.refs_7_), channel_id=1, source_target_pairs={{0,4},{4,6},{6,2},{2,0},{1,5},{5,7},{7,3},{3,1},{8,12},{12,14},{14... | collective-permute-start | bytes 1572872 | tf_op jit(solution)/shard_map/ppermute | solution.py:544
  18.0 1.5 %collective-permute-start.5 = (bf16[2,4,2,128,128]{4,3,2,1,0:T(8,128)(2,1)S(1)}, bf16[2,4,2,128,128]{4,3,2,1,0:T(8,128)(2,1)S(1)}, u32[]{:S(2)}, u32[]{:S(2)}) collective-permute-start(bf16[2,4,2,128,128]{4,3,2,1,0:T(8,128)(2,1)S(1)} %collective-permute-done.2.refs_2_.refs_7_), channel_id=1, source_target_pairs={{0,16},{8,24},{16,0},{24,8},{1,17},{9,25},{17,1},{25,9},{2,18},{10... | collective-permute-start | bytes 1572872 | tf_op jit(solution)/shard_map/ppermute | solution.py:544
  19.5 0.5 collective-permute-start.3
  20.0 9.8 %shard_map.115 = (f32[4,4,512,128]{3,2,1,0:T(8,128)S(1)}, f32[4,4,512,128]{3,2,1,0:T(8,128)S(1)}, f32[4,4,512,128]{3,2,1,0:T(8,128)S(1)}) custom-call(s32[4]{0:T(128)S(1)} %compare_convert_fusion.needed_ref, bf16[1,256,32,128]{3,2,1,0:T(8,128)(2,1)} %refs_0_.3, bf16[2,4,2,128,128]{4,3,2,1,0:T(8,128)(2,1)S(1)} %shard_map.113.refs_1_.refs_6_, ...), custom_call_target="tpu_custom_call" | custom-call | flops 8589934592 | bytes 12000000 | tf_op jit(solution)/shard_map/pallas_call | solution.py:200
  29.9 1.9 %copy-done.10 = f32[4,4,512,128]{3,2,1,0:T(8,128)} copy-done((f32[4,4,512,128]{3,2,1,0:T(8,128)}, f32[4,4,512,128]{3,2,1,0:T(8,128)S(1)}, u32[]{:S(2)}) %copy-start.10) | copy-done | bytes 4194328
  31.8 2.0 %copy-done.12 = f32[4,4,512,128]{3,2,1,0:T(8,128)} copy-done((f32[4,4,512,128]{3,2,1,0:T(8,128)}, f32[4,4,512,128]{3,2,1,0:T(8,128)S(1)}, u32[]{:S(2)}) %copy-start.12) | copy-done | bytes 4194328
  33.9 2.0 %copy-done.14 = f32[4,4,512,128]{3,2,1,0:T(8,128)} copy-done((f32[4,4,512,128]{3,2,1,0:T(8,128)}, f32[4,4,512,128]{3,2,1,0:T(8,128)S(1)}, u32[]{:S(2)}) %copy-start.14) | copy-done | bytes 4194328
  35.9 0.8 copy-done.2
  36.7 0.0 collective-permute-done.6.refs_1_.refs_8_
  36.7 0.0 collective-permute-done.5.refs_15_
  36.7 0.0 collective-permute-done.4.refs_11_
  36.7 0.8 copy-done
  37.5 0.0 collective-permute-start.10
  37.5 0.5 collective-permute-start.9
  38.0 0.0 collective-permute-start.8
  38.0 0.5 collective-permute-start.7
  38.6 0.1 copy.17
  38.7 0.1 broadcast_in_dim.15
  38.8 0.1 copy.16
  38.9 0.1 reshape.39.refs_0_
  39.0 0.1 select_reduce_fusion.refs_1_
  39.1 6.5 %shard_map.116 = (f32[16,128,128]{2,1,0:T(8,128)S(1)}, f32[16,8,128]{2,1,0:T(8,128)S(1)}) custom-call(s32[32]{0:T(128)S(1)} %copy-done.9, s32[2]{0:T(128)S(1)} %pad_add_fusion.meta_ref.refs_2_, bf16[32,128,128]{2,1,0:T(8,128)(2,1)} %bitcast.12, bf16[32,16,128]{2,1,0:T(8,128)(2,1)} %bitcast.20, bf16[32,16,128]{2,1,0:T(8,128)(2,1)} %bitcast.22, ...), custom_call_target="tpu_custom_call" | custom-call | flops 2147483648 | bytes 7000000 | tf_op jit(solution)/shard_map/pallas_call | solution.py:293
  45.7 5.8 %collective-permute-done.10.refs_2_.refs_9_ = bf16[2,4,2,128,128]{4,3,2,1,0:T(8,128)(2,1)} collective-permute-done((bf16[2,4,2,128,128]{4,3,2,1,0:T(8,128)(2,1)S(1)}, bf16[2,4,2,128,128]{4,3,2,1,0:T(8,128)(2,1)}, u32[]{:S(2)}, u32[]{:S(2)}) %collective-permute-start.10) | collective-permute-done | bytes 524320 | tf_op jit(solution)/shard_map/ppermute | solution.py:544
  51.4 0.0 copy-start.5
  51.5 0.6 collective-permute-start.13
  52.1 0.5 collective-permute-start.11
  52.6 2.2 %copy-done.15 = f32[4,4,512,128]{3,2,1,0:T(8,128)S(1)} copy-done((f32[4,4,512,128]{3,2,1,0:T(8,128)S(1)}, f32[4,4,512,128]{3,2,1,0:T(8,128)}, u32[]{:S(2)}) %copy-start.15) | copy-done | bytes 4194328
  54.8 14.3 %shard_map.117 = bf16[1,256,32,128]{3,2,1,0:T(8,128)(2,1)} custom-call(s32[4]{0:T(128)S(1)} %compare_convert_fusion.needed_ref, bf16[1,256,32,128]{3,2,1,0:T(8,128)(2,1)} %refs_0_.3, bf16[2,4,2,128,128]{4,3,2,1,0:T(8,128)(2,1)S(1)} %collective-permute-done.6.refs_1_.refs_8_, bf16[2,4,2,128,128]{4,3,2,1,0:T(8,128)(2,1)} %collective-permute-done.10.refs_2_.refs_9_, ...), custom_call_target="tpu_custom_call" | custom-call | flops 8589934592 | bytes 12000000 | tf_op jit(solution)/shard_map/pallas_call | solution.py:200
  69.1 0.1 collective-permute-start.14
  69.2 1.9 %collective-permute-done.14.refs_21_ = bf16[2,4,2,128,128]{4,3,2,1,0:T(8,128)(2,1)S(1)} collective-permute-done((bf16[2,4,2,128,128]{4,3,2,1,0:T(8,128)(2,1)S(1)}, bf16[2,4,2,128,128]{4,3,2,1,0:T(8,128)(2,1)S(1)}, u32[]{:S(2)}, u32[]{:S(2)}) %collective-permute-start.14) | collective-permute-done | bytes 524320 | tf_op jit(solution)/shard_map/ppermute | solution.py:544
  71.1 8.1 %shard_map.119 = bf16[16,128,128]{2,1,0:T(8,128)(2,1)S(1)} custom-call(s32[128]{0:T(128)S(1)} %reshape.39.refs_0_, s32[16]{0:T(128)S(1)} %select_reduce_fusion.refs_1_, s32[2]{0:T(128)S(1)} %pad_add_fusion.meta_ref.refs_2_, bf16[32,128,128]{2,1,0:T(8,128)(2,1)} %bitcast.13, f32[16,128,128]{2,1,0:T(8,128)S(1)} %copy-done.5, ...), custom_call_target="tpu_custom_call" | custom-call | flops 2147483648 | bytes 8000000 | tf_op jit(solution)/shard_map/pallas_call | solution.py:401
  79.3 1.6 %collective-permute-start.15 = (bf16[16,128,128]{2,1,0:T(8,128)(2,1)S(1)}, bf16[16,128,128]{2,1,0:T(8,128)(2,1)S(1)}, u32[]{:S(2)}, u32[]{:S(2)}) collective-permute-start(bf16[16,128,128]{2,1,0:T(8,128)(2,1)S(1)} %shard_map.119), channel_id=1, source_target_pairs={{0,1},{1,0},{2,3},{3,2},{4,5},{5,4},{6,7},{7,6},{8,9},{9,8},{10,11... | collective-permute-start | bytes 1572872 | tf_op jit(solution)/shard_map/ppermute | solution.py:574
  80.9 8.2 %shard_map.118.refs_0_ = bf16[16,128,128]{2,1,0:T(8,128)(2,1)S(1)} custom-call(s32[128]{0:T(128)S(1)} %reshape.39.refs_0_, s32[16]{0:T(128)S(1)} %select_reduce_fusion.refs_1_, s32[2]{0:T(128)S(1)} %pad_add_fusion.meta_ref.refs_2_, bf16[32,128,128]{2,1,0:T(8,128)(2,1)} %bitcast.14, f32[16,128,128]{2,1,0:T(8,128)S(1)} %get-tuple-element.54.refs_4_, ...), custom_call_target="tpu_custom_call" | custom-call | flops 2147483648 | bytes 8000000 | tf_op jit(solution)/shard_map/pallas_call | solution.py:401
  89.0 4.3 %collective-permute-done.15.refs_1_ = bf16[16,128,128]{2,1,0:T(8,128)(2,1)S(1)} collective-permute-done((bf16[16,128,128]{2,1,0:T(8,128)(2,1)S(1)}, bf16[16,128,128]{2,1,0:T(8,128)(2,1)S(1)}, u32[]{:S(2)}, u32[]{:S(2)}) %collective-permute-start.15) | collective-permute-done | bytes 524320 | tf_op jit(solution)/shard_map/ppermute | solution.py:574
  93.3 1.8 %shard_map.120 = bf16[16,4,8192]{2,1,0:T(4,128)(2,1)} custom-call(s32[2]{0:T(128)S(1)} %pad_add_fusion.meta_ref.refs_2_, bf16[16,128,128]{2,1,0:T(8,128)(2,1)S(1)} %shard_map.118.refs_0_, bf16[16,128,128]{2,1,0:T(8,128)(2,1)S(1)} %collective-permute-done.15.refs_1_), custom_call_target="tpu_custom_call" | custom-call | bytes 2000000 | tf_op jit(solution)/shard_map/pallas_call | solution.py:459
  (34 shorter events, 0.1 us)
Async XLA Ops:
  0.6 1.0 %copy-start.6 = (bf16[1,256,4,128]{3,2,1,0:T(4,128)(2,1)S(1)}, bf16[1,256,4,128]{3,2,1,0:T(4,128)(2,1)}, u32[]{:S(2)}) copy-start(bf16[1,256,4,128]{3,2,1,0:T(4,128)(2,1)} %param.11) | copy-start | bytes 786436
  1.6 0.9 copy-start.7
  3.0 13.7 %collective-permute-start.2 = (bf16[2,4,2,128,128]{4,3,2,1,0:T(8,128)(2,1)S(1)}, bf16[2,4,2,128,128]{4,3,2,1,0:T(8,128)(2,1)S(1)}, u32[]{:S(2)}, u32[]{:S(2)}) collective-permute-start(bf16[2,4,2,128,128]{4,3,2,1,0:T(8,128)(2,1)S(1)} %shard_map.113.refs_1_.refs_6_), channel_id=1, source_target_pairs={{0,4},{4,6},{6,2},{2,0},{1,5},{5,7},{7,3},{3,1},{8,12},{12,14},{14... | collective-permute-start | bytes 1572872 | tf_op jit(solution)/shard_map/ppermute | solution.py:544
  3.4 13.4 %collective-permute-start.1 = (bf16[2,4,2,128,128]{4,3,2,1,0:T(8,128)(2,1)S(1)}, bf16[2,4,2,128,128]{4,3,2,1,0:T(8,128)(2,1)S(1)}, u32[]{:S(2)}, u32[]{:S(2)}) collective-permute-start(bf16[2,4,2,128,128]{4,3,2,1,0:T(8,128)(2,1)S(1)} %shard_map.113.refs_1_.refs_6_), channel_id=1, source_target_pairs={{0,16},{8,24},{16,0},{24,8},{1,17},{9,25},{17,1},{25,9},{2,18},{10... | collective-permute-start | bytes 1572872 | tf_op jit(solution)/shard_map/ppermute | solution.py:544
  4.9 11.9 %collective-permute-start = (bf16[2,4,2,128,128]{4,3,2,1,0:T(8,128)(2,1)S(1)}, bf16[2,4,2,128,128]{4,3,2,1,0:T(8,128)(2,1)S(1)}, u32[]{:S(2)}, u32[]{:S(2)}) collective-permute-start(bf16[2,4,2,128,128]{4,3,2,1,0:T(8,128)(2,1)S(1)} %shard_map.113.refs_1_.refs_6_), channel_id=1, source_target_pairs={{0,8},{8,0},{16,24},{24,16},{1,9},{9,1},{17,25},{25,17},{2,10},{10... | collective-permute-start | bytes 1572872 | tf_op jit(solution)/shard_map/ppermute | solution.py:544
  5.0 0.7 copy-start.8
  11.9 1.0 %copy-start.4 = (f32[16,128,128]{2,1,0:T(8,128)}, f32[16,128,128]{2,1,0:T(8,128)S(1)}, u32[]{:S(2)}) copy-start(f32[16,128,128]{2,1,0:T(8,128)S(1)} %get-tuple-element.64.refs_4_) | copy-start | bytes 3145732
  16.8 21.7 %copy-start.16 = (s32[32,4]{0,1:T(4,128)S(1)}, s32[32,4]{0,1:T(4,128)}, u32[]{:S(2)}) copy-start(s32[32,4]{0,1:T(4,128)} %param.19) | copy-start | bytes 1540
  16.8 22.3 %copy-start.9 = (s32[32]{0:T(128)S(1)}, s32[32]{0:T(128)}, u32[]{:S(2)}) copy-start(s32[32]{0:T(128)} %len_ref.3) | copy-start | bytes 388
  16.8 19.9 %collective-permute-start.6 = (bf16[2,4,2,128,128]{4,3,2,1,0:T(8,128)(2,1)S(1)}, bf16[2,4,2,128,128]{4,3,2,1,0:T(8,128)(2,1)S(1)}, u32[]{:S(2)}, u32[]{:S(2)}) collective-permute-start(bf16[2,4,2,128,128]{4,3,2,1,0:T(8,128)(2,1)S(1)} %collective-permute-done.2.refs_2_.refs_7_), channel_id=1, source_target_pairs={{0,4},{4,6},{6,2},{2,0},{1,5},{5,7},{7,3},{3,1},{8,12},{12,14},{14... | collective-permute-start | bytes 1572872 | tf_op jit(solution)/shard_map/ppermute | solution.py:544
  18.0 18.7 %collective-permute-start.5 = (bf16[2,4,2,128,128]{4,3,2,1,0:T(8,128)(2,1)S(1)}, bf16[2,4,2,128,128]{4,3,2,1,0:T(8,128)(2,1)S(1)}, u32[]{:S(2)}, u32[]{:S(2)}) collective-permute-start(bf16[2,4,2,128,128]{4,3,2,1,0:T(8,128)(2,1)S(1)} %collective-permute-done.2.refs_2_.refs_7_), channel_id=1, source_target_pairs={{0,16},{8,24},{16,0},{24,8},{1,17},{9,25},{17,1},{25,9},{2,18},{10... | collective-permute-start | bytes 1572872 | tf_op jit(solution)/shard_map/ppermute | solution.py:544
  19.5 17.2 %collective-permute-start.4 = (bf16[2,4,2,128,128]{4,3,2,1,0:T(8,128)(2,1)S(1)}, bf16[2,4,2,128,128]{4,3,2,1,0:T(8,128)(2,1)S(1)}, u32[]{:S(2)}, u32[]{:S(2)}) collective-permute-start(bf16[2,4,2,128,128]{4,3,2,1,0:T(8,128)(2,1)S(1)} %collective-permute-done.2.refs_2_.refs_7_), channel_id=1, source_target_pairs={{0,8},{8,0},{16,24},{24,16},{1,9},{9,1},{17,25},{25,17},{2,10},{10... | collective-permute-start | bytes 1572872 | tf_op jit(solution)/shard_map/ppermute | solution.py:544
  19.5 16.3 %collective-permute-start.3 = (bf16[2,4,2,128,128]{4,3,2,1,0:T(8,128)(2,1)S(1)}, bf16[2,4,2,128,128]{4,3,2,1,0:T(8,128)(2,1)S(1)}, u32[]{:S(2)}, u32[]{:S(2)}) collective-permute-start(bf16[2,4,2,128,128]{4,3,2,1,0:T(8,128)(2,1)S(1)} %collective-permute-done.1.refs_14_), channel_id=1, source_target_pairs={{0,8},{8,0},{16,24},{24,16},{1,9},{9,1},{17,25},{25,17},{2,10},{10... | collective-permute-start | bytes 1572872 | tf_op jit(solution)/shard_map/ppermute | solution.py:544
  29.9 2.0 %copy-start.10 = (f32[4,4,512,128]{3,2,1,0:T(8,128)}, f32[4,4,512,128]{3,2,1,0:T(8,128)S(1)}, u32[]{:S(2)}) copy-start(f32[4,4,512,128]{3,2,1,0:T(8,128)S(1)} %get-tuple-element.47.refs_3_) | copy-start | bytes 12582916
  31.8 2.0 %copy-start.12 = (f32[4,4,512,128]{3,2,1,0:T(8,128)}, f32[4,4,512,128]{3,2,1,0:T(8,128)S(1)}, u32[]{:S(2)}) copy-start(f32[4,4,512,128]{3,2,1,0:T(8,128)S(1)} %get-tuple-element.48.refs_4_) | copy-start | bytes 12582916
  33.9 2.0 %copy-start.14 = (f32[4,4,512,128]{3,2,1,0:T(8,128)}, f32[4,4,512,128]{3,2,1,0:T(8,128)S(1)}, u32[]{:S(2)}) copy-start(f32[4,4,512,128]{3,2,1,0:T(8,128)S(1)} %get-tuple-element.49.refs_5_) | copy-start | bytes 12582916
  35.9 0.8 copy-start.2
  36.7 0.8 copy-start
  37.5 13.9 %collective-permute-start.10 = (bf16[2,4,2,128,128]{4,3,2,1,0:T(8,128)(2,1)S(1)}, bf16[2,4,2,128,128]{4,3,2,1,0:T(8,128)(2,1)}, u32[]{:S(2)}, u32[]{:S(2)}) collective-permute-start(bf16[2,4,2,128,128]{4,3,2,1,0:T(8,128)(2,1)S(1)} %collective-permute-done.6.refs_1_.refs_8_), channel_id=1, source_target_pairs={{0,4},{4,6},{6,2},{2,0},{1,5},{5,7},{7,3},{3,1},{8,12},{12,14},{14... | collective-permute-start | bytes 1572872 | tf_op jit(solution)/shard_map/ppermute | solution.py:544
  37.5 13.9 %collective-permute-start.9 = (bf16[2,4,2,128,128]{4,3,2,1,0:T(8,128)(2,1)S(1)}, bf16[2,4,2,128,128]{4,3,2,1,0:T(8,128)(2,1)}, u32[]{:S(2)}, u32[]{:S(2)}) collective-permute-start(bf16[2,4,2,128,128]{4,3,2,1,0:T(8,128)(2,1)S(1)} %collective-permute-done.6.refs_1_.refs_8_), channel_id=1, source_target_pairs={{0,16},{8,24},{16,0},{24,8},{1,17},{9,25},{17,1},{25,9},{2,18},{10... | collective-permute-start | bytes 1572872 | tf_op jit(solution)/shard_map/ppermute | solution.py:544
  38.0 13.4 %collective-permute-start.8 = (bf16[2,4,2,128,128]{4,3,2,1,0:T(8,128)(2,1)S(1)}, bf16[2,4,2,128,128]{4,3,2,1,0:T(8,128)(2,1)}, u32[]{:S(2)}, u32[]{:S(2)}) collective-permute-start(bf16[2,4,2,128,128]{4,3,2,1,0:T(8,128)(2,1)S(1)} %collective-permute-done.6.refs_1_.refs_8_), channel_id=1, source_target_pairs={{0,8},{8,0},{16,24},{24,16},{1,9},{9,1},{17,25},{25,17},{2,10},{10... | collective-permute-start | bytes 1572872 | tf_op jit(solution)/shard_map/ppermute | solution.py:544
  38.0 7.6 %collective-permute-start.7 = (bf16[2,4,2,128,128]{4,3,2,1,0:T(8,128)(2,1)S(1)}, bf16[2,4,2,128,128]{4,3,2,1,0:T(8,128)(2,1)}, u32[]{:S(2)}, u32[]{:S(2)}) collective-permute-start(bf16[2,4,2,128,128]{4,3,2,1,0:T(8,128)(2,1)S(1)} %collective-permute-done.5.refs_15_), channel_id=1, source_target_pairs={{0,8},{8,0},{16,24},{24,16},{1,9},{9,1},{17,25},{25,17},{2,10},{10... | collective-permute-start | bytes 1572872 | tf_op jit(solution)/shard_map/ppermute | solution.py:544
  39.1 13.5 %copy-start.11 = (f32[4,4,512,128]{3,2,1,0:T(8,128)S(1)}, f32[4,4,512,128]{3,2,1,0:T(8,128)}, u32[]{:S(2)}) copy-start(f32[4,4,512,128]{3,2,1,0:T(8,128)} %copy-done.10) | copy-start | bytes 12582916
  39.1 13.5 %copy-start.13 = (f32[4,4,512,128]{3,2,1,0:T(8,128)S(1)}, f32[4,4,512,128]{3,2,1,0:T(8,128)}, u32[]{:S(2)}) copy-start(f32[4,4,512,128]{3,2,1,0:T(8,128)} %copy-done.12) | copy-start | bytes 12582916
  51.4 19.7 %copy-start.1 = (bf16[2,4,2,128,128]{4,3,2,1,0:T(8,128)(2,1)S(1)}, bf16[2,4,2,128,128]{4,3,2,1,0:T(8,128)(2,1)}, u32[]{:S(2)}) copy-start(bf16[2,4,2,128,128]{4,3,2,1,0:T(8,128)(2,1)} %copy-done) | copy-start | bytes 1572868
  51.4 19.7 %copy-start.3 = (bf16[2,4,2,128,128]{4,3,2,1,0:T(8,128)(2,1)S(1)}, bf16[2,4,2,128,128]{4,3,2,1,0:T(8,128)(2,1)}, u32[]{:S(2)}) copy-start(bf16[2,4,2,128,128]{4,3,2,1,0:T(8,128)(2,1)} %copy-done.2) | copy-start | bytes 1572868
  51.4 19.7 %copy-start.5 = (f32[16,128,128]{2,1,0:T(8,128)S(1)}, f32[16,128,128]{2,1,0:T(8,128)}, u32[]{:S(2)}) copy-start(f32[16,128,128]{2,1,0:T(8,128)} %copy-done.4) | copy-start | bytes 3145732
  51.5 17.7 %collective-permute-start.13 = (bf16[2,4,2,128,128]{4,3,2,1,0:T(8,128)(2,1)}, bf16[2,4,2,128,128]{4,3,2,1,0:T(8,128)(2,1)S(1)}, u32[]{:S(2)}, u32[]{:S(2)}) collective-permute-start(bf16[2,4,2,128,128]{4,3,2,1,0:T(8,128)(2,1)} %collective-permute-done.10.refs_2_.refs_9_), channel_id=1, source_target_pairs={{0,16},{8,24},{16,0},{24,8},{1,17},{9,25},{17,1},{25,9},{2,18},{10... | collective-permute-start | bytes 1572872 | tf_op jit(solution)/shard_map/ppermute | solution.py:544
  52.1 17.1 %collective-permute-start.12 = (bf16[2,4,2,128,128]{4,3,2,1,0:T(8,128)(2,1)}, bf16[2,4,2,128,128]{4,3,2,1,0:T(8,128)(2,1)S(1)}, u32[]{:S(2)}, u32[]{:S(2)}) collective-permute-start(bf16[2,4,2,128,128]{4,3,2,1,0:T(8,128)(2,1)} %collective-permute-done.10.refs_2_.refs_9_), channel_id=1, source_target_pairs={{0,8},{8,0},{16,24},{24,16},{1,9},{9,1},{17,25},{25,17},{2,10},{10... | collective-permute-start | bytes 1572872 | tf_op jit(solution)/shard_map/ppermute | solution.py:544
  52.1 17.0 %collective-permute-start.11 = (bf16[2,4,2,128,128]{4,3,2,1,0:T(8,128)(2,1)}, bf16[2,4,2,128,128]{4,3,2,1,0:T(8,128)(2,1)S(1)}, u32[]{:S(2)}, u32[]{:S(2)}) collective-permute-start(bf16[2,4,2,128,128]{4,3,2,1,0:T(8,128)(2,1)} %collective-permute-done.9.refs_16_), channel_id=1, source_target_pairs={{0,8},{8,0},{16,24},{24,16},{1,9},{9,1},{17,25},{25,17},{2,10},{10... | collective-permute-start | bytes 1572872 | tf_op jit(solution)/shard_map/ppermute | solution.py:544
  52.6 2.2 %copy-start.15 = (f32[4,4,512,128]{3,2,1,0:T(8,128)S(1)}, f32[4,4,512,128]{3,2,1,0:T(8,128)}, u32[]{:S(2)}) copy-start(f32[4,4,512,128]{3,2,1,0:T(8,128)} %copy-done.14) | copy-start | bytes 12582916
  69.1 2.0 %collective-permute-start.14 = (bf16[2,4,2,128,128]{4,3,2,1,0:T(8,128)(2,1)S(1)}, bf16[2,4,2,128,128]{4,3,2,1,0:T(8,128)(2,1)S(1)}, u32[]{:S(2)}, u32[]{:S(2)}) collective-permute-start(bf16[2,4,2,128,128]{4,3,2,1,0:T(8,128)(2,1)S(1)} %collective-permute-done.13.refs_17_), channel_id=1, source_target_pairs={{0,8},{8,0},{16,24},{24,16},{1,9},{9,1},{17,25},{25,17},{2,10},{10... | collective-permute-start | bytes 1572872 | tf_op jit(solution)/shard_map/ppermute | solution.py:544
  79.3 14.0 %collective-permute-start.15 = (bf16[16,128,128]{2,1,0:T(8,128)(2,1)S(1)}, bf16[16,128,128]{2,1,0:T(8,128)(2,1)S(1)}, u32[]{:S(2)}, u32[]{:S(2)}) collective-permute-start(bf16[16,128,128]{2,1,0:T(8,128)(2,1)S(1)} %shard_map.119), channel_id=1, source_target_pairs={{0,1},{1,0},{2,3},{3,2},{4,5},{5,4},{6,7},{7,6},{8,9},{9,8},{10,11... | collective-permute-start | bytes 1572872 | tf_op jit(solution)/shard_map/ppermute | solution.py:574

commit v11 on v10

--- a/solution.py
+++ b/solution.py
@@ -11,7 +11,7 @@
 PAGE = 128
 LOG2E = 1.4426950408889634
 NEG = -1e30
-VMEM_LIMIT = 32 * 1024 * 1024
+VMEM_LIMIT = 16 * 1024 * 1024
 
 
 def nt(a, b):
@@ -57,10 +57,11 @@
     _, tokens, heads, width = k.shape
     return pl.pallas_call(
         functools.partial(split_kernel, heads, tokens),
-        out_shape=jax.ShapeDtypeStruct((tokens // PAGE, heads, 2, PAGE, width), jnp.bfloat16),
+        out_specs=pl.BlockSpec(memory_space=pltpu.VMEM),
+        out_shape=pltpu.VMEM((tokens // PAGE, heads, 2, PAGE, width), jnp.bfloat16),
         compiler_params=params(),
         cost_estimate=pl.CostEstimate(flops=10**8, bytes_accessed=2 * 10**6, transcendentals=0),
-    )(k.reshape(tokens * heads, width), v.reshape(tokens * heads, width))
+    )(*in_hbm(k.reshape(tokens * heads, width), v.reshape(tokens * heads, width)))
 
 
 def prefill_kernel(own, count, slots, group, tokens, scale, needed_ref, *refs):
@@ -310,14 +311,17 @@
     )(lens, meta, *in_hbm(q, dk, dv, ck, cv))
 
 
-def decode_kernel(slots, extra, steps, target, targets, heads, group, scale, *refs):
+def decode_kernel(
+    slots, extra, steps, target, targets, part, parts, heads, group, scale, *refs
+):
     slot_ref, pick_ref, meta_ref = refs[:3]
     q_ref, acc_ref, ml_ref = refs[3:6]
     blocks = refs[6 : 6 + slots]
     out_ref, buf, sems = refs[6 + slots :]
     block, lanes, width = q_ref.shape
     i = pl.program_id(0)
-    first = (lax.rem(meta_ref[1] + target, targets) * pl.num_programs(0) + i) * block
+    kept = (part * pl.num_programs(0) + i) * block
+    first = lax.rem(meta_ref[1] + target, targets) * (parts * pl.num_programs(0) * block) + kept
 
     def copies():
         for s in range(slots):
@@ -356,18 +360,17 @@
             scores.append((r, places, s))
         weights = []
         for r, places, s in scores:
-            old = ml_ref[i * block + r, 0:1]
+            old = ml_ref[kept + r, 0:1]
             m = jnp.max(functools.reduce(jnp.maximum, s), axis=0, keepdims=True)
             m = jnp.maximum(m, old)
             p = [jnp.exp2((a - m) * scale) for a in s]
             shrink = jnp.exp2((old - m) * scale)
             l = jnp.sum(functools.reduce(jnp.add, p), axis=0, keepdims=True)
-            l = ml_ref[i * block + r, 4:5] * shrink + l
+            l = ml_ref[kept + r, 4:5] * shrink + l
             p = jnp.concatenate([a.astype(jnp.bfloat16) for a in p], axis=0)
             weights.append((r, places, p, shrink, l))
         results = []
         for r, places, p, shrink, l in weights:
-            part = None
             values = [
                 jnp.concatenate([buf[place, h, 1] for place in places], axis=1)
                 for h in range(heads)
@@ -376,8 +379,8 @@
                 pair = nn(jnp.concatenate(values[h : h + both], axis=0), p)
                 for w in range(both):
                     mine = pair[w * width : (w + 1) * width]
-                    part = mine if h + w == 0 else jnp.where(lane_head == h + w, mine, part)
-            results.append((r, ((acc_ref[i * block + r] * shrink + part) / l).astype(jnp.bfloat16)))
+                    found = mine if h + w == 0 else jnp.where(lane_head == h + w, mine, found)
+            results.append((r, ((acc_ref[kept + r] * shrink + found) / l).astype(jnp.bfloat16)))
         for r, result in results:
             out_ref[r] = nt(order, result).astype(jnp.bfloat16)
         return carry
@@ -385,15 +388,15 @@
     lax.fori_loop(0, block // unroll, body, 0)
 
 
-def decode(q, acc, ml, blocks, scalars, target, targets, extra, steps, heads, group):
+def decode(q, acc, ml, blocks, scalars, target, targets, part, parts, extra, steps, heads, group):
     requests, lanes, width = q.shape
-    per_target = requests // targets
-    block = math.gcd(16, per_target)
-    per_block = per_target // block
+    count = requests // targets // parts
+    block = math.gcd(16, count)
+    per_block = count // block
     slots = len(blocks)
 
     def here(i, slot, pick, meta):
-        return (lax.rem(meta[1] + target, targets) * per_block + i, 0, 0)
+        return ((lax.rem(meta[1] + target, targets) * parts + part) * per_block + i, 0, 0)
 
     in_specs = [pl.BlockSpec((block,) + q.shape[1:], here)]
     in_specs += [pl.BlockSpec(memory_space=pltpu.VMEM)] * 2
@@ -406,6 +409,8 @@
             steps,
             target,
             targets,
+            part,
+            parts,
             heads,
             group,
             LOG2E / math.sqrt(width),
@@ -420,54 +425,56 @@
                 pltpu.SemaphoreType.DMA((slots,)),
             ],
         ),
-        out_shape=jax.ShapeDtypeStruct((per_target, lanes, width), jnp.bfloat16),
+        out_shape=jax.ShapeDtypeStruct((count, lanes, width), jnp.bfloat16),
         compiler_params=params(),
         cost_estimate=pl.CostEstimate(
-            flops=per_target * lanes * extra * PAGE * width * 16,
-            bytes_accessed=8 * 10**6,
-            transcendentals=per_target * lanes * extra * PAGE,
+            flops=10**6, bytes_accessed=10**6, transcendentals=0
         ),
     )(*scalars, *in_hbm(q), acc, ml, *blocks)
 
 
-def join_kernel(targets, chunks, steps, meta_ref, *refs):
+def join_kernel(counts, steps, meta_ref, *refs):
     out_ref = refs[-1]
     k = pl.program_id(0)
     rows = refs[0].shape[1]
-    each = rows // steps
-    for s in range(targets):
+    targets = len(counts)
+    sources = iter(refs)
+    for s, count in enumerate(counts):
+        parts = [next(sources) for _ in range(count)]
+
         @pl.when(lax.rem(meta_ref[1] + (targets - s), targets) == k)
         def _():
-            for c in range(chunks):
-                source = refs[s * chunks + c]
+            for n, source in enumerate(parts):
 
                 def body(r, carry):
                     value = source[r]
-                    for g in range(each):
-                        out_ref[r, :, (c * each + g) * 128 : (c * each + g + 1) * 128] = value[
+                    for g in range(rows // steps):
+                        out_ref[n * source.shape[0] + r, :, g * 128 : (g + 1) * 128] = value[
                             g * steps : (g + 1) * steps
                         ]
                     return carry
 
-                lax.fori_loop(0, out_ref.shape[0], body, 0)
-
-
-def join(pieces, meta, steps, targets, chunks):
-    per_target, rows, width = pieces[0].shape
-    half = chunks * (rows // steps) * width
-    spec = pl.BlockSpec((per_target, rows, width), lambda k, *_: (0, 0, 0))
+                lax.fori_loop(0, source.shape[0], body, 0)
+
+
+def join(pieces, meta, steps):
+    flat = [a for parts in pieces for a in parts]
+    rows, width = flat[0].shape[1:]
+    targets = len(pieces)
+    per_target = sum(a.shape[0] for a in pieces[0])
+    half = rows // steps * width
     return pl.pallas_call(
-        functools.partial(join_kernel, targets, chunks, steps),
+        functools.partial(join_kernel, [len(parts) for parts in pieces], steps),
         grid_spec=pltpu.PrefetchScalarGridSpec(
             num_scalar_prefetch=1,
             grid=(targets,),
-            in_specs=[spec] * len(pieces),
+            in_specs=[pl.BlockSpec(a.shape, lambda k, *_: (0, 0, 0)) for a in flat],
             out_specs=pl.BlockSpec((per_target, steps, half), lambda k, *_: (0, 0, k)),
         ),
         out_shape=jax.ShapeDtypeStruct((per_target, steps, half * targets), jnp.bfloat16),
-        compiler_params=pltpu.CompilerParams(vmem_limit_bytes=16 * 1024 * 1024),
+        compiler_params=params(),
         cost_estimate=pl.CostEstimate(flops=0, bytes_accessed=2 * 10**6, transcendentals=0),
-    )(meta, *pieces)
+    )(meta, *flat)
 
 
 def ring_place(index, size):
@@ -568,12 +575,22 @@
     blocks = [gathered[r, s] for r in range(roles) for s in range(ring)]
     pieces = [None] * targets
     for s in reversed(range(targets)):
-        out = decode(raw[0], *cached[s], blocks, scalars, s, targets, extra, steps, heads, group)
-        if s:
-            shift = [(j, (j + s) % targets) for j in range(targets)]
-            out = lax.ppermute(out, "tp", shift)
-        pieces[s] = out
-    decode_out = join(pieces, scalars[2], steps, targets, 1)
+        parts = math.gcd(2, requests // targets) if s else 1
+        pieces[s] = []
+        if s == 0 and targets > 1:
+            sent = [p[0] for p in pieces[1:]]
+            cached[0], sent = lax.optimization_barrier((cached[0], sent))
+            for p, a in zip(pieces[1:], sent):
+                p[0] = a
+        for part in range(parts):
+            out = decode(
+                raw[0], *cached[s], blocks, scalars, s, targets, part, parts, extra, steps, heads, group
+            )
+            if s:
+                shift = [(j, (j + s) % targets) for j in range(targets)]
+                out = lax.ppermute(out, "tp", shift)
+            pieces[s].append(out)
+    decode_out = join(pieces, scalars[2], steps)
     return (prefill_out, decode_out)
 
 

time: 95.6 us -> 94.6 us (0.990)
  Pallas kernels: 55.5 us -> 59.3 us
  waiting for transfers between devices: 15.9 us -> 12.4 us
  local copies, waits for them, and re-layouts: 13.7 us -> 11.8 us
    ppermute x1 -> x2, waiting for transfers between devices: 4.26 us -> 0.77 us  [shards(): out = lax.ppermute(out, 'tp', shift)]
    pallas_call x2 -> x3, Pallas kernels: 16.3 us -> 19.1 us  [decode(): pl.pallas_call(functools.partial(decode_kernel, slots, extra, steps, targ...]
    unnamed x34 -> x30, local copies, waits for them, and re-layouts: 13.3 us -> 11.4 us
    pallas_call x2, Pallas kernels: 2.25 us -> 3.29 us  [the longest x1 1.77 us: join(): pl.pallas_call(functools.partial(join_kernel, [len(parts) for parts in pi...]
    ppermute x1 -> x2, starting transfers between devices: 1.58 us -> 2.16 us  [shards(): out = lax.ppermute(out, 'tp', shift)]
  transfers between devices with their start and end apart: 16 -> 17, of which waited for: 5 -> 5; matrix products, arithmetic and copies ran while one was open for 1% -> 1% of each run, Pallas kernels for 47% -> 54%
where the time goes in v11:
time: 94.6 us; the launch traced here: 94.1 us
  Pallas kernels  59.3 us (63%)
  waiting for transfers between devices  12.4 us (13%)
  local copies, waits for them, and re-layouts  11.8 us (12%)
  starting transfers between devices  9.48 us (10%)
    pallas_call x2, Pallas kernels, prefill(): pl.pallas_call(functools.partial(prefill_kernel, own, count, slots, group...  24.2 us
    pallas_call x3, Pallas kernels, decode(): pl.pallas_call(functools.partial(decode_kernel, slots, extra, steps, targ...  19.1 us
    pallas_call x2, Pallas kernels, cache_part(): pl.pallas_call(functools.partial(cache_kernel, steps, heads, group, targe...  12.8 us
    ppermute x15, waiting for transfers between devices, shards(): lax.ppermute(gathered[of], axis, pairs)  11.6 us
    unnamed x30, local copies, waits for them, and re-layouts  11.4 us
    ppermute x15, starting transfers between devices, shards(): lax.ppermute(gathered[of], axis, pairs)  7.32 us
    ppermute x2, starting transfers between devices, shards(): out = lax.ppermute(out, 'tp', shift)  2.16 us
  transfers between devices with their start and end apart: 17, of which 5 were waited for; matrix products, arithmetic and copies ran while one was open for 1% of the time, Pallas kernels for 54%

profile of v11, /device:TPU:24, one launch (start us, length us, event | category | flops | bytes accessed | tf_op | source)
XLA Modules:
  0.0 94.1 jit_solution(10114711676825845913)
XLA Ops:
  0.6 1.5 %shard_map.113.refs_1_.refs_6_ = bf16[2,4,2,128,128]{4,3,2,1,0:T(8,128)(2,1)S(1)} custom-call(bf16[1024,128]{1,0:T(8,128)(2,1)} %bitcast.22, bf16[1024,128]{1,0:T(8,128)(2,1)} %bitcast.23), custom_call_target="tpu_custom_call" | custom-call | flops 100000000 | bytes 2000000 | tf_op jit(solution)/shard_map/pallas_call | solution.py:58
  2.1 0.4 collective-permute-start.2
  2.5 1.5 %collective-permute-start.1 = (bf16[2,4,2,128,128]{4,3,2,1,0:T(8,128)(2,1)S(1)}, bf16[2,4,2,128,128]{4,3,2,1,0:T(8,128)(2,1)S(1)}, u32[]{:S(2)}, u32[]{:S(2)}) collective-permute-start(bf16[2,4,2,128,128]{4,3,2,1,0:T(8,128)(2,1)S(1)} %shard_map.113.refs_1_.refs_6_), channel_id=1, source_target_pairs={{0,16},{8,24},{16,0},{24,8},{1,17},{9,25},{17,1},{25,9},{2,18},{10... | collective-permute-start | bytes 1572872 | tf_op jit(solution)/shard_map/ppermute | solution.py:551
  4.0 0.0 collective-permute-start
  4.0 0.1 pad_add_fusion.meta_ref.refs_2_
  4.1 0.7 copy-done.6
  4.8 6.2 %shard_map.114 = (f32[16,128,128]{2,1,0:T(8,128)S(1)}, f32[16,8,128]{2,1,0:T(8,128)S(1)}) custom-call(s32[32]{0:T(128)S(1)} %copy-done.6, s32[2]{0:T(128)S(1)} %pad_add_fusion.meta_ref.refs_2_, bf16[32,128,128]{2,1,0:T(8,128)(2,1)} %bitcast.9, bf16[32,16,128]{2,1,0:T(8,128)(2,1)} %bitcast.18, bf16[32,16,128]{2,1,0:T(8,128)(2,1)} %bitcast.20, ...), custom_call_target="tpu_custom_call" | custom-call | flops 2147483648 | bytes 7000000 | tf_op jit(solution)/shard_map/pallas_call | solution.py:294
  11.0 0.0 copy-start.4
  11.0 1.0 %copy-done.4 = f32[16,128,128]{2,1,0:T(8,128)} copy-done((f32[16,128,128]{2,1,0:T(8,128)}, f32[16,128,128]{2,1,0:T(8,128)S(1)}, u32[]{:S(2)}) %copy-start.4) | copy-done | bytes 1048600
  12.0 3.9 %collective-permute-done.2.refs_2_.refs_7_ = bf16[2,4,2,128,128]{4,3,2,1,0:T(8,128)(2,1)S(1)} collective-permute-done((bf16[2,4,2,128,128]{4,3,2,1,0:T(8,128)(2,1)S(1)}, bf16[2,4,2,128,128]{4,3,2,1,0:T(8,128)(2,1)S(1)}, u32[]{:S(2)}, u32[]{:S(2)}) %collective-permute-start.2) | collective-permute-done | bytes 524320 | tf_op jit(solution)/shard_map/ppermute | solution.py:551
  15.9 0.1 collective-permute-done.1.refs_14_
  15.9 0.0 collective-permute-done.refs_10_
  15.9 1.2 %collective-permute-start.6 = (bf16[2,4,2,128,128]{4,3,2,1,0:T(8,128)(2,1)S(1)}, bf16[2,4,2,128,128]{4,3,2,1,0:T(8,128)(2,1)S(1)}, u32[]{:S(2)}, u32[]{:S(2)}) collective-permute-start(bf16[2,4,2,128,128]{4,3,2,1,0:T(8,128)(2,1)S(1)} %collective-permute-done.2.refs_2_.refs_7_), channel_id=1, source_target_pairs={{0,4},{4,6},{6,2},{2,0},{1,5},{5,7},{7,3},{3,1},{8,12},{12,14},{14... | collective-permute-start | bytes 1572872 | tf_op jit(solution)/shard_map/ppermute | solution.py:551
  17.2 1.5 %collective-permute-start.5 = (bf16[2,4,2,128,128]{4,3,2,1,0:T(8,128)(2,1)S(1)}, bf16[2,4,2,128,128]{4,3,2,1,0:T(8,128)(2,1)S(1)}, u32[]{:S(2)}, u32[]{:S(2)}) collective-permute-start(bf16[2,4,2,128,128]{4,3,2,1,0:T(8,128)(2,1)S(1)} %collective-permute-done.2.refs_2_.refs_7_), channel_id=1, source_target_pairs={{0,16},{8,24},{16,0},{24,8},{1,17},{9,25},{17,1},{25,9},{2,18},{10... | collective-permute-start | bytes 1572872 | tf_op jit(solution)/shard_map/ppermute | solution.py:551
  18.7 0.0 collective-permute-start.4
  18.7 0.5 collective-permute-start.3
  19.2 9.8 %shard_map.115 = (f32[4,4,512,128]{3,2,1,0:T(8,128)S(1)}, f32[4,4,512,128]{3,2,1,0:T(8,128)S(1)}, f32[4,4,512,128]{3,2,1,0:T(8,128)S(1)}) custom-call(s32[4]{0:T(128)S(1)} %compare_convert_fusion.needed_ref, bf16[1,256,32,128]{3,2,1,0:T(8,128)(2,1)} %refs_0_.3, bf16[2,4,2,128,128]{4,3,2,1,0:T(8,128)(2,1)S(1)} %shard_map.113.refs_1_.refs_6_, ...), custom_call_target="tpu_custom_call" | custom-call | flops 8589934592 | bytes 12000000 | tf_op jit(solution)/shard_map/pallas_call | solution.py:201
  29.0 1.9 %copy-done.8 = f32[4,4,512,128]{3,2,1,0:T(8,128)} copy-done((f32[4,4,512,128]{3,2,1,0:T(8,128)}, f32[4,4,512,128]{3,2,1,0:T(8,128)S(1)}, u32[]{:S(2)}) %copy-start.8) | copy-done | bytes 4194328
  31.0 2.0 %copy-done.10 = f32[4,4,512,128]{3,2,1,0:T(8,128)} copy-done((f32[4,4,512,128]{3,2,1,0:T(8,128)}, f32[4,4,512,128]{3,2,1,0:T(8,128)S(1)}, u32[]{:S(2)}) %copy-start.10) | copy-done | bytes 4194328
  33.0 2.0 %copy-done.12 = f32[4,4,512,128]{3,2,1,0:T(8,128)} copy-done((f32[4,4,512,128]{3,2,1,0:T(8,128)}, f32[4,4,512,128]{3,2,1,0:T(8,128)S(1)}, u32[]{:S(2)}) %copy-start.12) | copy-done | bytes 4194328
  35.0 0.0 collective-permute-done.3.refs_18_
  35.0 0.8 copy-done.2
  35.8 0.0 collective-permute-done.4.refs_11_
  35.8 0.8 copy-done
  36.6 0.0 collective-permute-start.10
  36.6 0.5 collective-permute-start.9
  37.2 0.5 collective-permute-start.7
  37.7 0.1 copy.17
  37.8 0.1 broadcast_in_dim.15
  37.9 0.1 copy.16
  38.0 0.1 reshape.39.refs_0_
  38.1 0.1 select_reduce_fusion.refs_1_
  38.2 6.5 %shard_map.116 = (f32[16,128,128]{2,1,0:T(8,128)S(1)}, f32[16,8,128]{2,1,0:T(8,128)S(1)}) custom-call(s32[32]{0:T(128)S(1)} %copy-done.7, s32[2]{0:T(128)S(1)} %pad_add_fusion.meta_ref.refs_2_, bf16[32,128,128]{2,1,0:T(8,128)(2,1)} %bitcast.10, bf16[32,16,128]{2,1,0:T(8,128)(2,1)} %bitcast.19, bf16[32,16,128]{2,1,0:T(8,128)(2,1)} %bitcast.21, ...), custom_call_target="tpu_custom_call" | custom-call | flops 2147483648 | bytes 7000000 | tf_op jit(solution)/shard_map/pallas_call | solution.py:294
  44.8 5.8 %collective-permute-done.10.refs_2_.refs_9_ = bf16[2,4,2,128,128]{4,3,2,1,0:T(8,128)(2,1)} collective-permute-done((bf16[2,4,2,128,128]{4,3,2,1,0:T(8,128)(2,1)S(1)}, bf16[2,4,2,128,128]{4,3,2,1,0:T(8,128)(2,1)}, u32[]{:S(2)}, u32[]{:S(2)}) %collective-permute-start.10) | collective-permute-done | bytes 524320 | tf_op jit(solution)/shard_map/ppermute | solution.py:551
  50.6 0.0 copy-start.5
  50.6 0.6 collective-permute-start.13
  51.2 0.5 collective-permute-start.11
  51.7 2.2 %copy-done.13 = f32[4,4,512,128]{3,2,1,0:T(8,128)S(1)} copy-done((f32[4,4,512,128]{3,2,1,0:T(8,128)S(1)}, f32[4,4,512,128]{3,2,1,0:T(8,128)}, u32[]{:S(2)}) %copy-start.13) | copy-done | bytes 4194328
  53.9 14.3 %shard_map.117 = bf16[1,256,32,128]{3,2,1,0:T(8,128)(2,1)} custom-call(s32[4]{0:T(128)S(1)} %compare_convert_fusion.needed_ref, bf16[1,256,32,128]{3,2,1,0:T(8,128)(2,1)} %refs_0_.3, bf16[2,4,2,128,128]{4,3,2,1,0:T(8,128)(2,1)S(1)} %collective-permute-done.6.refs_1_.refs_8_, bf16[2,4,2,128,128]{4,3,2,1,0:T(8,128)(2,1)} %collective-permute-done.10.refs_2_.refs_9_, ...), custom_call_target="tpu_custom_call" | custom-call | flops 8589934592 | bytes 12000000 | tf_op jit(solution)/shard_map/pallas_call | solution.py:201
  68.3 0.1 collective-permute-start.14
  68.4 1.9 %collective-permute-done.14.refs_21_ = bf16[2,4,2,128,128]{4,3,2,1,0:T(8,128)(2,1)S(1)} collective-permute-done((bf16[2,4,2,128,128]{4,3,2,1,0:T(8,128)(2,1)S(1)}, bf16[2,4,2,128,128]{4,3,2,1,0:T(8,128)(2,1)S(1)}, u32[]{:S(2)}, u32[]{:S(2)}) %collective-permute-start.14) | collective-permute-done | bytes 524320 | tf_op jit(solution)/shard_map/ppermute | solution.py:551
  70.3 5.5 %shard_map.118 = bf16[8,128,128]{2,1,0:T(8,128)(2,1)S(1)} custom-call(s32[128]{0:T(128)S(1)} %reshape.39.refs_0_, s32[16]{0:T(128)S(1)} %select_reduce_fusion.refs_1_, s32[2]{0:T(128)S(1)} %pad_add_fusion.meta_ref.refs_2_, bf16[32,128,128]{2,1,0:T(8,128)(2,1)} %bitcast.11, f32[16,128,128]{2,1,0:T(8,128)S(1)} %copy-done.5, ...), custom_call_target="tpu_custom_call" | custom-call | flops 1000000 | bytes 1000000 | tf_op jit(solution)/shard_map/pallas_call | solution.py:404
  75.8 1.6 %collective-permute-start.15 = (bf16[8,128,128]{2,1,0:T(8,128)(2,1)S(1)}, bf16[8,128,128]{2,1,0:T(8,128)(2,1)S(1)}, u32[]{:S(2)}, u32[]{:S(2)}) collective-permute-start(bf16[8,128,128]{2,1,0:T(8,128)(2,1)S(1)} %shard_map.118), channel_id=1, source_target_pairs={{0,1},{1,0},{2,3},{3,2},{4,5},{5,4},{6,7},{7,6},{8,9},{9,8},{10,11... | collective-permute-start | bytes 786440 | tf_op jit(solution)/shard_map/ppermute | solution.py:591
  77.3 5.5 %shard_map.120 = bf16[8,128,128]{2,1,0:T(8,128)(2,1)S(1)} custom-call(s32[128]{0:T(128)S(1)} %reshape.39.refs_0_, s32[16]{0:T(128)S(1)} %select_reduce_fusion.refs_1_, s32[2]{0:T(128)S(1)} %pad_add_fusion.meta_ref.refs_2_, bf16[32,128,128]{2,1,0:T(8,128)(2,1)} %bitcast.12, f32[16,128,128]{2,1,0:T(8,128)S(1)} %copy-done.5, ...), custom_call_target="tpu_custom_call" | custom-call | flops 1000000 | bytes 1000000 | tf_op jit(solution)/shard_map/pallas_call | solution.py:404
  82.8 0.6 collective-permute-start.16
  83.4 0.8 collective-permute-done.15.refs_1_
  84.2 8.2 %shard_map.119.refs_0_ = bf16[16,128,128]{2,1,0:T(8,128)(2,1)S(1)} custom-call(s32[128]{0:T(128)S(1)} %reshape.39.refs_0_, s32[16]{0:T(128)S(1)} %select_reduce_fusion.refs_1_, s32[2]{0:T(128)S(1)} %pad_add_fusion.meta_ref.refs_2_, bf16[32,128,128]{2,1,0:T(8,128)(2,1)} %bitcast.13, f32[16,128,128]{2,1,0:T(8,128)S(1)} %get-tuple-element.69.refs_4_, ...), custom_call_target="tpu_custom_call" | custom-call | flops 1000000 | bytes 1000000 | tf_op jit(solution)/shard_map/pallas_call | solution.py:404
  92.4 1.8 %shard_map.121 = bf16[16,4,8192]{2,1,0:T(4,128)(2,1)} custom-call(s32[2]{0:T(128)S(1)} %pad_add_fusion.meta_ref.refs_2_, bf16[16,128,128]{2,1,0:T(8,128)(2,1)S(1)} %shard_map.119.refs_0_, bf16[8,128,128]{2,1,0:T(8,128)(2,1)S(1)} %collective-permute-done.15.refs_1_, bf16[8,128,128]{2,1,0:T(8,128)(2,1)S(1)} %collective-permute-done.16.refs_2_), custom_call_target="tpu_custom_call" | custom-call | bytes 2000000 | tf_op jit(solution)/shard_map/pallas_call | solution.py:466
  (33 shorter events, 0.1 us)
Async XLA Ops:
  2.1 13.7 %collective-permute-start.2 = (bf16[2,4,2,128,128]{4,3,2,1,0:T(8,128)(2,1)S(1)}, bf16[2,4,2,128,128]{4,3,2,1,0:T(8,128)(2,1)S(1)}, u32[]{:S(2)}, u32[]{:S(2)}) collective-permute-start(bf16[2,4,2,128,128]{4,3,2,1,0:T(8,128)(2,1)S(1)} %shard_map.113.refs_1_.refs_6_), channel_id=1, source_target_pairs={{0,4},{4,6},{6,2},{2,0},{1,5},{5,7},{7,3},{3,1},{8,12},{12,14},{14... | collective-permute-start | bytes 1572872 | tf_op jit(solution)/shard_map/ppermute | solution.py:551
  2.5 13.4 %collective-permute-start.1 = (bf16[2,4,2,128,128]{4,3,2,1,0:T(8,128)(2,1)S(1)}, bf16[2,4,2,128,128]{4,3,2,1,0:T(8,128)(2,1)S(1)}, u32[]{:S(2)}, u32[]{:S(2)}) collective-permute-start(bf16[2,4,2,128,128]{4,3,2,1,0:T(8,128)(2,1)S(1)} %shard_map.113.refs_1_.refs_6_), channel_id=1, source_target_pairs={{0,16},{8,24},{16,0},{24,8},{1,17},{9,25},{17,1},{25,9},{2,18},{10... | collective-permute-start | bytes 1572872 | tf_op jit(solution)/shard_map/ppermute | solution.py:551
  4.0 11.9 %collective-permute-start = (bf16[2,4,2,128,128]{4,3,2,1,0:T(8,128)(2,1)S(1)}, bf16[2,4,2,128,128]{4,3,2,1,0:T(8,128)(2,1)S(1)}, u32[]{:S(2)}, u32[]{:S(2)}) collective-permute-start(bf16[2,4,2,128,128]{4,3,2,1,0:T(8,128)(2,1)S(1)} %shard_map.113.refs_1_.refs_6_), channel_id=1, source_target_pairs={{0,8},{8,0},{16,24},{24,16},{1,9},{9,1},{17,25},{25,17},{2,10},{10... | collective-permute-start | bytes 1572872 | tf_op jit(solution)/shard_map/ppermute | solution.py:551
  4.1 0.7 copy-start.6
  11.0 1.0 %copy-start.4 = (f32[16,128,128]{2,1,0:T(8,128)}, f32[16,128,128]{2,1,0:T(8,128)S(1)}, u32[]{:S(2)}) copy-start(f32[16,128,128]{2,1,0:T(8,128)S(1)} %get-tuple-element.59.refs_4_) | copy-start | bytes 3145732
  15.9 21.7 %copy-start.14 = (s32[32,4]{0,1:T(4,128)S(1)}, s32[32,4]{0,1:T(4,128)}, u32[]{:S(2)}) copy-start(s32[32,4]{0,1:T(4,128)} %param.19) | copy-start | bytes 1540
  15.9 22.3 %copy-start.7 = (s32[32]{0:T(128)S(1)}, s32[32]{0:T(128)}, u32[]{:S(2)}) copy-start(s32[32]{0:T(128)} %len_ref.3) | copy-start | bytes 388
  15.9 19.9 %collective-permute-start.6 = (bf16[2,4,2,128,128]{4,3,2,1,0:T(8,128)(2,1)S(1)}, bf16[2,4,2,128,128]{4,3,2,1,0:T(8,128)(2,1)S(1)}, u32[]{:S(2)}, u32[]{:S(2)}) collective-permute-start(bf16[2,4,2,128,128]{4,3,2,1,0:T(8,128)(2,1)S(1)} %collective-permute-done.2.refs_2_.refs_7_), channel_id=1, source_target_pairs={{0,4},{4,6},{6,2},{2,0},{1,5},{5,7},{7,3},{3,1},{8,12},{12,14},{14... | collective-permute-start | bytes 1572872 | tf_op jit(solution)/shard_map/ppermute | solution.py:551
  17.2 18.7 %collective-permute-start.5 = (bf16[2,4,2,128,128]{4,3,2,1,0:T(8,128)(2,1)S(1)}, bf16[2,4,2,128,128]{4,3,2,1,0:T(8,128)(2,1)S(1)}, u32[]{:S(2)}, u32[]{:S(2)}) collective-permute-start(bf16[2,4,2,128,128]{4,3,2,1,0:T(8,128)(2,1)S(1)} %collective-permute-done.2.refs_2_.refs_7_), channel_id=1, source_target_pairs={{0,16},{8,24},{16,0},{24,8},{1,17},{9,25},{17,1},{25,9},{2,18},{10... | collective-permute-start | bytes 1572872 | tf_op jit(solution)/shard_map/ppermute | solution.py:551
  18.7 17.2 %collective-permute-start.4 = (bf16[2,4,2,128,128]{4,3,2,1,0:T(8,128)(2,1)S(1)}, bf16[2,4,2,128,128]{4,3,2,1,0:T(8,128)(2,1)S(1)}, u32[]{:S(2)}, u32[]{:S(2)}) collective-permute-start(bf16[2,4,2,128,128]{4,3,2,1,0:T(8,128)(2,1)S(1)} %collective-permute-done.2.refs_2_.refs_7_), channel_id=1, source_target_pairs={{0,8},{8,0},{16,24},{24,16},{1,9},{9,1},{17,25},{25,17},{2,10},{10... | collective-permute-start | bytes 1572872 | tf_op jit(solution)/shard_map/ppermute | solution.py:551
  18.7 16.3 %collective-permute-start.3 = (bf16[2,4,2,128,128]{4,3,2,1,0:T(8,128)(2,1)S(1)}, bf16[2,4,2,128,128]{4,3,2,1,0:T(8,128)(2,1)S(1)}, u32[]{:S(2)}, u32[]{:S(2)}) collective-permute-start(bf16[2,4,2,128,128]{4,3,2,1,0:T(8,128)(2,1)S(1)} %collective-permute-done.1.refs_14_), channel_id=1, source_target_pairs={{0,8},{8,0},{16,24},{24,16},{1,9},{9,1},{17,25},{25,17},{2,10},{10... | collective-permute-start | bytes 1572872 | tf_op jit(solution)/shard_map/ppermute | solution.py:551
  29.0 2.0 %copy-start.8 = (f32[4,4,512,128]{3,2,1,0:T(8,128)}, f32[4,4,512,128]{3,2,1,0:T(8,128)S(1)}, u32[]{:S(2)}) copy-start(f32[4,4,512,128]{3,2,1,0:T(8,128)S(1)} %get-tuple-element.50.refs_3_) | copy-start | bytes 12582916
  31.0 2.0 %copy-start.10 = (f32[4,4,512,128]{3,2,1,0:T(8,128)}, f32[4,4,512,128]{3,2,1,0:T(8,128)S(1)}, u32[]{:S(2)}) copy-start(f32[4,4,512,128]{3,2,1,0:T(8,128)S(1)} %get-tuple-element.51.refs_4_) | copy-start | bytes 12582916
  33.0 2.0 %copy-start.12 = (f32[4,4,512,128]{3,2,1,0:T(8,128)}, f32[4,4,512,128]{3,2,1,0:T(8,128)S(1)}, u32[]{:S(2)}) copy-start(f32[4,4,512,128]{3,2,1,0:T(8,128)S(1)} %get-tuple-element.52.refs_5_) | copy-start | bytes 12582916
  35.0 0.8 copy-start.2
  35.8 0.8 copy-start
  36.6 13.9 %collective-permute-start.10 = (bf16[2,4,2,128,128]{4,3,2,1,0:T(8,128)(2,1)S(1)}, bf16[2,4,2,128,128]{4,3,2,1,0:T(8,128)(2,1)}, u32[]{:S(2)}, u32[]{:S(2)}) collective-permute-start(bf16[2,4,2,128,128]{4,3,2,1,0:T(8,128)(2,1)S(1)} %collective-permute-done.6.refs_1_.refs_8_), channel_id=1, source_target_pairs={{0,4},{4,6},{6,2},{2,0},{1,5},{5,7},{7,3},{3,1},{8,12},{12,14},{14... | collective-permute-start | bytes 1572872 | tf_op jit(solution)/shard_map/ppermute | solution.py:551
  36.6 13.9 %collective-permute-start.9 = (bf16[2,4,2,128,128]{4,3,2,1,0:T(8,128)(2,1)S(1)}, bf16[2,4,2,128,128]{4,3,2,1,0:T(8,128)(2,1)}, u32[]{:S(2)}, u32[]{:S(2)}) collective-permute-start(bf16[2,4,2,128,128]{4,3,2,1,0:T(8,128)(2,1)S(1)} %collective-permute-done.6.refs_1_.refs_8_), channel_id=1, source_target_pairs={{0,16},{8,24},{16,0},{24,8},{1,17},{9,25},{17,1},{25,9},{2,18},{10... | collective-permute-start | bytes 1572872 | tf_op jit(solution)/shard_map/ppermute | solution.py:551
  37.2 13.4 %collective-permute-start.8 = (bf16[2,4,2,128,128]{4,3,2,1,0:T(8,128)(2,1)S(1)}, bf16[2,4,2,128,128]{4,3,2,1,0:T(8,128)(2,1)}, u32[]{:S(2)}, u32[]{:S(2)}) collective-permute-start(bf16[2,4,2,128,128]{4,3,2,1,0:T(8,128)(2,1)S(1)} %collective-permute-done.6.refs_1_.refs_8_), channel_id=1, source_target_pairs={{0,8},{8,0},{16,24},{24,16},{1,9},{9,1},{17,25},{25,17},{2,10},{10... | collective-permute-start | bytes 1572872 | tf_op jit(solution)/shard_map/ppermute | solution.py:551
  37.2 7.6 %collective-permute-start.7 = (bf16[2,4,2,128,128]{4,3,2,1,0:T(8,128)(2,1)S(1)}, bf16[2,4,2,128,128]{4,3,2,1,0:T(8,128)(2,1)}, u32[]{:S(2)}, u32[]{:S(2)}) collective-permute-start(bf16[2,4,2,128,128]{4,3,2,1,0:T(8,128)(2,1)S(1)} %collective-permute-done.5.refs_15_), channel_id=1, source_target_pairs={{0,8},{8,0},{16,24},{24,16},{1,9},{9,1},{17,25},{25,17},{2,10},{10... | collective-permute-start | bytes 1572872 | tf_op jit(solution)/shard_map/ppermute | solution.py:551
  38.2 13.5 %copy-start.9 = (f32[4,4,512,128]{3,2,1,0:T(8,128)S(1)}, f32[4,4,512,128]{3,2,1,0:T(8,128)}, u32[]{:S(2)}) copy-start(f32[4,4,512,128]{3,2,1,0:T(8,128)} %copy-done.8) | copy-start | bytes 12582916
  38.2 13.5 %copy-start.11 = (f32[4,4,512,128]{3,2,1,0:T(8,128)S(1)}, f32[4,4,512,128]{3,2,1,0:T(8,128)}, u32[]{:S(2)}) copy-start(f32[4,4,512,128]{3,2,1,0:T(8,128)} %copy-done.10) | copy-start | bytes 12582916
  50.6 19.7 %copy-start.1 = (bf16[2,4,2,128,128]{4,3,2,1,0:T(8,128)(2,1)S(1)}, bf16[2,4,2,128,128]{4,3,2,1,0:T(8,128)(2,1)}, u32[]{:S(2)}) copy-start(bf16[2,4,2,128,128]{4,3,2,1,0:T(8,128)(2,1)} %copy-done) | copy-start | bytes 1572868
  50.6 19.7 %copy-start.3 = (bf16[2,4,2,128,128]{4,3,2,1,0:T(8,128)(2,1)S(1)}, bf16[2,4,2,128,128]{4,3,2,1,0:T(8,128)(2,1)}, u32[]{:S(2)}) copy-start(bf16[2,4,2,128,128]{4,3,2,1,0:T(8,128)(2,1)} %copy-done.2) | copy-start | bytes 1572868
  50.6 19.7 %copy-start.5 = (f32[16,128,128]{2,1,0:T(8,128)S(1)}, f32[16,128,128]{2,1,0:T(8,128)}, u32[]{:S(2)}) copy-start(f32[16,128,128]{2,1,0:T(8,128)} %copy-done.4) | copy-start | bytes 3145732
  50.6 17.7 %collective-permute-start.13 = (bf16[2,4,2,128,128]{4,3,2,1,0:T(8,128)(2,1)}, bf16[2,4,2,128,128]{4,3,2,1,0:T(8,128)(2,1)S(1)}, u32[]{:S(2)}, u32[]{:S(2)}) collective-permute-start(bf16[2,4,2,128,128]{4,3,2,1,0:T(8,128)(2,1)} %collective-permute-done.10.refs_2_.refs_9_), channel_id=1, source_target_pairs={{0,16},{8,24},{16,0},{24,8},{1,17},{9,25},{17,1},{25,9},{2,18},{10... | collective-permute-start | bytes 1572872 | tf_op jit(solution)/shard_map/ppermute | solution.py:551
  51.2 17.1 %collective-permute-start.12 = (bf16[2,4,2,128,128]{4,3,2,1,0:T(8,128)(2,1)}, bf16[2,4,2,128,128]{4,3,2,1,0:T(8,128)(2,1)S(1)}, u32[]{:S(2)}, u32[]{:S(2)}) collective-permute-start(bf16[2,4,2,128,128]{4,3,2,1,0:T(8,128)(2,1)} %collective-permute-done.10.refs_2_.refs_9_), channel_id=1, source_target_pairs={{0,8},{8,0},{16,24},{24,16},{1,9},{9,1},{17,25},{25,17},{2,10},{10... | collective-permute-start | bytes 1572872 | tf_op jit(solution)/shard_map/ppermute | solution.py:551
  51.2 17.1 %collective-permute-start.11 = (bf16[2,4,2,128,128]{4,3,2,1,0:T(8,128)(2,1)}, bf16[2,4,2,128,128]{4,3,2,1,0:T(8,128)(2,1)S(1)}, u32[]{:S(2)}, u32[]{:S(2)}) collective-permute-start(bf16[2,4,2,128,128]{4,3,2,1,0:T(8,128)(2,1)} %collective-permute-done.9.refs_16_), channel_id=1, source_target_pairs={{0,8},{8,0},{16,24},{24,16},{1,9},{9,1},{17,25},{25,17},{2,10},{10... | collective-permute-start | bytes 1572872 | tf_op jit(solution)/shard_map/ppermute | solution.py:551
  51.7 2.2 %copy-start.13 = (f32[4,4,512,128]{3,2,1,0:T(8,128)S(1)}, f32[4,4,512,128]{3,2,1,0:T(8,128)}, u32[]{:S(2)}) copy-start(f32[4,4,512,128]{3,2,1,0:T(8,128)} %copy-done.12) | copy-start | bytes 12582916
  68.3 2.0 %collective-permute-start.14 = (bf16[2,4,2,128,128]{4,3,2,1,0:T(8,128)(2,1)S(1)}, bf16[2,4,2,128,128]{4,3,2,1,0:T(8,128)(2,1)S(1)}, u32[]{:S(2)}, u32[]{:S(2)}) collective-permute-start(bf16[2,4,2,128,128]{4,3,2,1,0:T(8,128)(2,1)S(1)} %collective-permute-done.13.refs_17_), channel_id=1, source_target_pairs={{0,8},{8,0},{16,24},{24,16},{1,9},{9,1},{17,25},{25,17},{2,10},{10... | collective-permute-start | bytes 1572872 | tf_op jit(solution)/shard_map/ppermute | solution.py:551
  75.8 8.4 %collective-permute-start.15 = (bf16[8,128,128]{2,1,0:T(8,128)(2,1)S(1)}, bf16[8,128,128]{2,1,0:T(8,128)(2,1)S(1)}, u32[]{:S(2)}, u32[]{:S(2)}) collective-permute-start(bf16[8,128,128]{2,1,0:T(8,128)(2,1)S(1)} %shard_map.118), channel_id=1, source_target_pairs={{0,1},{1,0},{2,3},{3,2},{4,5},{5,4},{6,7},{7,6},{8,9},{9,8},{10,11... | collective-permute-start | bytes 786440 | tf_op jit(solution)/shard_map/ppermute | solution.py:591
  82.8 9.5 %collective-permute-start.16 = (bf16[8,128,128]{2,1,0:T(8,128)(2,1)S(1)}, bf16[8,128,128]{2,1,0:T(8,128)(2,1)S(1)}, u32[]{:S(2)}, u32[]{:S(2)}) collective-permute-start(bf16[8,128,128]{2,1,0:T(8,128)(2,1)S(1)} %shard_map.120), channel_id=1, source_target_pairs={{0,1},{1,0},{2,3},{3,2},{4,5},{5,4},{6,7},{7,6},{8,9},{9,8},{10,11... | collective-permute-start | bytes 786440 | tf_op jit(solution)/shard_map/ppermute | solution.py:591

commit v12 on v11

--- a/solution.py
+++ b/solution.py
@@ -311,28 +311,43 @@
     )(lens, meta, *in_hbm(q, dk, dv, ck, cv))
 
 
+def collect_kernel(pick_ref, *refs):
+    blocks, out_ref, sems = refs[:-2], refs[-2], refs[-1]
+    copies = [
+        pltpu.make_async_copy(block.at[pick_ref[s]], out_ref.at[s], sems.at[s])
+        for s, block in enumerate(blocks)
+    ]
+    for copy in copies:
+        copy.start()
+    for copy in copies:
+        copy.wait()
+
+
+def collect(pick, blocks):
+    slots = len(blocks)
+    return pl.pallas_call(
+        collect_kernel,
+        grid_spec=pltpu.PrefetchScalarGridSpec(
+            num_scalar_prefetch=1,
+            grid=(1,),
+            in_specs=[pl.BlockSpec(memory_space=pl.ANY)] * slots,
+            out_specs=pl.BlockSpec(memory_space=pltpu.VMEM),
+            scratch_shapes=[pltpu.SemaphoreType.DMA((slots,))],
+        ),
+        out_shape=pltpu.VMEM((slots,) + blocks[0].shape[1:], jnp.bfloat16),
+        compiler_params=params(),
+        cost_estimate=pl.CostEstimate(flops=0, bytes_accessed=8 * 10**6, transcendentals=0),
+    )(pick, *blocks)
+
+
 def decode_kernel(
-    slots, extra, steps, target, targets, part, parts, heads, group, scale, *refs
+    extra, steps, target, targets, part, parts, heads, group, scale, slot_ref, meta_ref, *refs
 ):
-    slot_ref, pick_ref, meta_ref = refs[:3]
-    q_ref, acc_ref, ml_ref = refs[3:6]
-    blocks = refs[6 : 6 + slots]
-    out_ref, buf, sems = refs[6 + slots :]
+    q_ref, acc_ref, ml_ref, buf, out_ref = refs
     block, lanes, width = q_ref.shape
     i = pl.program_id(0)
     kept = (part * pl.num_programs(0) + i) * block
     first = lax.rem(meta_ref[1] + target, targets) * (parts * pl.num_programs(0) * block) + kept
-
-    def copies():
-        for s in range(slots):
-            yield pltpu.make_async_copy(blocks[s].at[pick_ref[s]], buf.at[s], sems.at[s])
-
-    @pl.when(i == 0)
-    def _():
-        for copy in copies():
-            copy.start()
-        for copy in copies():
-            copy.wait()
 
     per_step = heads * group
     row_head = lax.broadcasted_iota(jnp.int32, (lanes, width), 0) % per_step // group
@@ -388,23 +403,19 @@
     lax.fori_loop(0, block // unroll, body, 0)
 
 
-def decode(q, acc, ml, blocks, scalars, target, targets, part, parts, extra, steps, heads, group):
+def decode(q, acc, ml, pages, slot, meta, target, targets, part, parts, extra, steps, heads, group):
     requests, lanes, width = q.shape
     count = requests // targets // parts
     block = math.gcd(16, count)
     per_block = count // block
-    slots = len(blocks)
-
-    def here(i, slot, pick, meta):
+
+    def here(i, slot, meta):
         return ((lax.rem(meta[1] + target, targets) * parts + part) * per_block + i, 0, 0)
 
-    in_specs = [pl.BlockSpec((block,) + q.shape[1:], here)]
-    in_specs += [pl.BlockSpec(memory_space=pltpu.VMEM)] * 2
-    in_specs += [pl.BlockSpec(memory_space=pl.ANY)] * slots
+    on_chip = pl.BlockSpec(memory_space=pltpu.VMEM)
     return pl.pallas_call(
         functools.partial(
             decode_kernel,
-            slots,
             extra,
             steps,
             target,
@@ -416,21 +427,17 @@
             LOG2E / math.sqrt(width),
         ),
         grid_spec=pltpu.PrefetchScalarGridSpec(
-            num_scalar_prefetch=3,
+            num_scalar_prefetch=2,
             grid=(per_block,),
-            in_specs=in_specs,
+            in_specs=[pl.BlockSpec((block,) + q.shape[1:], here)] + [on_chip] * 3,
             out_specs=pl.BlockSpec((block, lanes, width), lambda i, *_: (i, 0, 0)),
-            scratch_shapes=[
-                pltpu.VMEM((slots, heads, 2, PAGE, width), jnp.bfloat16),
-                pltpu.SemaphoreType.DMA((slots,)),
-            ],
         ),
         out_shape=jax.ShapeDtypeStruct((count, lanes, width), jnp.bfloat16),
         compiler_params=params(),
         cost_estimate=pl.CostEstimate(
             flops=10**6, bytes_accessed=10**6, transcendentals=0
         ),
-    )(*scalars, *in_hbm(q), acc, ml, *blocks)
+    )(slot, meta, *in_hbm(q), acc, ml, pages)
 
 
 def join_kernel(counts, steps, meta_ref, *refs):
@@ -553,26 +560,29 @@
         if k == 0:
             beside = cache(targets - 1)
         if k == 1:
-            beside = prefill(prefill_q, [gathered[0, s] for s in (0, 1)], (0, 1), needed, None)
+            beside = scalars, {s: cache(s) for s in range(targets - 1)}
+        if k == ring - 2:
+            first = tuple(range(ring - 1))
+            beside = prefill(prefill_q, [gathered[0, s] for s in first], first, needed, None)
         if k == ring - 1:
-            later = tuple(range(2, ring))
-            beside = prefill(prefill_q, [gathered[0, s] for s in later], later, needed, state)
-        if k == ring - 2 and k > 1:
-            beside = scalars, {s: cache(s) for s in range(targets - 1)}
+            final = (ring - 1,)
+            beside = prefill(prefill_q, [gathered[0, s] for s in final], final, needed, state)
         arrived, beside = lax.optimization_barrier((arrived, beside))
         if k == 0:
             cached = {targets - 1: beside}
         if k == 1:
-            state = beside
-        if k == ring - 2 and k > 1:
             scalars, others = beside
             cached.update(others)
+        if k == ring - 2:
+            state = beside
         if k == ring - 1:
             prefill_out = beside
         gathered.update(zip(names, arrived))
         fresh = names
 
     blocks = [gathered[r, s] for r in range(roles) for s in range(ring)]
+    slot, pick, meta = scalars
+    pages = collect(pick, blocks)
     pieces = [None] * targets
     for s in reversed(range(targets)):
         parts = math.gcd(2, requests // targets) if s else 1
@@ -584,13 +594,13 @@
                 p[0] = a
         for part in range(parts):
             out = decode(
-                raw[0], *cached[s], blocks, scalars, s, targets, part, parts, extra, steps, heads, group
+                raw[0], *cached[s], pages, slot, meta, s, targets, part, parts, extra, steps, heads, group
             )
             if s:
                 shift = [(j, (j + s) % targets) for j in range(targets)]
                 out = lax.ppermute(out, "tp", shift)
             pieces[s].append(out)
-    decode_out = join(pieces, scalars[2], steps)
+    decode_out = join(pieces, meta, steps)
     return (prefill_out, decode_out)
 
 

time: 94.6 us -> 88.9 us (0.940)
  local copies, waits for them, and re-layouts: 11.8 us -> 1.05 us
  waiting for transfers between devices: 12.4 us -> 17 us
  Pallas kernels: 59.3 us -> 57.1 us
  starting transfers between devices: 9.48 us -> 11.6 us
    unnamed x30 -> x6, local copies, waits for them, and re-layouts: 11.4 us -> 0.66 us
    ppermute x15, waiting for transfers between devices: 11.6 us -> 14.7 us  [shards(): lax.ppermute(gathered[of], axis, pairs)]
    pallas_call x3 -> x4, Pallas kernels: 19.1 us -> 16.9 us  [the longest x3 15 us: decode(): pl.pallas_call(functools.partial(decode_kernel, extra, steps, target, tar...]
    ppermute x15, starting transfers between devices: 7.32 us -> 9.42 us  [shards(): lax.ppermute(gathered[of], axis, pairs)]
    ppermute x2, waiting for transfers between devices: 0.77 us -> 2.34 us  [shards(): out = lax.ppermute(out, 'tp', shift)]
  transfers between devices with their start and end apart: 17 -> 17, of which waited for: 5 -> 7; matrix products, arithmetic and copies ran while one was open for 1% -> 1% of each run, Pallas kernels for 54% -> 54%
where the time goes in v12:
time: 88.9 us; the launch traced here: 87.8 us
  Pallas kernels  57.1 us (64%)
  waiting for transfers between devices  17 us (19%)
  starting transfers between devices  11.6 us (13%)
  local copies, waits for them, and re-layouts  1.05 us (1%)
    pallas_call x2, Pallas kernels, prefill(): pl.pallas_call(functools.partial(prefill_kernel, own, count, slots, group...  24.5 us
    pallas_call x3, Pallas kernels, decode(): pl.pallas_call(functools.partial(decode_kernel, extra, steps, target, tar...  15 us
    ppermute x15, waiting for transfers between devices, shards(): lax.ppermute(gathered[of], axis, pairs)  14.7 us
    pallas_call x2, Pallas kernels, cache_part(): pl.pallas_call(functools.partial(cache_kernel, steps, heads, group, targe...  12.5 us
    ppermute x15, starting transfers between devices, shards(): lax.ppermute(gathered[of], axis, pairs)  9.42 us
    ppermute x2, waiting for transfers between devices, shards(): out = lax.ppermute(out, 'tp', shift)  2.34 us
    ppermute x2, starting transfers between devices, shards(): out = lax.ppermute(out, 'tp', shift)  2.16 us
    pallas_call x1, Pallas kernels, collect(): pl.pallas_call(collect_kernel, grid_spec=pltpu.PrefetchScalarGridSpec(num...  1.95 us
  transfers between devices with their start and end apart: 17, of which 7 were waited for; matrix products, arithmetic and copies ran while one was open for 1% of the time, Pallas kernels for 54%

profile of v12, /device:TPU:24, one launch (start us, length us, event | category | flops | bytes accessed | tf_op | source)
XLA Modules:
  0.0 87.8 jit_solution(2203182003709700029)
XLA Ops:
  0.6 1.5 %shard_map.113.refs_1_.refs_0_ = bf16[2,4,2,128,128]{4,3,2,1,0:T(8,128)(2,1)S(1)} custom-call(bf16[1024,128]{1,0:T(8,128)(2,1)} %bitcast.22, bf16[1024,128]{1,0:T(8,128)(2,1)} %bitcast.23), custom_call_target="tpu_custom_call" | custom-call | flops 100000000 | bytes 2000000 | tf_op jit(solution)/shard_map/pallas_call | solution.py:58
  2.1 0.4 collective-permute-start.2
  2.5 1.5 %collective-permute-start.1 = (bf16[2,4,2,128,128]{4,3,2,1,0:T(8,128)(2,1)S(1)}, bf16[2,4,2,128,128]{4,3,2,1,0:T(8,128)(2,1)S(1)}, u32[]{:S(2)}, u32[]{:S(2)}) collective-permute-start(bf16[2,4,2,128,128]{4,3,2,1,0:T(8,128)(2,1)S(1)} %shard_map.113.refs_1_.refs_0_), channel_id=1, source_target_pairs={{0,16},{8,24},{16,0},{24,8},{1,17},{9,25},{17,1},{25,9},{2,18},{10... | collective-permute-start | bytes 1572872 | tf_op jit(solution)/shard_map/ppermute | solution.py:558
  4.0 0.0 collective-permute-start
  4.0 0.1 pad_add_fusion.meta_ref
  4.1 0.7 copy-done
  4.8 6.2 %shard_map.114 = (f32[16,128,128]{2,1,0:T(8,128)S(1)}, f32[16,8,128]{2,1,0:T(8,128)S(1)}) custom-call(s32[32]{0:T(128)S(1)} %copy-done, s32[2]{0:T(128)S(1)} %pad_add_fusion.meta_ref, bf16[32,128,128]{2,1,0:T(8,128)(2,1)} %bitcast.9, bf16[32,16,128]{2,1,0:T(8,128)(2,1)} %bitcast.18, bf16[32,16,128]{2,1,0:T(8,128)(2,1)} %bitcast.20, ...), custom_call_target="tpu_custom_call" | custom-call | flops 2147483648 | bytes 7000000 | tf_op jit(solution)/shard_map/pallas_call | solution.py:294
  11.0 4.8 %collective-permute-done.2.refs_2_.refs_1_ = bf16[2,4,2,128,128]{4,3,2,1,0:T(8,128)(2,1)S(1)} collective-permute-done((bf16[2,4,2,128,128]{4,3,2,1,0:T(8,128)(2,1)S(1)}, bf16[2,4,2,128,128]{4,3,2,1,0:T(8,128)(2,1)S(1)}, u32[]{:S(2)}, u32[]{:S(2)}) %collective-permute-start.2) | collective-permute-done | bytes 524320 | tf_op jit(solution)/shard_map/ppermute | solution.py:558
  15.9 0.1 collective-permute-done.1.refs_8_
  15.9 0.0 collective-permute-done.refs_4_
  15.9 1.2 %collective-permute-start.6 = (bf16[2,4,2,128,128]{4,3,2,1,0:T(8,128)(2,1)S(1)}, bf16[2,4,2,128,128]{4,3,2,1,0:T(8,128)(2,1)}, u32[]{:S(2)}, u32[]{:S(2)}) collective-permute-start(bf16[2,4,2,128,128]{4,3,2,1,0:T(8,128)(2,1)S(1)} %collective-permute-done.2.refs_2_.refs_1_), channel_id=1, source_target_pairs={{0,4},{4,6},{6,2},{2,0},{1,5},{5,7},{7,3},{3,1},{8,12},{12,14},{14... | collective-permute-start | bytes 1572872 | tf_op jit(solution)/shard_map/ppermute | solution.py:558
  17.1 1.5 %collective-permute-start.5 = (bf16[2,4,2,128,128]{4,3,2,1,0:T(8,128)(2,1)S(1)}, bf16[2,4,2,128,128]{4,3,2,1,0:T(8,128)(2,1)}, u32[]{:S(2)}, u32[]{:S(2)}) collective-permute-start(bf16[2,4,2,128,128]{4,3,2,1,0:T(8,128)(2,1)S(1)} %collective-permute-done.2.refs_2_.refs_1_), channel_id=1, source_target_pairs={{0,16},{8,24},{16,0},{24,8},{1,17},{9,25},{17,1},{25,9},{2,18},{10... | collective-permute-start | bytes 1572872 | tf_op jit(solution)/shard_map/ppermute | solution.py:558
  18.6 0.0 collective-permute-start.4
  18.6 0.5 collective-permute-start.3
  19.1 0.1 copy.17
  19.2 0.1 broadcast_in_dim.15
  19.3 0.1 copy.16
  19.4 0.1 reshape.39.slot_ref
  19.6 0.1 select_reduce_fusion.pick_ref
  19.7 6.2 %shard_map.115 = (f32[16,128,128]{2,1,0:T(8,128)S(1)}, f32[16,8,128]{2,1,0:T(8,128)S(1)}) custom-call(s32[32]{0:T(128)S(1)} %copy-done.1, s32[2]{0:T(128)S(1)} %pad_add_fusion.meta_ref, bf16[32,128,128]{2,1,0:T(8,128)(2,1)} %bitcast.10, bf16[32,16,128]{2,1,0:T(8,128)(2,1)} %bitcast.19, bf16[32,16,128]{2,1,0:T(8,128)(2,1)} %bitcast.21, ...), custom_call_target="tpu_custom_call" | custom-call | flops 2147483648 | bytes 7000000 | tf_op jit(solution)/shard_map/pallas_call | solution.py:294
  25.9 0.0 collective-permute-done.3.refs_12_
  25.9 2.8 %collective-permute-done.6.refs_3_.refs_2_ = bf16[2,4,2,128,128]{4,3,2,1,0:T(8,128)(2,1)} collective-permute-done((bf16[2,4,2,128,128]{4,3,2,1,0:T(8,128)(2,1)S(1)}, bf16[2,4,2,128,128]{4,3,2,1,0:T(8,128)(2,1)}, u32[]{:S(2)}, u32[]{:S(2)}) %collective-permute-start.6) | collective-permute-done | bytes 524320 | tf_op jit(solution)/shard_map/ppermute | solution.py:558
  28.8 1.0 %collective-permute-done.5.refs_9_ = bf16[2,4,2,128,128]{4,3,2,1,0:T(8,128)(2,1)} collective-permute-done((bf16[2,4,2,128,128]{4,3,2,1,0:T(8,128)(2,1)S(1)}, bf16[2,4,2,128,128]{4,3,2,1,0:T(8,128)(2,1)}, u32[]{:S(2)}, u32[]{:S(2)}) %collective-permute-start.5) | collective-permute-done | bytes 524320 | tf_op jit(solution)/shard_map/ppermute | solution.py:558
  29.7 0.0 collective-permute-done.4.refs_5_
  29.7 1.5 %collective-permute-start.10 = (bf16[2,4,2,128,128]{4,3,2,1,0:T(8,128)(2,1)}, bf16[2,4,2,128,128]{4,3,2,1,0:T(8,128)(2,1)S(1)}, u32[]{:S(2)}, u32[]{:S(2)}) collective-permute-start(bf16[2,4,2,128,128]{4,3,2,1,0:T(8,128)(2,1)} %collective-permute-done.6.refs_3_.refs_2_), channel_id=1, source_target_pairs={{0,4},{4,6},{6,2},{2,0},{1,5},{5,7},{7,3},{3,1},{8,12},{12,14},{14... | collective-permute-start | bytes 1572872 | tf_op jit(solution)/shard_map/ppermute | solution.py:558
  31.3 1.5 %collective-permute-start.9 = (bf16[2,4,2,128,128]{4,3,2,1,0:T(8,128)(2,1)}, bf16[2,4,2,128,128]{4,3,2,1,0:T(8,128)(2,1)S(1)}, u32[]{:S(2)}, u32[]{:S(2)}) collective-permute-start(bf16[2,4,2,128,128]{4,3,2,1,0:T(8,128)(2,1)} %collective-permute-done.6.refs_3_.refs_2_), channel_id=1, source_target_pairs={{0,16},{8,24},{16,0},{24,8},{1,17},{9,25},{17,1},{25,9},{2,18},{10... | collective-permute-start | bytes 1572872 | tf_op jit(solution)/shard_map/ppermute | solution.py:558
  32.8 0.0 collective-permute-start.8
  32.8 0.5 collective-permute-start.7
  33.3 15.0 %shard_map.116 = (f32[4,4,512,128]{3,2,1,0:T(8,128)S(1)}, f32[4,4,512,128]{3,2,1,0:T(8,128)S(1)}, f32[4,4,512,128]{3,2,1,0:T(8,128)S(1)}) custom-call(s32[4]{0:T(128)S(1)} %compare_convert_fusion.needed_ref, bf16[1,256,32,128]{3,2,1,0:T(8,128)(2,1)} %refs_0_.3, bf16[2,4,2,128,128]{4,3,2,1,0:T(8,128)(2,1)S(1)} %shard_map.113.refs_1_.refs_0_, ...), custom_call_target="tpu_custom_call" | custom-call | flops 12884901888 | bytes 12000000 | tf_op jit(solution)/shard_map/pallas_call | solution.py:201
  48.2 0.0 collective-permute-done.7.refs_13_
  48.3 0.0 collective-permute-done.8.refs_6_
  48.3 0.1 collective-permute-start.11
  48.3 0.6 collective-permute-start.13
  48.9 0.2 collective-permute-start.12
  49.1 9.5 %shard_map.117 = bf16[1,256,32,128]{3,2,1,0:T(8,128)(2,1)} custom-call(s32[4]{0:T(128)S(1)} %compare_convert_fusion.needed_ref, bf16[1,256,32,128]{3,2,1,0:T(8,128)(2,1)} %refs_0_.3, bf16[2,4,2,128,128]{4,3,2,1,0:T(8,128)(2,1)S(1)} %collective-permute-done.10.refs_1_.refs_3_, f32[4,4,512,128]{3,2,1,0:T(8,128)S(1)} %get-tuple-element.50.refs_2_, ...), custom_call_target="tpu_custom_call" | custom-call | flops 4294967296 | bytes 12000000 | tf_op jit(solution)/shard_map/pallas_call | solution.py:201
  58.6 0.0 collective-permute-done.11.refs_14_
  58.6 4.1 %collective-permute-done.13.refs_11_ = bf16[2,4,2,128,128]{4,3,2,1,0:T(8,128)(2,1)S(1)} collective-permute-done((bf16[2,4,2,128,128]{4,3,2,1,0:T(8,128)(2,1)S(1)}, bf16[2,4,2,128,128]{4,3,2,1,0:T(8,128)(2,1)S(1)}, u32[]{:S(2)}, u32[]{:S(2)}) %collective-permute-start.13) | collective-permute-done | bytes 524320 | tf_op jit(solution)/shard_map/ppermute | solution.py:558
  62.7 0.0 collective-permute-done.12.refs_7_
  62.7 0.0 collective-permute-start.14
  62.7 1.9 %collective-permute-done.14.refs_15_ = bf16[2,4,2,128,128]{4,3,2,1,0:T(8,128)(2,1)S(1)} collective-permute-done((bf16[2,4,2,128,128]{4,3,2,1,0:T(8,128)(2,1)S(1)}, bf16[2,4,2,128,128]{4,3,2,1,0:T(8,128)(2,1)S(1)}, u32[]{:S(2)}, u32[]{:S(2)}) %collective-permute-start.14) | collective-permute-done | bytes 524320 | tf_op jit(solution)/shard_map/ppermute | solution.py:558
  64.6 2.0 %shard_map.118.refs_3_ = bf16[16,4,2,128,128]{4,3,2,1,0:T(8,128)(2,1)S(1)} custom-call(s32[16]{0:T(128)S(1)} %select_reduce_fusion.pick_ref, bf16[2,4,2,128,128]{4,3,2,1,0:T(8,128)(2,1)S(1)} %shard_map.113.refs_1_.refs_0_, bf16[2,4,2,128,128]{4,3,2,1,0:T(8,128)(2,1)S(1)} %collective-permute-done.2.refs_2_.refs_1_, ...), custom_call_target="tpu_custom_call" | custom-call | bytes 8000000 | tf_op jit(solution)/shard_map/pallas_call | solution.py:328
  66.6 4.1 %shard_map.119 = bf16[8,128,128]{2,1,0:T(8,128)(2,1)S(1)} custom-call(s32[128]{0:T(128)S(1)} %reshape.39.slot_ref, s32[2]{0:T(128)S(1)} %pad_add_fusion.meta_ref, bf16[32,128,128]{2,1,0:T(8,128)(2,1)} %bitcast.11, f32[16,128,128]{2,1,0:T(8,128)S(1)} %get-tuple-element.58.refs_1_, f32[16,8,128]{2,1,0:T(8,128)S(1)} %get-tuple-element.59.refs_2_, ...), custom_call_target="tpu_custom_call" | custom-call | flops 1000000 | bytes 1000000 | tf_op jit(solution)/shard_map/pallas_call | solution.py:416
  70.7 1.6 %collective-permute-start.15 = (bf16[8,128,128]{2,1,0:T(8,128)(2,1)S(1)}, bf16[8,128,128]{2,1,0:T(8,128)(2,1)S(1)}, u32[]{:S(2)}, u32[]{:S(2)}) collective-permute-start(bf16[8,128,128]{2,1,0:T(8,128)(2,1)S(1)} %shard_map.119), channel_id=1, source_target_pairs={{0,1},{1,0},{2,3},{3,2},{4,5},{5,4},{6,7},{7,6},{8,9},{9,8},{10,11... | collective-permute-start | bytes 786440 | tf_op jit(solution)/shard_map/ppermute | solution.py:601
  72.2 4.1 %shard_map.121 = bf16[8,128,128]{2,1,0:T(8,128)(2,1)S(1)} custom-call(s32[128]{0:T(128)S(1)} %reshape.39.slot_ref, s32[2]{0:T(128)S(1)} %pad_add_fusion.meta_ref, bf16[32,128,128]{2,1,0:T(8,128)(2,1)} %bitcast.12, f32[16,128,128]{2,1,0:T(8,128)S(1)} %get-tuple-element.58.refs_1_, f32[16,8,128]{2,1,0:T(8,128)S(1)} %get-tuple-element.59.refs_2_, ...), custom_call_target="tpu_custom_call" | custom-call | flops 1000000 | bytes 1000000 | tf_op jit(solution)/shard_map/pallas_call | solution.py:416
  76.3 0.6 collective-permute-start.16
  76.9 2.3 %collective-permute-done.15.refs_1_ = bf16[8,128,128]{2,1,0:T(8,128)(2,1)S(1)} collective-permute-done((bf16[8,128,128]{2,1,0:T(8,128)(2,1)S(1)}, bf16[8,128,128]{2,1,0:T(8,128)(2,1)S(1)}, u32[]{:S(2)}, u32[]{:S(2)}) %collective-permute-start.15) | collective-permute-done | bytes 262176 | tf_op jit(solution)/shard_map/ppermute | solution.py:601
  79.2 6.8 %shard_map.120.refs_0_ = bf16[16,128,128]{2,1,0:T(8,128)(2,1)S(1)} custom-call(s32[128]{0:T(128)S(1)} %reshape.39.slot_ref, s32[2]{0:T(128)S(1)} %pad_add_fusion.meta_ref, bf16[32,128,128]{2,1,0:T(8,128)(2,1)} %bitcast.13, f32[16,128,128]{2,1,0:T(8,128)S(1)} %get-tuple-element.69.refs_1_, f32[16,8,128]{2,1,0:T(8,128)S(1)} %get-tuple-element.70.refs_2_, ...), custom_call_target="tpu_custom_call" | custom-call | flops 1000000 | bytes 1000000 | tf_op jit(solution)/shard_map/pallas_call | solution.py:416
  86.0 1.8 %shard_map.122 = bf16[16,4,8192]{2,1,0:T(4,128)(2,1)} custom-call(s32[2]{0:T(128)S(1)} %pad_add_fusion.meta_ref, bf16[16,128,128]{2,1,0:T(8,128)(2,1)S(1)} %shard_map.120.refs_0_, bf16[8,128,128]{2,1,0:T(8,128)(2,1)S(1)} %collective-permute-done.15.refs_1_, bf16[8,128,128]{2,1,0:T(8,128)(2,1)S(1)} %collective-permute-done.16.refs_2_), custom_call_target="tpu_custom_call" | custom-call | bytes 2000000 | tf_op jit(solution)/shard_map/pallas_call | solution.py:473
  (10 shorter events, 0.1 us)
Async XLA Ops:
  2.1 13.7 %collective-permute-start.2 = (bf16[2,4,2,128,128]{4,3,2,1,0:T(8,128)(2,1)S(1)}, bf16[2,4,2,128,128]{4,3,2,1,0:T(8,128)(2,1)S(1)}, u32[]{:S(2)}, u32[]{:S(2)}) collective-permute-start(bf16[2,4,2,128,128]{4,3,2,1,0:T(8,128)(2,1)S(1)} %shard_map.113.refs_1_.refs_0_), channel_id=1, source_target_pairs={{0,4},{4,6},{6,2},{2,0},{1,5},{5,7},{7,3},{3,1},{8,12},{12,14},{14... | collective-permute-start | bytes 1572872 | tf_op jit(solution)/shard_map/ppermute | solution.py:558
  2.5 13.4 %collective-permute-start.1 = (bf16[2,4,2,128,128]{4,3,2,1,0:T(8,128)(2,1)S(1)}, bf16[2,4,2,128,128]{4,3,2,1,0:T(8,128)(2,1)S(1)}, u32[]{:S(2)}, u32[]{:S(2)}) collective-permute-start(bf16[2,4,2,128,128]{4,3,2,1,0:T(8,128)(2,1)S(1)} %shard_map.113.refs_1_.refs_0_), channel_id=1, source_target_pairs={{0,16},{8,24},{16,0},{24,8},{1,17},{9,25},{17,1},{25,9},{2,18},{10... | collective-permute-start | bytes 1572872 | tf_op jit(solution)/shard_map/ppermute | solution.py:558
  4.0 11.9 %collective-permute-start = (bf16[2,4,2,128,128]{4,3,2,1,0:T(8,128)(2,1)S(1)}, bf16[2,4,2,128,128]{4,3,2,1,0:T(8,128)(2,1)S(1)}, u32[]{:S(2)}, u32[]{:S(2)}) collective-permute-start(bf16[2,4,2,128,128]{4,3,2,1,0:T(8,128)(2,1)S(1)} %shard_map.113.refs_1_.refs_0_), channel_id=1, source_target_pairs={{0,8},{8,0},{16,24},{24,16},{1,9},{9,1},{17,25},{25,17},{2,10},{10... | collective-permute-start | bytes 1572872 | tf_op jit(solution)/shard_map/ppermute | solution.py:558
  4.1 0.7 copy-start
  4.8 14.3 %copy-start.2 = (s32[32,4]{0,1:T(4,128)S(1)}, s32[32,4]{0,1:T(4,128)}, u32[]{:S(2)}) copy-start(s32[32,4]{0,1:T(4,128)} %param.19) | copy-start | bytes 1540
  4.8 14.9 %copy-start.1 = (s32[32]{0:T(128)S(1)}, s32[32]{0:T(128)}, u32[]{:S(2)}) copy-start(s32[32]{0:T(128)} %len_ref.3) | copy-start | bytes 388
  15.9 12.8 %collective-permute-start.6 = (bf16[2,4,2,128,128]{4,3,2,1,0:T(8,128)(2,1)S(1)}, bf16[2,4,2,128,128]{4,3,2,1,0:T(8,128)(2,1)}, u32[]{:S(2)}, u32[]{:S(2)}) collective-permute-start(bf16[2,4,2,128,128]{4,3,2,1,0:T(8,128)(2,1)S(1)} %collective-permute-done.2.refs_2_.refs_1_), channel_id=1, source_target_pairs={{0,4},{4,6},{6,2},{2,0},{1,5},{5,7},{7,3},{3,1},{8,12},{12,14},{14... | collective-permute-start | bytes 1572872 | tf_op jit(solution)/shard_map/ppermute | solution.py:558
  17.1 12.6 %collective-permute-start.5 = (bf16[2,4,2,128,128]{4,3,2,1,0:T(8,128)(2,1)S(1)}, bf16[2,4,2,128,128]{4,3,2,1,0:T(8,128)(2,1)}, u32[]{:S(2)}, u32[]{:S(2)}) collective-permute-start(bf16[2,4,2,128,128]{4,3,2,1,0:T(8,128)(2,1)S(1)} %collective-permute-done.2.refs_2_.refs_1_), channel_id=1, source_target_pairs={{0,16},{8,24},{16,0},{24,8},{1,17},{9,25},{17,1},{25,9},{2,18},{10... | collective-permute-start | bytes 1572872 | tf_op jit(solution)/shard_map/ppermute | solution.py:558
  18.6 11.1 %collective-permute-start.4 = (bf16[2,4,2,128,128]{4,3,2,1,0:T(8,128)(2,1)S(1)}, bf16[2,4,2,128,128]{4,3,2,1,0:T(8,128)(2,1)}, u32[]{:S(2)}, u32[]{:S(2)}) collective-permute-start(bf16[2,4,2,128,128]{4,3,2,1,0:T(8,128)(2,1)S(1)} %collective-permute-done.2.refs_2_.refs_1_), channel_id=1, source_target_pairs={{0,8},{8,0},{16,24},{24,16},{1,9},{9,1},{17,25},{25,17},{2,10},{10... | collective-permute-start | bytes 1572872 | tf_op jit(solution)/shard_map/ppermute | solution.py:558
  18.6 7.3 %collective-permute-start.3 = (bf16[2,4,2,128,128]{4,3,2,1,0:T(8,128)(2,1)S(1)}, bf16[2,4,2,128,128]{4,3,2,1,0:T(8,128)(2,1)}, u32[]{:S(2)}, u32[]{:S(2)}) collective-permute-start(bf16[2,4,2,128,128]{4,3,2,1,0:T(8,128)(2,1)S(1)} %collective-permute-done.1.refs_8_), channel_id=1, source_target_pairs={{0,8},{8,0},{16,24},{24,16},{1,9},{9,1},{17,25},{25,17},{2,10},{10... | collective-permute-start | bytes 1572872 | tf_op jit(solution)/shard_map/ppermute | solution.py:558
  29.7 18.5 %collective-permute-start.10 = (bf16[2,4,2,128,128]{4,3,2,1,0:T(8,128)(2,1)}, bf16[2,4,2,128,128]{4,3,2,1,0:T(8,128)(2,1)S(1)}, u32[]{:S(2)}, u32[]{:S(2)}) collective-permute-start(bf16[2,4,2,128,128]{4,3,2,1,0:T(8,128)(2,1)} %collective-permute-done.6.refs_3_.refs_2_), channel_id=1, source_target_pairs={{0,4},{4,6},{6,2},{2,0},{1,5},{5,7},{7,3},{3,1},{8,12},{12,14},{14... | collective-permute-start | bytes 1572872 | tf_op jit(solution)/shard_map/ppermute | solution.py:558
  31.3 17.0 %collective-permute-start.9 = (bf16[2,4,2,128,128]{4,3,2,1,0:T(8,128)(2,1)}, bf16[2,4,2,128,128]{4,3,2,1,0:T(8,128)(2,1)S(1)}, u32[]{:S(2)}, u32[]{:S(2)}) collective-permute-start(bf16[2,4,2,128,128]{4,3,2,1,0:T(8,128)(2,1)} %collective-permute-done.6.refs_3_.refs_2_), channel_id=1, source_target_pairs={{0,16},{8,24},{16,0},{24,8},{1,17},{9,25},{17,1},{25,9},{2,18},{10... | collective-permute-start | bytes 1572872 | tf_op jit(solution)/shard_map/ppermute | solution.py:558
  32.8 15.5 %collective-permute-start.8 = (bf16[2,4,2,128,128]{4,3,2,1,0:T(8,128)(2,1)}, bf16[2,4,2,128,128]{4,3,2,1,0:T(8,128)(2,1)S(1)}, u32[]{:S(2)}, u32[]{:S(2)}) collective-permute-start(bf16[2,4,2,128,128]{4,3,2,1,0:T(8,128)(2,1)} %collective-permute-done.6.refs_3_.refs_2_), channel_id=1, source_target_pairs={{0,8},{8,0},{16,24},{24,16},{1,9},{9,1},{17,25},{25,17},{2,10},{10... | collective-permute-start | bytes 1572872 | tf_op jit(solution)/shard_map/ppermute | solution.py:558
  32.8 15.5 %collective-permute-start.7 = (bf16[2,4,2,128,128]{4,3,2,1,0:T(8,128)(2,1)}, bf16[2,4,2,128,128]{4,3,2,1,0:T(8,128)(2,1)S(1)}, u32[]{:S(2)}, u32[]{:S(2)}) collective-permute-start(bf16[2,4,2,128,128]{4,3,2,1,0:T(8,128)(2,1)} %collective-permute-done.5.refs_9_), channel_id=1, source_target_pairs={{0,8},{8,0},{16,24},{24,16},{1,9},{9,1},{17,25},{25,17},{2,10},{10... | collective-permute-start | bytes 1572872 | tf_op jit(solution)/shard_map/ppermute | solution.py:558
  48.3 10.4 %collective-permute-start.11 = (bf16[2,4,2,128,128]{4,3,2,1,0:T(8,128)(2,1)S(1)}, bf16[2,4,2,128,128]{4,3,2,1,0:T(8,128)(2,1)S(1)}, u32[]{:S(2)}, u32[]{:S(2)}) collective-permute-start(bf16[2,4,2,128,128]{4,3,2,1,0:T(8,128)(2,1)S(1)} %collective-permute-done.9.refs_10_), channel_id=1, source_target_pairs={{0,8},{8,0},{16,24},{24,16},{1,9},{9,1},{17,25},{25,17},{2,10},{10... | collective-permute-start | bytes 1572872 | tf_op jit(solution)/shard_map/ppermute | solution.py:558
  48.3 14.3 %collective-permute-start.13 = (bf16[2,4,2,128,128]{4,3,2,1,0:T(8,128)(2,1)S(1)}, bf16[2,4,2,128,128]{4,3,2,1,0:T(8,128)(2,1)S(1)}, u32[]{:S(2)}, u32[]{:S(2)}) collective-permute-start(bf16[2,4,2,128,128]{4,3,2,1,0:T(8,128)(2,1)S(1)} %collective-permute-done.10.refs_1_.refs_3_), channel_id=1, source_target_pairs={{0,16},{8,24},{16,0},{24,8},{1,17},{9,25},{17,1},{25,9},{2,18},{10... | collective-permute-start | bytes 1572872 | tf_op jit(solution)/shard_map/ppermute | solution.py:558
  48.9 13.7 %collective-permute-start.12 = (bf16[2,4,2,128,128]{4,3,2,1,0:T(8,128)(2,1)S(1)}, bf16[2,4,2,128,128]{4,3,2,1,0:T(8,128)(2,1)S(1)}, u32[]{:S(2)}, u32[]{:S(2)}) collective-permute-start(bf16[2,4,2,128,128]{4,3,2,1,0:T(8,128)(2,1)S(1)} %collective-permute-done.10.refs_1_.refs_3_), channel_id=1, source_target_pairs={{0,8},{8,0},{16,24},{24,16},{1,9},{9,1},{17,25},{25,17},{2,10},{10... | collective-permute-start | bytes 1572872 | tf_op jit(solution)/shard_map/ppermute | solution.py:558
  62.7 1.9 %collective-permute-start.14 = (bf16[2,4,2,128,128]{4,3,2,1,0:T(8,128)(2,1)S(1)}, bf16[2,4,2,128,128]{4,3,2,1,0:T(8,128)(2,1)S(1)}, u32[]{:S(2)}, u32[]{:S(2)}) collective-permute-start(bf16[2,4,2,128,128]{4,3,2,1,0:T(8,128)(2,1)S(1)} %collective-permute-done.13.refs_11_), channel_id=1, source_target_pairs={{0,8},{8,0},{16,24},{24,16},{1,9},{9,1},{17,25},{25,17},{2,10},{10... | collective-permute-start | bytes 1572872 | tf_op jit(solution)/shard_map/ppermute | solution.py:558
  70.7 8.6 %collective-permute-start.15 = (bf16[8,128,128]{2,1,0:T(8,128)(2,1)S(1)}, bf16[8,128,128]{2,1,0:T(8,128)(2,1)S(1)}, u32[]{:S(2)}, u32[]{:S(2)}) collective-permute-start(bf16[8,128,128]{2,1,0:T(8,128)(2,1)S(1)} %shard_map.119), channel_id=1, source_target_pairs={{0,1},{1,0},{2,3},{3,2},{4,5},{5,4},{6,7},{7,6},{8,9},{9,8},{10,11... | collective-permute-start | bytes 786440 | tf_op jit(solution)/shard_map/ppermute | solution.py:601
  76.3 9.7 %collective-permute-start.16 = (bf16[8,128,128]{2,1,0:T(8,128)(2,1)S(1)}, bf16[8,128,128]{2,1,0:T(8,128)(2,1)S(1)}, u32[]{:S(2)}, u32[]{:S(2)}) collective-permute-start(bf16[8,128,128]{2,1,0:T(8,128)(2,1)S(1)} %shard_map.121), channel_id=1, source_target_pairs={{0,1},{1,0},{2,3},{3,2},{4,5},{5,4},{6,7},{7,6},{8,9},{9,8},{10,11... | collective-permute-start | bytes 786440 | tf_op jit(solution)/shard_map/ppermute | solution.py:601

commit v13 on v12

--- a/solution.py
+++ b/solution.py
@@ -64,7 +64,7 @@
     )(*in_hbm(k.reshape(tokens * heads, width), v.reshape(tokens * heads, width)))
 
 
-def prefill_kernel(own, count, slots, group, tokens, scale, needed_ref, *refs):
+def prefill_kernel(own, done, count, slots, group, tokens, scale, needed_ref, *refs):
     q_ref = refs[0]
     blocks = refs[1 : 1 + count]
     refs = refs[1 + count :]
@@ -72,8 +72,11 @@
     if own:
         acc_ref, m_ref, l_ref, buf, s_ref, sems = refs
         acc_ref, m_ref, l_ref = acc_ref.at[i], m_ref.at[i], l_ref.at[i]
+    elif done:
+        old_acc_ref, old_m_ref, old_l_ref, out_ref, buf, s_ref, acc_ref, m_ref, l_ref, sems = refs
     else:
-        old_acc_ref, old_m_ref, old_l_ref, out_ref, buf, s_ref, acc_ref, m_ref, l_ref, sems = refs
+        old_acc_ref, old_m_ref, old_l_ref, acc_ref, top_ref, l_ref, buf, s_ref, m_ref, sems = refs
+        acc_ref, l_ref = acc_ref.at[i], l_ref.at[i]
     pages, heads = blocks[0].shape[:2]
     block = q_ref.shape[1]
     rest = range(1 if own else 0, count)
@@ -156,6 +159,8 @@
             share = jnp.exp2((old_m_ref[i, h, at] - m) * scale)
             l_ref[h, at] = old_l_ref[i, h, at] * share
             acc_ref[h, at] = old_acc_ref[i, h, at] * share
+            if not done:
+                top_ref[i, h, at] = m
 
     def weigh(b, carry):
         for h, at in parts:
@@ -166,7 +171,7 @@
         return carry
 
     lax.fori_loop(0, total, weigh, 0)
-    if not own:
+    if done:
         out = []
         for h in range(heads):
             l = jnp.sum(l_ref[h], axis=1, keepdims=True)
@@ -174,7 +179,7 @@
         out_ref[0] = jnp.concatenate(out, axis=1).astype(out_ref.dtype)
 
 
-def prefill(q, blocks, slots, needed, state):
+def prefill(q, blocks, slots, needed, state, done):
     _, tokens, q_heads, width = q.shape
     own = state is None
     count = len(blocks)
@@ -190,17 +195,24 @@
         pltpu.VMEM((count,) + blocks[0].shape, jnp.bfloat16),
         pltpu.VMEM((count, heads, rows, tokens), jnp.float32),
     ]
+    aliases = {}
     if own:
         in_specs = [q_spec, own_spec] + [any_spec] * (count - 1)
-        out_specs, state = [on_chip] * 3, ()
-        out_shape = [pltpu.VMEM((tokens // block, heads, rows, width), jnp.float32)] * 3
+        state = ()
     else:
         in_specs = [q_spec] + [any_spec] * count + [on_chip] * 3
+    if done:
         out_specs, out_shape = q_spec, jax.ShapeDtypeStruct(q.shape, jnp.bfloat16)
         scratch += [pltpu.VMEM((heads, rows, width), jnp.float32)] * 3
+    else:
+        out_specs = [on_chip] * 3
+        out_shape = [pltpu.VMEM((tokens // block, heads, rows, width), jnp.float32)] * 3
+        if not own:
+            aliases = {2 + count + j: j for j in range(3)}
+            scratch += [pltpu.VMEM((heads, rows, width), jnp.float32)]
     return pl.pallas_call(
         functools.partial(
-            prefill_kernel, own, count, slots, group, tokens, LOG2E / math.sqrt(width)
+            prefill_kernel, own, done, count, slots, group, tokens, LOG2E / math.sqrt(width)
         ),
         grid_spec=pltpu.PrefetchScalarGridSpec(
             num_scalar_prefetch=1,
@@ -210,6 +222,7 @@
             scratch_shapes=scratch + [pltpu.SemaphoreType.DMA((count,))],
         ),
         out_shape=out_shape,
+        input_output_aliases=aliases,
         compiler_params=params(),
         cost_estimate=pl.CostEstimate(
             flops=16 * q_heads * tokens * tokens * count * width,
@@ -543,6 +556,7 @@
         return cache_part(*raw, lens, meta, target, targets, steps, heads, group)
 
     gathered = {(0, 0): split_heads(prefill_k, prefill_v)}
+    state = None
     fresh = [(0, 0)]
     for k in range(ring + len(flips) - 1):
         sends = []
@@ -558,24 +572,18 @@
         arrived = [lax.ppermute(gathered[of], axis, pairs) for _, of, _, axis, pairs in sends]
         beside = ()
         if k == 0:
-            beside = cache(targets - 1)
-        if k == 1:
-            beside = scalars, {s: cache(s) for s in range(targets - 1)}
-        if k == ring - 2:
-            first = tuple(range(ring - 1))
-            beside = prefill(prefill_q, [gathered[0, s] for s in first], first, needed, None)
-        if k == ring - 1:
-            final = (ring - 1,)
-            beside = prefill(prefill_q, [gathered[0, s] for s in final], final, needed, state)
+            beside = scalars, {s: cache(s) for s in range(targets)}
+        else:
+            slots = (0, 1) if k == 1 else (k,)
+            if k < ring:
+                mine = [gathered[0, s] for s in slots]
+                beside = prefill(prefill_q, mine, slots, needed, state, k == ring - 1)
         arrived, beside = lax.optimization_barrier((arrived, beside))
         if k == 0:
-            cached = {targets - 1: beside}
-        if k == 1:
-            scalars, others = beside
-            cached.update(others)
-        if k == ring - 2:
+            scalars, cached = beside
+        elif k < ring - 1:
             state = beside
-        if k == ring - 1:
+        elif k == ring - 1:
             prefill_out = beside
         gathered.update(zip(names, arrived))
         fresh = names
@@ -585,14 +593,14 @@
     pages = collect(pick, blocks)
     pieces = [None] * targets
     for s in reversed(range(targets)):
-        parts = math.gcd(2, requests // targets) if s else 1
+        parts = math.gcd(2, requests // targets)
         pieces[s] = []
-        if s == 0 and targets > 1:
-            sent = [p[0] for p in pieces[1:]]
-            cached[0], sent = lax.optimization_barrier((cached[0], sent))
-            for p, a in zip(pieces[1:], sent):
-                p[0] = a
         for part in range(parts):
+            if s == 0 and part == parts - 1 and targets > 1:
+                sent = [p[0] for p in pieces[1:]]
+                cached[0], sent = lax.optimization_barrier((cached[0], sent))
+                for p, a in zip(pieces[1:], sent):
+                    p[0] = a
             out = decode(
                 raw[0], *cached[s], pages, slot, meta, s, targets, part, parts, extra, steps, heads, group
             )

time: 88.9 us -> 91.5 us (1.029)
  the two profiles are of different devices: /device:TPU:24 before, /device:TPU:0 now
where the time goes in v13:
time: 91.5 us; the launch traced here: 91 us
  Pallas kernels  49.6 us (54%)
  waiting for transfers between devices  25.7 us (28%)
  starting transfers between devices  13 us (14%)
  local copies, waits for them, and re-layouts  1.04 us (1%)
  other arithmetic  0.93 us (1%)
    ppermute x15, waiting for transfers between devices, shards(): lax.ppermute(gathered[of], axis, pairs)  25.7 us
    pallas_call x4, Pallas kernels, decode(): pl.pallas_call(functools.partial(decode_kernel, extra, steps, target, tar...  16.3 us
    pallas_call x3, Pallas kernels, prefill(): pl.pallas_call(functools.partial(prefill_kernel, own, done, count, slots,...  16.2 us
    pallas_call x2, Pallas kernels, cache_part(): pl.pallas_call(functools.partial(cache_kernel, steps, heads, group, targe...  12.5 us
    ppermute x15, starting transfers between devices, shards(): lax.ppermute(gathered[of], axis, pairs)  10.8 us
    ppermute x2, starting transfers between devices, shards(): out = lax.ppermute(out, 'tp', shift)  2.16 us
  transfers between devices with their start and end apart: 17, of which 6 were waited for; matrix products, arithmetic and copies ran while one was open for 1% of the time, Pallas kernels for 45%

profile of v13, /device:TPU:0, one launch (start us, length us, event | category | flops | bytes accessed | tf_op | source)
XLA Modules:
  0.0 91.0 jit_solution(395666027577961749)
XLA Ops:
  0.6 1.5 %shard_map.113.refs_1_.refs_0_ = bf16[2,4,2,128,128]{4,3,2,1,0:T(8,128)(2,1)S(1)} custom-call(bf16[1024,128]{1,0:T(8,128)(2,1)} %bitcast.23, bf16[1024,128]{1,0:T(8,128)(2,1)} %bitcast.24), custom_call_target="tpu_custom_call" | custom-call | flops 100000000 | bytes 2000000 | tf_op jit(solution)/shard_map/pallas_call | solution.py:58
  2.1 4.1 %collective-permute-start.2 = (bf16[2,4,2,128,128]{4,3,2,1,0:T(8,128)(2,1)S(1)}, bf16[2,4,2,128,128]{4,3,2,1,0:T(8,128)(2,1)S(1)}, u32[]{:S(2)}, u32[]{:S(2)}) collective-permute-start(bf16[2,4,2,128,128]{4,3,2,1,0:T(8,128)(2,1)S(1)} %shard_map.113.refs_1_.refs_0_), channel_id=1, source_target_pairs={{0,4},{4,6},{6,2},{2,0},{1,5},{5,7},{7,3},{3,1},{8,12},{12,14},{14... | collective-permute-start | bytes 1572872 | tf_op jit(solution)/shard_map/ppermute | solution.py:572
  6.2 1.5 %collective-permute-start.1 = (bf16[2,4,2,128,128]{4,3,2,1,0:T(8,128)(2,1)S(1)}, bf16[2,4,2,128,128]{4,3,2,1,0:T(8,128)(2,1)S(1)}, u32[]{:S(2)}, u32[]{:S(2)}) collective-permute-start(bf16[2,4,2,128,128]{4,3,2,1,0:T(8,128)(2,1)S(1)} %shard_map.113.refs_1_.refs_0_), channel_id=1, source_target_pairs={{0,16},{8,24},{16,0},{24,8},{1,17},{9,25},{17,1},{25,9},{2,18},{10... | collective-permute-start | bytes 1572872 | tf_op jit(solution)/shard_map/ppermute | solution.py:572
  7.7 0.7 add_select_fusion
  8.5 0.1 pad_add_fusion.meta_ref
  8.5 0.1 copy.20
  8.6 0.1 broadcast_in_dim.15
  8.7 0.1 copy.19
  8.8 0.1 reshape.34.slot_ref
  8.9 0.1 select_reduce_fusion.pick_ref
  9.1 0.0 copy-start
  9.1 0.6 copy-done
  9.7 6.2 %shard_map.115 = (f32[16,128,128]{2,1,0:T(8,128)S(1)}, f32[16,8,128]{2,1,0:T(8,128)S(1)}) custom-call(s32[32]{0:T(128)S(1)} %copy-done, s32[2]{0:T(128)S(1)} %pad_add_fusion.meta_ref, bf16[32,128,128]{2,1,0:T(8,128)(2,1)} %bitcast.9, bf16[32,16,128]{2,1,0:T(8,128)(2,1)} %bitcast.19, bf16[32,16,128]{2,1,0:T(8,128)(2,1)} %bitcast.21, ...), custom_call_target="tpu_custom_call" | custom-call | flops 2147483648 | bytes 7000000 | tf_op jit(solution)/shard_map/pallas_call | solution.py:307
  16.0 6.3 %shard_map.114 = (f32[16,128,128]{2,1,0:T(8,128)S(1)}, f32[16,8,128]{2,1,0:T(8,128)S(1)}) custom-call(s32[32]{0:T(128)S(1)} %copy-done, s32[2]{0:T(128)S(1)} %pad_add_fusion.meta_ref, bf16[32,128,128]{2,1,0:T(8,128)(2,1)} %bitcast.10, bf16[32,16,128]{2,1,0:T(8,128)(2,1)} %bitcast.20, bf16[32,16,128]{2,1,0:T(8,128)(2,1)} %bitcast.22, ...), custom_call_target="tpu_custom_call" | custom-call | flops 2147483648 | bytes 7000000 | tf_op jit(solution)/shard_map/pallas_call | solution.py:307
  22.2 0.0 collective-permute-done.2.refs_2_.refs_1_
  22.2 0.0 collective-permute-done.refs_4_
  22.3 1.6 %collective-permute-start.6 = (bf16[2,4,2,128,128]{4,3,2,1,0:T(8,128)(2,1)S(1)}, bf16[2,4,2,128,128]{4,3,2,1,0:T(8,128)(2,1)S(1)}, u32[]{:S(2)}, u32[]{:S(2)}) collective-permute-start(bf16[2,4,2,128,128]{4,3,2,1,0:T(8,128)(2,1)S(1)} %collective-permute-done.2.refs_2_.refs_1_), channel_id=1, source_target_pairs={{0,4},{4,6},{6,2},{2,0},{1,5},{5,7},{7,3},{3,1},{8,12},{12,14},{14... | collective-permute-start | bytes 1572872 | tf_op jit(solution)/shard_map/ppermute | solution.py:572
  23.9 0.5 collective-permute-start.5
  24.4 0.0 collective-permute-start.4
  24.4 0.5 collective-permute-start.3
  24.9 5.7 %shard_map.116 = (f32[4,4,512,128]{3,2,1,0:T(8,128)S(1)}, f32[4,4,512,128]{3,2,1,0:T(8,128)S(1)}, f32[4,4,512,128]{3,2,1,0:T(8,128)S(1)}) custom-call(s32[4]{0:T(128)S(1)} %compare_convert_fusion.needed_ref, bf16[1,256,32,128]{3,2,1,0:T(8,128)(2,1)} %refs_0_.5, bf16[2,4,2,128,128]{4,3,2,1,0:T(8,128)(2,1)S(1)} %shard_map.113.refs_1_.refs_0_, ...), custom_call_target="tpu_custom_call" | custom-call | flops 8589934592 | bytes 12000000 | tf_op jit(solution)/shard_map/pallas_call | solution.py:213
  30.7 0.0 collective-permute-done.3.refs_12_
  30.7 6.0 %collective-permute-done.6.refs_1_.refs_2_ = bf16[2,4,2,128,128]{4,3,2,1,0:T(8,128)(2,1)S(1)} collective-permute-done((bf16[2,4,2,128,128]{4,3,2,1,0:T(8,128)(2,1)S(1)}, bf16[2,4,2,128,128]{4,3,2,1,0:T(8,128)(2,1)S(1)}, u32[]{:S(2)}, u32[]{:S(2)}) %collective-permute-start.6) | collective-permute-done | bytes 524320 | tf_op jit(solution)/shard_map/ppermute | solution.py:572
  36.6 1.3 %collective-permute-done.5.refs_9_ = bf16[2,4,2,128,128]{4,3,2,1,0:T(8,128)(2,1)S(1)} collective-permute-done((bf16[2,4,2,128,128]{4,3,2,1,0:T(8,128)(2,1)S(1)}, bf16[2,4,2,128,128]{4,3,2,1,0:T(8,128)(2,1)S(1)}, u32[]{:S(2)}, u32[]{:S(2)}) %collective-permute-start.5) | collective-permute-done | bytes 524320 | tf_op jit(solution)/shard_map/ppermute | solution.py:572
  37.9 0.0 collective-permute-done.4.refs_5_
  37.9 0.0 collective-permute-start.7
  37.9 1.2 %collective-permute-start.10 = (bf16[2,4,2,128,128]{4,3,2,1,0:T(8,128)(2,1)S(1)}, bf16[2,4,2,128,128]{4,3,2,1,0:T(8,128)(2,1)S(1)}, u32[]{:S(2)}, u32[]{:S(2)}) collective-permute-start(bf16[2,4,2,128,128]{4,3,2,1,0:T(8,128)(2,1)S(1)} %collective-permute-done.6.refs_1_.refs_2_), channel_id=1, source_target_pairs={{0,4},{4,6},{6,2},{2,0},{1,5},{5,7},{7,3},{3,1},{8,12},{12,14},{14... | collective-permute-start | bytes 1572872 | tf_op jit(solution)/shard_map/ppermute | solution.py:572
  39.2 0.5 collective-permute-start.9
  39.7 0.0 collective-permute-start.8
  39.7 4.3 %shard_map.117 = (f32[4,4,512,128]{3,2,1,0:T(8,128)S(1)}, f32[4,4,512,128]{3,2,1,0:T(8,128)S(1)}, f32[4,4,512,128]{3,2,1,0:T(8,128)S(1)}) custom-call(s32[4]{0:T(128)S(1)} %compare_convert_fusion.needed_ref, bf16[1,256,32,128]{3,2,1,0:T(8,128)(2,1)} %refs_0_.5, ...), custom_call_target="tpu_custom_call", output_to_operand_aliasing={{0}: (3, {}), {1}: (4, {}), {2}: (5, {})} | custom-call | flops 4294967296 | bytes 12000000 | tf_op jit(solution)/shard_map/pallas_call | solution.py:213
  44.1 0.0 collective-permute-done.7.refs_13_
  44.1 8.2 %collective-permute-done.10.refs_1_.refs_3_ = bf16[2,4,2,128,128]{4,3,2,1,0:T(8,128)(2,1)S(1)} collective-permute-done((bf16[2,4,2,128,128]{4,3,2,1,0:T(8,128)(2,1)S(1)}, bf16[2,4,2,128,128]{4,3,2,1,0:T(8,128)(2,1)S(1)}, u32[]{:S(2)}, u32[]{:S(2)}) %collective-permute-start.10) | collective-permute-done | bytes 524320 | tf_op jit(solution)/shard_map/ppermute | solution.py:572
  52.3 0.9 collective-permute-done.9.refs_10_
  53.2 0.5 collective-permute-start.13
  53.7 0.2 collective-permute-start.12
  54.0 6.1 %shard_map.118 = bf16[1,256,32,128]{3,2,1,0:T(8,128)(2,1)} custom-call(s32[4]{0:T(128)S(1)} %compare_convert_fusion.needed_ref, bf16[1,256,32,128]{3,2,1,0:T(8,128)(2,1)} %refs_0_.5, bf16[2,4,2,128,128]{4,3,2,1,0:T(8,128)(2,1)S(1)} %collective-permute-done.10.refs_1_.refs_3_, f32[4,4,512,128]{3,2,1,0:T(8,128)S(1)} %get-tuple-element.62.refs_2_, ...), custom_call_target="tpu_custom_call" | custom-call | flops 4294967296 | bytes 12000000 | tf_op jit(solution)/shard_map/pallas_call | solution.py:213
  60.1 7.4 %collective-permute-done.13.refs_11_ = bf16[2,4,2,128,128]{4,3,2,1,0:T(8,128)(2,1)S(1)} collective-permute-done((bf16[2,4,2,128,128]{4,3,2,1,0:T(8,128)(2,1)S(1)}, bf16[2,4,2,128,128]{4,3,2,1,0:T(8,128)(2,1)S(1)}, u32[]{:S(2)}, u32[]{:S(2)}) %collective-permute-start.13) | collective-permute-done | bytes 524320 | tf_op jit(solution)/shard_map/ppermute | solution.py:572
  67.5 0.0 collective-permute-done.12.refs_7_
  67.5 0.0 collective-permute-start.14
  67.5 1.9 %collective-permute-done.14.refs_15_ = bf16[2,4,2,128,128]{4,3,2,1,0:T(8,128)(2,1)S(1)} collective-permute-done((bf16[2,4,2,128,128]{4,3,2,1,0:T(8,128)(2,1)S(1)}, bf16[2,4,2,128,128]{4,3,2,1,0:T(8,128)(2,1)S(1)}, u32[]{:S(2)}, u32[]{:S(2)}) %collective-permute-start.14) | collective-permute-done | bytes 524320 | tf_op jit(solution)/shard_map/ppermute | solution.py:572
  69.5 1.2 %shard_map.119.refs_3_ = bf16[16,4,2,128,128]{4,3,2,1,0:T(8,128)(2,1)S(1)} custom-call(s32[16]{0:T(128)S(1)} %select_reduce_fusion.pick_ref, bf16[2,4,2,128,128]{4,3,2,1,0:T(8,128)(2,1)S(1)} %shard_map.113.refs_1_.refs_0_, bf16[2,4,2,128,128]{4,3,2,1,0:T(8,128)(2,1)S(1)} %collective-permute-done.2.refs_2_.refs_1_, ...), custom_call_target="tpu_custom_call" | custom-call | bytes 8000000 | tf_op jit(solution)/shard_map/pallas_call | solution.py:341
  70.7 4.1 %shard_map.121 = bf16[8,128,128]{2,1,0:T(8,128)(2,1)S(1)} custom-call(s32[128]{0:T(128)S(1)} %reshape.34.slot_ref, s32[2]{0:T(128)S(1)} %pad_add_fusion.meta_ref, bf16[32,128,128]{2,1,0:T(8,128)(2,1)} %bitcast.11, f32[16,128,128]{2,1,0:T(8,128)S(1)} %get-tuple-element.79.refs_1_, f32[16,8,128]{2,1,0:T(8,128)S(1)} %get-tuple-element.80.refs_2_, ...), custom_call_target="tpu_custom_call" | custom-call | flops 1000000 | bytes 1000000 | tf_op jit(solution)/shard_map/pallas_call | solution.py:429
  74.8 1.6 %collective-permute-start.15 = (bf16[8,128,128]{2,1,0:T(8,128)(2,1)S(1)}, bf16[8,128,128]{2,1,0:T(8,128)(2,1)S(1)}, u32[]{:S(2)}, u32[]{:S(2)}) collective-permute-start(bf16[8,128,128]{2,1,0:T(8,128)(2,1)S(1)} %shard_map.121), channel_id=1, source_target_pairs={{0,1},{1,0},{2,3},{3,2},{4,5},{5,4},{6,7},{7,6},{8,9},{9,8},{10,11... | collective-permute-start | bytes 786440 | tf_op jit(solution)/shard_map/ppermute | solution.py:609
  76.4 4.1 %shard_map.123 = bf16[8,128,128]{2,1,0:T(8,128)(2,1)S(1)} custom-call(s32[128]{0:T(128)S(1)} %reshape.34.slot_ref, s32[2]{0:T(128)S(1)} %pad_add_fusion.meta_ref, bf16[32,128,128]{2,1,0:T(8,128)(2,1)} %bitcast.12, f32[16,128,128]{2,1,0:T(8,128)S(1)} %get-tuple-element.79.refs_1_, f32[16,8,128]{2,1,0:T(8,128)S(1)} %get-tuple-element.80.refs_2_, ...), custom_call_target="tpu_custom_call" | custom-call | flops 1000000 | bytes 1000000 | tf_op jit(solution)/shard_map/pallas_call | solution.py:429
  80.4 0.6 collective-permute-start.16
  81.0 4.1 %shard_map.120.refs_0_ = bf16[8,128,128]{2,1,0:T(8,128)(2,1)S(1)} custom-call(s32[128]{0:T(128)S(1)} %reshape.34.slot_ref, s32[2]{0:T(128)S(1)} %pad_add_fusion.meta_ref, bf16[32,128,128]{2,1,0:T(8,128)(2,1)} %bitcast.13, f32[16,128,128]{2,1,0:T(8,128)S(1)} %get-tuple-element.81.refs_1_, f32[16,8,128]{2,1,0:T(8,128)S(1)} %get-tuple-element.82.refs_2_, ...), custom_call_target="tpu_custom_call" | custom-call | flops 1000000 | bytes 1000000 | tf_op jit(solution)/shard_map/pallas_call | solution.py:429
  85.1 4.1 %shard_map.122.refs_1_ = bf16[8,128,128]{2,1,0:T(8,128)(2,1)S(1)} custom-call(s32[128]{0:T(128)S(1)} %reshape.34.slot_ref, s32[2]{0:T(128)S(1)} %pad_add_fusion.meta_ref, bf16[32,128,128]{2,1,0:T(8,128)(2,1)} %bitcast.14, f32[16,128,128]{2,1,0:T(8,128)S(1)} %get-tuple-element.81.refs_1_, f32[16,8,128]{2,1,0:T(8,128)S(1)} %get-tuple-element.82.refs_2_, ...), custom_call_target="tpu_custom_call" | custom-call | flops 1000000 | bytes 1000000 | tf_op jit(solution)/shard_map/pallas_call | solution.py:429
  89.2 1.8 %shard_map.124 = bf16[16,4,8192]{2,1,0:T(4,128)(2,1)} custom-call(s32[2]{0:T(128)S(1)} %pad_add_fusion.meta_ref, bf16[8,128,128]{2,1,0:T(8,128)(2,1)S(1)} %shard_map.120.refs_0_, bf16[8,128,128]{2,1,0:T(8,128)(2,1)S(1)} %shard_map.122.refs_1_, bf16[8,128,128]{2,1,0:T(8,128)(2,1)S(1)} %collective-permute-done.15.refs_2_, ...), custom_call_target="tpu_custom_call" | custom-call | bytes 2000000 | tf_op jit(solution)/shard_map/pallas_call | solution.py:486
  (8 shorter events, 0.0 us)
Async XLA Ops:
  2.1 20.1 %collective-permute-start.2 = (bf16[2,4,2,128,128]{4,3,2,1,0:T(8,128)(2,1)S(1)}, bf16[2,4,2,128,128]{4,3,2,1,0:T(8,128)(2,1)S(1)}, u32[]{:S(2)}, u32[]{:S(2)}) collective-permute-start(bf16[2,4,2,128,128]{4,3,2,1,0:T(8,128)(2,1)S(1)} %shard_map.113.refs_1_.refs_0_), channel_id=1, source_target_pairs={{0,4},{4,6},{6,2},{2,0},{1,5},{5,7},{7,3},{3,1},{8,12},{12,14},{14... | collective-permute-start | bytes 1572872 | tf_op jit(solution)/shard_map/ppermute | solution.py:572
  6.2 16.0 %collective-permute-start.1 = (bf16[2,4,2,128,128]{4,3,2,1,0:T(8,128)(2,1)S(1)}, bf16[2,4,2,128,128]{4,3,2,1,0:T(8,128)(2,1)S(1)}, u32[]{:S(2)}, u32[]{:S(2)}) collective-permute-start(bf16[2,4,2,128,128]{4,3,2,1,0:T(8,128)(2,1)S(1)} %shard_map.113.refs_1_.refs_0_), channel_id=1, source_target_pairs={{0,16},{8,24},{16,0},{24,8},{1,17},{9,25},{17,1},{25,9},{2,18},{10... | collective-permute-start | bytes 1572872 | tf_op jit(solution)/shard_map/ppermute | solution.py:572
  7.7 14.5 %collective-permute-start = (bf16[2,4,2,128,128]{4,3,2,1,0:T(8,128)(2,1)S(1)}, bf16[2,4,2,128,128]{4,3,2,1,0:T(8,128)(2,1)S(1)}, u32[]{:S(2)}, u32[]{:S(2)}) collective-permute-start(bf16[2,4,2,128,128]{4,3,2,1,0:T(8,128)(2,1)S(1)} %shard_map.113.refs_1_.refs_0_), channel_id=1, source_target_pairs={{0,8},{8,0},{16,24},{24,16},{1,9},{9,1},{17,25},{25,17},{2,10},{10... | collective-permute-start | bytes 1572872 | tf_op jit(solution)/shard_map/ppermute | solution.py:572
  9.1 0.7 copy-start
  22.3 14.4 %collective-permute-start.6 = (bf16[2,4,2,128,128]{4,3,2,1,0:T(8,128)(2,1)S(1)}, bf16[2,4,2,128,128]{4,3,2,1,0:T(8,128)(2,1)S(1)}, u32[]{:S(2)}, u32[]{:S(2)}) collective-permute-start(bf16[2,4,2,128,128]{4,3,2,1,0:T(8,128)(2,1)S(1)} %collective-permute-done.2.refs_2_.refs_1_), channel_id=1, source_target_pairs={{0,4},{4,6},{6,2},{2,0},{1,5},{5,7},{7,3},{3,1},{8,12},{12,14},{14... | collective-permute-start | bytes 1572872 | tf_op jit(solution)/shard_map/ppermute | solution.py:572
  23.9 14.1 %collective-permute-start.5 = (bf16[2,4,2,128,128]{4,3,2,1,0:T(8,128)(2,1)S(1)}, bf16[2,4,2,128,128]{4,3,2,1,0:T(8,128)(2,1)S(1)}, u32[]{:S(2)}, u32[]{:S(2)}) collective-permute-start(bf16[2,4,2,128,128]{4,3,2,1,0:T(8,128)(2,1)S(1)} %collective-permute-done.2.refs_2_.refs_1_), channel_id=1, source_target_pairs={{0,16},{8,24},{16,0},{24,8},{1,17},{9,25},{17,1},{25,9},{2,18},{10... | collective-permute-start | bytes 1572872 | tf_op jit(solution)/shard_map/ppermute | solution.py:572
  24.4 13.5 %collective-permute-start.4 = (bf16[2,4,2,128,128]{4,3,2,1,0:T(8,128)(2,1)S(1)}, bf16[2,4,2,128,128]{4,3,2,1,0:T(8,128)(2,1)S(1)}, u32[]{:S(2)}, u32[]{:S(2)}) collective-permute-start(bf16[2,4,2,128,128]{4,3,2,1,0:T(8,128)(2,1)S(1)} %collective-permute-done.2.refs_2_.refs_1_), channel_id=1, source_target_pairs={{0,8},{8,0},{16,24},{24,16},{1,9},{9,1},{17,25},{25,17},{2,10},{10... | collective-permute-start | bytes 1572872 | tf_op jit(solution)/shard_map/ppermute | solution.py:572
  24.4 6.2 %collective-permute-start.3 = (bf16[2,4,2,128,128]{4,3,2,1,0:T(8,128)(2,1)S(1)}, bf16[2,4,2,128,128]{4,3,2,1,0:T(8,128)(2,1)S(1)}, u32[]{:S(2)}, u32[]{:S(2)}) collective-permute-start(bf16[2,4,2,128,128]{4,3,2,1,0:T(8,128)(2,1)S(1)} %collective-permute-done.1.refs_8_), channel_id=1, source_target_pairs={{0,8},{8,0},{16,24},{24,16},{1,9},{9,1},{17,25},{25,17},{2,10},{10... | collective-permute-start | bytes 1572872 | tf_op jit(solution)/shard_map/ppermute | solution.py:572
  37.9 6.1 %collective-permute-start.7 = (bf16[2,4,2,128,128]{4,3,2,1,0:T(8,128)(2,1)S(1)}, bf16[2,4,2,128,128]{4,3,2,1,0:T(8,128)(2,1)S(1)}, u32[]{:S(2)}, u32[]{:S(2)}) collective-permute-start(bf16[2,4,2,128,128]{4,3,2,1,0:T(8,128)(2,1)S(1)} %collective-permute-done.5.refs_9_), channel_id=1, source_target_pairs={{0,8},{8,0},{16,24},{24,16},{1,9},{9,1},{17,25},{25,17},{2,10},{10... | collective-permute-start | bytes 1572872 | tf_op jit(solution)/shard_map/ppermute | solution.py:572
  37.9 14.3 %collective-permute-start.10 = (bf16[2,4,2,128,128]{4,3,2,1,0:T(8,128)(2,1)S(1)}, bf16[2,4,2,128,128]{4,3,2,1,0:T(8,128)(2,1)S(1)}, u32[]{:S(2)}, u32[]{:S(2)}) collective-permute-start(bf16[2,4,2,128,128]{4,3,2,1,0:T(8,128)(2,1)S(1)} %collective-permute-done.6.refs_1_.refs_2_), channel_id=1, source_target_pairs={{0,4},{4,6},{6,2},{2,0},{1,5},{5,7},{7,3},{3,1},{8,12},{12,14},{14... | collective-permute-start | bytes 1572872 | tf_op jit(solution)/shard_map/ppermute | solution.py:572
  39.2 14.0 %collective-permute-start.9 = (bf16[2,4,2,128,128]{4,3,2,1,0:T(8,128)(2,1)S(1)}, bf16[2,4,2,128,128]{4,3,2,1,0:T(8,128)(2,1)S(1)}, u32[]{:S(2)}, u32[]{:S(2)}) collective-permute-start(bf16[2,4,2,128,128]{4,3,2,1,0:T(8,128)(2,1)S(1)} %collective-permute-done.6.refs_1_.refs_2_), channel_id=1, source_target_pairs={{0,16},{8,24},{16,0},{24,8},{1,17},{9,25},{17,1},{25,9},{2,18},{10... | collective-permute-start | bytes 1572872 | tf_op jit(solution)/shard_map/ppermute | solution.py:572
  39.7 13.5 %collective-permute-start.8 = (bf16[2,4,2,128,128]{4,3,2,1,0:T(8,128)(2,1)S(1)}, bf16[2,4,2,128,128]{4,3,2,1,0:T(8,128)(2,1)S(1)}, u32[]{:S(2)}, u32[]{:S(2)}) collective-permute-start(bf16[2,4,2,128,128]{4,3,2,1,0:T(8,128)(2,1)S(1)} %collective-permute-done.6.refs_1_.refs_2_), channel_id=1, source_target_pairs={{0,8},{8,0},{16,24},{24,16},{1,9},{9,1},{17,25},{25,17},{2,10},{10... | collective-permute-start | bytes 1572872 | tf_op jit(solution)/shard_map/ppermute | solution.py:572
  53.2 6.9 %collective-permute-start.11 = (bf16[2,4,2,128,128]{4,3,2,1,0:T(8,128)(2,1)S(1)}, bf16[2,4,2,128,128]{4,3,2,1,0:T(8,128)(2,1)S(1)}, u32[]{:S(2)}, u32[]{:S(2)}) collective-permute-start(bf16[2,4,2,128,128]{4,3,2,1,0:T(8,128)(2,1)S(1)} %collective-permute-done.9.refs_10_), channel_id=1, source_target_pairs={{0,8},{8,0},{16,24},{24,16},{1,9},{9,1},{17,25},{25,17},{2,10},{10... | collective-permute-start | bytes 1572872 | tf_op jit(solution)/shard_map/ppermute | solution.py:572
  53.2 14.3 %collective-permute-start.13 = (bf16[2,4,2,128,128]{4,3,2,1,0:T(8,128)(2,1)S(1)}, bf16[2,4,2,128,128]{4,3,2,1,0:T(8,128)(2,1)S(1)}, u32[]{:S(2)}, u32[]{:S(2)}) collective-permute-start(bf16[2,4,2,128,128]{4,3,2,1,0:T(8,128)(2,1)S(1)} %collective-permute-done.10.refs_1_.refs_3_), channel_id=1, source_target_pairs={{0,16},{8,24},{16,0},{24,8},{1,17},{9,25},{17,1},{25,9},{2,18},{10... | collective-permute-start | bytes 1572872 | tf_op jit(solution)/shard_map/ppermute | solution.py:572
  53.7 13.8 %collective-permute-start.12 = (bf16[2,4,2,128,128]{4,3,2,1,0:T(8,128)(2,1)S(1)}, bf16[2,4,2,128,128]{4,3,2,1,0:T(8,128)(2,1)S(1)}, u32[]{:S(2)}, u32[]{:S(2)}) collective-permute-start(bf16[2,4,2,128,128]{4,3,2,1,0:T(8,128)(2,1)S(1)} %collective-permute-done.10.refs_1_.refs_3_), channel_id=1, source_target_pairs={{0,8},{8,0},{16,24},{24,16},{1,9},{9,1},{17,25},{25,17},{2,10},{10... | collective-permute-start | bytes 1572872 | tf_op jit(solution)/shard_map/ppermute | solution.py:572
  67.5 1.9 %collective-permute-start.14 = (bf16[2,4,2,128,128]{4,3,2,1,0:T(8,128)(2,1)S(1)}, bf16[2,4,2,128,128]{4,3,2,1,0:T(8,128)(2,1)S(1)}, u32[]{:S(2)}, u32[]{:S(2)}) collective-permute-start(bf16[2,4,2,128,128]{4,3,2,1,0:T(8,128)(2,1)S(1)} %collective-permute-done.13.refs_11_), channel_id=1, source_target_pairs={{0,8},{8,0},{16,24},{24,16},{1,9},{9,1},{17,25},{25,17},{2,10},{10... | collective-permute-start | bytes 1572872 | tf_op jit(solution)/shard_map/ppermute | solution.py:572
  74.8 10.3 %collective-permute-start.15 = (bf16[8,128,128]{2,1,0:T(8,128)(2,1)S(1)}, bf16[8,128,128]{2,1,0:T(8,128)(2,1)S(1)}, u32[]{:S(2)}, u32[]{:S(2)}) collective-permute-start(bf16[8,128,128]{2,1,0:T(8,128)(2,1)S(1)} %shard_map.121), channel_id=1, source_target_pairs={{0,1},{1,0},{2,3},{3,2},{4,5},{5,4},{6,7},{7,6},{8,9},{9,8},{10,11... | collective-permute-start | bytes 786440 | tf_op jit(solution)/shard_map/ppermute | solution.py:609
  80.4 8.8 %collective-permute-start.16 = (bf16[8,128,128]{2,1,0:T(8,128)(2,1)S(1)}, bf16[8,128,128]{2,1,0:T(8,128)(2,1)S(1)}, u32[]{:S(2)}, u32[]{:S(2)}) collective-permute-start(bf16[8,128,128]{2,1,0:T(8,128)(2,1)S(1)} %shard_map.123), channel_id=1, source_target_pairs={{0,1},{1,0},{2,3},{3,2},{4,5},{5,4},{6,7},{7,6},{8,9},{9,8},{10,11... | collective-permute-start | bytes 786440 | tf_op jit(solution)/shard_map/ppermute | solution.py:609

commit v14 on v13

--- a/solution.py
+++ b/solution.py
@@ -233,7 +233,7 @@
 
 
 def cache_kernel(
-    steps, heads, group, target, targets, scale, len_ref, meta_ref, *refs
+    steps, heads, group, target, targets, part, parts, scale, len_ref, meta_ref, *refs
 ):
     q_ref, dk_ref, dv_ref, ck_ref, cv_ref, acc_ref, ml_ref = refs
     block, rows, width = q_ref.shape
@@ -254,7 +254,8 @@
     new_allowed = new_place <= step
     low = lax.broadcasted_iota(jnp.int32, (rows, width), 1) < 4
     i = pl.program_id(0)
-    first = (lax.rem(meta_ref[1] + target, targets) * pl.num_programs(0) + i) * block
+    place_here = lax.rem(meta_ref[1] + target, targets) * parts + part
+    first = (place_here * pl.num_programs(0) + i) * block
     unroll = math.gcd(4, block)
 
     def body(g, carry):
@@ -293,20 +294,28 @@
     lax.fori_loop(0, block // unroll, body, 0)
 
 
-def cache_part(q, dk, dv, ck, cv, lens, meta, target, targets, steps, heads, group):
+def cache_part(q, dk, dv, ck, cv, lens, meta, target, targets, part, parts, steps, heads, group):
     requests, rows, width = q.shape
-    per_target = requests // targets
-    block = math.gcd(8, per_target)
-    per_block = per_target // block
+    count = requests // targets // parts
+    block = math.gcd(4, count)
+    per_block = count // block
 
     def here(i, lens, meta):
-        return (lax.rem(meta[1] + target, targets) * per_block + i, 0, 0)
+        return ((lax.rem(meta[1] + target, targets) * parts + part) * per_block + i, 0, 0)
 
     spec = [pl.BlockSpec((block,) + a.shape[1:], here) for a in (q, dk, dv, ck, cv)]
-    shapes = [(per_target, width, rows), (per_target, 8, rows)]
+    shapes = [(count, width, rows), (count, 8, rows)]
     return pl.pallas_call(
         functools.partial(
-            cache_kernel, steps, heads, group, target, targets, LOG2E / math.sqrt(width)
+            cache_kernel,
+            steps,
+            heads,
+            group,
+            target,
+            targets,
+            part,
+            parts,
+            LOG2E / math.sqrt(width),
         ),
         grid_spec=pltpu.PrefetchScalarGridSpec(
             num_scalar_prefetch=2,
@@ -317,9 +326,9 @@
         out_shape=[pltpu.VMEM(a, jnp.float32) for a in shapes],
         compiler_params=params(),
         cost_estimate=pl.CostEstimate(
-            flops=per_target * rows * ck.shape[1] * width * 16,
+            flops=count * rows * ck.shape[1] * width * 16,
             bytes_accessed=7 * 10**6,
-            transcendentals=per_target * rows * ck.shape[1],
+            transcendentals=count * rows * ck.shape[1],
         ),
     )(lens, meta, *in_hbm(q, dk, dv, ck, cv))
 
@@ -359,8 +368,9 @@
     q_ref, acc_ref, ml_ref, buf, out_ref = refs
     block, lanes, width = q_ref.shape
     i = pl.program_id(0)
-    kept = (part * pl.num_programs(0) + i) * block
-    first = lax.rem(meta_ref[1] + target, targets) * (parts * pl.num_programs(0) * block) + kept
+    kept = i * block
+    place_here = lax.rem(meta_ref[1] + target, targets) * parts + part
+    first = place_here * pl.num_programs(0) * block + kept
 
     per_step = heads * group
     row_head = lax.broadcasted_iota(jnp.int32, (lanes, width), 0) % per_step // group
@@ -551,9 +561,12 @@
         a.reshape(requests, -1, width) for a in (decode_q, decode_k, decode_v, cache_k, cache_v)
     ]
 
-    def cache(target):
-        lens = cache_len.astype(jnp.int32)
-        return cache_part(*raw, lens, meta, target, targets, steps, heads, group)
+    parts = math.gcd(2, requests // targets)
+    lens = cache_len.astype(jnp.int32)
+    latest = (0, parts - 1)
+
+    def cache(where, arrays):
+        return cache_part(*arrays, lens, meta, where[0], targets, where[1], parts, steps, heads, group)
 
     gathered = {(0, 0): split_heads(prefill_k, prefill_v)}
     state = None
@@ -572,19 +585,23 @@
         arrived = [lax.ppermute(gathered[of], axis, pairs) for _, of, _, axis, pairs in sends]
         beside = ()
         if k == 0:
-            beside = scalars, {s: cache(s) for s in range(targets)}
+            pairs = [(s, part) for s in range(targets) for part in range(parts)]
+            beside = scalars, {w: cache(w, raw) for w in pairs if w != latest}
         else:
             slots = (0, 1) if k == 1 else (k,)
             if k < ring:
                 mine = [gathered[0, s] for s in slots]
                 beside = prefill(prefill_q, mine, slots, needed, state, k == ring - 1)
+            if k == ring - 1:
+                arrays, prefill_out = lax.optimization_barrier((raw, beside))
+                beside = prefill_out, cache(latest, arrays)
         arrived, beside = lax.optimization_barrier((arrived, beside))
         if k == 0:
             scalars, cached = beside
         elif k < ring - 1:
             state = beside
         elif k == ring - 1:
-            prefill_out = beside
+            prefill_out, cached[latest] = beside
         gathered.update(zip(names, arrived))
         fresh = names
 
@@ -593,16 +610,16 @@
     pages = collect(pick, blocks)
     pieces = [None] * targets
     for s in reversed(range(targets)):
-        parts = math.gcd(2, requests // targets)
         pieces[s] = []
         for part in range(parts):
-            if s == 0 and part == parts - 1 and targets > 1:
+            if (s, part) == latest and targets > 1:
                 sent = [p[0] for p in pieces[1:]]
-                cached[0], sent = lax.optimization_barrier((cached[0], sent))
+                cached[latest], sent = lax.optimization_barrier((cached[latest], sent))
                 for p, a in zip(pieces[1:], sent):
                     p[0] = a
+            state = cached[s, part]
             out = decode(
-                raw[0], *cached[s], pages, slot, meta, s, targets, part, parts, extra, steps, heads, group
+                raw[0], *state, pages, slot, meta, s, targets, part, parts, extra, steps, heads, group
             )
             if s:
                 shift = [(j, (j + s) % targets) for j in range(targets)]

time: 91.5 us -> 90.7 us (level)
  waiting for transfers between devices: 25.7 us -> 21.8 us
  Pallas kernels: 49.6 us -> 52.5 us
    ppermute x15, waiting for transfers between devices: 25.7 us -> 21.8 us  [shards(): lax.ppermute(gathered[of], axis, pairs)]
    pallas_call x2 -> x4, Pallas kernels: 12.5 us -> 15.5 us  [cache_part(): pl.pallas_call(functools.partial(cache_kernel, steps, heads, group, targe...]
  transfers between devices with their start and end apart: 17 -> 17, of which waited for: 6 -> 6; matrix products, arithmetic and copies ran while one was open for 1% -> 1% of each run, Pallas kernels for 45% -> 49%
where the time goes in v14:
time: 90.7 us; the launch traced here: 90.1 us
  Pallas kernels  52.5 us (58%)
  waiting for transfers between devices  21.8 us (24%)
  starting transfers between devices  13 us (14%)
  local copies, waits for them, and re-layouts  1.05 us (1%)
  other arithmetic  0.93 us (1%)
    ppermute x15, waiting for transfers between devices, shards(): lax.ppermute(gathered[of], axis, pairs)  21.8 us
    pallas_call x4, Pallas kernels, decode(): pl.pallas_call(functools.partial(decode_kernel, extra, steps, target, tar...  16.4 us
    pallas_call x3, Pallas kernels, prefill(): pl.pallas_call(functools.partial(prefill_kernel, own, done, count, slots,...  16.2 us
    pallas_call x4, Pallas kernels, cache_part(): pl.pallas_call(functools.partial(cache_kernel, steps, heads, group, targe...  15.5 us
    ppermute x15, starting transfers between devices, shards(): lax.ppermute(gathered[of], axis, pairs)  10.8 us
    ppermute x2, starting transfers between devices, shards(): out = lax.ppermute(out, 'tp', shift)  2.16 us
  transfers between devices with their start and end apart: 17, of which 6 were waited for; matrix products, arithmetic and copies ran while one was open for 1% of the time, Pallas kernels for 49%

profile of v14, /device:TPU:0, one launch (start us, length us, event | category | flops | bytes accessed | tf_op | source)
XLA Modules:
  0.0 90.1 jit_solution(16136520128579448334)
XLA Ops:
  0.6 1.5 %shard_map.113.refs_1_.refs_0_ = bf16[2,4,2,128,128]{4,3,2,1,0:T(8,128)(2,1)S(1)} custom-call(bf16[1024,128]{1,0:T(8,128)(2,1)} %bitcast.33, bf16[1024,128]{1,0:T(8,128)(2,1)} %bitcast.34), custom_call_target="tpu_custom_call" | custom-call | flops 100000000 | bytes 2000000 | tf_op jit(solution)/shard_map/pallas_call | solution.py:58
  2.1 4.1 %collective-permute-start.2 = (bf16[2,4,2,128,128]{4,3,2,1,0:T(8,128)(2,1)S(1)}, bf16[2,4,2,128,128]{4,3,2,1,0:T(8,128)(2,1)S(1)}, u32[]{:S(2)}, u32[]{:S(2)}) collective-permute-start(bf16[2,4,2,128,128]{4,3,2,1,0:T(8,128)(2,1)S(1)} %shard_map.113.refs_1_.refs_0_), channel_id=1, source_target_pairs={{0,4},{4,6},{6,2},{2,0},{1,5},{5,7},{7,3},{3,1},{8,12},{12,14},{14... | collective-permute-start | bytes 1572872 | tf_op jit(solution)/shard_map/ppermute | solution.py:585
  6.2 1.5 %collective-permute-start.1 = (bf16[2,4,2,128,128]{4,3,2,1,0:T(8,128)(2,1)S(1)}, bf16[2,4,2,128,128]{4,3,2,1,0:T(8,128)(2,1)S(1)}, u32[]{:S(2)}, u32[]{:S(2)}) collective-permute-start(bf16[2,4,2,128,128]{4,3,2,1,0:T(8,128)(2,1)S(1)} %shard_map.113.refs_1_.refs_0_), channel_id=1, source_target_pairs={{0,16},{8,24},{16,0},{24,8},{1,17},{9,25},{17,1},{25,9},{2,18},{10... | collective-permute-start | bytes 1572872 | tf_op jit(solution)/shard_map/ppermute | solution.py:585
  7.7 0.7 add_select_fusion
  8.4 0.1 copy.20
  8.5 0.1 broadcast_in_dim.15
  8.6 0.1 copy.19
  8.7 0.1 reshape.34.slot_ref
  8.8 0.1 pad_add_fusion.meta_ref
  8.9 0.7 copy-done
  9.6 3.9 %shard_map.116 = (f32[8,128,128]{2,1,0:T(8,128)S(1)}, f32[8,8,128]{2,1,0:T(8,128)S(1)}) custom-call(s32[32]{0:T(128)S(1)} %copy-done, s32[2]{0:T(128)S(1)} %pad_add_fusion.meta_ref, bf16[32,128,128]{2,1,0:T(8,128)(2,1)} %bitcast.9, bf16[32,16,128]{2,1,0:T(8,128)(2,1)} %bitcast.25, bf16[32,16,128]{2,1,0:T(8,128)(2,1)} %bitcast.29, ...), custom_call_target="tpu_custom_call" | custom-call | flops 1073741824 | bytes 7000000 | tf_op jit(solution)/shard_map/pallas_call | solution.py:308
  13.4 0.0 copy-start.1
  13.5 3.9 %shard_map.115 = (f32[8,128,128]{2,1,0:T(8,128)S(1)}, f32[8,8,128]{2,1,0:T(8,128)S(1)}) custom-call(s32[32]{0:T(128)S(1)} %copy-done, s32[2]{0:T(128)S(1)} %pad_add_fusion.meta_ref, bf16[32,128,128]{2,1,0:T(8,128)(2,1)} %bitcast.10, bf16[32,16,128]{2,1,0:T(8,128)(2,1)} %bitcast.26, bf16[32,16,128]{2,1,0:T(8,128)(2,1)} %bitcast.30, ...), custom_call_target="tpu_custom_call" | custom-call | flops 1073741824 | bytes 7000000 | tf_op jit(solution)/shard_map/pallas_call | solution.py:308
  17.3 3.9 %shard_map.114 = (f32[8,128,128]{2,1,0:T(8,128)S(1)}, f32[8,8,128]{2,1,0:T(8,128)S(1)}) custom-call(s32[32]{0:T(128)S(1)} %copy-done.1, s32[2]{0:T(128)S(1)} %pad_add_fusion.meta_ref, bf16[32,128,128]{2,1,0:T(8,128)(2,1)} %bitcast.11, bf16[32,16,128]{2,1,0:T(8,128)(2,1)} %bitcast.27, bf16[32,16,128]{2,1,0:T(8,128)(2,1)} %bitcast.31, ...), custom_call_target="tpu_custom_call" | custom-call | flops 1073741824 | bytes 7000000 | tf_op jit(solution)/shard_map/pallas_call | solution.py:308
  21.2 0.1 select_reduce_fusion.pick_ref
  21.4 0.0 collective-permute-done.1.refs_8_
  21.4 1.6 %collective-permute-start.6 = (bf16[2,4,2,128,128]{4,3,2,1,0:T(8,128)(2,1)S(1)}, bf16[2,4,2,128,128]{4,3,2,1,0:T(8,128)(2,1)S(1)}, u32[]{:S(2)}, u32[]{:S(2)}) collective-permute-start(bf16[2,4,2,128,128]{4,3,2,1,0:T(8,128)(2,1)S(1)} %collective-permute-done.2.refs_2_.refs_1_), channel_id=1, source_target_pairs={{0,4},{4,6},{6,2},{2,0},{1,5},{5,7},{7,3},{3,1},{8,12},{12,14},{14... | collective-permute-start | bytes 1572872 | tf_op jit(solution)/shard_map/ppermute | solution.py:585
  23.0 0.5 collective-permute-start.5
  23.5 0.0 collective-permute-start.4
  23.5 0.5 collective-permute-start.3
  24.0 5.7 %shard_map.117 = (f32[4,4,512,128]{3,2,1,0:T(8,128)S(1)}, f32[4,4,512,128]{3,2,1,0:T(8,128)S(1)}, f32[4,4,512,128]{3,2,1,0:T(8,128)S(1)}) custom-call(s32[4]{0:T(128)S(1)} %compare_convert_fusion.needed_ref, bf16[1,256,32,128]{3,2,1,0:T(8,128)(2,1)} %refs_0_.5, bf16[2,4,2,128,128]{4,3,2,1,0:T(8,128)(2,1)S(1)} %shard_map.113.refs_1_.refs_0_, ...), custom_call_target="tpu_custom_call" | custom-call | flops 8589934592 | bytes 12000000 | tf_op jit(solution)/shard_map/pallas_call | solution.py:213
  29.8 6.0 %collective-permute-done.6.refs_1_.refs_2_ = bf16[2,4,2,128,128]{4,3,2,1,0:T(8,128)(2,1)S(1)} collective-permute-done((bf16[2,4,2,128,128]{4,3,2,1,0:T(8,128)(2,1)S(1)}, bf16[2,4,2,128,128]{4,3,2,1,0:T(8,128)(2,1)S(1)}, u32[]{:S(2)}, u32[]{:S(2)}) %collective-permute-start.6) | collective-permute-done | bytes 524320 | tf_op jit(solution)/shard_map/ppermute | solution.py:585
  35.8 1.3 %collective-permute-done.5.refs_9_ = bf16[2,4,2,128,128]{4,3,2,1,0:T(8,128)(2,1)S(1)} collective-permute-done((bf16[2,4,2,128,128]{4,3,2,1,0:T(8,128)(2,1)S(1)}, bf16[2,4,2,128,128]{4,3,2,1,0:T(8,128)(2,1)S(1)}, u32[]{:S(2)}, u32[]{:S(2)}) %collective-permute-start.5) | collective-permute-done | bytes 524320 | tf_op jit(solution)/shard_map/ppermute | solution.py:585
  37.1 0.0 collective-permute-done.4.refs_5_
  37.1 0.0 collective-permute-start.7
  37.1 1.2 %collective-permute-start.10 = (bf16[2,4,2,128,128]{4,3,2,1,0:T(8,128)(2,1)S(1)}, bf16[2,4,2,128,128]{4,3,2,1,0:T(8,128)(2,1)S(1)}, u32[]{:S(2)}, u32[]{:S(2)}) collective-permute-start(bf16[2,4,2,128,128]{4,3,2,1,0:T(8,128)(2,1)S(1)} %collective-permute-done.6.refs_1_.refs_2_), channel_id=1, source_target_pairs={{0,4},{4,6},{6,2},{2,0},{1,5},{5,7},{7,3},{3,1},{8,12},{12,14},{14... | collective-permute-start | bytes 1572872 | tf_op jit(solution)/shard_map/ppermute | solution.py:585
  38.3 0.5 collective-permute-start.9
  38.8 4.3 %shard_map.118 = (f32[4,4,512,128]{3,2,1,0:T(8,128)S(1)}, f32[4,4,512,128]{3,2,1,0:T(8,128)S(1)}, f32[4,4,512,128]{3,2,1,0:T(8,128)S(1)}) custom-call(s32[4]{0:T(128)S(1)} %compare_convert_fusion.needed_ref, bf16[1,256,32,128]{3,2,1,0:T(8,128)(2,1)} %refs_0_.5, ...), custom_call_target="tpu_custom_call", output_to_operand_aliasing={{0}: (3, {}), {1}: (4, {}), {2}: (5, {})} | custom-call | flops 4294967296 | bytes 12000000 | tf_op jit(solution)/shard_map/pallas_call | solution.py:213
  43.2 0.0 collective-permute-done.7.refs_13_
  43.2 8.2 %collective-permute-done.10.refs_1_.refs_3_ = bf16[2,4,2,128,128]{4,3,2,1,0:T(8,128)(2,1)S(1)} collective-permute-done((bf16[2,4,2,128,128]{4,3,2,1,0:T(8,128)(2,1)S(1)}, bf16[2,4,2,128,128]{4,3,2,1,0:T(8,128)(2,1)S(1)}, u32[]{:S(2)}, u32[]{:S(2)}) %collective-permute-start.10) | collective-permute-done | bytes 524320 | tf_op jit(solution)/shard_map/ppermute | solution.py:585
  51.4 0.9 %collective-permute-done.9.refs_10_ = bf16[2,4,2,128,128]{4,3,2,1,0:T(8,128)(2,1)S(1)} collective-permute-done((bf16[2,4,2,128,128]{4,3,2,1,0:T(8,128)(2,1)S(1)}, bf16[2,4,2,128,128]{4,3,2,1,0:T(8,128)(2,1)S(1)}, u32[]{:S(2)}, u32[]{:S(2)}) %collective-permute-start.9) | collective-permute-done | bytes 524320 | tf_op jit(solution)/shard_map/ppermute | solution.py:585
  52.3 0.0 collective-permute-done.8.refs_6_
  52.3 0.0 collective-permute-start.11
  52.3 0.5 collective-permute-start.13
  52.9 0.2 collective-permute-start.12
  53.1 6.1 %shard_map.119 = bf16[1,256,32,128]{3,2,1,0:T(8,128)(2,1)} custom-call(s32[4]{0:T(128)S(1)} %compare_convert_fusion.needed_ref, bf16[1,256,32,128]{3,2,1,0:T(8,128)(2,1)} %refs_0_.5, bf16[2,4,2,128,128]{4,3,2,1,0:T(8,128)(2,1)S(1)} %collective-permute-done.10.refs_1_.refs_3_, f32[4,4,512,128]{3,2,1,0:T(8,128)S(1)} %get-tuple-element.78.refs_2_, ...), custom_call_target="tpu_custom_call" | custom-call | flops 4294967296 | bytes 12000000 | tf_op jit(solution)/shard_map/pallas_call | solution.py:213
  59.2 3.9 %shard_map.120 = (f32[8,128,128]{2,1,0:T(8,128)S(1)}, f32[8,8,128]{2,1,0:T(8,128)S(1)}) custom-call(s32[32]{0:T(128)S(1)} %copy-done.1, s32[2]{0:T(128)S(1)} %pad_add_fusion.meta_ref, bf16[32,128,128]{2,1,0:T(8,128)(2,1)} %bitcast.12, bf16[32,16,128]{2,1,0:T(8,128)(2,1)} %bitcast.28, bf16[32,16,128]{2,1,0:T(8,128)(2,1)} %bitcast.32, ...), custom_call_target="tpu_custom_call" | custom-call | flops 1073741824 | bytes 7000000 | tf_op jit(solution)/shard_map/pallas_call | solution.py:308
  63.1 0.0 collective-permute-done.11.refs_14_
  63.1 3.5 %collective-permute-done.13.refs_11_ = bf16[2,4,2,128,128]{4,3,2,1,0:T(8,128)(2,1)S(1)} collective-permute-done((bf16[2,4,2,128,128]{4,3,2,1,0:T(8,128)(2,1)S(1)}, bf16[2,4,2,128,128]{4,3,2,1,0:T(8,128)(2,1)S(1)}, u32[]{:S(2)}, u32[]{:S(2)}) %collective-permute-start.13) | collective-permute-done | bytes 524320 | tf_op jit(solution)/shard_map/ppermute | solution.py:585
  66.7 1.9 %collective-permute-done.14.refs_15_ = bf16[2,4,2,128,128]{4,3,2,1,0:T(8,128)(2,1)S(1)} collective-permute-done((bf16[2,4,2,128,128]{4,3,2,1,0:T(8,128)(2,1)S(1)}, bf16[2,4,2,128,128]{4,3,2,1,0:T(8,128)(2,1)S(1)}, u32[]{:S(2)}, u32[]{:S(2)}) %collective-permute-start.14) | collective-permute-done | bytes 524320 | tf_op jit(solution)/shard_map/ppermute | solution.py:585
  68.6 1.2 %shard_map.121.refs_3_ = bf16[16,4,2,128,128]{4,3,2,1,0:T(8,128)(2,1)S(1)} custom-call(s32[16]{0:T(128)S(1)} %select_reduce_fusion.pick_ref, bf16[2,4,2,128,128]{4,3,2,1,0:T(8,128)(2,1)S(1)} %shard_map.113.refs_1_.refs_0_, bf16[2,4,2,128,128]{4,3,2,1,0:T(8,128)(2,1)S(1)} %collective-permute-done.2.refs_2_.refs_1_, ...), custom_call_target="tpu_custom_call" | custom-call | bytes 8000000 | tf_op jit(solution)/shard_map/pallas_call | solution.py:350
  69.8 4.1 %shard_map.123 = bf16[8,128,128]{2,1,0:T(8,128)(2,1)S(1)} custom-call(s32[128]{0:T(128)S(1)} %reshape.34.slot_ref, s32[2]{0:T(128)S(1)} %pad_add_fusion.meta_ref, bf16[32,128,128]{2,1,0:T(8,128)(2,1)} %bitcast.13, f32[8,128,128]{2,1,0:T(8,128)S(1)} %get-tuple-element.105.refs_1_, f32[8,8,128]{2,1,0:T(8,128)S(1)} %get-tuple-element.106.refs_2_, ...), custom_call_target="tpu_custom_call" | custom-call | flops 1000000 | bytes 1000000 | tf_op jit(solution)/shard_map/pallas_call | solution.py:439
  73.9 1.6 %collective-permute-start.15 = (bf16[8,128,128]{2,1,0:T(8,128)(2,1)S(1)}, bf16[8,128,128]{2,1,0:T(8,128)(2,1)S(1)}, u32[]{:S(2)}, u32[]{:S(2)}) collective-permute-start(bf16[8,128,128]{2,1,0:T(8,128)(2,1)S(1)} %shard_map.123), channel_id=1, source_target_pairs={{0,1},{1,0},{2,3},{3,2},{4,5},{5,4},{6,7},{7,6},{8,9},{9,8},{10,11... | collective-permute-start | bytes 786440 | tf_op jit(solution)/shard_map/ppermute | solution.py:626
  75.5 4.1 %shard_map.125 = bf16[8,128,128]{2,1,0:T(8,128)(2,1)S(1)} custom-call(s32[128]{0:T(128)S(1)} %reshape.34.slot_ref, s32[2]{0:T(128)S(1)} %pad_add_fusion.meta_ref, bf16[32,128,128]{2,1,0:T(8,128)(2,1)} %bitcast.14, f32[8,128,128]{2,1,0:T(8,128)S(1)} %get-tuple-element.110.refs_1_, f32[8,8,128]{2,1,0:T(8,128)S(1)} %get-tuple-element.111.refs_2_, ...), custom_call_target="tpu_custom_call" | custom-call | flops 1000000 | bytes 1000000 | tf_op jit(solution)/shard_map/pallas_call | solution.py:439
  79.6 0.6 collective-permute-start.16
  80.1 4.1 %shard_map.122.refs_0_ = bf16[8,128,128]{2,1,0:T(8,128)(2,1)S(1)} custom-call(s32[128]{0:T(128)S(1)} %reshape.34.slot_ref, s32[2]{0:T(128)S(1)} %pad_add_fusion.meta_ref, bf16[32,128,128]{2,1,0:T(8,128)(2,1)} %bitcast.15, f32[8,128,128]{2,1,0:T(8,128)S(1)} %get-tuple-element.92.refs_1_, f32[8,8,128]{2,1,0:T(8,128)S(1)} %get-tuple-element.93.refs_2_, ...), custom_call_target="tpu_custom_call" | custom-call | flops 1000000 | bytes 1000000 | tf_op jit(solution)/shard_map/pallas_call | solution.py:439
  84.2 4.1 %shard_map.124.refs_1_ = bf16[8,128,128]{2,1,0:T(8,128)(2,1)S(1)} custom-call(s32[128]{0:T(128)S(1)} %reshape.34.slot_ref, s32[2]{0:T(128)S(1)} %pad_add_fusion.meta_ref, bf16[32,128,128]{2,1,0:T(8,128)(2,1)} %bitcast.16, f32[8,128,128]{2,1,0:T(8,128)S(1)} %get-tuple-element.107.refs_1_, f32[8,8,128]{2,1,0:T(8,128)S(1)} %get-tuple-element.108.refs_2_, ...), custom_call_target="tpu_custom_call" | custom-call | flops 1000000 | bytes 1000000 | tf_op jit(solution)/shard_map/pallas_call | solution.py:439
  88.4 1.8 %shard_map.126 = bf16[16,4,8192]{2,1,0:T(4,128)(2,1)} custom-call(s32[2]{0:T(128)S(1)} %pad_add_fusion.meta_ref, bf16[8,128,128]{2,1,0:T(8,128)(2,1)S(1)} %shard_map.122.refs_0_, bf16[8,128,128]{2,1,0:T(8,128)(2,1)S(1)} %shard_map.124.refs_1_, bf16[8,128,128]{2,1,0:T(8,128)(2,1)S(1)} %collective-permute-done.15.refs_2_, ...), custom_call_target="tpu_custom_call" | custom-call | bytes 2000000 | tf_op jit(solution)/shard_map/pallas_call | solution.py:496
  (12 shorter events, 0.0 us)
Async XLA Ops:
  2.1 19.2 %collective-permute-start.2 = (bf16[2,4,2,128,128]{4,3,2,1,0:T(8,128)(2,1)S(1)}, bf16[2,4,2,128,128]{4,3,2,1,0:T(8,128)(2,1)S(1)}, u32[]{:S(2)}, u32[]{:S(2)}) collective-permute-start(bf16[2,4,2,128,128]{4,3,2,1,0:T(8,128)(2,1)S(1)} %shard_map.113.refs_1_.refs_0_), channel_id=1, source_target_pairs={{0,4},{4,6},{6,2},{2,0},{1,5},{5,7},{7,3},{3,1},{8,12},{12,14},{14... | collective-permute-start | bytes 1572872 | tf_op jit(solution)/shard_map/ppermute | solution.py:585
  6.2 15.1 %collective-permute-start.1 = (bf16[2,4,2,128,128]{4,3,2,1,0:T(8,128)(2,1)S(1)}, bf16[2,4,2,128,128]{4,3,2,1,0:T(8,128)(2,1)S(1)}, u32[]{:S(2)}, u32[]{:S(2)}) collective-permute-start(bf16[2,4,2,128,128]{4,3,2,1,0:T(8,128)(2,1)S(1)} %shard_map.113.refs_1_.refs_0_), channel_id=1, source_target_pairs={{0,16},{8,24},{16,0},{24,8},{1,17},{9,25},{17,1},{25,9},{2,18},{10... | collective-permute-start | bytes 1572872 | tf_op jit(solution)/shard_map/ppermute | solution.py:585
  7.7 13.6 %collective-permute-start = (bf16[2,4,2,128,128]{4,3,2,1,0:T(8,128)(2,1)S(1)}, bf16[2,4,2,128,128]{4,3,2,1,0:T(8,128)(2,1)S(1)}, u32[]{:S(2)}, u32[]{:S(2)}) collective-permute-start(bf16[2,4,2,128,128]{4,3,2,1,0:T(8,128)(2,1)S(1)} %shard_map.113.refs_1_.refs_0_), channel_id=1, source_target_pairs={{0,8},{8,0},{16,24},{24,16},{1,9},{9,1},{17,25},{25,17},{2,10},{10... | collective-permute-start | bytes 1572872 | tf_op jit(solution)/shard_map/ppermute | solution.py:585
  8.9 0.7 copy-start
  13.4 3.9 %copy-start.1 = (s32[32]{0:T(128)S(1)}, s32[32]{0:T(128)}, u32[]{:S(2)}) copy-start(s32[32]{0:T(128)} %len_ref.7) | copy-start | bytes 388
  21.4 14.4 %collective-permute-start.6 = (bf16[2,4,2,128,128]{4,3,2,1,0:T(8,128)(2,1)S(1)}, bf16[2,4,2,128,128]{4,3,2,1,0:T(8,128)(2,1)S(1)}, u32[]{:S(2)}, u32[]{:S(2)}) collective-permute-start(bf16[2,4,2,128,128]{4,3,2,1,0:T(8,128)(2,1)S(1)} %collective-permute-done.2.refs_2_.refs_1_), channel_id=1, source_target_pairs={{0,4},{4,6},{6,2},{2,0},{1,5},{5,7},{7,3},{3,1},{8,12},{12,14},{14... | collective-permute-start | bytes 1572872 | tf_op jit(solution)/shard_map/ppermute | solution.py:585
  23.0 14.1 %collective-permute-start.5 = (bf16[2,4,2,128,128]{4,3,2,1,0:T(8,128)(2,1)S(1)}, bf16[2,4,2,128,128]{4,3,2,1,0:T(8,128)(2,1)S(1)}, u32[]{:S(2)}, u32[]{:S(2)}) collective-permute-start(bf16[2,4,2,128,128]{4,3,2,1,0:T(8,128)(2,1)S(1)} %collective-permute-done.2.refs_2_.refs_1_), channel_id=1, source_target_pairs={{0,16},{8,24},{16,0},{24,8},{1,17},{9,25},{17,1},{25,9},{2,18},{10... | collective-permute-start | bytes 1572872 | tf_op jit(solution)/shard_map/ppermute | solution.py:585
  23.5 13.5 %collective-permute-start.4 = (bf16[2,4,2,128,128]{4,3,2,1,0:T(8,128)(2,1)S(1)}, bf16[2,4,2,128,128]{4,3,2,1,0:T(8,128)(2,1)S(1)}, u32[]{:S(2)}, u32[]{:S(2)}) collective-permute-start(bf16[2,4,2,128,128]{4,3,2,1,0:T(8,128)(2,1)S(1)} %collective-permute-done.2.refs_2_.refs_1_), channel_id=1, source_target_pairs={{0,8},{8,0},{16,24},{24,16},{1,9},{9,1},{17,25},{25,17},{2,10},{10... | collective-permute-start | bytes 1572872 | tf_op jit(solution)/shard_map/ppermute | solution.py:585
  23.5 6.3 %collective-permute-start.3 = (bf16[2,4,2,128,128]{4,3,2,1,0:T(8,128)(2,1)S(1)}, bf16[2,4,2,128,128]{4,3,2,1,0:T(8,128)(2,1)S(1)}, u32[]{:S(2)}, u32[]{:S(2)}) collective-permute-start(bf16[2,4,2,128,128]{4,3,2,1,0:T(8,128)(2,1)S(1)} %collective-permute-done.1.refs_8_), channel_id=1, source_target_pairs={{0,8},{8,0},{16,24},{24,16},{1,9},{9,1},{17,25},{25,17},{2,10},{10... | collective-permute-start | bytes 1572872 | tf_op jit(solution)/shard_map/ppermute | solution.py:585
  37.1 6.1 %collective-permute-start.7 = (bf16[2,4,2,128,128]{4,3,2,1,0:T(8,128)(2,1)S(1)}, bf16[2,4,2,128,128]{4,3,2,1,0:T(8,128)(2,1)S(1)}, u32[]{:S(2)}, u32[]{:S(2)}) collective-permute-start(bf16[2,4,2,128,128]{4,3,2,1,0:T(8,128)(2,1)S(1)} %collective-permute-done.5.refs_9_), channel_id=1, source_target_pairs={{0,8},{8,0},{16,24},{24,16},{1,9},{9,1},{17,25},{25,17},{2,10},{10... | collective-permute-start | bytes 1572872 | tf_op jit(solution)/shard_map/ppermute | solution.py:585
  37.1 14.3 %collective-permute-start.10 = (bf16[2,4,2,128,128]{4,3,2,1,0:T(8,128)(2,1)S(1)}, bf16[2,4,2,128,128]{4,3,2,1,0:T(8,128)(2,1)S(1)}, u32[]{:S(2)}, u32[]{:S(2)}) collective-permute-start(bf16[2,4,2,128,128]{4,3,2,1,0:T(8,128)(2,1)S(1)} %collective-permute-done.6.refs_1_.refs_2_), channel_id=1, source_target_pairs={{0,4},{4,6},{6,2},{2,0},{1,5},{5,7},{7,3},{3,1},{8,12},{12,14},{14... | collective-permute-start | bytes 1572872 | tf_op jit(solution)/shard_map/ppermute | solution.py:585
  38.3 14.0 %collective-permute-start.9 = (bf16[2,4,2,128,128]{4,3,2,1,0:T(8,128)(2,1)S(1)}, bf16[2,4,2,128,128]{4,3,2,1,0:T(8,128)(2,1)S(1)}, u32[]{:S(2)}, u32[]{:S(2)}) collective-permute-start(bf16[2,4,2,128,128]{4,3,2,1,0:T(8,128)(2,1)S(1)} %collective-permute-done.6.refs_1_.refs_2_), channel_id=1, source_target_pairs={{0,16},{8,24},{16,0},{24,8},{1,17},{9,25},{17,1},{25,9},{2,18},{10... | collective-permute-start | bytes 1572872 | tf_op jit(solution)/shard_map/ppermute | solution.py:585
  38.8 13.5 %collective-permute-start.8 = (bf16[2,4,2,128,128]{4,3,2,1,0:T(8,128)(2,1)S(1)}, bf16[2,4,2,128,128]{4,3,2,1,0:T(8,128)(2,1)S(1)}, u32[]{:S(2)}, u32[]{:S(2)}) collective-permute-start(bf16[2,4,2,128,128]{4,3,2,1,0:T(8,128)(2,1)S(1)} %collective-permute-done.6.refs_1_.refs_2_), channel_id=1, source_target_pairs={{0,8},{8,0},{16,24},{24,16},{1,9},{9,1},{17,25},{25,17},{2,10},{10... | collective-permute-start | bytes 1572872 | tf_op jit(solution)/shard_map/ppermute | solution.py:585
  52.3 10.8 %collective-permute-start.11 = (bf16[2,4,2,128,128]{4,3,2,1,0:T(8,128)(2,1)S(1)}, bf16[2,4,2,128,128]{4,3,2,1,0:T(8,128)(2,1)S(1)}, u32[]{:S(2)}, u32[]{:S(2)}) collective-permute-start(bf16[2,4,2,128,128]{4,3,2,1,0:T(8,128)(2,1)S(1)} %collective-permute-done.9.refs_10_), channel_id=1, source_target_pairs={{0,8},{8,0},{16,24},{24,16},{1,9},{9,1},{17,25},{25,17},{2,10},{10... | collective-permute-start | bytes 1572872 | tf_op jit(solution)/shard_map/ppermute | solution.py:585
  52.3 14.3 %collective-permute-start.13 = (bf16[2,4,2,128,128]{4,3,2,1,0:T(8,128)(2,1)S(1)}, bf16[2,4,2,128,128]{4,3,2,1,0:T(8,128)(2,1)S(1)}, u32[]{:S(2)}, u32[]{:S(2)}) collective-permute-start(bf16[2,4,2,128,128]{4,3,2,1,0:T(8,128)(2,1)S(1)} %collective-permute-done.10.refs_1_.refs_3_), channel_id=1, source_target_pairs={{0,16},{8,24},{16,0},{24,8},{1,17},{9,25},{17,1},{25,9},{2,18},{10... | collective-permute-start | bytes 1572872 | tf_op jit(solution)/shard_map/ppermute | solution.py:585
  52.9 13.8 %collective-permute-start.12 = (bf16[2,4,2,128,128]{4,3,2,1,0:T(8,128)(2,1)S(1)}, bf16[2,4,2,128,128]{4,3,2,1,0:T(8,128)(2,1)S(1)}, u32[]{:S(2)}, u32[]{:S(2)}) collective-permute-start(bf16[2,4,2,128,128]{4,3,2,1,0:T(8,128)(2,1)S(1)} %collective-permute-done.10.refs_1_.refs_3_), channel_id=1, source_target_pairs={{0,8},{8,0},{16,24},{24,16},{1,9},{9,1},{17,25},{25,17},{2,10},{10... | collective-permute-start | bytes 1572872 | tf_op jit(solution)/shard_map/ppermute | solution.py:585
  66.7 1.9 %collective-permute-start.14 = (bf16[2,4,2,128,128]{4,3,2,1,0:T(8,128)(2,1)S(1)}, bf16[2,4,2,128,128]{4,3,2,1,0:T(8,128)(2,1)S(1)}, u32[]{:S(2)}, u32[]{:S(2)}) collective-permute-start(bf16[2,4,2,128,128]{4,3,2,1,0:T(8,128)(2,1)S(1)} %collective-permute-done.13.refs_11_), channel_id=1, source_target_pairs={{0,8},{8,0},{16,24},{24,16},{1,9},{9,1},{17,25},{25,17},{2,10},{10... | collective-permute-start | bytes 1572872 | tf_op jit(solution)/shard_map/ppermute | solution.py:585
  73.9 10.3 %collective-permute-start.15 = (bf16[8,128,128]{2,1,0:T(8,128)(2,1)S(1)}, bf16[8,128,128]{2,1,0:T(8,128)(2,1)S(1)}, u32[]{:S(2)}, u32[]{:S(2)}) collective-permute-start(bf16[8,128,128]{2,1,0:T(8,128)(2,1)S(1)} %shard_map.123), channel_id=1, source_target_pairs={{0,1},{1,0},{2,3},{3,2},{4,5},{5,4},{6,7},{7,6},{8,9},{9,8},{10,11... | collective-permute-start | bytes 786440 | tf_op jit(solution)/shard_map/ppermute | solution.py:626
  79.6 8.8 %collective-permute-start.16 = (bf16[8,128,128]{2,1,0:T(8,128)(2,1)S(1)}, bf16[8,128,128]{2,1,0:T(8,128)(2,1)S(1)}, u32[]{:S(2)}, u32[]{:S(2)}) collective-permute-start(bf16[8,128,128]{2,1,0:T(8,128)(2,1)S(1)} %shard_map.125), channel_id=1, source_target_pairs={{0,1},{1,0},{2,3},{3,2},{4,5},{5,4},{6,7},{7,6},{8,9},{9,8},{10,11... | collective-permute-start | bytes 786440 | tf_op jit(solution)/shard_map/ppermute | solution.py:626

commit v15 on v12

--- a/solution.py
+++ b/solution.py
@@ -70,10 +70,10 @@
     refs = refs[1 + count :]
     i = pl.program_id(0)
     if own:
+        old_acc_ref, old_m_ref, old_l_ref, out_ref, buf, s_ref, acc_ref, m_ref, l_ref, sems = refs
+    else:
         acc_ref, m_ref, l_ref, buf, s_ref, sems = refs
         acc_ref, m_ref, l_ref = acc_ref.at[i], m_ref.at[i], l_ref.at[i]
-    else:
-        old_acc_ref, old_m_ref, old_l_ref, out_ref, buf, s_ref, acc_ref, m_ref, l_ref, sems = refs
     pages, heads = blocks[0].shape[:2]
     block = q_ref.shape[1]
     rest = range(1 if own else 0, count)
@@ -126,14 +126,19 @@
 
     last = count - 1
     if own:
-        for n, (h, at) in enumerate(parts):
-            row = lax.broadcasted_iota(jnp.int32, (piece, tokens), 0) + n * piece % rows
-            allowed = lax.broadcasted_iota(jnp.int32, (piece, tokens), 1) <= row // group + i * block
-            s = jnp.where(allowed, nt(q[n], keys(blocks[0], h)), NEG)
-            s_ref[last, h, at] = s
-            m_ref[h, at] = fold(s, jnp.maximum)
+        m_ref[...] = old_m_ref[i]
+        for j in range(pages):
+            @pl.when((i + 1) * block > j * PAGE)
+            def _():
+                for n, (h, at) in enumerate(parts):
+                    row = lax.broadcasted_iota(jnp.int32, (piece, PAGE), 0) + n * piece % rows
+                    column = lax.broadcasted_iota(jnp.int32, (piece, PAGE), 1) + j * PAGE
+                    s = nt(q[n], blocks[0][j, h, 0])
+                    s = jnp.where(column <= row // group + i * block, s, NEG)
+                    s_ref[last, h, at, pl.ds(j * PAGE, PAGE)] = s
+                    m_ref[h, at] = jnp.maximum(m_ref[h, at], s)
     else:
-        m_ref[...] = old_m_ref[i]
+        m_ref[...] = jnp.full(m_ref.shape, NEG, jnp.float32)
 
     def look(b, carry):
         for n, (h, at) in enumerate(parts):
@@ -148,14 +153,21 @@
         m = jnp.broadcast_to(jnp.max(m, axis=1, keepdims=True), m.shape)
         m_ref[h, at] = m
         if own:
-            p = weights(last, h, at, m)
-            l_ref[h, at] = functools.reduce(jnp.add, p)
-            p = jnp.concatenate([a.astype(jnp.bfloat16) for a in p], axis=1)
-            acc_ref[h, at] = nt(p, values(blocks[0], h))
-        else:
             share = jnp.exp2((old_m_ref[i, h, at] - m) * scale)
             l_ref[h, at] = old_l_ref[i, h, at] * share
             acc_ref[h, at] = old_acc_ref[i, h, at] * share
+        else:
+            l_ref[h, at] = jnp.zeros(m.shape, jnp.float32)
+            acc_ref[h, at] = jnp.zeros(m.shape, jnp.float32)
+    if own:
+        for j in range(pages):
+            @pl.when((i + 1) * block > j * PAGE)
+            def _():
+                for h, at in parts:
+                    p = s_ref[last, h, at, pl.ds(j * PAGE, PAGE)]
+                    p = jnp.exp2((p - m_ref[h, at]) * scale)
+                    l_ref[h, at] = l_ref[h, at] + p
+                    acc_ref[h, at] = acc_ref[h, at] + nt(p.astype(jnp.bfloat16), blocks[0][j, h, 1])
 
     def weigh(b, carry):
         for h, at in parts:
@@ -166,7 +178,7 @@
         return carry
 
     lax.fori_loop(0, total, weigh, 0)
-    if not own:
+    if own:
         out = []
         for h in range(heads):
             l = jnp.sum(l_ref[h], axis=1, keepdims=True)
@@ -176,7 +188,7 @@
 
 def prefill(q, blocks, slots, needed, state):
     _, tokens, q_heads, width = q.shape
-    own = state is None
+    own = state is not None
     count = len(blocks)
     heads = blocks[0].shape[1]
     group = q_heads // heads
@@ -191,13 +203,13 @@
         pltpu.VMEM((count, heads, rows, tokens), jnp.float32),
     ]
     if own:
-        in_specs = [q_spec, own_spec] + [any_spec] * (count - 1)
+        in_specs = [q_spec, own_spec] + [any_spec] * (count - 1) + [on_chip] * 3
+        out_specs, out_shape = q_spec, jax.ShapeDtypeStruct(q.shape, jnp.bfloat16)
+        scratch += [pltpu.VMEM((heads, rows, width), jnp.float32)] * 3
+    else:
+        in_specs = [q_spec] + [any_spec] * count
         out_specs, state = [on_chip] * 3, ()
         out_shape = [pltpu.VMEM((tokens // block, heads, rows, width), jnp.float32)] * 3
-    else:
-        in_specs = [q_spec] + [any_spec] * count + [on_chip] * 3
-        out_specs, out_shape = q_spec, jax.ShapeDtypeStruct(q.shape, jnp.bfloat16)
-        scratch += [pltpu.VMEM((heads, rows, width), jnp.float32)] * 3
     return pl.pallas_call(
         functools.partial(
             prefill_kernel, own, count, slots, group, tokens, LOG2E / math.sqrt(width)
@@ -562,11 +574,13 @@
         if k == 1:
             beside = scalars, {s: cache(s) for s in range(targets - 1)}
         if k == ring - 2:
-            first = tuple(range(ring - 1))
-            beside = prefill(prefill_q, [gathered[0, s] for s in first], first, needed, None)
+            slots = tuple(range(1, ring - 1))
+            mine = [gathered[0, s] for s in slots]
+            beside = prefill(prefill_q, mine, slots, needed, None)
         if k == ring - 1:
-            final = (ring - 1,)
-            beside = prefill(prefill_q, [gathered[0, s] for s in final], final, needed, state)
+            slots = (0, ring - 1)
+            mine = [gathered[0, s] for s in slots]
+            beside = prefill(prefill_q, mine, slots, needed, state)
         arrived, beside = lax.optimization_barrier((arrived, beside))
         if k == 0:
             cached = {targets - 1: beside}
@@ -585,14 +599,14 @@
     pages = collect(pick, blocks)
     pieces = [None] * targets
     for s in reversed(range(targets)):
-        parts = math.gcd(2, requests // targets) if s else 1
+        parts = math.gcd(2, requests // targets)
         pieces[s] = []
-        if s == 0 and targets > 1:
-            sent = [p[0] for p in pieces[1:]]
-            cached[0], sent = lax.optimization_barrier((cached[0], sent))
-            for p, a in zip(pieces[1:], sent):
-                p[0] = a
         for part in range(parts):
+            if s == 0 and part == parts - 1 and targets > 1:
+                sent = [p[0] for p in pieces[1:]]
+                cached[0], sent = lax.optimization_barrier((cached[0], sent))
+                for p, a in zip(pieces[1:], sent):
+                    p[0] = a
             out = decode(
                 raw[0], *cached[s], pages, slot, meta, s, targets, part, parts, extra, steps, heads, group
             )

time: 88.9 us -> 85.7 us (0.964)
  waiting for transfers between devices: 17 us -> 10.6 us
  Pallas kernels: 57.1 us -> 60.7 us
    ppermute x15, waiting for transfers between devices: 14.7 us -> 10.6 us  [shards(): lax.ppermute(gathered[of], axis, pairs)]
    ppermute x2, waiting for transfers between devices: 2.34 us -> 0.01 us  [shards(): out = lax.ppermute(out, 'tp', shift)]
    pallas_call x2, Pallas kernels: 24.5 us -> 26.6 us  [prefill(): pl.pallas_call(functools.partial(prefill_kernel, own, count, slots, group...]
    pallas_call x3 -> x4, Pallas kernels: 15 us -> 16.4 us  [decode(): pl.pallas_call(functools.partial(decode_kernel, extra, steps, target, tar...]
  transfers between devices with their start and end apart: 17 -> 17, of which waited for: 7 -> 5; matrix products, arithmetic and copies ran while one was open for 1% -> 1% of each run, Pallas kernels for 54% -> 60%
where the time goes in v15:
time: 85.7 us; the launch traced here: 85.3 us
  Pallas kernels  60.7 us (71%)
  starting transfers between devices  11.9 us (14%)
  waiting for transfers between devices  10.6 us (12%)
  local copies, waits for them, and re-layouts  1.05 us (1%)
    pallas_call x2, Pallas kernels, prefill(): pl.pallas_call(functools.partial(prefill_kernel, own, count, slots, group...  26.6 us
    pallas_call x4, Pallas kernels, decode(): pl.pallas_call(functools.partial(decode_kernel, extra, steps, target, tar...  16.4 us
    pallas_call x2, Pallas kernels, cache_part(): pl.pallas_call(functools.partial(cache_kernel, steps, heads, group, targe...  12.5 us
    ppermute x15, waiting for transfers between devices, shards(): lax.ppermute(gathered[of], axis, pairs)  10.6 us
    ppermute x15, starting transfers between devices, shards(): lax.ppermute(gathered[of], axis, pairs)  9.79 us
    ppermute x2, starting transfers between devices, shards(): out = lax.ppermute(out, 'tp', shift)  2.16 us
    pallas_call x1, Pallas kernels, collect(): pl.pallas_call(collect_kernel, grid_spec=pltpu.PrefetchScalarGridSpec(num...  1.95 us
    pallas_call x1, Pallas kernels, join(): pl.pallas_call(functools.partial(join_kernel, [len(parts) for parts in pi...  1.78 us
  transfers between devices with their start and end apart: 17, of which 5 were waited for; matrix products, arithmetic and copies ran while one was open for 1% of the time, Pallas kernels for 60%

profile of v15, /device:TPU:24, one launch (start us, length us, event | category | flops | bytes accessed | tf_op | source)
XLA Modules:
  0.0 85.3 jit_solution(12355694374736630845)
XLA Ops:
  0.6 1.5 %shard_map.113.refs_1_.refs_0_ = bf16[2,4,2,128,128]{4,3,2,1,0:T(8,128)(2,1)S(1)} custom-call(bf16[1024,128]{1,0:T(8,128)(2,1)} %bitcast.23, bf16[1024,128]{1,0:T(8,128)(2,1)} %bitcast.24), custom_call_target="tpu_custom_call" | custom-call | flops 100000000 | bytes 2000000 | tf_op jit(solution)/shard_map/pallas_call | solution.py:58
  2.1 0.4 collective-permute-start.2
  2.5 1.5 %collective-permute-start.1 = (bf16[2,4,2,128,128]{4,3,2,1,0:T(8,128)(2,1)S(1)}, bf16[2,4,2,128,128]{4,3,2,1,0:T(8,128)(2,1)S(1)}, u32[]{:S(2)}, u32[]{:S(2)}) collective-permute-start(bf16[2,4,2,128,128]{4,3,2,1,0:T(8,128)(2,1)S(1)} %shard_map.113.refs_1_.refs_0_), channel_id=1, source_target_pairs={{0,16},{8,24},{16,0},{24,8},{1,17},{9,25},{17,1},{25,9},{2,18},{10... | collective-permute-start | bytes 1572872 | tf_op jit(solution)/shard_map/ppermute | solution.py:570
  4.0 0.0 collective-permute-start
  4.0 0.1 pad_add_fusion.meta_ref
  4.1 0.7 copy-done
  4.8 6.2 %shard_map.114 = (f32[16,128,128]{2,1,0:T(8,128)S(1)}, f32[16,8,128]{2,1,0:T(8,128)S(1)}) custom-call(s32[32]{0:T(128)S(1)} %copy-done, s32[2]{0:T(128)S(1)} %pad_add_fusion.meta_ref, bf16[32,128,128]{2,1,0:T(8,128)(2,1)} %bitcast.9, bf16[32,16,128]{2,1,0:T(8,128)(2,1)} %bitcast.19, bf16[32,16,128]{2,1,0:T(8,128)(2,1)} %bitcast.21, ...), custom_call_target="tpu_custom_call" | custom-call | flops 2147483648 | bytes 7000000 | tf_op jit(solution)/shard_map/pallas_call | solution.py:306
  11.0 4.8 %collective-permute-done.2.refs_1_ = bf16[2,4,2,128,128]{4,3,2,1,0:T(8,128)(2,1)S(1)} collective-permute-done((bf16[2,4,2,128,128]{4,3,2,1,0:T(8,128)(2,1)S(1)}, bf16[2,4,2,128,128]{4,3,2,1,0:T(8,128)(2,1)S(1)}, u32[]{:S(2)}, u32[]{:S(2)}) %collective-permute-start.2) | collective-permute-done | bytes 524320 | tf_op jit(solution)/shard_map/ppermute | solution.py:570
  15.9 0.1 collective-permute-done.1.refs_8_
  15.9 0.0 collective-permute-done.refs_4_
  15.9 1.2 %collective-permute-start.6 = (bf16[2,4,2,128,128]{4,3,2,1,0:T(8,128)(2,1)S(1)}, bf16[2,4,2,128,128]{4,3,2,1,0:T(8,128)(2,1)}, u32[]{:S(2)}, u32[]{:S(2)}) collective-permute-start(bf16[2,4,2,128,128]{4,3,2,1,0:T(8,128)(2,1)S(1)} %collective-permute-done.2.refs_1_), channel_id=1, source_target_pairs={{0,4},{4,6},{6,2},{2,0},{1,5},{5,7},{7,3},{3,1},{8,12},{12,14},{14... | collective-permute-start | bytes 1572872 | tf_op jit(solution)/shard_map/ppermute | solution.py:570
  17.1 1.5 %collective-permute-start.5 = (bf16[2,4,2,128,128]{4,3,2,1,0:T(8,128)(2,1)S(1)}, bf16[2,4,2,128,128]{4,3,2,1,0:T(8,128)(2,1)}, u32[]{:S(2)}, u32[]{:S(2)}) collective-permute-start(bf16[2,4,2,128,128]{4,3,2,1,0:T(8,128)(2,1)S(1)} %collective-permute-done.2.refs_1_), channel_id=1, source_target_pairs={{0,16},{8,24},{16,0},{24,8},{1,17},{9,25},{17,1},{25,9},{2,18},{10... | collective-permute-start | bytes 1572872 | tf_op jit(solution)/shard_map/ppermute | solution.py:570
  18.6 0.0 collective-permute-start.4
  18.6 0.5 collective-permute-start.3
  19.1 0.1 copy.17
  19.2 0.1 broadcast_in_dim.15
  19.3 0.1 copy.16
  19.4 0.1 reshape.39.slot_ref
  19.6 0.1 select_reduce_fusion.pick_ref
  19.7 6.2 %shard_map.115 = (f32[16,128,128]{2,1,0:T(8,128)S(1)}, f32[16,8,128]{2,1,0:T(8,128)S(1)}) custom-call(s32[32]{0:T(128)S(1)} %copy-done.1, s32[2]{0:T(128)S(1)} %pad_add_fusion.meta_ref, bf16[32,128,128]{2,1,0:T(8,128)(2,1)} %bitcast.10, bf16[32,16,128]{2,1,0:T(8,128)(2,1)} %bitcast.20, bf16[32,16,128]{2,1,0:T(8,128)(2,1)} %bitcast.22, ...), custom_call_target="tpu_custom_call" | custom-call | flops 2147483648 | bytes 7000000 | tf_op jit(solution)/shard_map/pallas_call | solution.py:306
  25.9 0.0 collective-permute-done.3.refs_12_
  25.9 2.8 %collective-permute-done.6.refs_2_ = bf16[2,4,2,128,128]{4,3,2,1,0:T(8,128)(2,1)} collective-permute-done((bf16[2,4,2,128,128]{4,3,2,1,0:T(8,128)(2,1)S(1)}, bf16[2,4,2,128,128]{4,3,2,1,0:T(8,128)(2,1)}, u32[]{:S(2)}, u32[]{:S(2)}) %collective-permute-start.6) | collective-permute-done | bytes 524320 | tf_op jit(solution)/shard_map/ppermute | solution.py:570
  28.8 1.0 %collective-permute-done.5.refs_9_ = bf16[2,4,2,128,128]{4,3,2,1,0:T(8,128)(2,1)} collective-permute-done((bf16[2,4,2,128,128]{4,3,2,1,0:T(8,128)(2,1)S(1)}, bf16[2,4,2,128,128]{4,3,2,1,0:T(8,128)(2,1)}, u32[]{:S(2)}, u32[]{:S(2)}) %collective-permute-start.5) | collective-permute-done | bytes 524320 | tf_op jit(solution)/shard_map/ppermute | solution.py:570
  29.7 0.0 collective-permute-done.4.refs_5_
  29.7 1.5 %collective-permute-start.10 = (bf16[2,4,2,128,128]{4,3,2,1,0:T(8,128)(2,1)}, bf16[2,4,2,128,128]{4,3,2,1,0:T(8,128)(2,1)S(1)}, u32[]{:S(2)}, u32[]{:S(2)}) collective-permute-start(bf16[2,4,2,128,128]{4,3,2,1,0:T(8,128)(2,1)} %collective-permute-done.6.refs_2_), channel_id=1, source_target_pairs={{0,4},{4,6},{6,2},{2,0},{1,5},{5,7},{7,3},{3,1},{8,12},{12,14},{14... | collective-permute-start | bytes 1572872 | tf_op jit(solution)/shard_map/ppermute | solution.py:570
  31.3 1.5 %collective-permute-start.9 = (bf16[2,4,2,128,128]{4,3,2,1,0:T(8,128)(2,1)}, bf16[2,4,2,128,128]{4,3,2,1,0:T(8,128)(2,1)S(1)}, u32[]{:S(2)}, u32[]{:S(2)}) collective-permute-start(bf16[2,4,2,128,128]{4,3,2,1,0:T(8,128)(2,1)} %collective-permute-done.6.refs_2_), channel_id=1, source_target_pairs={{0,16},{8,24},{16,0},{24,8},{1,17},{9,25},{17,1},{25,9},{2,18},{10... | collective-permute-start | bytes 1572872 | tf_op jit(solution)/shard_map/ppermute | solution.py:570
  32.8 0.0 collective-permute-start.8
  32.8 0.5 collective-permute-start.7
  33.3 13.1 %shard_map.116 = (f32[4,4,512,128]{3,2,1,0:T(8,128)S(1)}, f32[4,4,512,128]{3,2,1,0:T(8,128)S(1)}, f32[4,4,512,128]{3,2,1,0:T(8,128)S(1)}) custom-call(s32[4]{0:T(128)S(1)} %compare_convert_fusion.needed_ref, bf16[1,256,32,128]{3,2,1,0:T(8,128)(2,1)} %refs_0_.3, bf16[2,4,2,128,128]{4,3,2,1,0:T(8,128)(2,1)S(1)} %collective-permute-done.2.refs_1_, ...), custom_call_target="tpu_custom_call" | custom-call | flops 8589934592 | bytes 12000000 | tf_op jit(solution)/shard_map/pallas_call | solution.py:213
  46.4 0.0 collective-permute-done.7.refs_13_
  46.4 0.0 collective-permute-done.10.refs_2_.refs_3_
  46.4 0.0 collective-permute-done.9.refs_10_
  46.5 0.0 collective-permute-done.8.refs_6_
  46.5 0.6 collective-permute-start.13
  47.1 0.5 collective-permute-start.11
  47.6 13.4 %shard_map.117 = bf16[1,256,32,128]{3,2,1,0:T(8,128)(2,1)} custom-call(s32[4]{0:T(128)S(1)} %compare_convert_fusion.needed_ref, bf16[1,256,32,128]{3,2,1,0:T(8,128)(2,1)} %refs_0_.3, bf16[2,4,2,128,128]{4,3,2,1,0:T(8,128)(2,1)S(1)} %shard_map.113.refs_1_.refs_0_, bf16[2,4,2,128,128]{4,3,2,1,0:T(8,128)(2,1)S(1)} %collective-permute-done.10.refs_2_.refs_3_, ...), custom_call_target="tpu_custom_call" | custom-call | flops 8589934592 | bytes 12000000 | tf_op jit(solution)/shard_map/pallas_call | solution.py:213
  61.0 0.0 collective-permute-done.11.refs_14_
  61.1 0.1 collective-permute-start.14
  61.1 1.9 %collective-permute-done.14.refs_15_ = bf16[2,4,2,128,128]{4,3,2,1,0:T(8,128)(2,1)S(1)} collective-permute-done((bf16[2,4,2,128,128]{4,3,2,1,0:T(8,128)(2,1)S(1)}, bf16[2,4,2,128,128]{4,3,2,1,0:T(8,128)(2,1)S(1)}, u32[]{:S(2)}, u32[]{:S(2)}) %collective-permute-start.14) | collective-permute-done | bytes 524320 | tf_op jit(solution)/shard_map/ppermute | solution.py:570
  63.0 2.0 %shard_map.118.refs_3_ = bf16[16,4,2,128,128]{4,3,2,1,0:T(8,128)(2,1)S(1)} custom-call(s32[16]{0:T(128)S(1)} %select_reduce_fusion.pick_ref, bf16[2,4,2,128,128]{4,3,2,1,0:T(8,128)(2,1)S(1)} %shard_map.113.refs_1_.refs_0_, bf16[2,4,2,128,128]{4,3,2,1,0:T(8,128)(2,1)S(1)} %collective-permute-done.2.refs_1_, ...), custom_call_target="tpu_custom_call" | custom-call | bytes 8000000 | tf_op jit(solution)/shard_map/pallas_call | solution.py:340
  65.0 4.1 %shard_map.120 = bf16[8,128,128]{2,1,0:T(8,128)(2,1)S(1)} custom-call(s32[128]{0:T(128)S(1)} %reshape.39.slot_ref, s32[2]{0:T(128)S(1)} %pad_add_fusion.meta_ref, bf16[32,128,128]{2,1,0:T(8,128)(2,1)} %bitcast.11, f32[16,128,128]{2,1,0:T(8,128)S(1)} %get-tuple-element.67.refs_1_, f32[16,8,128]{2,1,0:T(8,128)S(1)} %get-tuple-element.68.refs_2_, ...), custom_call_target="tpu_custom_call" | custom-call | flops 1000000 | bytes 1000000 | tf_op jit(solution)/shard_map/pallas_call | solution.py:428
  69.1 1.6 %collective-permute-start.15 = (bf16[8,128,128]{2,1,0:T(8,128)(2,1)S(1)}, bf16[8,128,128]{2,1,0:T(8,128)(2,1)S(1)}, u32[]{:S(2)}, u32[]{:S(2)}) collective-permute-start(bf16[8,128,128]{2,1,0:T(8,128)(2,1)S(1)} %shard_map.120), channel_id=1, source_target_pairs={{0,1},{1,0},{2,3},{3,2},{4,5},{5,4},{6,7},{7,6},{8,9},{9,8},{10,11... | collective-permute-start | bytes 786440 | tf_op jit(solution)/shard_map/ppermute | solution.py:615
  70.7 4.1 %shard_map.122 = bf16[8,128,128]{2,1,0:T(8,128)(2,1)S(1)} custom-call(s32[128]{0:T(128)S(1)} %reshape.39.slot_ref, s32[2]{0:T(128)S(1)} %pad_add_fusion.meta_ref, bf16[32,128,128]{2,1,0:T(8,128)(2,1)} %bitcast.12, f32[16,128,128]{2,1,0:T(8,128)S(1)} %get-tuple-element.67.refs_1_, f32[16,8,128]{2,1,0:T(8,128)S(1)} %get-tuple-element.68.refs_2_, ...), custom_call_target="tpu_custom_call" | custom-call | flops 1000000 | bytes 1000000 | tf_op jit(solution)/shard_map/pallas_call | solution.py:428
  74.8 0.6 collective-permute-start.16
  75.3 4.1 %shard_map.119.refs_0_ = bf16[8,128,128]{2,1,0:T(8,128)(2,1)S(1)} custom-call(s32[128]{0:T(128)S(1)} %reshape.39.slot_ref, s32[2]{0:T(128)S(1)} %pad_add_fusion.meta_ref, bf16[32,128,128]{2,1,0:T(8,128)(2,1)} %bitcast.13, f32[16,128,128]{2,1,0:T(8,128)S(1)} %get-tuple-element.69.refs_1_, f32[16,8,128]{2,1,0:T(8,128)S(1)} %get-tuple-element.70.refs_2_, ...), custom_call_target="tpu_custom_call" | custom-call | flops 1000000 | bytes 1000000 | tf_op jit(solution)/shard_map/pallas_call | solution.py:428
  79.4 4.1 %shard_map.121.refs_1_ = bf16[8,128,128]{2,1,0:T(8,128)(2,1)S(1)} custom-call(s32[128]{0:T(128)S(1)} %reshape.39.slot_ref, s32[2]{0:T(128)S(1)} %pad_add_fusion.meta_ref, bf16[32,128,128]{2,1,0:T(8,128)(2,1)} %bitcast.14, f32[16,128,128]{2,1,0:T(8,128)S(1)} %get-tuple-element.69.refs_1_, f32[16,8,128]{2,1,0:T(8,128)S(1)} %get-tuple-element.70.refs_2_, ...), custom_call_target="tpu_custom_call" | custom-call | flops 1000000 | bytes 1000000 | tf_op jit(solution)/shard_map/pallas_call | solution.py:428
  83.5 0.0 collective-permute-done.16.refs_3_
  83.6 1.8 %shard_map.123 = bf16[16,4,8192]{2,1,0:T(4,128)(2,1)} custom-call(s32[2]{0:T(128)S(1)} %pad_add_fusion.meta_ref, bf16[8,128,128]{2,1,0:T(8,128)(2,1)S(1)} %shard_map.119.refs_0_, bf16[8,128,128]{2,1,0:T(8,128)(2,1)S(1)} %shard_map.121.refs_1_, bf16[8,128,128]{2,1,0:T(8,128)(2,1)S(1)} %collective-permute-done.15.refs_2_, ...), custom_call_target="tpu_custom_call" | custom-call | bytes 2000000 | tf_op jit(solution)/shard_map/pallas_call | solution.py:485
  (11 shorter events, 0.1 us)
Async XLA Ops:
  2.1 13.7 %collective-permute-start.2 = (bf16[2,4,2,128,128]{4,3,2,1,0:T(8,128)(2,1)S(1)}, bf16[2,4,2,128,128]{4,3,2,1,0:T(8,128)(2,1)S(1)}, u32[]{:S(2)}, u32[]{:S(2)}) collective-permute-start(bf16[2,4,2,128,128]{4,3,2,1,0:T(8,128)(2,1)S(1)} %shard_map.113.refs_1_.refs_0_), channel_id=1, source_target_pairs={{0,4},{4,6},{6,2},{2,0},{1,5},{5,7},{7,3},{3,1},{8,12},{12,14},{14... | collective-permute-start | bytes 1572872 | tf_op jit(solution)/shard_map/ppermute | solution.py:570
  2.5 13.4 %collective-permute-start.1 = (bf16[2,4,2,128,128]{4,3,2,1,0:T(8,128)(2,1)S(1)}, bf16[2,4,2,128,128]{4,3,2,1,0:T(8,128)(2,1)S(1)}, u32[]{:S(2)}, u32[]{:S(2)}) collective-permute-start(bf16[2,4,2,128,128]{4,3,2,1,0:T(8,128)(2,1)S(1)} %shard_map.113.refs_1_.refs_0_), channel_id=1, source_target_pairs={{0,16},{8,24},{16,0},{24,8},{1,17},{9,25},{17,1},{25,9},{2,18},{10... | collective-permute-start | bytes 1572872 | tf_op jit(solution)/shard_map/ppermute | solution.py:570
  4.0 11.9 %collective-permute-start = (bf16[2,4,2,128,128]{4,3,2,1,0:T(8,128)(2,1)S(1)}, bf16[2,4,2,128,128]{4,3,2,1,0:T(8,128)(2,1)S(1)}, u32[]{:S(2)}, u32[]{:S(2)}) collective-permute-start(bf16[2,4,2,128,128]{4,3,2,1,0:T(8,128)(2,1)S(1)} %shard_map.113.refs_1_.refs_0_), channel_id=1, source_target_pairs={{0,8},{8,0},{16,24},{24,16},{1,9},{9,1},{17,25},{25,17},{2,10},{10... | collective-permute-start | bytes 1572872 | tf_op jit(solution)/shard_map/ppermute | solution.py:570
  4.1 0.7 copy-start
  4.8 14.3 %copy-start.2 = (s32[32,4]{0,1:T(4,128)S(1)}, s32[32,4]{0,1:T(4,128)}, u32[]{:S(2)}) copy-start(s32[32,4]{0,1:T(4,128)} %param.19) | copy-start | bytes 1540
  4.8 14.9 %copy-start.1 = (s32[32]{0:T(128)S(1)}, s32[32]{0:T(128)}, u32[]{:S(2)}) copy-start(s32[32]{0:T(128)} %len_ref.3) | copy-start | bytes 388
  15.9 12.8 %collective-permute-start.6 = (bf16[2,4,2,128,128]{4,3,2,1,0:T(8,128)(2,1)S(1)}, bf16[2,4,2,128,128]{4,3,2,1,0:T(8,128)(2,1)}, u32[]{:S(2)}, u32[]{:S(2)}) collective-permute-start(bf16[2,4,2,128,128]{4,3,2,1,0:T(8,128)(2,1)S(1)} %collective-permute-done.2.refs_1_), channel_id=1, source_target_pairs={{0,4},{4,6},{6,2},{2,0},{1,5},{5,7},{7,3},{3,1},{8,12},{12,14},{14... | collective-permute-start | bytes 1572872 | tf_op jit(solution)/shard_map/ppermute | solution.py:570
  17.1 12.6 %collective-permute-start.5 = (bf16[2,4,2,128,128]{4,3,2,1,0:T(8,128)(2,1)S(1)}, bf16[2,4,2,128,128]{4,3,2,1,0:T(8,128)(2,1)}, u32[]{:S(2)}, u32[]{:S(2)}) collective-permute-start(bf16[2,4,2,128,128]{4,3,2,1,0:T(8,128)(2,1)S(1)} %collective-permute-done.2.refs_1_), channel_id=1, source_target_pairs={{0,16},{8,24},{16,0},{24,8},{1,17},{9,25},{17,1},{25,9},{2,18},{10... | collective-permute-start | bytes 1572872 | tf_op jit(solution)/shard_map/ppermute | solution.py:570
  18.6 11.1 %collective-permute-start.4 = (bf16[2,4,2,128,128]{4,3,2,1,0:T(8,128)(2,1)S(1)}, bf16[2,4,2,128,128]{4,3,2,1,0:T(8,128)(2,1)}, u32[]{:S(2)}, u32[]{:S(2)}) collective-permute-start(bf16[2,4,2,128,128]{4,3,2,1,0:T(8,128)(2,1)S(1)} %collective-permute-done.2.refs_1_), channel_id=1, source_target_pairs={{0,8},{8,0},{16,24},{24,16},{1,9},{9,1},{17,25},{25,17},{2,10},{10... | collective-permute-start | bytes 1572872 | tf_op jit(solution)/shard_map/ppermute | solution.py:570
  18.6 7.3 %collective-permute-start.3 = (bf16[2,4,2,128,128]{4,3,2,1,0:T(8,128)(2,1)S(1)}, bf16[2,4,2,128,128]{4,3,2,1,0:T(8,128)(2,1)}, u32[]{:S(2)}, u32[]{:S(2)}) collective-permute-start(bf16[2,4,2,128,128]{4,3,2,1,0:T(8,128)(2,1)S(1)} %collective-permute-done.1.refs_8_), channel_id=1, source_target_pairs={{0,8},{8,0},{16,24},{24,16},{1,9},{9,1},{17,25},{25,17},{2,10},{10... | collective-permute-start | bytes 1572872 | tf_op jit(solution)/shard_map/ppermute | solution.py:570
  29.7 16.7 %collective-permute-start.10 = (bf16[2,4,2,128,128]{4,3,2,1,0:T(8,128)(2,1)}, bf16[2,4,2,128,128]{4,3,2,1,0:T(8,128)(2,1)S(1)}, u32[]{:S(2)}, u32[]{:S(2)}) collective-permute-start(bf16[2,4,2,128,128]{4,3,2,1,0:T(8,128)(2,1)} %collective-permute-done.6.refs_2_), channel_id=1, source_target_pairs={{0,4},{4,6},{6,2},{2,0},{1,5},{5,7},{7,3},{3,1},{8,12},{12,14},{14... | collective-permute-start | bytes 1572872 | tf_op jit(solution)/shard_map/ppermute | solution.py:570
  31.3 15.2 %collective-permute-start.9 = (bf16[2,4,2,128,128]{4,3,2,1,0:T(8,128)(2,1)}, bf16[2,4,2,128,128]{4,3,2,1,0:T(8,128)(2,1)S(1)}, u32[]{:S(2)}, u32[]{:S(2)}) collective-permute-start(bf16[2,4,2,128,128]{4,3,2,1,0:T(8,128)(2,1)} %collective-permute-done.6.refs_2_), channel_id=1, source_target_pairs={{0,16},{8,24},{16,0},{24,8},{1,17},{9,25},{17,1},{25,9},{2,18},{10... | collective-permute-start | bytes 1572872 | tf_op jit(solution)/shard_map/ppermute | solution.py:570
  32.8 13.7 %collective-permute-start.8 = (bf16[2,4,2,128,128]{4,3,2,1,0:T(8,128)(2,1)}, bf16[2,4,2,128,128]{4,3,2,1,0:T(8,128)(2,1)S(1)}, u32[]{:S(2)}, u32[]{:S(2)}) collective-permute-start(bf16[2,4,2,128,128]{4,3,2,1,0:T(8,128)(2,1)} %collective-permute-done.6.refs_2_), channel_id=1, source_target_pairs={{0,8},{8,0},{16,24},{24,16},{1,9},{9,1},{17,25},{25,17},{2,10},{10... | collective-permute-start | bytes 1572872 | tf_op jit(solution)/shard_map/ppermute | solution.py:570
  32.8 13.7 %collective-permute-start.7 = (bf16[2,4,2,128,128]{4,3,2,1,0:T(8,128)(2,1)}, bf16[2,4,2,128,128]{4,3,2,1,0:T(8,128)(2,1)S(1)}, u32[]{:S(2)}, u32[]{:S(2)}) collective-permute-start(bf16[2,4,2,128,128]{4,3,2,1,0:T(8,128)(2,1)} %collective-permute-done.5.refs_9_), channel_id=1, source_target_pairs={{0,8},{8,0},{16,24},{24,16},{1,9},{9,1},{17,25},{25,17},{2,10},{10... | collective-permute-start | bytes 1572872 | tf_op jit(solution)/shard_map/ppermute | solution.py:570
  46.5 14.6 %collective-permute-start.13 = (bf16[2,4,2,128,128]{4,3,2,1,0:T(8,128)(2,1)S(1)}, bf16[2,4,2,128,128]{4,3,2,1,0:T(8,128)(2,1)S(1)}, u32[]{:S(2)}, u32[]{:S(2)}) collective-permute-start(bf16[2,4,2,128,128]{4,3,2,1,0:T(8,128)(2,1)S(1)} %collective-permute-done.10.refs_2_.refs_3_), channel_id=1, source_target_pairs={{0,16},{8,24},{16,0},{24,8},{1,17},{9,25},{17,1},{25,9},{2,18},{10... | collective-permute-start | bytes 1572872 | tf_op jit(solution)/shard_map/ppermute | solution.py:570
  47.1 14.0 %collective-permute-start.12 = (bf16[2,4,2,128,128]{4,3,2,1,0:T(8,128)(2,1)S(1)}, bf16[2,4,2,128,128]{4,3,2,1,0:T(8,128)(2,1)S(1)}, u32[]{:S(2)}, u32[]{:S(2)}) collective-permute-start(bf16[2,4,2,128,128]{4,3,2,1,0:T(8,128)(2,1)S(1)} %collective-permute-done.10.refs_2_.refs_3_), channel_id=1, source_target_pairs={{0,8},{8,0},{16,24},{24,16},{1,9},{9,1},{17,25},{25,17},{2,10},{10... | collective-permute-start | bytes 1572872 | tf_op jit(solution)/shard_map/ppermute | solution.py:570
  47.1 13.9 %collective-permute-start.11 = (bf16[2,4,2,128,128]{4,3,2,1,0:T(8,128)(2,1)S(1)}, bf16[2,4,2,128,128]{4,3,2,1,0:T(8,128)(2,1)S(1)}, u32[]{:S(2)}, u32[]{:S(2)}) collective-permute-start(bf16[2,4,2,128,128]{4,3,2,1,0:T(8,128)(2,1)S(1)} %collective-permute-done.9.refs_10_), channel_id=1, source_target_pairs={{0,8},{8,0},{16,24},{24,16},{1,9},{9,1},{17,25},{25,17},{2,10},{10... | collective-permute-start | bytes 1572872 | tf_op jit(solution)/shard_map/ppermute | solution.py:570
  61.1 2.0 %collective-permute-start.14 = (bf16[2,4,2,128,128]{4,3,2,1,0:T(8,128)(2,1)S(1)}, bf16[2,4,2,128,128]{4,3,2,1,0:T(8,128)(2,1)S(1)}, u32[]{:S(2)}, u32[]{:S(2)}) collective-permute-start(bf16[2,4,2,128,128]{4,3,2,1,0:T(8,128)(2,1)S(1)} %collective-permute-done.13.refs_11_), channel_id=1, source_target_pairs={{0,8},{8,0},{16,24},{24,16},{1,9},{9,1},{17,25},{25,17},{2,10},{10... | collective-permute-start | bytes 1572872 | tf_op jit(solution)/shard_map/ppermute | solution.py:570
  69.1 10.3 %collective-permute-start.15 = (bf16[8,128,128]{2,1,0:T(8,128)(2,1)S(1)}, bf16[8,128,128]{2,1,0:T(8,128)(2,1)S(1)}, u32[]{:S(2)}, u32[]{:S(2)}) collective-permute-start(bf16[8,128,128]{2,1,0:T(8,128)(2,1)S(1)} %shard_map.120), channel_id=1, source_target_pairs={{0,1},{1,0},{2,3},{3,2},{4,5},{5,4},{6,7},{7,6},{8,9},{9,8},{10,11... | collective-permute-start | bytes 786440 | tf_op jit(solution)/shard_map/ppermute | solution.py:615
  74.8 8.8 %collective-permute-start.16 = (bf16[8,128,128]{2,1,0:T(8,128)(2,1)S(1)}, bf16[8,128,128]{2,1,0:T(8,128)(2,1)S(1)}, u32[]{:S(2)}, u32[]{:S(2)}) collective-permute-start(bf16[8,128,128]{2,1,0:T(8,128)(2,1)S(1)} %shard_map.122), channel_id=1, source_target_pairs={{0,1},{1,0},{2,3},{3,2},{4,5},{5,4},{6,7},{7,6},{8,9},{9,8},{10,11... | collective-permute-start | bytes 786440 | tf_op jit(solution)/shard_map/ppermute | solution.py:615

commit v16 on v15

--- a/solution.py
+++ b/solution.py
@@ -94,10 +94,6 @@
             @pl.when(flag == 1)
             def _():
                 copy.start()
-        for flag, copy in copies():
-            @pl.when(flag == 1)
-            def _():
-                copy.wait()
 
     rows = block * group
     piece = min(rows, 256)
@@ -139,6 +135,13 @@
                     m_ref[h, at] = jnp.maximum(m_ref[h, at], s)
     else:
         m_ref[...] = jnp.full(m_ref.shape, NEG, jnp.float32)
+
+    @pl.when(i == 0)
+    def _():
+        for flag, copy in copies():
+            @pl.when(flag == 1)
+            def _():
+                copy.wait()
 
     def look(b, carry):
         for n, (h, at) in enumerate(parts):
@@ -323,40 +326,44 @@
     )(lens, meta, *in_hbm(q, dk, dv, ck, cv))
 
 
-def collect_kernel(pick_ref, *refs):
-    blocks, out_ref, sems = refs[:-2], refs[-2], refs[-1]
+def collect_kernel(pick_ref, q_ref, *refs):
+    blocks, (out_ref, q_out_ref, sems) = refs[:-3], refs[-3:]
     copies = [
         pltpu.make_async_copy(block.at[pick_ref[s]], out_ref.at[s], sems.at[s])
         for s, block in enumerate(blocks)
     ]
+    copies.append(pltpu.make_async_copy(q_ref, q_out_ref, sems.at[len(blocks)]))
     for copy in copies:
         copy.start()
     for copy in copies:
         copy.wait()
 
 
-def collect(pick, blocks):
+def collect(pick, q, blocks):
     slots = len(blocks)
     return pl.pallas_call(
         collect_kernel,
         grid_spec=pltpu.PrefetchScalarGridSpec(
             num_scalar_prefetch=1,
             grid=(1,),
-            in_specs=[pl.BlockSpec(memory_space=pl.ANY)] * slots,
-            out_specs=pl.BlockSpec(memory_space=pltpu.VMEM),
-            scratch_shapes=[pltpu.SemaphoreType.DMA((slots,))],
-        ),
-        out_shape=pltpu.VMEM((slots,) + blocks[0].shape[1:], jnp.bfloat16),
+            in_specs=[pl.BlockSpec(memory_space=pl.ANY)] * (1 + slots),
+            out_specs=[pl.BlockSpec(memory_space=pltpu.VMEM)] * 2,
+            scratch_shapes=[pltpu.SemaphoreType.DMA((slots + 1,))],
+        ),
+        out_shape=[
+            pltpu.VMEM((slots,) + blocks[0].shape[1:], jnp.bfloat16),
+            pltpu.VMEM(q.shape, jnp.bfloat16),
+        ],
         compiler_params=params(),
         cost_estimate=pl.CostEstimate(flops=0, bytes_accessed=8 * 10**6, transcendentals=0),
-    )(pick, *blocks)
+    )(pick, *in_hbm(q), *blocks)
 
 
 def decode_kernel(
-    extra, steps, target, targets, part, parts, heads, group, scale, slot_ref, meta_ref, *refs
+    extra, steps, target, targets, part, parts, heads, group, block, scale, slot_ref, meta_ref, *refs
 ):
     q_ref, acc_ref, ml_ref, buf, out_ref = refs
-    block, lanes, width = q_ref.shape
+    lanes, width = q_ref.shape[1:]
     i = pl.program_id(0)
     kept = (part * pl.num_programs(0) + i) * block
     first = lax.rem(meta_ref[1] + target, targets) * (parts * pl.num_programs(0) * block) + kept
@@ -373,7 +380,7 @@
         scores = []
         for u in range(unroll):
             r = g * unroll + u
-            q = q_ref[r]
+            q = q_ref[first + r]
             places = [slot_ref[(first + r) * extra + j] for j in range(extra)]
             spread = jnp.concatenate([q * a for a in head_rows], axis=1)
             keys = [
@@ -409,7 +416,7 @@
                     found = mine if h + w == 0 else jnp.where(lane_head == h + w, mine, found)
             results.append((r, ((acc_ref[kept + r] * shrink + found) / l).astype(jnp.bfloat16)))
         for r, result in results:
-            out_ref[r] = nt(order, result).astype(jnp.bfloat16)
+            out_ref[i * block + r] = nt(order, result).astype(jnp.bfloat16)
         return carry
 
     lax.fori_loop(0, block // unroll, body, 0)
@@ -420,9 +427,6 @@
     count = requests // targets // parts
     block = math.gcd(16, count)
     per_block = count // block
-
-    def here(i, slot, meta):
-        return ((lax.rem(meta[1] + target, targets) * parts + part) * per_block + i, 0, 0)
 
     on_chip = pl.BlockSpec(memory_space=pltpu.VMEM)
     return pl.pallas_call(
@@ -436,20 +440,21 @@
             parts,
             heads,
             group,
+            block,
             LOG2E / math.sqrt(width),
         ),
         grid_spec=pltpu.PrefetchScalarGridSpec(
             num_scalar_prefetch=2,
             grid=(per_block,),
-            in_specs=[pl.BlockSpec((block,) + q.shape[1:], here)] + [on_chip] * 3,
-            out_specs=pl.BlockSpec((block, lanes, width), lambda i, *_: (i, 0, 0)),
-        ),
-        out_shape=jax.ShapeDtypeStruct((count, lanes, width), jnp.bfloat16),
+            in_specs=[on_chip] * 4,
+            out_specs=on_chip,
+        ),
+        out_shape=pltpu.VMEM((count, lanes, width), jnp.bfloat16),
         compiler_params=params(),
         cost_estimate=pl.CostEstimate(
             flops=10**6, bytes_accessed=10**6, transcendentals=0
         ),
-    )(slot, meta, *in_hbm(q), acc, ml, pages)
+    )(slot, meta, q, acc, ml, pages)
 
 
 def join_kernel(counts, steps, meta_ref, *refs):
@@ -487,7 +492,7 @@
         grid_spec=pltpu.PrefetchScalarGridSpec(
             num_scalar_prefetch=1,
             grid=(targets,),
-            in_specs=[pl.BlockSpec(a.shape, lambda k, *_: (0, 0, 0)) for a in flat],
+            in_specs=[pl.BlockSpec(memory_space=pltpu.VMEM)] * len(flat),
             out_specs=pl.BlockSpec((per_target, steps, half), lambda k, *_: (0, 0, k)),
         ),
         out_shape=jax.ShapeDtypeStruct((per_target, steps, half * targets), jnp.bfloat16),
@@ -596,7 +601,7 @@
 
     blocks = [gathered[r, s] for r in range(roles) for s in range(ring)]
     slot, pick, meta = scalars
-    pages = collect(pick, blocks)
+    pages, queries = collect(pick, raw[0], blocks)
     pieces = [None] * targets
     for s in reversed(range(targets)):
         parts = math.gcd(2, requests // targets)
@@ -608,7 +613,7 @@
                 for p, a in zip(pieces[1:], sent):
                     p[0] = a
             out = decode(
-                raw[0], *cached[s], pages, slot, meta, s, targets, part, parts, extra, steps, heads, group
+                queries, *cached[s], pages, slot, meta, s, targets, part, parts, extra, steps, heads, group
             )
             if s:
                 shift = [(j, (j + s) % targets) for j in range(targets)]

time: 85.7 us -> 84.6 us (0.987)
  Pallas kernels: 60.7 us -> 57.2 us
  waiting for transfers between devices: 10.6 us -> 13.1 us
    pallas_call x4, Pallas kernels: 16.4 us -> 12.5 us  [decode(): pl.pallas_call(functools.partial(decode_kernel, extra, steps, target, tar...]
    ppermute x2, waiting for transfers between devices: 0.01 us -> 2.45 us  [shards(): out = lax.ppermute(out, 'tp', shift)]
  transfers between devices with their start and end apart: 17 -> 17, of which waited for: 5 -> 7; matrix products, arithmetic and copies ran while one was open for 1% -> 1% of each run, Pallas kernels for 60% -> 57%
where the time goes in v16:
time: 84.6 us; the launch traced here: 84.3 us
  Pallas kernels  57.2 us (68%)
  waiting for transfers between devices  13.1 us (15%)
  starting transfers between devices  11.9 us (14%)
  local copies, waits for them, and re-layouts  1.05 us (1%)
    pallas_call x2, Pallas kernels, prefill(): pl.pallas_call(functools.partial(prefill_kernel, own, count, slots, group...  26.5 us
    pallas_call x4, Pallas kernels, decode(): pl.pallas_call(functools.partial(decode_kernel, extra, steps, target, tar...  12.5 us
    pallas_call x2, Pallas kernels, cache_part(): pl.pallas_call(functools.partial(cache_kernel, steps, heads, group, targe...  12.5 us
    ppermute x15, waiting for transfers between devices, shards(): lax.ppermute(gathered[of], axis, pairs)  10.6 us
    ppermute x15, starting transfers between devices, shards(): lax.ppermute(gathered[of], axis, pairs)  9.77 us
    ppermute x2, waiting for transfers between devices, shards(): out = lax.ppermute(out, 'tp', shift)  2.45 us
    pallas_call x1, Pallas kernels, collect(): pl.pallas_call(collect_kernel, grid_spec=pltpu.PrefetchScalarGridSpec(num...  2.44 us
    ppermute x2, starting transfers between devices, shards(): out = lax.ppermute(out, 'tp', shift)  2.16 us
  transfers between devices with their start and end apart: 17, of which 7 were waited for; matrix products, arithmetic and copies ran while one was open for 1% of the time, Pallas kernels for 57%

profile of v16, /device:TPU:24, one launch (start us, length us, event | category | flops | bytes accessed | tf_op | source)
XLA Modules:
  0.0 84.3 jit_solution(3803746679378865136)
XLA Ops:
  0.6 1.5 %shard_map.113.refs_1_.refs_0_ = bf16[2,4,2,128,128]{4,3,2,1,0:T(8,128)(2,1)S(1)} custom-call(bf16[1024,128]{1,0:T(8,128)(2,1)} %bitcast.20, bf16[1024,128]{1,0:T(8,128)(2,1)} %bitcast.21), custom_call_target="tpu_custom_call" | custom-call | flops 100000000 | bytes 2000000 | tf_op jit(solution)/shard_map/pallas_call | solution.py:58
  2.1 0.4 collective-permute-start.2
  2.5 1.5 %collective-permute-start.1 = (bf16[2,4,2,128,128]{4,3,2,1,0:T(8,128)(2,1)S(1)}, bf16[2,4,2,128,128]{4,3,2,1,0:T(8,128)(2,1)S(1)}, u32[]{:S(2)}, u32[]{:S(2)}) collective-permute-start(bf16[2,4,2,128,128]{4,3,2,1,0:T(8,128)(2,1)S(1)} %shard_map.113.refs_1_.refs_0_), channel_id=1, source_target_pairs={{0,16},{8,24},{16,0},{24,8},{1,17},{9,25},{17,1},{25,9},{2,18},{10... | collective-permute-start | bytes 1572872 | tf_op jit(solution)/shard_map/ppermute | solution.py:575
  4.0 0.0 collective-permute-start
  4.0 0.1 pad_add_fusion.meta_ref
  4.1 0.7 copy-done
  4.8 6.2 %shard_map.114 = (f32[16,128,128]{2,1,0:T(8,128)S(1)}, f32[16,8,128]{2,1,0:T(8,128)S(1)}) custom-call(s32[32]{0:T(128)S(1)} %copy-done, s32[2]{0:T(128)S(1)} %pad_add_fusion.meta_ref, bf16[32,128,128]{2,1,0:T(8,128)(2,1)} %bitcast.13, bf16[32,16,128]{2,1,0:T(8,128)(2,1)} %bitcast.16, bf16[32,16,128]{2,1,0:T(8,128)(2,1)} %bitcast.18, ...), custom_call_target="tpu_custom_call" | custom-call | flops 2147483648 | bytes 7000000 | tf_op jit(solution)/shard_map/pallas_call | solution.py:309
  11.0 4.8 %collective-permute-done.2.refs_1_ = bf16[2,4,2,128,128]{4,3,2,1,0:T(8,128)(2,1)S(1)} collective-permute-done((bf16[2,4,2,128,128]{4,3,2,1,0:T(8,128)(2,1)S(1)}, bf16[2,4,2,128,128]{4,3,2,1,0:T(8,128)(2,1)S(1)}, u32[]{:S(2)}, u32[]{:S(2)}) %collective-permute-start.2) | collective-permute-done | bytes 524320 | tf_op jit(solution)/shard_map/ppermute | solution.py:575
  15.9 0.1 collective-permute-done.1.refs_8_
  15.9 0.0 collective-permute-done.refs_4_
  15.9 1.2 %collective-permute-start.6 = (bf16[2,4,2,128,128]{4,3,2,1,0:T(8,128)(2,1)S(1)}, bf16[2,4,2,128,128]{4,3,2,1,0:T(8,128)(2,1)}, u32[]{:S(2)}, u32[]{:S(2)}) collective-permute-start(bf16[2,4,2,128,128]{4,3,2,1,0:T(8,128)(2,1)S(1)} %collective-permute-done.2.refs_1_), channel_id=1, source_target_pairs={{0,4},{4,6},{6,2},{2,0},{1,5},{5,7},{7,3},{3,1},{8,12},{12,14},{14... | collective-permute-start | bytes 1572872 | tf_op jit(solution)/shard_map/ppermute | solution.py:575
  17.1 1.5 %collective-permute-start.5 = (bf16[2,4,2,128,128]{4,3,2,1,0:T(8,128)(2,1)S(1)}, bf16[2,4,2,128,128]{4,3,2,1,0:T(8,128)(2,1)}, u32[]{:S(2)}, u32[]{:S(2)}) collective-permute-start(bf16[2,4,2,128,128]{4,3,2,1,0:T(8,128)(2,1)S(1)} %collective-permute-done.2.refs_1_), channel_id=1, source_target_pairs={{0,16},{8,24},{16,0},{24,8},{1,17},{9,25},{17,1},{25,9},{2,18},{10... | collective-permute-start | bytes 1572872 | tf_op jit(solution)/shard_map/ppermute | solution.py:575
  18.6 0.0 collective-permute-start.4
  18.6 0.5 collective-permute-start.3
  19.1 0.1 copy.17
  19.2 0.1 broadcast_in_dim.15
  19.3 0.1 copy.16
  19.4 0.1 reshape.39.slot_ref
  19.6 0.1 select_reduce_fusion.pick_ref
  19.7 6.2 %shard_map.115 = (f32[16,128,128]{2,1,0:T(8,128)S(1)}, f32[16,8,128]{2,1,0:T(8,128)S(1)}) custom-call(s32[32]{0:T(128)S(1)} %copy-done.1, s32[2]{0:T(128)S(1)} %pad_add_fusion.meta_ref, bf16[32,128,128]{2,1,0:T(8,128)(2,1)} %bitcast.14, bf16[32,16,128]{2,1,0:T(8,128)(2,1)} %bitcast.17, bf16[32,16,128]{2,1,0:T(8,128)(2,1)} %bitcast.19, ...), custom_call_target="tpu_custom_call" | custom-call | flops 2147483648 | bytes 7000000 | tf_op jit(solution)/shard_map/pallas_call | solution.py:309
  25.9 0.0 collective-permute-done.3.refs_12_
  25.9 2.8 %collective-permute-done.6.refs_2_ = bf16[2,4,2,128,128]{4,3,2,1,0:T(8,128)(2,1)} collective-permute-done((bf16[2,4,2,128,128]{4,3,2,1,0:T(8,128)(2,1)S(1)}, bf16[2,4,2,128,128]{4,3,2,1,0:T(8,128)(2,1)}, u32[]{:S(2)}, u32[]{:S(2)}) %collective-permute-start.6) | collective-permute-done | bytes 524320 | tf_op jit(solution)/shard_map/ppermute | solution.py:575
  28.8 1.0 %collective-permute-done.5.refs_9_ = bf16[2,4,2,128,128]{4,3,2,1,0:T(8,128)(2,1)} collective-permute-done((bf16[2,4,2,128,128]{4,3,2,1,0:T(8,128)(2,1)S(1)}, bf16[2,4,2,128,128]{4,3,2,1,0:T(8,128)(2,1)}, u32[]{:S(2)}, u32[]{:S(2)}) %collective-permute-start.5) | collective-permute-done | bytes 524320 | tf_op jit(solution)/shard_map/ppermute | solution.py:575
  29.7 0.0 collective-permute-done.4.refs_5_
  29.7 1.5 %collective-permute-start.10 = (bf16[2,4,2,128,128]{4,3,2,1,0:T(8,128)(2,1)}, bf16[2,4,2,128,128]{4,3,2,1,0:T(8,128)(2,1)S(1)}, u32[]{:S(2)}, u32[]{:S(2)}) collective-permute-start(bf16[2,4,2,128,128]{4,3,2,1,0:T(8,128)(2,1)} %collective-permute-done.6.refs_2_), channel_id=1, source_target_pairs={{0,4},{4,6},{6,2},{2,0},{1,5},{5,7},{7,3},{3,1},{8,12},{12,14},{14... | collective-permute-start | bytes 1572872 | tf_op jit(solution)/shard_map/ppermute | solution.py:575
  31.3 1.5 %collective-permute-start.9 = (bf16[2,4,2,128,128]{4,3,2,1,0:T(8,128)(2,1)}, bf16[2,4,2,128,128]{4,3,2,1,0:T(8,128)(2,1)S(1)}, u32[]{:S(2)}, u32[]{:S(2)}) collective-permute-start(bf16[2,4,2,128,128]{4,3,2,1,0:T(8,128)(2,1)} %collective-permute-done.6.refs_2_), channel_id=1, source_target_pairs={{0,16},{8,24},{16,0},{24,8},{1,17},{9,25},{17,1},{25,9},{2,18},{10... | collective-permute-start | bytes 1572872 | tf_op jit(solution)/shard_map/ppermute | solution.py:575
  32.8 0.0 collective-permute-start.8
  32.8 0.5 collective-permute-start.7
  33.3 13.1 %shard_map.116 = (f32[4,4,512,128]{3,2,1,0:T(8,128)S(1)}, f32[4,4,512,128]{3,2,1,0:T(8,128)S(1)}, f32[4,4,512,128]{3,2,1,0:T(8,128)S(1)}) custom-call(s32[4]{0:T(128)S(1)} %compare_convert_fusion.needed_ref, bf16[1,256,32,128]{3,2,1,0:T(8,128)(2,1)} %refs_0_.3, bf16[2,4,2,128,128]{4,3,2,1,0:T(8,128)(2,1)S(1)} %collective-permute-done.2.refs_1_, ...), custom_call_target="tpu_custom_call" | custom-call | flops 8589934592 | bytes 12000000 | tf_op jit(solution)/shard_map/pallas_call | solution.py:216
  46.3 0.0 collective-permute-done.10.refs_2_.refs_3_
  46.4 0.0 collective-permute-done.9.refs_10_
  46.4 0.6 collective-permute-start.13
  47.0 0.0 collective-permute-start.12
  47.0 0.5 collective-permute-start.11
  47.5 13.4 %shard_map.117 = bf16[1,256,32,128]{3,2,1,0:T(8,128)(2,1)} custom-call(s32[4]{0:T(128)S(1)} %compare_convert_fusion.needed_ref, bf16[1,256,32,128]{3,2,1,0:T(8,128)(2,1)} %refs_0_.3, bf16[2,4,2,128,128]{4,3,2,1,0:T(8,128)(2,1)S(1)} %shard_map.113.refs_1_.refs_0_, bf16[2,4,2,128,128]{4,3,2,1,0:T(8,128)(2,1)S(1)} %collective-permute-done.10.refs_2_.refs_3_, ...), custom_call_target="tpu_custom_call" | custom-call | flops 8589934592 | bytes 12000000 | tf_op jit(solution)/shard_map/pallas_call | solution.py:216
  60.9 0.0 collective-permute-done.12.refs_7_
  61.0 0.1 collective-permute-start.14
  61.0 1.9 %collective-permute-done.14.refs_15_ = bf16[2,4,2,128,128]{4,3,2,1,0:T(8,128)(2,1)S(1)} collective-permute-done((bf16[2,4,2,128,128]{4,3,2,1,0:T(8,128)(2,1)S(1)}, bf16[2,4,2,128,128]{4,3,2,1,0:T(8,128)(2,1)S(1)}, u32[]{:S(2)}, u32[]{:S(2)}) %collective-permute-start.14) | collective-permute-done | bytes 524320 | tf_op jit(solution)/shard_map/ppermute | solution.py:575
  62.9 2.4 %shard_map.118 = (bf16[16,4,2,128,128]{4,3,2,1,0:T(8,128)(2,1)S(1)}, bf16[32,128,128]{2,1,0:T(8,128)(2,1)S(1)}) custom-call(s32[16]{0:T(128)S(1)} %select_reduce_fusion.pick_ref, bf16[32,128,128]{2,1,0:T(8,128)(2,1)} %bitcast.15, bf16[2,4,2,128,128]{4,3,2,1,0:T(8,128)(2,1)S(1)} %shard_map.113.refs_1_.refs_0_, ...), custom_call_target="tpu_custom_call" | custom-call | bytes 8000000 | tf_op jit(solution)/shard_map/pallas_call | solution.py:344
  65.4 3.1 %shard_map.120 = bf16[8,128,128]{2,1,0:T(8,128)(2,1)S(1)} custom-call(s32[128]{0:T(128)S(1)} %reshape.39.slot_ref, s32[2]{0:T(128)S(1)} %pad_add_fusion.meta_ref, bf16[32,128,128]{2,1,0:T(8,128)(2,1)S(1)} %get-tuple-element.67.refs_0_, f32[16,128,128]{2,1,0:T(8,128)S(1)} %get-tuple-element.71.refs_1_, f32[16,8,128]{2,1,0:T(8,128)S(1)} %get-tuple-element.72.refs_2_, ...), custom_call_target="tpu_custom_call" | custom-call | flops 1000000 | bytes 1000000 | tf_op jit(solution)/shard_map/pallas_call | solution.py:432
  68.5 1.6 %collective-permute-start.15 = (bf16[8,128,128]{2,1,0:T(8,128)(2,1)S(1)}, bf16[8,128,128]{2,1,0:T(8,128)(2,1)S(1)}, u32[]{:S(2)}, u32[]{:S(2)}) collective-permute-start(bf16[8,128,128]{2,1,0:T(8,128)(2,1)S(1)} %shard_map.120), channel_id=1, source_target_pairs={{0,1},{1,0},{2,3},{3,2},{4,5},{5,4},{6,7},{7,6},{8,9},{9,8},{10,11... | collective-permute-start | bytes 786440 | tf_op jit(solution)/shard_map/ppermute | solution.py:620
  70.1 3.1 %shard_map.122 = bf16[8,128,128]{2,1,0:T(8,128)(2,1)S(1)} custom-call(s32[128]{0:T(128)S(1)} %reshape.39.slot_ref, s32[2]{0:T(128)S(1)} %pad_add_fusion.meta_ref, bf16[32,128,128]{2,1,0:T(8,128)(2,1)S(1)} %get-tuple-element.67.refs_0_, f32[16,128,128]{2,1,0:T(8,128)S(1)} %get-tuple-element.71.refs_1_, f32[16,8,128]{2,1,0:T(8,128)S(1)} %get-tuple-element.72.refs_2_, ...), custom_call_target="tpu_custom_call" | custom-call | flops 1000000 | bytes 1000000 | tf_op jit(solution)/shard_map/pallas_call | solution.py:432
  73.3 0.6 collective-permute-start.16
  73.8 3.1 %shard_map.119.refs_0_ = bf16[8,128,128]{2,1,0:T(8,128)(2,1)S(1)} custom-call(s32[128]{0:T(128)S(1)} %reshape.39.slot_ref, s32[2]{0:T(128)S(1)} %pad_add_fusion.meta_ref, bf16[32,128,128]{2,1,0:T(8,128)(2,1)S(1)} %get-tuple-element.67.refs_0_, f32[16,128,128]{2,1,0:T(8,128)S(1)} %get-tuple-element.73.refs_1_, f32[16,8,128]{2,1,0:T(8,128)S(1)} %get-tuple-element.74.refs_2_, ...), custom_call_target="tpu_custom_call" | custom-call | flops 1000000 | bytes 1000000 | tf_op jit(solution)/shard_map/pallas_call | solution.py:432
  77.0 0.8 collective-permute-done.15.refs_2_
  77.7 3.1 %shard_map.121.refs_1_ = bf16[8,128,128]{2,1,0:T(8,128)(2,1)S(1)} custom-call(s32[128]{0:T(128)S(1)} %reshape.39.slot_ref, s32[2]{0:T(128)S(1)} %pad_add_fusion.meta_ref, bf16[32,128,128]{2,1,0:T(8,128)(2,1)S(1)} %get-tuple-element.67.refs_0_, f32[16,128,128]{2,1,0:T(8,128)S(1)} %get-tuple-element.73.refs_1_, f32[16,8,128]{2,1,0:T(8,128)S(1)} %get-tuple-element.74.refs_2_, ...), custom_call_target="tpu_custom_call" | custom-call | flops 1000000 | bytes 1000000 | tf_op jit(solution)/shard_map/pallas_call | solution.py:432
  80.9 1.7 %collective-permute-done.16.refs_3_ = bf16[8,128,128]{2,1,0:T(8,128)(2,1)S(1)} collective-permute-done((bf16[8,128,128]{2,1,0:T(8,128)(2,1)S(1)}, bf16[8,128,128]{2,1,0:T(8,128)(2,1)S(1)}, u32[]{:S(2)}, u32[]{:S(2)}) %collective-permute-start.16) | collective-permute-done | bytes 262176 | tf_op jit(solution)/shard_map/ppermute | solution.py:620
  82.6 1.8 %shard_map.123 = bf16[16,4,8192]{2,1,0:T(4,128)(2,1)} custom-call(s32[2]{0:T(128)S(1)} %pad_add_fusion.meta_ref, bf16[8,128,128]{2,1,0:T(8,128)(2,1)S(1)} %shard_map.119.refs_0_, bf16[8,128,128]{2,1,0:T(8,128)(2,1)S(1)} %shard_map.121.refs_1_, bf16[8,128,128]{2,1,0:T(8,128)(2,1)S(1)} %collective-permute-done.15.refs_2_, ...), custom_call_target="tpu_custom_call" | custom-call | bytes 2000000 | tf_op jit(solution)/shard_map/pallas_call | solution.py:490
  (11 shorter events, 0.1 us)
Async XLA Ops:
  2.1 13.7 %collective-permute-start.2 = (bf16[2,4,2,128,128]{4,3,2,1,0:T(8,128)(2,1)S(1)}, bf16[2,4,2,128,128]{4,3,2,1,0:T(8,128)(2,1)S(1)}, u32[]{:S(2)}, u32[]{:S(2)}) collective-permute-start(bf16[2,4,2,128,128]{4,3,2,1,0:T(8,128)(2,1)S(1)} %shard_map.113.refs_1_.refs_0_), channel_id=1, source_target_pairs={{0,4},{4,6},{6,2},{2,0},{1,5},{5,7},{7,3},{3,1},{8,12},{12,14},{14... | collective-permute-start | bytes 1572872 | tf_op jit(solution)/shard_map/ppermute | solution.py:575
  2.5 13.4 %collective-permute-start.1 = (bf16[2,4,2,128,128]{4,3,2,1,0:T(8,128)(2,1)S(1)}, bf16[2,4,2,128,128]{4,3,2,1,0:T(8,128)(2,1)S(1)}, u32[]{:S(2)}, u32[]{:S(2)}) collective-permute-start(bf16[2,4,2,128,128]{4,3,2,1,0:T(8,128)(2,1)S(1)} %shard_map.113.refs_1_.refs_0_), channel_id=1, source_target_pairs={{0,16},{8,24},{16,0},{24,8},{1,17},{9,25},{17,1},{25,9},{2,18},{10... | collective-permute-start | bytes 1572872 | tf_op jit(solution)/shard_map/ppermute | solution.py:575
  4.0 11.9 %collective-permute-start = (bf16[2,4,2,128,128]{4,3,2,1,0:T(8,128)(2,1)S(1)}, bf16[2,4,2,128,128]{4,3,2,1,0:T(8,128)(2,1)S(1)}, u32[]{:S(2)}, u32[]{:S(2)}) collective-permute-start(bf16[2,4,2,128,128]{4,3,2,1,0:T(8,128)(2,1)S(1)} %shard_map.113.refs_1_.refs_0_), channel_id=1, source_target_pairs={{0,8},{8,0},{16,24},{24,16},{1,9},{9,1},{17,25},{25,17},{2,10},{10... | collective-permute-start | bytes 1572872 | tf_op jit(solution)/shard_map/ppermute | solution.py:575
  4.1 0.7 copy-start
  4.8 14.3 %copy-start.2 = (s32[32,4]{0,1:T(4,128)S(1)}, s32[32,4]{0,1:T(4,128)}, u32[]{:S(2)}) copy-start(s32[32,4]{0,1:T(4,128)} %param.19) | copy-start | bytes 1540
  4.8 14.9 %copy-start.1 = (s32[32]{0:T(128)S(1)}, s32[32]{0:T(128)}, u32[]{:S(2)}) copy-start(s32[32]{0:T(128)} %len_ref.3) | copy-start | bytes 388
  15.9 12.8 %collective-permute-start.6 = (bf16[2,4,2,128,128]{4,3,2,1,0:T(8,128)(2,1)S(1)}, bf16[2,4,2,128,128]{4,3,2,1,0:T(8,128)(2,1)}, u32[]{:S(2)}, u32[]{:S(2)}) collective-permute-start(bf16[2,4,2,128,128]{4,3,2,1,0:T(8,128)(2,1)S(1)} %collective-permute-done.2.refs_1_), channel_id=1, source_target_pairs={{0,4},{4,6},{6,2},{2,0},{1,5},{5,7},{7,3},{3,1},{8,12},{12,14},{14... | collective-permute-start | bytes 1572872 | tf_op jit(solution)/shard_map/ppermute | solution.py:575
  17.1 12.6 %collective-permute-start.5 = (bf16[2,4,2,128,128]{4,3,2,1,0:T(8,128)(2,1)S(1)}, bf16[2,4,2,128,128]{4,3,2,1,0:T(8,128)(2,1)}, u32[]{:S(2)}, u32[]{:S(2)}) collective-permute-start(bf16[2,4,2,128,128]{4,3,2,1,0:T(8,128)(2,1)S(1)} %collective-permute-done.2.refs_1_), channel_id=1, source_target_pairs={{0,16},{8,24},{16,0},{24,8},{1,17},{9,25},{17,1},{25,9},{2,18},{10... | collective-permute-start | bytes 1572872 | tf_op jit(solution)/shard_map/ppermute | solution.py:575
  18.6 11.1 %collective-permute-start.4 = (bf16[2,4,2,128,128]{4,3,2,1,0:T(8,128)(2,1)S(1)}, bf16[2,4,2,128,128]{4,3,2,1,0:T(8,128)(2,1)}, u32[]{:S(2)}, u32[]{:S(2)}) collective-permute-start(bf16[2,4,2,128,128]{4,3,2,1,0:T(8,128)(2,1)S(1)} %collective-permute-done.2.refs_1_), channel_id=1, source_target_pairs={{0,8},{8,0},{16,24},{24,16},{1,9},{9,1},{17,25},{25,17},{2,10},{10... | collective-permute-start | bytes 1572872 | tf_op jit(solution)/shard_map/ppermute | solution.py:575
  18.6 7.3 %collective-permute-start.3 = (bf16[2,4,2,128,128]{4,3,2,1,0:T(8,128)(2,1)S(1)}, bf16[2,4,2,128,128]{4,3,2,1,0:T(8,128)(2,1)}, u32[]{:S(2)}, u32[]{:S(2)}) collective-permute-start(bf16[2,4,2,128,128]{4,3,2,1,0:T(8,128)(2,1)S(1)} %collective-permute-done.1.refs_8_), channel_id=1, source_target_pairs={{0,8},{8,0},{16,24},{24,16},{1,9},{9,1},{17,25},{25,17},{2,10},{10... | collective-permute-start | bytes 1572872 | tf_op jit(solution)/shard_map/ppermute | solution.py:575
  29.7 16.6 %collective-permute-start.10 = (bf16[2,4,2,128,128]{4,3,2,1,0:T(8,128)(2,1)}, bf16[2,4,2,128,128]{4,3,2,1,0:T(8,128)(2,1)S(1)}, u32[]{:S(2)}, u32[]{:S(2)}) collective-permute-start(bf16[2,4,2,128,128]{4,3,2,1,0:T(8,128)(2,1)} %collective-permute-done.6.refs_2_), channel_id=1, source_target_pairs={{0,4},{4,6},{6,2},{2,0},{1,5},{5,7},{7,3},{3,1},{8,12},{12,14},{14... | collective-permute-start | bytes 1572872 | tf_op jit(solution)/shard_map/ppermute | solution.py:575
  31.3 15.1 %collective-permute-start.9 = (bf16[2,4,2,128,128]{4,3,2,1,0:T(8,128)(2,1)}, bf16[2,4,2,128,128]{4,3,2,1,0:T(8,128)(2,1)S(1)}, u32[]{:S(2)}, u32[]{:S(2)}) collective-permute-start(bf16[2,4,2,128,128]{4,3,2,1,0:T(8,128)(2,1)} %collective-permute-done.6.refs_2_), channel_id=1, source_target_pairs={{0,16},{8,24},{16,0},{24,8},{1,17},{9,25},{17,1},{25,9},{2,18},{10... | collective-permute-start | bytes 1572872 | tf_op jit(solution)/shard_map/ppermute | solution.py:575
  32.8 13.6 %collective-permute-start.8 = (bf16[2,4,2,128,128]{4,3,2,1,0:T(8,128)(2,1)}, bf16[2,4,2,128,128]{4,3,2,1,0:T(8,128)(2,1)S(1)}, u32[]{:S(2)}, u32[]{:S(2)}) collective-permute-start(bf16[2,4,2,128,128]{4,3,2,1,0:T(8,128)(2,1)} %collective-permute-done.6.refs_2_), channel_id=1, source_target_pairs={{0,8},{8,0},{16,24},{24,16},{1,9},{9,1},{17,25},{25,17},{2,10},{10... | collective-permute-start | bytes 1572872 | tf_op jit(solution)/shard_map/ppermute | solution.py:575
  32.8 13.6 %collective-permute-start.7 = (bf16[2,4,2,128,128]{4,3,2,1,0:T(8,128)(2,1)}, bf16[2,4,2,128,128]{4,3,2,1,0:T(8,128)(2,1)S(1)}, u32[]{:S(2)}, u32[]{:S(2)}) collective-permute-start(bf16[2,4,2,128,128]{4,3,2,1,0:T(8,128)(2,1)} %collective-permute-done.5.refs_9_), channel_id=1, source_target_pairs={{0,8},{8,0},{16,24},{24,16},{1,9},{9,1},{17,25},{25,17},{2,10},{10... | collective-permute-start | bytes 1572872 | tf_op jit(solution)/shard_map/ppermute | solution.py:575
  46.4 14.6 %collective-permute-start.13 = (bf16[2,4,2,128,128]{4,3,2,1,0:T(8,128)(2,1)S(1)}, bf16[2,4,2,128,128]{4,3,2,1,0:T(8,128)(2,1)S(1)}, u32[]{:S(2)}, u32[]{:S(2)}) collective-permute-start(bf16[2,4,2,128,128]{4,3,2,1,0:T(8,128)(2,1)S(1)} %collective-permute-done.10.refs_2_.refs_3_), channel_id=1, source_target_pairs={{0,16},{8,24},{16,0},{24,8},{1,17},{9,25},{17,1},{25,9},{2,18},{10... | collective-permute-start | bytes 1572872 | tf_op jit(solution)/shard_map/ppermute | solution.py:575
  47.0 14.0 %collective-permute-start.12 = (bf16[2,4,2,128,128]{4,3,2,1,0:T(8,128)(2,1)S(1)}, bf16[2,4,2,128,128]{4,3,2,1,0:T(8,128)(2,1)S(1)}, u32[]{:S(2)}, u32[]{:S(2)}) collective-permute-start(bf16[2,4,2,128,128]{4,3,2,1,0:T(8,128)(2,1)S(1)} %collective-permute-done.10.refs_2_.refs_3_), channel_id=1, source_target_pairs={{0,8},{8,0},{16,24},{24,16},{1,9},{9,1},{17,25},{25,17},{2,10},{10... | collective-permute-start | bytes 1572872 | tf_op jit(solution)/shard_map/ppermute | solution.py:575
  47.0 14.0 %collective-permute-start.11 = (bf16[2,4,2,128,128]{4,3,2,1,0:T(8,128)(2,1)S(1)}, bf16[2,4,2,128,128]{4,3,2,1,0:T(8,128)(2,1)S(1)}, u32[]{:S(2)}, u32[]{:S(2)}) collective-permute-start(bf16[2,4,2,128,128]{4,3,2,1,0:T(8,128)(2,1)S(1)} %collective-permute-done.9.refs_10_), channel_id=1, source_target_pairs={{0,8},{8,0},{16,24},{24,16},{1,9},{9,1},{17,25},{25,17},{2,10},{10... | collective-permute-start | bytes 1572872 | tf_op jit(solution)/shard_map/ppermute | solution.py:575
  61.0 2.0 %collective-permute-start.14 = (bf16[2,4,2,128,128]{4,3,2,1,0:T(8,128)(2,1)S(1)}, bf16[2,4,2,128,128]{4,3,2,1,0:T(8,128)(2,1)S(1)}, u32[]{:S(2)}, u32[]{:S(2)}) collective-permute-start(bf16[2,4,2,128,128]{4,3,2,1,0:T(8,128)(2,1)S(1)} %collective-permute-done.13.refs_11_), channel_id=1, source_target_pairs={{0,8},{8,0},{16,24},{24,16},{1,9},{9,1},{17,25},{25,17},{2,10},{10... | collective-permute-start | bytes 1572872 | tf_op jit(solution)/shard_map/ppermute | solution.py:575
  68.5 9.2 %collective-permute-start.15 = (bf16[8,128,128]{2,1,0:T(8,128)(2,1)S(1)}, bf16[8,128,128]{2,1,0:T(8,128)(2,1)S(1)}, u32[]{:S(2)}, u32[]{:S(2)}) collective-permute-start(bf16[8,128,128]{2,1,0:T(8,128)(2,1)S(1)} %shard_map.120), channel_id=1, source_target_pairs={{0,1},{1,0},{2,3},{3,2},{4,5},{5,4},{6,7},{7,6},{8,9},{9,8},{10,11... | collective-permute-start | bytes 786440 | tf_op jit(solution)/shard_map/ppermute | solution.py:620
  73.3 9.3 %collective-permute-start.16 = (bf16[8,128,128]{2,1,0:T(8,128)(2,1)S(1)}, bf16[8,128,128]{2,1,0:T(8,128)(2,1)S(1)}, u32[]{:S(2)}, u32[]{:S(2)}) collective-permute-start(bf16[8,128,128]{2,1,0:T(8,128)(2,1)S(1)} %shard_map.122), channel_id=1, source_target_pairs={{0,1},{1,0},{2,3},{3,2},{4,5},{5,4},{6,7},{7,6},{8,9},{9,8},{10,11... | collective-permute-start | bytes 786440 | tf_op jit(solution)/shard_map/ppermute | solution.py:620

commit v17 on v16

--- a/solution.py
+++ b/solution.py
@@ -457,10 +457,19 @@
     )(slot, meta, q, acc, ml, pages)
 
 
+def put(out_ref, source, offset, steps):
+    def body(r, carry):
+        value = source[r]
+        for g in range(source.shape[1] // steps):
+            out_ref[offset + r, :, g * 128 : (g + 1) * 128] = value[g * steps : (g + 1) * steps]
+        return carry
+
+    lax.fori_loop(0, source.shape[0], body, 0)
+
+
 def join_kernel(counts, steps, meta_ref, *refs):
     out_ref = refs[-1]
     k = pl.program_id(0)
-    rows = refs[0].shape[1]
     targets = len(counts)
     sources = iter(refs)
     for s, count in enumerate(counts):
@@ -469,36 +478,56 @@
         @pl.when(lax.rem(meta_ref[1] + (targets - s), targets) == k)
         def _():
             for n, source in enumerate(parts):
-
-                def body(r, carry):
-                    value = source[r]
-                    for g in range(rows // steps):
-                        out_ref[n * source.shape[0] + r, :, g * 128 : (g + 1) * 128] = value[
-                            g * steps : (g + 1) * steps
-                        ]
-                    return carry
-
-                lax.fori_loop(0, source.shape[0], body, 0)
+                put(out_ref, source, n * source.shape[0], steps)
+
+
+def join_last_kernel(steps, meta_ref, *refs):
+    sources, out_ref = refs[:-2], refs[-1]
+    for s, source in enumerate(sources):
+        @pl.when(pl.program_id(0) == s)
+        def _():
+            put(out_ref, source, 0, steps)
 
 
 def join(pieces, meta, steps):
-    flat = [a for parts in pieces for a in parts]
-    rows, width = flat[0].shape[1:]
-    targets = len(pieces)
-    per_target = sum(a.shape[0] for a in pieces[0])
+    targets, parts = len(pieces), len(pieces[0])
+    count, rows, width = pieces[0][0].shape
     half = rows // steps * width
-    return pl.pallas_call(
-        functools.partial(join_kernel, [len(parts) for parts in pieces], steps),
+    early = [pieces[0]] + [p[:-1] for p in pieces[1:]]
+    late = [p[-1] for p in pieces[1:]]
+    flat = [a for p in early for a in p]
+    on_chip = pl.BlockSpec(memory_space=pltpu.VMEM)
+    shape = jax.ShapeDtypeStruct((parts * count, steps, half * targets), jnp.bfloat16)
+    out = pl.pallas_call(
+        functools.partial(join_kernel, [len(p) for p in early], steps),
         grid_spec=pltpu.PrefetchScalarGridSpec(
             num_scalar_prefetch=1,
             grid=(targets,),
-            in_specs=[pl.BlockSpec(memory_space=pltpu.VMEM)] * len(flat),
-            out_specs=pl.BlockSpec((per_target, steps, half), lambda k, *_: (0, 0, k)),
-        ),
-        out_shape=jax.ShapeDtypeStruct((per_target, steps, half * targets), jnp.bfloat16),
+            in_specs=[on_chip] * len(flat),
+            out_specs=pl.BlockSpec((parts * count, steps, half), lambda k, *_: (0, 0, k)),
+        ),
+        out_shape=shape,
         compiler_params=params(),
         cost_estimate=pl.CostEstimate(flops=0, bytes_accessed=2 * 10**6, transcendentals=0),
     )(meta, *flat)
+    if not late:
+        return out
+    return pl.pallas_call(
+        functools.partial(join_last_kernel, steps),
+        grid_spec=pltpu.PrefetchScalarGridSpec(
+            num_scalar_prefetch=1,
+            grid=(targets - 1,),
+            in_specs=[on_chip] * len(late) + [pl.BlockSpec(memory_space=pl.ANY)],
+            out_specs=pl.BlockSpec(
+                (count, steps, half),
+                lambda s, meta: (parts - 1, 0, lax.rem(meta[1] + targets - 1 - s, targets)),
+            ),
+        ),
+        out_shape=shape,
+        input_output_aliases={1 + len(late): 0},
+        compiler_params=params(),
+        cost_estimate=pl.CostEstimate(flops=0, bytes_accessed=10**6, transcendentals=0),
+    )(meta, *late, out)
 
 
 def ring_place(index, size):
@@ -569,7 +598,7 @@
                     pairs = [(j, j ^ flip) for j in range(roles)]
                     sends.append((flip, (code, s), (code ^ flip, s), "role", pairs))
             if code == 0 and s + 1 < ring:
-                sends.append((roles, (code, s), (0, s + 1), "ctx", along))
+                sends.append((roles if k else 1.5, (code, s), (0, s + 1), "ctx", along))
         sends.sort(key=lambda a: a[0])
         names = [to for _, _, to, _, _ in sends]
         arrived = [lax.ppermute(gathered[of], axis, pairs) for _, of, _, axis, pairs in sends]

time: 84.6 us -> 84.8 us (level)
  Pallas kernels: 57.2 us -> 58.5 us
  starting transfers between devices: 11.9 us -> 10.7 us
    ppermute x15, waiting for transfers between devices: 10.6 us -> 12.4 us  [shards(): lax.ppermute(gathered[of], axis, pairs)]
    ppermute x2, waiting for transfers between devices: 2.45 us -> 0.77 us  [shards(): out = lax.ppermute(out, 'tp', shift)]
    pallas_call x1 -> x2, Pallas kernels: 1.77 us -> 3.07 us  [the longest x1 1.73 us: join(): pl.pallas_call(functools.partial(join_kernel, [len(p) for p in early], st...]
    ppermute x15, starting transfers between devices: 9.77 us -> 8.55 us  [shards(): lax.ppermute(gathered[of], axis, pairs)]
  transfers between devices with their start and end apart: 17 -> 17, of which waited for: 7 -> 6; matrix products, arithmetic and copies ran while one was open for 1% -> 1% of each run, Pallas kernels for 57% -> 59%
where the time goes in v17:
time: 84.8 us; the launch traced here: 84.5 us
  Pallas kernels  58.5 us (69%)
  waiting for transfers between devices  13.2 us (16%)
  starting transfers between devices  10.7 us (13%)
  local copies, waits for them, and re-layouts  1.05 us (1%)
    pallas_call x2, Pallas kernels, prefill(): pl.pallas_call(functools.partial(prefill_kernel, own, count, slots, group...  26.5 us
    pallas_call x4, Pallas kernels, decode(): pl.pallas_call(functools.partial(decode_kernel, extra, steps, target, tar...  12.5 us
    pallas_call x2, Pallas kernels, cache_part(): pl.pallas_call(functools.partial(cache_kernel, steps, heads, group, targe...  12.5 us
    ppermute x15, waiting for transfers between devices, shards(): lax.ppermute(gathered[of], axis, pairs)  12.4 us
    ppermute x15, starting transfers between devices, shards(): lax.ppermute(gathered[of], axis, pairs)  8.55 us
    pallas_call x1, Pallas kernels, collect(): pl.pallas_call(collect_kernel, grid_spec=pltpu.PrefetchScalarGridSpec(num...  2.44 us
    ppermute x2, starting transfers between devices, shards(): out = lax.ppermute(out, 'tp', shift)  2.16 us
    pallas_call x1, Pallas kernels, join(): pl.pallas_call(functools.partial(join_kernel, [len(p) for p in early], st...  1.73 us
  transfers between devices with their start and end apart: 17, of which 6 were waited for; matrix products, arithmetic and copies ran while one was open for 1% of the time, Pallas kernels for 59%

profile of v17, /device:TPU:24, one launch (start us, length us, event | category | flops | bytes accessed | tf_op | source)
XLA Modules:
  0.0 84.5 jit_solution(11212572038671723527)
XLA Ops:
  0.6 1.5 %shard_map.113.refs_1_.refs_0_ = bf16[2,4,2,128,128]{4,3,2,1,0:T(8,128)(2,1)S(1)} custom-call(bf16[1024,128]{1,0:T(8,128)(2,1)} %bitcast.20, bf16[1024,128]{1,0:T(8,128)(2,1)} %bitcast.21), custom_call_target="tpu_custom_call" | custom-call | flops 100000000 | bytes 2000000 | tf_op jit(solution)/shard_map/pallas_call | solution.py:58
  2.1 1.6 %collective-permute-start.2 = (bf16[2,4,2,128,128]{4,3,2,1,0:T(8,128)(2,1)S(1)}, bf16[2,4,2,128,128]{4,3,2,1,0:T(8,128)(2,1)S(1)}, u32[]{:S(2)}, u32[]{:S(2)}) collective-permute-start(bf16[2,4,2,128,128]{4,3,2,1,0:T(8,128)(2,1)S(1)} %shard_map.113.refs_1_.refs_0_), channel_id=1, source_target_pairs={{0,16},{8,24},{16,0},{24,8},{1,17},{9,25},{17,1},{25,9},{2,18},{10... | collective-permute-start | bytes 1572872 | tf_op jit(solution)/shard_map/ppermute | solution.py:604
  3.7 0.3 collective-permute-start.1
  4.0 0.0 collective-permute-start
  4.0 0.1 pad_add_fusion.meta_ref
  4.1 0.7 copy-done
  4.8 6.2 %shard_map.114 = (f32[16,128,128]{2,1,0:T(8,128)S(1)}, f32[16,8,128]{2,1,0:T(8,128)S(1)}) custom-call(s32[32]{0:T(128)S(1)} %copy-done, s32[2]{0:T(128)S(1)} %pad_add_fusion.meta_ref, bf16[32,128,128]{2,1,0:T(8,128)(2,1)} %bitcast.13, bf16[32,16,128]{2,1,0:T(8,128)(2,1)} %bitcast.16, bf16[32,16,128]{2,1,0:T(8,128)(2,1)} %bitcast.18, ...), custom_call_target="tpu_custom_call" | custom-call | flops 2147483648 | bytes 7000000 | tf_op jit(solution)/shard_map/pallas_call | solution.py:309
  11.0 4.8 %collective-permute-done.2.refs_8_ = bf16[2,4,2,128,128]{4,3,2,1,0:T(8,128)(2,1)S(1)} collective-permute-done((bf16[2,4,2,128,128]{4,3,2,1,0:T(8,128)(2,1)S(1)}, bf16[2,4,2,128,128]{4,3,2,1,0:T(8,128)(2,1)S(1)}, u32[]{:S(2)}, u32[]{:S(2)}) %collective-permute-start.2) | collective-permute-done | bytes 524320 | tf_op jit(solution)/shard_map/ppermute | solution.py:604
  15.9 1.2 %collective-permute-done.1.refs_1_ = bf16[2,4,2,128,128]{4,3,2,1,0:T(8,128)(2,1)S(1)} collective-permute-done((bf16[2,4,2,128,128]{4,3,2,1,0:T(8,128)(2,1)S(1)}, bf16[2,4,2,128,128]{4,3,2,1,0:T(8,128)(2,1)S(1)}, u32[]{:S(2)}, u32[]{:S(2)}) %collective-permute-start.1) | collective-permute-done | bytes 524320 | tf_op jit(solution)/shard_map/ppermute | solution.py:604
  17.1 0.0 collective-permute-done.refs_4_
  17.1 1.2 %collective-permute-start.6 = (bf16[2,4,2,128,128]{4,3,2,1,0:T(8,128)(2,1)S(1)}, bf16[2,4,2,128,128]{4,3,2,1,0:T(8,128)(2,1)}, u32[]{:S(2)}, u32[]{:S(2)}) collective-permute-start(bf16[2,4,2,128,128]{4,3,2,1,0:T(8,128)(2,1)S(1)} %collective-permute-done.1.refs_1_), channel_id=1, source_target_pairs={{0,4},{4,6},{6,2},{2,0},{1,5},{5,7},{7,3},{3,1},{8,12},{12,14},{14... | collective-permute-start | bytes 1572872 | tf_op jit(solution)/shard_map/ppermute | solution.py:604
  18.3 0.5 collective-permute-start.5
  18.9 0.0 collective-permute-start.3
  18.9 0.5 collective-permute-start.4
  19.4 0.1 copy.18
  19.5 0.1 broadcast_in_dim.15
  19.6 0.1 copy.17
  19.7 0.1 reshape.39.slot_ref
  19.8 0.1 select_reduce_fusion.pick_ref
  19.9 6.3 %shard_map.115 = (f32[16,128,128]{2,1,0:T(8,128)S(1)}, f32[16,8,128]{2,1,0:T(8,128)S(1)}) custom-call(s32[32]{0:T(128)S(1)} %copy-done.1, s32[2]{0:T(128)S(1)} %pad_add_fusion.meta_ref, bf16[32,128,128]{2,1,0:T(8,128)(2,1)} %bitcast.14, bf16[32,16,128]{2,1,0:T(8,128)(2,1)} %bitcast.17, bf16[32,16,128]{2,1,0:T(8,128)(2,1)} %bitcast.19, ...), custom_call_target="tpu_custom_call" | custom-call | flops 2147483648 | bytes 7000000 | tf_op jit(solution)/shard_map/pallas_call | solution.py:309
  26.2 0.0 collective-permute-done.4.refs_12_
  26.2 3.5 %collective-permute-done.6.refs_2_ = bf16[2,4,2,128,128]{4,3,2,1,0:T(8,128)(2,1)} collective-permute-done((bf16[2,4,2,128,128]{4,3,2,1,0:T(8,128)(2,1)S(1)}, bf16[2,4,2,128,128]{4,3,2,1,0:T(8,128)(2,1)}, u32[]{:S(2)}, u32[]{:S(2)}) %collective-permute-start.6) | collective-permute-done | bytes 524320 | tf_op jit(solution)/shard_map/ppermute | solution.py:604
  29.7 1.0 %collective-permute-done.5.refs_9_ = bf16[2,4,2,128,128]{4,3,2,1,0:T(8,128)(2,1)} collective-permute-done((bf16[2,4,2,128,128]{4,3,2,1,0:T(8,128)(2,1)S(1)}, bf16[2,4,2,128,128]{4,3,2,1,0:T(8,128)(2,1)}, u32[]{:S(2)}, u32[]{:S(2)}) %collective-permute-start.5) | collective-permute-done | bytes 524320 | tf_op jit(solution)/shard_map/ppermute | solution.py:604
  30.6 0.0 collective-permute-done.3.refs_5_
  30.6 1.2 %collective-permute-start.10 = (bf16[2,4,2,128,128]{4,3,2,1,0:T(8,128)(2,1)}, bf16[2,4,2,128,128]{4,3,2,1,0:T(8,128)(2,1)S(1)}, u32[]{:S(2)}, u32[]{:S(2)}) collective-permute-start(bf16[2,4,2,128,128]{4,3,2,1,0:T(8,128)(2,1)} %collective-permute-done.6.refs_2_), channel_id=1, source_target_pairs={{0,4},{4,6},{6,2},{2,0},{1,5},{5,7},{7,3},{3,1},{8,12},{12,14},{14... | collective-permute-start | bytes 1572872 | tf_op jit(solution)/shard_map/ppermute | solution.py:604
  31.8 0.5 collective-permute-start.9
  32.4 0.5 collective-permute-start.7
  32.9 13.1 %shard_map.116 = (f32[4,4,512,128]{3,2,1,0:T(8,128)S(1)}, f32[4,4,512,128]{3,2,1,0:T(8,128)S(1)}, f32[4,4,512,128]{3,2,1,0:T(8,128)S(1)}) custom-call(s32[4]{0:T(128)S(1)} %compare_convert_fusion.needed_ref, bf16[1,256,32,128]{3,2,1,0:T(8,128)(2,1)} %refs_0_.3, bf16[2,4,2,128,128]{4,3,2,1,0:T(8,128)(2,1)S(1)} %collective-permute-done.1.refs_1_, ...), custom_call_target="tpu_custom_call" | custom-call | flops 8589934592 | bytes 12000000 | tf_op jit(solution)/shard_map/pallas_call | solution.py:216
  45.9 0.0 collective-permute-done.10.refs_2_.refs_3_
  45.9 0.0 collective-permute-done.9.refs_10_
  46.0 1.6 %collective-permute-start.13 = (bf16[2,4,2,128,128]{4,3,2,1,0:T(8,128)(2,1)S(1)}, bf16[2,4,2,128,128]{4,3,2,1,0:T(8,128)(2,1)S(1)}, u32[]{:S(2)}, u32[]{:S(2)}) collective-permute-start(bf16[2,4,2,128,128]{4,3,2,1,0:T(8,128)(2,1)S(1)} %collective-permute-done.10.refs_2_.refs_3_), channel_id=1, source_target_pairs={{0,16},{8,24},{16,0},{24,8},{1,17},{9,25},{17,1},{25,9},{2,18},{10... | collective-permute-start | bytes 1572872 | tf_op jit(solution)/shard_map/ppermute | solution.py:604
  47.5 0.5 collective-permute-start.11
  48.0 13.4 %shard_map.117 = bf16[1,256,32,128]{3,2,1,0:T(8,128)(2,1)} custom-call(s32[4]{0:T(128)S(1)} %compare_convert_fusion.needed_ref, bf16[1,256,32,128]{3,2,1,0:T(8,128)(2,1)} %refs_0_.3, bf16[2,4,2,128,128]{4,3,2,1,0:T(8,128)(2,1)S(1)} %shard_map.113.refs_1_.refs_0_, bf16[2,4,2,128,128]{4,3,2,1,0:T(8,128)(2,1)S(1)} %collective-permute-done.10.refs_2_.refs_3_, ...), custom_call_target="tpu_custom_call" | custom-call | flops 8589934592 | bytes 12000000 | tf_op jit(solution)/shard_map/pallas_call | solution.py:216
  61.5 0.0 collective-permute-done.11.refs_14_
  61.5 0.0 collective-permute-done.12.refs_7_
  61.5 0.1 collective-permute-start.14
  61.6 1.9 %collective-permute-done.14.refs_15_ = bf16[2,4,2,128,128]{4,3,2,1,0:T(8,128)(2,1)S(1)} collective-permute-done((bf16[2,4,2,128,128]{4,3,2,1,0:T(8,128)(2,1)S(1)}, bf16[2,4,2,128,128]{4,3,2,1,0:T(8,128)(2,1)S(1)}, u32[]{:S(2)}, u32[]{:S(2)}) %collective-permute-start.14) | collective-permute-done | bytes 524320 | tf_op jit(solution)/shard_map/ppermute | solution.py:604
  63.5 2.4 %shard_map.118 = (bf16[16,4,2,128,128]{4,3,2,1,0:T(8,128)(2,1)S(1)}, bf16[32,128,128]{2,1,0:T(8,128)(2,1)S(1)}) custom-call(s32[16]{0:T(128)S(1)} %select_reduce_fusion.pick_ref, bf16[32,128,128]{2,1,0:T(8,128)(2,1)} %bitcast.15, bf16[2,4,2,128,128]{4,3,2,1,0:T(8,128)(2,1)S(1)} %shard_map.113.refs_1_.refs_0_, ...), custom_call_target="tpu_custom_call" | custom-call | bytes 8000000 | tf_op jit(solution)/shard_map/pallas_call | solution.py:344
  65.9 3.1 %shard_map.121 = bf16[8,128,128]{2,1,0:T(8,128)(2,1)S(1)} custom-call(s32[128]{0:T(128)S(1)} %reshape.39.slot_ref, s32[2]{0:T(128)S(1)} %pad_add_fusion.meta_ref, bf16[32,128,128]{2,1,0:T(8,128)(2,1)S(1)} %get-tuple-element.67.refs_0_, f32[16,128,128]{2,1,0:T(8,128)S(1)} %get-tuple-element.68.refs_1_, f32[16,8,128]{2,1,0:T(8,128)S(1)} %get-tuple-element.69.refs_2_, ...), custom_call_target="tpu_custom_call" | custom-call | flops 1000000 | bytes 1000000 | tf_op jit(solution)/shard_map/pallas_call | solution.py:432
  69.1 1.6 %collective-permute-start.16 = (bf16[8,128,128]{2,1,0:T(8,128)(2,1)S(1)}, bf16[8,128,128]{2,1,0:T(8,128)(2,1)S(1)}, u32[]{:S(2)}, u32[]{:S(2)}) collective-permute-start(bf16[8,128,128]{2,1,0:T(8,128)(2,1)S(1)} %shard_map.121), channel_id=1, source_target_pairs={{0,1},{1,0},{2,3},{3,2},{4,5},{5,4},{6,7},{7,6},{8,9},{9,8},{10,11... | collective-permute-start | bytes 786440 | tf_op jit(solution)/shard_map/ppermute | solution.py:649
  70.6 3.1 %shard_map.119 = bf16[8,128,128]{2,1,0:T(8,128)(2,1)S(1)} custom-call(s32[128]{0:T(128)S(1)} %reshape.39.slot_ref, s32[2]{0:T(128)S(1)} %pad_add_fusion.meta_ref, bf16[32,128,128]{2,1,0:T(8,128)(2,1)S(1)} %get-tuple-element.67.refs_0_, f32[16,128,128]{2,1,0:T(8,128)S(1)} %get-tuple-element.68.refs_1_, f32[16,8,128]{2,1,0:T(8,128)S(1)} %get-tuple-element.69.refs_2_, ...), custom_call_target="tpu_custom_call" | custom-call | flops 1000000 | bytes 1000000 | tf_op jit(solution)/shard_map/pallas_call | solution.py:432
  73.8 0.6 collective-permute-start.15
  74.4 3.1 %shard_map.120.refs_0_ = bf16[8,128,128]{2,1,0:T(8,128)(2,1)S(1)} custom-call(s32[128]{0:T(128)S(1)} %reshape.39.slot_ref, s32[2]{0:T(128)S(1)} %pad_add_fusion.meta_ref, bf16[32,128,128]{2,1,0:T(8,128)(2,1)S(1)} %get-tuple-element.67.refs_0_, f32[16,128,128]{2,1,0:T(8,128)S(1)} %get-tuple-element.73.refs_1_, f32[16,8,128]{2,1,0:T(8,128)S(1)} %get-tuple-element.74.refs_2_, ...), custom_call_target="tpu_custom_call" | custom-call | flops 1000000 | bytes 1000000 | tf_op jit(solution)/shard_map/pallas_call | solution.py:432
  77.5 0.8 collective-permute-done.16.refs_2_
  78.3 3.1 %shard_map.122.refs_1_ = bf16[8,128,128]{2,1,0:T(8,128)(2,1)S(1)} custom-call(s32[128]{0:T(128)S(1)} %reshape.39.slot_ref, s32[2]{0:T(128)S(1)} %pad_add_fusion.meta_ref, bf16[32,128,128]{2,1,0:T(8,128)(2,1)S(1)} %get-tuple-element.67.refs_0_, f32[16,128,128]{2,1,0:T(8,128)S(1)} %get-tuple-element.73.refs_1_, f32[16,8,128]{2,1,0:T(8,128)S(1)} %get-tuple-element.74.refs_2_, ...), custom_call_target="tpu_custom_call" | custom-call | flops 1000000 | bytes 1000000 | tf_op jit(solution)/shard_map/pallas_call | solution.py:432
  81.4 1.7 %shard_map.123.refs_1_ = bf16[16,4,8192]{2,1,0:T(4,128)(2,1)} custom-call(s32[2]{0:T(128)S(1)} %pad_add_fusion.meta_ref, bf16[8,128,128]{2,1,0:T(8,128)(2,1)S(1)} %shard_map.120.refs_0_, bf16[8,128,128]{2,1,0:T(8,128)(2,1)S(1)} %shard_map.122.refs_1_, bf16[8,128,128]{2,1,0:T(8,128)(2,1)S(1)} %collective-permute-done.16.refs_2_), custom_call_target="tpu_custom_call" | custom-call | bytes 2000000 | tf_op jit(solution)/shard_map/pallas_call | solution.py:501
  83.2 0.0 collective-permute-done.15.refs_0_
  83.2 1.3 %shard_map.124 = bf16[16,4,8192]{2,1,0:T(4,128)(2,1)} custom-call(s32[2]{0:T(128)S(1)} %pad_add_fusion.meta_ref, bf16[8,128,128]{2,1,0:T(8,128)(2,1)S(1)} %collective-permute-done.15.refs_0_, bf16[16,4,8192]{2,1,0:T(4,128)(2,1)} %shard_map.123.refs_1_), custom_call_target="tpu_custom_call", output_to_operand_aliasing={{}: (2, {})} | custom-call | bytes 1000000 | tf_op jit(solution)/shard_map/pallas_call | solution.py:515
  (12 shorter events, 0.1 us)
Async XLA Ops:
  2.1 13.7 %collective-permute-start.2 = (bf16[2,4,2,128,128]{4,3,2,1,0:T(8,128)(2,1)S(1)}, bf16[2,4,2,128,128]{4,3,2,1,0:T(8,128)(2,1)S(1)}, u32[]{:S(2)}, u32[]{:S(2)}) collective-permute-start(bf16[2,4,2,128,128]{4,3,2,1,0:T(8,128)(2,1)S(1)} %shard_map.113.refs_1_.refs_0_), channel_id=1, source_target_pairs={{0,16},{8,24},{16,0},{24,8},{1,17},{9,25},{17,1},{25,9},{2,18},{10... | collective-permute-start | bytes 1572872 | tf_op jit(solution)/shard_map/ppermute | solution.py:604
  3.7 13.4 %collective-permute-start.1 = (bf16[2,4,2,128,128]{4,3,2,1,0:T(8,128)(2,1)S(1)}, bf16[2,4,2,128,128]{4,3,2,1,0:T(8,128)(2,1)S(1)}, u32[]{:S(2)}, u32[]{:S(2)}) collective-permute-start(bf16[2,4,2,128,128]{4,3,2,1,0:T(8,128)(2,1)S(1)} %shard_map.113.refs_1_.refs_0_), channel_id=1, source_target_pairs={{0,4},{4,6},{6,2},{2,0},{1,5},{5,7},{7,3},{3,1},{8,12},{12,14},{14... | collective-permute-start | bytes 1572872 | tf_op jit(solution)/shard_map/ppermute | solution.py:604
  4.0 13.1 %collective-permute-start = (bf16[2,4,2,128,128]{4,3,2,1,0:T(8,128)(2,1)S(1)}, bf16[2,4,2,128,128]{4,3,2,1,0:T(8,128)(2,1)S(1)}, u32[]{:S(2)}, u32[]{:S(2)}) collective-permute-start(bf16[2,4,2,128,128]{4,3,2,1,0:T(8,128)(2,1)S(1)} %shard_map.113.refs_1_.refs_0_), channel_id=1, source_target_pairs={{0,8},{8,0},{16,24},{24,16},{1,9},{9,1},{17,25},{25,17},{2,10},{10... | collective-permute-start | bytes 1572872 | tf_op jit(solution)/shard_map/ppermute | solution.py:604
  4.1 0.7 copy-start
  4.8 14.6 %copy-start.2 = (s32[32,4]{0,1:T(4,128)S(1)}, s32[32,4]{0,1:T(4,128)}, u32[]{:S(2)}) copy-start(s32[32,4]{0,1:T(4,128)} %param.19) | copy-start | bytes 1540
  4.8 15.2 %copy-start.1 = (s32[32]{0:T(128)S(1)}, s32[32]{0:T(128)}, u32[]{:S(2)}) copy-start(s32[32]{0:T(128)} %len_ref.3) | copy-start | bytes 388
  17.1 12.6 %collective-permute-start.6 = (bf16[2,4,2,128,128]{4,3,2,1,0:T(8,128)(2,1)S(1)}, bf16[2,4,2,128,128]{4,3,2,1,0:T(8,128)(2,1)}, u32[]{:S(2)}, u32[]{:S(2)}) collective-permute-start(bf16[2,4,2,128,128]{4,3,2,1,0:T(8,128)(2,1)S(1)} %collective-permute-done.1.refs_1_), channel_id=1, source_target_pairs={{0,4},{4,6},{6,2},{2,0},{1,5},{5,7},{7,3},{3,1},{8,12},{12,14},{14... | collective-permute-start | bytes 1572872 | tf_op jit(solution)/shard_map/ppermute | solution.py:604
  18.3 12.3 %collective-permute-start.5 = (bf16[2,4,2,128,128]{4,3,2,1,0:T(8,128)(2,1)S(1)}, bf16[2,4,2,128,128]{4,3,2,1,0:T(8,128)(2,1)}, u32[]{:S(2)}, u32[]{:S(2)}) collective-permute-start(bf16[2,4,2,128,128]{4,3,2,1,0:T(8,128)(2,1)S(1)} %collective-permute-done.1.refs_1_), channel_id=1, source_target_pairs={{0,16},{8,24},{16,0},{24,8},{1,17},{9,25},{17,1},{25,9},{2,18},{10... | collective-permute-start | bytes 1572872 | tf_op jit(solution)/shard_map/ppermute | solution.py:604
  18.9 11.8 %collective-permute-start.3 = (bf16[2,4,2,128,128]{4,3,2,1,0:T(8,128)(2,1)S(1)}, bf16[2,4,2,128,128]{4,3,2,1,0:T(8,128)(2,1)}, u32[]{:S(2)}, u32[]{:S(2)}) collective-permute-start(bf16[2,4,2,128,128]{4,3,2,1,0:T(8,128)(2,1)S(1)} %collective-permute-done.1.refs_1_), channel_id=1, source_target_pairs={{0,8},{8,0},{16,24},{24,16},{1,9},{9,1},{17,25},{25,17},{2,10},{10... | collective-permute-start | bytes 1572872 | tf_op jit(solution)/shard_map/ppermute | solution.py:604
  18.9 7.3 %collective-permute-start.4 = (bf16[2,4,2,128,128]{4,3,2,1,0:T(8,128)(2,1)S(1)}, bf16[2,4,2,128,128]{4,3,2,1,0:T(8,128)(2,1)}, u32[]{:S(2)}, u32[]{:S(2)}) collective-permute-start(bf16[2,4,2,128,128]{4,3,2,1,0:T(8,128)(2,1)S(1)} %collective-permute-done.2.refs_8_), channel_id=1, source_target_pairs={{0,8},{8,0},{16,24},{24,16},{1,9},{9,1},{17,25},{25,17},{2,10},{10... | collective-permute-start | bytes 1572872 | tf_op jit(solution)/shard_map/ppermute | solution.py:604
  30.6 15.3 %collective-permute-start.10 = (bf16[2,4,2,128,128]{4,3,2,1,0:T(8,128)(2,1)}, bf16[2,4,2,128,128]{4,3,2,1,0:T(8,128)(2,1)S(1)}, u32[]{:S(2)}, u32[]{:S(2)}) collective-permute-start(bf16[2,4,2,128,128]{4,3,2,1,0:T(8,128)(2,1)} %collective-permute-done.6.refs_2_), channel_id=1, source_target_pairs={{0,4},{4,6},{6,2},{2,0},{1,5},{5,7},{7,3},{3,1},{8,12},{12,14},{14... | collective-permute-start | bytes 1572872 | tf_op jit(solution)/shard_map/ppermute | solution.py:604
  31.8 14.1 %collective-permute-start.9 = (bf16[2,4,2,128,128]{4,3,2,1,0:T(8,128)(2,1)}, bf16[2,4,2,128,128]{4,3,2,1,0:T(8,128)(2,1)S(1)}, u32[]{:S(2)}, u32[]{:S(2)}) collective-permute-start(bf16[2,4,2,128,128]{4,3,2,1,0:T(8,128)(2,1)} %collective-permute-done.6.refs_2_), channel_id=1, source_target_pairs={{0,16},{8,24},{16,0},{24,8},{1,17},{9,25},{17,1},{25,9},{2,18},{10... | collective-permute-start | bytes 1572872 | tf_op jit(solution)/shard_map/ppermute | solution.py:604
  32.3 13.6 %collective-permute-start.8 = (bf16[2,4,2,128,128]{4,3,2,1,0:T(8,128)(2,1)}, bf16[2,4,2,128,128]{4,3,2,1,0:T(8,128)(2,1)S(1)}, u32[]{:S(2)}, u32[]{:S(2)}) collective-permute-start(bf16[2,4,2,128,128]{4,3,2,1,0:T(8,128)(2,1)} %collective-permute-done.6.refs_2_), channel_id=1, source_target_pairs={{0,8},{8,0},{16,24},{24,16},{1,9},{9,1},{17,25},{25,17},{2,10},{10... | collective-permute-start | bytes 1572872 | tf_op jit(solution)/shard_map/ppermute | solution.py:604
  32.4 13.6 %collective-permute-start.7 = (bf16[2,4,2,128,128]{4,3,2,1,0:T(8,128)(2,1)}, bf16[2,4,2,128,128]{4,3,2,1,0:T(8,128)(2,1)S(1)}, u32[]{:S(2)}, u32[]{:S(2)}) collective-permute-start(bf16[2,4,2,128,128]{4,3,2,1,0:T(8,128)(2,1)} %collective-permute-done.5.refs_9_), channel_id=1, source_target_pairs={{0,8},{8,0},{16,24},{24,16},{1,9},{9,1},{17,25},{25,17},{2,10},{10... | collective-permute-start | bytes 1572872 | tf_op jit(solution)/shard_map/ppermute | solution.py:604
  46.0 15.5 %collective-permute-start.13 = (bf16[2,4,2,128,128]{4,3,2,1,0:T(8,128)(2,1)S(1)}, bf16[2,4,2,128,128]{4,3,2,1,0:T(8,128)(2,1)S(1)}, u32[]{:S(2)}, u32[]{:S(2)}) collective-permute-start(bf16[2,4,2,128,128]{4,3,2,1,0:T(8,128)(2,1)S(1)} %collective-permute-done.10.refs_2_.refs_3_), channel_id=1, source_target_pairs={{0,16},{8,24},{16,0},{24,8},{1,17},{9,25},{17,1},{25,9},{2,18},{10... | collective-permute-start | bytes 1572872 | tf_op jit(solution)/shard_map/ppermute | solution.py:604
  47.5 14.0 %collective-permute-start.12 = (bf16[2,4,2,128,128]{4,3,2,1,0:T(8,128)(2,1)S(1)}, bf16[2,4,2,128,128]{4,3,2,1,0:T(8,128)(2,1)S(1)}, u32[]{:S(2)}, u32[]{:S(2)}) collective-permute-start(bf16[2,4,2,128,128]{4,3,2,1,0:T(8,128)(2,1)S(1)} %collective-permute-done.10.refs_2_.refs_3_), channel_id=1, source_target_pairs={{0,8},{8,0},{16,24},{24,16},{1,9},{9,1},{17,25},{25,17},{2,10},{10... | collective-permute-start | bytes 1572872 | tf_op jit(solution)/shard_map/ppermute | solution.py:604
  47.5 14.0 %collective-permute-start.11 = (bf16[2,4,2,128,128]{4,3,2,1,0:T(8,128)(2,1)S(1)}, bf16[2,4,2,128,128]{4,3,2,1,0:T(8,128)(2,1)S(1)}, u32[]{:S(2)}, u32[]{:S(2)}) collective-permute-start(bf16[2,4,2,128,128]{4,3,2,1,0:T(8,128)(2,1)S(1)} %collective-permute-done.9.refs_10_), channel_id=1, source_target_pairs={{0,8},{8,0},{16,24},{24,16},{1,9},{9,1},{17,25},{25,17},{2,10},{10... | collective-permute-start | bytes 1572872 | tf_op jit(solution)/shard_map/ppermute | solution.py:604
  61.5 2.0 %collective-permute-start.14 = (bf16[2,4,2,128,128]{4,3,2,1,0:T(8,128)(2,1)S(1)}, bf16[2,4,2,128,128]{4,3,2,1,0:T(8,128)(2,1)S(1)}, u32[]{:S(2)}, u32[]{:S(2)}) collective-permute-start(bf16[2,4,2,128,128]{4,3,2,1,0:T(8,128)(2,1)S(1)} %collective-permute-done.13.refs_11_), channel_id=1, source_target_pairs={{0,8},{8,0},{16,24},{24,16},{1,9},{9,1},{17,25},{25,17},{2,10},{10... | collective-permute-start | bytes 1572872 | tf_op jit(solution)/shard_map/ppermute | solution.py:604
  69.1 9.2 %collective-permute-start.16 = (bf16[8,128,128]{2,1,0:T(8,128)(2,1)S(1)}, bf16[8,128,128]{2,1,0:T(8,128)(2,1)S(1)}, u32[]{:S(2)}, u32[]{:S(2)}) collective-permute-start(bf16[8,128,128]{2,1,0:T(8,128)(2,1)S(1)} %shard_map.121), channel_id=1, source_target_pairs={{0,1},{1,0},{2,3},{3,2},{4,5},{5,4},{6,7},{7,6},{8,9},{9,8},{10,11... | collective-permute-start | bytes 786440 | tf_op jit(solution)/shard_map/ppermute | solution.py:649
  73.8 9.4 %collective-permute-start.15 = (bf16[8,128,128]{2,1,0:T(8,128)(2,1)S(1)}, bf16[8,128,128]{2,1,0:T(8,128)(2,1)S(1)}, u32[]{:S(2)}, u32[]{:S(2)}) collective-permute-start(bf16[8,128,128]{2,1,0:T(8,128)(2,1)S(1)} %shard_map.119), channel_id=1, source_target_pairs={{0,1},{1,0},{2,3},{3,2},{4,5},{5,4},{6,7},{7,6},{8,9},{9,8},{10,11... | collective-permute-start | bytes 786440 | tf_op jit(solution)/shard_map/ppermute | solution.py:649

commit v18 on v17

--- a/solution.py
+++ b/solution.py
@@ -143,6 +143,16 @@
             def _():
                 copy.wait()
 
+    def sweep(step):
+        if len(rest) > 2:
+            lax.fori_loop(0, total, step, 0)
+            return
+        for n in range(1, len(rest) + 1):
+            @pl.when(total == n)
+            def _():
+                for b in range(n):
+                    step(b, 0)
+
     def look(b, carry):
         for n, (h, at) in enumerate(parts):
             s = nt(q[n], keys(buf.at[b], h))
@@ -150,7 +160,7 @@
             m_ref[h, at] = jnp.maximum(m_ref[h, at], fold(s, jnp.maximum))
         return carry
 
-    lax.fori_loop(0, total, look, 0)
+    sweep(look)
     for h, at in parts:
         m = m_ref[h, at]
         m = jnp.broadcast_to(jnp.max(m, axis=1, keepdims=True), m.shape)
@@ -180,7 +190,7 @@
             acc_ref[h, at] = acc_ref[h, at] + nt(p, values(buf.at[b], h))
         return carry
 
-    lax.fori_loop(0, total, weigh, 0)
+    sweep(weigh)
     if own:
         out = []
         for h in range(heads):
@@ -598,7 +608,7 @@
                     pairs = [(j, j ^ flip) for j in range(roles)]
                     sends.append((flip, (code, s), (code ^ flip, s), "role", pairs))
             if code == 0 and s + 1 < ring:
-                sends.append((roles if k else 1.5, (code, s), (0, s + 1), "ctx", along))
+                sends.append((roles, (code, s), (0, s + 1), "ctx", along))
         sends.sort(key=lambda a: a[0])
         names = [to for _, _, to, _, _ in sends]
         arrived = [lax.ppermute(gathered[of], axis, pairs) for _, of, _, axis, pairs in sends]

time: 84.8 us -> 83.2 us (0.981)
  waiting for transfers between devices: 13.2 us -> 11.4 us
  Pallas kernels: 58.5 us -> 56.9 us
  starting transfers between devices: 10.7 us -> 11.9 us
    ppermute x15, waiting for transfers between devices: 12.4 us -> 10.6 us  [shards(): lax.ppermute(gathered[of], axis, pairs)]
    pallas_call x2, Pallas kernels: 26.5 us -> 24.9 us  [prefill(): pl.pallas_call(functools.partial(prefill_kernel, own, count, slots, group...]
    ppermute x15, starting transfers between devices: 8.55 us -> 9.75 us  [shards(): lax.ppermute(gathered[of], axis, pairs)]
where the time goes in v18:
time: 83.2 us; the launch traced here: 82.3 us
  Pallas kernels  56.9 us (68%)
  starting transfers between devices  11.9 us (14%)
  waiting for transfers between devices  11.4 us (14%)
  local copies, waits for them, and re-layouts  1.05 us (1%)
    pallas_call x2, Pallas kernels, prefill(): pl.pallas_call(functools.partial(prefill_kernel, own, count, slots, group...  24.9 us
    pallas_call x4, Pallas kernels, decode(): pl.pallas_call(functools.partial(decode_kernel, extra, steps, target, tar...  12.5 us
    pallas_call x2, Pallas kernels, cache_part(): pl.pallas_call(functools.partial(cache_kernel, steps, heads, group, targe...  12.5 us
    ppermute x15, waiting for transfers between devices, shards(): lax.ppermute(gathered[of], axis, pairs)  10.6 us
    ppermute x15, starting transfers between devices, shards(): lax.ppermute(gathered[of], axis, pairs)  9.75 us
    pallas_call x1, Pallas kernels, collect(): pl.pallas_call(collect_kernel, grid_spec=pltpu.PrefetchScalarGridSpec(num...  2.44 us
    ppermute x2, starting transfers between devices, shards(): out = lax.ppermute(out, 'tp', shift)  2.16 us
    pallas_call x1, Pallas kernels, join(): pl.pallas_call(functools.partial(join_kernel, [len(p) for p in early], st...  1.73 us
  transfers between devices with their start and end apart: 17, of which 6 were waited for; matrix products, arithmetic and copies ran while one was open for 1% of the time, Pallas kernels for 59%

profile of v18, /device:TPU:24, one launch (start us, length us, event | category | flops | bytes accessed | tf_op | source)
XLA Modules:
  0.0 82.3 jit_solution(4055025383112248267)
XLA Ops:
  0.6 1.5 %shard_map.113.refs_1_.refs_0_ = bf16[2,4,2,128,128]{4,3,2,1,0:T(8,128)(2,1)S(1)} custom-call(bf16[1024,128]{1,0:T(8,128)(2,1)} %bitcast.20, bf16[1024,128]{1,0:T(8,128)(2,1)} %bitcast.21), custom_call_target="tpu_custom_call" | custom-call | flops 100000000 | bytes 2000000 | tf_op jit(solution)/shard_map/pallas_call | solution.py:58
  2.1 0.4 collective-permute-start.2
  2.5 1.5 %collective-permute-start.1 = (bf16[2,4,2,128,128]{4,3,2,1,0:T(8,128)(2,1)S(1)}, bf16[2,4,2,128,128]{4,3,2,1,0:T(8,128)(2,1)S(1)}, u32[]{:S(2)}, u32[]{:S(2)}) collective-permute-start(bf16[2,4,2,128,128]{4,3,2,1,0:T(8,128)(2,1)S(1)} %shard_map.113.refs_1_.refs_0_), channel_id=1, source_target_pairs={{0,16},{8,24},{16,0},{24,8},{1,17},{9,25},{17,1},{25,9},{2,18},{10... | collective-permute-start | bytes 1572872 | tf_op jit(solution)/shard_map/ppermute | solution.py:614
  4.0 0.0 collective-permute-start
  4.0 0.1 pad_add_fusion.meta_ref
  4.1 0.7 copy-done
  4.8 6.2 %shard_map.114 = (f32[16,128,128]{2,1,0:T(8,128)S(1)}, f32[16,8,128]{2,1,0:T(8,128)S(1)}) custom-call(s32[32]{0:T(128)S(1)} %copy-done, s32[2]{0:T(128)S(1)} %pad_add_fusion.meta_ref, bf16[32,128,128]{2,1,0:T(8,128)(2,1)} %bitcast.13, bf16[32,16,128]{2,1,0:T(8,128)(2,1)} %bitcast.16, bf16[32,16,128]{2,1,0:T(8,128)(2,1)} %bitcast.18, ...), custom_call_target="tpu_custom_call" | custom-call | flops 2147483648 | bytes 7000000 | tf_op jit(solution)/shard_map/pallas_call | solution.py:319
  11.0 4.8 %collective-permute-done.2.refs_1_ = bf16[2,4,2,128,128]{4,3,2,1,0:T(8,128)(2,1)S(1)} collective-permute-done((bf16[2,4,2,128,128]{4,3,2,1,0:T(8,128)(2,1)S(1)}, bf16[2,4,2,128,128]{4,3,2,1,0:T(8,128)(2,1)S(1)}, u32[]{:S(2)}, u32[]{:S(2)}) %collective-permute-start.2) | collective-permute-done | bytes 524320 | tf_op jit(solution)/shard_map/ppermute | solution.py:614
  15.9 0.1 collective-permute-done.1.refs_8_
  15.9 0.0 collective-permute-done.refs_4_
  15.9 1.2 %collective-permute-start.6 = (bf16[2,4,2,128,128]{4,3,2,1,0:T(8,128)(2,1)S(1)}, bf16[2,4,2,128,128]{4,3,2,1,0:T(8,128)(2,1)}, u32[]{:S(2)}, u32[]{:S(2)}) collective-permute-start(bf16[2,4,2,128,128]{4,3,2,1,0:T(8,128)(2,1)S(1)} %collective-permute-done.2.refs_1_), channel_id=1, source_target_pairs={{0,4},{4,6},{6,2},{2,0},{1,5},{5,7},{7,3},{3,1},{8,12},{12,14},{14... | collective-permute-start | bytes 1572872 | tf_op jit(solution)/shard_map/ppermute | solution.py:614
  17.1 1.5 %collective-permute-start.5 = (bf16[2,4,2,128,128]{4,3,2,1,0:T(8,128)(2,1)S(1)}, bf16[2,4,2,128,128]{4,3,2,1,0:T(8,128)(2,1)}, u32[]{:S(2)}, u32[]{:S(2)}) collective-permute-start(bf16[2,4,2,128,128]{4,3,2,1,0:T(8,128)(2,1)S(1)} %collective-permute-done.2.refs_1_), channel_id=1, source_target_pairs={{0,16},{8,24},{16,0},{24,8},{1,17},{9,25},{17,1},{25,9},{2,18},{10... | collective-permute-start | bytes 1572872 | tf_op jit(solution)/shard_map/ppermute | solution.py:614
  18.6 0.0 collective-permute-start.4
  18.6 0.5 collective-permute-start.3
  19.1 0.1 copy.18
  19.2 0.1 broadcast_in_dim.15
  19.3 0.1 copy.17
  19.4 0.1 reshape.39.slot_ref
  19.6 0.1 select_reduce_fusion.pick_ref
  19.7 6.2 %shard_map.115 = (f32[16,128,128]{2,1,0:T(8,128)S(1)}, f32[16,8,128]{2,1,0:T(8,128)S(1)}) custom-call(s32[32]{0:T(128)S(1)} %copy-done.1, s32[2]{0:T(128)S(1)} %pad_add_fusion.meta_ref, bf16[32,128,128]{2,1,0:T(8,128)(2,1)} %bitcast.14, bf16[32,16,128]{2,1,0:T(8,128)(2,1)} %bitcast.17, bf16[32,16,128]{2,1,0:T(8,128)(2,1)} %bitcast.19, ...), custom_call_target="tpu_custom_call" | custom-call | flops 2147483648 | bytes 7000000 | tf_op jit(solution)/shard_map/pallas_call | solution.py:319
  25.9 0.0 collective-permute-done.3.refs_12_
  25.9 2.8 %collective-permute-done.6.refs_2_ = bf16[2,4,2,128,128]{4,3,2,1,0:T(8,128)(2,1)} collective-permute-done((bf16[2,4,2,128,128]{4,3,2,1,0:T(8,128)(2,1)S(1)}, bf16[2,4,2,128,128]{4,3,2,1,0:T(8,128)(2,1)}, u32[]{:S(2)}, u32[]{:S(2)}) %collective-permute-start.6) | collective-permute-done | bytes 524320 | tf_op jit(solution)/shard_map/ppermute | solution.py:614
  28.8 1.0 %collective-permute-done.5.refs_9_ = bf16[2,4,2,128,128]{4,3,2,1,0:T(8,128)(2,1)} collective-permute-done((bf16[2,4,2,128,128]{4,3,2,1,0:T(8,128)(2,1)S(1)}, bf16[2,4,2,128,128]{4,3,2,1,0:T(8,128)(2,1)}, u32[]{:S(2)}, u32[]{:S(2)}) %collective-permute-start.5) | collective-permute-done | bytes 524320 | tf_op jit(solution)/shard_map/ppermute | solution.py:614
  29.7 1.5 %collective-permute-start.10 = (bf16[2,4,2,128,128]{4,3,2,1,0:T(8,128)(2,1)}, bf16[2,4,2,128,128]{4,3,2,1,0:T(8,128)(2,1)S(1)}, u32[]{:S(2)}, u32[]{:S(2)}) collective-permute-start(bf16[2,4,2,128,128]{4,3,2,1,0:T(8,128)(2,1)} %collective-permute-done.6.refs_2_), channel_id=1, source_target_pairs={{0,4},{4,6},{6,2},{2,0},{1,5},{5,7},{7,3},{3,1},{8,12},{12,14},{14... | collective-permute-start | bytes 1572872 | tf_op jit(solution)/shard_map/ppermute | solution.py:614
  31.3 1.5 %collective-permute-start.9 = (bf16[2,4,2,128,128]{4,3,2,1,0:T(8,128)(2,1)}, bf16[2,4,2,128,128]{4,3,2,1,0:T(8,128)(2,1)S(1)}, u32[]{:S(2)}, u32[]{:S(2)}) collective-permute-start(bf16[2,4,2,128,128]{4,3,2,1,0:T(8,128)(2,1)} %collective-permute-done.6.refs_2_), channel_id=1, source_target_pairs={{0,16},{8,24},{16,0},{24,8},{1,17},{9,25},{17,1},{25,9},{2,18},{10... | collective-permute-start | bytes 1572872 | tf_op jit(solution)/shard_map/ppermute | solution.py:614
  32.8 0.0 collective-permute-start.8
  32.8 0.5 collective-permute-start.7
  33.3 11.4 %shard_map.116 = (f32[4,4,512,128]{3,2,1,0:T(8,128)S(1)}, f32[4,4,512,128]{3,2,1,0:T(8,128)S(1)}, f32[4,4,512,128]{3,2,1,0:T(8,128)S(1)}) custom-call(s32[4]{0:T(128)S(1)} %compare_convert_fusion.needed_ref, bf16[1,256,32,128]{3,2,1,0:T(8,128)(2,1)} %refs_0_.3, bf16[2,4,2,128,128]{4,3,2,1,0:T(8,128)(2,1)S(1)} %collective-permute-done.2.refs_1_, ...), custom_call_target="tpu_custom_call" | custom-call | flops 8589934592 | bytes 12000000 | tf_op jit(solution)/shard_map/pallas_call | solution.py:226
  44.7 0.0 collective-permute-done.10.refs_2_.refs_3_
  44.7 0.0 collective-permute-done.9.refs_10_
  44.8 0.6 collective-permute-start.13
  45.4 0.5 collective-permute-start.11
  45.9 13.4 %shard_map.117 = bf16[1,256,32,128]{3,2,1,0:T(8,128)(2,1)} custom-call(s32[4]{0:T(128)S(1)} %compare_convert_fusion.needed_ref, bf16[1,256,32,128]{3,2,1,0:T(8,128)(2,1)} %refs_0_.3, bf16[2,4,2,128,128]{4,3,2,1,0:T(8,128)(2,1)S(1)} %shard_map.113.refs_1_.refs_0_, bf16[2,4,2,128,128]{4,3,2,1,0:T(8,128)(2,1)S(1)} %collective-permute-done.10.refs_2_.refs_3_, ...), custom_call_target="tpu_custom_call" | custom-call | flops 8589934592 | bytes 12000000 | tf_op jit(solution)/shard_map/pallas_call | solution.py:226
  59.3 0.0 collective-permute-done.13.refs_11_
  59.3 0.0 collective-permute-done.12.refs_7_
  59.3 0.1 collective-permute-start.14
  59.4 1.9 %collective-permute-done.14.refs_15_ = bf16[2,4,2,128,128]{4,3,2,1,0:T(8,128)(2,1)S(1)} collective-permute-done((bf16[2,4,2,128,128]{4,3,2,1,0:T(8,128)(2,1)S(1)}, bf16[2,4,2,128,128]{4,3,2,1,0:T(8,128)(2,1)S(1)}, u32[]{:S(2)}, u32[]{:S(2)}) %collective-permute-start.14) | collective-permute-done | bytes 524320 | tf_op jit(solution)/shard_map/ppermute | solution.py:614
  61.3 2.4 %shard_map.118 = (bf16[16,4,2,128,128]{4,3,2,1,0:T(8,128)(2,1)S(1)}, bf16[32,128,128]{2,1,0:T(8,128)(2,1)S(1)}) custom-call(s32[16]{0:T(128)S(1)} %select_reduce_fusion.pick_ref, bf16[32,128,128]{2,1,0:T(8,128)(2,1)} %bitcast.15, bf16[2,4,2,128,128]{4,3,2,1,0:T(8,128)(2,1)S(1)} %shard_map.113.refs_1_.refs_0_, ...), custom_call_target="tpu_custom_call" | custom-call | bytes 8000000 | tf_op jit(solution)/shard_map/pallas_call | solution.py:354
  63.7 3.1 %shard_map.121 = bf16[8,128,128]{2,1,0:T(8,128)(2,1)S(1)} custom-call(s32[128]{0:T(128)S(1)} %reshape.39.slot_ref, s32[2]{0:T(128)S(1)} %pad_add_fusion.meta_ref, bf16[32,128,128]{2,1,0:T(8,128)(2,1)S(1)} %get-tuple-element.67.refs_0_, f32[16,128,128]{2,1,0:T(8,128)S(1)} %get-tuple-element.68.refs_1_, f32[16,8,128]{2,1,0:T(8,128)S(1)} %get-tuple-element.69.refs_2_, ...), custom_call_target="tpu_custom_call" | custom-call | flops 1000000 | bytes 1000000 | tf_op jit(solution)/shard_map/pallas_call | solution.py:442
  66.9 1.6 %collective-permute-start.16 = (bf16[8,128,128]{2,1,0:T(8,128)(2,1)S(1)}, bf16[8,128,128]{2,1,0:T(8,128)(2,1)S(1)}, u32[]{:S(2)}, u32[]{:S(2)}) collective-permute-start(bf16[8,128,128]{2,1,0:T(8,128)(2,1)S(1)} %shard_map.121), channel_id=1, source_target_pairs={{0,1},{1,0},{2,3},{3,2},{4,5},{5,4},{6,7},{7,6},{8,9},{9,8},{10,11... | collective-permute-start | bytes 786440 | tf_op jit(solution)/shard_map/ppermute | solution.py:659
  68.5 3.1 %shard_map.119 = bf16[8,128,128]{2,1,0:T(8,128)(2,1)S(1)} custom-call(s32[128]{0:T(128)S(1)} %reshape.39.slot_ref, s32[2]{0:T(128)S(1)} %pad_add_fusion.meta_ref, bf16[32,128,128]{2,1,0:T(8,128)(2,1)S(1)} %get-tuple-element.67.refs_0_, f32[16,128,128]{2,1,0:T(8,128)S(1)} %get-tuple-element.68.refs_1_, f32[16,8,128]{2,1,0:T(8,128)S(1)} %get-tuple-element.69.refs_2_, ...), custom_call_target="tpu_custom_call" | custom-call | flops 1000000 | bytes 1000000 | tf_op jit(solution)/shard_map/pallas_call | solution.py:442
  71.6 0.6 collective-permute-start.15
  72.2 3.1 %shard_map.120.refs_0_ = bf16[8,128,128]{2,1,0:T(8,128)(2,1)S(1)} custom-call(s32[128]{0:T(128)S(1)} %reshape.39.slot_ref, s32[2]{0:T(128)S(1)} %pad_add_fusion.meta_ref, bf16[32,128,128]{2,1,0:T(8,128)(2,1)S(1)} %get-tuple-element.67.refs_0_, f32[16,128,128]{2,1,0:T(8,128)S(1)} %get-tuple-element.73.refs_1_, f32[16,8,128]{2,1,0:T(8,128)S(1)} %get-tuple-element.74.refs_2_, ...), custom_call_target="tpu_custom_call" | custom-call | flops 1000000 | bytes 1000000 | tf_op jit(solution)/shard_map/pallas_call | solution.py:442
  75.3 0.8 collective-permute-done.16.refs_2_
  76.1 3.1 %shard_map.122.refs_1_ = bf16[8,128,128]{2,1,0:T(8,128)(2,1)S(1)} custom-call(s32[128]{0:T(128)S(1)} %reshape.39.slot_ref, s32[2]{0:T(128)S(1)} %pad_add_fusion.meta_ref, bf16[32,128,128]{2,1,0:T(8,128)(2,1)S(1)} %get-tuple-element.67.refs_0_, f32[16,128,128]{2,1,0:T(8,128)S(1)} %get-tuple-element.73.refs_1_, f32[16,8,128]{2,1,0:T(8,128)S(1)} %get-tuple-element.74.refs_2_, ...), custom_call_target="tpu_custom_call" | custom-call | flops 1000000 | bytes 1000000 | tf_op jit(solution)/shard_map/pallas_call | solution.py:442
  79.3 1.7 %shard_map.123.refs_1_ = bf16[16,4,8192]{2,1,0:T(4,128)(2,1)} custom-call(s32[2]{0:T(128)S(1)} %pad_add_fusion.meta_ref, bf16[8,128,128]{2,1,0:T(8,128)(2,1)S(1)} %shard_map.120.refs_0_, bf16[8,128,128]{2,1,0:T(8,128)(2,1)S(1)} %shard_map.122.refs_1_, bf16[8,128,128]{2,1,0:T(8,128)(2,1)S(1)} %collective-permute-done.16.refs_2_), custom_call_target="tpu_custom_call" | custom-call | bytes 2000000 | tf_op jit(solution)/shard_map/pallas_call | solution.py:511
  81.0 0.0 collective-permute-done.15.refs_0_
  81.0 1.3 %shard_map.124 = bf16[16,4,8192]{2,1,0:T(4,128)(2,1)} custom-call(s32[2]{0:T(128)S(1)} %pad_add_fusion.meta_ref, bf16[8,128,128]{2,1,0:T(8,128)(2,1)S(1)} %collective-permute-done.15.refs_0_, bf16[16,4,8192]{2,1,0:T(4,128)(2,1)} %shard_map.123.refs_1_), custom_call_target="tpu_custom_call", output_to_operand_aliasing={{}: (2, {})} | custom-call | bytes 1000000 | tf_op jit(solution)/shard_map/pallas_call | solution.py:525
  (12 shorter events, 0.1 us)
Async XLA Ops:
  2.1 13.7 %collective-permute-start.2 = (bf16[2,4,2,128,128]{4,3,2,1,0:T(8,128)(2,1)S(1)}, bf16[2,4,2,128,128]{4,3,2,1,0:T(8,128)(2,1)S(1)}, u32[]{:S(2)}, u32[]{:S(2)}) collective-permute-start(bf16[2,4,2,128,128]{4,3,2,1,0:T(8,128)(2,1)S(1)} %shard_map.113.refs_1_.refs_0_), channel_id=1, source_target_pairs={{0,4},{4,6},{6,2},{2,0},{1,5},{5,7},{7,3},{3,1},{8,12},{12,14},{14... | collective-permute-start | bytes 1572872 | tf_op jit(solution)/shard_map/ppermute | solution.py:614
  2.5 13.4 %collective-permute-start.1 = (bf16[2,4,2,128,128]{4,3,2,1,0:T(8,128)(2,1)S(1)}, bf16[2,4,2,128,128]{4,3,2,1,0:T(8,128)(2,1)S(1)}, u32[]{:S(2)}, u32[]{:S(2)}) collective-permute-start(bf16[2,4,2,128,128]{4,3,2,1,0:T(8,128)(2,1)S(1)} %shard_map.113.refs_1_.refs_0_), channel_id=1, source_target_pairs={{0,16},{8,24},{16,0},{24,8},{1,17},{9,25},{17,1},{25,9},{2,18},{10... | collective-permute-start | bytes 1572872 | tf_op jit(solution)/shard_map/ppermute | solution.py:614
  4.0 11.9 %collective-permute-start = (bf16[2,4,2,128,128]{4,3,2,1,0:T(8,128)(2,1)S(1)}, bf16[2,4,2,128,128]{4,3,2,1,0:T(8,128)(2,1)S(1)}, u32[]{:S(2)}, u32[]{:S(2)}) collective-permute-start(bf16[2,4,2,128,128]{4,3,2,1,0:T(8,128)(2,1)S(1)} %shard_map.113.refs_1_.refs_0_), channel_id=1, source_target_pairs={{0,8},{8,0},{16,24},{24,16},{1,9},{9,1},{17,25},{25,17},{2,10},{10... | collective-permute-start | bytes 1572872 | tf_op jit(solution)/shard_map/ppermute | solution.py:614
  4.1 0.7 copy-start
  4.8 14.3 %copy-start.2 = (s32[32,4]{0,1:T(4,128)S(1)}, s32[32,4]{0,1:T(4,128)}, u32[]{:S(2)}) copy-start(s32[32,4]{0,1:T(4,128)} %param.19) | copy-start | bytes 1540
  4.8 14.9 %copy-start.1 = (s32[32]{0:T(128)S(1)}, s32[32]{0:T(128)}, u32[]{:S(2)}) copy-start(s32[32]{0:T(128)} %len_ref.3) | copy-start | bytes 388
  15.9 12.8 %collective-permute-start.6 = (bf16[2,4,2,128,128]{4,3,2,1,0:T(8,128)(2,1)S(1)}, bf16[2,4,2,128,128]{4,3,2,1,0:T(8,128)(2,1)}, u32[]{:S(2)}, u32[]{:S(2)}) collective-permute-start(bf16[2,4,2,128,128]{4,3,2,1,0:T(8,128)(2,1)S(1)} %collective-permute-done.2.refs_1_), channel_id=1, source_target_pairs={{0,4},{4,6},{6,2},{2,0},{1,5},{5,7},{7,3},{3,1},{8,12},{12,14},{14... | collective-permute-start | bytes 1572872 | tf_op jit(solution)/shard_map/ppermute | solution.py:614
  17.1 12.6 %collective-permute-start.5 = (bf16[2,4,2,128,128]{4,3,2,1,0:T(8,128)(2,1)S(1)}, bf16[2,4,2,128,128]{4,3,2,1,0:T(8,128)(2,1)}, u32[]{:S(2)}, u32[]{:S(2)}) collective-permute-start(bf16[2,4,2,128,128]{4,3,2,1,0:T(8,128)(2,1)S(1)} %collective-permute-done.2.refs_1_), channel_id=1, source_target_pairs={{0,16},{8,24},{16,0},{24,8},{1,17},{9,25},{17,1},{25,9},{2,18},{10... | collective-permute-start | bytes 1572872 | tf_op jit(solution)/shard_map/ppermute | solution.py:614
  18.6 11.1 %collective-permute-start.4 = (bf16[2,4,2,128,128]{4,3,2,1,0:T(8,128)(2,1)S(1)}, bf16[2,4,2,128,128]{4,3,2,1,0:T(8,128)(2,1)}, u32[]{:S(2)}, u32[]{:S(2)}) collective-permute-start(bf16[2,4,2,128,128]{4,3,2,1,0:T(8,128)(2,1)S(1)} %collective-permute-done.2.refs_1_), channel_id=1, source_target_pairs={{0,8},{8,0},{16,24},{24,16},{1,9},{9,1},{17,25},{25,17},{2,10},{10... | collective-permute-start | bytes 1572872 | tf_op jit(solution)/shard_map/ppermute | solution.py:614
  18.6 7.3 %collective-permute-start.3 = (bf16[2,4,2,128,128]{4,3,2,1,0:T(8,128)(2,1)S(1)}, bf16[2,4,2,128,128]{4,3,2,1,0:T(8,128)(2,1)}, u32[]{:S(2)}, u32[]{:S(2)}) collective-permute-start(bf16[2,4,2,128,128]{4,3,2,1,0:T(8,128)(2,1)S(1)} %collective-permute-done.1.refs_8_), channel_id=1, source_target_pairs={{0,8},{8,0},{16,24},{24,16},{1,9},{9,1},{17,25},{25,17},{2,10},{10... | collective-permute-start | bytes 1572872 | tf_op jit(solution)/shard_map/ppermute | solution.py:614
  29.7 15.0 %collective-permute-start.10 = (bf16[2,4,2,128,128]{4,3,2,1,0:T(8,128)(2,1)}, bf16[2,4,2,128,128]{4,3,2,1,0:T(8,128)(2,1)S(1)}, u32[]{:S(2)}, u32[]{:S(2)}) collective-permute-start(bf16[2,4,2,128,128]{4,3,2,1,0:T(8,128)(2,1)} %collective-permute-done.6.refs_2_), channel_id=1, source_target_pairs={{0,4},{4,6},{6,2},{2,0},{1,5},{5,7},{7,3},{3,1},{8,12},{12,14},{14... | collective-permute-start | bytes 1572872 | tf_op jit(solution)/shard_map/ppermute | solution.py:614
  31.3 13.5 %collective-permute-start.9 = (bf16[2,4,2,128,128]{4,3,2,1,0:T(8,128)(2,1)}, bf16[2,4,2,128,128]{4,3,2,1,0:T(8,128)(2,1)S(1)}, u32[]{:S(2)}, u32[]{:S(2)}) collective-permute-start(bf16[2,4,2,128,128]{4,3,2,1,0:T(8,128)(2,1)} %collective-permute-done.6.refs_2_), channel_id=1, source_target_pairs={{0,16},{8,24},{16,0},{24,8},{1,17},{9,25},{17,1},{25,9},{2,18},{10... | collective-permute-start | bytes 1572872 | tf_op jit(solution)/shard_map/ppermute | solution.py:614
  32.8 12.0 %collective-permute-start.8 = (bf16[2,4,2,128,128]{4,3,2,1,0:T(8,128)(2,1)}, bf16[2,4,2,128,128]{4,3,2,1,0:T(8,128)(2,1)S(1)}, u32[]{:S(2)}, u32[]{:S(2)}) collective-permute-start(bf16[2,4,2,128,128]{4,3,2,1,0:T(8,128)(2,1)} %collective-permute-done.6.refs_2_), channel_id=1, source_target_pairs={{0,8},{8,0},{16,24},{24,16},{1,9},{9,1},{17,25},{25,17},{2,10},{10... | collective-permute-start | bytes 1572872 | tf_op jit(solution)/shard_map/ppermute | solution.py:614
  32.8 12.0 %collective-permute-start.7 = (bf16[2,4,2,128,128]{4,3,2,1,0:T(8,128)(2,1)}, bf16[2,4,2,128,128]{4,3,2,1,0:T(8,128)(2,1)S(1)}, u32[]{:S(2)}, u32[]{:S(2)}) collective-permute-start(bf16[2,4,2,128,128]{4,3,2,1,0:T(8,128)(2,1)} %collective-permute-done.5.refs_9_), channel_id=1, source_target_pairs={{0,8},{8,0},{16,24},{24,16},{1,9},{9,1},{17,25},{25,17},{2,10},{10... | collective-permute-start | bytes 1572872 | tf_op jit(solution)/shard_map/ppermute | solution.py:614
  44.8 14.5 %collective-permute-start.13 = (bf16[2,4,2,128,128]{4,3,2,1,0:T(8,128)(2,1)S(1)}, bf16[2,4,2,128,128]{4,3,2,1,0:T(8,128)(2,1)S(1)}, u32[]{:S(2)}, u32[]{:S(2)}) collective-permute-start(bf16[2,4,2,128,128]{4,3,2,1,0:T(8,128)(2,1)S(1)} %collective-permute-done.10.refs_2_.refs_3_), channel_id=1, source_target_pairs={{0,16},{8,24},{16,0},{24,8},{1,17},{9,25},{17,1},{25,9},{2,18},{10... | collective-permute-start | bytes 1572872 | tf_op jit(solution)/shard_map/ppermute | solution.py:614
  45.4 14.0 %collective-permute-start.12 = (bf16[2,4,2,128,128]{4,3,2,1,0:T(8,128)(2,1)S(1)}, bf16[2,4,2,128,128]{4,3,2,1,0:T(8,128)(2,1)S(1)}, u32[]{:S(2)}, u32[]{:S(2)}) collective-permute-start(bf16[2,4,2,128,128]{4,3,2,1,0:T(8,128)(2,1)S(1)} %collective-permute-done.10.refs_2_.refs_3_), channel_id=1, source_target_pairs={{0,8},{8,0},{16,24},{24,16},{1,9},{9,1},{17,25},{25,17},{2,10},{10... | collective-permute-start | bytes 1572872 | tf_op jit(solution)/shard_map/ppermute | solution.py:614
  45.4 13.9 %collective-permute-start.11 = (bf16[2,4,2,128,128]{4,3,2,1,0:T(8,128)(2,1)S(1)}, bf16[2,4,2,128,128]{4,3,2,1,0:T(8,128)(2,1)S(1)}, u32[]{:S(2)}, u32[]{:S(2)}) collective-permute-start(bf16[2,4,2,128,128]{4,3,2,1,0:T(8,128)(2,1)S(1)} %collective-permute-done.9.refs_10_), channel_id=1, source_target_pairs={{0,8},{8,0},{16,24},{24,16},{1,9},{9,1},{17,25},{25,17},{2,10},{10... | collective-permute-start | bytes 1572872 | tf_op jit(solution)/shard_map/ppermute | solution.py:614
  59.3 2.0 %collective-permute-start.14 = (bf16[2,4,2,128,128]{4,3,2,1,0:T(8,128)(2,1)S(1)}, bf16[2,4,2,128,128]{4,3,2,1,0:T(8,128)(2,1)S(1)}, u32[]{:S(2)}, u32[]{:S(2)}) collective-permute-start(bf16[2,4,2,128,128]{4,3,2,1,0:T(8,128)(2,1)S(1)} %collective-permute-done.13.refs_11_), channel_id=1, source_target_pairs={{0,8},{8,0},{16,24},{24,16},{1,9},{9,1},{17,25},{25,17},{2,10},{10... | collective-permute-start | bytes 1572872 | tf_op jit(solution)/shard_map/ppermute | solution.py:614
  66.9 9.2 %collective-permute-start.16 = (bf16[8,128,128]{2,1,0:T(8,128)(2,1)S(1)}, bf16[8,128,128]{2,1,0:T(8,128)(2,1)S(1)}, u32[]{:S(2)}, u32[]{:S(2)}) collective-permute-start(bf16[8,128,128]{2,1,0:T(8,128)(2,1)S(1)} %shard_map.121), channel_id=1, source_target_pairs={{0,1},{1,0},{2,3},{3,2},{4,5},{5,4},{6,7},{7,6},{8,9},{9,8},{10,11... | collective-permute-start | bytes 786440 | tf_op jit(solution)/shard_map/ppermute | solution.py:659
  71.6 9.4 %collective-permute-start.15 = (bf16[8,128,128]{2,1,0:T(8,128)(2,1)S(1)}, bf16[8,128,128]{2,1,0:T(8,128)(2,1)S(1)}, u32[]{:S(2)}, u32[]{:S(2)}) collective-permute-start(bf16[8,128,128]{2,1,0:T(8,128)(2,1)S(1)} %shard_map.119), channel_id=1, source_target_pairs={{0,1},{1,0},{2,3},{3,2},{4,5},{5,4},{6,7},{7,6},{8,9},{9,8},{10,11... | collective-permute-start | bytes 786440 | tf_op jit(solution)/shard_map/ppermute | solution.py:659
